TPU v7x, 32 devices: a whole 2x2x4 slice. The times are simulated.
32 devices in a mesh: groups: 2 (over y), row: 4 (over z), col: 4 (over x, core).
Axes of the slice: x: 2, y: 2, z: 4, core: 2. Of those that a mesh axis runs over, the one named last changes fastest.
Arguments:
- gradient: bfloat16 [8192, 4096], P(('groups', 'row'), 'col'), parts along dimension 0, may hold values from -6 to 6
- first_moment: float32 [8192, 4096], P(('groups', 'row'), 'col'), parts along dimension 0, may hold values from -4 to 4
- second_moment: float32 [8192, 4096], P(('groups', 'row'), 'col'), parts along dimension 0, may hold values from 0.01 to 1
- left_basis: bfloat16 [8192, 4096], P(('groups', 'col'), 'row'), parts along dimension 0, may hold values from -0.09375 to 0.09375
- right_basis: bfloat16 [8192, 4096], P(('groups', 'row'), 'col'), parts along dimension 0, may hold values from -0.09375 to 0.09375
Outputs:
- new_first: float32 [8192, 4096], P(('groups', 'row'), 'col'), parts along dimension 0
- new_second: float32 [8192, 4096], P(('groups', 'row'), 'col'), parts along dimension 0
- update: float32 [8192, 4096], P(('groups', 'row'), 'col'), parts along dimension 0
There are 2 independent parts, one for each index of `groups`. A program takes and returns all parts, laid end to end along the dimension named above; each array names one. Nothing has to cross between parts.
All inputs are finite; a program needn't handle non-finite values.
Results may differ from a plain program's by a relative error of at most 0.0003.
Values may be sent and summed in bfloat16 or wider, within the bound.
No kernel may reach another device: no remote copies, remote signals or barrier semaphores. Data moves between devices by JAX's collectives and lax.ppermute only.
A program may use at most 128 MiB of HBM per device.

v0:
```python
import jax
import jax.numpy as jnp
from jax import lax
from jax.sharding import PartitionSpec as P

BETA_ONE = 0.9
BETA_TWO = 0.95
EPSILON = 1e-08


def local(gradient, first_moment, second_moment, left_basis, right_basis):
    highest = lax.Precision.HIGHEST
    left_cols = lax.all_gather(left_basis, "col", axis=0, tiled=True)
    right_cols = lax.all_gather(right_basis, "row", axis=0, tiled=True)
    basis_rows = left_cols
    halfway = lax.dot_general(
        basis_rows,
        lax.all_gather(gradient, "row", axis=0, tiled=True),
        (((0,), (0,)), ((), ())),
        preferred_element_type=jnp.float32,
    )
    basis_rows = right_cols.astype(jnp.float32)
    rotated = jnp.dot(
        lax.all_gather(halfway, "col", axis=1, tiled=True), basis_rows, precision=highest
    )
    new_first = BETA_ONE * first_moment + (1.0 - BETA_ONE) * rotated
    new_second = BETA_TWO * second_moment + (1.0 - BETA_TWO) * rotated * rotated
    normed = new_first / (jnp.sqrt(new_second) + EPSILON)
    basis_rows = right_cols.astype(jnp.float32)
    restored = lax.psum_scatter(
        lax.dot_general(basis_rows, normed, (((1,), (1,)), ((), ())), precision=highest),
        "col",
        scatter_dimension=0,
        tiled=True,
    )
    basis_rows = left_cols.astype(jnp.float32)
    update = lax.psum_scatter(
        lax.dot_general(basis_rows, restored, (((1,), (1,)), ((), ())), precision=highest),
        "row",
        scatter_dimension=0,
        tiled=True,
    )
    return (new_first, new_second, update)


def solution(mesh):
    return jax.shard_map(
        local,
        mesh=mesh,
        in_specs=(
            P(("groups", "row"), "col"),
            P(("groups", "row"), "col"),
            P(("groups", "row"), "col"),
            P(("groups", "col"), "row"),
            P(("groups", "row"), "col"),
        ),
        out_specs=(
            P(("groups", "row"), "col"),
            P(("groups", "row"), "col"),
            P(("groups", "row"), "col"),
        ),
        check_vma=False,
    )
```

profile of v0, /device:TPU:0, one launch (start us, length us, event | category | flops | bytes accessed | tf_op | source)
XLA Modules:
  0.0 1024.2 jit_solution(18021629821378556326)
XLA Ops:
  7.2 0.0 all-gather.7.cloned.1.call-start
  7.2 0.7 all-gather.7.cloned.1.call-update
  7.9 0.0 all-gather.5.cloned.1.call-start
  7.9 0.7 all-gather.5.cloned.1.call-update
  8.6 0.0 all-gather.11.cloned.1.call-start
  8.7 0.7 all-gather.11.cloned.1.call-update
  9.4 0.0 all-gather.9.cloned.1.call-start
  9.4 152.5 %all-gather.7.cloned.1.call-done = bf16[4096,1024]{1,0:T(8,128)(2,1)} async-done(((bf16[1024,1024]{1,0:T(8,128)(2,1)}), bf16[4096,1024]{1,0:T(8,128)(2,1)}) %all-gather.7.cloned.1.call-update) | async-done | bytes 8388624 | tf_op jit(solution)/shard_map/all_gather | solution.py:18
  161.9 58.1 %all-gather.5.cloned.1.call-done = bf16[4096,1024]{1,0:T(8,128)(2,1)} async-done(((bf16[1024,1024]{1,0:T(8,128)(2,1)}), bf16[4096,1024]{1,0:T(8,128)(2,1)}) %all-gather.5.cloned.1.call-update) | async-done | bytes 8388624 | tf_op jit(solution)/shard_map/all_gather | solution.py:13
  220.0 15.0 %fusion.6 = f32[1024,1024]{1,0:T(8,128)} fusion(bf16[4096,1024]{1,0:T(8,128)(2,1)} %all-gather.5.cloned.1.call-done, bf16[4096,1024]{1,0:T(8,128)(2,1)} %all-gather.7.cloned.1.call-done), kind=kOutput, calls=%fused_computation.10 | convolution fusion | flops 8589934592 | bytes 20971520 | tf_op jit(solution)/shard_map/dot_general | solution.py:16
  235.1 0.0 all-gather.9.cloned.1.call-update
  235.1 0.0 reduce-scatter.3.cloned.1.call-start
  235.1 136.1 %all-gather.11.cloned.1.call-done = bf16[4096,1024]{1,0:T(8,128)(2,1)} async-done(((bf16[1024,1024]{1,0:T(8,128)(2,1)}), bf16[4096,1024]{1,0:T(8,128)(2,1)}) %all-gather.11.cloned.1.call-update) | async-done | bytes 8388624 | tf_op jit(solution)/shard_map/all_gather | solution.py:14
  371.3 106.2 %all-gather.9.cloned.1.call-done = f32[1024,4096]{1,0:T(8,128)} async-done(((f32[1024,1024]{1,0:T(8,128)}), f32[1024,4096]{1,0:T(8,128)}) %all-gather.9.cloned.1.call-update) | async-done | bytes 16777232 | tf_op jit(solution)/shard_map/all_gather | solution.py:24
  477.5 0.0 copy-start
  477.5 33.4 %fusion = (f32[1024,1024]{1,0:T(8,128)S(1)}, f32[1024,1024]{1,0:T(8,128)S(1)}) fusion(f32[1024,1024]{1,0:T(8,128)} %param.7, f32[1024,1024]{1,0:T(8,128)} %param.6, f32[1024,4096]{1,0:T(8,128)} %all-gather.9.cloned.1.call-done, bf16[4096,1024]{1,0:T(8,128)(2,1)} %all-gather.11.cloned.1.call-done), kind=kOutput, calls=%fused_computation.3 | convolution fusion | flops 51546947584 | bytes 41943040 | tf_op jit(solution)/shard_map/dot_general | solution.py:23
  510.9 0.0 copy-start.1
  510.9 0.0 copy-start.2
  510.9 2.0 copy-done.1
  512.9 1.4 copy-done.2
  514.3 0.0 copy-done
  514.3 33.4 %convolution_bitcast_fusion.1 = f32[4096,1024]{0,1:T(8,128)} fusion(bf16[4096,1024]{1,0:T(8,128)(2,1)S(1)} %copy-done, f32[1024,1024]{1,0:T(8,128)S(1)} %get-tuple-element.7, f32[1024,1024]{1,0:T(8,128)S(1)} %get-tuple-element.6), kind=kOutput, calls=%fused_computation.1 | convolution fusion | flops 51541704704 | bytes 33554432 | tf_op jit(solution)/shard_map/dot_general | solution.py:31
  547.7 0.0 reduce-scatter.3.cloned.1.call-update
  547.8 0.0 reduce-scatter.5.cloned.1.call-start
  547.8 126.2 %reduce-scatter.3.cloned.1.call-done = f32[1024,1024]{0,1:T(8,128)} async-done(((f32[4096,1024]{0,1:T(8,128)}), f32[1024,1024]{0,1:T(8,128)}) %reduce-scatter.3.cloned.1.call-update) | async-done | bytes 4194320 | tf_op jit(solution)/shard_map/reduce_scatter | solution.py:30
  674.0 57.5 %convolution_bitcast_fusion = f32[4096,1024]{0,1:T(8,128)} fusion(f32[1024,1024]{0,1:T(8,128)} %reduce-scatter.3.cloned.1.call-done, bf16[4096,1024]{1,0:T(8,128)(2,1)} %all-gather.5.cloned.1.call-done), kind=kOutput, calls=%fused_computation | convolution fusion | flops 51539607552 | bytes 29360128 | tf_op jit(solution)/shard_map/dot_general | solution.py:38
  731.5 0.0 reduce-scatter.5.cloned.1.call-update
  731.5 280.5 %reduce-scatter.5.cloned.1.call-done = f32[1024,1024]{0,1:T(8,128)} async-done(((f32[4096,1024]{0,1:T(8,128)}), f32[1024,1024]{0,1:T(8,128)}) %reduce-scatter.5.cloned.1.call-update) | async-done | bytes 4194320 | tf_op jit(solution)/shard_map/reduce_scatter | solution.py:37
  1012.0 5.3 copy.8
Async XLA Ops:
  7.2 154.8 %all-gather.7.cloned.1.call-start = ((), (), s32[]{:S(2)}) async-start(), calls=%async_computation.3 | async-start | bytes 10485760 | tf_op jit(solution)/shard_map/all_gather | solution.py:18
  7.9 212.1 %all-gather.5.cloned.1.call-start = ((), (), s32[]{:S(2)}) async-start(), calls=%async_computation.2 | async-start | bytes 10485760 | tf_op jit(solution)/shard_map/all_gather | solution.py:13
  8.6 362.6 %all-gather.11.cloned.1.call-start = ((), (), s32[]{:S(2)}) async-start(), calls=%async_computation.5 | async-start | bytes 10485760 | tf_op jit(solution)/shard_map/all_gather | solution.py:14
  9.4 468.1 %all-gather.9.cloned.1.call-start = ((), (), s32[]{:S(2)}) async-start(), calls=%async_computation.4 | async-start | bytes 20971520 | tf_op jit(solution)/shard_map/all_gather | solution.py:24
  235.1 438.9 %reduce-scatter.3.cloned.1.call-start = ((), (), s32[]{:S(2)}) async-start(), calls=%async_computation.6 | async-start | bytes 20971520 | tf_op jit(solution)/shard_map/reduce_scatter | solution.py:30
  477.5 36.8 %copy-start = (bf16[4096,1024]{1,0:T(8,128)(2,1)S(1)}, bf16[4096,1024]{1,0:T(8,128)(2,1)}, u32[]{:S(2)}) copy-start(bf16[4096,1024]{1,0:T(8,128)(2,1)} %all-gather.11.cloned.1.call-done) | copy-start | bytes 25165828
  510.9 2.0 copy-start.1
  510.9 3.4 copy-start.2
  547.8 464.3 %reduce-scatter.5.cloned.1.call-start = ((), (), s32[]{:S(2)}) async-start(), calls=%async_computation.7 | async-start | bytes 20971520 | tf_op jit(solution)/shard_map/reduce_scatter | solution.py:37
Sparse Core Ops, SparseCore 0:
  9.6 152.3 all-gather.6
  163.5 56.5 all-gather.4
  221.6 149.6 all-gather.10
  373.3 104.1 all-gather.8
  547.9 126.0 reduce-scatter.2
  731.7 280.3 reduce-scatter.4
where the time goes:
time: 1020 us
  waiting for transfers between devices  862 us (85%)
  matrix products  139 us (14%)
  between operations  14.1 us (1%)
    reduce_scatter x1, waiting for transfers between devices, local(): lax.psum_scatter(lax.dot_general(basis_rows, restored, (((1,), (1,)), (()...  280 us
    all_gather x1, waiting for transfers between devices, local(): lax.all_gather(gradient, 'row', axis=0, tiled=True)  153 us
    all_gather x1, waiting for transfers between devices, local(): right_cols = lax.all_gather(right_basis, 'row', axis=0, tiled=True)  136 us
    reduce_scatter x1, waiting for transfers between devices, local(): lax.psum_scatter(lax.dot_general(basis_rows, normed, (((1,), (1,)), ((),...  126 us
    all_gather x1, waiting for transfers between devices, local(): lax.all_gather(halfway, 'col', axis=1, tiled=True)  106 us
    all_gather x1, waiting for transfers between devices, local(): left_cols = lax.all_gather(left_basis, 'col', axis=0, tiled=True)  58.1 us
    dot_general x1, matrix products, local(): lax.dot_general(basis_rows, restored, (((1,), (1,)), ((), ())), precision...  57.5 us
    dot_general x1, matrix products, local(): jnp.dot(lax.all_gather(halfway, 'col', axis=1, tiled=True), basis_rows, p...  33.4 us
  transfers between devices with their start and end apart: 6, of which 6 were waited for; matrix products, arithmetic and copies ran while one was open for 1% of the time, Pallas kernels for 0%

commit v1 on v0

v1 whole, which is shorter than its diff:
```python
import jax
import jax.numpy as jnp
from jax import lax
from jax.sharding import PartitionSpec as P

BETA_ONE = 0.9
BETA_TWO = 0.95
EPSILON = 1e-08
CHUNKS = 4
F32 = jnp.float32
BF16 = jnp.bfloat16


def split(value):
    high = lax.reduce_precision(value, exponent_bits=8, mantissa_bits=7)
    return high.astype(BF16), (value - high).astype(BF16)


def dot(a, b, dims):
    return lax.dot_general(a, b, (dims, ((), ())), preferred_element_type=F32)


def build(cols):
    def swap(value, distance):
        return lax.ppermute(value, "col", [(i, i ^ distance) for i in range(cols)])

    def gather_col(block):
        me = lax.axis_index("col")
        out = jnp.zeros((cols,) + block.shape, block.dtype)
        held = {0: block}
        for distance in range(2, cols, 2):
            held[distance] = swap(block, distance)
        for distance in range(0, cols, 2):
            held[distance + 1] = swap(held[distance], 1)
        for distance, value in held.items():
            out = lax.dynamic_update_index_in_dim(out, value, me ^ distance, 0)
        return out

    def scatter_col(part):
        total = None
        for distance in list(range(2, cols, 2)) + [0]:
            term = swap(part(distance ^ 1), 1) + part(distance)
            if distance:
                term = swap(term, distance)
            total = term if total is None else total + term
        return total

    def local(gradient, first_moment, second_moment, left_basis, right_basis):
        me = lax.axis_index("col")
        depth, width = gradient.shape
        grad_cols = lax.all_gather(gradient, "row", axis=0, tiled=True)
        left_cols = gather_col(left_basis)
        left_cols = left_cols.reshape(-1, left_cols.shape[-1])
        right_cols = lax.all_gather(right_basis, "row", axis=0, tiled=True)
        halfway = dot(left_cols, grad_cols, ((0,), (0,)))
        high, low = split(halfway)
        high, low = gather_col(high), gather_col(low)
        by_col = right_cols.reshape(cols, width, width)
        rotated = dot(high, by_col, ((0, 2), (0, 1))) + dot(low, by_col, ((0, 2), (0, 1)))
        new_first = BETA_ONE * first_moment + (1.0 - BETA_ONE) * rotated
        new_second = BETA_TWO * second_moment + (1.0 - BETA_TWO) * rotated * rotated
        normed = new_first / (jnp.sqrt(new_second) + EPSILON)
        high, low = split(normed)
        piece = width // CHUNKS
        updates = []
        for chunk in range(CHUNKS):

            def part(distance):
                rows = lax.dynamic_slice_in_dim(
                    right_cols, (me ^ distance) * width + chunk * piece, piece, 0
                )
                return dot(high, rows, ((1,), (1,))) + dot(low, rows, ((1,), (1,)))

            s_high, s_low = split(scatter_col(part))
            product = dot(left_cols, s_high, ((1,), (0,))) + dot(left_cols, s_low, ((1,), (0,)))
            updates.append(lax.psum_scatter(product, "row", scatter_dimension=0, tiled=True))
        return (new_first, new_second, jnp.concatenate(updates, axis=1))

    return local


def solution(mesh):
    return jax.shard_map(
        build(mesh.shape["col"]),
        mesh=mesh,
        in_specs=(
            P(("groups", "row"), "col"),
            P(("groups", "row"), "col"),
            P(("groups", "row"), "col"),
            P(("groups", "col"), "row"),
            P(("groups", "row"), "col"),
        ),
        out_specs=(
            P(("groups", "row"), "col"),
            P(("groups", "row"), "col"),
            P(("groups", "row"), "col"),
        ),
        check_vma=False,
    )
```

time: 1020 us -> 740 us (0.73); the launches traced: 1020 us -> 730 us
  waiting for transfers between devices: 862 us -> 472 us
  matrix products: 139 us -> 178 us
  local copies, waits for them, and re-layouts: 8.72 us -> 37.8 us
  starting transfers between devices: 0.24 us -> 15.6 us
  other arithmetic: 0 us -> 12.7 us
    reduce_scatter x2 -> x4, waiting for transfers between devices: 407 us -> 150 us  [local(): lax.psum_scatter(product, 'row', scatter_dimension=0, tiled=True)]
    all_gather x3 -> x1, waiting for transfers between devices: 317 us -> 89.3 us  [local(): grad_cols = lax.all_gather(gradient, 'row', axis=0, tiled=True)]
    ppermute x0 -> x21, waiting for transfers between devices: none -> 204 us  [swap(): return lax.ppermute(value, 'col', [(i, i ^ distance) for i in range(cols)])]
    all_gather x1, waiting for transfers between devices: 136 us -> 26.9 us  [local(): right_cols = lax.all_gather(right_basis, 'row', axis=0, tiled=True)]
    dot_general x4 -> x43, matrix products: 139 us -> 178 us  [dot(): return lax.dot_general(a, b, (dims, ((), ())), preferred_element_type=F32)]
    dynamic_update_slice x0 -> x10, local copies, waits for them, and re-layouts: none -> 27.9 us  [gather_col(): out = lax.dynamic_update_index_in_dim(out, value, me ^ distance, 0)]
    ppermute x0 -> x21, starting transfers between devices: none -> 14.8 us  [swap(): return lax.ppermute(value, 'col', [(i, i ^ distance) for i in range(cols)])]
  transfers between devices with their start and end apart: 6 -> 27, of which waited for: 6 -> 11; matrix products, arithmetic and copies ran while one was open for 1% -> 25% of each run, Pallas kernels for 0% -> 0%
where the time goes in v1:
time: 740 us; the launch traced here: 730 us
  waiting for transfers between devices  472 us (64%)
  matrix products  178 us (24%)
  local copies, waits for them, and re-layouts  37.8 us (5%)
  starting transfers between devices  15.6 us (2%)
  between operations  15 us (2%)
  other arithmetic  12.7 us (2%)
    ppermute x21, waiting for transfers between devices, swap(): return lax.ppermute(value, 'col', [(i, i ^ distance) for i in range(cols)])  204 us
    dot_general x43, matrix products, dot(): return lax.dot_general(a, b, (dims, ((), ())), preferred_element_type=F32)  178 us
    reduce_scatter x4, waiting for transfers between devices, local(): lax.psum_scatter(product, 'row', scatter_dimension=0, tiled=True)  150 us
    all_gather x1, waiting for transfers between devices, local(): grad_cols = lax.all_gather(gradient, 'row', axis=0, tiled=True)  89.3 us
    dynamic_update_slice x10, local copies, waits for them, and re-layouts, gather_col(): out = lax.dynamic_update_index_in_dim(out, value, me ^ distance, 0)  27.9 us
    all_gather x1, waiting for transfers between devices, local(): right_cols = lax.all_gather(right_basis, 'row', axis=0, tiled=True)  26.9 us
  transfers between devices with their start and end apart: 27, of which 11 were waited for; matrix products, arithmetic and copies ran while one was open for 25% of the time, Pallas kernels for 0%

profile of v1, /device:TPU:0, one launch (start us, length us, event | category | flops | bytes accessed | tf_op | source)
XLA Modules:
  0.0 730.3 jit_solution(1968491915082035800)
XLA Ops:
  8.8 3.0 collective-permute-start
  11.7 45.7 %collective-permute-done = bf16[1024,1024]{1,0:T(8,128)(2,1)} collective-permute-done((bf16[1024,1024]{1,0:T(8,128)(2,1)S(1)}, bf16[1024,1024]{1,0:T(8,128)(2,1)}, u32[]{:S(2)}, u32[]{:S(2)}) %collective-permute-start) | collective-permute-done | bytes 2097184 | tf_op jit(solution)/shard_map/ppermute | solution.py:25
  57.5 4.3 broadcast.3.clone.1
  63.3 3.1 bitcast_dynamic-update-slice_fusion.10
  66.4 3.1 bitcast_dynamic-update-slice_fusion.9
  69.5 3.1 bitcast_dynamic-update-slice_fusion.8
  72.6 89.3 %all-gather.3.cloned.1.call-done = bf16[4096,1024]{1,0:T(8,128)(2,1)} async-done(((bf16[1024,1024]{1,0:T(8,128)(2,1)}), bf16[4096,1024]{1,0:T(8,128)(2,1)}) %all-gather.3.cloned.1.call-update) | async-done | bytes 8388624 | tf_op jit(solution)/shard_map/all_gather | solution.py:51
  163.0 14.7 %bitcast_dynamic-update-slice_fusion.7 = (bf16[4,1024,1024]{2,1,0:T(8,128)(2,1)S(1)}, bf16[1024,1024]{1,0:T(8,128)(2,1)}, f32[1024,1024]{1,0:T(8,128)S(1)}) fusion(bf16[4,1024,1024]{2,1,0:T(8,128)(2,1)S(1)} %broadcast.3.clone, s32[]{:T(128)S(6)} %select_n.69, bf16[4096,1024]{1,0:T(8,128)(2,1)} %bitcast.4, bf16[4096,1024]{1,0:T(8,128)(2,1)} %all-gather.3.cloned.1.call-done), kind=kOutput, calls=%fused_computation.23 | convolution fusion | flops 8592031744 | bytes 25165828 | tf_op jit(solution)/shard_map/dot_general | solution.py:20
  179.2 4.4 broadcast.3
  183.6 3.0 bitcast_dynamic-update-slice_fusion.3
  188.5 37.9 %collective-permute-done.3 = bf16[1024,1024]{1,0:T(8,128)(2,1)S(1)} collective-permute-done((bf16[1024,1024]{1,0:T(8,128)(2,1)}, bf16[1024,1024]{1,0:T(8,128)(2,1)S(1)}, u32[]{:S(2)}, u32[]{:S(2)}) %collective-permute-start.3) | collective-permute-done | bytes 2097184 | tf_op jit(solution)/shard_map/ppermute | solution.py:25
  226.4 44.1 %collective-permute-done.6 = bf16[1024,1024]{1,0:T(8,128)(2,1)} collective-permute-done((bf16[1024,1024]{1,0:T(8,128)(2,1)}, bf16[1024,1024]{1,0:T(8,128)(2,1)}, u32[]{:S(2)}, u32[]{:S(2)}) %collective-permute-start.6) | collective-permute-done | bytes 2097184 | tf_op jit(solution)/shard_map/ppermute | solution.py:25
  272.1 3.1 bitcast_dynamic-update-slice_fusion.2
  275.2 3.1 bitcast_dynamic-update-slice_fusion.5
  278.3 3.1 bitcast_dynamic-update-slice_fusion.1
  281.4 3.1 bitcast_dynamic-update-slice_fusion.4
  284.5 26.9 %all-gather.5.cloned.1.call-done = bf16[4096,1024]{1,0:T(8,128)(2,1)} async-done(((bf16[1024,1024]{1,0:T(8,128)(2,1)}), bf16[4096,1024]{1,0:T(8,128)(2,1)}) %all-gather.5.cloned.1.call-update) | async-done | bytes 8388624 | tf_op jit(solution)/shard_map/all_gather | solution.py:54
  311.4 15.1 %fusion.113 = f32[1024,1024,1]{1,0,2:T(8,128)} fusion(bf16[4,1024,1024]{2,1,0:T(8,128)(2,1)} %bitcast_dynamic-update-slice_fusion.4, bf16[4,1024,1024]{2,1,0:T(8,128)(2,1)} %bitcast.76), kind=kOutput, calls=%fused_computation.156 | convolution fusion | flops 8589934592 | bytes 20971520 | tf_op jit(solution)/shard_map/dot_general | solution.py:20
  326.5 3.2 bitcast_dynamic-update-slice_fusion
  329.7 17.8 %fusion.1 = (bf16[1024,1024]{1,0:T(8,128)(2,1)S(1)}, f32[1024,1024]{1,0:T(8,128)}, f32[1024,1024]{1,0:T(8,128)}) fusion(f32[1024,1024]{1,0:T(8,128)} %param.7, f32[1024,1024]{1,0:T(8,128)} %param.6, bf16[4,1024,1024]{2,1,0:T(8,128)(2,1)} %bitcast_dynamic-update-slice_fusion, bf16[4,1024,1024]{2,1,0:T(8,128)(2,1)S(1)} %bitcast.77, f32[1024,1024,1]{1,0,2:T(8,128)} %fusion.113), kind=kOutput, calls=%fused_computation.10 | convolution fusion | flops 8603566080 | bytes 39845888 | tf_op jit(solution)/shard_map/dot_general | solution.py:20
  347.5 4.9 reduce-precision_convert_fusion
  354.0 2.4 fusion.71
  356.5 2.9 convolution_add_fusion.17
  361.7 3.1 fusion.10
  366.2 2.4 fusion.68
  368.6 2.2 fusion.9
  370.8 19.3 %collective-permute-done.10 = f32[1024,256]{1,0:T(8,128)S(1)} collective-permute-done((f32[1024,256]{1,0:T(8,128)}, f32[1024,256]{1,0:T(8,128)S(1)}, u32[]{:S(2)}, u32[]{:S(2)}) %collective-permute-start.10) | collective-permute-done | bytes 1048608 | tf_op jit(solution)/shard_map/ppermute | solution.py:25
  390.1 5.8 fusion.21
  395.9 8.1 %convolution_add_fusion.3 = f32[4096,256]{1,0:T(8,128)} fusion(f32[4096,256]{1,0:T(8,128)S(1)} %fusion.21, bf16[4096,1024]{1,0:T(8,128)(2,1)} %bitcast.4, f32[1024,256]{1,0:T(8,128)S(1)} %collective-permute-done.10, f32[1024,256]{1,0:T(8,128)S(1)} %fusion.9), kind=kOutput, calls=%fused_computation.8 | convolution fusion | flops 2149318656 | bytes 18874368 | tf_op jit(solution)/shard_map/dot_general | solution.py:20
  404.3 2.4 fusion.65
  406.7 1.8 convolution_add_fusion.15
  408.6 2.6 fusion.59
  411.2 3.0 convolution_add_fusion.13
  414.6 1.8 fusion.62
  416.4 3.1 fusion.8
  421.1 2.4 fusion.56
  423.5 2.2 fusion.7
  425.7 19.2 %collective-permute-done.13 = f32[1024,256]{1,0:T(8,128)S(1)} collective-permute-done((f32[1024,256]{1,0:T(8,128)}, f32[1024,256]{1,0:T(8,128)S(1)}, u32[]{:S(2)}, u32[]{:S(2)}) %collective-permute-start.13) | collective-permute-done | bytes 1048608 | tf_op jit(solution)/shard_map/ppermute | solution.py:25
  444.9 5.8 fusion.19
  450.8 8.0 %convolution_add_fusion.2 = f32[4096,256]{1,0:T(8,128)} fusion(f32[4096,256]{1,0:T(8,128)S(1)} %fusion.19, bf16[4096,1024]{1,0:T(8,128)(2,1)} %bitcast.4, f32[1024,256]{1,0:T(8,128)S(1)} %collective-permute-done.13, f32[1024,256]{1,0:T(8,128)S(1)} %fusion.7), kind=kOutput, calls=%fused_computation.7 | convolution fusion | flops 2149318656 | bytes 18874368 | tf_op jit(solution)/shard_map/dot_general | solution.py:20
  459.0 2.4 fusion.53
  461.5 1.8 convolution_add_fusion.11
  463.4 2.4 fusion.47
  465.8 2.9 convolution_add_fusion.9
  471.0 3.2 fusion.6
  475.9 2.4 fusion.44
  478.3 2.3 fusion.5
  480.6 19.0 %collective-permute-done.16 = f32[1024,256]{1,0:T(8,128)S(1)} collective-permute-done((f32[1024,256]{1,0:T(8,128)}, f32[1024,256]{1,0:T(8,128)S(1)}, u32[]{:S(2)}, u32[]{:S(2)}) %collective-permute-start.16) | collective-permute-done | bytes 1048608 | tf_op jit(solution)/shard_map/ppermute | solution.py:25
  499.5 5.8 fusion.17
  505.4 8.1 %convolution_add_fusion.1 = f32[4096,256]{1,0:T(8,128)} fusion(f32[4096,256]{1,0:T(8,128)S(1)} %fusion.17, bf16[4096,1024]{1,0:T(8,128)(2,1)} %bitcast.4, f32[1024,256]{1,0:T(8,128)S(1)} %collective-permute-done.16, f32[1024,256]{1,0:T(8,128)S(1)} %fusion.5), kind=kOutput, calls=%fused_computation.6 | convolution fusion | flops 2149318656 | bytes 18874368 | tf_op jit(solution)/shard_map/dot_general | solution.py:20
  513.8 2.4 fusion.41
  516.2 2.8 convolution_add_fusion.7
  519.0 2.4 fusion.35
  521.4 1.9 convolution_add_fusion.5
  524.0 1.8 fusion.38
  525.8 3.1 fusion.4
  530.6 2.4 fusion.32
  533.0 2.2 fusion.3
  535.2 19.1 %collective-permute-done.19 = f32[1024,256]{1,0:T(8,128)} collective-permute-done((f32[1024,256]{1,0:T(8,128)}, f32[1024,256]{1,0:T(8,128)}, u32[]{:S(2)}, u32[]{:S(2)}) %collective-permute-start.19) | collective-permute-done | bytes 1048608 | tf_op jit(solution)/shard_map/ppermute | solution.py:25
  554.3 6.0 fusion.15
  560.3 8.3 %convolution_add_fusion = f32[4096,256]{1,0:T(8,128)} fusion(f32[4096,256]{1,0:T(8,128)S(1)} %fusion.15, bf16[4096,1024]{1,0:T(8,128)(2,1)} %bitcast.4, f32[1024,256]{1,0:T(8,128)} %collective-permute-done.19, f32[1024,256]{1,0:T(8,128)S(1)} %fusion.3), kind=kOutput, calls=%fused_computation.5 | convolution fusion | flops 2149318656 | bytes 18874368 | tf_op jit(solution)/shard_map/dot_general | solution.py:20
  568.7 69.4 %reduce-scatter.9.cloned.1.call-done = f32[1024,256]{1,0:T(8,128)} async-done(((f32[4096,256]{1,0:T(8,128)}), f32[1024,256]{1,0:T(8,128)}) %reduce-scatter.9.cloned.1.call-update) | async-done | bytes 1048592 | tf_op jit(solution)/shard_map/reduce_scatter | solution.py:76
  638.1 80.1 %reduce-scatter.11.cloned.1.call-done = f32[1024,256]{1,0:T(8,128)} async-done(((f32[4096,256]{1,0:T(8,128)}), f32[1024,256]{1,0:T(8,128)}) %reduce-scatter.11.cloned.1.call-update) | async-done | bytes 1048592 | tf_op jit(solution)/shard_map/reduce_scatter | solution.py:76
  718.2 4.8 pad_maximum_fusion
  (71 shorter events, 23.4 us)
Async XLA Ops:
  7.2 1.6 copy-start.7
  7.2 154.8 %all-gather.3.cloned.1.call-start = ((), (), s32[]{:S(2)}) async-start(), calls=%async_computation.4 | async-start | bytes 10485760 | tf_op jit(solution)/shard_map/all_gather | solution.py:51
  7.9 303.5 %all-gather.5.cloned.1.call-start = ((), (), s32[]{:S(2)}) async-start(), calls=%async_computation.5 | async-start | bytes 10485760 | tf_op jit(solution)/shard_map/all_gather | solution.py:54
  8.7 560.1 %reduce-scatter.5.cloned.1.call-start = ((), (), s32[]{:S(2)}) async-start(), calls=%async_computation.6 | async-start | bytes 5242880 | tf_op jit(solution)/shard_map/reduce_scatter | solution.py:76
  8.8 48.7 %collective-permute-start = (bf16[1024,1024]{1,0:T(8,128)(2,1)S(1)}, bf16[1024,1024]{1,0:T(8,128)(2,1)}, u32[]{:S(2)}, u32[]{:S(2)}) collective-permute-start(bf16[1024,1024]{1,0:T(8,128)(2,1)S(1)} %copy-done.7), channel_id=1, source_target_pairs={{0,2},{1,3},{2,0},{3,1},{4,6},{5,7},{6,4},{7,5},{8,10},{9,11},{10,... | collective-permute-start | bytes 6291464 | tf_op jit(solution)/shard_map/ppermute | solution.py:25
  11.7 54.7 %collective-permute-start.1 = (bf16[1024,1024]{1,0:T(8,128)(2,1)S(1)}, bf16[1024,1024]{1,0:T(8,128)(2,1)}, u32[]{:S(2)}, u32[]{:S(2)}) collective-permute-start(bf16[1024,1024]{1,0:T(8,128)(2,1)S(1)} %copy-done.7), channel_id=1, source_target_pairs={{0,1},{1,0},{2,3},{3,2},{4,5},{5,4},{6,7},{7,6},{8,9},{9,8},{10,11... | collective-permute-start | bytes 6291464 | tf_op jit(solution)/shard_map/ppermute | solution.py:25
  57.5 12.1 %collective-permute-start.2 = (bf16[1024,1024]{1,0:T(8,128)(2,1)}, bf16[1024,1024]{1,0:T(8,128)(2,1)}, u32[]{:S(2)}, u32[]{:S(2)}) collective-permute-start(bf16[1024,1024]{1,0:T(8,128)(2,1)} %collective-permute-done), channel_id=1, source_target_pairs={{0,1},{1,0},{2,3},{3,2},{4,5},{5,4},{6,7},{7,6},{8,9},{9,8},{10,11... | collective-permute-start | bytes 6291464 | tf_op jit(solution)/shard_map/ppermute | solution.py:25
  177.7 5.9 copy-start.1
  177.7 48.7 %collective-permute-start.3 = (bf16[1024,1024]{1,0:T(8,128)(2,1)}, bf16[1024,1024]{1,0:T(8,128)(2,1)S(1)}, u32[]{:S(2)}, u32[]{:S(2)}) collective-permute-start(bf16[1024,1024]{1,0:T(8,128)(2,1)} %get-tuple-element.9), channel_id=1, source_target_pairs={{0,2},{1,3},{2,0},{3,1},{4,6},{5,7},{6,4},{7,5},{8,10},{9,11},{10,... | collective-permute-start | bytes 6291464 | tf_op jit(solution)/shard_map/ppermute | solution.py:25
  186.6 83.9 %collective-permute-start.6 = (bf16[1024,1024]{1,0:T(8,128)(2,1)}, bf16[1024,1024]{1,0:T(8,128)(2,1)}, u32[]{:S(2)}, u32[]{:S(2)}) collective-permute-start(bf16[1024,1024]{1,0:T(8,128)(2,1)} %get-tuple-element.7), channel_id=1, source_target_pairs={{0,2},{1,3},{2,0},{3,1},{4,6},{5,7},{6,4},{7,5},{8,10},{9,11},{10,... | collective-permute-start | bytes 6291464 | tf_op jit(solution)/shard_map/ppermute | solution.py:25
  188.0 87.2 %collective-permute-start.4 = (bf16[1024,1024]{1,0:T(8,128)(2,1)}, bf16[1024,1024]{1,0:T(8,128)(2,1)}, u32[]{:S(2)}, u32[]{:S(2)}) collective-permute-start(bf16[1024,1024]{1,0:T(8,128)(2,1)} %get-tuple-element.9), channel_id=1, source_target_pairs={{0,1},{1,0},{2,3},{3,2},{4,5},{5,4},{6,7},{7,6},{8,9},{9,8},{10,11... | collective-permute-start | bytes 6291464 | tf_op jit(solution)/shard_map/ppermute | solution.py:25
  188.0 90.3 %collective-permute-start.7 = (bf16[1024,1024]{1,0:T(8,128)(2,1)}, bf16[1024,1024]{1,0:T(8,128)(2,1)}, u32[]{:S(2)}, u32[]{:S(2)}) collective-permute-start(bf16[1024,1024]{1,0:T(8,128)(2,1)} %get-tuple-element.7), channel_id=1, source_target_pairs={{0,1},{1,0},{2,3},{3,2},{4,5},{5,4},{6,7},{7,6},{8,9},{9,8},{10,11... | collective-permute-start | bytes 6291464 | tf_op jit(solution)/shard_map/ppermute | solution.py:25
  226.4 55.0 %collective-permute-start.5 = (bf16[1024,1024]{1,0:T(8,128)(2,1)S(1)}, bf16[1024,1024]{1,0:T(8,128)(2,1)}, u32[]{:S(2)}, u32[]{:S(2)}) collective-permute-start(bf16[1024,1024]{1,0:T(8,128)(2,1)S(1)} %collective-permute-done.3), channel_id=1, source_target_pairs={{0,1},{1,0},{2,3},{3,2},{4,5},{5,4},{6,7},{7,6},{8,9},{9,8},{10,11... | collective-permute-start | bytes 6291464 | tf_op jit(solution)/shard_map/ppermute | solution.py:25
  270.6 55.9 %collective-permute-start.8 = (bf16[1024,1024]{1,0:T(8,128)(2,1)}, bf16[1024,1024]{1,0:T(8,128)(2,1)}, u32[]{:S(2)}, u32[]{:S(2)}) collective-permute-start(bf16[1024,1024]{1,0:T(8,128)(2,1)} %collective-permute-done.6), channel_id=1, source_target_pairs={{0,1},{1,0},{2,3},{3,2},{4,5},{5,4},{6,7},{7,6},{8,9},{9,8},{10,11... | collective-permute-start | bytes 6291464 | tf_op jit(solution)/shard_map/ppermute | solution.py:25
  311.4 18.2 %copy-start = (bf16[4096,1024]{1,0:T(8,128)(2,1)S(1)}, bf16[4096,1024]{1,0:T(8,128)(2,1)}, u32[]{:S(2)}) copy-start(bf16[4096,1024]{1,0:T(8,128)(2,1)} %all-gather.5.cloned.1.call-done) | copy-start | bytes 25165828
  352.4 1.5 copy-start.2
  353.9 7.7 %collective-permute-start.9 = (f32[1024,256]{1,0:T(8,128)S(1)}, f32[1024,256]{1,0:T(8,128)}, u32[]{:S(2)}, u32[]{:S(2)}) collective-permute-start(f32[1024,256]{1,0:T(8,128)S(1)} %convolution_add_fusion.19), channel_id=1, source_target_pairs={{0,1},{1,0},{2,3},{3,2},{4,5},{5,4},{6,7},{7,6},{8,9},{9,8},{10,11... | collective-permute-start | bytes 3145736 | tf_op jit(solution)/shard_map/ppermute | solution.py:25
  356.5 3.4 copy-start.3
  359.4 9.2 %collective-permute-start.11 = (f32[1024,256]{1,0:T(8,128)}, f32[1024,256]{1,0:T(8,128)}, u32[]{:S(2)}, u32[]{:S(2)}) collective-permute-start(f32[1024,256]{1,0:T(8,128)} %convolution_add_fusion.17), channel_id=1, source_target_pairs={{0,1},{1,0},{2,3},{3,2},{4,5},{5,4},{6,7},{7,6},{8,9},{9,8},{10,11... | collective-permute-start | bytes 3145736 | tf_op jit(solution)/shard_map/ppermute | solution.py:25
  364.8 25.3 %collective-permute-start.10 = (f32[1024,256]{1,0:T(8,128)}, f32[1024,256]{1,0:T(8,128)S(1)}, u32[]{:S(2)}, u32[]{:S(2)}) collective-permute-start(f32[1024,256]{1,0:T(8,128)} %fusion.10), channel_id=1, source_target_pairs={{0,2},{1,3},{2,0},{3,1},{4,6},{5,7},{6,4},{7,5},{8,10},{9,11},{10,... | collective-permute-start | bytes 3145736 | tf_op jit(solution)/shard_map/ppermute | solution.py:25
  404.0 164.7 %reduce-scatter.7.cloned.1.call-start = ((), (), s32[]{:S(2)}) async-start(), calls=%async_computation.7 | async-start | bytes 5242880 | tf_op jit(solution)/shard_map/reduce_scatter | solution.py:76
  408.5 7.9 %collective-permute-start.12 = (f32[1024,256]{1,0:T(8,128)S(1)}, f32[1024,256]{1,0:T(8,128)}, u32[]{:S(2)}, u32[]{:S(2)}) collective-permute-start(f32[1024,256]{1,0:T(8,128)S(1)} %convolution_add_fusion.15), channel_id=1, source_target_pairs={{0,1},{1,0},{2,3},{3,2},{4,5},{5,4},{6,7},{7,6},{8,9},{9,8},{10,11... | collective-permute-start | bytes 3145736 | tf_op jit(solution)/shard_map/ppermute | solution.py:25
  411.2 3.4 copy-start.4
  414.2 9.3 %collective-permute-start.14 = (f32[1024,256]{1,0:T(8,128)}, f32[1024,256]{1,0:T(8,128)}, u32[]{:S(2)}, u32[]{:S(2)}) collective-permute-start(f32[1024,256]{1,0:T(8,128)} %convolution_add_fusion.13), channel_id=1, source_target_pairs={{0,1},{1,0},{2,3},{3,2},{4,5},{5,4},{6,7},{7,6},{8,9},{9,8},{10,11... | collective-permute-start | bytes 3145736 | tf_op jit(solution)/shard_map/ppermute | solution.py:25
  419.5 25.4 %collective-permute-start.13 = (f32[1024,256]{1,0:T(8,128)}, f32[1024,256]{1,0:T(8,128)S(1)}, u32[]{:S(2)}, u32[]{:S(2)}) collective-permute-start(f32[1024,256]{1,0:T(8,128)} %fusion.8), channel_id=1, source_target_pairs={{0,2},{1,3},{2,0},{3,1},{4,6},{5,7},{6,4},{7,5},{8,10},{9,11},{10,... | collective-permute-start | bytes 3145736 | tf_op jit(solution)/shard_map/ppermute | solution.py:25
  458.8 179.3 %reduce-scatter.9.cloned.1.call-start = ((), (), s32[]{:S(2)}) async-start(), calls=%async_computation.8 | async-start | bytes 5242880 | tf_op jit(solution)/shard_map/reduce_scatter | solution.py:76
  463.3 7.7 %collective-permute-start.15 = (f32[1024,256]{1,0:T(8,128)S(1)}, f32[1024,256]{1,0:T(8,128)}, u32[]{:S(2)}, u32[]{:S(2)}) collective-permute-start(f32[1024,256]{1,0:T(8,128)S(1)} %convolution_add_fusion.11), channel_id=1, source_target_pairs={{0,1},{1,0},{2,3},{3,2},{4,5},{5,4},{6,7},{7,6},{8,9},{9,8},{10,11... | collective-permute-start | bytes 3145736 | tf_op jit(solution)/shard_map/ppermute | solution.py:25
  465.8 3.4 copy-start.5
  468.7 9.6 %collective-permute-start.17 = (f32[1024,256]{1,0:T(8,128)}, f32[1024,256]{1,0:T(8,128)}, u32[]{:S(2)}, u32[]{:S(2)}) collective-permute-start(f32[1024,256]{1,0:T(8,128)} %convolution_add_fusion.9), channel_id=1, source_target_pairs={{0,1},{1,0},{2,3},{3,2},{4,5},{5,4},{6,7},{7,6},{8,9},{9,8},{10,11... | collective-permute-start | bytes 3145736 | tf_op jit(solution)/shard_map/ppermute | solution.py:25
  474.2 25.3 %collective-permute-start.16 = (f32[1024,256]{1,0:T(8,128)}, f32[1024,256]{1,0:T(8,128)S(1)}, u32[]{:S(2)}, u32[]{:S(2)}) collective-permute-start(f32[1024,256]{1,0:T(8,128)} %fusion.6), channel_id=1, source_target_pairs={{0,2},{1,3},{2,0},{3,1},{4,6},{5,7},{6,4},{7,5},{8,10},{9,11},{10,... | collective-permute-start | bytes 3145736 | tf_op jit(solution)/shard_map/ppermute | solution.py:25
  513.5 204.8 %reduce-scatter.11.cloned.1.call-start = ((), (), s32[]{:S(2)}) async-start(), calls=%async_computation.9 | async-start | bytes 5242880 | tf_op jit(solution)/shard_map/reduce_scatter | solution.py:76
  519.0 6.8 collective-permute-start.18
  521.4 2.5 copy-start.6
  523.4 9.6 %collective-permute-start.20 = (f32[1024,256]{1,0:T(8,128)S(1)}, f32[1024,256]{1,0:T(8,128)}, u32[]{:S(2)}, u32[]{:S(2)}) collective-permute-start(f32[1024,256]{1,0:T(8,128)S(1)} %convolution_add_fusion.5), channel_id=1, source_target_pairs={{0,1},{1,0},{2,3},{3,2},{4,5},{5,4},{6,7},{7,6},{8,9},{9,8},{10,11... | collective-permute-start | bytes 3145736 | tf_op jit(solution)/shard_map/ppermute | solution.py:25
  528.9 25.4 %collective-permute-start.19 = (f32[1024,256]{1,0:T(8,128)}, f32[1024,256]{1,0:T(8,128)}, u32[]{:S(2)}, u32[]{:S(2)}) collective-permute-start(f32[1024,256]{1,0:T(8,128)} %fusion.4), channel_id=1, source_target_pairs={{0,2},{1,3},{2,0},{3,1},{4,6},{5,7},{6,4},{7,5},{8,10},{9,11},{10,... | collective-permute-start | bytes 3145736 | tf_op jit(solution)/shard_map/ppermute | solution.py:25
Sparse Core Ops, SparseCore 0:
  9.6 152.3 all-gather.2
  163.5 147.8 all-gather.4
  404.2 74.9 reduce-scatter.4
  481.4 77.2 reduce-scatter.6
  560.8 77.2 reduce-scatter.8
  640.9 77.2 reduce-scatter.10

commit v2 on v1

v2 whole, which is shorter than its diff:
```python
import functools
import jax
import jax.numpy as jnp
from jax import lax
from jax.experimental import pallas as pl
from jax.experimental.pallas import tpu as pltpu
from jax.sharding import PartitionSpec as P

BETA_ONE = 0.9
BETA_TWO = 0.95
EPSILON = 1e-08
CHUNKS = 4
EXTRA = 16
F32 = jnp.float32
BF16 = jnp.bfloat16
MIB = 2**20


def params(mib):
    return pltpu.CompilerParams(vmem_limit_bytes=mib * MIB)


def cost(flops, moved):
    return pl.CostEstimate(flops=int(flops), bytes_accessed=int(moved), transcendentals=0)


def split(value):
    high = lax.reduce_precision(value, exponent_bits=8, mantissa_bits=7)
    return high.astype(BF16), (value - high).astype(BF16)


def kernel_split(value):
    high = value.astype(BF16)
    return high, (value - high.astype(F32)).astype(BF16)


def dot(a, b, dims):
    return lax.dot_general(a, b, (dims, ((), ())), preferred_element_type=F32)


def rotate_part_kernel(me_ref, *refs, cols, half):
    pieces, (right, out) = refs[:-2], refs[-2:]
    tile = out.shape[0]
    total = None
    for at, piece in enumerate(pieces):
        start = (me_ref[0] ^ (at // 2)) * (2 * half) + (at % 2) * half
        rows = right[pl.ds(pl.multiple_of(start, half), half), :]
        term = dot(piece[...].reshape(2 * tile, half), rows, ((1,), (0,)))
        total = term if total is None else total + term
    out[...] = total[:tile] + total[tile:]


def rotate_part(me, pieces, right):
    _, depth, half = pieces[0].shape
    cols = len(pieces) // 2
    width = right.shape[1]
    tile = min(256, depth)
    return pl.pallas_call(
        functools.partial(rotate_part_kernel, cols=cols, half=half),
        grid_spec=pltpu.PrefetchScalarGridSpec(
            num_scalar_prefetch=1,
            grid=(depth // tile,),
            in_specs=[pl.BlockSpec((2, tile, half), lambda i, s: (0, i, 0))] * len(pieces)
            + [pl.BlockSpec(right.shape, lambda i, s: (0, 0), pipeline_mode=pl.Buffered(1))],
            out_specs=pl.BlockSpec((tile, width), lambda i, s: (i, 0)),
        ),
        out_shape=jax.ShapeDtypeStruct((depth, width), F32),
        compiler_params=params(40),
        cost_estimate=cost(8 * depth * width * half * cols, 20 * depth * width),
        name="rotate_part",
    )(me, *pieces, right)


def rotate_kernel(place_ref, part, *refs, count):
    pieces, (above, below, first, second, new_first, new_second, normed) = (
        refs[:count],
        refs[count:],
    )
    tile = first.shape[0]
    half = pieces[0].shape[2]
    rotated = part[...]
    for at, piece in enumerate(pieces):
        rows = pl.ds(at * half, half)
        last = jnp.where(place_ref[0] == 0, above[rows, :], below[rows, :])
        both = dot(piece[...].reshape(2 * tile, half), last, ((1,), (0,)))
        rotated = rotated + both[:tile] + both[tile:]
    one = BETA_ONE * first[...] + (1.0 - BETA_ONE) * rotated
    two = BETA_TWO * second[...] + (1.0 - BETA_TWO) * rotated * rotated
    new_first[...] = one
    new_second[...] = two
    high, low = kernel_split(one / (jnp.sqrt(two) + EPSILON))
    normed[0] = high
    normed[1] = low


def rotate(place, part, pieces, above, below, first, second):
    depth, width = first.shape
    half = pieces[0].shape[2]
    tile = min(256, depth)
    block = pl.BlockSpec((tile, width), lambda i, s: (i, 0))
    pair = pl.BlockSpec((2, tile, width), lambda i, s: (0, i, 0))
    whole = pl.BlockSpec(above.shape, lambda i, s: (0, 0), pipeline_mode=pl.Buffered(1))
    return pl.pallas_call(
        functools.partial(rotate_kernel, count=len(pieces)),
        grid_spec=pltpu.PrefetchScalarGridSpec(
            num_scalar_prefetch=1,
            grid=(depth // tile,),
            in_specs=[block]
            + [pl.BlockSpec((2, tile, half), lambda i, s: (0, i, 0))] * len(pieces)
            + [whole, whole, block, block],
            out_specs=[block, block, pair],
        ),
        out_shape=[
            jax.ShapeDtypeStruct((depth, width), F32),
            jax.ShapeDtypeStruct((depth, width), F32),
            jax.ShapeDtypeStruct((2, depth, width), BF16),
        ],
        compiler_params=params(36),
        cost_estimate=cost(4 * depth * width * half * len(pieces), 30 * depth * width),
        name="rotate",
    )(place, part, *pieces, above, below, first, second)


def restore_kernel(me_ref, normed, *refs, cols):
    rows, (keep, mate) = refs[:cols], refs[cols:]
    tile = normed.shape[1]
    both = normed[...].reshape(2 * tile, normed.shape[2])
    for distance in range(cols):
        term = dot(both, rows[distance][...], ((1,), (1,)))
        (mate if distance % 2 else keep)[distance // 2] = term[:tile] + term[tile:]


def restore(me, normed, right, chunk, piece, cols, width):
    _, depth, inner = normed.shape
    tile = min(512, depth)
    per = width // piece

    def at(distance):
        return lambda i, s: ((s[0] ^ distance) * per + chunk, 0)

    out = pl.BlockSpec((cols // 2, tile, piece), lambda i, s: (0, i, 0))
    return pl.pallas_call(
        functools.partial(restore_kernel, cols=cols),
        grid_spec=pltpu.PrefetchScalarGridSpec(
            num_scalar_prefetch=1,
            grid=(depth // tile,),
            in_specs=[pl.BlockSpec((2, tile, inner), lambda i, s: (0, i, 0))]
            + [pl.BlockSpec((piece, inner), at(d)) for d in range(cols)],
            out_specs=[out, out],
        ),
        out_shape=[jax.ShapeDtypeStruct((cols // 2, depth, piece), F32)] * 2,
        compiler_params=params(36),
        cost_estimate=cost(4 * depth * inner * piece * cols, 8 * depth * piece * cols),
        name="restore",
    )(me, normed, *([right] * cols))


TOP = 7.5


def encode(value, inverse):
    code = jnp.abs(value) * (inverse * 2.0**TOP)
    for _ in range(4):
        code = code * code
    return jnp.where(value < 0, -code, code).astype(BF16)


def decode(code, scale):
    code = code.astype(F32)
    size = jnp.abs(code)
    root = jnp.exp2(jnp.log2(size) * 0.0625 - TOP) * scale
    root = jnp.where(size > 0, root, 0.0)
    return jnp.where(code < 0, -root, root)


def scale_of(message, depth):
    return jnp.max(message[depth : depth + EXTRA, :].astype(F32), axis=(0, 1), keepdims=True)


def send_kernel(*refs, terms, tile):
    parts, (message, own, total) = refs[:terms], refs[terms:]
    depth, piece = total.shape

    def add(i, top):
        rows = pl.ds(pl.multiple_of(i * tile, tile), tile)
        value = parts[0][rows, :]
        for part in parts[1:]:
            value = value + part[rows, :]
        total[rows, :] = value
        high, low = kernel_split(value)
        own[rows, :piece] = high
        own[rows, piece:] = low
        return jnp.maximum(top, jnp.abs(value))

    top = lax.fori_loop(0, depth // tile, add, jnp.zeros((tile, piece), F32))
    top = jnp.maximum(jnp.max(top, axis=(0, 1), keepdims=True), 1e-30)
    scale = jnp.broadcast_to(top, (EXTRA, piece)).astype(BF16)
    message[depth : depth + EXTRA, :] = scale
    inverse = 1.0 / jnp.max(scale.astype(F32), axis=(0, 1), keepdims=True)

    def put(i, carry):
        rows = pl.ds(pl.multiple_of(i * tile, tile), tile)
        message[rows, :] = encode(total[rows, :], inverse)
        return carry

    lax.fori_loop(0, depth // tile, put, 0)


def send(parts):
    depth, piece = parts[0].shape
    tile = min(64, depth)
    return pl.pallas_call(
        functools.partial(send_kernel, terms=len(parts), tile=tile),
        out_shape=[
            jax.ShapeDtypeStruct((depth + EXTRA, piece), BF16),
            jax.ShapeDtypeStruct((depth, 2 * piece), BF16),
        ],
        scratch_shapes=[pltpu.VMEM((depth, piece), F32)],
        compiler_params=params(24),
        cost_estimate=cost(400 * depth * piece, 18 * depth * piece),
        name="send",
    )(*parts)


def update_kernel(place_ref, own, *refs, lines, tile):
    ups, downs = refs[: lines - 1], refs[lines - 1 : 2 * lines - 2]
    left, out, held = refs[2 * lines - 2], refs[-2], refs[-1]
    depth, piece = out.shape
    inner = held.shape[0]
    step = pl.program_id(0)

    @pl.when(step == 0)
    def _():
        held[...] = own[...]

    for back in range(1, lines):

        @pl.when(step == back)
        def _(back=back):
            up, down = ups[back - 1], downs[lines - back - 1]
            below = place_ref[0] >= back
            scale = jnp.where(below, scale_of(up, inner), scale_of(down, inner))

            def unpack(i, carry):
                rows = pl.ds(pl.multiple_of(i * tile, tile), tile)
                value = decode(jnp.where(below, up[rows, :], down[rows, :]), scale)
                high, low = kernel_split(value)
                held[rows, :piece] = high
                held[rows, piece:] = low
                return carry

            lax.fori_loop(0, inner // tile, unpack, 0)

    both = dot(left[...].reshape(depth, inner), held[...], ((1,), (0,)))
    term = both[:, :piece] + both[:, piece:]

    @pl.when(step == 0)
    def _():
        out[...] = term

    @pl.when(step > 0)
    def _():
        out[...] += term


def update_chunk(place, own, ups, downs, left, update, chunk, depth, width):
    cols, lines, quarter, inner = left.shape
    piece = own.shape[1] // 2
    tile = min(64, inner)
    message = pl.BlockSpec((inner + EXTRA, piece), lambda i, s: (0, 0))
    extra = [] if update is None else [update]
    return pl.pallas_call(
        functools.partial(update_kernel, lines=lines, tile=tile),
        grid_spec=pltpu.PrefetchScalarGridSpec(
            num_scalar_prefetch=1,
            grid=(lines,),
            in_specs=[pl.BlockSpec((inner, 2 * piece), lambda i, s: (0, 0))]
            + [message] * (2 * lines - 2)
            + [pl.BlockSpec((cols, 1, quarter, inner), lambda i, s: (0, i, 0, 0))]
            + [pl.BlockSpec(memory_space=pl.ANY)] * len(extra),
            out_specs=pl.BlockSpec((depth, piece), lambda i, s: (0, chunk)),
            scratch_shapes=[pltpu.VMEM((inner, 2 * piece), BF16)],
        ),
        out_shape=jax.ShapeDtypeStruct((depth, width), F32),
        input_output_aliases={2 * lines + 1: 0} if extra else {},
        compiler_params=params(36),
        cost_estimate=cost(4 * depth * inner * piece * lines, 12 * depth * piece * lines),
        name="update_chunk",
    )(place, own, *ups, *downs, left, *extra)


def build(lines, cols):
    def swap(value, distance):
        return lax.ppermute(value, "col", [(i, i ^ distance) for i in range(cols)])

    def up(value, senders):
        return lax.ppermute(value, "row", [(i, i + 1) for i in senders])

    def down(value, senders):
        return lax.ppermute(value, "row", [(i, i - 1) for i in senders])

    def spread(block):
        held = {0: block}
        for step in range(1, lines):
            held[-step] = up(held[1 - step], range(step - 1, lines - 1))
            held[step] = down(held[step - 1], range(1, lines - step + 1))
        return held

    def by_distance(block):
        held = {0: block}
        for distance in range(2, cols, 2):
            held[distance] = swap(block, distance)
        for distance in range(0, cols, 2):
            held[distance + 1] = swap(held[distance], 1)
        return held

    def place_by_distance(block, me):
        out = jnp.zeros((cols,) + block.shape, block.dtype)
        for distance, value in by_distance(block).items():
            out = lax.dynamic_update_index_in_dim(out, value, me ^ distance, 0)
        return out

    def local(gradient, first_moment, second_moment, left_basis, right_basis):
        me, place = lax.axis_index("col"), lax.axis_index("row")
        depth, width = gradient.shape
        half = width // 2
        index, spot = jnp.reshape(me, (1,)), jnp.reshape(place, (1,))
        far = lines - 1

        left = place_by_distance(left_basis, me).reshape(-1, left_basis.shape[1])
        pieces = {}
        for side in range(2):
            grads = spread(gradient[:, side * half : (side + 1) * half])
            halfway = None
            for offset, value in grads.items():
                if abs(offset) == far:
                    continue
                rows = lax.dynamic_slice_in_dim(left, (place + offset) * depth, depth, 0)
                term = dot(rows, value, ((0,), (0,)))
                halfway = term if halfway is None else halfway + term
            rows = lax.dynamic_slice_in_dim(left, (far - place) * depth, depth, 0)
            last = jnp.where(place == 0, grads[far], grads[-far])
            halfway = halfway + dot(rows, last, ((0,), (0,)))
            for distance, value in by_distance(jnp.stack(split(halfway))).items():
                pieces[distance, side] = value

        right = jnp.zeros(((lines + 1) * depth, width), BF16)
        ends = []
        for side in range(2):
            rights = spread(lax.slice_in_dim(right_basis, side * depth // 2, (side + 1) * depth // 2))
            for offset, value in rights.items():
                if abs(offset) == far:
                    continue
                there = place + offset
                there = jnp.where((there >= 0) & (there < lines), there, lines)
                right = lax.dynamic_update_slice_in_dim(
                    right, value, there * depth + side * depth // 2, 0
                )
            ends.append((rights[far], rights[-far]))
        above = jnp.concatenate([end[0] for end in ends])
        below = jnp.concatenate([end[1] for end in ends])

        ordered = [pieces[distance, side] for distance in range(cols) for side in range(2)]
        part = rotate_part(index, ordered, right)
        span = depth // half
        lasts = []
        for at in range(span):
            chosen = None
            for distance in range(cols):
                for side in [at] if span == 2 else range(2):
                    value = pieces[distance, side]
                    here = (me ^ distance) * 2 + side == (far - place) * span + at
                    chosen = value if chosen is None else jnp.where(here, value, chosen)
            lasts.append(chosen)
        new_first, new_second, normed = rotate(
            spot, part, lasts, above, below, first_moment, second_moment
        )
        there = jnp.where((place == 0) | (place == far), far - place, lines)
        last = jnp.where(place == 0, above, below)
        right = lax.dynamic_update_slice_in_dim(right, last, there * depth, 0)

        left_late, last = lax.optimization_barrier((left, last))
        quarter = depth // cols
        backs = []
        for back in range(lines):
            to = lax.rem(place + back, lines)
            rows = lax.dynamic_slice_in_dim(left_late, to * depth + me * quarter, quarter, 0)
            if back:
                rows = lax.ppermute(rows, "row", [(i, (i + back) % lines) for i in range(lines)])
            backs.append(rows)
        left_rows = place_by_distance(jnp.stack(backs), me)

        piece = width // CHUNKS
        update = None
        sums = []
        for chunk in range(CHUNKS):
            if chunk >= 2:
                normed, sums[chunk - 2] = lax.optimization_barrier((normed, sums[chunk - 2]))
            keep, mate = restore(index, normed, right, chunk, piece, cols, width)
            mate = swap(mate, 1)
            sums.append((keep, mate))
            if cols > 2:
                sums[chunk] = (keep, mate, [keep[d] + mate[d] for d in range(1, cols // 2)])
        for chunk in range(CHUNKS):
            keep, mate = sums[chunk][:2]
            parts = [keep[0], mate[0]]
            for at, value in enumerate(sums[chunk][2] if cols > 2 else []):
                parts.append(swap(value, 2 * at + 2))
            message, own = send(parts)
            arrived = spread(message)
            ups = [arrived[-step] for step in range(1, lines)]
            downs = [arrived[step] for step in range(1, lines)]
            update = update_chunk(
                spot, own, ups, downs, left_rows, update, chunk, depth, width
            )
        return (new_first, new_second, update)

    return local


def solution(mesh):
    return jax.shard_map(
        build(mesh.shape["row"], mesh.shape["col"]),
        mesh=mesh,
        in_specs=(
            P(("groups", "row"), "col"),
            P(("groups", "row"), "col"),
            P(("groups", "row"), "col"),
            P(("groups", "col"), "row"),
            P(("groups", "row"), "col"),
        ),
        out_specs=(
            P(("groups", "row"), "col"),
            P(("groups", "row"), "col"),
            P(("groups", "row"), "col"),
        ),
        check_vma=False,
    )
```

time: 740 us -> 723 us (0.977)
  matrix products: 178 us -> 37.5 us
  starting transfers between devices: 15.6 us -> 137 us
  Pallas kernels: 0 us -> 108 us
  waiting for transfers between devices: 472 us -> 367 us
  between operations: 15 us -> 1.96 us
  local copies, waits for them, and re-layouts: 37.8 us -> 46 us
    ppermute x0 -> x51, waiting for transfers between devices: none -> 242 us  [the longest x24 198 us: down(): return lax.ppermute(value, 'row', [(i, i - 1) for i in senders])]
    reduce_scatter x4 -> x0, waiting for transfers between devices: 150 us -> none  [local(): lax.psum_scatter(product, 'row', scatter_dimension=0, tiled=True)]
    dot_general x43 -> x12, matrix products: 178 us -> 37.5 us  [dot(): return lax.dot_general(a, b, (dims, ((), ())), preferred_element_type=F32)]
    ppermute x0 -> x51, starting transfers between devices: none -> 122 us  [the longest x24 70.2 us: up(): return lax.ppermute(value, 'row', [(i, i + 1) for i in senders])]
    all_gather x2 -> x0, waiting for transfers between devices: 116 us -> none  [the longest x1 89.3 us: local(): grad_cols = lax.all_gather(gradient, 'row', axis=0, tiled=True)]
    pallas_call x0 -> x14, Pallas kernels: none -> 108 us  [the longest x4 38.3 us: update_chunk(): pl.pallas_call(functools.partial(update_kernel, lines=lines, tile=tile),...]
    ppermute x21 -> x20, waiting for transfers between devices: 204 us -> 125 us  [swap(): return lax.ppermute(value, 'col', [(i, i ^ distance) for i in range(cols)])]
    another operation x3 -> x1, local copies, waits for them, and re-layouts: 9.79 us -> 1.88 us  [local(): left_rows = place_by_distance(jnp.stack(backs), me)]
  transfers between devices with their start and end apart: 27 -> 71, of which waited for: 11 -> 29; matrix products, arithmetic and copies ran while one was open for 25% -> 13% of each run, Pallas kernels for 0% -> 7%
where the time goes in v2:
time: 723 us; the launch traced here: 713 us
  waiting for transfers between devices  367 us (51%)
  starting transfers between devices  137 us (19%)
  Pallas kernels  108 us (15%)
  local copies, waits for them, and re-layouts  46 us (6%)
  matrix products  37.5 us (5%)
  other arithmetic  16.3 us (2%)
    ppermute x24, waiting for transfers between devices, down(): return lax.ppermute(value, 'row', [(i, i - 1) for i in senders])  198 us
    ppermute x20, waiting for transfers between devices, swap(): return lax.ppermute(value, 'col', [(i, i ^ distance) for i in range(cols)])  125 us
    ppermute x24, starting transfers between devices, up(): return lax.ppermute(value, 'row', [(i, i + 1) for i in senders])  70.2 us
    pallas_call x4, Pallas kernels, update_chunk(): pl.pallas_call(functools.partial(update_kernel, lines=lines, tile=tile),...  38.3 us
    dot_general x12, matrix products, dot(): return lax.dot_general(a, b, (dims, ((), ())), preferred_element_type=F32)  37.5 us
    ppermute x3, waiting for transfers between devices, local(): lax.ppermute(rows, 'row', [(i, (i + back) % lines) for i in range(lines)])  33.3 us
    ppermute x24, starting transfers between devices, down(): return lax.ppermute(value, 'row', [(i, i - 1) for i in senders])  31.2 us
    pallas_call x4, Pallas kernels, restore(): pl.pallas_call(functools.partial(restore_kernel, cols=cols), grid_spec=pl...  30.1 us
  transfers between devices with their start and end apart: 71, of which 29 were waited for; matrix products, arithmetic and copies ran while one was open for 13% of the time, Pallas kernels for 7%

profile of v2, /device:TPU:0, one launch (start us, length us, event | category | flops | bytes accessed | tf_op | source)
XLA Modules:
  0.0 712.7 jit_solution(11699851676887858897)
XLA Ops:
  0.6 3.0 collective-permute-start
  3.6 2.6 fusion.61
  7.6 5.5 collective-permute-start.9
  13.1 36.5 %collective-permute-done = bf16[1024,1024]{1,0:T(8,128)(2,1)} collective-permute-done((bf16[1024,1024]{1,0:T(8,128)(2,1)}, bf16[1024,1024]{1,0:T(8,128)(2,1)}, u32[]{:S(2)}, u32[]{:S(2)}) %collective-permute-start) | collective-permute-done | bytes 2097184 | tf_op jit(solution)/shard_map/ppermute | solution.py:294
  50.9 5.8 collective-permute-start.3
  59.6 4.3 broadcast_in_dim.35
  68.6 4.9 bitcast_dynamic-update-slice_fusion.6
  77.5 6.6 collective-permute-start.21
  85.4 14.5 %collective-permute-done.12 = bf16[1024,512]{1,0:T(8,128)(2,1)} collective-permute-done((bf16[1024,512]{1,0:T(8,128)(2,1)}, bf16[1024,512]{1,0:T(8,128)(2,1)}, u32[]{:S(2)}, u32[]{:S(2)}) %collective-permute-start.12) | collective-permute-done | bytes 1048608 | tf_op jit(solution)/shard_map/ppermute | solution.py:300
  103.7 3.1 bitcast_dynamic-update-slice_fusion.4
  106.8 2.9 fusion.22
  109.6 2.9 fusion.24
  112.5 3.1 fusion.14
  115.7 3.1 fusion.16
  118.8 3.1 fusion.6
  122.0 3.1 fusion.10
  125.1 3.1 fusion.18
  129.6 3.1 fusion.8
  134.3 3.1 fusion.12
  137.4 7.4 %collective-permute-done.13 = bf16[1024,512]{1,0:T(8,128)(2,1)S(1)} collective-permute-done((bf16[1024,512]{1,0:T(8,128)(2,1)}, bf16[1024,512]{1,0:T(8,128)(2,1)S(1)}, u32[]{:S(2)}, u32[]{:S(2)}) %collective-permute-start.13) | collective-permute-done | bytes 1048608 | tf_op jit(solution)/shard_map/ppermute | solution.py:300
  146.9 3.1 fusion.20
  150.0 3.3 fusion.29
  153.3 10.2 %collective-permute-start.25 = (bf16[512,1024]{1,0:T(8,128)(2,1)}, bf16[512,1024]{1,0:T(8,128)(2,1)S(1)}, u32[]{:S(2)}, u32[]{:S(2)}) collective-permute-start(bf16[512,1024]{1,0:T(8,128)(2,1)} %get-tuple-element.71), channel_id=1, source_target_pairs={{0,4},{4,8},{8,12},{1,5},{5,9},{9,13},{2,6},{6,10},{10,14},{3,7},{... | collective-permute-start | bytes 3145736 | tf_op jit(solution)/shard_map/ppermute | solution.py:297
  163.7 3.6 collective-permute-done.22
  169.0 20.8 %collective-permute-done.26 = bf16[512,1024]{1,0:T(8,128)(2,1)S(1)} collective-permute-done((bf16[512,1024]{1,0:T(8,128)(2,1)}, bf16[512,1024]{1,0:T(8,128)(2,1)S(1)}, u32[]{:S(2)}, u32[]{:S(2)}) %collective-permute-start.26) | collective-permute-done | bytes 1048608 | tf_op jit(solution)/shard_map/ppermute | solution.py:300
  191.1 21.2 %collective-permute-done.7 = bf16[1024,512]{1,0:T(8,128)(2,1)S(1)} collective-permute-done((bf16[1024,512]{1,0:T(8,128)(2,1)}, bf16[1024,512]{1,0:T(8,128)(2,1)S(1)}, u32[]{:S(2)}, u32[]{:S(2)}) %collective-permute-start.7) | collective-permute-done | bytes 1048608 | tf_op jit(solution)/shard_map/ppermute | solution.py:300
  215.3 3.3 fusion.28
  221.7 13.0 %collective-permute-done.24 = bf16[512,1024]{1,0:T(8,128)(2,1)S(1)} collective-permute-done((bf16[512,1024]{1,0:T(8,128)(2,1)S(1)}, bf16[512,1024]{1,0:T(8,128)(2,1)S(1)}, u32[]{:S(2)}, u32[]{:S(2)}) %collective-permute-start.24) | collective-permute-done | bytes 1048608 | tf_op jit(solution)/shard_map/ppermute | solution.py:300
  236.0 21.2 %collective-permute-done.28 = bf16[512,1024]{1,0:T(8,128)(2,1)S(1)} collective-permute-done((bf16[512,1024]{1,0:T(8,128)(2,1)S(1)}, bf16[512,1024]{1,0:T(8,128)(2,1)S(1)}, u32[]{:S(2)}, u32[]{:S(2)}) %collective-permute-start.28) | collective-permute-done | bytes 1048608 | tf_op jit(solution)/shard_map/ppermute | solution.py:300
  260.1 19.5 %collective-permute-done.29 = bf16[512,1024]{1,0:T(8,128)(2,1)S(1)} collective-permute-done((bf16[512,1024]{1,0:T(8,128)(2,1)S(1)}, bf16[512,1024]{1,0:T(8,128)(2,1)S(1)}, u32[]{:S(2)}, u32[]{:S(2)}) %collective-permute-start.29) | collective-permute-done | bytes 1048608 | tf_op jit(solution)/shard_map/ppermute | solution.py:300
  279.7 22.2 %collective-permute-done.30 = bf16[512,1024]{1,0:T(8,128)(2,1)S(1)} collective-permute-done((bf16[512,1024]{1,0:T(8,128)(2,1)S(1)}, bf16[512,1024]{1,0:T(8,128)(2,1)S(1)}, u32[]{:S(2)}, u32[]{:S(2)}) %collective-permute-start.30) | collective-permute-done | bytes 1048608 | tf_op jit(solution)/shard_map/ppermute | solution.py:300
  302.4 3.4 collective-permute-done.17.refs_4_
  309.3 2.4 constant_dynamic-update-slice_fusion.11
  321.2 24.3 %rotate_part.1.part = f32[1024,1024]{1,0:T(8,128)} custom-call(s32[1]{0:T(128)} %bitcast.1.me_ref, bf16[2,1024,512]{2,1,0:T(8,128)(2,1)} %pad_maximum_fusion.refs_0_, bf16[2,1024,512]{2,1,0:T(8,128)(2,1)S(1)} %pad_maximum_fusion.1.refs_1_, bf16[2,1024,512]{2,1,0:T(8,128)(2,1)} %collective-permute-done.15.refs_2_, ...), custom_call_target="tpu_custom_call" | custom-call | flops 17179869184 | bytes 20971520 | tf_op jit(solution)/shard_map/rotate_part/pallas_call | solution.py:58
  345.5 3.3 constant_dynamic-update-slice_fusion.4
  353.9 11.0 %rotate.1 = (f32[1024,1024]{1,0:T(8,128)}, f32[1024,1024]{1,0:T(8,128)}, bf16[2,1024,1024]{2,1,0:T(8,128)(2,1)S(1)}) custom-call(s32[1]{0:T(128)} %bitcast.place_ref, f32[1024,1024]{1,0:T(8,128)S(1)} %copy-done.2, bf16[2,1024,512]{2,1,0:T(8,128)(2,1)S(1)} %select_select_fusion.1.refs_0_, bf16[2,1024,512]{2,1,0:T(8,128)(2,1)S(1)} %select_select_fusion.refs_1_, ...), custom_call_target="tpu_custom_call" | custom-call | flops 4294967296 | bytes 31457280 | tf_op jit(solution)/shard_map/rotate/pallas_call | solution.py:103
  364.9 8.9 %restore.4 = (f32[2,1024,256]{2,1,0:T(8,128)S(1)}, f32[2,1024,256]{2,1,0:T(8,128)}) custom-call(s32[1]{0:T(128)} %bitcast.1.me_ref, bf16[2,1024,1024]{2,1,0:T(8,128)(2,1)S(1)} %get-tuple-element.39.normed, bf16[5120,1024]{1,0:T(8,128)(2,1)} %get-tuple-element.59.refs_0_.refs_1_.refs_2_.refs_3_, ...), custom_call_target="tpu_custom_call" | custom-call | flops 4294967296 | bytes 8388608 | tf_op jit(solution)/shard_map/restore/pallas_call | solution.py:142
  374.2 7.7 %restore.5 = (f32[2,1024,256]{2,1,0:T(8,128)S(1)}, f32[2,1024,256]{2,1,0:T(8,128)}) custom-call(s32[1]{0:T(128)} %bitcast.1.me_ref, bf16[2,1024,1024]{2,1,0:T(8,128)(2,1)S(1)} %get-tuple-element.39.normed, bf16[5120,1024]{1,0:T(8,128)(2,1)} %get-tuple-element.59.refs_0_.refs_1_.refs_2_.refs_3_, ...), custom_call_target="tpu_custom_call" | custom-call | flops 4294967296 | bytes 8388608 | tf_op jit(solution)/shard_map/restore/pallas_call | solution.py:142
  384.2 2.4 collective-permute-start.43
  386.6 17.5 %collective-permute-start.44 = (bf16[256,1024]{1,0:T(8,128)(2,1)S(1)}, bf16[256,1024]{1,0:T(8,128)(2,1)S(1)}, u32[]{:S(2)}, u32[]{:S(2)}) collective-permute-start(bf16[256,1024]{1,0:T(8,128)(2,1)S(1)} %get-tuple-element.63), channel_id=1, source_target_pairs={{0,8},{4,12},{8,0},{12,4},{1,9},{5,13},{9,1},{13,5},{2,10},{6,14},... | collective-permute-start | bytes 1572872 | tf_op jit(solution)/shard_map/ppermute | solution.py:389
  404.9 11.5 %collective-permute-done.43 = bf16[256,1024]{1,0:T(8,128)(2,1)S(1)} collective-permute-done((bf16[256,1024]{1,0:T(8,128)(2,1)S(1)}, bf16[256,1024]{1,0:T(8,128)(2,1)S(1)}, u32[]{:S(2)}, u32[]{:S(2)}) %collective-permute-start.43) | collective-permute-done | bytes 524320 | tf_op jit(solution)/shard_map/ppermute | solution.py:389
  416.4 21.8 %collective-permute-done.44 = bf16[256,1024]{1,0:T(8,128)(2,1)S(1)} collective-permute-done((bf16[256,1024]{1,0:T(8,128)(2,1)S(1)}, bf16[256,1024]{1,0:T(8,128)(2,1)S(1)}, u32[]{:S(2)}, u32[]{:S(2)}) %collective-permute-start.44) | collective-permute-done | bytes 524320 | tf_op jit(solution)/shard_map/ppermute | solution.py:389
  444.3 6.7 restore.7
  452.5 6.7 restore.6
  459.7 50.9 %collective-permute-done.64.refs_2_ = f32[1024,256]{1,0:T(8,128)S(1)} collective-permute-done((f32[1024,256]{1,0:T(8,128)S(1)}, f32[1024,256]{1,0:T(8,128)S(1)}, u32[]{:S(2)}, u32[]{:S(2)}) %collective-permute-start.64) | collective-permute-done | bytes 1048608 | tf_op jit(solution)/shard_map/ppermute | solution.py:294
  514.7 20.5 %collective-permute-done.57.refs_2_ = f32[1024,256]{1,0:T(8,128)S(1)} collective-permute-done((f32[1024,256]{1,0:T(8,128)S(1)}, f32[1024,256]{1,0:T(8,128)S(1)}, u32[]{:S(2)}, u32[]{:S(2)}) %collective-permute-start.57) | collective-permute-done | bytes 1048608 | tf_op jit(solution)/shard_map/ppermute | solution.py:294
  535.2 13.8 %collective-permute-start.65 = (bf16[1040,256]{1,0:T(8,128)(2,1)S(1)}, bf16[1040,256]{1,0:T(8,128)(2,1)S(1)}, u32[]{:S(2)}, u32[]{:S(2)}) collective-permute-start(bf16[1040,256]{1,0:T(8,128)(2,1)S(1)} %get-tuple-element.58), channel_id=1, source_target_pairs={{0,4},{4,8},{8,12},{1,5},{5,9},{9,13},{2,6},{6,10},{10,14},{3,7},{... | collective-permute-start | bytes 1597448 | tf_op jit(solution)/shard_map/ppermute | solution.py:297
  552.7 4.6 collective-permute-start.58
  557.2 4.2 collective-permute-done.65.refs_0_
  563.1 2.5 collective-permute-done.68.refs_3_
  566.3 4.2 collective-permute-done.58.refs_0_
  573.2 5.6 collective-permute-done.61.refs_3_
  580.9 9.1 %collective-permute-done.69.refs_4_ = bf16[1040,256]{1,0:T(8,128)(2,1)S(1)} collective-permute-done((bf16[1040,256]{1,0:T(8,128)(2,1)S(1)}, bf16[1040,256]{1,0:T(8,128)(2,1)S(1)}, u32[]{:S(2)}, u32[]{:S(2)}) %collective-permute-start.69) | collective-permute-done | bytes 532512 | tf_op jit(solution)/shard_map/ppermute | solution.py:300
  592.0 5.9 collective-permute-done.50.refs_2_
  600.2 6.7 collective-permute-done.62.refs_4_
  609.3 7.8 %collective-permute-done.36.refs_2_ = f32[1024,256]{1,0:T(8,128)S(1)} collective-permute-done((f32[1024,256]{1,0:T(8,128)S(1)}, f32[1024,256]{1,0:T(8,128)S(1)}, u32[]{:S(2)}, u32[]{:S(2)}) %collective-permute-start.36) | collective-permute-done | bytes 1048608 | tf_op jit(solution)/shard_map/ppermute | solution.py:294
  622.9 5.8 collective-permute-start.37
  637.6 10.0 %collective-permute-done.40.refs_3_ = bf16[1040,256]{1,0:T(8,128)(2,1)S(1)} collective-permute-done((bf16[1040,256]{1,0:T(8,128)(2,1)S(1)}, bf16[1040,256]{1,0:T(8,128)(2,1)S(1)}, u32[]{:S(2)}, u32[]{:S(2)}) %collective-permute-start.40) | collective-permute-done | bytes 532512 | tf_op jit(solution)/shard_map/ppermute | solution.py:300
  651.5 7.5 %collective-permute-done.55.refs_4_ = bf16[1040,256]{1,0:T(8,128)(2,1)S(1)} collective-permute-done((bf16[1040,256]{1,0:T(8,128)(2,1)S(1)}, bf16[1040,256]{1,0:T(8,128)(2,1)S(1)}, u32[]{:S(2)}, u32[]{:S(2)}) %collective-permute-start.55) | collective-permute-done | bytes 532512 | tf_op jit(solution)/shard_map/ppermute | solution.py:300
  660.6 9.6 %update_chunk.4.refs_7_ = f32[1024,1024]{1,0:T(8,128)} custom-call(s32[1]{0:T(128)} %bitcast.place_ref, bf16[1024,512]{1,0:T(8,128)(2,1)S(1)} %get-tuple-element.57.own, bf16[1040,256]{1,0:T(8,128)(2,1)S(1)} %collective-permute-done.65.refs_0_, bf16[1040,256]{1,0:T(8,128)(2,1)S(1)} %collective-permute-done.66.refs_1_, ...), custom_call_target="tpu_custom_call" | custom-call | flops 4294967296 | bytes 12582912 | tf_op jit(solution)/shard_map/update_chunk/pallas_call | solution.py:272
  670.8 11.0 %collective-permute-done.41.refs_4_ = bf16[1040,256]{1,0:T(8,128)(2,1)S(1)} collective-permute-done((bf16[1040,256]{1,0:T(8,128)(2,1)S(1)}, bf16[1040,256]{1,0:T(8,128)(2,1)S(1)}, u32[]{:S(2)}, u32[]{:S(2)}) %collective-permute-start.41) | collective-permute-done | bytes 532512 | tf_op jit(solution)/shard_map/ppermute | solution.py:300
  683.2 9.6 %update_chunk.5.refs_7_ = f32[1024,1024]{1,0:T(8,128)} custom-call(s32[1]{0:T(128)} %bitcast.place_ref, bf16[1024,512]{1,0:T(8,128)(2,1)S(1)} %get-tuple-element.52.own, bf16[1040,256]{1,0:T(8,128)(2,1)S(1)} %collective-permute-done.58.refs_0_, bf16[1040,256]{1,0:T(8,128)(2,1)S(1)} %collective-permute-done.59.refs_1_, ...), custom_call_target="tpu_custom_call", output_to_operand_aliasing={{}: (9, {})} | custom-call | flops 4294967296 | bytes 12582912 | tf_op jit(solution)/shard_map/update_chunk/pallas_call | solution.py:272
  693.3 9.6 %update_chunk.6.refs_7_ = f32[1024,1024]{1,0:T(8,128)} custom-call(s32[1]{0:T(128)} %bitcast.place_ref, bf16[1024,512]{1,0:T(8,128)(2,1)S(1)} %get-tuple-element.47.own, bf16[1040,256]{1,0:T(8,128)(2,1)S(1)} %collective-permute-done.51.refs_0_, bf16[1040,256]{1,0:T(8,128)(2,1)S(1)} %collective-permute-done.52.refs_1_, ...), custom_call_target="tpu_custom_call", output_to_operand_aliasing={{}: (9, {})} | custom-call | flops 4294967296 | bytes 12582912 | tf_op jit(solution)/shard_map/update_chunk/pallas_call | solution.py:272
  702.9 9.6 %update_chunk.7 = f32[1024,1024]{1,0:T(8,128)} custom-call(s32[1]{0:T(128)} %bitcast.place_ref, bf16[1024,512]{1,0:T(8,128)(2,1)S(1)} %get-tuple-element.42.own, bf16[1040,256]{1,0:T(8,128)(2,1)S(1)} %collective-permute-done.37.refs_0_, bf16[1040,256]{1,0:T(8,128)(2,1)S(1)} %collective-permute-done.38.refs_1_, ...), custom_call_target="tpu_custom_call", output_to_operand_aliasing={{}: (9, {})} | custom-call | flops 4294967296 | bytes 12582912 | tf_op jit(solution)/shard_map/update_chunk/pallas_call | solution.py:272
  (221 shorter events, 111.2 us)
Async XLA Ops:
  0.6 49.0 %collective-permute-start = (bf16[1024,1024]{1,0:T(8,128)(2,1)}, bf16[1024,1024]{1,0:T(8,128)(2,1)}, u32[]{:S(2)}, u32[]{:S(2)}) collective-permute-start(bf16[1024,1024]{1,0:T(8,128)(2,1)} %param.8), channel_id=1, source_target_pairs={{0,2},{1,3},{2,0},{3,1},{4,6},{5,7},{6,4},{7,5},{8,10},{9,11},{10,... | collective-permute-start | bytes 6291464 | tf_op jit(solution)/shard_map/ppermute | solution.py:294
  3.6 54.3 %collective-permute-start.1 = (bf16[1024,1024]{1,0:T(8,128)(2,1)}, bf16[1024,1024]{1,0:T(8,128)(2,1)S(1)}, u32[]{:S(2)}, u32[]{:S(2)}) collective-permute-start(bf16[1024,1024]{1,0:T(8,128)(2,1)} %param.8), channel_id=1, source_target_pairs={{0,1},{1,0},{2,3},{3,2},{4,5},{5,4},{6,7},{7,6},{8,9},{9,8},{10,11... | collective-permute-start | bytes 6291464 | tf_op jit(solution)/shard_map/ppermute | solution.py:294
  6.3 44.6 %collective-permute-start.10 = (bf16[1024,512]{1,0:T(8,128)(2,1)}, bf16[1024,512]{1,0:T(8,128)(2,1)}, u32[]{:S(2)}, u32[]{:S(2)}) collective-permute-start(bf16[1024,512]{1,0:T(8,128)(2,1)} %get-tuple-element.76), channel_id=1, source_target_pairs={{4,0},{8,4},{12,8},{5,1},{9,5},{13,9},{6,2},{10,6},{14,10},{7,3},{... | collective-permute-start | bytes 3145736 | tf_op jit(solution)/shard_map/ppermute | solution.py:300
  7.6 49.1 %collective-permute-start.9 = (bf16[1024,512]{1,0:T(8,128)(2,1)}, bf16[1024,512]{1,0:T(8,128)(2,1)}, u32[]{:S(2)}, u32[]{:S(2)}) collective-permute-start(bf16[1024,512]{1,0:T(8,128)(2,1)} %get-tuple-element.76), channel_id=1, source_target_pairs={{0,4},{4,8},{8,12},{1,5},{5,9},{9,13},{2,6},{6,10},{10,14},{3,7},{... | collective-permute-start | bytes 3145736 | tf_op jit(solution)/shard_map/ppermute | solution.py:297
  49.6 53.4 %collective-permute-start.2 = (bf16[1024,1024]{1,0:T(8,128)(2,1)}, bf16[1024,1024]{1,0:T(8,128)(2,1)}, u32[]{:S(2)}, u32[]{:S(2)}) collective-permute-start(bf16[1024,1024]{1,0:T(8,128)(2,1)} %collective-permute-done), channel_id=1, source_target_pairs={{0,1},{1,0},{2,3},{3,2},{4,5},{5,4},{6,7},{7,6},{8,9},{9,8},{10,11... | collective-permute-start | bytes 6291464 | tf_op jit(solution)/shard_map/ppermute | solution.py:294
  49.6 27.9 %collective-permute-start.4 = (bf16[1024,512]{1,0:T(8,128)(2,1)S(1)}, bf16[1024,512]{1,0:T(8,128)(2,1)}, u32[]{:S(2)}, u32[]{:S(2)}) collective-permute-start(bf16[1024,512]{1,0:T(8,128)(2,1)S(1)} %get-tuple-element.77), channel_id=1, source_target_pairs={{4,0},{8,4},{12,8},{5,1},{9,5},{13,9},{6,2},{10,6},{14,10},{7,3},{... | collective-permute-start | bytes 3145736 | tf_op jit(solution)/shard_map/ppermute | solution.py:300
  50.9 33.2 %collective-permute-start.3 = (bf16[1024,512]{1,0:T(8,128)(2,1)S(1)}, bf16[1024,512]{1,0:T(8,128)(2,1)}, u32[]{:S(2)}, u32[]{:S(2)}) collective-permute-start(bf16[1024,512]{1,0:T(8,128)(2,1)S(1)} %get-tuple-element.77), channel_id=1, source_target_pairs={{0,4},{4,8},{8,12},{1,5},{5,9},{9,13},{2,6},{6,10},{10,14},{3,7},{... | collective-permute-start | bytes 3145736 | tf_op jit(solution)/shard_map/ppermute | solution.py:297
  56.7 43.3 %collective-permute-start.12 = (bf16[1024,512]{1,0:T(8,128)(2,1)}, bf16[1024,512]{1,0:T(8,128)(2,1)}, u32[]{:S(2)}, u32[]{:S(2)}) collective-permute-start(bf16[1024,512]{1,0:T(8,128)(2,1)} %collective-permute-done.10), channel_id=1, source_target_pairs={{4,0},{8,4},{5,1},{9,5},{6,2},{10,6},{7,3},{11,7},{20,16},{24,20},... | collective-permute-start | bytes 3145736 | tf_op jit(solution)/shard_map/ppermute | solution.py:300
  58.0 43.7 %collective-permute-start.11 = (bf16[1024,512]{1,0:T(8,128)(2,1)}, bf16[1024,512]{1,0:T(8,128)(2,1)}, u32[]{:S(2)}, u32[]{:S(2)}) collective-permute-start(bf16[1024,512]{1,0:T(8,128)(2,1)} %collective-permute-done.9), channel_id=1, source_target_pairs={{4,8},{8,12},{5,9},{9,13},{6,10},{10,14},{7,11},{11,15},{20,24},{2... | collective-permute-start | bytes 3145736 | tf_op jit(solution)/shard_map/ppermute | solution.py:297
  77.5 75.8 %collective-permute-start.21 = (bf16[512,1024]{1,0:T(8,128)(2,1)}, bf16[512,1024]{1,0:T(8,128)(2,1)}, u32[]{:S(2)}, u32[]{:S(2)}) collective-permute-start(bf16[512,1024]{1,0:T(8,128)(2,1)} %get-tuple-element.73), channel_id=1, source_target_pairs={{0,4},{4,8},{8,12},{1,5},{5,9},{9,13},{2,6},{6,10},{10,14},{3,7},{... | collective-permute-start | bytes 3145736 | tf_op jit(solution)/shard_map/ppermute | solution.py:297
  84.2 44.1 %collective-permute-start.6 = (bf16[1024,512]{1,0:T(8,128)(2,1)}, bf16[1024,512]{1,0:T(8,128)(2,1)}, u32[]{:S(2)}, u32[]{:S(2)}) collective-permute-start(bf16[1024,512]{1,0:T(8,128)(2,1)} %collective-permute-done.4), channel_id=1, source_target_pairs={{4,0},{8,4},{5,1},{9,5},{6,2},{10,6},{7,3},{11,7},{20,16},{24,20},... | collective-permute-start | bytes 3145736 | tf_op jit(solution)/shard_map/ppermute | solution.py:300
  100.0 32.7 %collective-permute-start.5 = (bf16[1024,512]{1,0:T(8,128)(2,1)}, bf16[1024,512]{1,0:T(8,128)(2,1)}, u32[]{:S(2)}, u32[]{:S(2)}) collective-permute-start(bf16[1024,512]{1,0:T(8,128)(2,1)} %collective-permute-done.3), channel_id=1, source_target_pairs={{4,8},{8,12},{5,9},{9,13},{6,10},{10,14},{7,11},{11,15},{20,24},{2... | collective-permute-start | bytes 3145736 | tf_op jit(solution)/shard_map/ppermute | solution.py:297
  101.6 43.2 %collective-permute-start.13 = (bf16[1024,512]{1,0:T(8,128)(2,1)}, bf16[1024,512]{1,0:T(8,128)(2,1)S(1)}, u32[]{:S(2)}, u32[]{:S(2)}) collective-permute-start(bf16[1024,512]{1,0:T(8,128)(2,1)} %collective-permute-done.12), channel_id=1, source_target_pairs={{4,0},{5,1},{6,2},{7,3},{20,16},{21,17},{22,18},{23,19}} | collective-permute-start | bytes 3145736 | tf_op jit(solution)/shard_map/ppermute | solution.py:300
  102.9 43.2 %collective-permute-start.14 = (bf16[1024,512]{1,0:T(8,128)(2,1)}, bf16[1024,512]{1,0:T(8,128)(2,1)S(1)}, u32[]{:S(2)}, u32[]{:S(2)}) collective-permute-start(bf16[1024,512]{1,0:T(8,128)(2,1)} %collective-permute-done.11), channel_id=1, source_target_pairs={{8,12},{9,13},{10,14},{11,15},{24,28},{25,29},{26,30},{27,31}} | collective-permute-start | bytes 3145736 | tf_op jit(solution)/shard_map/ppermute | solution.py:297
  128.3 39.0 %collective-permute-start.22 = (bf16[512,1024]{1,0:T(8,128)(2,1)}, bf16[512,1024]{1,0:T(8,128)(2,1)S(1)}, u32[]{:S(2)}, u32[]{:S(2)}) collective-permute-start(bf16[512,1024]{1,0:T(8,128)(2,1)} %get-tuple-element.73), channel_id=1, source_target_pairs={{4,0},{8,4},{12,8},{5,1},{9,5},{13,9},{6,2},{10,6},{14,10},{7,3},{... | collective-permute-start | bytes 3145736 | tf_op jit(solution)/shard_map/ppermute | solution.py:300
  132.7 57.0 %collective-permute-start.26 = (bf16[512,1024]{1,0:T(8,128)(2,1)}, bf16[512,1024]{1,0:T(8,128)(2,1)S(1)}, u32[]{:S(2)}, u32[]{:S(2)}) collective-permute-start(bf16[512,1024]{1,0:T(8,128)(2,1)} %get-tuple-element.71), channel_id=1, source_target_pairs={{4,0},{8,4},{12,8},{5,1},{9,5},{13,9},{6,2},{10,6},{14,10},{7,3},{... | collective-permute-start | bytes 3145736 | tf_op jit(solution)/shard_map/ppermute | solution.py:300
  144.8 67.4 %collective-permute-start.7 = (bf16[1024,512]{1,0:T(8,128)(2,1)}, bf16[1024,512]{1,0:T(8,128)(2,1)S(1)}, u32[]{:S(2)}, u32[]{:S(2)}) collective-permute-start(bf16[1024,512]{1,0:T(8,128)(2,1)} %collective-permute-done.6), channel_id=1, source_target_pairs={{4,0},{5,1},{6,2},{7,3},{20,16},{21,17},{22,18},{23,19}} | collective-permute-start | bytes 3145736 | tf_op jit(solution)/shard_map/ppermute | solution.py:300
  146.1 67.4 %collective-permute-start.8 = (bf16[1024,512]{1,0:T(8,128)(2,1)}, bf16[1024,512]{1,0:T(8,128)(2,1)S(1)}, u32[]{:S(2)}, u32[]{:S(2)}) collective-permute-start(bf16[1024,512]{1,0:T(8,128)(2,1)} %collective-permute-done.5), channel_id=1, source_target_pairs={{8,12},{9,13},{10,14},{11,15},{24,28},{25,29},{26,30},{27,31}} | collective-permute-start | bytes 3145736 | tf_op jit(solution)/shard_map/ppermute | solution.py:297
  153.3 67.4 %collective-permute-start.25 = (bf16[512,1024]{1,0:T(8,128)(2,1)}, bf16[512,1024]{1,0:T(8,128)(2,1)S(1)}, u32[]{:S(2)}, u32[]{:S(2)}) collective-permute-start(bf16[512,1024]{1,0:T(8,128)(2,1)} %get-tuple-element.71), channel_id=1, source_target_pairs={{0,4},{4,8},{8,12},{1,5},{5,9},{9,13},{2,6},{6,10},{10,14},{3,7},{... | collective-permute-start | bytes 3145736 | tf_op jit(solution)/shard_map/ppermute | solution.py:297
  167.3 53.7 %collective-permute-start.23 = (bf16[512,1024]{1,0:T(8,128)(2,1)}, bf16[512,1024]{1,0:T(8,128)(2,1)}, u32[]{:S(2)}, u32[]{:S(2)}) collective-permute-start(bf16[512,1024]{1,0:T(8,128)(2,1)} %collective-permute-done.21), channel_id=1, source_target_pairs={{4,8},{8,12},{5,9},{9,13},{6,10},{10,14},{7,11},{11,15},{20,24},{2... | collective-permute-start | bytes 3145736 | tf_op jit(solution)/shard_map/ppermute | solution.py:297
  189.8 44.9 %collective-permute-start.24 = (bf16[512,1024]{1,0:T(8,128)(2,1)S(1)}, bf16[512,1024]{1,0:T(8,128)(2,1)S(1)}, u32[]{:S(2)}, u32[]{:S(2)}) collective-permute-start(bf16[512,1024]{1,0:T(8,128)(2,1)S(1)} %collective-permute-done.22), channel_id=1, source_target_pairs={{4,0},{8,4},{5,1},{9,5},{6,2},{10,6},{7,3},{11,7},{20,16},{24,20},... | collective-permute-start | bytes 3145736 | tf_op jit(solution)/shard_map/ppermute | solution.py:300
  212.2 44.9 %collective-permute-start.28 = (bf16[512,1024]{1,0:T(8,128)(2,1)S(1)}, bf16[512,1024]{1,0:T(8,128)(2,1)S(1)}, u32[]{:S(2)}, u32[]{:S(2)}) collective-permute-start(bf16[512,1024]{1,0:T(8,128)(2,1)S(1)} %collective-permute-done.26), channel_id=1, source_target_pairs={{4,0},{8,4},{5,1},{9,5},{6,2},{10,6},{7,3},{11,7},{20,16},{24,20},... | collective-permute-start | bytes 3145736 | tf_op jit(solution)/shard_map/ppermute | solution.py:300
  213.5 88.3 %collective-permute-start.18 = (bf16[2,1024,512]{2,1,0:T(8,128)(2,1)S(1)}, bf16[2,1024,512]{2,1,0:T(8,128)(2,1)}, u32[]{:S(2)}, u32[]{:S(2)}) collective-permute-start(bf16[2,1024,512]{2,1,0:T(8,128)(2,1)S(1)} %pad_maximum_fusion.1.refs_1_), channel_id=1, source_target_pairs={{0,2},{1,3},{2,0},{3,1},{4,6},{5,7},{6,4},{7,5},{8,10},{9,11},{10,... | collective-permute-start | bytes 6291464 | tf_op jit(solution)/shard_map/ppermute | solution.py:294
  220.7 85.1 %collective-permute-start.17 = (bf16[2,1024,512]{2,1,0:T(8,128)(2,1)}, bf16[2,1024,512]{2,1,0:T(8,128)(2,1)}, u32[]{:S(2)}, u32[]{:S(2)}) collective-permute-start(bf16[2,1024,512]{2,1,0:T(8,128)(2,1)} %pad_maximum_fusion.refs_0_), channel_id=1, source_target_pairs={{0,2},{1,3},{2,0},{3,1},{4,6},{5,7},{6,4},{7,5},{8,10},{9,11},{10,... | collective-permute-start | bytes 6291464 | tf_op jit(solution)/shard_map/ppermute | solution.py:294
  221.0 37.5 %collective-permute-start.27 = (bf16[512,1024]{1,0:T(8,128)(2,1)S(1)}, bf16[512,1024]{1,0:T(8,128)(2,1)S(1)}, u32[]{:S(2)}, u32[]{:S(2)}) collective-permute-start(bf16[512,1024]{1,0:T(8,128)(2,1)S(1)} %collective-permute-done.25), channel_id=1, source_target_pairs={{4,8},{8,12},{5,9},{9,13},{6,10},{10,14},{7,11},{11,15},{20,24},{2... | collective-permute-start | bytes 3145736 | tf_op jit(solution)/shard_map/ppermute | solution.py:297
  234.7 44.9 %collective-permute-start.29 = (bf16[512,1024]{1,0:T(8,128)(2,1)S(1)}, bf16[512,1024]{1,0:T(8,128)(2,1)S(1)}, u32[]{:S(2)}, u32[]{:S(2)}) collective-permute-start(bf16[512,1024]{1,0:T(8,128)(2,1)S(1)} %collective-permute-done.24), channel_id=1, source_target_pairs={{4,0},{5,1},{6,2},{7,3},{20,16},{21,17},{22,18},{23,19}} | collective-permute-start | bytes 3145736 | tf_op jit(solution)/shard_map/ppermute | solution.py:300
  257.2 44.7 %collective-permute-start.30 = (bf16[512,1024]{1,0:T(8,128)(2,1)S(1)}, bf16[512,1024]{1,0:T(8,128)(2,1)S(1)}, u32[]{:S(2)}, u32[]{:S(2)}) collective-permute-start(bf16[512,1024]{1,0:T(8,128)(2,1)S(1)} %collective-permute-done.28), channel_id=1, source_target_pairs={{4,0},{5,1},{6,2},{7,3},{20,16},{21,17},{22,18},{23,19}} | collective-permute-start | bytes 3145736 | tf_op jit(solution)/shard_map/ppermute | solution.py:300
  258.5 54.3 %collective-permute-start.31 = (bf16[512,1024]{1,0:T(8,128)(2,1)}, bf16[512,1024]{1,0:T(8,128)(2,1)}, u32[]{:S(2)}, u32[]{:S(2)}) collective-permute-start(bf16[512,1024]{1,0:T(8,128)(2,1)} %collective-permute-done.23), channel_id=1, source_target_pairs={{8,12},{9,13},{10,14},{11,15},{24,28},{25,29},{26,30},{27,31}} | collective-permute-start | bytes 3145736 | tf_op jit(solution)/shard_map/ppermute | solution.py:297
  279.7 41.5 %collective-permute-start.16 = (bf16[2,1024,512]{2,1,0:T(8,128)(2,1)S(1)}, bf16[2,1024,512]{2,1,0:T(8,128)(2,1)}, u32[]{:S(2)}, u32[]{:S(2)}) collective-permute-start(bf16[2,1024,512]{2,1,0:T(8,128)(2,1)S(1)} %pad_maximum_fusion.1.refs_1_), channel_id=1, source_target_pairs={{0,1},{1,0},{2,3},{3,2},{4,5},{5,4},{6,7},{7,6},{8,9},{9,8},{10,11... | collective-permute-start | bytes 6291464 | tf_op jit(solution)/shard_map/ppermute | solution.py:294
  301.8 19.3 %collective-permute-start.15 = (bf16[2,1024,512]{2,1,0:T(8,128)(2,1)}, bf16[2,1024,512]{2,1,0:T(8,128)(2,1)}, u32[]{:S(2)}, u32[]{:S(2)}) collective-permute-start(bf16[2,1024,512]{2,1,0:T(8,128)(2,1)} %pad_maximum_fusion.refs_0_), channel_id=1, source_target_pairs={{0,1},{1,0},{2,3},{3,2},{4,5},{5,4},{6,7},{7,6},{8,9},{9,8},{10,11... | collective-permute-start | bytes 6291464 | tf_op jit(solution)/shard_map/ppermute | solution.py:294
  301.9 19.3 %collective-permute-start.20 = (bf16[2,1024,512]{2,1,0:T(8,128)(2,1)}, bf16[2,1024,512]{2,1,0:T(8,128)(2,1)}, u32[]{:S(2)}, u32[]{:S(2)}) collective-permute-start(bf16[2,1024,512]{2,1,0:T(8,128)(2,1)} %collective-permute-done.18.refs_5_), channel_id=1, source_target_pairs={{0,1},{1,0},{2,3},{3,2},{4,5},{5,4},{6,7},{7,6},{8,9},{9,8},{10,11... | collective-permute-start | bytes 6291464 | tf_op jit(solution)/shard_map/ppermute | solution.py:294
  373.8 68.3 %collective-permute-start.33 = (f32[2,1024,256]{2,1,0:T(8,128)}, f32[2,1024,256]{2,1,0:T(8,128)}, u32[]{:S(2)}, u32[]{:S(2)}) collective-permute-start(f32[2,1024,256]{2,1,0:T(8,128)} %get-tuple-element.35), channel_id=1, source_target_pairs={{0,1},{1,0},{2,3},{3,2},{4,5},{5,4},{6,7},{7,6},{8,9},{9,8},{10,11... | collective-permute-start | bytes 6291464 | tf_op jit(solution)/shard_map/ppermute | solution.py:294
  381.9 69.1 %collective-permute-start.34 = (f32[2,1024,256]{2,1,0:T(8,128)}, f32[2,1024,256]{2,1,0:T(8,128)}, u32[]{:S(2)}, u32[]{:S(2)}) collective-permute-start(f32[2,1024,256]{2,1,0:T(8,128)} %get-tuple-element.38), channel_id=1, source_target_pairs={{0,1},{1,0},{2,3},{3,2},{4,5},{5,4},{6,7},{7,6},{8,9},{9,8},{10,11... | collective-permute-start | bytes 6291464 | tf_op jit(solution)/shard_map/ppermute | solution.py:294
  384.2 32.2 %collective-permute-start.43 = (bf16[256,1024]{1,0:T(8,128)(2,1)S(1)}, bf16[256,1024]{1,0:T(8,128)(2,1)S(1)}, u32[]{:S(2)}, u32[]{:S(2)}) collective-permute-start(bf16[256,1024]{1,0:T(8,128)(2,1)S(1)} %get-tuple-element.64), channel_id=1, source_target_pairs={{0,4},{4,8},{8,12},{12,0},{1,5},{5,9},{9,13},{13,1},{2,6},{6,10},{... | collective-permute-start | bytes 1572872 | tf_op jit(solution)/shard_map/ppermute | solution.py:389
  386.6 51.6 %collective-permute-start.44 = (bf16[256,1024]{1,0:T(8,128)(2,1)S(1)}, bf16[256,1024]{1,0:T(8,128)(2,1)S(1)}, u32[]{:S(2)}, u32[]{:S(2)}) collective-permute-start(bf16[256,1024]{1,0:T(8,128)(2,1)S(1)} %get-tuple-element.63), channel_id=1, source_target_pairs={{0,8},{4,12},{8,0},{12,4},{1,9},{5,13},{9,1},{13,5},{2,10},{6,14},... | collective-permute-start | bytes 1572872 | tf_op jit(solution)/shard_map/ppermute | solution.py:389
  404.1 34.1 %collective-permute-start.45 = (bf16[256,1024]{1,0:T(8,128)(2,1)S(1)}, bf16[256,1024]{1,0:T(8,128)(2,1)S(1)}, u32[]{:S(2)}, u32[]{:S(2)}) collective-permute-start(bf16[256,1024]{1,0:T(8,128)(2,1)S(1)} %get-tuple-element.62), channel_id=1, source_target_pairs={{0,12},{4,0},{8,4},{12,8},{1,13},{5,1},{9,5},{13,9},{2,14},{6,2},{... | collective-permute-start | bytes 1572872 | tf_op jit(solution)/shard_map/ppermute | solution.py:389
  439.9 111.4 %collective-permute-start.46 = (bf16[4,256,1024]{2,1,0:T(8,128)(2,1)}, bf16[4,256,1024]{2,1,0:T(8,128)(2,1)}, u32[]{:S(2)}, u32[]{:S(2)}) collective-permute-start(bf16[4,256,1024]{2,1,0:T(8,128)(2,1)} %pad_maximum_fusion.2), channel_id=1, source_target_pairs={{0,2},{1,3},{2,0},{3,1},{4,6},{5,7},{6,4},{7,5},{8,10},{9,11},{10,... | collective-permute-start | bytes 6291464 | tf_op jit(solution)/shard_map/ppermute | solution.py:294
  442.1 110.5 %collective-permute-start.47 = (bf16[4,256,1024]{2,1,0:T(8,128)(2,1)}, bf16[4,256,1024]{2,1,0:T(8,128)(2,1)S(1)}, u32[]{:S(2)}, u32[]{:S(2)}) collective-permute-start(bf16[4,256,1024]{2,1,0:T(8,128)(2,1)} %pad_maximum_fusion.2), channel_id=1, source_target_pairs={{0,1},{1,0},{2,3},{3,2},{4,5},{5,4},{6,7},{7,6},{8,9},{9,8},{10,11... | collective-permute-start | bytes 6291464 | tf_op jit(solution)/shard_map/ppermute | solution.py:294
  443.5 67.1 %collective-permute-start.64 = (f32[1024,256]{1,0:T(8,128)S(1)}, f32[1024,256]{1,0:T(8,128)S(1)}, u32[]{:S(2)}, u32[]{:S(2)}) collective-permute-start(f32[1024,256]{1,0:T(8,128)S(1)} %fusion.33), channel_id=1, source_target_pairs={{0,2},{1,3},{2,0},{3,1},{4,6},{5,7},{6,4},{7,5},{8,10},{9,11},{10,... | collective-permute-start | bytes 3145736 | tf_op jit(solution)/shard_map/ppermute | solution.py:294
  452.4 109.1 %collective-permute-start.49 = (f32[2,1024,256]{2,1,0:T(8,128)S(1)}, f32[2,1024,256]{2,1,0:T(8,128)S(1)}, u32[]{:S(2)}, u32[]{:S(2)}) collective-permute-start(f32[2,1024,256]{2,1,0:T(8,128)S(1)} %get-tuple-element.46), channel_id=1, source_target_pairs={{0,1},{1,0},{2,3},{3,2},{4,5},{5,4},{6,7},{7,6},{8,9},{9,8},{10,11... | collective-permute-start | bytes 6291464 | tf_op jit(solution)/shard_map/ppermute | solution.py:294
  459.2 112.6 %collective-permute-start.35 = (f32[2,1024,256]{2,1,0:T(8,128)S(1)}, f32[2,1024,256]{2,1,0:T(8,128)S(1)}, u32[]{:S(2)}, u32[]{:S(2)}) collective-permute-start(f32[2,1024,256]{2,1,0:T(8,128)S(1)} %get-tuple-element.41), channel_id=1, source_target_pairs={{0,1},{1,0},{2,3},{3,2},{4,5},{5,4},{6,7},{7,6},{8,9},{9,8},{10,11... | collective-permute-start | bytes 6291464 | tf_op jit(solution)/shard_map/ppermute | solution.py:294
  510.6 24.6 %collective-permute-start.57 = (f32[1024,256]{1,0:T(8,128)S(1)}, f32[1024,256]{1,0:T(8,128)S(1)}, u32[]{:S(2)}, u32[]{:S(2)}) collective-permute-start(f32[1024,256]{1,0:T(8,128)S(1)} %fusion.32), channel_id=1, source_target_pairs={{0,2},{1,3},{2,0},{3,1},{4,6},{5,7},{6,4},{7,5},{8,10},{9,11},{10,... | collective-permute-start | bytes 3145736 | tf_op jit(solution)/shard_map/ppermute | solution.py:294
  535.2 26.3 %collective-permute-start.65 = (bf16[1040,256]{1,0:T(8,128)(2,1)S(1)}, bf16[1040,256]{1,0:T(8,128)(2,1)S(1)}, u32[]{:S(2)}, u32[]{:S(2)}) collective-permute-start(bf16[1040,256]{1,0:T(8,128)(2,1)S(1)} %get-tuple-element.58), channel_id=1, source_target_pairs={{0,4},{4,8},{8,12},{1,5},{5,9},{9,13},{2,6},{6,10},{10,14},{3,7},{... | collective-permute-start | bytes 1597448 | tf_op jit(solution)/shard_map/ppermute | solution.py:297
  552.7 17.8 %collective-permute-start.58 = (bf16[1040,256]{1,0:T(8,128)(2,1)S(1)}, bf16[1040,256]{1,0:T(8,128)(2,1)S(1)}, u32[]{:S(2)}, u32[]{:S(2)}) collective-permute-start(bf16[1040,256]{1,0:T(8,128)(2,1)S(1)} %get-tuple-element.53), channel_id=1, source_target_pairs={{0,4},{4,8},{8,12},{1,5},{5,9},{9,13},{2,6},{6,10},{10,14},{3,7},{... | collective-permute-start | bytes 1597448 | tf_op jit(solution)/shard_map/ppermute | solution.py:297
  561.5 60.7 %collective-permute-start.48 = (bf16[4,256,1024]{2,1,0:T(8,128)(2,1)}, bf16[4,256,1024]{2,1,0:T(8,128)(2,1)}, u32[]{:S(2)}, u32[]{:S(2)}) collective-permute-start(bf16[4,256,1024]{2,1,0:T(8,128)(2,1)} %collective-permute-done.46), channel_id=1, source_target_pairs={{0,1},{1,0},{2,3},{3,2},{4,5},{5,4},{6,7},{7,6},{8,9},{9,8},{10,11... | collective-permute-start | bytes 6291464 | tf_op jit(solution)/shard_map/ppermute | solution.py:294
  561.5 17.3 %collective-permute-start.61 = (bf16[1040,256]{1,0:T(8,128)(2,1)S(1)}, bf16[1040,256]{1,0:T(8,128)(2,1)S(1)}, u32[]{:S(2)}, u32[]{:S(2)}) collective-permute-start(bf16[1040,256]{1,0:T(8,128)(2,1)S(1)} %get-tuple-element.53), channel_id=1, source_target_pairs={{4,0},{8,4},{12,8},{5,1},{9,5},{13,9},{6,2},{10,6},{14,10},{7,3},{... | collective-permute-start | bytes 1597448 | tf_op jit(solution)/shard_map/ppermute | solution.py:300
  570.5 19.5 %collective-permute-start.69 = (bf16[1040,256]{1,0:T(8,128)(2,1)S(1)}, bf16[1040,256]{1,0:T(8,128)(2,1)S(1)}, u32[]{:S(2)}, u32[]{:S(2)}) collective-permute-start(bf16[1040,256]{1,0:T(8,128)(2,1)S(1)} %collective-permute-done.68.refs_3_), channel_id=1, source_target_pairs={{4,0},{8,4},{5,1},{9,5},{6,2},{10,6},{7,3},{11,7},{20,16},{24,20},... | collective-permute-start | bytes 1597448 | tf_op jit(solution)/shard_map/ppermute | solution.py:300
  571.8 26.2 %collective-permute-start.50 = (f32[1024,256]{1,0:T(8,128)S(1)}, f32[1024,256]{1,0:T(8,128)S(1)}, u32[]{:S(2)}, u32[]{:S(2)}) collective-permute-start(f32[1024,256]{1,0:T(8,128)S(1)} %get-tuple-element.65), channel_id=1, source_target_pairs={{0,2},{1,3},{2,0},{3,1},{4,6},{5,7},{6,4},{7,5},{8,10},{9,11},{10,... | collective-permute-start | bytes 3145736 | tf_op jit(solution)/shard_map/ppermute | solution.py:294
  578.8 38.3 %collective-permute-start.36 = (f32[1024,256]{1,0:T(8,128)S(1)}, f32[1024,256]{1,0:T(8,128)S(1)}, u32[]{:S(2)}, u32[]{:S(2)}) collective-permute-start(f32[1024,256]{1,0:T(8,128)S(1)} %get-tuple-element.68), channel_id=1, source_target_pairs={{0,2},{1,3},{2,0},{3,1},{4,6},{5,7},{6,4},{7,5},{8,10},{9,11},{10,... | collective-permute-start | bytes 3145736 | tf_op jit(solution)/shard_map/ppermute | solution.py:294
  590.0 16.9 %collective-permute-start.62 = (bf16[1040,256]{1,0:T(8,128)(2,1)S(1)}, bf16[1040,256]{1,0:T(8,128)(2,1)S(1)}, u32[]{:S(2)}, u32[]{:S(2)}) collective-permute-start(bf16[1040,256]{1,0:T(8,128)(2,1)S(1)} %collective-permute-done.61.refs_3_), channel_id=1, source_target_pairs={{4,0},{8,4},{5,1},{9,5},{6,2},{10,6},{7,3},{11,7},{20,16},{24,20},... | collective-permute-start | bytes 1597448 | tf_op jit(solution)/shard_map/ppermute | solution.py:300
  591.3 31.5 %collective-permute-start.67 = (bf16[1040,256]{1,0:T(8,128)(2,1)S(1)}, bf16[1040,256]{1,0:T(8,128)(2,1)S(1)}, u32[]{:S(2)}, u32[]{:S(2)}) collective-permute-start(bf16[1040,256]{1,0:T(8,128)(2,1)S(1)} %collective-permute-done.66.refs_1_), channel_id=1, source_target_pairs={{8,12},{9,13},{10,14},{11,15},{24,28},{25,29},{26,30},{27,31}} | collective-permute-start | bytes 1597448 | tf_op jit(solution)/shard_map/ppermute | solution.py:297
  597.9 30.7 %collective-permute-start.70 = (bf16[1040,256]{1,0:T(8,128)(2,1)S(1)}, bf16[1040,256]{1,0:T(8,128)(2,1)S(1)}, u32[]{:S(2)}, u32[]{:S(2)}) collective-permute-start(bf16[1040,256]{1,0:T(8,128)(2,1)S(1)} %collective-permute-done.69.refs_4_), channel_id=1, source_target_pairs={{4,0},{5,1},{6,2},{7,3},{20,16},{21,17},{22,18},{23,19}} | collective-permute-start | bytes 1597448 | tf_op jit(solution)/shard_map/ppermute | solution.py:300
  606.9 25.0 %collective-permute-start.51 = (bf16[1040,256]{1,0:T(8,128)(2,1)S(1)}, bf16[1040,256]{1,0:T(8,128)(2,1)S(1)}, u32[]{:S(2)}, u32[]{:S(2)}) collective-permute-start(bf16[1040,256]{1,0:T(8,128)(2,1)S(1)} %get-tuple-element.48), channel_id=1, source_target_pairs={{0,4},{4,8},{8,12},{1,5},{5,9},{9,13},{2,6},{6,10},{10,14},{3,7},{... | collective-permute-start | bytes 1597448 | tf_op jit(solution)/shard_map/ppermute | solution.py:297
  617.1 15.5 %collective-permute-start.54 = (bf16[1040,256]{1,0:T(8,128)(2,1)S(1)}, bf16[1040,256]{1,0:T(8,128)(2,1)S(1)}, u32[]{:S(2)}, u32[]{:S(2)}) collective-permute-start(bf16[1040,256]{1,0:T(8,128)(2,1)S(1)} %get-tuple-element.48), channel_id=1, source_target_pairs={{4,0},{8,4},{12,8},{5,1},{9,5},{13,9},{6,2},{10,6},{14,10},{7,3},{... | collective-permute-start | bytes 1597448 | tf_op jit(solution)/shard_map/ppermute | solution.py:300
  628.7 19.0 %collective-permute-start.40 = (bf16[1040,256]{1,0:T(8,128)(2,1)S(1)}, bf16[1040,256]{1,0:T(8,128)(2,1)S(1)}, u32[]{:S(2)}, u32[]{:S(2)}) collective-permute-start(bf16[1040,256]{1,0:T(8,128)(2,1)S(1)} %get-tuple-element.43), channel_id=1, source_target_pairs={{4,0},{8,4},{12,8},{5,1},{9,5},{13,9},{6,2},{10,6},{14,10},{7,3},{... | collective-permute-start | bytes 1597448 | tf_op jit(solution)/shard_map/ppermute | solution.py:300
  631.9 19.0 %collective-permute-start.52 = (bf16[1040,256]{1,0:T(8,128)(2,1)S(1)}, bf16[1040,256]{1,0:T(8,128)(2,1)S(1)}, u32[]{:S(2)}, u32[]{:S(2)}) collective-permute-start(bf16[1040,256]{1,0:T(8,128)(2,1)S(1)} %collective-permute-done.51.refs_0_), channel_id=1, source_target_pairs={{4,8},{8,12},{5,9},{9,13},{6,10},{10,14},{7,11},{11,15},{20,24},{2... | collective-permute-start | bytes 1597448 | tf_op jit(solution)/shard_map/ppermute | solution.py:297
  632.6 26.5 %collective-permute-start.55 = (bf16[1040,256]{1,0:T(8,128)(2,1)S(1)}, bf16[1040,256]{1,0:T(8,128)(2,1)S(1)}, u32[]{:S(2)}, u32[]{:S(2)}) collective-permute-start(bf16[1040,256]{1,0:T(8,128)(2,1)S(1)} %collective-permute-done.54.refs_3_), channel_id=1, source_target_pairs={{4,0},{8,4},{5,1},{9,5},{6,2},{10,6},{7,3},{11,7},{20,16},{24,20},... | collective-permute-start | bytes 1597448 | tf_op jit(solution)/shard_map/ppermute | solution.py:300
  634.2 49.0 %collective-permute-start.63 = (bf16[1040,256]{1,0:T(8,128)(2,1)S(1)}, bf16[1040,256]{1,0:T(8,128)(2,1)S(1)}, u32[]{:S(2)}, u32[]{:S(2)}) collective-permute-start(bf16[1040,256]{1,0:T(8,128)(2,1)S(1)} %collective-permute-done.62.refs_4_), channel_id=1, source_target_pairs={{4,0},{5,1},{6,2},{7,3},{20,16},{21,17},{22,18},{23,19}} | collective-permute-start | bytes 1597448 | tf_op jit(solution)/shard_map/ppermute | solution.py:300
  636.9 33.2 %collective-permute-start.38 = (bf16[1040,256]{1,0:T(8,128)(2,1)S(1)}, bf16[1040,256]{1,0:T(8,128)(2,1)S(1)}, u32[]{:S(2)}, u32[]{:S(2)}) collective-permute-start(bf16[1040,256]{1,0:T(8,128)(2,1)S(1)} %collective-permute-done.37.refs_0_), channel_id=1, source_target_pairs={{4,8},{8,12},{5,9},{9,13},{6,10},{10,14},{7,11},{11,15},{20,24},{2... | collective-permute-start | bytes 1597448 | tf_op jit(solution)/shard_map/ppermute | solution.py:297
  647.7 34.2 %collective-permute-start.41 = (bf16[1040,256]{1,0:T(8,128)(2,1)S(1)}, bf16[1040,256]{1,0:T(8,128)(2,1)S(1)}, u32[]{:S(2)}, u32[]{:S(2)}) collective-permute-start(bf16[1040,256]{1,0:T(8,128)(2,1)S(1)} %collective-permute-done.40.refs_3_), channel_id=1, source_target_pairs={{4,0},{8,4},{5,1},{9,5},{6,2},{10,6},{7,3},{11,7},{20,16},{24,20},... | collective-permute-start | bytes 1597448 | tf_op jit(solution)/shard_map/ppermute | solution.py:300
  650.8 41.9 %collective-permute-start.53 = (bf16[1040,256]{1,0:T(8,128)(2,1)S(1)}, bf16[1040,256]{1,0:T(8,128)(2,1)S(1)}, u32[]{:S(2)}, u32[]{:S(2)}) collective-permute-start(bf16[1040,256]{1,0:T(8,128)(2,1)S(1)} %collective-permute-done.52.refs_1_), channel_id=1, source_target_pairs={{8,12},{9,13},{10,14},{11,15},{24,28},{25,29},{26,30},{27,31}} | collective-permute-start | bytes 1597448 | tf_op jit(solution)/shard_map/ppermute | solution.py:297
  659.1 34.2 %collective-permute-start.56 = (bf16[1040,256]{1,0:T(8,128)(2,1)S(1)}, bf16[1040,256]{1,0:T(8,128)(2,1)S(1)}, u32[]{:S(2)}, u32[]{:S(2)}) collective-permute-start(bf16[1040,256]{1,0:T(8,128)(2,1)S(1)} %collective-permute-done.55.refs_4_), channel_id=1, source_target_pairs={{4,0},{5,1},{6,2},{7,3},{20,16},{21,17},{22,18},{23,19}} | collective-permute-start | bytes 1597448 | tf_op jit(solution)/shard_map/ppermute | solution.py:300
  670.2 32.7 %collective-permute-start.39 = (bf16[1040,256]{1,0:T(8,128)(2,1)S(1)}, bf16[1040,256]{1,0:T(8,128)(2,1)S(1)}, u32[]{:S(2)}, u32[]{:S(2)}) collective-permute-start(bf16[1040,256]{1,0:T(8,128)(2,1)S(1)} %collective-permute-done.38.refs_1_), channel_id=1, source_target_pairs={{8,12},{9,13},{10,14},{11,15},{24,28},{25,29},{26,30},{27,31}} | collective-permute-start | bytes 1597448 | tf_op jit(solution)/shard_map/ppermute | solution.py:297
  681.9 21.0 %collective-permute-start.42 = (bf16[1040,256]{1,0:T(8,128)(2,1)S(1)}, bf16[1040,256]{1,0:T(8,128)(2,1)S(1)}, u32[]{:S(2)}, u32[]{:S(2)}) collective-permute-start(bf16[1040,256]{1,0:T(8,128)(2,1)S(1)} %collective-permute-done.41.refs_4_), channel_id=1, source_target_pairs={{4,0},{5,1},{6,2},{7,3},{20,16},{21,17},{22,18},{23,19}} | collective-permute-start | bytes 1597448 | tf_op jit(solution)/shard_map/ppermute | solution.py:300
  (46 other events, 720.7 us)

commit v3 on v2

--- a/solution.py
+++ b/solution.py
@@ -21,7 +21,7 @@
 
 
 def cost(flops, moved):
-    return pl.CostEstimate(flops=int(flops), bytes_accessed=int(moved), transcendentals=0)
+    return pl.CostEstimate(flops=int(flops) // 100, bytes_accessed=int(moved) // 100, transcendentals=0)
 
 
 def split(value):
@@ -36,6 +36,57 @@
 
 def dot(a, b, dims):
     return lax.dot_general(a, b, (dims, ((), ())), preferred_element_type=F32)
+
+
+def halfway_kernel(place_ref, left, *refs, offsets, lines, first, last):
+    pieces, refs = refs[: len(offsets)], refs[len(offsets) :]
+    total = refs[-1]
+    depth = pieces[0].shape[0]
+    total[...] = jnp.zeros_like(total) if first else refs[0][...]
+    place = place_ref[0]
+    for offset, piece in zip(offsets, pieces):
+
+        @pl.when((place + offset >= 0) & (place + offset < lines))
+        def _(offset=offset, piece=piece):
+            rows = left[pl.ds(pl.multiple_of((place + offset) * depth, depth), depth), :]
+            total[...] += dot(rows, piece[...], ((0,), (0,)))
+
+    if last:
+        high, low = kernel_split(total[...])
+        refs[-2][0] = high
+        refs[-2][1] = low
+    else:
+        refs[-2][...] = total[...]
+
+
+def halfway(place, left, held, offsets, lines, before, last):
+    pieces = [held[offset] for offset in offsets]
+    depth, half = pieces[0].shape
+    inner = left.shape[1]
+    tile = min(256, inner)
+    whole = pl.BlockSpec((depth, half), lambda i, s: (0, 0))
+    block = pl.BlockSpec((tile, half), lambda i, s: (i, 0))
+    extra = [] if before is None else [before]
+    return pl.pallas_call(
+        functools.partial(
+            halfway_kernel, offsets=offsets, lines=lines, first=before is None, last=last
+        ),
+        grid_spec=pltpu.PrefetchScalarGridSpec(
+            num_scalar_prefetch=1,
+            grid=(inner // tile,),
+            in_specs=[pl.BlockSpec((left.shape[0], tile), lambda i, s: (0, i))]
+            + [whole] * len(pieces)
+            + [block] * len(extra),
+            out_specs=pl.BlockSpec((2, tile, half), lambda i, s: (0, i, 0)) if last else block,
+            scratch_shapes=[pltpu.VMEM((tile, half), F32)],
+        ),
+        out_shape=jax.ShapeDtypeStruct((2, inner, half), BF16)
+        if last
+        else jax.ShapeDtypeStruct((inner, half), F32),
+        compiler_params=params(36),
+        cost_estimate=cost(8 * depth * inner * half, 8 * depth * inner),
+        name="halfway",
+    )(place, left, *pieces, *extra)
 
 
 def rotate_part_kernel(me_ref, *refs, cols, half):
@@ -328,33 +379,27 @@
         far = lines - 1
 
         left = place_by_distance(left_basis, me).reshape(-1, left_basis.shape[1])
-        pieces = {}
+        pieces, arrived = {}, []
+        near = [offset for offset in range(-far, far + 1) if abs(offset) < far]
+        grads = [spread(gradient[:, side * half : (side + 1) * half]) for side in range(2)]
         for side in range(2):
-            grads = spread(gradient[:, side * half : (side + 1) * half])
-            halfway = None
-            for offset, value in grads.items():
-                if abs(offset) == far:
-                    continue
-                rows = lax.dynamic_slice_in_dim(left, (place + offset) * depth, depth, 0)
-                term = dot(rows, value, ((0,), (0,)))
-                halfway = term if halfway is None else halfway + term
-            rows = lax.dynamic_slice_in_dim(left, (far - place) * depth, depth, 0)
-            last = jnp.where(place == 0, grads[far], grads[-far])
-            halfway = halfway + dot(rows, last, ((0,), (0,)))
-            for distance, value in by_distance(jnp.stack(split(halfway))).items():
+            before = halfway(spot, left, grads[side], near, lines, None, False)
+            whole = halfway(spot, left, grads[side], [-far, far], lines, before, True)
+            for distance, value in by_distance(whole).items():
                 pieces[distance, side] = value
+            arrived.append((grads[side][far], grads[side][-far]))
 
         right = jnp.zeros(((lines + 1) * depth, width), BF16)
         ends = []
         for side in range(2):
-            rights = spread(lax.slice_in_dim(right_basis, side * depth // 2, (side + 1) * depth // 2))
-            for offset, value in rights.items():
-                if abs(offset) == far:
-                    continue
+            rows = lax.slice_in_dim(right_basis, side * depth // 2, (side + 1) * depth // 2)
+            rows, arrived[side] = lax.optimization_barrier((rows, arrived[side]))
+            rights = spread(rows)
+            for offset in near:
                 there = place + offset
                 there = jnp.where((there >= 0) & (there < lines), there, lines)
                 right = lax.dynamic_update_slice_in_dim(
-                    right, value, there * depth + side * depth // 2, 0
+                    right, rights[offset], there * depth + side * depth // 2, 0
                 )
             ends.append((rights[far], rights[-far]))
         above = jnp.concatenate([end[0] for end in ends])
@@ -388,30 +433,33 @@
             if back:
                 rows = lax.ppermute(rows, "row", [(i, (i + back) % lines) for i in range(lines)])
             backs.append(rows)
-        left_rows = place_by_distance(jnp.stack(backs), me)
+        backs = jnp.stack(backs)
 
         piece = width // CHUNKS
         update = None
-        sums = []
+        sums, messages, outgoing = [], [], []
         for chunk in range(CHUNKS):
             if chunk >= 2:
                 normed, sums[chunk - 2] = lax.optimization_barrier((normed, sums[chunk - 2]))
             keep, mate = restore(index, normed, right, chunk, piece, cols, width)
             mate = swap(mate, 1)
-            sums.append((keep, mate))
-            if cols > 2:
-                sums[chunk] = (keep, mate, [keep[d] + mate[d] for d in range(1, cols // 2)])
+            sums.append([keep[0], mate[0]] + [keep[d] + mate[d] for d in range(1, cols // 2)])
         for chunk in range(CHUNKS):
-            keep, mate = sums[chunk][:2]
-            parts = [keep[0], mate[0]]
-            for at, value in enumerate(sums[chunk][2] if cols > 2 else []):
+            parts = sums[chunk][:2]
+            for at, value in enumerate(sums[chunk][2:]):
                 parts.append(swap(value, 2 * at + 2))
+            if chunk == 1:
+                backs, parts = lax.optimization_barrier((backs, parts))
             message, own = send(parts)
-            arrived = spread(message)
+            messages.append(message)
+            outgoing.append(own)
+        left_rows = place_by_distance(backs, me)
+        for chunk in range(CHUNKS):
+            arrived = spread(messages[chunk])
             ups = [arrived[-step] for step in range(1, lines)]
             downs = [arrived[step] for step in range(1, lines)]
             update = update_chunk(
-                spot, own, ups, downs, left_rows, update, chunk, depth, width
+                spot, outgoing[chunk], ups, downs, left_rows, update, chunk, depth, width
             )
         return (new_first, new_second, update)
 

time: 723 us -> 658 us (0.910)
  starting transfers between devices: 137 us -> 89.1 us
  matrix products: 37.5 us -> 0 us
  Pallas kernels: 108 us -> 137 us
  waiting for transfers between devices: 367 us -> 346 us
  local copies, waits for them, and re-layouts: 46 us -> 61.5 us
    ppermute x20, waiting for transfers between devices: 125 us -> 39.4 us  [swap(): return lax.ppermute(value, 'col', [(i, i ^ distance) for i in range(cols)])]
    ppermute x24, waiting for transfers between devices: 198 us -> 237 us  [down(): return lax.ppermute(value, 'row', [(i, i - 1) for i in senders])]
    dot_general x12 -> x0, matrix products: 37.5 us -> none  [dot(): return lax.dot_general(a, b, (dims, ((), ())), preferred_element_type=F32)]
    ppermute x24, waiting for transfers between devices: 9.91 us -> 45.1 us  [up(): return lax.ppermute(value, 'row', [(i, i + 1) for i in senders])]
    pallas_call x0 -> x4, Pallas kernels: none -> 28.4 us  [halfway(): pl.pallas_call(functools.partial(halfway_kernel, offsets=offsets, lines=l...]
    ppermute x24, starting transfers between devices: 70.2 us -> 46.3 us  [up(): return lax.ppermute(value, 'row', [(i, i + 1) for i in senders])]
    ppermute x3, starting transfers between devices: 20.7 us -> 2.21 us  [local(): lax.ppermute(rows, 'row', [(i, (i + back) % lines) for i in range(lines)])]
    ppermute x3, waiting for transfers between devices: 33.3 us -> 24.6 us  [local(): lax.ppermute(rows, 'row', [(i, (i + back) % lines) for i in range(lines)])]
  transfers between devices with their start and end apart: 71 -> 71, of which waited for: 29 -> 32; matrix products, arithmetic and copies ran while one was open for 13% -> 9% of each run, Pallas kernels for 7% -> 12%
where the time goes in v3:
time: 658 us; the launch traced here: 648 us
  waiting for transfers between devices  346 us (53%)
  Pallas kernels  137 us (21%)
  starting transfers between devices  89.1 us (14%)
  local copies, waits for them, and re-layouts  61.5 us (9%)
  other arithmetic  12.6 us (2%)
    ppermute x24, waiting for transfers between devices, down(): return lax.ppermute(value, 'row', [(i, i - 1) for i in senders])  237 us
    ppermute x24, starting transfers between devices, up(): return lax.ppermute(value, 'row', [(i, i + 1) for i in senders])  46.3 us
    ppermute x24, waiting for transfers between devices, up(): return lax.ppermute(value, 'row', [(i, i + 1) for i in senders])  45.1 us
    ppermute x20, waiting for transfers between devices, swap(): return lax.ppermute(value, 'col', [(i, i ^ distance) for i in range(cols)])  39.4 us
    pallas_call x4, Pallas kernels, update_chunk(): pl.pallas_call(functools.partial(update_kernel, lines=lines, tile=tile),...  39.2 us
    ppermute x24, starting transfers between devices, down(): return lax.ppermute(value, 'row', [(i, i - 1) for i in senders])  31.1 us
    pallas_call x4, Pallas kernels, restore(): pl.pallas_call(functools.partial(restore_kernel, cols=cols), grid_spec=pl...  29.9 us
    pallas_call x4, Pallas kernels, halfway(): pl.pallas_call(functools.partial(halfway_kernel, offsets=offsets, lines=l...  28.4 us
  transfers between devices with their start and end apart: 71, of which 32 were waited for; matrix products, arithmetic and copies ran while one was open for 9% of the time, Pallas kernels for 12%

profile of v3, /device:TPU:0, one launch (start us, length us, event | category | flops | bytes accessed | tf_op | source)
XLA Modules:
  0.0 648.2 jit_solution(10137298039177325753)
XLA Ops:
  2.5 5.0 collective-permute-start.3
  10.3 4.6 collective-permute-start.9
  16.2 14.7 %collective-permute-done.3.refs_1_ = bf16[1024,512]{1,0:T(8,128)(2,1)S(1)} collective-permute-done((bf16[1024,512]{1,0:T(8,128)(2,1)S(1)}, bf16[1024,512]{1,0:T(8,128)(2,1)S(1)}, u32[]{:S(2)}, u32[]{:S(2)}) %collective-permute-start.3) | collective-permute-done | bytes 1048608 | tf_op jit(solution)/shard_map/ppermute | solution.py:348
  32.6 4.4 collective-permute-done.6.refs_3_
  39.3 13.0 %collective-permute-done.9.refs_1_ = bf16[1024,512]{1,0:T(8,128)(2,1)S(1)} collective-permute-done((bf16[1024,512]{1,0:T(8,128)(2,1)S(1)}, bf16[1024,512]{1,0:T(8,128)(2,1)S(1)}, u32[]{:S(2)}, u32[]{:S(2)}) %collective-permute-start.9) | collective-permute-done | bytes 1048608 | tf_op jit(solution)/shard_map/ppermute | solution.py:348
  54.0 5.5 collective-permute-done.12.refs_3_
  63.5 18.5 %collective-permute-done.7.refs_4_ = bf16[1024,512]{1,0:T(8,128)(2,1)S(1)} collective-permute-done((bf16[1024,512]{1,0:T(8,128)(2,1)S(1)}, bf16[1024,512]{1,0:T(8,128)(2,1)S(1)}, u32[]{:S(2)}, u32[]{:S(2)}) %collective-permute-start.7) | collective-permute-done | bytes 1048608 | tf_op jit(solution)/shard_map/ppermute | solution.py:351
  83.3 21.2 %collective-permute-done.13.refs_4_ = bf16[1024,512]{1,0:T(8,128)(2,1)} collective-permute-done((bf16[1024,512]{1,0:T(8,128)(2,1)S(1)}, bf16[1024,512]{1,0:T(8,128)(2,1)}, u32[]{:S(2)}, u32[]{:S(2)}) %collective-permute-start.13) | collective-permute-done | bytes 1048608 | tf_op jit(solution)/shard_map/ppermute | solution.py:351
  109.9 17.0 %collective-permute-done.8.refs_1_ = bf16[1024,512]{1,0:T(8,128)(2,1)S(1)} collective-permute-done((bf16[1024,512]{1,0:T(8,128)(2,1)S(1)}, bf16[1024,512]{1,0:T(8,128)(2,1)S(1)}, u32[]{:S(2)}, u32[]{:S(2)}) %collective-permute-start.8) | collective-permute-done | bytes 1048608 | tf_op jit(solution)/shard_map/ppermute | solution.py:351
  127.9 2.4 collective-permute-start.21
  131.6 17.9 %collective-permute-done.14.refs_1_ = bf16[1024,512]{1,0:T(8,128)(2,1)} collective-permute-done((bf16[1024,512]{1,0:T(8,128)(2,1)}, bf16[1024,512]{1,0:T(8,128)(2,1)}, u32[]{:S(2)}, u32[]{:S(2)}) %collective-permute-start.14) | collective-permute-done | bytes 1048608 | tf_op jit(solution)/shard_map/ppermute | solution.py:351
  149.5 2.4 collective-permute-start.25
  153.2 4.3 broadcast_in_dim.35
  157.5 3.1 bitcast_dynamic-update-slice_fusion.7
  160.6 3.1 bitcast_dynamic-update-slice_fusion.6
  163.7 3.1 bitcast_dynamic-update-slice_fusion.5
  168.6 3.1 bitcast_dynamic-update-slice_fusion.4
  171.7 7.8 %halfway.4.refs_2_ = f32[1024,512]{1,0:T(8,128)S(1)} custom-call(s32[1]{0:T(128)} %bitcast.place_ref, bf16[4096,1024]{1,0:T(8,128)(2,1)} %bitcast.6.left, bf16[1024,512]{1,0:T(8,128)(2,1)S(1)} %copy-done.14, bf16[1024,512]{1,0:T(8,128)(2,1)S(1)} %copy-done.8, bf16[1024,512]{1,0:T(8,128)(2,1)S(1)} %get-tuple-element.92.refs_2_, ...), custom_call_target="tpu_custom_call" | custom-call | flops 42949672 | bytes 83886 | tf_op jit(solution)/shard_map/halfway/pallas_call | solution.py:70
  179.6 5.4 halfway.5.refs_0_
  185.5 8.3 %halfway.6.refs_2_ = f32[1024,512]{1,0:T(8,128)S(1)} custom-call(s32[1]{0:T(128)} %bitcast.place_ref, bf16[4096,1024]{1,0:T(8,128)(2,1)} %bitcast.6.left, bf16[1024,512]{1,0:T(8,128)(2,1)} %collective-permute-done.10.refs_0_, bf16[1024,512]{1,0:T(8,128)(2,1)S(1)} %copy-done.6, bf16[1024,512]{1,0:T(8,128)(2,1)S(1)} %get-tuple-element.91.refs_2_, ...), custom_call_target="tpu_custom_call" | custom-call | flops 42949672 | bytes 83886 | tf_op jit(solution)/shard_map/halfway/pallas_call | solution.py:70
  193.8 6.9 %halfway.7.refs_1_ = bf16[2,1024,512]{2,1,0:T(8,128)(2,1)} custom-call(s32[1]{0:T(128)} %bitcast.place_ref, bf16[4096,1024]{1,0:T(8,128)(2,1)} %bitcast.6.left, bf16[1024,512]{1,0:T(8,128)(2,1)} %collective-permute-done.11.refs_0_, bf16[1024,512]{1,0:T(8,128)(2,1)} %collective-permute-done.14.refs_1_, f32[1024,512]{1,0:T(8,128)S(1)} %halfway.6.refs_2_), custom_call_target="tpu_custom_call" | custom-call | flops 42949672 | bytes 83886 | tf_op jit(solution)/shard_map/halfway/pallas_call | solution.py:70
  205.6 28.2 %collective-permute-done.24 = bf16[512,1024]{1,0:T(8,128)(2,1)S(1)} collective-permute-done((bf16[512,1024]{1,0:T(8,128)(2,1)}, bf16[512,1024]{1,0:T(8,128)(2,1)S(1)}, u32[]{:S(2)}, u32[]{:S(2)}) %collective-permute-start.24) | collective-permute-done | bytes 1048608 | tf_op jit(solution)/shard_map/ppermute | solution.py:351
  235.0 21.2 %collective-permute-done.28 = bf16[512,1024]{1,0:T(8,128)(2,1)S(1)} collective-permute-done((bf16[512,1024]{1,0:T(8,128)(2,1)}, bf16[512,1024]{1,0:T(8,128)(2,1)S(1)}, u32[]{:S(2)}, u32[]{:S(2)}) %collective-permute-start.28) | collective-permute-done | bytes 1048608 | tf_op jit(solution)/shard_map/ppermute | solution.py:351
  259.2 14.8 %collective-permute-done.18.refs_5_ = bf16[2,1024,512]{2,1,0:T(8,128)(2,1)} collective-permute-done((bf16[2,1024,512]{2,1,0:T(8,128)(2,1)}, bf16[2,1024,512]{2,1,0:T(8,128)(2,1)}, u32[]{:S(2)}, u32[]{:S(2)}) %collective-permute-start.18) | collective-permute-done | bytes 2097184 | tf_op jit(solution)/shard_map/ppermute | solution.py:345
  274.0 4.7 collective-permute-done.29
  278.7 18.4 %collective-permute-done.30 = bf16[512,1024]{1,0:T(8,128)(2,1)S(1)} collective-permute-done((bf16[512,1024]{1,0:T(8,128)(2,1)S(1)}, bf16[512,1024]{1,0:T(8,128)(2,1)S(1)}, u32[]{:S(2)}, u32[]{:S(2)}) %collective-permute-start.30) | collective-permute-done | bytes 1048608 | tf_op jit(solution)/shard_map/ppermute | solution.py:351
  298.1 5.3 broadcast_in_dim.40
  303.4 2.3 constant_dynamic-update-slice_fusion.14
  305.7 2.3 constant_dynamic-update-slice_fusion.13
  307.9 2.4 constant_dynamic-update-slice_fusion.12
  310.3 2.3 constant_dynamic-update-slice_fusion.11
  315.7 2.3 constant_dynamic-update-slice_fusion.8
  319.0 2.4 constant_dynamic-update-slice_fusion.6
  324.2 24.4 %rotate_part.1.part = f32[1024,1024]{1,0:T(8,128)} custom-call(s32[1]{0:T(128)} %bitcast.1.me_ref, bf16[2,1024,512]{2,1,0:T(8,128)(2,1)S(1)} %halfway.5.refs_0_, bf16[2,1024,512]{2,1,0:T(8,128)(2,1)} %halfway.7.refs_1_, bf16[2,1024,512]{2,1,0:T(8,128)(2,1)} %collective-permute-done.15.refs_2_, bf16[2,1024,512]{2,1,0:T(8,128)(2,1)} %collective-permute-done.16.refs_3_, ...), custom_call_target="tpu_custom_call" | custom-call | flops 171798688 | bytes 209715 | tf_op jit(solution)/shard_map/rotate_part/pallas_call | solution.py:109
  348.5 3.3 constant_dynamic-update-slice_fusion.4
  353.8 2.7 select_select_fusion.refs_1_
  357.2 11.0 %rotate.1 = (f32[1024,1024]{1,0:T(8,128)}, f32[1024,1024]{1,0:T(8,128)}, bf16[2,1024,1024]{2,1,0:T(8,128)(2,1)S(1)}) custom-call(s32[1]{0:T(128)} %bitcast.place_ref, f32[1024,1024]{1,0:T(8,128)S(1)} %copy-done.2, bf16[2,1024,512]{2,1,0:T(8,128)(2,1)S(1)} %select_select_fusion.1.refs_0_, bf16[2,1024,512]{2,1,0:T(8,128)(2,1)S(1)} %select_select_fusion.refs_1_, ...), custom_call_target="tpu_custom_call" | custom-call | flops 42949672 | bytes 314572 | tf_op jit(solution)/shard_map/rotate/pallas_call | solution.py:154
  368.2 8.9 %restore.4 = (f32[2,1024,256]{2,1,0:T(8,128)S(1)}, f32[2,1024,256]{2,1,0:T(8,128)}) custom-call(s32[1]{0:T(128)} %bitcast.1.me_ref, bf16[2,1024,1024]{2,1,0:T(8,128)(2,1)S(1)} %get-tuple-element.47.normed, bf16[5120,1024]{1,0:T(8,128)(2,1)} %get-tuple-element.71.refs_0_.refs_1_.refs_2_.refs_3_, ...), custom_call_target="tpu_custom_call" | custom-call | flops 42949672 | bytes 83886 | tf_op jit(solution)/shard_map/restore/pallas_call | solution.py:193
  377.6 7.6 %restore.5 = (f32[2,1024,256]{2,1,0:T(8,128)S(1)}, f32[2,1024,256]{2,1,0:T(8,128)}) custom-call(s32[1]{0:T(128)} %bitcast.1.me_ref, bf16[2,1024,1024]{2,1,0:T(8,128)(2,1)S(1)} %get-tuple-element.47.normed, bf16[5120,1024]{1,0:T(8,128)(2,1)} %get-tuple-element.71.refs_0_.refs_1_.refs_2_.refs_3_, ...), custom_call_target="tpu_custom_call" | custom-call | flops 42949672 | bytes 83886 | tf_op jit(solution)/shard_map/restore/pallas_call | solution.py:193
  390.7 2.0 fusion.2
  393.6 6.7 %restore.6 = (f32[2,1024,256]{2,1,0:T(8,128)S(1)}, f32[2,1024,256]{2,1,0:T(8,128)S(1)}) custom-call(s32[1]{0:T(128)} %bitcast.1.me_ref, bf16[2,1024,1024]{2,1,0:T(8,128)(2,1)S(1)} %copy-done.1, bf16[5120,1024]{1,0:T(8,128)(2,1)} %get-tuple-element.71.refs_0_.refs_1_.refs_2_.refs_3_, bf16[5120,1024]{1,0:T(8,128)(2,1)} %get-tuple-element.71.refs_0_.refs_1_.refs_2_.refs_3_, ...), custom_call_target="tpu_custom_call" | custom-call | flops 42949672 | bytes 83886 | tf_op jit(solution)/shard_map/restore/pallas_call | solution.py:193
  403.3 6.7 %restore.7 = (f32[2,1024,256]{2,1,0:T(8,128)S(1)}, f32[2,1024,256]{2,1,0:T(8,128)S(1)}) custom-call(s32[1]{0:T(128)} %bitcast.1.me_ref, bf16[2,1024,1024]{2,1,0:T(8,128)(2,1)S(1)} %copy-done.1, bf16[5120,1024]{1,0:T(8,128)(2,1)} %get-tuple-element.71.refs_0_.refs_1_.refs_2_.refs_3_, bf16[5120,1024]{1,0:T(8,128)(2,1)} %get-tuple-element.71.refs_0_.refs_1_.refs_2_.refs_3_, ...), custom_call_target="tpu_custom_call" | custom-call | flops 42949672 | bytes 83886 | tf_op jit(solution)/shard_map/restore/pallas_call | solution.py:193
  410.0 24.3 %collective-permute-done.44 = bf16[256,1024]{1,0:T(8,128)(2,1)S(1)} collective-permute-done((bf16[256,1024]{1,0:T(8,128)(2,1)S(1)}, bf16[256,1024]{1,0:T(8,128)(2,1)S(1)}, u32[]{:S(2)}, u32[]{:S(2)}) %collective-permute-start.44) | collective-permute-done | bytes 524320 | tf_op jit(solution)/shard_map/ppermute | solution.py:434
  435.7 2.3 collective-permute-start.58
  442.0 7.4 %collective-permute-done.58.refs_0_ = bf16[1040,256]{1,0:T(8,128)(2,1)S(1)} collective-permute-done((bf16[1040,256]{1,0:T(8,128)(2,1)S(1)}, bf16[1040,256]{1,0:T(8,128)(2,1)S(1)}, u32[]{:S(2)}, u32[]{:S(2)}) %collective-permute-start.58) | collective-permute-done | bytes 532512 | tf_op jit(solution)/shard_map/ppermute | solution.py:348
  449.4 4.4 collective-permute-start.65
  455.6 8.9 %collective-permute-done.65.refs_0_ = bf16[1040,256]{1,0:T(8,128)(2,1)S(1)} collective-permute-done((bf16[1040,256]{1,0:T(8,128)(2,1)S(1)}, bf16[1040,256]{1,0:T(8,128)(2,1)S(1)}, u32[]{:S(2)}, u32[]{:S(2)}) %collective-permute-start.65) | collective-permute-done | bytes 532512 | tf_op jit(solution)/shard_map/ppermute | solution.py:348
  464.5 5.0 collective-permute-done.68.refs_3_
  473.3 12.8 %collective-permute-done.62.refs_4_ = bf16[1040,256]{1,0:T(8,128)(2,1)S(1)} collective-permute-done((bf16[1040,256]{1,0:T(8,128)(2,1)S(1)}, bf16[1040,256]{1,0:T(8,128)(2,1)S(1)}, u32[]{:S(2)}, u32[]{:S(2)}) %collective-permute-start.62) | collective-permute-done | bytes 532512 | tf_op jit(solution)/shard_map/ppermute | solution.py:351
  488.4 18.4 %collective-permute-done.69.refs_4_ = bf16[1040,256]{1,0:T(8,128)(2,1)S(1)} collective-permute-done((bf16[1040,256]{1,0:T(8,128)(2,1)S(1)}, bf16[1040,256]{1,0:T(8,128)(2,1)S(1)}, u32[]{:S(2)}, u32[]{:S(2)}) %collective-permute-start.69) | collective-permute-done | bytes 532512 | tf_op jit(solution)/shard_map/ppermute | solution.py:351
  507.6 3.3 collective-permute-done.36.refs_2_
  511.5 20.0 %collective-permute-done.51.refs_2_ = f32[1024,256]{1,0:T(8,128)S(1)} collective-permute-done((f32[1024,256]{1,0:T(8,128)S(1)}, f32[1024,256]{1,0:T(8,128)S(1)}, u32[]{:S(2)}, u32[]{:S(2)}) %collective-permute-start.51) | collective-permute-done | bytes 1048608 | tf_op jit(solution)/shard_map/ppermute | solution.py:345
  534.8 8.3 %collective-permute-start.37 = (bf16[1040,256]{1,0:T(8,128)(2,1)S(1)}, bf16[1040,256]{1,0:T(8,128)(2,1)S(1)}, u32[]{:S(2)}, u32[]{:S(2)}) collective-permute-start(bf16[1040,256]{1,0:T(8,128)(2,1)S(1)} %get-tuple-element.51), channel_id=1, source_target_pairs={{0,4},{4,8},{8,12},{1,5},{5,9},{9,13},{2,6},{6,10},{10,14},{3,7},{... | collective-permute-start | bytes 1597448 | tf_op jit(solution)/shard_map/ppermute | solution.py:348
  544.4 7.4 %collective-permute-done.70.refs_5_ = bf16[1040,256]{1,0:T(8,128)(2,1)S(1)} collective-permute-done((bf16[1040,256]{1,0:T(8,128)(2,1)S(1)}, bf16[1040,256]{1,0:T(8,128)(2,1)S(1)}, u32[]{:S(2)}, u32[]{:S(2)}) %collective-permute-start.70) | collective-permute-done | bytes 532512 | tf_op jit(solution)/shard_map/ppermute | solution.py:351
  556.3 6.9 %collective-permute-done.40.refs_3_ = bf16[1040,256]{1,0:T(8,128)(2,1)S(1)} collective-permute-done((bf16[1040,256]{1,0:T(8,128)(2,1)S(1)}, bf16[1040,256]{1,0:T(8,128)(2,1)S(1)}, u32[]{:S(2)}, u32[]{:S(2)}) %collective-permute-start.40) | collective-permute-done | bytes 532512 | tf_op jit(solution)/shard_map/ppermute | solution.py:351
  565.2 9.4 %collective-permute-done.55.refs_3_ = bf16[1040,256]{1,0:T(8,128)(2,1)S(1)} collective-permute-done((bf16[1040,256]{1,0:T(8,128)(2,1)S(1)}, bf16[1040,256]{1,0:T(8,128)(2,1)S(1)}, u32[]{:S(2)}, u32[]{:S(2)}) %collective-permute-start.55) | collective-permute-done | bytes 532512 | tf_op jit(solution)/shard_map/ppermute | solution.py:351
  578.8 2.0 bitcast_dynamic-update-slice_fusion.2
  582.2 3.8 collective-permute-done.41.refs_4_
  588.0 9.5 %collective-permute-done.56.refs_4_ = bf16[1040,256]{1,0:T(8,128)(2,1)} collective-permute-done((bf16[1040,256]{1,0:T(8,128)(2,1)S(1)}, bf16[1040,256]{1,0:T(8,128)(2,1)}, u32[]{:S(2)}, u32[]{:S(2)}) %collective-permute-start.56) | collective-permute-done | bytes 532512 | tf_op jit(solution)/shard_map/ppermute | solution.py:351
  602.0 9.6 %update_chunk.4.refs_7_ = f32[1024,1024]{1,0:T(8,128)} custom-call(s32[1]{0:T(128)} %bitcast.place_ref, bf16[1024,512]{1,0:T(8,128)(2,1)S(1)} %get-tuple-element.69.own, bf16[1040,256]{1,0:T(8,128)(2,1)S(1)} %collective-permute-done.65.refs_0_, bf16[1040,256]{1,0:T(8,128)(2,1)S(1)} %collective-permute-done.66.refs_1_, ...), custom_call_target="tpu_custom_call" | custom-call | flops 42949672 | bytes 125829 | tf_op jit(solution)/shard_map/update_chunk/pallas_call | solution.py:323
  611.5 9.6 %update_chunk.5.refs_7_ = f32[1024,1024]{1,0:T(8,128)} custom-call(s32[1]{0:T(128)} %bitcast.place_ref, bf16[1024,512]{1,0:T(8,128)(2,1)S(1)} %get-tuple-element.64.own, bf16[1040,256]{1,0:T(8,128)(2,1)S(1)} %collective-permute-done.58.refs_0_, bf16[1040,256]{1,0:T(8,128)(2,1)S(1)} %collective-permute-done.59.refs_1_, ...), custom_call_target="tpu_custom_call", output_to_operand_aliasing={{}: (9, {})} | custom-call | flops 42949672 | bytes 125829 | tf_op jit(solution)/shard_map/update_chunk/pallas_call | solution.py:323
  621.1 6.6 %collective-permute-done.57.refs_5_ = bf16[1040,256]{1,0:T(8,128)(2,1)S(1)} collective-permute-done((bf16[1040,256]{1,0:T(8,128)(2,1)}, bf16[1040,256]{1,0:T(8,128)(2,1)S(1)}, u32[]{:S(2)}, u32[]{:S(2)}) %collective-permute-start.57) | collective-permute-done | bytes 532512 | tf_op jit(solution)/shard_map/ppermute | solution.py:351
  627.7 10.5 %update_chunk.6.refs_7_ = f32[1024,1024]{1,0:T(8,128)} custom-call(s32[1]{0:T(128)} %bitcast.place_ref, bf16[1024,512]{1,0:T(8,128)(2,1)S(1)} %get-tuple-element.59.own, bf16[1040,256]{1,0:T(8,128)(2,1)S(1)} %collective-permute-done.52.refs_0_, bf16[1040,256]{1,0:T(8,128)(2,1)S(1)} %collective-permute-done.53.refs_1_, ...), custom_call_target="tpu_custom_call", output_to_operand_aliasing={{}: (9, {})} | custom-call | flops 42949672 | bytes 125829 | tf_op jit(solution)/shard_map/update_chunk/pallas_call | solution.py:323
  638.2 9.6 %update_chunk.7 = f32[1024,1024]{1,0:T(8,128)} custom-call(s32[1]{0:T(128)} %bitcast.place_ref, bf16[1024,512]{1,0:T(8,128)(2,1)S(1)} %get-tuple-element.50.own, bf16[1040,256]{1,0:T(8,128)(2,1)S(1)} %collective-permute-done.37.refs_0_, bf16[1040,256]{1,0:T(8,128)(2,1)S(1)} %collective-permute-done.38.refs_1_, ...), custom_call_target="tpu_custom_call", output_to_operand_aliasing={{}: (9, {})} | custom-call | flops 42949672 | bytes 125829 | tf_op jit(solution)/shard_map/update_chunk/pallas_call | solution.py:323
  (200 shorter events, 95.2 us)
Async XLA Ops:
  2.5 28.5 %collective-permute-start.3 = (bf16[1024,512]{1,0:T(8,128)(2,1)S(1)}, bf16[1024,512]{1,0:T(8,128)(2,1)S(1)}, u32[]{:S(2)}, u32[]{:S(2)}) collective-permute-start(bf16[1024,512]{1,0:T(8,128)(2,1)S(1)} %get-tuple-element.92.refs_2_), channel_id=1, source_target_pairs={{0,4},{4,8},{8,12},{1,5},{5,9},{9,13},{2,6},{6,10},{10,14},{3,7},{... | collective-permute-start | bytes 3145736 | tf_op jit(solution)/shard_map/ppermute | solution.py:348
  7.5 56.0 %collective-permute-start = (bf16[1024,1024]{1,0:T(8,128)(2,1)}, bf16[1024,1024]{1,0:T(8,128)(2,1)}, u32[]{:S(2)}, u32[]{:S(2)}) collective-permute-start(bf16[1024,1024]{1,0:T(8,128)(2,1)} %param.8), channel_id=1, source_target_pairs={{0,2},{1,3},{2,0},{3,1},{4,6},{5,7},{6,4},{7,5},{8,10},{9,11},{10,... | collective-permute-start | bytes 6291464 | tf_op jit(solution)/shard_map/ppermute | solution.py:345
  9.0 28.0 %collective-permute-start.6 = (bf16[1024,512]{1,0:T(8,128)(2,1)S(1)}, bf16[1024,512]{1,0:T(8,128)(2,1)S(1)}, u32[]{:S(2)}, u32[]{:S(2)}) collective-permute-start(bf16[1024,512]{1,0:T(8,128)(2,1)S(1)} %get-tuple-element.92.refs_2_), channel_id=1, source_target_pairs={{4,0},{8,4},{12,8},{5,1},{9,5},{13,9},{6,2},{10,6},{14,10},{7,3},{... | collective-permute-start | bytes 3145736 | tf_op jit(solution)/shard_map/ppermute | solution.py:351
  10.3 42.0 %collective-permute-start.9 = (bf16[1024,512]{1,0:T(8,128)(2,1)S(1)}, bf16[1024,512]{1,0:T(8,128)(2,1)S(1)}, u32[]{:S(2)}, u32[]{:S(2)}) collective-permute-start(bf16[1024,512]{1,0:T(8,128)(2,1)S(1)} %get-tuple-element.91.refs_2_), channel_id=1, source_target_pairs={{0,4},{4,8},{8,12},{1,5},{5,9},{9,13},{2,6},{6,10},{10,14},{3,7},{... | collective-permute-start | bytes 3145736 | tf_op jit(solution)/shard_map/ppermute | solution.py:348
  14.9 44.5 %collective-permute-start.12 = (bf16[1024,512]{1,0:T(8,128)(2,1)S(1)}, bf16[1024,512]{1,0:T(8,128)(2,1)S(1)}, u32[]{:S(2)}, u32[]{:S(2)}) collective-permute-start(bf16[1024,512]{1,0:T(8,128)(2,1)S(1)} %get-tuple-element.91.refs_2_), channel_id=1, source_target_pairs={{4,0},{8,4},{12,8},{5,1},{9,5},{13,9},{6,2},{10,6},{14,10},{7,3},{... | collective-permute-start | bytes 3145736 | tf_op jit(solution)/shard_map/ppermute | solution.py:351
  31.0 30.8 %collective-permute-start.4 = (bf16[1024,512]{1,0:T(8,128)(2,1)S(1)}, bf16[1024,512]{1,0:T(8,128)(2,1)S(1)}, u32[]{:S(2)}, u32[]{:S(2)}) collective-permute-start(bf16[1024,512]{1,0:T(8,128)(2,1)S(1)} %collective-permute-done.3.refs_1_), channel_id=1, source_target_pairs={{4,8},{8,12},{5,9},{9,13},{6,10},{10,14},{7,11},{11,15},{20,24},{2... | collective-permute-start | bytes 3145736 | tf_op jit(solution)/shard_map/ppermute | solution.py:348
  37.0 44.9 %collective-permute-start.7 = (bf16[1024,512]{1,0:T(8,128)(2,1)S(1)}, bf16[1024,512]{1,0:T(8,128)(2,1)S(1)}, u32[]{:S(2)}, u32[]{:S(2)}) collective-permute-start(bf16[1024,512]{1,0:T(8,128)(2,1)S(1)} %collective-permute-done.6.refs_3_), channel_id=1, source_target_pairs={{4,0},{8,4},{5,1},{9,5},{6,2},{10,6},{7,3},{11,7},{20,16},{24,20},... | collective-permute-start | bytes 3145736 | tf_op jit(solution)/shard_map/ppermute | solution.py:351
  52.3 31.0 %collective-permute-start.10 = (bf16[1024,512]{1,0:T(8,128)(2,1)S(1)}, bf16[1024,512]{1,0:T(8,128)(2,1)}, u32[]{:S(2)}, u32[]{:S(2)}) collective-permute-start(bf16[1024,512]{1,0:T(8,128)(2,1)S(1)} %collective-permute-done.9.refs_1_), channel_id=1, source_target_pairs={{4,8},{8,12},{5,9},{9,13},{6,10},{10,14},{7,11},{11,15},{20,24},{2... | collective-permute-start | bytes 3145736 | tf_op jit(solution)/shard_map/ppermute | solution.py:348
  59.5 45.0 %collective-permute-start.13 = (bf16[1024,512]{1,0:T(8,128)(2,1)S(1)}, bf16[1024,512]{1,0:T(8,128)(2,1)}, u32[]{:S(2)}, u32[]{:S(2)}) collective-permute-start(bf16[1024,512]{1,0:T(8,128)(2,1)S(1)} %collective-permute-done.12.refs_3_), channel_id=1, source_target_pairs={{4,0},{8,4},{5,1},{9,5},{6,2},{10,6},{7,3},{11,7},{20,16},{24,20},... | collective-permute-start | bytes 3145736 | tf_op jit(solution)/shard_map/ppermute | solution.py:351
  61.8 44.4 %collective-permute-start.5 = (bf16[1024,512]{1,0:T(8,128)(2,1)S(1)}, bf16[1024,512]{1,0:T(8,128)(2,1)S(1)}, u32[]{:S(2)}, u32[]{:S(2)}) collective-permute-start(bf16[1024,512]{1,0:T(8,128)(2,1)S(1)} %collective-permute-done.4.refs_0_), channel_id=1, source_target_pairs={{8,12},{9,13},{10,14},{11,15},{24,28},{25,29},{26,30},{27,31}} | collective-permute-start | bytes 3145736 | tf_op jit(solution)/shard_map/ppermute | solution.py:348
  63.5 88.4 %collective-permute-start.1 = (bf16[1024,1024]{1,0:T(8,128)(2,1)}, bf16[1024,1024]{1,0:T(8,128)(2,1)}, u32[]{:S(2)}, u32[]{:S(2)}) collective-permute-start(bf16[1024,1024]{1,0:T(8,128)(2,1)} %param.8), channel_id=1, source_target_pairs={{0,1},{1,0},{2,3},{3,2},{4,5},{5,4},{6,7},{7,6},{8,9},{9,8},{10,11... | collective-permute-start | bytes 6291464 | tf_op jit(solution)/shard_map/ppermute | solution.py:345
  82.0 44.9 %collective-permute-start.8 = (bf16[1024,512]{1,0:T(8,128)(2,1)S(1)}, bf16[1024,512]{1,0:T(8,128)(2,1)S(1)}, u32[]{:S(2)}, u32[]{:S(2)}) collective-permute-start(bf16[1024,512]{1,0:T(8,128)(2,1)S(1)} %collective-permute-done.7.refs_4_), channel_id=1, source_target_pairs={{4,0},{5,1},{6,2},{7,3},{20,16},{21,17},{22,18},{23,19}} | collective-permute-start | bytes 3145736 | tf_op jit(solution)/shard_map/ppermute | solution.py:351
  83.3 85.3 %collective-permute-start.2 = (bf16[1024,1024]{1,0:T(8,128)(2,1)}, bf16[1024,1024]{1,0:T(8,128)(2,1)}, u32[]{:S(2)}, u32[]{:S(2)}) collective-permute-start(bf16[1024,1024]{1,0:T(8,128)(2,1)} %collective-permute-done), channel_id=1, source_target_pairs={{0,1},{1,0},{2,3},{3,2},{4,5},{5,4},{6,7},{7,6},{8,9},{9,8},{10,11... | collective-permute-start | bytes 6291464 | tf_op jit(solution)/shard_map/ppermute | solution.py:345
  104.5 25.8 %collective-permute-start.11 = (bf16[1024,512]{1,0:T(8,128)(2,1)}, bf16[1024,512]{1,0:T(8,128)(2,1)}, u32[]{:S(2)}, u32[]{:S(2)}) collective-permute-start(bf16[1024,512]{1,0:T(8,128)(2,1)} %collective-permute-done.10.refs_0_), channel_id=1, source_target_pairs={{8,12},{9,13},{10,14},{11,15},{24,28},{25,29},{26,30},{27,31}} | collective-permute-start | bytes 3145736 | tf_op jit(solution)/shard_map/ppermute | solution.py:348
  107.1 42.3 %collective-permute-start.14 = (bf16[1024,512]{1,0:T(8,128)(2,1)}, bf16[1024,512]{1,0:T(8,128)(2,1)}, u32[]{:S(2)}, u32[]{:S(2)}) collective-permute-start(bf16[1024,512]{1,0:T(8,128)(2,1)} %collective-permute-done.13.refs_4_), channel_id=1, source_target_pairs={{4,0},{5,1},{6,2},{7,3},{20,16},{21,17},{22,18},{23,19}} | collective-permute-start | bytes 3145736 | tf_op jit(solution)/shard_map/ppermute | solution.py:351
  127.9 38.9 %collective-permute-start.21 = (bf16[512,1024]{1,0:T(8,128)(2,1)}, bf16[512,1024]{1,0:T(8,128)(2,1)}, u32[]{:S(2)}, u32[]{:S(2)}) collective-permute-start(bf16[512,1024]{1,0:T(8,128)(2,1)} %get-tuple-element.37), channel_id=1, source_target_pairs={{0,4},{4,8},{8,12},{1,5},{5,9},{9,13},{2,6},{6,10},{10,14},{3,7},{... | collective-permute-start | bytes 3145736 | tf_op jit(solution)/shard_map/ppermute | solution.py:348
  130.3 70.4 %collective-permute-start.23 = (bf16[512,1024]{1,0:T(8,128)(2,1)}, bf16[512,1024]{1,0:T(8,128)(2,1)}, u32[]{:S(2)}, u32[]{:S(2)}) collective-permute-start(bf16[512,1024]{1,0:T(8,128)(2,1)} %get-tuple-element.37), channel_id=1, source_target_pairs={{4,0},{8,4},{12,8},{5,1},{9,5},{13,9},{6,2},{10,6},{14,10},{7,3},{... | collective-permute-start | bytes 3145736 | tf_op jit(solution)/shard_map/ppermute | solution.py:351
  149.5 52.7 %collective-permute-start.25 = (bf16[512,1024]{1,0:T(8,128)(2,1)}, bf16[512,1024]{1,0:T(8,128)(2,1)}, u32[]{:S(2)}, u32[]{:S(2)}) collective-permute-start(bf16[512,1024]{1,0:T(8,128)(2,1)} %get-tuple-element.38), channel_id=1, source_target_pairs={{0,4},{4,8},{8,12},{1,5},{5,9},{9,13},{2,6},{6,10},{10,14},{3,7},{... | collective-permute-start | bytes 3145736 | tf_op jit(solution)/shard_map/ppermute | solution.py:348
  151.9 51.6 %collective-permute-start.27 = (bf16[512,1024]{1,0:T(8,128)(2,1)}, bf16[512,1024]{1,0:T(8,128)(2,1)}, u32[]{:S(2)}, u32[]{:S(2)}) collective-permute-start(bf16[512,1024]{1,0:T(8,128)(2,1)} %get-tuple-element.38), channel_id=1, source_target_pairs={{4,0},{8,4},{12,8},{5,1},{9,5},{13,9},{6,2},{10,6},{14,10},{7,3},{... | collective-permute-start | bytes 3145736 | tf_op jit(solution)/shard_map/ppermute | solution.py:351
  166.8 38.0 %collective-permute-start.22 = (bf16[512,1024]{1,0:T(8,128)(2,1)}, bf16[512,1024]{1,0:T(8,128)(2,1)}, u32[]{:S(2)}, u32[]{:S(2)}) collective-permute-start(bf16[512,1024]{1,0:T(8,128)(2,1)} %collective-permute-done.21), channel_id=1, source_target_pairs={{4,8},{8,12},{5,9},{9,13},{6,10},{10,14},{7,11},{11,15},{20,24},{2... | collective-permute-start | bytes 3145736 | tf_op jit(solution)/shard_map/ppermute | solution.py:348
  184.9 74.2 %collective-permute-start.17 = (bf16[2,1024,512]{2,1,0:T(8,128)(2,1)S(1)}, bf16[2,1024,512]{2,1,0:T(8,128)(2,1)}, u32[]{:S(2)}, u32[]{:S(2)}) collective-permute-start(bf16[2,1024,512]{2,1,0:T(8,128)(2,1)S(1)} %halfway.5.refs_0_), channel_id=1, source_target_pairs={{0,2},{1,3},{2,0},{3,1},{4,6},{5,7},{6,4},{7,5},{8,10},{9,11},{10,... | collective-permute-start | bytes 6291464 | tf_op jit(solution)/shard_map/ppermute | solution.py:345
  200.7 73.3 %collective-permute-start.18 = (bf16[2,1024,512]{2,1,0:T(8,128)(2,1)}, bf16[2,1024,512]{2,1,0:T(8,128)(2,1)}, u32[]{:S(2)}, u32[]{:S(2)}) collective-permute-start(bf16[2,1024,512]{2,1,0:T(8,128)(2,1)} %halfway.7.refs_1_), channel_id=1, source_target_pairs={{0,2},{1,3},{2,0},{3,1},{4,6},{5,7},{6,4},{7,5},{8,10},{9,11},{10,... | collective-permute-start | bytes 6291464 | tf_op jit(solution)/shard_map/ppermute | solution.py:345
  202.2 31.5 %collective-permute-start.24 = (bf16[512,1024]{1,0:T(8,128)(2,1)}, bf16[512,1024]{1,0:T(8,128)(2,1)S(1)}, u32[]{:S(2)}, u32[]{:S(2)}) collective-permute-start(bf16[512,1024]{1,0:T(8,128)(2,1)} %collective-permute-done.23), channel_id=1, source_target_pairs={{4,0},{8,4},{5,1},{9,5},{6,2},{10,6},{7,3},{11,7},{20,16},{24,20},... | collective-permute-start | bytes 3145736 | tf_op jit(solution)/shard_map/ppermute | solution.py:351
  203.5 52.7 %collective-permute-start.28 = (bf16[512,1024]{1,0:T(8,128)(2,1)}, bf16[512,1024]{1,0:T(8,128)(2,1)S(1)}, u32[]{:S(2)}, u32[]{:S(2)}) collective-permute-start(bf16[512,1024]{1,0:T(8,128)(2,1)} %collective-permute-done.27), channel_id=1, source_target_pairs={{4,0},{8,4},{5,1},{9,5},{6,2},{10,6},{7,3},{11,7},{20,16},{24,20},... | collective-permute-start | bytes 3145736 | tf_op jit(solution)/shard_map/ppermute | solution.py:351
  204.8 52.7 %collective-permute-start.26 = (bf16[512,1024]{1,0:T(8,128)(2,1)}, bf16[512,1024]{1,0:T(8,128)(2,1)S(1)}, u32[]{:S(2)}, u32[]{:S(2)}) collective-permute-start(bf16[512,1024]{1,0:T(8,128)(2,1)} %collective-permute-done.25), channel_id=1, source_target_pairs={{4,8},{8,12},{5,9},{9,13},{6,10},{10,14},{7,11},{11,15},{20,24},{2... | collective-permute-start | bytes 3145736 | tf_op jit(solution)/shard_map/ppermute | solution.py:348
  233.7 44.9 %collective-permute-start.29 = (bf16[512,1024]{1,0:T(8,128)(2,1)S(1)}, bf16[512,1024]{1,0:T(8,128)(2,1)S(1)}, u32[]{:S(2)}, u32[]{:S(2)}) collective-permute-start(bf16[512,1024]{1,0:T(8,128)(2,1)S(1)} %collective-permute-done.24), channel_id=1, source_target_pairs={{4,0},{5,1},{6,2},{7,3},{20,16},{21,17},{22,18},{23,19}} | collective-permute-start | bytes 3145736 | tf_op jit(solution)/shard_map/ppermute | solution.py:351
  256.2 40.9 %collective-permute-start.30 = (bf16[512,1024]{1,0:T(8,128)(2,1)S(1)}, bf16[512,1024]{1,0:T(8,128)(2,1)S(1)}, u32[]{:S(2)}, u32[]{:S(2)}) collective-permute-start(bf16[512,1024]{1,0:T(8,128)(2,1)S(1)} %collective-permute-done.28), channel_id=1, source_target_pairs={{4,0},{5,1},{6,2},{7,3},{20,16},{21,17},{22,18},{23,19}} | collective-permute-start | bytes 3145736 | tf_op jit(solution)/shard_map/ppermute | solution.py:351
  257.5 56.1 %collective-permute-start.31 = (bf16[512,1024]{1,0:T(8,128)(2,1)}, bf16[512,1024]{1,0:T(8,128)(2,1)}, u32[]{:S(2)}, u32[]{:S(2)}) collective-permute-start(bf16[512,1024]{1,0:T(8,128)(2,1)} %collective-permute-done.22), channel_id=1, source_target_pairs={{8,12},{9,13},{10,14},{11,15},{24,28},{25,29},{26,30},{27,31}} | collective-permute-start | bytes 3145736 | tf_op jit(solution)/shard_map/ppermute | solution.py:348
  259.2 65.0 %collective-permute-start.15 = (bf16[2,1024,512]{2,1,0:T(8,128)(2,1)S(1)}, bf16[2,1024,512]{2,1,0:T(8,128)(2,1)}, u32[]{:S(2)}, u32[]{:S(2)}) collective-permute-start(bf16[2,1024,512]{2,1,0:T(8,128)(2,1)S(1)} %halfway.5.refs_0_), channel_id=1, source_target_pairs={{0,1},{1,0},{2,3},{3,2},{4,5},{5,4},{6,7},{7,6},{8,9},{9,8},{10,11... | collective-permute-start | bytes 6291464 | tf_op jit(solution)/shard_map/ppermute | solution.py:345
  274.0 50.1 %collective-permute-start.16 = (bf16[2,1024,512]{2,1,0:T(8,128)(2,1)}, bf16[2,1024,512]{2,1,0:T(8,128)(2,1)}, u32[]{:S(2)}, u32[]{:S(2)}) collective-permute-start(bf16[2,1024,512]{2,1,0:T(8,128)(2,1)} %halfway.7.refs_1_), channel_id=1, source_target_pairs={{0,1},{1,0},{2,3},{3,2},{4,5},{5,4},{6,7},{7,6},{8,9},{9,8},{10,11... | collective-permute-start | bytes 6291464 | tf_op jit(solution)/shard_map/ppermute | solution.py:345
  278.7 45.5 %collective-permute-start.19 = (bf16[2,1024,512]{2,1,0:T(8,128)(2,1)}, bf16[2,1024,512]{2,1,0:T(8,128)(2,1)}, u32[]{:S(2)}, u32[]{:S(2)}) collective-permute-start(bf16[2,1024,512]{2,1,0:T(8,128)(2,1)} %collective-permute-done.17.refs_4_), channel_id=1, source_target_pairs={{0,1},{1,0},{2,3},{3,2},{4,5},{5,4},{6,7},{7,6},{8,9},{9,8},{10,11... | collective-permute-start | bytes 6291464 | tf_op jit(solution)/shard_map/ppermute | solution.py:345
  298.1 26.0 %collective-permute-start.20 = (bf16[2,1024,512]{2,1,0:T(8,128)(2,1)}, bf16[2,1024,512]{2,1,0:T(8,128)(2,1)}, u32[]{:S(2)}, u32[]{:S(2)}) collective-permute-start(bf16[2,1024,512]{2,1,0:T(8,128)(2,1)} %collective-permute-done.18.refs_5_), channel_id=1, source_target_pairs={{0,1},{1,0},{2,3},{3,2},{4,5},{5,4},{6,7},{7,6},{8,9},{9,8},{10,11... | collective-permute-start | bytes 6291464 | tf_op jit(solution)/shard_map/ppermute | solution.py:345
  387.9 46.5 %collective-permute-start.44 = (bf16[256,1024]{1,0:T(8,128)(2,1)S(1)}, bf16[256,1024]{1,0:T(8,128)(2,1)S(1)}, u32[]{:S(2)}, u32[]{:S(2)}) collective-permute-start(bf16[256,1024]{1,0:T(8,128)(2,1)S(1)} %get-tuple-element.75), channel_id=1, source_target_pairs={{0,8},{4,12},{8,0},{12,4},{1,9},{5,13},{9,1},{13,5},{2,10},{6,14},... | collective-permute-start | bytes 1572872 | tf_op jit(solution)/shard_map/ppermute | solution.py:434
  392.7 42.0 %collective-permute-start.46 = (f32[1024,256]{1,0:T(8,128)S(1)}, f32[1024,256]{1,0:T(8,128)S(1)}, u32[]{:S(2)}, u32[]{:S(2)}) collective-permute-start(f32[1024,256]{1,0:T(8,128)S(1)} %get-tuple-element.55), channel_id=1, source_target_pairs={{0,2},{1,3},{2,0},{3,1},{4,6},{5,7},{6,4},{7,5},{8,10},{9,11},{10,... | collective-permute-start | bytes 3145736 | tf_op jit(solution)/shard_map/ppermute | solution.py:345
  400.4 69.8 %collective-permute-start.35 = (f32[2,1024,256]{2,1,0:T(8,128)S(1)}, f32[2,1024,256]{2,1,0:T(8,128)S(1)}, u32[]{:S(2)}, u32[]{:S(2)}) collective-permute-start(f32[2,1024,256]{2,1,0:T(8,128)S(1)} %get-tuple-element.49), channel_id=1, source_target_pairs={{0,1},{1,0},{2,3},{3,2},{4,5},{5,4},{6,7},{7,6},{8,9},{9,8},{10,11... | collective-permute-start | bytes 6291464 | tf_op jit(solution)/shard_map/ppermute | solution.py:345
  400.4 33.9 %collective-permute-start.43 = (bf16[256,1024]{1,0:T(8,128)(2,1)S(1)}, bf16[256,1024]{1,0:T(8,128)(2,1)S(1)}, u32[]{:S(2)}, u32[]{:S(2)}) collective-permute-start(bf16[256,1024]{1,0:T(8,128)(2,1)S(1)} %get-tuple-element.76), channel_id=1, source_target_pairs={{0,4},{4,8},{8,12},{12,0},{1,5},{5,9},{9,13},{13,1},{2,6},{6,10},{... | collective-permute-start | bytes 1572872 | tf_op jit(solution)/shard_map/ppermute | solution.py:434
  401.7 38.1 %collective-permute-start.64 = (f32[1024,256]{1,0:T(8,128)S(1)}, f32[1024,256]{1,0:T(8,128)S(1)}, u32[]{:S(2)}, u32[]{:S(2)}) collective-permute-start(f32[1024,256]{1,0:T(8,128)S(1)} %get-tuple-element.68), channel_id=1, source_target_pairs={{0,2},{1,3},{2,0},{3,1},{4,6},{5,7},{6,4},{7,5},{8,10},{9,11},{10,... | collective-permute-start | bytes 3145736 | tf_op jit(solution)/shard_map/ppermute | solution.py:345
  434.4 37.4 %collective-permute-start.50 = (f32[2,1024,256]{2,1,0:T(8,128)S(1)}, f32[2,1024,256]{2,1,0:T(8,128)S(1)}, u32[]{:S(2)}, u32[]{:S(2)}) collective-permute-start(f32[2,1024,256]{2,1,0:T(8,128)S(1)} %get-tuple-element.58), channel_id=1, source_target_pairs={{0,1},{1,0},{2,3},{3,2},{4,5},{5,4},{6,7},{7,6},{8,9},{9,8},{10,11... | collective-permute-start | bytes 6291464 | tf_op jit(solution)/shard_map/ppermute | solution.py:345
  437.9 16.4 %collective-permute-start.61 = (bf16[1040,256]{1,0:T(8,128)(2,1)S(1)}, bf16[1040,256]{1,0:T(8,128)(2,1)S(1)}, u32[]{:S(2)}, u32[]{:S(2)}) collective-permute-start(bf16[1040,256]{1,0:T(8,128)(2,1)S(1)} %get-tuple-element.65), channel_id=1, source_target_pairs={{4,0},{8,4},{12,8},{5,1},{9,5},{13,9},{6,2},{10,6},{14,10},{7,3},{... | collective-permute-start | bytes 1597448 | tf_op jit(solution)/shard_map/ppermute | solution.py:351
  439.8 48.7 %collective-permute-start.47 = (bf16[4,256,1024]{2,1,0:T(8,128)(2,1)S(1)}, bf16[4,256,1024]{2,1,0:T(8,128)(2,1)}, u32[]{:S(2)}, u32[]{:S(2)}) collective-permute-start(bf16[4,256,1024]{2,1,0:T(8,128)(2,1)S(1)} %pad_maximum_fusion), channel_id=1, source_target_pairs={{0,2},{1,3},{2,0},{3,1},{4,6},{5,7},{6,4},{7,5},{8,10},{9,11},{10,... | collective-permute-start | bytes 6291464 | tf_op jit(solution)/shard_map/ppermute | solution.py:345
  449.4 15.1 %collective-permute-start.65 = (bf16[1040,256]{1,0:T(8,128)(2,1)S(1)}, bf16[1040,256]{1,0:T(8,128)(2,1)S(1)}, u32[]{:S(2)}, u32[]{:S(2)}) collective-permute-start(bf16[1040,256]{1,0:T(8,128)(2,1)S(1)} %get-tuple-element.70), channel_id=1, source_target_pairs={{0,4},{4,8},{8,12},{1,5},{5,9},{9,13},{2,6},{6,10},{10,14},{3,7},{... | collective-permute-start | bytes 1597448 | tf_op jit(solution)/shard_map/ppermute | solution.py:348
  454.3 15.2 %collective-permute-start.68 = (bf16[1040,256]{1,0:T(8,128)(2,1)S(1)}, bf16[1040,256]{1,0:T(8,128)(2,1)S(1)}, u32[]{:S(2)}, u32[]{:S(2)}) collective-permute-start(bf16[1040,256]{1,0:T(8,128)(2,1)S(1)} %get-tuple-element.70), channel_id=1, source_target_pairs={{4,0},{8,4},{12,8},{5,1},{9,5},{13,9},{6,2},{10,6},{14,10},{7,3},{... | collective-permute-start | bytes 1597448 | tf_op jit(solution)/shard_map/ppermute | solution.py:351
  464.5 88.7 %collective-permute-start.48 = (bf16[4,256,1024]{2,1,0:T(8,128)(2,1)S(1)}, bf16[4,256,1024]{2,1,0:T(8,128)(2,1)S(1)}, u32[]{:S(2)}, u32[]{:S(2)}) collective-permute-start(bf16[4,256,1024]{2,1,0:T(8,128)(2,1)S(1)} %pad_maximum_fusion), channel_id=1, source_target_pairs={{0,1},{1,0},{2,3},{3,2},{4,5},{5,4},{6,7},{7,6},{8,9},{9,8},{10,11... | collective-permute-start | bytes 6291464 | tf_op jit(solution)/shard_map/ppermute | solution.py:345
  470.2 16.0 %collective-permute-start.62 = (bf16[1040,256]{1,0:T(8,128)(2,1)S(1)}, bf16[1040,256]{1,0:T(8,128)(2,1)S(1)}, u32[]{:S(2)}, u32[]{:S(2)}) collective-permute-start(bf16[1040,256]{1,0:T(8,128)(2,1)S(1)} %collective-permute-done.61.refs_3_), channel_id=1, source_target_pairs={{4,0},{8,4},{5,1},{9,5},{6,2},{10,6},{7,3},{11,7},{20,16},{24,20},... | collective-permute-start | bytes 1597448 | tf_op jit(solution)/shard_map/ppermute | solution.py:351
  471.8 14.7 %collective-permute-start.66 = (bf16[1040,256]{1,0:T(8,128)(2,1)S(1)}, bf16[1040,256]{1,0:T(8,128)(2,1)S(1)}, u32[]{:S(2)}, u32[]{:S(2)}) collective-permute-start(bf16[1040,256]{1,0:T(8,128)(2,1)S(1)} %collective-permute-done.65.refs_0_), channel_id=1, source_target_pairs={{4,8},{8,12},{5,9},{9,13},{6,10},{10,14},{7,11},{11,15},{20,24},{2... | collective-permute-start | bytes 1597448 | tf_op jit(solution)/shard_map/ppermute | solution.py:348
  472.8 38.1 %collective-permute-start.36 = (f32[1024,256]{1,0:T(8,128)S(1)}, f32[1024,256]{1,0:T(8,128)S(1)}, u32[]{:S(2)}, u32[]{:S(2)}) collective-permute-start(f32[1024,256]{1,0:T(8,128)S(1)} %get-tuple-element.80), channel_id=1, source_target_pairs={{0,2},{1,3},{2,0},{3,1},{4,6},{5,7},{6,4},{7,5},{8,10},{9,11},{10,... | collective-permute-start | bytes 3145736 | tf_op jit(solution)/shard_map/ppermute | solution.py:345
  486.1 45.4 %collective-permute-start.51 = (f32[1024,256]{1,0:T(8,128)S(1)}, f32[1024,256]{1,0:T(8,128)S(1)}, u32[]{:S(2)}, u32[]{:S(2)}) collective-permute-start(f32[1024,256]{1,0:T(8,128)S(1)} %get-tuple-element.77), channel_id=1, source_target_pairs={{0,2},{1,3},{2,0},{3,1},{4,6},{5,7},{6,4},{7,5},{8,10},{9,11},{10,... | collective-permute-start | bytes 3145736 | tf_op jit(solution)/shard_map/ppermute | solution.py:345
  486.4 20.4 %collective-permute-start.69 = (bf16[1040,256]{1,0:T(8,128)(2,1)S(1)}, bf16[1040,256]{1,0:T(8,128)(2,1)S(1)}, u32[]{:S(2)}, u32[]{:S(2)}) collective-permute-start(bf16[1040,256]{1,0:T(8,128)(2,1)S(1)} %collective-permute-done.68.refs_3_), channel_id=1, source_target_pairs={{4,0},{8,4},{5,1},{9,5},{6,2},{10,6},{7,3},{11,7},{20,16},{24,20},... | collective-permute-start | bytes 1597448 | tf_op jit(solution)/shard_map/ppermute | solution.py:351
  488.4 109.8 %collective-permute-start.49 = (bf16[4,256,1024]{2,1,0:T(8,128)(2,1)}, bf16[4,256,1024]{2,1,0:T(8,128)(2,1)}, u32[]{:S(2)}, u32[]{:S(2)}) collective-permute-start(bf16[4,256,1024]{2,1,0:T(8,128)(2,1)} %collective-permute-done.47), channel_id=1, source_target_pairs={{0,1},{1,0},{2,3},{3,2},{4,5},{5,4},{6,7},{7,6},{8,9},{9,8},{10,11... | collective-permute-start | bytes 6291464 | tf_op jit(solution)/shard_map/ppermute | solution.py:345
  506.9 27.9 %collective-permute-start.60 = (bf16[1040,256]{1,0:T(8,128)(2,1)S(1)}, bf16[1040,256]{1,0:T(8,128)(2,1)S(1)}, u32[]{:S(2)}, u32[]{:S(2)}) collective-permute-start(bf16[1040,256]{1,0:T(8,128)(2,1)S(1)} %collective-permute-done.59.refs_1_), channel_id=1, source_target_pairs={{8,12},{9,13},{10,14},{11,15},{24,28},{25,29},{26,30},{27,31}} | collective-permute-start | bytes 1597448 | tf_op jit(solution)/shard_map/ppermute | solution.py:348
  510.8 32.3 %collective-permute-start.67 = (bf16[1040,256]{1,0:T(8,128)(2,1)S(1)}, bf16[1040,256]{1,0:T(8,128)(2,1)S(1)}, u32[]{:S(2)}, u32[]{:S(2)}) collective-permute-start(bf16[1040,256]{1,0:T(8,128)(2,1)S(1)} %collective-permute-done.66.refs_1_), channel_id=1, source_target_pairs={{8,12},{9,13},{10,14},{11,15},{24,28},{25,29},{26,30},{27,31}} | collective-permute-start | bytes 1597448 | tf_op jit(solution)/shard_map/ppermute | solution.py:348
  531.5 20.2 %collective-permute-start.70 = (bf16[1040,256]{1,0:T(8,128)(2,1)S(1)}, bf16[1040,256]{1,0:T(8,128)(2,1)S(1)}, u32[]{:S(2)}, u32[]{:S(2)}) collective-permute-start(bf16[1040,256]{1,0:T(8,128)(2,1)S(1)} %collective-permute-done.69.refs_4_), channel_id=1, source_target_pairs={{4,0},{5,1},{6,2},{7,3},{20,16},{21,17},{22,18},{23,19}} | collective-permute-start | bytes 1597448 | tf_op jit(solution)/shard_map/ppermute | solution.py:351
  534.8 20.8 %collective-permute-start.37 = (bf16[1040,256]{1,0:T(8,128)(2,1)S(1)}, bf16[1040,256]{1,0:T(8,128)(2,1)S(1)}, u32[]{:S(2)}, u32[]{:S(2)}) collective-permute-start(bf16[1040,256]{1,0:T(8,128)(2,1)S(1)} %get-tuple-element.51), channel_id=1, source_target_pairs={{0,4},{4,8},{8,12},{1,5},{5,9},{9,13},{2,6},{6,10},{10,14},{3,7},{... | collective-permute-start | bytes 1597448 | tf_op jit(solution)/shard_map/ppermute | solution.py:348
  543.1 20.1 %collective-permute-start.40 = (bf16[1040,256]{1,0:T(8,128)(2,1)S(1)}, bf16[1040,256]{1,0:T(8,128)(2,1)S(1)}, u32[]{:S(2)}, u32[]{:S(2)}) collective-permute-start(bf16[1040,256]{1,0:T(8,128)(2,1)S(1)} %get-tuple-element.51), channel_id=1, source_target_pairs={{4,0},{8,4},{12,8},{5,1},{9,5},{13,9},{6,2},{10,6},{14,10},{7,3},{... | collective-permute-start | bytes 1597448 | tf_op jit(solution)/shard_map/ppermute | solution.py:351
  553.3 21.3 %collective-permute-start.55 = (bf16[1040,256]{1,0:T(8,128)(2,1)S(1)}, bf16[1040,256]{1,0:T(8,128)(2,1)S(1)}, u32[]{:S(2)}, u32[]{:S(2)}) collective-permute-start(bf16[1040,256]{1,0:T(8,128)(2,1)S(1)} %get-tuple-element.60), channel_id=1, source_target_pairs={{4,0},{8,4},{12,8},{5,1},{9,5},{13,9},{6,2},{10,6},{14,10},{7,3},{... | collective-permute-start | bytes 1597448 | tf_op jit(solution)/shard_map/ppermute | solution.py:351
  555.6 25.3 %collective-permute-start.38 = (bf16[1040,256]{1,0:T(8,128)(2,1)S(1)}, bf16[1040,256]{1,0:T(8,128)(2,1)S(1)}, u32[]{:S(2)}, u32[]{:S(2)}) collective-permute-start(bf16[1040,256]{1,0:T(8,128)(2,1)S(1)} %collective-permute-done.37.refs_0_), channel_id=1, source_target_pairs={{4,8},{8,12},{5,9},{9,13},{6,10},{10,14},{7,11},{11,15},{20,24},{2... | collective-permute-start | bytes 1597448 | tf_op jit(solution)/shard_map/ppermute | solution.py:348
  563.2 22.8 %collective-permute-start.41 = (bf16[1040,256]{1,0:T(8,128)(2,1)S(1)}, bf16[1040,256]{1,0:T(8,128)(2,1)S(1)}, u32[]{:S(2)}, u32[]{:S(2)}) collective-permute-start(bf16[1040,256]{1,0:T(8,128)(2,1)S(1)} %collective-permute-done.40.refs_3_), channel_id=1, source_target_pairs={{4,0},{8,4},{5,1},{9,5},{6,2},{10,6},{7,3},{11,7},{20,16},{24,20},... | collective-permute-start | bytes 1597448 | tf_op jit(solution)/shard_map/ppermute | solution.py:351
  564.5 22.2 %collective-permute-start.53 = (bf16[1040,256]{1,0:T(8,128)(2,1)S(1)}, bf16[1040,256]{1,0:T(8,128)(2,1)S(1)}, u32[]{:S(2)}, u32[]{:S(2)}) collective-permute-start(bf16[1040,256]{1,0:T(8,128)(2,1)S(1)} %collective-permute-done.52.refs_0_), channel_id=1, source_target_pairs={{4,8},{8,12},{5,9},{9,13},{6,10},{10,14},{7,11},{11,15},{20,24},{2... | collective-permute-start | bytes 1597448 | tf_op jit(solution)/shard_map/ppermute | solution.py:348
  574.6 22.9 %collective-permute-start.56 = (bf16[1040,256]{1,0:T(8,128)(2,1)S(1)}, bf16[1040,256]{1,0:T(8,128)(2,1)}, u32[]{:S(2)}, u32[]{:S(2)}) collective-permute-start(bf16[1040,256]{1,0:T(8,128)(2,1)S(1)} %collective-permute-done.55.refs_3_), channel_id=1, source_target_pairs={{4,0},{8,4},{5,1},{9,5},{6,2},{10,6},{7,3},{11,7},{20,16},{24,20},... | collective-permute-start | bytes 1597448 | tf_op jit(solution)/shard_map/ppermute | solution.py:351
  580.9 30.7 %collective-permute-start.63 = (bf16[1040,256]{1,0:T(8,128)(2,1)S(1)}, bf16[1040,256]{1,0:T(8,128)(2,1)S(1)}, u32[]{:S(2)}, u32[]{:S(2)}) collective-permute-start(bf16[1040,256]{1,0:T(8,128)(2,1)S(1)} %collective-permute-done.62.refs_4_), channel_id=1, source_target_pairs={{4,0},{5,1},{6,2},{7,3},{20,16},{21,17},{22,18},{23,19}} | collective-permute-start | bytes 1597448 | tf_op jit(solution)/shard_map/ppermute | solution.py:351
  586.0 52.2 %collective-permute-start.39 = (bf16[1040,256]{1,0:T(8,128)(2,1)S(1)}, bf16[1040,256]{1,0:T(8,128)(2,1)S(1)}, u32[]{:S(2)}, u32[]{:S(2)}) collective-permute-start(bf16[1040,256]{1,0:T(8,128)(2,1)S(1)} %collective-permute-done.38.refs_1_), channel_id=1, source_target_pairs={{8,12},{9,13},{10,14},{11,15},{24,28},{25,29},{26,30},{27,31}} | collective-permute-start | bytes 1597448 | tf_op jit(solution)/shard_map/ppermute | solution.py:348
  586.7 51.5 %collective-permute-start.42 = (bf16[1040,256]{1,0:T(8,128)(2,1)S(1)}, bf16[1040,256]{1,0:T(8,128)(2,1)S(1)}, u32[]{:S(2)}, u32[]{:S(2)}) collective-permute-start(bf16[1040,256]{1,0:T(8,128)(2,1)S(1)} %collective-permute-done.41.refs_4_), channel_id=1, source_target_pairs={{4,0},{5,1},{6,2},{7,3},{20,16},{21,17},{22,18},{23,19}} | collective-permute-start | bytes 1597448 | tf_op jit(solution)/shard_map/ppermute | solution.py:351
  597.5 23.6 %collective-permute-start.54 = (bf16[1040,256]{1,0:T(8,128)(2,1)S(1)}, bf16[1040,256]{1,0:T(8,128)(2,1)S(1)}, u32[]{:S(2)}, u32[]{:S(2)}) collective-permute-start(bf16[1040,256]{1,0:T(8,128)(2,1)S(1)} %collective-permute-done.53.refs_1_), channel_id=1, source_target_pairs={{8,12},{9,13},{10,14},{11,15},{24,28},{25,29},{26,30},{27,31}} | collective-permute-start | bytes 1597448 | tf_op jit(solution)/shard_map/ppermute | solution.py:348
  598.2 29.5 %collective-permute-start.57 = (bf16[1040,256]{1,0:T(8,128)(2,1)}, bf16[1040,256]{1,0:T(8,128)(2,1)S(1)}, u32[]{:S(2)}, u32[]{:S(2)}) collective-permute-start(bf16[1040,256]{1,0:T(8,128)(2,1)} %collective-permute-done.56.refs_4_), channel_id=1, source_target_pairs={{4,0},{5,1},{6,2},{7,3},{20,16},{21,17},{22,18},{23,19}} | collective-permute-start | bytes 1597448 | tf_op jit(solution)/shard_map/ppermute | solution.py:351
  (41 other events, 520.5 us)

commit v4 on v2

v4 whole, which is shorter than its diff:
```python
import functools
import jax
import jax.numpy as jnp
from jax import lax
from jax.experimental import pallas as pl
from jax.experimental.pallas import tpu as pltpu
from jax.sharding import PartitionSpec as P

BETA_ONE = 0.9
BETA_TWO = 0.95
EPSILON = 1e-08
CHUNKS = 4
EXTRA = 16
F32 = jnp.float32
BF16 = jnp.bfloat16
MIB = 2**20


def params(mib):
    return pltpu.CompilerParams(vmem_limit_bytes=mib * MIB)


def cost(flops, moved):
    return pl.CostEstimate(flops=int(flops) // 100, bytes_accessed=int(moved) // 100, transcendentals=0)


def split(value):
    high = lax.reduce_precision(value, exponent_bits=8, mantissa_bits=7)
    return high.astype(BF16), (value - high).astype(BF16)


def kernel_split(value):
    high = value.astype(BF16)
    return high, (value - high.astype(F32)).astype(BF16)


def dot(a, b, dims):
    return lax.dot_general(a, b, (dims, ((), ())), preferred_element_type=F32)


def flip_kernel(me_ref, rows, out):
    out[...] = rows[...].T


def flip(me, rows, cols):
    piece, width = rows.shape[0] // cols, rows.shape[1]
    return pl.pallas_call(
        flip_kernel,
        grid_spec=pltpu.PrefetchScalarGridSpec(
            num_scalar_prefetch=1,
            grid=(cols,),
            in_specs=[pl.BlockSpec((piece, width), lambda d, s: (s[0] ^ d, 0))],
            out_specs=pl.BlockSpec((width, piece), lambda d, s: (0, d)),
        ),
        out_shape=jax.ShapeDtypeStruct((width, cols * piece), BF16),
        compiler_params=params(16),
        cost_estimate=cost(0, 4 * rows.size),
        name="flip",
    )(me, rows)


def rotate_part_kernel(me_ref, *refs, cols, count, piece):
    pieces, refs = refs[:cols], refs[cols:]
    parts, (out, rows) = refs[:count], refs[count:]
    tile = out.shape[0]

    @pl.when(pl.program_id(0) == 0)
    def _():
        for distance in range(cols):
            start = pl.multiple_of((me_ref[0] ^ distance) * piece, piece)
            for at, part in enumerate(parts):
                rows[distance, pl.ds(at * piece, piece), :] = part[pl.ds(start, piece), :]

    total = None
    for distance in range(cols):
        both = pieces[distance][...].reshape(2 * tile, count * piece)
        term = dot(both, rows[distance], ((1,), (0,)))
        total = term if total is None else total + term
    out[...] = total[:tile] + total[tile:]


def rotate_part(me, pieces, parts):
    cols, count = len(pieces), len(parts)
    _, depth, _ = pieces[0].shape
    piece, width = parts[0].shape[0] // cols, parts[0].shape[1]
    tile = min(256, depth)
    whole = pl.BlockSpec(parts[0].shape, lambda i, s: (0, 0), pipeline_mode=pl.Buffered(1))
    return pl.pallas_call(
        functools.partial(rotate_part_kernel, cols=cols, count=count, piece=piece),
        grid_spec=pltpu.PrefetchScalarGridSpec(
            num_scalar_prefetch=1,
            grid=(depth // tile,),
            in_specs=[pl.BlockSpec((2, tile, count * piece), lambda i, s: (0, i, 0))] * cols
            + [whole] * count,
            out_specs=pl.BlockSpec((tile, width), lambda i, s: (i, 0)),
            scratch_shapes=[pltpu.VMEM((cols, count * piece, width), BF16)],
        ),
        out_shape=jax.ShapeDtypeStruct((depth, width), F32),
        compiler_params=params(44),
        cost_estimate=cost(4 * depth * width * piece * count * cols, 20 * depth * width),
        name="rotate_part",
    )(me, *pieces, *parts)


def rotate_kernel(me_ref, part, *refs, cols, piece):
    pieces, (right, first, second, new_first, new_second, normed) = refs[:cols], refs[cols:]
    tile = first.shape[0]
    total = None
    for distance in range(cols):
        start = pl.multiple_of((me_ref[0] ^ distance) * piece, piece)
        both = pieces[distance][...].reshape(2 * tile, piece)
        term = dot(both, right[pl.ds(start, piece), :], ((1,), (0,)))
        total = term if total is None else total + term
    rotated = part[...] + total[:tile] + total[tile:]
    one = BETA_ONE * first[...] + (1.0 - BETA_ONE) * rotated
    two = BETA_TWO * second[...] + (1.0 - BETA_TWO) * rotated * rotated
    new_first[...] = one
    new_second[...] = two
    high, low = kernel_split(one / (jnp.sqrt(two) + EPSILON))
    normed[0] = high
    normed[1] = low


def rotate(me, part, pieces, right, first, second):
    cols = len(pieces)
    depth, width = first.shape
    piece = right.shape[0] // cols
    tile = min(256, depth)
    final = width // piece - 1
    block = pl.BlockSpec((tile, width), lambda i, s: (i, 0))
    pair = pl.BlockSpec((2, tile, width), lambda i, s: (0, i, 0))
    return pl.pallas_call(
        functools.partial(rotate_kernel, cols=cols, piece=piece),
        grid_spec=pltpu.PrefetchScalarGridSpec(
            num_scalar_prefetch=1,
            grid=(depth // tile,),
            in_specs=[block]
            + [pl.BlockSpec((2, tile, piece), lambda i, s: (0, i, final))] * cols
            + [
                pl.BlockSpec(right.shape, lambda i, s: (0, 0), pipeline_mode=pl.Buffered(1)),
                block,
                block,
            ],
            out_specs=[block, block, pair],
        ),
        out_shape=[
            jax.ShapeDtypeStruct((depth, width), F32),
            jax.ShapeDtypeStruct((depth, width), F32),
            jax.ShapeDtypeStruct((2, depth, width), BF16),
        ],
        compiler_params=params(32),
        cost_estimate=cost(4 * depth * width * piece * cols, 30 * depth * width),
        name="rotate",
    )(me, part, *pieces, right, first, second)


def restore_kernel(normed, flipped, keep, mate, *, cols):
    tile = normed.shape[1]
    piece = keep.shape[2]
    both = dot(normed[...].reshape(2 * tile, normed.shape[2]), flipped[...], ((1,), (0,)))
    term = both[:tile] + both[tile:]
    for distance in range(cols):
        out = mate if distance % 2 else keep
        out[distance // 2] = term[:, distance * piece : (distance + 1) * piece]


def restore(normed, flipped, cols):
    _, depth, inner = normed.shape
    piece = flipped.shape[1] // cols
    tile = min(256, depth)
    out = pl.BlockSpec((cols // 2, tile, piece), lambda i: (0, i, 0))
    return pl.pallas_call(
        functools.partial(restore_kernel, cols=cols),
        grid=(depth // tile,),
        in_specs=[
            pl.BlockSpec((2, tile, inner), lambda i: (0, i, 0)),
            pl.BlockSpec(flipped.shape, lambda i: (0, 0), pipeline_mode=pl.Buffered(1)),
        ],
        out_specs=[out, out],
        out_shape=[jax.ShapeDtypeStruct((cols // 2, depth, piece), F32)] * 2,
        compiler_params=params(24),
        cost_estimate=cost(4 * depth * inner * piece * cols, 8 * depth * piece * cols),
        name="restore",
    )(normed, flipped)


TOP = 7.5


def encode(value, inverse):
    code = jnp.abs(value) * (inverse * 2.0**TOP)
    for _ in range(4):
        code = code * code
    return jnp.where(value < 0, -code, code).astype(BF16)


def decode(code, scale):
    code = code.astype(F32)
    size = jnp.abs(code)
    root = jnp.exp2(jnp.log2(size) * 0.0625 - TOP) * scale
    root = jnp.where(size > 0, root, 0.0)
    return jnp.where(code < 0, -root, root)


def scale_of(message, depth):
    return jnp.max(message[depth : depth + EXTRA, :].astype(F32), axis=(0, 1), keepdims=True)


def send_kernel(*refs, terms, tile):
    parts, (message, total) = refs[:terms], refs[terms:]
    depth, piece = total.shape

    def add(i, top):
        rows = pl.ds(pl.multiple_of(i * tile, tile), tile)
        value = parts[0][rows, :]
        for part in parts[1:]:
            value = value + part[rows, :]
        total[rows, :] = value
        return jnp.maximum(top, jnp.abs(value))

    top = lax.fori_loop(0, depth // tile, add, jnp.zeros((tile, piece), F32))
    top = jnp.maximum(jnp.max(top, axis=(0, 1), keepdims=True), 1e-30)
    scale = jnp.broadcast_to(top, (EXTRA, piece)).astype(BF16)
    message[depth : depth + EXTRA, :] = scale
    inverse = 1.0 / jnp.max(scale.astype(F32), axis=(0, 1), keepdims=True)

    def put(i, carry):
        rows = pl.ds(pl.multiple_of(i * tile, tile), tile)
        message[rows, :] = encode(total[rows, :], inverse)
        return carry

    lax.fori_loop(0, depth // tile, put, 0)


def send(parts):
    depth, piece = parts[0].shape
    tile = min(64, depth)
    return pl.pallas_call(
        functools.partial(send_kernel, terms=len(parts), tile=tile),
        out_shape=jax.ShapeDtypeStruct((depth + EXTRA, piece), BF16),
        scratch_shapes=[pltpu.VMEM((depth, piece), F32)],
        compiler_params=params(24),
        cost_estimate=cost(400 * depth * piece, 18 * depth * piece),
        name="send",
    )(*parts)


def update_kernel(place_ref, message, left, *refs, tile):
    out, held = refs[-2:]
    depth, piece = out.shape
    inner = held.shape[0]
    scale = scale_of(message, inner)

    def unpack(i, carry):
        rows = pl.ds(pl.multiple_of(i * tile, tile), tile)
        high, low = kernel_split(decode(message[rows, :], scale))
        held[rows, :piece] = high
        held[rows, piece:] = low
        return carry

    lax.fori_loop(0, inner // tile, unpack, 0)
    both = dot(left[...].reshape(depth, inner), held[...], ((1,), (0,)))
    term = both[:, :piece] + both[:, piece:]

    @pl.when(pl.program_id(0) == 0)
    def _():
        out[...] = term

    @pl.when(pl.program_id(0) > 0)
    def _():
        out[...] += term


def update_chunk(place, messages, left, update, chunk, depth, width):
    cols, lines, quarter, inner = left.shape
    piece = messages.shape[1]
    tile = min(64, inner)
    extra = [] if update is None else [update]
    return pl.pallas_call(
        functools.partial(update_kernel, tile=tile),
        grid_spec=pltpu.PrefetchScalarGridSpec(
            num_scalar_prefetch=1,
            grid=(lines,),
            in_specs=[
                pl.BlockSpec((inner + EXTRA, piece), lambda i, s: (i, 0)),
                pl.BlockSpec(
                    (cols, 1, quarter, inner),
                    lambda i, s: (0, lax.rem(s[0] + lines - i, lines), 0, 0),
                ),
            ]
            + [pl.BlockSpec(memory_space=pl.ANY)] * len(extra),
            out_specs=pl.BlockSpec((depth, piece), lambda i, s: (0, chunk)),
            scratch_shapes=[pltpu.VMEM((inner, 2 * piece), BF16)],
        ),
        out_shape=jax.ShapeDtypeStruct((depth, width), F32),
        input_output_aliases={3: 0} if extra else {},
        compiler_params=params(24),
        cost_estimate=cost(4 * depth * inner * piece * lines, 12 * depth * piece * lines),
        name="update_chunk",
    )(place, messages, left, *extra)


def build(lines, cols):
    def swap(value, distance):
        return lax.ppermute(value, "col", [(i, i ^ distance) for i in range(cols)])

    def by_distance(block):
        held = {0: block}
        for distance in range(2, cols, 2):
            held[distance] = swap(block, distance)
        for distance in range(0, cols, 2):
            held[distance + 1] = swap(held[distance], 1)
        return held

    def place_by_distance(block, me):
        out = jnp.zeros((cols,) + block.shape, block.dtype)
        for distance, value in by_distance(block).items():
            out = lax.dynamic_update_index_in_dim(out, value, me ^ distance, 0)
        return out

    def gather_row(value):
        return lax.all_gather(value, "row", axis=0, tiled=True)

    def local(gradient, first_moment, second_moment, left_basis, right_basis):
        me, place = lax.axis_index("col"), lax.axis_index("row")
        depth, width = gradient.shape
        piece = width // CHUNKS
        index, spot = jnp.reshape(me, (1,)), jnp.reshape(place, (1,))

        gradients = gather_row(gradient)
        if depth == width:
            parts = [
                gather_row(lax.slice_in_dim(right_basis, p * piece, (p + 1) * piece))
                for p in range(CHUNKS)
            ]
        else:
            blocks = gather_row(right_basis).reshape(cols, CHUNKS, piece, width)
            parts = [blocks[:, p].reshape(cols * piece, width) for p in range(CHUNKS)]

        left = place_by_distance(left_basis, me).reshape(-1, left_basis.shape[1])
        halfway = dot(left, gradients, ((0,), (0,)))
        pieces = by_distance(jnp.stack(split(halfway)))
        pieces = [pieces[distance] for distance in range(cols)]

        flipped = [flip(index, part, cols) for part in parts]
        part = rotate_part(index, pieces, parts[:-1])
        new_first, new_second, normed = rotate(
            index, part, pieces, parts[-1], first_moment, second_moment
        )

        left_late, parts[-1] = lax.optimization_barrier((left, parts[-1]))
        quarter = depth // cols
        backs = []
        for back in range(lines):
            to = lax.rem(place + back, lines)
            rows = lax.dynamic_slice_in_dim(left_late, to * depth + me * quarter, quarter, 0)
            if back:
                rows = lax.ppermute(rows, "row", [(i, (i + back) % lines) for i in range(lines)])
            backs.append(rows)
        backs = jnp.stack(backs)

        sums, messages = [], []
        for chunk in range(CHUNKS):
            if chunk >= 2:
                normed, sums[chunk - 2] = lax.optimization_barrier((normed, sums[chunk - 2]))
            keep, mate = restore(normed, flipped[chunk], cols)
            mate = swap(mate, 1)
            sums.append([keep[0], mate[0]] + [keep[d] + mate[d] for d in range(1, cols // 2)])
        for chunk in range(CHUNKS):
            terms = sums[chunk][:2]
            for at, value in enumerate(sums[chunk][2:]):
                terms.append(swap(value, 2 * at + 2))
            if chunk == 1:
                backs, terms = lax.optimization_barrier((backs, terms))
            messages.append(gather_row(send(terms)))
        left_rows = place_by_distance(backs, me)
        update = None
        for chunk in range(CHUNKS):
            update = update_chunk(spot, messages[chunk], left_rows, update, chunk, depth, width)
        return (new_first, new_second, update)

    return local


def solution(mesh):
    return jax.shard_map(
        build(mesh.shape["row"], mesh.shape["col"]),
        mesh=mesh,
        in_specs=(
            P(("groups", "row"), "col"),
            P(("groups", "row"), "col"),
            P(("groups", "row"), "col"),
            P(("groups", "col"), "row"),
            P(("groups", "row"), "col"),
        ),
        out_specs=(
            P(("groups", "row"), "col"),
            P(("groups", "row"), "col"),
            P(("groups", "row"), "col"),
        ),
        check_vma=False,
    )
```

time: 723 us -> 668 us (0.924)
  starting transfers between devices: 137 us -> 15.3 us
  waiting for transfers between devices: 367 us -> 441 us
  matrix products: 37.5 us -> 13.7 us
  between operations: 1.96 us -> 14.2 us
  local copies, waits for them, and re-layouts: 46 us -> 56.7 us
    ppermute x48 -> x0, waiting for transfers between devices: 208 us -> none  [the longest x24 198 us: down(): return lax.ppermute(value, 'row', [(i, i - 1) for i in senders])]
    all_gather x0 -> x9, waiting for transfers between devices: none -> 155 us  [gather_row(): return lax.all_gather(value, 'row', axis=0, tiled=True)]
    ppermute x20 -> x17, waiting for transfers between devices: 125 us -> 232 us  [swap(): return lax.ppermute(value, 'col', [(i, i ^ distance) for i in range(cols)])]
    ppermute x48 -> x0, starting transfers between devices: 101 us -> none  [the longest x24 70.2 us: up(): return lax.ppermute(value, 'row', [(i, i + 1) for i in senders])]
    unnamed x80 -> x56, local copies, waits for them, and re-layouts: 3.12 us -> 35.9 us
    dot_general x12 -> x1, matrix products: 37.5 us -> 13.7 us  [dot(): return lax.dot_general(a, b, (dims, ((), ())), preferred_element_type=F32)]
    ppermute x3, waiting for transfers between devices: 33.3 us -> 52.7 us  [local(): lax.ppermute(rows, 'row', [(i, (i + back) % lines) for i in range(lines)])]
    ppermute x3, starting transfers between devices: 20.7 us -> 4.07 us  [local(): lax.ppermute(rows, 'row', [(i, (i + back) % lines) for i in range(lines)])]
  transfers between devices with their start and end apart: 71 -> 29, of which waited for: 29 -> 14; matrix products, arithmetic and copies ran while one was open for 13% -> 7% of each run, Pallas kernels for 7% -> 11%
where the time goes in v4:
time: 668 us; the launch traced here: 656 us
  waiting for transfers between devices  441 us (66%)
  Pallas kernels  104 us (16%)
  local copies, waits for them, and re-layouts  56.7 us (8%)
  starting transfers between devices  15.3 us (2%)
  between operations  14.2 us (2%)
  matrix products  13.7 us (2%)
  other arithmetic  12.1 us (2%)
    ppermute x17, waiting for transfers between devices, swap(): return lax.ppermute(value, 'col', [(i, i ^ distance) for i in range(cols)])  232 us
    all_gather x9, waiting for transfers between devices, gather_row(): return lax.all_gather(value, 'row', axis=0, tiled=True)  155 us
    ppermute x3, waiting for transfers between devices, local(): lax.ppermute(rows, 'row', [(i, (i + back) % lines) for i in range(lines)])  52.7 us
    pallas_call x4, Pallas kernels, update_chunk(): pl.pallas_call(functools.partial(update_kernel, tile=tile), grid_spec=plt...  40.9 us
    unnamed x56, local copies, waits for them, and re-layouts  35.9 us
    pallas_call x4, Pallas kernels, restore(): pl.pallas_call(functools.partial(restore_kernel, cols=cols), grid=(depth...  23.7 us
    pallas_call x1, Pallas kernels, rotate_part(): pl.pallas_call(functools.partial(rotate_part_kernel, cols=cols, count=cou...  17 us
    dot_general x1, matrix products, dot(): return lax.dot_general(a, b, (dims, ((), ())), preferred_element_type=F32)  13.7 us
  transfers between devices with their start and end apart: 29, of which 14 were waited for; matrix products, arithmetic and copies ran while one was open for 7% of the time, Pallas kernels for 11%

profile of v4, /device:TPU:0, one launch (start us, length us, event | category | flops | bytes accessed | tf_op | source)
XLA Modules:
  0.0 656.4 jit_solution(8876160837895663951)
XLA Ops:
  8.0 3.0 collective-permute-start
  11.0 1.3 fusion.7
  12.5 44.5 %collective-permute-done = bf16[1024,1024]{1,0:T(8,128)(2,1)} collective-permute-done((bf16[1024,1024]{1,0:T(8,128)(2,1)}, bf16[1024,1024]{1,0:T(8,128)(2,1)}, u32[]{:S(2)}, u32[]{:S(2)}) %collective-permute-start) | collective-permute-done | bytes 2097184 | tf_op jit(solution)/shard_map/ppermute | solution.py:305
  57.0 4.4 broadcast_in_dim.32
  61.4 1.5 bitcast_dynamic-update-slice_fusion.7
  62.9 3.1 bitcast_dynamic-update-slice_fusion.6
  66.0 1.6 bitcast_dynamic-update-slice_fusion.5
  67.6 3.1 bitcast_dynamic-update-slice_fusion.4
  70.7 91.3 %all-gather.10.cloned.1.call-done = bf16[4096,1024]{1,0:T(8,128)(2,1)} async-done(((bf16[1024,1024]{1,0:T(8,128)(2,1)}), bf16[4096,1024]{1,0:T(8,128)(2,1)}) %all-gather.10.cloned.1.call-update) | async-done | bytes 8388624 | tf_op jit(solution)/shard_map/all_gather | solution.py:322
  161.9 13.7 %fusion.2 = (bf16[1,1024,1024]{2,1,0:T(8,128)(2,1)S(1)}, bf16[1,1024,1024]{2,1,0:T(8,128)(2,1)S(1)}) fusion(bf16[4096,1024]{1,0:T(8,128)(2,1)} %bitcast.5, bf16[4096,1024]{1,0:T(8,128)(2,1)} %all-gather.10.cloned.1.call-done), kind=kOutput, calls=%fused_computation.5 | convolution fusion | flops 8594128896 | bytes 20971520 | tf_op jit(solution)/shard_map/dot_general | solution.py:38
  175.7 2.4 pad_maximum_fusion.refs_0_
  178.1 1.5 collective-permute-start.4
  179.7 91.2 %collective-permute-done.4.refs_2_ = bf16[2,1024,1024]{2,1,0:T(8,128)(2,1)} collective-permute-done((bf16[2,1024,1024]{2,1,0:T(8,128)(2,1)}, bf16[2,1024,1024]{2,1,0:T(8,128)(2,1)}, u32[]{:S(2)}, u32[]{:S(2)}) %collective-permute-start.4) | collective-permute-done | bytes 4194336 | tf_op jit(solution)/shard_map/ppermute | solution.py:305
  271.2 1.6 copy-done.15
  273.8 1.3 copy-done.17
  275.2 25.5 %all-gather.16.cloned.1.call-done.refs_6_.rows = bf16[1024,1024]{1,0:T(8,128)(2,1)} async-done(((bf16[256,1024]{1,0:T(8,128)(2,1)}), bf16[1024,1024]{1,0:T(8,128)(2,1)}) %all-gather.16.cloned.1.call-update) | async-done | bytes 2097168 | tf_op jit(solution)/shard_map/all_gather | solution.py:322
  300.7 1.6 copy-done.11
  302.3 1.6 copy-done.13
  303.9 17.0 %rotate_part.1.part = f32[1024,1024]{1,0:T(8,128)} custom-call(s32[1]{0:T(128)} %bitcast.me_ref, bf16[2,1024,1024]{2,1,0:T(8,128)(2,1)} %pad_maximum_fusion.refs_0_, bf16[2,1024,1024]{2,1,0:T(8,128)(2,1)} %collective-permute-done.3.refs_1_, bf16[2,1024,1024]{2,1,0:T(8,128)(2,1)} %collective-permute-done.4.refs_2_, ...), custom_call_target="tpu_custom_call" | custom-call | flops 128849016 | bytes 209715 | tf_op jit(solution)/shard_map/rotate_part/pallas_call | solution.py:88
  320.8 26.3 %all-gather.18.cloned.1.call-done.refs_4_.rows = bf16[1024,1024]{1,0:T(8,128)(2,1)} async-done(((bf16[256,1024]{1,0:T(8,128)(2,1)}), bf16[1024,1024]{1,0:T(8,128)(2,1)}) %all-gather.18.cloned.1.call-update) | async-done | bytes 2097168 | tf_op jit(solution)/shard_map/all_gather | solution.py:322
  347.1 2.2 copy-done.8
  349.3 1.6 copy-done.9
  350.9 11.6 %rotate.1 = (f32[1024,1024]{1,0:T(8,128)}, f32[1024,1024]{1,0:T(8,128)}, bf16[2,1024,1024]{2,1,0:T(8,128)(2,1)S(1)}) custom-call(s32[1]{0:T(128)} %bitcast.me_ref, f32[1024,1024]{1,0:T(8,128)S(1)} %copy-done.8, bf16[2,1024,1024]{2,1,0:T(8,128)(2,1)} %pad_maximum_fusion.refs_0_, bf16[2,1024,1024]{2,1,0:T(8,128)(2,1)} %collective-permute-done.3.refs_1_, ...), custom_call_target="tpu_custom_call" | custom-call | flops 42949672 | bytes 314572 | tf_op jit(solution)/shard_map/rotate/pallas_call | solution.py:132
  362.5 5.6 restore.4
  368.1 4.1 collective-permute-done.6
  372.6 1.5 collective-permute-start.19
  375.1 5.6 restore.5
  380.8 1.3 copy-done.24
  382.1 15.8 %collective-permute-done.19.refs_2_ = f32[1024,256]{1,0:T(8,128)S(1)} collective-permute-done((f32[1024,256]{1,0:T(8,128)S(1)}, f32[1024,256]{1,0:T(8,128)S(1)}, u32[]{:S(2)}, u32[]{:S(2)}) %collective-permute-start.19) | collective-permute-done | bytes 1048608 | tf_op jit(solution)/shard_map/ppermute | solution.py:305
  397.8 1.7 send.7
  399.6 3.4 fusion.5
  403.0 1.5 collective-permute-start.13
  404.5 2.0 dynamic-slice_bitcast_fusion
  406.5 1.7 collective-permute-start.11
  408.2 2.3 collective-permute-start.12
  411.6 6.2 restore.7
  417.8 16.0 %collective-permute-done.10 = bf16[256,1024]{1,0:T(8,128)(2,1)S(1)} collective-permute-done((bf16[256,1024]{1,0:T(8,128)(2,1)S(1)}, bf16[256,1024]{1,0:T(8,128)(2,1)S(1)}, u32[]{:S(2)}, u32[]{:S(2)}) %collective-permute-start.10) | collective-permute-done | bytes 524320 | tf_op jit(solution)/shard_map/ppermute | solution.py:358
  433.9 36.7 %collective-permute-done.11 = bf16[256,1024]{1,0:T(8,128)(2,1)S(1)} collective-permute-done((bf16[256,1024]{1,0:T(8,128)(2,1)S(1)}, bf16[256,1024]{1,0:T(8,128)(2,1)S(1)}, u32[]{:S(2)}, u32[]{:S(2)}) %collective-permute-start.11) | collective-permute-done | bytes 524320 | tf_op jit(solution)/shard_map/ppermute | solution.py:358
  470.6 1.6 pad_maximum_fusion.1
  472.1 1.6 send.6
  473.9 2.6 fusion.3
  478.7 6.3 restore.6
  485.0 12.6 %collective-permute-done.18.refs_2_ = f32[1024,256]{1,0:T(8,128)S(1)} collective-permute-done((f32[1024,256]{1,0:T(8,128)S(1)}, f32[1024,256]{1,0:T(8,128)S(1)}, u32[]{:S(2)}, u32[]{:S(2)}) %collective-permute-start.18) | collective-permute-done | bytes 1048608 | tf_op jit(solution)/shard_map/ppermute | solution.py:305
  497.6 1.7 send.5
  499.7 1.8 fusion.4
  501.5 2.1 collective-permute-start.9
  503.6 60.5 %collective-permute-done.9.refs_2_ = f32[1024,256]{1,0:T(8,128)S(1)} collective-permute-done((f32[1024,256]{1,0:T(8,128)S(1)}, f32[1024,256]{1,0:T(8,128)S(1)}, u32[]{:S(2)}, u32[]{:S(2)}) %collective-permute-start.9) | collective-permute-done | bytes 1048608 | tf_op jit(solution)/shard_map/ppermute | solution.py:305
  564.1 1.6 send.4
  567.7 1.9 bitcast_dynamic-update-slice_fusion.2
  569.6 2.5 collective-permute-done.15
  573.5 3.4 copy-done
  576.9 3.4 copy-done.1
  580.2 1.6 copy-done.19
  581.8 10.2 %update_chunk.4.refs_0_ = f32[1024,1024]{1,0:T(8,128)} custom-call(s32[1]{0:T(128)} %bitcast.8.place_ref, bf16[4160,256]{1,0:T(8,128)(2,1)S(1)} %copy-done.19, bf16[4,4,256,1024]{3,2,1,0:T(8,128)(2,1)S(1)} %copy-done.1), custom_call_target="tpu_custom_call" | custom-call | flops 42949672 | bytes 125829 | tf_op jit(solution)/shard_map/update_chunk/pallas_call | solution.py:279
  592.1 3.6 copy-done.2
  595.6 1.7 copy-done.20
  597.3 10.2 %update_chunk.5.refs_0_ = f32[1024,1024]{1,0:T(8,128)} custom-call(s32[1]{0:T(128)} %bitcast.8.place_ref, bf16[4160,256]{1,0:T(8,128)(2,1)S(1)} %copy-done.20, bf16[4,4,256,1024]{3,2,1,0:T(8,128)(2,1)S(1)} %copy-done.2, f32[1024,1024]{1,0:T(8,128)} %update_chunk.4.refs_0_), custom_call_target="tpu_custom_call", output_to_operand_aliasing={{}: (3, {})} | custom-call | flops 42949672 | bytes 125829 | tf_op jit(solution)/shard_map/update_chunk/pallas_call | solution.py:279
  607.6 3.4 copy-done.3
  611.0 1.6 copy-done.21
  612.6 10.2 %update_chunk.6.refs_0_ = f32[1024,1024]{1,0:T(8,128)} custom-call(s32[1]{0:T(128)} %bitcast.8.place_ref, bf16[4160,256]{1,0:T(8,128)(2,1)S(1)} %copy-done.21, bf16[4,4,256,1024]{3,2,1,0:T(8,128)(2,1)S(1)} %copy-done.3, f32[1024,1024]{1,0:T(8,128)} %update_chunk.5.refs_0_), custom_call_target="tpu_custom_call", output_to_operand_aliasing={{}: (3, {})} | custom-call | flops 42949672 | bytes 125829 | tf_op jit(solution)/shard_map/update_chunk/pallas_call | solution.py:279
  622.8 11.9 %all-gather.20.cloned.1.call-done.message = bf16[4160,256]{1,0:T(8,128)(2,1)} async-done(((bf16[1040,256]{1,0:T(8,128)(2,1)}), bf16[4160,256]{1,0:T(8,128)(2,1)}) %all-gather.20.cloned.1.call-update) | async-done | bytes 2129936 | tf_op jit(solution)/shard_map/all_gather | solution.py:322
  634.7 3.4 copy-done.4
  638.0 1.6 copy-done.22
  639.6 10.2 %update_chunk.7 = f32[1024,1024]{1,0:T(8,128)} custom-call(s32[1]{0:T(128)} %bitcast.8.place_ref, bf16[4160,256]{1,0:T(8,128)(2,1)S(1)} %copy-done.22, bf16[4,4,256,1024]{3,2,1,0:T(8,128)(2,1)S(1)} %copy-done.4, f32[1024,1024]{1,0:T(8,128)} %update_chunk.6.refs_0_), custom_call_target="tpu_custom_call", output_to_operand_aliasing={{}: (3, {})} | custom-call | flops 42949672 | bytes 125829 | tf_op jit(solution)/shard_map/update_chunk/pallas_call | solution.py:279
  (96 shorter events, 10.9 us)
Async XLA Ops:
  7.2 3.8 copy-start.26
  7.2 154.8 %all-gather.10.cloned.1.call-start = ((), (), s32[]{:S(2)}) async-start(), calls=%async_computation | async-start | bytes 10485760 | tf_op jit(solution)/shard_map/all_gather | solution.py:322
  7.9 263.3 %all-gather.12.cloned.1.call-start = ((), (), s32[]{:S(2)}) async-start(), calls=%async_computation.1 | async-start | bytes 2621440 | tf_op jit(solution)/shard_map/all_gather | solution.py:322
  8.0 49.0 %collective-permute-start = (bf16[1024,1024]{1,0:T(8,128)(2,1)}, bf16[1024,1024]{1,0:T(8,128)(2,1)}, u32[]{:S(2)}, u32[]{:S(2)}) collective-permute-start(bf16[1024,1024]{1,0:T(8,128)(2,1)} %param.8), channel_id=1, source_target_pairs={{0,2},{1,3},{2,0},{3,1},{4,6},{5,7},{6,4},{7,5},{8,10},{9,11},{10,... | collective-permute-start | bytes 6291464 | tf_op jit(solution)/shard_map/ppermute | solution.py:305
  12.3 262.8 %all-gather.14.cloned.1.call-start = ((), (), s32[]{:S(2)}) async-start(), calls=%async_computation.2 | async-start | bytes 2621440 | tf_op jit(solution)/shard_map/all_gather | solution.py:322
  12.4 53.6 %collective-permute-start.1 = (bf16[1024,1024]{1,0:T(8,128)(2,1)}, bf16[1024,1024]{1,0:T(8,128)(2,1)S(1)}, u32[]{:S(2)}, u32[]{:S(2)}) collective-permute-start(bf16[1024,1024]{1,0:T(8,128)(2,1)} %param.8), channel_id=1, source_target_pairs={{0,1},{1,0},{2,3},{3,2},{4,5},{5,4},{6,7},{7,6},{8,9},{9,8},{10,11... | collective-permute-start | bytes 6291464 | tf_op jit(solution)/shard_map/ppermute | solution.py:305
  56.9 10.7 %collective-permute-start.2 = (bf16[1024,1024]{1,0:T(8,128)(2,1)}, bf16[1024,1024]{1,0:T(8,128)(2,1)}, u32[]{:S(2)}, u32[]{:S(2)}) collective-permute-start(bf16[1024,1024]{1,0:T(8,128)(2,1)} %collective-permute-done), channel_id=1, source_target_pairs={{0,1},{1,0},{2,3},{3,2},{4,5},{5,4},{6,7},{7,6},{8,9},{9,8},{10,11... | collective-permute-start | bytes 6291464 | tf_op jit(solution)/shard_map/ppermute | solution.py:305
  56.9 243.7 %all-gather.16.cloned.1.call-start = ((), (), s32[]{:S(2)}) async-start(), calls=%async_computation.3 | async-start | bytes 2621440 | tf_op jit(solution)/shard_map/all_gather | solution.py:322
  57.0 4.4 copy-start.27
  178.1 92.9 %collective-permute-start.4 = (bf16[2,1024,1024]{2,1,0:T(8,128)(2,1)}, bf16[2,1024,1024]{2,1,0:T(8,128)(2,1)}, u32[]{:S(2)}, u32[]{:S(2)}) collective-permute-start(bf16[2,1024,1024]{2,1,0:T(8,128)(2,1)} %pad_maximum_fusion.refs_0_), channel_id=1, source_target_pairs={{0,2},{1,3},{2,0},{3,1},{4,6},{5,7},{6,4},{7,5},{8,10},{9,11},{10,... | collective-permute-start | bytes 12582920 | tf_op jit(solution)/shard_map/ppermute | solution.py:305
  179.6 167.6 %all-gather.18.cloned.1.call-start = ((), (), s32[]{:S(2)}) async-start(), calls=%async_computation.4 | async-start | bytes 2621440 | tf_op jit(solution)/shard_map/all_gather | solution.py:322
  179.6 121.0 %collective-permute-start.3 = (bf16[2,1024,1024]{2,1,0:T(8,128)(2,1)}, bf16[2,1024,1024]{2,1,0:T(8,128)(2,1)}, u32[]{:S(2)}, u32[]{:S(2)}) collective-permute-start(bf16[2,1024,1024]{2,1,0:T(8,128)(2,1)} %pad_maximum_fusion.refs_0_), channel_id=1, source_target_pairs={{0,1},{1,0},{2,3},{3,2},{4,5},{5,4},{6,7},{7,6},{8,9},{9,8},{10,11... | collective-permute-start | bytes 12582920 | tf_op jit(solution)/shard_map/ppermute | solution.py:305
  270.9 29.7 %collective-permute-start.5 = (bf16[2,1024,1024]{2,1,0:T(8,128)(2,1)}, bf16[2,1024,1024]{2,1,0:T(8,128)(2,1)}, u32[]{:S(2)}, u32[]{:S(2)}) collective-permute-start(bf16[2,1024,1024]{2,1,0:T(8,128)(2,1)} %collective-permute-done.4.refs_2_), channel_id=1, source_target_pairs={{0,1},{1,0},{2,3},{3,2},{4,5},{5,4},{6,7},{7,6},{8,9},{9,8},{10,11... | collective-permute-start | bytes 12582920 | tf_op jit(solution)/shard_map/ppermute | solution.py:305
  271.0 305.9 %all-gather.26.cloned.1.call-start = ((), (), s32[]{:S(2)}) async-start(), calls=%async_computation.8 | async-start | bytes 2662400 | tf_op jit(solution)/shard_map/all_gather | solution.py:322
  271.2 1.6 copy-start.15
  272.8 27.9 %copy-start.16 = (bf16[1024,1024]{1,0:T(8,128)(2,1)S(1)}, bf16[1024,1024]{1,0:T(8,128)(2,1)}, u32[]{:S(2)}) copy-start(bf16[1024,1024]{1,0:T(8,128)(2,1)} %all-gather.12.cloned.1.call-done.refs_4_.rows) | copy-start | bytes 6291460
  273.8 1.3 copy-start.17
  300.7 1.6 copy-start.11
  302.3 1.6 copy-start.13
  347.1 2.2 copy-start.8
  349.3 1.6 copy-start.9
  350.9 11.6 %copy-start.18 = (bf16[1024,1024]{1,0:T(8,128)(2,1)S(1)}, bf16[1024,1024]{1,0:T(8,128)(2,1)}, u32[]{:S(2)}) copy-start(bf16[1024,1024]{1,0:T(8,128)(2,1)} %copy-done.17) | copy-start | bytes 6291460
  362.5 12.7 %copy-start.5 = (bf16[2,1024,1024]{2,1,0:T(8,128)(2,1)}, bf16[2,1024,1024]{2,1,0:T(8,128)(2,1)S(1)}, u32[]{:S(2)}) copy-start(bf16[2,1024,1024]{2,1,0:T(8,128)(2,1)S(1)} %get-tuple-element.35.normed) | copy-start | bytes 12582916
  368.1 4.2 collective-permute-start.6
  372.3 1.8 copy-start.14
  372.6 25.3 %collective-permute-start.19 = (f32[1024,256]{1,0:T(8,128)S(1)}, f32[1024,256]{1,0:T(8,128)S(1)}, u32[]{:S(2)}, u32[]{:S(2)}) collective-permute-start(f32[1024,256]{1,0:T(8,128)S(1)} %get-tuple-element.50), channel_id=1, source_target_pairs={{0,2},{1,3},{2,0},{3,1},{4,6},{5,7},{6,4},{7,5},{8,10},{9,11},{10,... | collective-permute-start | bytes 3145736 | tf_op jit(solution)/shard_map/ppermute | solution.py:305
  380.8 1.3 copy-start.24
  382.1 17.5 %collective-permute-start.7 = (f32[2,1024,256]{2,1,0:T(8,128)S(1)}, f32[2,1024,256]{2,1,0:T(8,128)}, u32[]{:S(2)}, u32[]{:S(2)}) collective-permute-start(f32[2,1024,256]{2,1,0:T(8,128)S(1)} %get-tuple-element.34), channel_id=1, source_target_pairs={{0,1},{1,0},{2,3},{3,2},{4,5},{5,4},{6,7},{7,6},{8,9},{9,8},{10,11... | collective-permute-start | bytes 6291464 | tf_op jit(solution)/shard_map/ppermute | solution.py:305
  399.5 192.5 %all-gather.24.cloned.1.call-start = ((), (), s32[]{:S(2)}) async-start(), calls=%async_computation.7 | async-start | bytes 2662400 | tf_op jit(solution)/shard_map/all_gather | solution.py:322
  403.0 69.1 %collective-permute-start.13 = (f32[1024,256]{1,0:T(8,128)}, f32[1024,256]{1,0:T(8,128)S(1)}, u32[]{:S(2)}, u32[]{:S(2)}) collective-permute-start(f32[1024,256]{1,0:T(8,128)} %get-tuple-element.41), channel_id=1, source_target_pairs={{0,2},{1,3},{2,0},{3,1},{4,6},{5,7},{6,4},{7,5},{8,10},{9,11},{10,... | collective-permute-start | bytes 3145736 | tf_op jit(solution)/shard_map/ppermute | solution.py:305
  404.5 6.0 copy-start.12
  406.5 27.4 %collective-permute-start.10 = (bf16[256,1024]{1,0:T(8,128)(2,1)S(1)}, bf16[256,1024]{1,0:T(8,128)(2,1)S(1)}, u32[]{:S(2)}, u32[]{:S(2)}) collective-permute-start(bf16[256,1024]{1,0:T(8,128)(2,1)S(1)} %get-tuple-element.54), channel_id=1, source_target_pairs={{0,4},{4,8},{8,12},{12,0},{1,5},{5,9},{9,13},{13,1},{2,6},{6,10},{... | collective-permute-start | bytes 1572872 | tf_op jit(solution)/shard_map/ppermute | solution.py:358
  406.5 64.0 %collective-permute-start.11 = (bf16[256,1024]{1,0:T(8,128)(2,1)S(1)}, bf16[256,1024]{1,0:T(8,128)(2,1)S(1)}, u32[]{:S(2)}, u32[]{:S(2)}) collective-permute-start(bf16[256,1024]{1,0:T(8,128)(2,1)S(1)} %get-tuple-element.53), channel_id=1, source_target_pairs={{0,8},{4,12},{8,0},{12,4},{1,9},{5,13},{9,1},{13,5},{2,10},{6,14},... | collective-permute-start | bytes 1572872 | tf_op jit(solution)/shard_map/ppermute | solution.py:358
  408.2 3.3 copy-start.6
  408.2 62.3 %collective-permute-start.12 = (bf16[256,1024]{1,0:T(8,128)(2,1)S(1)}, bf16[256,1024]{1,0:T(8,128)(2,1)S(1)}, u32[]{:S(2)}, u32[]{:S(2)}) collective-permute-start(bf16[256,1024]{1,0:T(8,128)(2,1)S(1)} %get-tuple-element.52), channel_id=1, source_target_pairs={{0,12},{4,0},{8,4},{12,8},{1,13},{5,1},{9,5},{13,9},{2,14},{6,2},{... | collective-permute-start | bytes 1572872 | tf_op jit(solution)/shard_map/ppermute | solution.py:358
  417.8 54.3 %copy-start.23 = (f32[2,1024,256]{2,1,0:T(8,128)}, f32[2,1024,256]{2,1,0:T(8,128)S(1)}, u32[]{:S(2)}) copy-start(f32[2,1024,256]{2,1,0:T(8,128)S(1)} %get-tuple-element.43) | copy-start | bytes 6291460
  417.8 56.0 %collective-permute-start.17 = (f32[2,1024,256]{2,1,0:T(8,128)}, f32[2,1024,256]{2,1,0:T(8,128)}, u32[]{:S(2)}, u32[]{:S(2)}) collective-permute-start(f32[2,1024,256]{2,1,0:T(8,128)} %get-tuple-element.44), channel_id=1, source_target_pairs={{0,1},{1,0},{2,3},{3,2},{4,5},{5,4},{6,7},{7,6},{8,9},{9,8},{10,11... | collective-permute-start | bytes 6291464 | tf_op jit(solution)/shard_map/ppermute | solution.py:305
  473.8 133.7 %all-gather.22.cloned.1.call-start = ((), (), s32[]{:S(2)}) async-start(), calls=%async_computation.6 | async-start | bytes 2662400 | tf_op jit(solution)/shard_map/all_gather | solution.py:322
  473.9 2.9 copy-start.10
  476.5 2.3 copy-start.7
  476.5 21.1 %collective-permute-start.18 = (f32[1024,256]{1,0:T(8,128)S(1)}, f32[1024,256]{1,0:T(8,128)S(1)}, u32[]{:S(2)}, u32[]{:S(2)}) collective-permute-start(f32[1024,256]{1,0:T(8,128)S(1)} %get-tuple-element.57), channel_id=1, source_target_pairs={{0,2},{1,3},{2,0},{3,1},{4,6},{5,7},{6,4},{7,5},{8,10},{9,11},{10,... | collective-permute-start | bytes 3145736 | tf_op jit(solution)/shard_map/ppermute | solution.py:305
  485.0 14.7 %collective-permute-start.8 = (f32[2,1024,256]{2,1,0:T(8,128)}, f32[2,1024,256]{2,1,0:T(8,128)}, u32[]{:S(2)}, u32[]{:S(2)}) collective-permute-start(f32[2,1024,256]{2,1,0:T(8,128)} %get-tuple-element.37), channel_id=1, source_target_pairs={{0,1},{1,0},{2,3},{3,2},{4,5},{5,4},{6,7},{7,6},{8,9},{9,8},{10,11... | collective-permute-start | bytes 6291464 | tf_op jit(solution)/shard_map/ppermute | solution.py:305
  499.3 135.3 %all-gather.20.cloned.1.call-start = ((), (), s32[]{:S(2)}) async-start(), calls=%async_computation.5 | async-start | bytes 2662400 | tf_op jit(solution)/shard_map/all_gather | solution.py:322
  499.6 66.2 %collective-permute-start.14 = (bf16[4,256,1024]{2,1,0:T(8,128)(2,1)}, bf16[4,256,1024]{2,1,0:T(8,128)(2,1)}, u32[]{:S(2)}, u32[]{:S(2)}) collective-permute-start(bf16[4,256,1024]{2,1,0:T(8,128)(2,1)} %pad_maximum_fusion.1), channel_id=1, source_target_pairs={{0,2},{1,3},{2,0},{3,1},{4,6},{5,7},{6,4},{7,5},{8,10},{9,11},{10,... | collective-permute-start | bytes 6291464 | tf_op jit(solution)/shard_map/ppermute | solution.py:305
  501.5 62.6 %collective-permute-start.9 = (f32[1024,256]{1,0:T(8,128)S(1)}, f32[1024,256]{1,0:T(8,128)S(1)}, u32[]{:S(2)}, u32[]{:S(2)}) collective-permute-start(f32[1024,256]{1,0:T(8,128)S(1)} %get-tuple-element.60), channel_id=1, source_target_pairs={{0,2},{1,3},{2,0},{3,1},{4,6},{5,7},{6,4},{7,5},{8,10},{9,11},{10,... | collective-permute-start | bytes 3145736 | tf_op jit(solution)/shard_map/ppermute | solution.py:305
  564.1 1.7 copy-start.25
  565.8 6.3 collective-permute-start.15
  565.8 7.3 %collective-permute-start.16 = (bf16[4,256,1024]{2,1,0:T(8,128)(2,1)}, bf16[4,256,1024]{2,1,0:T(8,128)(2,1)S(1)}, u32[]{:S(2)}, u32[]{:S(2)}) collective-permute-start(bf16[4,256,1024]{2,1,0:T(8,128)(2,1)} %collective-permute-done.14), channel_id=1, source_target_pairs={{0,1},{1,0},{2,3},{3,2},{4,5},{5,4},{6,7},{7,6},{8,9},{9,8},{10,11... | collective-permute-start | bytes 6291464 | tf_op jit(solution)/shard_map/ppermute | solution.py:305
  573.5 3.4 copy-start
  576.9 3.4 copy-start.1
  580.2 1.6 copy-start.19
  592.1 3.6 copy-start.2
  595.6 1.7 copy-start.20
  607.6 3.4 copy-start.3
  611.0 1.6 copy-start.21
  634.7 3.4 copy-start.4
  638.0 1.6 copy-start.22
Sparse Core Ops, SparseCore 0:
  9.6 152.3 all-gather.9
  163.5 44.1 all-gather.11
  209.9 44.6 all-gather.13
  256.0 44.6 all-gather.15
  302.6 44.4 all-gather.17
  399.6 84.5 all-gather.25
  485.7 50.2 all-gather.23
  537.6 45.2 all-gather.21
  584.5 50.1 all-gather.19

commit v5 on v4

--- a/solution.py
+++ b/solution.py
@@ -42,62 +42,67 @@
     out[...] = rows[...].T
 
 
-def flip(me, rows, cols):
-    piece, width = rows.shape[0] // cols, rows.shape[1]
+def flip(me, rows, cols, count=1, at=0):
+    piece, width = rows.shape[0] // cols // count, rows.shape[1]
     return pl.pallas_call(
         flip_kernel,
         grid_spec=pltpu.PrefetchScalarGridSpec(
             num_scalar_prefetch=1,
             grid=(cols,),
-            in_specs=[pl.BlockSpec((piece, width), lambda d, s: (s[0] ^ d, 0))],
+            in_specs=[pl.BlockSpec((piece, width), lambda d, s: ((s[0] ^ d) * count + at, 0))],
             out_specs=pl.BlockSpec((width, piece), lambda d, s: (0, d)),
         ),
         out_shape=jax.ShapeDtypeStruct((width, cols * piece), BF16),
         compiler_params=params(16),
-        cost_estimate=cost(0, 4 * rows.size),
+        cost_estimate=cost(0, 4 * piece * cols * width),
         name="flip",
     )(me, rows)
 
 
-def rotate_part_kernel(me_ref, *refs, cols, count, piece):
+def rotate_part_kernel(me_ref, *refs, cols, sizes):
     pieces, refs = refs[:cols], refs[cols:]
-    parts, (out, rows) = refs[:count], refs[count:]
+    parts, (out, rows) = refs[: len(sizes)], refs[len(sizes) :]
     tile = out.shape[0]
 
     @pl.when(pl.program_id(0) == 0)
     def _():
         for distance in range(cols):
-            start = pl.multiple_of((me_ref[0] ^ distance) * piece, piece)
-            for at, part in enumerate(parts):
-                rows[distance, pl.ds(at * piece, piece), :] = part[pl.ds(start, piece), :]
+            at = 0
+            for size, part in zip(sizes, parts):
+                start = pl.multiple_of((me_ref[0] ^ distance) * size, size)
+                rows[distance, pl.ds(at, size), :] = part[pl.ds(start, size), :]
+                at += size
 
     total = None
     for distance in range(cols):
-        both = pieces[distance][...].reshape(2 * tile, count * piece)
+        both = pieces[distance][...].reshape(2 * tile, sum(sizes))
         term = dot(both, rows[distance], ((1,), (0,)))
         total = term if total is None else total + term
     out[...] = total[:tile] + total[tile:]
 
 
 def rotate_part(me, pieces, parts):
-    cols, count = len(pieces), len(parts)
+    cols = len(pieces)
     _, depth, _ = pieces[0].shape
-    piece, width = parts[0].shape[0] // cols, parts[0].shape[1]
+    width = parts[0].shape[1]
+    sizes = [part.shape[0] // cols for part in parts]
     tile = min(256, depth)
-    whole = pl.BlockSpec(parts[0].shape, lambda i, s: (0, 0), pipeline_mode=pl.Buffered(1))
-    return pl.pallas_call(
-        functools.partial(rotate_part_kernel, cols=cols, count=count, piece=piece),
+    return pl.pallas_call(
+        functools.partial(rotate_part_kernel, cols=cols, sizes=sizes),
         grid_spec=pltpu.PrefetchScalarGridSpec(
             num_scalar_prefetch=1,
             grid=(depth // tile,),
-            in_specs=[pl.BlockSpec((2, tile, count * piece), lambda i, s: (0, i, 0))] * cols
-            + [whole] * count,
+            in_specs=[pl.BlockSpec((2, tile, sum(sizes)), lambda i, s: (0, i, 0))] * cols
+            + [
+                pl.BlockSpec(part.shape, lambda i, s: (0, 0), pipeline_mode=pl.Buffered(1))
+                for part in parts
+            ],
             out_specs=pl.BlockSpec((tile, width), lambda i, s: (i, 0)),
-            scratch_shapes=[pltpu.VMEM((cols, count * piece, width), BF16)],
+            scratch_shapes=[pltpu.VMEM((cols, sum(sizes), width), BF16)],
         ),
         out_shape=jax.ShapeDtypeStruct((depth, width), F32),
         compiler_params=params(44),
-        cost_estimate=cost(4 * depth * width * piece * count * cols, 20 * depth * width),
+        cost_estimate=cost(4 * depth * width * sum(sizes) * cols, 20 * depth * width),
         name="rotate_part",
     )(me, *pieces, *parts)
 
@@ -148,7 +153,7 @@
             jax.ShapeDtypeStruct((depth, width), F32),
             jax.ShapeDtypeStruct((2, depth, width), BF16),
         ],
-        compiler_params=params(32),
+        compiler_params=params(44),
         cost_estimate=cost(4 * depth * width * piece * cols, 30 * depth * width),
         name="rotate",
     )(me, part, *pieces, right, first, second)
@@ -206,15 +211,12 @@
     return jnp.max(message[depth : depth + EXTRA, :].astype(F32), axis=(0, 1), keepdims=True)
 
 
-def send_kernel(*refs, terms, tile):
-    parts, (message, total) = refs[:terms], refs[terms:]
+def fill(message, total, value_at, tile):
     depth, piece = total.shape
 
     def add(i, top):
         rows = pl.ds(pl.multiple_of(i * tile, tile), tile)
-        value = parts[0][rows, :]
-        for part in parts[1:]:
-            value = value + part[rows, :]
+        value = value_at(rows)
         total[rows, :] = value
         return jnp.maximum(top, jnp.abs(value))
 
@@ -232,17 +234,165 @@
     lax.fori_loop(0, depth // tile, put, 0)
 
 
-def send(parts):
-    depth, piece = parts[0].shape
+def summed(keep, mate, codes):
+    depth = keep.shape[1]
+    scales = [scale_of(code, depth) for code in codes]
+
+    def value_at(rows):
+        value = keep[0, rows, :] + mate[0, rows, :]
+        for code, scale in zip(codes, scales):
+            value = value + decode(code[rows, :], scale)
+        return value
+
+    return value_at
+
+
+def send_kernel(keep, mate, *refs, tile):
+    codes, (message, total) = refs[:-2], refs[-2:]
+    fill(message, total, summed(keep, mate, codes), tile)
+
+
+def send(keep, mate, distance, codes):
+    _, depth, piece = keep.shape
     tile = min(64, depth)
-    return pl.pallas_call(
-        functools.partial(send_kernel, terms=len(parts), tile=tile),
+    pair = pl.BlockSpec((1, depth, piece), lambda i: (distance // 2, 0, 0))
+    message = pl.BlockSpec((depth + EXTRA, piece), lambda i: (0, 0))
+    return pl.pallas_call(
+        functools.partial(send_kernel, tile=tile),
+        grid=(1,),
+        in_specs=[pair, pair] + [message] * len(codes),
+        out_specs=message,
         out_shape=jax.ShapeDtypeStruct((depth + EXTRA, piece), BF16),
         scratch_shapes=[pltpu.VMEM((depth, piece), F32)],
-        compiler_params=params(24),
+        compiler_params=params(16),
         cost_estimate=cost(400 * depth * piece, 18 * depth * piece),
         name="send",
-    )(*parts)
+    )(keep, mate, *codes)
+
+
+def expand_kernel(keep, mate, *refs, tile):
+    codes, (left, out, both) = refs[:-3], refs[-3:]
+    depth, piece = both.shape[0], out.shape[1]
+
+    @pl.when(pl.program_id(0) == 0)
+    def _():
+        value_at = summed(keep, mate, codes)
+
+        def put(i, carry):
+            rows = pl.ds(pl.multiple_of(i * tile, tile), tile)
+            high, low = kernel_split(value_at(rows))
+            both[rows, :piece] = high
+            both[rows, piece:] = low
+            return carry
+
+        lax.fori_loop(0, depth // tile, put, 0)
+
+    product = dot(left[...], both[...], ((1,), (0,)))
+    out[...] = product[:, :piece] + product[:, piece:]
+
+
+def expand(keep, mate, codes, left):
+    rows, inner = left.shape
+    _, depth, piece = keep.shape
+    step = min(1024, rows)
+    pair = pl.BlockSpec((1, depth, piece), lambda i: (0, 0, 0))
+    message = pl.BlockSpec((depth + EXTRA, piece), lambda i: (0, 0))
+    return pl.pallas_call(
+        functools.partial(expand_kernel, tile=min(64, depth)),
+        grid=(rows // step,),
+        in_specs=[pair, pair]
+        + [message] * len(codes)
+        + [pl.BlockSpec((step, inner), lambda i: (i, 0))],
+        out_specs=pl.BlockSpec((step, piece), lambda i: (i, 0)),
+        out_shape=jax.ShapeDtypeStruct((rows, piece), F32),
+        scratch_shapes=[pltpu.VMEM((depth, 2 * piece), BF16)],
+        compiler_params=params(36),
+        cost_estimate=cost(4 * rows * inner * piece, 4 * rows * piece + 2 * rows * inner),
+        name="expand",
+    )(keep, mate, *codes, left)
+
+
+def hop_kernel(place_ref, *refs, lines, step, tile):
+    blocks, refs = refs[:2], refs[2:]
+    arrived, outs, total = refs[:-3], refs[-3:-1], refs[-1]
+    depth = total.shape[0]
+    sends = (place_ref[0] < step, place_ref[0] >= lines - step)
+    for way in range(2):
+
+        @pl.when(sends[way])
+        def _(way=way):
+            scale = scale_of(arrived[way], depth) if arrived else None
+
+            def value_at(rows):
+                value = blocks[way][rows, :]
+                if arrived:
+                    value = value + decode(arrived[way][rows, :], scale)
+                return value
+
+            fill(outs[way], total, value_at, tile)
+
+
+def hop(place, product, arrived, lines, step):
+    depth, piece = product.shape[0] // lines, product.shape[1]
+    ahead = lines - step
+    message = pl.BlockSpec((depth + EXTRA, piece), lambda i, s: (0, 0))
+    return pl.pallas_call(
+        functools.partial(hop_kernel, lines=lines, step=step, tile=min(64, depth)),
+        grid_spec=pltpu.PrefetchScalarGridSpec(
+            num_scalar_prefetch=1,
+            grid=(1,),
+            in_specs=[
+                pl.BlockSpec(
+                    (depth, piece), lambda i, s: (jnp.minimum(s[0] + ahead, lines - 1), 0)
+                ),
+                pl.BlockSpec((depth, piece), lambda i, s: (jnp.maximum(s[0] - ahead, 0), 0)),
+            ]
+            + [message] * len(arrived),
+            out_specs=[message] * 2,
+            scratch_shapes=[pltpu.VMEM((depth, piece), F32)],
+        ),
+        out_shape=[jax.ShapeDtypeStruct((depth + EXTRA, piece), BF16)] * 2,
+        compiler_params=params(16),
+        cost_estimate=cost(400 * depth * piece, 12 * depth * piece),
+        name="hop",
+    )(place, product, product, *arrived)
+
+
+def finish_kernel(at_ref, block, up, down, *refs, tile):
+    out = refs[-1]
+    depth = out.shape[0]
+    scales = [scale_of(message, depth) for message in (up, down)]
+
+    def add(i, carry):
+        rows = pl.ds(pl.multiple_of(i * tile, tile), tile)
+        out[rows, :] = (
+            block[rows, :] + decode(up[rows, :], scales[0]) + decode(down[rows, :], scales[1])
+        )
+        return carry
+
+    lax.fori_loop(0, depth // tile, add, 0)
+
+
+def finish(at, product, arrived, update, chunk, depth, width):
+    piece = product.shape[1]
+    tile = min(64, depth)
+    message = pl.BlockSpec((depth + EXTRA, piece), lambda i, s: (0, 0))
+    extra = [] if update is None else [update]
+    return pl.pallas_call(
+        functools.partial(finish_kernel, tile=tile),
+        grid_spec=pltpu.PrefetchScalarGridSpec(
+            num_scalar_prefetch=1,
+            grid=(1,),
+            in_specs=[pl.BlockSpec((depth, piece), lambda i, s: (s[0], 0)), message, message]
+            + [pl.BlockSpec(memory_space=pl.ANY)] * len(extra),
+            out_specs=pl.BlockSpec((depth, piece), lambda i, s: (0, chunk)),
+        ),
+        out_shape=jax.ShapeDtypeStruct((depth, width), F32),
+        input_output_aliases={4: 0} if extra else {},
+        compiler_params=params(16),
+        cost_estimate=cost(400 * depth * piece, 12 * depth * piece),
+        name="finish",
+    )(at, product, *arrived, *extra)
 
 
 def update_kernel(place_ref, message, left, *refs, tile):
@@ -294,7 +444,7 @@
         ),
         out_shape=jax.ShapeDtypeStruct((depth, width), F32),
         input_output_aliases={3: 0} if extra else {},
-        compiler_params=params(24),
+        compiler_params=params(40),
         cost_estimate=cost(4 * depth * inner * piece * lines, 12 * depth * piece * lines),
         name="update_chunk",
     )(place, messages, left, *extra)
@@ -321,6 +471,12 @@
     def gather_row(value):
         return lax.all_gather(value, "row", axis=0, tiled=True)
 
+    def up(value, senders):
+        return lax.ppermute(value, "row", [(i, i + 1) for i in senders])
+
+    def down(value, senders):
+        return lax.ppermute(value, "row", [(i, i - 1) for i in senders])
+
     def local(gradient, first_moment, second_moment, left_basis, right_basis):
         me, place = lax.axis_index("col"), lax.axis_index("row")
         depth, width = gradient.shape
@@ -328,55 +484,63 @@
         index, spot = jnp.reshape(me, (1,)), jnp.reshape(place, (1,))
 
         gradients = gather_row(gradient)
+        early = CHUNKS - 1
         if depth == width:
-            parts = [
-                gather_row(lax.slice_in_dim(right_basis, p * piece, (p + 1) * piece))
-                for p in range(CHUNKS)
-            ]
+            near = gather_row(lax.slice_in_dim(right_basis, 0, early * piece))
+            final = gather_row(lax.slice_in_dim(right_basis, early * piece, width))
         else:
             blocks = gather_row(right_basis).reshape(cols, CHUNKS, piece, width)
-            parts = [blocks[:, p].reshape(cols * piece, width) for p in range(CHUNKS)]
+            near = blocks[:, :early].reshape(early * cols * piece, width)
+            final = blocks[:, early].reshape(cols * piece, width)
 
         left = place_by_distance(left_basis, me).reshape(-1, left_basis.shape[1])
-        halfway = dot(left, gradients, ((0,), (0,)))
-        pieces = by_distance(jnp.stack(split(halfway)))
-        pieces = [pieces[distance] for distance in range(cols)]
-
-        flipped = [flip(index, part, cols) for part in parts]
-        part = rotate_part(index, pieces, parts[:-1])
-        new_first, new_second, normed = rotate(
-            index, part, pieces, parts[-1], first_moment, second_moment
-        )
-
-        left_late, parts[-1] = lax.optimization_barrier((left, parts[-1]))
         quarter = depth // cols
         backs = []
         for back in range(lines):
             to = lax.rem(place + back, lines)
-            rows = lax.dynamic_slice_in_dim(left_late, to * depth + me * quarter, quarter, 0)
+            rows = lax.dynamic_slice_in_dim(left, to * depth + me * quarter, quarter, 0)
             if back:
                 rows = lax.ppermute(rows, "row", [(i, (i + back) % lines) for i in range(lines)])
             backs.append(rows)
-        backs = jnp.stack(backs)
-
-        sums, messages = [], []
+        left_rows = place_by_distance(jnp.stack(backs), me)
+        left, left_rows = lax.optimization_barrier((left, left_rows))
+
+        halfway = dot(left, gradients, ((0,), (0,)))
+        pieces = by_distance(jnp.stack(split(halfway)))
+        pieces = [pieces[distance] for distance in range(cols)]
+
+        flipped = [flip(index, near, cols, early, at) for at in range(early)]
+        flipped.append(flip(index, final, cols))
+        part = rotate_part(index, pieces, [near])
+        new_first, new_second, normed = rotate(
+            index, part, pieces, final, first_moment, second_moment
+        )
+
+        halves, coded = [], []
         for chunk in range(CHUNKS):
             if chunk >= 2:
-                normed, sums[chunk - 2] = lax.optimization_barrier((normed, sums[chunk - 2]))
+                normed, coded[chunk - 2] = lax.optimization_barrier((normed, coded[chunk - 2]))
             keep, mate = restore(normed, flipped[chunk], cols)
             mate = swap(mate, 1)
-            sums.append([keep[0], mate[0]] + [keep[d] + mate[d] for d in range(1, cols // 2)])
-        for chunk in range(CHUNKS):
-            terms = sums[chunk][:2]
-            for at, value in enumerate(sums[chunk][2:]):
-                terms.append(swap(value, 2 * at + 2))
-            if chunk == 1:
-                backs, terms = lax.optimization_barrier((backs, terms))
-            messages.append(gather_row(send(terms)))
-        left_rows = place_by_distance(backs, me)
-        update = None
-        for chunk in range(CHUNKS):
-            update = update_chunk(spot, messages[chunk], left_rows, update, chunk, depth, width)
+            halves.append((keep, mate))
+            coded.append([send(keep, mate, distance, []) for distance in range(2, cols, 2)])
+        crossed = [
+            [swap(code, 2 * at + 2) for at, code in enumerate(codes)] for codes in coded
+        ]
+        gathered = [gather_row(send(*halves[c], 0, crossed[c])) for c in (0, 3)]
+        products = [expand(*halves[c], crossed[c], left) for c in (1, 2)]
+        arrived = [(), ()]
+        for step in range(1, lines):
+            for at, product in enumerate(products):
+                upward, downward = hop(spot, product, arrived[at], lines, step)
+                arrived[at] = (
+                    up(upward, range(0, step)),
+                    down(downward, range(lines - step, lines)),
+                )
+        update = update_chunk(spot, gathered[0], left_rows, None, 0, depth, width)
+        for at, product in enumerate(products):
+            update = finish(spot, product, arrived[at], update, at + 1, depth, width)
+        update = update_chunk(spot, gathered[1], left_rows, update, 3, depth, width)
         return (new_first, new_second, update)
 
     return local

time: 668 us -> 624 us (0.934); the launches traced: 656 us -> 622 us
  waiting for transfers between devices: 441 us -> 375 us
  starting transfers between devices: 15.3 us -> 47.6 us
  Pallas kernels: 104 us -> 116 us
  other arithmetic: 12.1 us -> 4.25 us
    all_gather x9 -> x5, waiting for transfers between devices: 155 us -> 59.6 us  [gather_row(): return lax.all_gather(value, 'row', axis=0, tiled=True)]
    ppermute x0 -> x12, waiting for transfers between devices: none -> 33 us  [the longest x6 33 us: up(): return lax.ppermute(value, 'row', [(i, i + 1) for i in senders])]
    pallas_call x5 -> x17, Pallas kernels: 23.6 us -> 55.6 us  [the longest x1 17.9 us: rotate_part(): pl.pallas_call(functools.partial(rotate_part_kernel, cols=cols, sizes=siz...]
    ppermute x0 -> x12, starting transfers between devices: none -> 29.1 us  [the longest x6 23.5 us: up(): return lax.ppermute(value, 'row', [(i, i + 1) for i in senders])]
    pallas_call x4 -> x2, Pallas kernels: 40.9 us -> 20.4 us  [update_chunk(): pl.pallas_call(functools.partial(update_kernel, tile=tile), grid_spec=plt...]
    ppermute x17, waiting for transfers between devices: 232 us -> 218 us  [swap(): return lax.ppermute(value, 'col', [(i, i ^ distance) for i in range(cols)])]
    ppermute x3, waiting for transfers between devices: 52.7 us -> 64.3 us  [local(): lax.ppermute(rows, 'row', [(i, (i + back) % lines) for i in range(lines)])]
    add x4 -> x0, other arithmetic: 8.12 us -> none  [local(): keep[d] + mate[d]]
  transfers between devices with their start and end apart: 29 -> 37, of which waited for: 14 -> 17; matrix products, arithmetic and copies ran while one was open for 7% -> 5% of each run, Pallas kernels for 11% -> 12%
where the time goes in v5:
time: 624 us; the launch traced here: 622 us
  waiting for transfers between devices  375 us (60%)
  Pallas kernels  116 us (19%)
  local copies, waits for them, and re-layouts  50.8 us (8%)
  starting transfers between devices  47.6 us (8%)
  between operations  14.4 us (2%)
  matrix products  13.7 us (2%)
    ppermute x17, waiting for transfers between devices, swap(): return lax.ppermute(value, 'col', [(i, i ^ distance) for i in range(cols)])  218 us
    ppermute x3, waiting for transfers between devices, local(): lax.ppermute(rows, 'row', [(i, (i + back) % lines) for i in range(lines)])  64.3 us
    all_gather x5, waiting for transfers between devices, gather_row(): return lax.all_gather(value, 'row', axis=0, tiled=True)  59.6 us
    unnamed x66, local copies, waits for them, and re-layouts  36.5 us
    ppermute x6, waiting for transfers between devices, up(): return lax.ppermute(value, 'row', [(i, i + 1) for i in senders])  33 us
    pallas_call x4, Pallas kernels, restore(): pl.pallas_call(functools.partial(restore_kernel, cols=cols), grid=(depth...  23.6 us
    ppermute x6, starting transfers between devices, up(): return lax.ppermute(value, 'row', [(i, i + 1) for i in senders])  23.5 us
    pallas_call x2, Pallas kernels, update_chunk(): pl.pallas_call(functools.partial(update_kernel, tile=tile), grid_spec=plt...  20.4 us
  transfers between devices with their start and end apart: 37, of which 17 were waited for; matrix products, arithmetic and copies ran while one was open for 5% of the time, Pallas kernels for 12%

profile of v5, /device:TPU:0, one launch (start us, length us, event | category | flops | bytes accessed | tf_op | source)
XLA Modules:
  0.0 622.3 jit_solution(5662586367264063789)
XLA Ops:
  7.9 3.0 collective-permute-start
  11.0 45.8 %collective-permute-done = bf16[1024,1024]{1,0:T(8,128)(2,1)S(1)} collective-permute-done((bf16[1024,1024]{1,0:T(8,128)(2,1)}, bf16[1024,1024]{1,0:T(8,128)(2,1)S(1)}, u32[]{:S(2)}, u32[]{:S(2)}) %collective-permute-start) | collective-permute-done | bytes 2097184 | tf_op jit(solution)/shard_map/ppermute | solution.py:455
  59.0 1.9 bitcast_dynamic-update-slice_fusion.5
  61.1 1.9 bitcast_dynamic-update-slice_fusion.4
  63.2 1.9 collective-permute-start.3
  65.1 2.6 collective-permute-start.4
  69.0 22.1 %collective-permute-done.3 = bf16[256,1024]{1,0:T(8,128)(2,1)S(1)} collective-permute-done((bf16[256,1024]{1,0:T(8,128)(2,1)S(1)}, bf16[256,1024]{1,0:T(8,128)(2,1)S(1)}, u32[]{:S(2)}, u32[]{:S(2)}) %collective-permute-start.3) | collective-permute-done | bytes 524320 | tf_op jit(solution)/shard_map/ppermute | solution.py:503
  91.1 39.5 %collective-permute-done.4 = bf16[256,1024]{1,0:T(8,128)(2,1)S(1)} collective-permute-done((bf16[256,1024]{1,0:T(8,128)(2,1)S(1)}, bf16[256,1024]{1,0:T(8,128)(2,1)S(1)}, u32[]{:S(2)}, u32[]{:S(2)}) %collective-permute-start.4) | collective-permute-done | bytes 524320 | tf_op jit(solution)/shard_map/ppermute | solution.py:503
  130.6 2.7 collective-permute-done.5
  133.3 1.6 pad_maximum_fusion.1
  136.4 45.8 %collective-permute-done.6 = bf16[4,256,1024]{2,1,0:T(8,128)(2,1)} collective-permute-done((bf16[4,256,1024]{2,1,0:T(8,128)(2,1)}, bf16[4,256,1024]{2,1,0:T(8,128)(2,1)}, u32[]{:S(2)}, u32[]{:S(2)}) %collective-permute-start.6) | collective-permute-done | bytes 2097184 | tf_op jit(solution)/shard_map/ppermute | solution.py:455
  185.1 1.9 bitcast_dynamic-update-slice_fusion.2
  186.9 1.9 bitcast_dynamic-update-slice_fusion.1
  188.8 1.9 bitcast_dynamic-update-slice_fusion.left
  190.7 3.3 copy-done.9
  194.1 12.5 %all-gather.6.cloned.1.call-done = bf16[4096,1024]{1,0:T(8,128)(2,1)} async-done(((bf16[1024,1024]{1,0:T(8,128)(2,1)}), bf16[4096,1024]{1,0:T(8,128)(2,1)}) %all-gather.6.cloned.1.call-update) | async-done | bytes 8388624 | tf_op jit(solution)/shard_map/all_gather | solution.py:472
  206.6 13.7 %fusion.2 = (bf16[1,1024,1024]{2,1,0:T(8,128)(2,1)S(1)}, bf16[1,1024,1024]{2,1,0:T(8,128)(2,1)S(1)}) fusion(bf16[4096,1024]{1,0:T(8,128)(2,1)} %bitcast.33, bf16[4096,1024]{1,0:T(8,128)(2,1)} %all-gather.6.cloned.1.call-done), kind=kOutput, calls=%fused_computation.5 | convolution fusion | flops 8594128896 | bytes 20971520 | tf_op jit(solution)/shard_map/dot_general | solution.py:38
  220.3 2.4 pad_maximum_fusion.refs_0_
  224.2 91.4 %collective-permute-done.10.refs_2_ = bf16[2,1024,1024]{2,1,0:T(8,128)(2,1)} collective-permute-done((bf16[2,1024,1024]{2,1,0:T(8,128)(2,1)}, bf16[2,1024,1024]{2,1,0:T(8,128)(2,1)}, u32[]{:S(2)}, u32[]{:S(2)}) %collective-permute-start.10) | collective-permute-done | bytes 4194336 | tf_op jit(solution)/shard_map/ppermute | solution.py:455
  316.6 18.5 %all-gather.8.cloned.1.call-done.refs_4_.rows = bf16[3072,1024]{1,0:T(8,128)(2,1)} async-done(((bf16[768,1024]{1,0:T(8,128)(2,1)}), bf16[3072,1024]{1,0:T(8,128)(2,1)}) %all-gather.8.cloned.1.call-update) | async-done | bytes 6291472 | tf_op jit(solution)/shard_map/all_gather | solution.py:472
  335.2 2.8 copy-done.4
  339.0 17.9 %rotate_part.1.part = f32[1024,1024]{1,0:T(8,128)S(1)} custom-call(s32[1]{0:T(128)} %bitcast.me_ref, bf16[2,1024,1024]{2,1,0:T(8,128)(2,1)} %pad_maximum_fusion.refs_0_, bf16[2,1024,1024]{2,1,0:T(8,128)(2,1)} %collective-permute-done.9.refs_1_, bf16[2,1024,1024]{2,1,0:T(8,128)(2,1)} %collective-permute-done.10.refs_2_, ...), custom_call_target="tpu_custom_call" | custom-call | flops 128849016 | bytes 209715 | tf_op jit(solution)/shard_map/rotate_part/pallas_call | solution.py:90
  357.0 2.0 copy-done.14
  358.9 28.5 %all-gather.10.cloned.1.call-done.refs_4_.rows = bf16[1024,1024]{1,0:T(8,128)(2,1)} async-done(((bf16[256,1024]{1,0:T(8,128)(2,1)}), bf16[1024,1024]{1,0:T(8,128)(2,1)}) %all-gather.10.cloned.1.call-update) | async-done | bytes 2097168 | tf_op jit(solution)/shard_map/all_gather | solution.py:472
  387.5 1.6 copy-done.15
  389.1 12.2 %rotate.1 = (f32[1024,1024]{1,0:T(8,128)}, f32[1024,1024]{1,0:T(8,128)}, bf16[2,1024,1024]{2,1,0:T(8,128)(2,1)S(1)}) custom-call(s32[1]{0:T(128)} %bitcast.me_ref, f32[1024,1024]{1,0:T(8,128)} %copy-done.14, bf16[2,1024,1024]{2,1,0:T(8,128)(2,1)} %pad_maximum_fusion.refs_0_, bf16[2,1024,1024]{2,1,0:T(8,128)(2,1)} %collective-permute-done.9.refs_1_, ...), custom_call_target="tpu_custom_call" | custom-call | flops 42949672 | bytes 314572 | tf_op jit(solution)/shard_map/rotate/pallas_call | solution.py:137
  401.2 5.6 restore.4
  406.9 2.8 copy-done.5
  410.7 6.2 %restore.5 = (f32[2,1024,256]{2,1,0:T(8,128)S(1)}, f32[2,1024,256]{2,1,0:T(8,128)}) custom-call(bf16[2,1024,1024]{2,1,0:T(8,128)(2,1)S(1)} %get-tuple-element.41.normed, bf16[1024,1024]{1,0:T(8,128)(2,1)S(1)} %flip.5.flipped), custom_call_target="tpu_custom_call" | custom-call | flops 42949672 | bytes 83886 | tf_op jit(solution)/shard_map/restore/pallas_call | solution.py:177
  421.1 12.6 %collective-permute-done.31.refs_0_ = bf16[1040,256]{1,0:T(8,128)(2,1)S(1)} collective-permute-done((bf16[1040,256]{1,0:T(8,128)(2,1)S(1)}, bf16[1040,256]{1,0:T(8,128)(2,1)S(1)}, u32[]{:S(2)}, u32[]{:S(2)}) %collective-permute-start.31) | collective-permute-done | bytes 532512 | tf_op jit(solution)/shard_map/ppermute | solution.py:455
  433.7 2.4 send.11
  437.2 2.1 copy-done.18
  439.3 2.2 send.7
  441.5 5.6 restore.6
  448.3 6.2 %restore.7 = (f32[2,1024,256]{2,1,0:T(8,128)S(1)}, f32[2,1024,256]{2,1,0:T(8,128)}) custom-call(bf16[2,1024,1024]{2,1,0:T(8,128)(2,1)S(1)} %copy-done.13, bf16[1024,1024]{1,0:T(8,128)(2,1)S(1)} %flip.7.flipped), custom_call_target="tpu_custom_call" | custom-call | flops 42949672 | bytes 83886 | tf_op jit(solution)/shard_map/restore/pallas_call | solution.py:177
  457.2 1.5 collective-permute-start.15
  458.7 12.6 %collective-permute-done.15.refs_0_ = bf16[1040,256]{1,0:T(8,128)(2,1)S(1)} collective-permute-done((bf16[1040,256]{1,0:T(8,128)(2,1)S(1)}, bf16[1040,256]{1,0:T(8,128)(2,1)S(1)}, u32[]{:S(2)}, u32[]{:S(2)}) %collective-permute-start.15) | collective-permute-done | bytes 532512 | tf_op jit(solution)/shard_map/ppermute | solution.py:455
  471.3 2.4 send.9
  473.7 1.5 collective-permute-start.24
  475.3 1.6 copy-done.21
  476.8 2.0 send.10
  479.5 9.3 %collective-permute-done.24.refs_0_ = bf16[1040,256]{1,0:T(8,128)(2,1)S(1)} collective-permute-done((bf16[1040,256]{1,0:T(8,128)(2,1)S(1)}, bf16[1040,256]{1,0:T(8,128)(2,1)S(1)}, u32[]{:S(2)}, u32[]{:S(2)}) %collective-permute-start.24) | collective-permute-done | bytes 532512 | tf_op jit(solution)/shard_map/ppermute | solution.py:455
  488.8 3.6 copy-done.7
  492.4 7.1 %expand.3.refs_0_.refs_1_.block = f32[4096,256]{1,0:T(8,128)S(1)} custom-call(f32[2,1024,256]{2,1,0:T(8,128)S(1)} %copy-done.19, f32[2,1024,256]{2,1,0:T(8,128)} %collective-permute-done.13.mate, bf16[1040,256]{1,0:T(8,128)(2,1)S(1)} %collective-permute-done.24.refs_0_, bf16[4096,1024]{1,0:T(8,128)(2,1)S(1)} %bitcast.34), custom_call_target="tpu_custom_call" | custom-call | flops 42949672 | bytes 125829 | tf_op jit(solution)/shard_map/expand/pallas_call | solution.py:300
  500.3 1.7 collective-permute-start.25
  502.7 3.4 copy-done.8
  506.1 7.1 %expand.2.refs_0_.refs_1_.block = f32[4096,256]{1,0:T(8,128)S(1)} custom-call(f32[2,1024,256]{2,1,0:T(8,128)S(1)} %copy-done.22, f32[2,1024,256]{2,1,0:T(8,128)} %collective-permute-done.16.mate, bf16[1040,256]{1,0:T(8,128)(2,1)S(1)} %collective-permute-done.17.refs_0_, bf16[4096,1024]{1,0:T(8,128)(2,1)S(1)} %bitcast.35), custom_call_target="tpu_custom_call" | custom-call | flops 42949672 | bytes 125829 | tf_op jit(solution)/shard_map/expand/pallas_call | solution.py:300
  516.1 9.7 %collective-permute-done.25.refs_2_ = bf16[1040,256]{1,0:T(8,128)(2,1)S(1)} collective-permute-done((bf16[1040,256]{1,0:T(8,128)(2,1)S(1)}, bf16[1040,256]{1,0:T(8,128)(2,1)S(1)}, u32[]{:S(2)}, u32[]{:S(2)}) %collective-permute-start.25) | collective-permute-done | bytes 532512 | tf_op jit(solution)/shard_map/ppermute | solution.py:475
  527.3 4.4 collective-permute-start.27
  532.4 15.9 %collective-permute-done.18.refs_2_ = bf16[1040,256]{1,0:T(8,128)(2,1)S(1)} collective-permute-done((bf16[1040,256]{1,0:T(8,128)(2,1)S(1)}, bf16[1040,256]{1,0:T(8,128)(2,1)S(1)}, u32[]{:S(2)}, u32[]{:S(2)}) %collective-permute-start.18) | collective-permute-done | bytes 532512 | tf_op jit(solution)/shard_map/ppermute | solution.py:475
  549.8 4.4 collective-permute-start.20
  555.1 4.6 collective-permute-done.27.refs_2_
  561.2 5.9 collective-permute-start.29
  568.4 2.8 collective-permute-done.20.refs_2_
  571.1 2.5 hop.8
  573.6 5.9 collective-permute-start.22
  580.8 3.4 copy-done.10
  584.2 1.6 copy-done.23
  585.8 10.2 %update_chunk.2.refs_0_ = f32[1024,1024]{1,0:T(8,128)} custom-call(s32[1]{0:T(128)} %bitcast.16.place_ref.at_ref, bf16[4160,256]{1,0:T(8,128)(2,1)S(1)} %copy-done.23, bf16[4,4,256,1024]{3,2,1,0:T(8,128)(2,1)S(1)} %copy-done.10), custom_call_target="tpu_custom_call" | custom-call | flops 42949672 | bytes 125829 | tf_op jit(solution)/shard_map/update_chunk/pallas_call | solution.py:429
  596.0 2.2 finish.2.refs_0_
  598.3 2.2 finish.3.refs_0_
  600.5 3.4 copy-done.11
  603.9 1.6 copy-done.24
  605.5 10.2 %update_chunk.3 = f32[1024,1024]{1,0:T(8,128)} custom-call(s32[1]{0:T(128)} %bitcast.16.place_ref.at_ref, bf16[4160,256]{1,0:T(8,128)(2,1)S(1)} %copy-done.24, bf16[4,4,256,1024]{3,2,1,0:T(8,128)(2,1)S(1)} %copy-done.11, f32[1024,1024]{1,0:T(8,128)} %finish.3.refs_0_), custom_call_target="tpu_custom_call", output_to_operand_aliasing={{}: (3, {})} | custom-call | flops 42949672 | bytes 125829 | tf_op jit(solution)/shard_map/update_chunk/pallas_call | solution.py:429
  (126 shorter events, 36.3 us)
Async XLA Ops:
  7.2 199.4 %all-gather.6.cloned.1.call-start = ((), (), s32[]{:S(2)}) async-start(), calls=%async_computation | async-start | bytes 10485760 | tf_op jit(solution)/shard_map/all_gather | solution.py:472
  7.9 327.3 %all-gather.8.cloned.1.call-start = ((), (), s32[]{:S(2)}) async-start(), calls=%async_computation.1 | async-start | bytes 7864320 | tf_op jit(solution)/shard_map/all_gather | solution.py:472
  7.9 48.8 %collective-permute-start = (bf16[1024,1024]{1,0:T(8,128)(2,1)}, bf16[1024,1024]{1,0:T(8,128)(2,1)S(1)}, u32[]{:S(2)}, u32[]{:S(2)}) collective-permute-start(bf16[1024,1024]{1,0:T(8,128)(2,1)} %param.8), channel_id=1, source_target_pairs={{0,2},{1,3},{2,0},{3,1},{4,6},{5,7},{6,4},{7,5},{8,10},{9,11},{10,... | collective-permute-start | bytes 6291464 | tf_op jit(solution)/shard_map/ppermute | solution.py:455
  10.9 48.0 %collective-permute-start.1 = (bf16[1024,1024]{1,0:T(8,128)(2,1)}, bf16[1024,1024]{1,0:T(8,128)(2,1)}, u32[]{:S(2)}, u32[]{:S(2)}) collective-permute-start(bf16[1024,1024]{1,0:T(8,128)(2,1)} %param.8), channel_id=1, source_target_pairs={{0,1},{1,0},{2,3},{3,2},{4,5},{5,4},{6,7},{7,6},{8,9},{9,8},{10,11... | collective-permute-start | bytes 6291464 | tf_op jit(solution)/shard_map/ppermute | solution.py:455
  56.8 4.3 collective-permute-start.2
  56.8 1.6 copy-start.26
  63.0 71.9 %copy-start.6 = (bf16[4,1024,1024]{2,1,0:T(8,128)(2,1)}, bf16[4,1024,1024]{2,1,0:T(8,128)(2,1)S(1)}, u32[]{:S(2)}) copy-start(bf16[4,1024,1024]{2,1,0:T(8,128)(2,1)S(1)} %bitcast_dynamic-update-slice_fusion.4) | copy-start | bytes 25165828
  63.0 119.2 %copy-start.25 = (bf16[1024,1024]{1,0:T(8,128)(2,1)S(1)}, bf16[1024,1024]{1,0:T(8,128)(2,1)}, u32[]{:S(2)}) copy-start(bf16[1024,1024]{1,0:T(8,128)(2,1)} %param.9) | copy-start | bytes 6291460
  63.2 27.9 %collective-permute-start.3 = (bf16[256,1024]{1,0:T(8,128)(2,1)S(1)}, bf16[256,1024]{1,0:T(8,128)(2,1)S(1)}, u32[]{:S(2)}, u32[]{:S(2)}) collective-permute-start(bf16[256,1024]{1,0:T(8,128)(2,1)S(1)} %get-tuple-element.64), channel_id=1, source_target_pairs={{0,4},{4,8},{8,12},{12,0},{1,5},{5,9},{9,13},{13,1},{2,6},{6,10},{... | collective-permute-start | bytes 1572872 | tf_op jit(solution)/shard_map/ppermute | solution.py:503
  65.1 65.5 %collective-permute-start.4 = (bf16[256,1024]{1,0:T(8,128)(2,1)S(1)}, bf16[256,1024]{1,0:T(8,128)(2,1)S(1)}, u32[]{:S(2)}, u32[]{:S(2)}) collective-permute-start(bf16[256,1024]{1,0:T(8,128)(2,1)S(1)} %get-tuple-element.63), channel_id=1, source_target_pairs={{0,8},{4,12},{8,0},{12,4},{1,9},{5,13},{9,1},{13,5},{2,10},{6,14},... | collective-permute-start | bytes 1572872 | tf_op jit(solution)/shard_map/ppermute | solution.py:503
  67.7 65.6 %collective-permute-start.5 = (bf16[256,1024]{1,0:T(8,128)(2,1)S(1)}, bf16[256,1024]{1,0:T(8,128)(2,1)S(1)}, u32[]{:S(2)}, u32[]{:S(2)}) collective-permute-start(bf16[256,1024]{1,0:T(8,128)(2,1)S(1)} %get-tuple-element.62), channel_id=1, source_target_pairs={{0,12},{4,0},{8,4},{12,8},{1,13},{5,1},{9,5},{13,9},{2,14},{6,2},{... | collective-permute-start | bytes 1572872 | tf_op jit(solution)/shard_map/ppermute | solution.py:503
  130.6 5.8 copy-start.27
  133.3 3.1 copy-start.29
  134.9 47.3 %collective-permute-start.6 = (bf16[4,256,1024]{2,1,0:T(8,128)(2,1)}, bf16[4,256,1024]{2,1,0:T(8,128)(2,1)}, u32[]{:S(2)}, u32[]{:S(2)}) collective-permute-start(bf16[4,256,1024]{2,1,0:T(8,128)(2,1)} %pad_maximum_fusion.1), channel_id=1, source_target_pairs={{0,2},{1,3},{2,0},{3,1},{4,6},{5,7},{6,4},{7,5},{8,10},{9,11},{10,... | collective-permute-start | bytes 6291464 | tf_op jit(solution)/shard_map/ppermute | solution.py:455
  136.4 50.5 %collective-permute-start.7 = (bf16[4,256,1024]{2,1,0:T(8,128)(2,1)}, bf16[4,256,1024]{2,1,0:T(8,128)(2,1)}, u32[]{:S(2)}, u32[]{:S(2)}) collective-permute-start(bf16[4,256,1024]{2,1,0:T(8,128)(2,1)} %pad_maximum_fusion.1), channel_id=1, source_target_pairs={{0,1},{1,0},{2,3},{3,2},{4,5},{5,4},{6,7},{7,6},{8,9},{9,8},{10,11... | collective-permute-start | bytes 6291464 | tf_op jit(solution)/shard_map/ppermute | solution.py:455
  182.2 6.6 %collective-permute-start.8 = (bf16[4,256,1024]{2,1,0:T(8,128)(2,1)}, bf16[4,256,1024]{2,1,0:T(8,128)(2,1)}, u32[]{:S(2)}, u32[]{:S(2)}) collective-permute-start(bf16[4,256,1024]{2,1,0:T(8,128)(2,1)} %collective-permute-done.6), channel_id=1, source_target_pairs={{0,1},{1,0},{2,3},{3,2},{4,5},{5,4},{6,7},{7,6},{8,9},{9,8},{10,11... | collective-permute-start | bytes 6291464 | tf_op jit(solution)/shard_map/ppermute | solution.py:455
  183.5 204.0 %all-gather.10.cloned.1.call-start = ((), (), s32[]{:S(2)}) async-start(), calls=%async_computation.2 | async-start | bytes 2621440 | tf_op jit(solution)/shard_map/all_gather | solution.py:472
  190.7 3.3 copy-start.9
  222.7 92.8 %collective-permute-start.10 = (bf16[2,1024,1024]{2,1,0:T(8,128)(2,1)}, bf16[2,1024,1024]{2,1,0:T(8,128)(2,1)}, u32[]{:S(2)}, u32[]{:S(2)}) collective-permute-start(bf16[2,1024,1024]{2,1,0:T(8,128)(2,1)} %pad_maximum_fusion.refs_0_), channel_id=1, source_target_pairs={{0,2},{1,3},{2,0},{3,1},{4,6},{5,7},{6,4},{7,5},{8,10},{9,11},{10,... | collective-permute-start | bytes 12582920 | tf_op jit(solution)/shard_map/ppermute | solution.py:455
  224.2 114.8 %collective-permute-start.9 = (bf16[2,1024,1024]{2,1,0:T(8,128)(2,1)}, bf16[2,1024,1024]{2,1,0:T(8,128)(2,1)}, u32[]{:S(2)}, u32[]{:S(2)}) collective-permute-start(bf16[2,1024,1024]{2,1,0:T(8,128)(2,1)} %pad_maximum_fusion.refs_0_), channel_id=1, source_target_pairs={{0,1},{1,0},{2,3},{3,2},{4,5},{5,4},{6,7},{7,6},{8,9},{9,8},{10,11... | collective-permute-start | bytes 12582920 | tf_op jit(solution)/shard_map/ppermute | solution.py:455
  315.5 23.5 %collective-permute-start.11 = (bf16[2,1024,1024]{2,1,0:T(8,128)(2,1)}, bf16[2,1024,1024]{2,1,0:T(8,128)(2,1)}, u32[]{:S(2)}, u32[]{:S(2)}) collective-permute-start(bf16[2,1024,1024]{2,1,0:T(8,128)(2,1)} %collective-permute-done.10.refs_2_), channel_id=1, source_target_pairs={{0,1},{1,0},{2,3},{3,2},{4,5},{5,4},{6,7},{7,6},{8,9},{9,8},{10,11... | collective-permute-start | bytes 12582920 | tf_op jit(solution)/shard_map/ppermute | solution.py:455
  316.4 264.4 %all-gather.14.cloned.1.call-start = ((), (), s32[]{:S(2)}) async-start(), calls=%async_computation.4 | async-start | bytes 2662400 | tf_op jit(solution)/shard_map/all_gather | solution.py:472
  335.2 2.8 copy-start.4
  357.0 2.0 copy-start.14
  401.2 9.5 %copy-start.12 = (bf16[2,1024,1024]{2,1,0:T(8,128)(2,1)}, bf16[2,1024,1024]{2,1,0:T(8,128)(2,1)S(1)}, u32[]{:S(2)}) copy-start(bf16[2,1024,1024]{2,1,0:T(8,128)(2,1)S(1)} %get-tuple-element.41.normed) | copy-start | bytes 12582916
  406.8 11.9 %collective-permute-start.12 = (f32[2,1024,256]{2,1,0:T(8,128)S(1)}, f32[2,1024,256]{2,1,0:T(8,128)S(1)}, u32[]{:S(2)}, u32[]{:S(2)}) collective-permute-start(f32[2,1024,256]{2,1,0:T(8,128)S(1)} %get-tuple-element.37), channel_id=1, source_target_pairs={{0,1},{1,0},{2,3},{3,2},{4,5},{5,4},{6,7},{7,6},{8,9},{9,8},{10,11... | collective-permute-start | bytes 6291464 | tf_op jit(solution)/shard_map/ppermute | solution.py:455
  406.9 2.8 copy-start.5
  418.3 19.0 %collective-permute-start.13 = (f32[2,1024,256]{2,1,0:T(8,128)}, f32[2,1024,256]{2,1,0:T(8,128)}, u32[]{:S(2)}, u32[]{:S(2)}) collective-permute-start(f32[2,1024,256]{2,1,0:T(8,128)} %get-tuple-element.40), channel_id=1, source_target_pairs={{0,1},{1,0},{2,3},{3,2},{4,5},{5,4},{6,7},{7,6},{8,9},{9,8},{10,11... | collective-permute-start | bytes 6291464 | tf_op jit(solution)/shard_map/ppermute | solution.py:455
  418.8 17.4 %copy-start.16 = (bf16[1024,1024]{1,0:T(8,128)(2,1)S(1)}, bf16[1024,1024]{1,0:T(8,128)(2,1)}, u32[]{:S(2)}) copy-start(bf16[1024,1024]{1,0:T(8,128)(2,1)} %all-gather.10.cloned.1.call-done.refs_4_.rows) | copy-start | bytes 6291460
  419.6 14.1 %collective-permute-start.31 = (bf16[1040,256]{1,0:T(8,128)(2,1)S(1)}, bf16[1040,256]{1,0:T(8,128)(2,1)S(1)}, u32[]{:S(2)}, u32[]{:S(2)}) collective-permute-start(bf16[1040,256]{1,0:T(8,128)(2,1)S(1)} %send.6), channel_id=1, source_target_pairs={{0,2},{1,3},{2,0},{3,1},{4,6},{5,7},{6,4},{7,5},{8,10},{9,11},{10,... | collective-permute-start | bytes 1597448 | tf_op jit(solution)/shard_map/ppermute | solution.py:455
  436.1 164.4 %all-gather.12.cloned.1.call-start = ((), (), s32[]{:S(2)}) async-start(), calls=%async_computation.3 | async-start | bytes 2662400 | tf_op jit(solution)/shard_map/all_gather | solution.py:472
  436.1 5.4 copy-start.13
  436.2 11.0 %slice-start = ((s8[6291456]{0:T(1024)(128)(4,1)}), s8[4194304]{0:T(1024)(128)(4,1)S(1)}, s32[]{:S(2)}) async-start(s8[6291456]{0:T(1024)(128)(4,1)} %bitcast.30), calls=%async_computation.5 | async-start | bytes 8388608
  437.2 2.1 copy-start.18
  439.3 7.9 %slice-start.1 = ((s8[6291456]{0:T(1024)(128)(4,1)}), s8[2097152]{0:T(1024)(128)(4,1)S(1)}, s32[]{:S(2)}) async-start(s8[6291456]{0:T(1024)(128)(4,1)} %bitcast.30), calls=%async_computation.6 | async-start | bytes 4194304
  447.1 9.2 %collective-permute-start.14 = (f32[2,1024,256]{2,1,0:T(8,128)S(1)}, f32[2,1024,256]{2,1,0:T(8,128)S(1)}, u32[]{:S(2)}, u32[]{:S(2)}) collective-permute-start(f32[2,1024,256]{2,1,0:T(8,128)S(1)} %get-tuple-element.43), channel_id=1, source_target_pairs={{0,1},{1,0},{2,3},{3,2},{4,5},{5,4},{6,7},{7,6},{8,9},{9,8},{10,11... | collective-permute-start | bytes 6291464 | tf_op jit(solution)/shard_map/ppermute | solution.py:455
  455.9 19.3 %collective-permute-start.16 = (f32[2,1024,256]{2,1,0:T(8,128)}, f32[2,1024,256]{2,1,0:T(8,128)}, u32[]{:S(2)}, u32[]{:S(2)}) collective-permute-start(f32[2,1024,256]{2,1,0:T(8,128)} %get-tuple-element.46), channel_id=1, source_target_pairs={{0,1},{1,0},{2,3},{3,2},{4,5},{5,4},{6,7},{7,6},{8,9},{9,8},{10,11... | collective-permute-start | bytes 6291464 | tf_op jit(solution)/shard_map/ppermute | solution.py:455
  457.2 31.6 %copy-start.19 = (f32[2,1024,256]{2,1,0:T(8,128)S(1)}, f32[2,1024,256]{2,1,0:T(8,128)}, u32[]{:S(2)}) copy-start(f32[2,1024,256]{2,1,0:T(8,128)} %copy-done.17) | copy-start | bytes 6291460
  457.2 14.1 %collective-permute-start.15 = (bf16[1040,256]{1,0:T(8,128)(2,1)S(1)}, bf16[1040,256]{1,0:T(8,128)(2,1)S(1)}, u32[]{:S(2)}, u32[]{:S(2)}) collective-permute-start(bf16[1040,256]{1,0:T(8,128)(2,1)S(1)} %send.8), channel_id=1, source_target_pairs={{0,2},{1,3},{2,0},{3,1},{4,6},{5,7},{6,4},{7,5},{8,10},{9,11},{10,... | collective-permute-start | bytes 1597448 | tf_op jit(solution)/shard_map/ppermute | solution.py:455
  473.7 15.1 %collective-permute-start.24 = (bf16[1040,256]{1,0:T(8,128)(2,1)S(1)}, bf16[1040,256]{1,0:T(8,128)(2,1)S(1)}, u32[]{:S(2)}, u32[]{:S(2)}) collective-permute-start(bf16[1040,256]{1,0:T(8,128)(2,1)S(1)} %send.7), channel_id=1, source_target_pairs={{0,2},{1,3},{2,0},{3,1},{4,6},{5,7},{6,4},{7,5},{8,10},{9,11},{10,... | collective-permute-start | bytes 1597448 | tf_op jit(solution)/shard_map/ppermute | solution.py:455
  478.9 23.8 %collective-permute-start.17 = (bf16[1040,256]{1,0:T(8,128)(2,1)S(1)}, bf16[1040,256]{1,0:T(8,128)(2,1)S(1)}, u32[]{:S(2)}, u32[]{:S(2)}) collective-permute-start(bf16[1040,256]{1,0:T(8,128)(2,1)S(1)} %send.10), channel_id=1, source_target_pairs={{0,2},{1,3},{2,0},{3,1},{4,6},{5,7},{6,4},{7,5},{8,10},{9,11},{10,... | collective-permute-start | bytes 1597448 | tf_op jit(solution)/shard_map/ppermute | solution.py:455
  488.8 3.6 copy-start.7
  499.5 60.2 %copy-start = (f32[4096,256]{1,0:T(8,128)}, f32[4096,256]{1,0:T(8,128)S(1)}, u32[]{:S(2)}) copy-start(f32[4096,256]{1,0:T(8,128)S(1)} %expand.3.refs_0_.refs_1_.block) | copy-start | bytes 12582916
  499.5 3.2 copy-start.22
  500.3 25.5 %collective-permute-start.25 = (bf16[1040,256]{1,0:T(8,128)(2,1)S(1)}, bf16[1040,256]{1,0:T(8,128)(2,1)S(1)}, u32[]{:S(2)}, u32[]{:S(2)}) collective-permute-start(bf16[1040,256]{1,0:T(8,128)(2,1)S(1)} %get-tuple-element.54), channel_id=1, source_target_pairs={{0,4},{1,5},{2,6},{3,7},{16,20},{17,21},{18,22},{19,23}} | collective-permute-start | bytes 1597448 | tf_op jit(solution)/shard_map/ppermute | solution.py:475
  502.0 23.8 %collective-permute-start.26 = (bf16[1040,256]{1,0:T(8,128)(2,1)S(1)}, bf16[1040,256]{1,0:T(8,128)(2,1)S(1)}, u32[]{:S(2)}, u32[]{:S(2)}) collective-permute-start(bf16[1040,256]{1,0:T(8,128)(2,1)S(1)} %get-tuple-element.55), channel_id=1, source_target_pairs={{12,8},{13,9},{14,10},{15,11},{28,24},{29,25},{30,26},{31,27}} | collective-permute-start | bytes 1597448 | tf_op jit(solution)/shard_map/ppermute | solution.py:478
  502.7 3.4 copy-start.8
  513.2 57.9 %copy-start.2 = (f32[4096,256]{1,0:T(8,128)}, f32[4096,256]{1,0:T(8,128)S(1)}, u32[]{:S(2)}) copy-start(f32[4096,256]{1,0:T(8,128)S(1)} %expand.2.refs_0_.refs_1_.block) | copy-start | bytes 12582916
  514.0 34.3 %collective-permute-start.18 = (bf16[1040,256]{1,0:T(8,128)(2,1)S(1)}, bf16[1040,256]{1,0:T(8,128)(2,1)S(1)}, u32[]{:S(2)}, u32[]{:S(2)}) collective-permute-start(bf16[1040,256]{1,0:T(8,128)(2,1)S(1)} %get-tuple-element.47), channel_id=1, source_target_pairs={{0,4},{1,5},{2,6},{3,7},{16,20},{17,21},{18,22},{19,23}} | collective-permute-start | bytes 1597448 | tf_op jit(solution)/shard_map/ppermute | solution.py:475
  515.4 33.0 %collective-permute-start.19 = (bf16[1040,256]{1,0:T(8,128)(2,1)S(1)}, bf16[1040,256]{1,0:T(8,128)(2,1)S(1)}, u32[]{:S(2)}, u32[]{:S(2)}) collective-permute-start(bf16[1040,256]{1,0:T(8,128)(2,1)S(1)} %get-tuple-element.48), channel_id=1, source_target_pairs={{12,8},{13,9},{14,10},{15,11},{28,24},{29,25},{30,26},{31,27}} | collective-permute-start | bytes 1597448 | tf_op jit(solution)/shard_map/ppermute | solution.py:478
  527.3 32.5 %collective-permute-start.27 = (bf16[1040,256]{1,0:T(8,128)(2,1)S(1)}, bf16[1040,256]{1,0:T(8,128)(2,1)S(1)}, u32[]{:S(2)}, u32[]{:S(2)}) collective-permute-start(bf16[1040,256]{1,0:T(8,128)(2,1)S(1)} %get-tuple-element.56), channel_id=1, source_target_pairs={{0,4},{4,8},{1,5},{5,9},{2,6},{6,10},{3,7},{7,11},{16,20},{20,24},... | collective-permute-start | bytes 1597448 | tf_op jit(solution)/shard_map/ppermute | solution.py:475
  531.7 28.0 %collective-permute-start.28 = (bf16[1040,256]{1,0:T(8,128)(2,1)S(1)}, bf16[1040,256]{1,0:T(8,128)(2,1)S(1)}, u32[]{:S(2)}, u32[]{:S(2)}) collective-permute-start(bf16[1040,256]{1,0:T(8,128)(2,1)S(1)} %get-tuple-element.57), channel_id=1, source_target_pairs={{8,4},{12,8},{9,5},{13,9},{10,6},{14,10},{11,7},{15,11},{24,20},{2... | collective-permute-start | bytes 1597448 | tf_op jit(solution)/shard_map/ppermute | solution.py:478
  549.8 21.4 %collective-permute-start.20 = (bf16[1040,256]{1,0:T(8,128)(2,1)S(1)}, bf16[1040,256]{1,0:T(8,128)(2,1)S(1)}, u32[]{:S(2)}, u32[]{:S(2)}) collective-permute-start(bf16[1040,256]{1,0:T(8,128)(2,1)S(1)} %get-tuple-element.49), channel_id=1, source_target_pairs={{0,4},{4,8},{1,5},{5,9},{2,6},{6,10},{3,7},{7,11},{16,20},{20,24},... | collective-permute-start | bytes 1597448 | tf_op jit(solution)/shard_map/ppermute | solution.py:475
  554.2 16.9 %collective-permute-start.21 = (bf16[1040,256]{1,0:T(8,128)(2,1)S(1)}, bf16[1040,256]{1,0:T(8,128)(2,1)S(1)}, u32[]{:S(2)}, u32[]{:S(2)}) collective-permute-start(bf16[1040,256]{1,0:T(8,128)(2,1)S(1)} %get-tuple-element.50), channel_id=1, source_target_pairs={{8,4},{12,8},{9,5},{13,9},{10,6},{14,10},{11,7},{15,11},{24,20},{2... | collective-permute-start | bytes 1597448 | tf_op jit(solution)/shard_map/ppermute | solution.py:478
  561.2 34.8 %collective-permute-start.29 = (bf16[1040,256]{1,0:T(8,128)(2,1)S(1)}, bf16[1040,256]{1,0:T(8,128)(2,1)S(1)}, u32[]{:S(2)}, u32[]{:S(2)}) collective-permute-start(bf16[1040,256]{1,0:T(8,128)(2,1)S(1)} %get-tuple-element.58), channel_id=1, source_target_pairs={{0,4},{4,8},{8,12},{1,5},{5,9},{9,13},{2,6},{6,10},{10,14},{3,7},{... | collective-permute-start | bytes 1597448 | tf_op jit(solution)/shard_map/ppermute | solution.py:475
  567.1 28.9 %collective-permute-start.30 = (bf16[1040,256]{1,0:T(8,128)(2,1)S(1)}, bf16[1040,256]{1,0:T(8,128)(2,1)S(1)}, u32[]{:S(2)}, u32[]{:S(2)}) collective-permute-start(bf16[1040,256]{1,0:T(8,128)(2,1)S(1)} %get-tuple-element.59), channel_id=1, source_target_pairs={{4,0},{8,4},{12,8},{5,1},{9,5},{13,9},{6,2},{10,6},{14,10},{7,3},{... | collective-permute-start | bytes 1597448 | tf_op jit(solution)/shard_map/ppermute | solution.py:478
  573.6 24.7 %collective-permute-start.22 = (bf16[1040,256]{1,0:T(8,128)(2,1)}, bf16[1040,256]{1,0:T(8,128)(2,1)S(1)}, u32[]{:S(2)}, u32[]{:S(2)}) collective-permute-start(bf16[1040,256]{1,0:T(8,128)(2,1)} %get-tuple-element.51), channel_id=1, source_target_pairs={{0,4},{4,8},{8,12},{1,5},{5,9},{9,13},{2,6},{6,10},{10,14},{3,7},{... | collective-permute-start | bytes 1597448 | tf_op jit(solution)/shard_map/ppermute | solution.py:475
  579.5 18.8 %collective-permute-start.23 = (bf16[1040,256]{1,0:T(8,128)(2,1)}, bf16[1040,256]{1,0:T(8,128)(2,1)S(1)}, u32[]{:S(2)}, u32[]{:S(2)}) collective-permute-start(bf16[1040,256]{1,0:T(8,128)(2,1)} %get-tuple-element.52), channel_id=1, source_target_pairs={{4,0},{8,4},{12,8},{5,1},{9,5},{13,9},{6,2},{10,6},{14,10},{7,3},{... | collective-permute-start | bytes 1597448 | tf_op jit(solution)/shard_map/ppermute | solution.py:478
  580.8 3.4 copy-start.10
  584.2 1.6 copy-start.23
  585.8 10.2 %copy-start.1 = (f32[4096,256]{1,0:T(8,128)S(1)}, f32[4096,256]{1,0:T(8,128)}, u32[]{:S(2)}) copy-start(f32[4096,256]{1,0:T(8,128)} %copy-done) | copy-start | bytes 12582916
  596.0 2.3 copy-start.3
  600.5 3.4 copy-start.11
  603.9 1.6 copy-start.24
  (6 other events, 8.2 us)
Sparse Core Ops, SparseCore 0:
  9.6 196.9 all-gather.5
  208.7 126.3 all-gather.7
  337.3 50.1 all-gather.9
  436.2 45.3 all-gather.13
  483.0 65.0 all-gather.11

commit v6 on v5

--- a/solution.py
+++ b/solution.py
@@ -38,85 +38,170 @@
     return lax.dot_general(a, b, (dims, ((), ())), preferred_element_type=F32)
 
 
-def flip_kernel(me_ref, rows, out):
-    out[...] = rows[...].T
-
-
-def flip(me, rows, cols, count=1, at=0):
-    piece, width = rows.shape[0] // cols // count, rows.shape[1]
-    return pl.pallas_call(
-        flip_kernel,
+def halfway_kernel(place_ref, left, *refs, offsets, lines, first, last):
+    pieces, refs = refs[: len(offsets)], refs[len(offsets) :]
+    total = refs[-1]
+    depth = pieces[0].shape[0]
+    total[...] = jnp.zeros_like(total) if first else refs[0][...]
+    place = place_ref[0]
+    for offset, piece in zip(offsets, pieces):
+
+        @pl.when((place + offset >= 0) & (place + offset < lines))
+        def _(offset=offset, piece=piece):
+            rows = left[pl.ds(pl.multiple_of((place + offset) * depth, depth), depth), :]
+            total[...] += dot(rows, piece[...], ((0,), (0,)))
+
+    if last:
+        high, low = kernel_split(total[...])
+        refs[-2][0] = high
+        refs[-2][1] = low
+    else:
+        refs[-2][...] = total[...]
+
+
+def halfway(place, left, held, offsets, lines, before, last):
+    pieces = [held[offset] for offset in offsets]
+    depth, half = pieces[0].shape
+    inner = left.shape[1]
+    tile = min(256, inner)
+    whole = pl.BlockSpec((depth, half), lambda i, s: (0, 0))
+    block = pl.BlockSpec((tile, half), lambda i, s: (i, 0))
+    extra = [] if before is None else [before]
+    return pl.pallas_call(
+        functools.partial(
+            halfway_kernel, offsets=offsets, lines=lines, first=before is None, last=last
+        ),
+        grid_spec=pltpu.PrefetchScalarGridSpec(
+            num_scalar_prefetch=1,
+            grid=(inner // tile,),
+            in_specs=[pl.BlockSpec((left.shape[0], tile), lambda i, s: (0, i))]
+            + [whole] * len(pieces)
+            + [block] * len(extra),
+            out_specs=pl.BlockSpec((2, tile, half), lambda i, s: (0, i, 0)) if last else block,
+            scratch_shapes=[pltpu.VMEM((tile, half), F32)],
+        ),
+        out_shape=jax.ShapeDtypeStruct((2, inner, half), BF16)
+        if last
+        else jax.ShapeDtypeStruct((inner, half), F32),
+        compiler_params=params(48),
+        cost_estimate=cost(8 * depth * inner * half, 8 * depth * inner),
+        name="halfway",
+    )(place, left, *pieces, *extra)
+
+
+def flip_kernel(at_ref, rows, above, below, out, *, far):
+    me, place = at_ref[0], at_ref[1]
+    late = (me ^ pl.program_id(0)) == far - place
+
+    @pl.when(jnp.logical_not(late & ((place == 0) | (place == far))))
+    def _():
+        out[...] = rows[...].T
+
+    @pl.when(late & (place == 0))
+    def _():
+        out[...] = above[...].T
+
+    @pl.when(late & (place == far))
+    def _():
+        out[...] = below[...].T
+
+
+def flip(at, right, above, below, cols, lines, chunk, piece):
+    width = right.shape[1]
+    per = above.shape[0] // piece
+    if per * piece != width:
+        far, per = -1, 1
+    else:
+        far = lines - 1
+    last = pl.BlockSpec((piece, width), lambda d, s: (chunk if per > 1 else 0, 0))
+    return pl.pallas_call(
+        functools.partial(flip_kernel, far=far),
         grid_spec=pltpu.PrefetchScalarGridSpec(
             num_scalar_prefetch=1,
             grid=(cols,),
-            in_specs=[pl.BlockSpec((piece, width), lambda d, s: ((s[0] ^ d) * count + at, 0))],
+            in_specs=[
+                pl.BlockSpec((piece, width), lambda d, s: ((s[0] ^ d) * CHUNKS + chunk, 0)),
+                last,
+                last,
+            ],
             out_specs=pl.BlockSpec((width, piece), lambda d, s: (0, d)),
         ),
         out_shape=jax.ShapeDtypeStruct((width, cols * piece), BF16),
-        compiler_params=params(16),
+        compiler_params=params(48),
         cost_estimate=cost(0, 4 * piece * cols * width),
         name="flip",
-    )(me, rows)
-
-
-def rotate_part_kernel(me_ref, *refs, cols, sizes):
-    pieces, refs = refs[:cols], refs[cols:]
-    parts, (out, rows) = refs[: len(sizes)], refs[len(sizes) :]
+    )(at, right, above, below)
+
+
+def rotate_part_kernel(me_ref, *refs, cols, width):
+    pieces, (right, out) = refs[:cols], refs[cols:]
     tile = out.shape[0]
-
-    @pl.when(pl.program_id(0) == 0)
-    def _():
-        for distance in range(cols):
-            at = 0
-            for size, part in zip(sizes, parts):
-                start = pl.multiple_of((me_ref[0] ^ distance) * size, size)
-                rows[distance, pl.ds(at, size), :] = part[pl.ds(start, size), :]
-                at += size
-
     total = None
     for distance in range(cols):
-        both = pieces[distance][...].reshape(2 * tile, sum(sizes))
-        term = dot(both, rows[distance], ((1,), (0,)))
+        rows = right[pl.ds(pl.multiple_of((me_ref[0] ^ distance) * width, width), width), :]
+        term = dot(pieces[distance][...].reshape(2 * tile, width), rows, ((1,), (0,)))
         total = term if total is None else total + term
     out[...] = total[:tile] + total[tile:]
 
 
-def rotate_part(me, pieces, parts):
+def rotate_part(at, pieces, right):
     cols = len(pieces)
-    _, depth, _ = pieces[0].shape
-    width = parts[0].shape[1]
-    sizes = [part.shape[0] // cols for part in parts]
+    _, depth, width = pieces[0].shape
     tile = min(256, depth)
     return pl.pallas_call(
-        functools.partial(rotate_part_kernel, cols=cols, sizes=sizes),
+        functools.partial(rotate_part_kernel, cols=cols, width=width),
         grid_spec=pltpu.PrefetchScalarGridSpec(
             num_scalar_prefetch=1,
             grid=(depth // tile,),
-            in_specs=[pl.BlockSpec((2, tile, sum(sizes)), lambda i, s: (0, i, 0))] * cols
-            + [
-                pl.BlockSpec(part.shape, lambda i, s: (0, 0), pipeline_mode=pl.Buffered(1))
-                for part in parts
-            ],
+            in_specs=[pl.BlockSpec((2, tile, width), lambda i, s: (0, i, 0))] * cols
+            + [pl.BlockSpec(right.shape, lambda i, s: (0, 0), pipeline_mode=pl.Buffered(1))],
             out_specs=pl.BlockSpec((tile, width), lambda i, s: (i, 0)),
-            scratch_shapes=[pltpu.VMEM((cols, sum(sizes), width), BF16)],
         ),
         out_shape=jax.ShapeDtypeStruct((depth, width), F32),
-        compiler_params=params(44),
-        cost_estimate=cost(4 * depth * width * sum(sizes) * cols, 20 * depth * width),
+        compiler_params=params(48),
+        cost_estimate=cost(4 * depth * width * width * cols, 20 * depth * width),
         name="rotate_part",
-    )(me, *pieces, *parts)
-
-
-def rotate_kernel(me_ref, part, *refs, cols, piece):
-    pieces, (right, first, second, new_first, new_second, normed) = refs[:cols], refs[cols:]
-    tile = first.shape[0]
-    total = None
-    for distance in range(cols):
-        start = pl.multiple_of((me_ref[0] ^ distance) * piece, piece)
-        both = pieces[distance][...].reshape(2 * tile, piece)
-        term = dot(both, right[pl.ds(start, piece), :], ((1,), (0,)))
-        total = term if total is None else total + term
-    rotated = part[...] + total[:tile] + total[tile:]
+    )(at, *pieces, right)
+
+
+def rotate_kernel(at_ref, part, above, below, first, second, *refs, cols, lines):
+    pieces, (new_first, new_second, normed, held, last, arrived) = refs[:cols], refs[cols:]
+    tile, width = first.shape
+    depth = last.shape[0]
+    me, place = at_ref[0], at_ref[1]
+    step, steps = pl.program_id(0), held.shape[1] // tile
+    start = (lines - 1 - place) * depth
+    distance_now = me ^ (start // width)
+
+    def copy(distance, at):
+        rows = pl.ds(at * tile, tile)
+        if depth == width:
+            source = pieces[distance].at[:, rows, :]
+        else:
+            columns = pl.ds(pl.multiple_of(lax.rem(start, width), depth), depth)
+            source = pieces[distance].at[:, rows, columns]
+        return pltpu.make_async_copy(source, held.at[:, rows, :], arrived.at[at])
+
+    @pl.when(step == 0)
+    def _():
+        for distance in range(cols):
+
+            @pl.when(distance_now == distance)
+            def _(distance=distance):
+                for at in range(steps):
+                    copy(distance, at).start()
+
+        last[...] = jnp.where(place == 0, above[...], below[...])
+
+    for at in range(steps):
+
+        @pl.when(step == at)
+        def _(at=at):
+            copy(0, at).wait()
+
+    rows = pl.ds(pl.multiple_of(step * tile, tile), tile)
+    both = dot(held[:, rows, :].reshape(2 * tile, depth), last[...], ((1,), (0,)))
+    rotated = part[...] + both[:tile] + both[tile:]
     one = BETA_ONE * first[...] + (1.0 - BETA_ONE) * rotated
     two = BETA_TWO * second[...] + (1.0 - BETA_TWO) * rotated * rotated
     new_first[...] = one
@@ -126,37 +211,37 @@
     normed[1] = low
 
 
-def rotate(me, part, pieces, right, first, second):
+def rotate(at, part, pieces, above, below, first, second, lines):
     cols = len(pieces)
-    depth, width = first.shape
-    piece = right.shape[0] // cols
-    tile = min(256, depth)
-    final = width // piece - 1
+    rows, width = first.shape
+    depth = above.shape[0]
+    tile = min(256, rows)
     block = pl.BlockSpec((tile, width), lambda i, s: (i, 0))
     pair = pl.BlockSpec((2, tile, width), lambda i, s: (0, i, 0))
-    return pl.pallas_call(
-        functools.partial(rotate_kernel, cols=cols, piece=piece),
+    whole = pl.BlockSpec(above.shape, lambda i, s: (0, 0), pipeline_mode=pl.Buffered(1))
+    return pl.pallas_call(
+        functools.partial(rotate_kernel, cols=cols, lines=lines),
         grid_spec=pltpu.PrefetchScalarGridSpec(
             num_scalar_prefetch=1,
-            grid=(depth // tile,),
-            in_specs=[block]
-            + [pl.BlockSpec((2, tile, piece), lambda i, s: (0, i, final))] * cols
-            + [
-                pl.BlockSpec(right.shape, lambda i, s: (0, 0), pipeline_mode=pl.Buffered(1)),
-                block,
-                block,
+            grid=(rows // tile,),
+            in_specs=[block, whole, whole, block, block]
+            + [pl.BlockSpec(memory_space=pl.ANY)] * cols,
+            out_specs=[block, block, pair],
+            scratch_shapes=[
+                pltpu.VMEM((2, rows, depth), BF16),
+                pltpu.VMEM((depth, width), BF16),
+                pltpu.SemaphoreType.DMA((rows // tile,)),
             ],
-            out_specs=[block, block, pair],
         ),
         out_shape=[
-            jax.ShapeDtypeStruct((depth, width), F32),
-            jax.ShapeDtypeStruct((depth, width), F32),
-            jax.ShapeDtypeStruct((2, depth, width), BF16),
+            jax.ShapeDtypeStruct((rows, width), F32),
+            jax.ShapeDtypeStruct((rows, width), F32),
+            jax.ShapeDtypeStruct((2, rows, width), BF16),
         ],
-        compiler_params=params(44),
-        cost_estimate=cost(4 * depth * width * piece * cols, 30 * depth * width),
+        compiler_params=params(40),
+        cost_estimate=cost(4 * rows * width * depth, 30 * rows * width),
         name="rotate",
-    )(me, part, *pieces, right, first, second)
+    )(at, part, above, below, first, second, *pieces)
 
 
 def restore_kernel(normed, flipped, keep, mate, *, cols):
@@ -306,7 +391,7 @@
         out_specs=pl.BlockSpec((step, piece), lambda i: (i, 0)),
         out_shape=jax.ShapeDtypeStruct((rows, piece), F32),
         scratch_shapes=[pltpu.VMEM((depth, 2 * piece), BF16)],
-        compiler_params=params(36),
+        compiler_params=params(48),
         cost_estimate=cost(4 * rows * inner * piece, 4 * rows * piece + 2 * rows * inner),
         name="expand",
     )(keep, mate, *codes, left)
@@ -395,61 +480,6 @@
     )(at, product, *arrived, *extra)
 
 
-def update_kernel(place_ref, message, left, *refs, tile):
-    out, held = refs[-2:]
-    depth, piece = out.shape
-    inner = held.shape[0]
-    scale = scale_of(message, inner)
-
-    def unpack(i, carry):
-        rows = pl.ds(pl.multiple_of(i * tile, tile), tile)
-        high, low = kernel_split(decode(message[rows, :], scale))
-        held[rows, :piece] = high
-        held[rows, piece:] = low
-        return carry
-
-    lax.fori_loop(0, inner // tile, unpack, 0)
-    both = dot(left[...].reshape(depth, inner), held[...], ((1,), (0,)))
-    term = both[:, :piece] + both[:, piece:]
-
-    @pl.when(pl.program_id(0) == 0)
-    def _():
-        out[...] = term
-
-    @pl.when(pl.program_id(0) > 0)
-    def _():
-        out[...] += term
-
-
-def update_chunk(place, messages, left, update, chunk, depth, width):
-    cols, lines, quarter, inner = left.shape
-    piece = messages.shape[1]
-    tile = min(64, inner)
-    extra = [] if update is None else [update]
-    return pl.pallas_call(
-        functools.partial(update_kernel, tile=tile),
-        grid_spec=pltpu.PrefetchScalarGridSpec(
-            num_scalar_prefetch=1,
-            grid=(lines,),
-            in_specs=[
-                pl.BlockSpec((inner + EXTRA, piece), lambda i, s: (i, 0)),
-                pl.BlockSpec(
-                    (cols, 1, quarter, inner),
-                    lambda i, s: (0, lax.rem(s[0] + lines - i, lines), 0, 0),
-                ),
-            ]
-            + [pl.BlockSpec(memory_space=pl.ANY)] * len(extra),
-            out_specs=pl.BlockSpec((depth, piece), lambda i, s: (0, chunk)),
-            scratch_shapes=[pltpu.VMEM((inner, 2 * piece), BF16)],
-        ),
-        out_shape=jax.ShapeDtypeStruct((depth, width), F32),
-        input_output_aliases={3: 0} if extra else {},
-        compiler_params=params(40),
-        cost_estimate=cost(4 * depth * inner * piece * lines, 12 * depth * piece * lines),
-        name="update_chunk",
-    )(place, messages, left, *extra)
-
-
 def build(lines, cols):
     def swap(value, distance):
         return lax.ppermute(value, "col", [(i, i ^ distance) for i in range(cols)])
@@ -468,79 +498,94 @@
             out = lax.dynamic_update_index_in_dim(out, value, me ^ distance, 0)
         return out
 
-    def gather_row(value):
-        return lax.all_gather(value, "row", axis=0, tiled=True)
-
     def up(value, senders):
         return lax.ppermute(value, "row", [(i, i + 1) for i in senders])
 
     def down(value, senders):
         return lax.ppermute(value, "row", [(i, i - 1) for i in senders])
+
+    def walk(held, step):
+        held[-step] = up(held[1 - step], range(step - 1, lines - 1))
+        held[step] = down(held[step - 1], range(1, lines - step + 1))
 
     def local(gradient, first_moment, second_moment, left_basis, right_basis):
         me, place = lax.axis_index("col"), lax.axis_index("row")
         depth, width = gradient.shape
         piece = width // CHUNKS
-        index, spot = jnp.reshape(me, (1,)), jnp.reshape(place, (1,))
-
-        gradients = gather_row(gradient)
-        early = CHUNKS - 1
-        if depth == width:
-            near = gather_row(lax.slice_in_dim(right_basis, 0, early * piece))
-            final = gather_row(lax.slice_in_dim(right_basis, early * piece, width))
+        far = lines - 1
+        spot, at = jnp.reshape(place, (1,)), jnp.stack([me, place])
+        barrier = lax.optimization_barrier
+        near = [offset for offset in range(-far, far + 1) if abs(offset) < far]
+
+        left = place_by_distance(left_basis, me).reshape(-1, left_basis.shape[1])
+        grads = {0: gradient}
+        for step in range(1, lines):
+            if step == far:
+                left, grads[1 - step], grads[step - 1] = barrier(
+                    (left, grads[1 - step], grads[step - 1])
+                )
+            walk(grads, step)
+        before = halfway(spot, left, grads, near, lines, None, False)
+
+        own, before, grads[-far], grads[far] = barrier(
+            (right_basis, before, grads[-far], grads[far])
+        )
+        rights = {0: own}
+        right = jnp.zeros(((lines + 1) * depth, width), BF16)
+
+        def put(right, offset):
+            there = place + offset
+            there = jnp.where((there >= 0) & (there < lines), there, lines)
+            return lax.dynamic_update_slice_in_dim(right, rights[offset], there * depth, 0)
+
+        right = put(right, 0)
+        for step in range(1, lines):
+            if step == far:
+                right, rights[1 - step], rights[step - 1] = barrier(
+                    (right, rights[1 - step], rights[step - 1])
+                )
+            walk(rights, step)
+            if step < far or depth != width:
+                right = put(put(right, -step), step)
+        above, below = rights[far], rights[-far]
+
+        whole = halfway(spot, left, grads, [-far, far], lines, before, True)
+        pieces = by_distance(whole)
+        pieces = [pieces[distance] for distance in range(cols)]
+        part = rotate_part(at, pieces, right)
+        part, above, below = barrier((part, above, below))
+        if depth != width:
+            above_now, below_now = jnp.zeros_like(above), jnp.zeros_like(below)
         else:
-            blocks = gather_row(right_basis).reshape(cols, CHUNKS, piece, width)
-            near = blocks[:, :early].reshape(early * cols * piece, width)
-            final = blocks[:, early].reshape(cols * piece, width)
-
-        left = place_by_distance(left_basis, me).reshape(-1, left_basis.shape[1])
-        quarter = depth // cols
-        backs = []
-        for back in range(lines):
-            to = lax.rem(place + back, lines)
-            rows = lax.dynamic_slice_in_dim(left, to * depth + me * quarter, quarter, 0)
-            if back:
-                rows = lax.ppermute(rows, "row", [(i, (i + back) % lines) for i in range(lines)])
-            backs.append(rows)
-        left_rows = place_by_distance(jnp.stack(backs), me)
-        left, left_rows = lax.optimization_barrier((left, left_rows))
-
-        halfway = dot(left, gradients, ((0,), (0,)))
-        pieces = by_distance(jnp.stack(split(halfway)))
-        pieces = [pieces[distance] for distance in range(cols)]
-
-        flipped = [flip(index, near, cols, early, at) for at in range(early)]
-        flipped.append(flip(index, final, cols))
-        part = rotate_part(index, pieces, [near])
+            above_now, below_now = above, below
         new_first, new_second, normed = rotate(
-            index, part, pieces, final, first_moment, second_moment
+            at, part, pieces, above_now, below_now, first_moment, second_moment, lines
         )
 
         halves, coded = [], []
         for chunk in range(CHUNKS):
             if chunk >= 2:
-                normed, coded[chunk - 2] = lax.optimization_barrier((normed, coded[chunk - 2]))
-            keep, mate = restore(normed, flipped[chunk], cols)
+                normed, coded[chunk - 2] = barrier((normed, coded[chunk - 2]))
+            flipped = flip(at, right, above, below, cols, lines, chunk, piece)
+            keep, mate = restore(normed, flipped, cols)
             mate = swap(mate, 1)
             halves.append((keep, mate))
             coded.append([send(keep, mate, distance, []) for distance in range(2, cols, 2)])
         crossed = [
-            [swap(code, 2 * at + 2) for at, code in enumerate(codes)] for codes in coded
+            [swap(code, 2 * index + 2) for index, code in enumerate(codes)] for codes in coded
         ]
-        gathered = [gather_row(send(*halves[c], 0, crossed[c])) for c in (0, 3)]
-        products = [expand(*halves[c], crossed[c], left) for c in (1, 2)]
-        arrived = [(), ()]
+        products = [expand(*halves[c], crossed[c], left) for c in range(CHUNKS)]
+        arrived = [()] * CHUNKS
         for step in range(1, lines):
-            for at, product in enumerate(products):
-                upward, downward = hop(spot, product, arrived[at], lines, step)
-                arrived[at] = (
+            for chunk, product in enumerate(products):
+                upward, downward = hop(spot, product, arrived[chunk], lines, step)
+                arrived[chunk] = (
                     up(upward, range(0, step)),
                     down(downward, range(lines - step, lines)),
                 )
-        update = update_chunk(spot, gathered[0], left_rows, None, 0, depth, width)
-        for at, product in enumerate(products):
-            update = finish(spot, product, arrived[at], update, at + 1, depth, width)
-        update = update_chunk(spot, gathered[1], left_rows, update, 3, depth, width)
+        update = None
+        for chunk, product in enumerate(products):
+            update = finish(spot, product, arrived[chunk], update, chunk, depth, width)
         return (new_first, new_second, update)
 
     return local

time: 624 us -> 576 us (0.923)
  waiting for transfers between devices: 375 us -> 258 us
  Pallas kernels: 116 us -> 176 us
  starting transfers between devices: 47.6 us -> 84.7 us
  matrix products: 13.7 us -> 0 us
  between operations: 14.4 us -> 1.39 us
    ppermute x17 -> x14, waiting for transfers between devices: 218 us -> 92.9 us  [swap(): return lax.ppermute(value, 'col', [(i, i ^ distance) for i in range(cols)])]
    ppermute x6 -> x18, waiting for transfers between devices: 0.02 us -> 96.6 us  [down(): return lax.ppermute(value, 'row', [(i, i - 1) for i in senders])]
    ppermute x3 -> x0, waiting for transfers between devices: 64.3 us -> none  [local(): lax.ppermute(rows, 'row', [(i, (i + back) % lines) for i in range(lines)])]
    all_gather x5 -> x0, waiting for transfers between devices: 59.6 us -> none  [gather_row(): return lax.all_gather(value, 'row', axis=0, tiled=True)]
    ppermute x6 -> x18, waiting for transfers between devices: 33 us -> 68.7 us  [up(): return lax.ppermute(value, 'row', [(i, i + 1) for i in senders])]
    ppermute x6 -> x18, starting transfers between devices: 23.5 us -> 57.3 us  [up(): return lax.ppermute(value, 'row', [(i, i + 1) for i in senders])]
    pallas_call x2 -> x4, Pallas kernels: 14.2 us -> 38.4 us  [expand(): pl.pallas_call(functools.partial(expand_kernel, tile=min(64, depth)), gri...]
    pallas_call x8, Pallas kernels: 54.7 us -> 76.1 us  [the longest x2 24.5 us: halfway(): pl.pallas_call(functools.partial(halfway_kernel, offsets=offsets, lines=l...]
  transfers between devices with their start and end apart: 37 -> 50, of which waited for: 17 -> 17; matrix products, arithmetic and copies ran while one was open for 5% -> 5% of each run, Pallas kernels for 12% -> 23%
where the time goes in v6:
time: 576 us; the launch traced here: 568 us
  waiting for transfers between devices  258 us (45%)
  Pallas kernels  176 us (31%)
  starting transfers between devices  84.7 us (15%)
  local copies, waits for them, and re-layouts  48.4 us (8%)
    ppermute x18, waiting for transfers between devices, down(): return lax.ppermute(value, 'row', [(i, i - 1) for i in senders])  96.6 us
    ppermute x14, waiting for transfers between devices, swap(): return lax.ppermute(value, 'col', [(i, i ^ distance) for i in range(cols)])  92.9 us
    ppermute x18, waiting for transfers between devices, up(): return lax.ppermute(value, 'row', [(i, i + 1) for i in senders])  68.7 us
    ppermute x18, starting transfers between devices, up(): return lax.ppermute(value, 'row', [(i, i + 1) for i in senders])  57.3 us
    pallas_call x4, Pallas kernels, expand(): pl.pallas_call(functools.partial(expand_kernel, tile=min(64, depth)), gri...  38.4 us
    pallas_call x4, Pallas kernels, restore(): pl.pallas_call(functools.partial(restore_kernel, cols=cols), grid=(depth...  25.1 us
    pallas_call x2, Pallas kernels, halfway(): pl.pallas_call(functools.partial(halfway_kernel, offsets=offsets, lines=l...  24.5 us
    pallas_call x1, Pallas kernels, rotate_part(): pl.pallas_call(functools.partial(rotate_part_kernel, cols=cols, width=wid...  23.9 us
  transfers between devices with their start and end apart: 50, of which 17 were waited for; matrix products, arithmetic and copies ran while one was open for 5% of the time, Pallas kernels for 23%

profile of v6, /device:TPU:0, one launch (start us, length us, event | category | flops | bytes accessed | tf_op | source)
XLA Modules:
  0.0 568.3 jit_solution(2779888490825950689)
XLA Ops:
  0.6 3.0 collective-permute-start
  3.6 3.6 collective-permute-start.3
  8.6 41.0 %collective-permute-done = bf16[1024,1024]{1,0:T(8,128)(2,1)} collective-permute-done((bf16[1024,1024]{1,0:T(8,128)(2,1)}, bf16[1024,1024]{1,0:T(8,128)(2,1)}, u32[]{:S(2)}, u32[]{:S(2)}) %collective-permute-start) | collective-permute-done | bytes 2097184 | tf_op jit(solution)/shard_map/ppermute | solution.py:485
  49.6 2.4 collective-permute-done.3.refs_1_
  52.0 2.0 collective-permute-start.4
  54.0 2.2 collective-permute-done.5.refs_3_
  65.1 3.3 copy-done.17
  68.4 37.3 %collective-permute-done.6.refs_4_ = bf16[1024,1024]{1,0:T(8,128)(2,1)} collective-permute-done((bf16[1024,1024]{1,0:T(8,128)(2,1)}, bf16[1024,1024]{1,0:T(8,128)(2,1)}, u32[]{:S(2)}, u32[]{:S(2)}) %collective-permute-start.6) | collective-permute-done | bytes 2097184 | tf_op jit(solution)/shard_map/ppermute | solution.py:505
  105.7 2.1 collective-permute-start.7
  109.1 14.7 %halfway.2.refs_2_ = f32[1024,1024]{1,0:T(8,128)} custom-call(s32[1]{0:T(128)} %bitcast.1.place_ref.at_ref, bf16[4096,1024]{1,0:T(8,128)(2,1)} %bitcast.11, bf16[1024,1024]{1,0:T(8,128)(2,1)} %collective-permute-done.4.refs_0_, bf16[1024,1024]{1,0:T(8,128)(2,1)S(1)} %collective-permute-done.3.refs_1_, bf16[1024,1024]{1,0:T(8,128)(2,1)} %refs_2_.1, ...), custom_call_target="tpu_custom_call" | custom-call | flops 85899344 | bytes 83886 | tf_op jit(solution)/shard_map/halfway/pallas_call | solution.py:70
  123.7 31.6 %collective-permute-done.8.refs_1_ = bf16[1024,1024]{1,0:T(8,128)(2,1)} collective-permute-done((bf16[1024,1024]{1,0:T(8,128)(2,1)}, bf16[1024,1024]{1,0:T(8,128)(2,1)}, u32[]{:S(2)}, u32[]{:S(2)}) %collective-permute-start.8) | collective-permute-done | bytes 2097184 | tf_op jit(solution)/shard_map/ppermute | solution.py:505
  155.3 9.8 %halfway.3.refs_0_ = bf16[2,1024,1024]{2,1,0:T(8,128)(2,1)} custom-call(s32[1]{0:T(128)} %bitcast.1.place_ref.at_ref, bf16[4096,1024]{1,0:T(8,128)(2,1)} %bitcast.12, bf16[1024,1024]{1,0:T(8,128)(2,1)} %collective-permute-done.7.refs_0_, bf16[1024,1024]{1,0:T(8,128)(2,1)} %collective-permute-done.8.refs_1_, f32[1024,1024]{1,0:T(8,128)} %halfway.2.refs_2_), custom_call_target="tpu_custom_call" | custom-call | flops 85899344 | bytes 83886 | tf_op jit(solution)/shard_map/halfway/pallas_call | solution.py:70
  165.6 2.6 collective-permute-start.12
  169.5 39.3 %collective-permute-done.12 = bf16[1024,1024]{1,0:T(8,128)(2,1)} collective-permute-done((bf16[1024,1024]{1,0:T(8,128)(2,1)S(1)}, bf16[1024,1024]{1,0:T(8,128)(2,1)}, u32[]{:S(2)}, u32[]{:S(2)}) %collective-permute-start.12) | collective-permute-done | bytes 2097184 | tf_op jit(solution)/shard_map/ppermute | solution.py:502
  208.9 2.0 collective-permute-start.14
  210.8 3.5 collective-permute-done.13
  215.8 39.0 %collective-permute-done.10.refs_2_ = bf16[2,1024,1024]{2,1,0:T(8,128)(2,1)} collective-permute-done((bf16[2,1024,1024]{2,1,0:T(8,128)(2,1)}, bf16[2,1024,1024]{2,1,0:T(8,128)(2,1)}, u32[]{:S(2)}, u32[]{:S(2)}) %collective-permute-start.10) | collective-permute-done | bytes 4194336 | tf_op jit(solution)/shard_map/ppermute | solution.py:485
  254.8 5.3 broadcast_in_dim.24
  261.6 3.1 constant_dynamic-update-slice_fusion.3
  264.7 3.1 constant_dynamic-update-slice_fusion.2
  267.8 3.1 constant_dynamic-update-slice_fusion.1
  270.9 3.1 constant_dynamic-update-slice_fusion.refs_4_.rows
  276.3 23.9 %rotate_part.1.part = f32[1024,1024]{1,0:T(8,128)S(1)} custom-call(s32[2]{0:T(128)S(1)} %pad_add_fusion.me_ref.at_ref, bf16[2,1024,1024]{2,1,0:T(8,128)(2,1)} %halfway.3.refs_0_, bf16[2,1024,1024]{2,1,0:T(8,128)(2,1)} %collective-permute-done.9.refs_1_, bf16[2,1024,1024]{2,1,0:T(8,128)(2,1)} %collective-permute-done.10.refs_2_, ...), custom_call_target="tpu_custom_call" | custom-call | flops 171798688 | bytes 209715 | tf_op jit(solution)/shard_map/rotate_part/pallas_call | solution.py:151
  300.2 2.0 copy-done.9
  302.2 21.9 %collective-permute-done.16.above = bf16[1024,1024]{1,0:T(8,128)(2,1)S(1)} collective-permute-done((bf16[1024,1024]{1,0:T(8,128)(2,1)}, bf16[1024,1024]{1,0:T(8,128)(2,1)S(1)}, u32[]{:S(2)}, u32[]{:S(2)}) %collective-permute-start.16) | collective-permute-done | bytes 2097184 | tf_op jit(solution)/shard_map/ppermute | solution.py:505
  325.4 3.7 flip.4.flipped
  330.7 2.2 copy-done.10
  332.9 12.9 %rotate.1 = (f32[1024,1024]{1,0:T(8,128)}, f32[1024,1024]{1,0:T(8,128)}, bf16[2,1024,1024]{2,1,0:T(8,128)(2,1)S(1)}) custom-call(s32[2]{0:T(128)S(1)} %pad_add_fusion.me_ref.at_ref, f32[1024,1024]{1,0:T(8,128)S(1)} %copy-done.10, bf16[1024,1024]{1,0:T(8,128)(2,1)S(1)} %collective-permute-done.16.above, bf16[1024,1024]{1,0:T(8,128)(2,1)S(1)} %copy-done.8, ...), custom_call_target="tpu_custom_call" | custom-call | flops 42949672 | bytes 314572 | tf_op jit(solution)/shard_map/rotate/pallas_call | solution.py:222
  345.8 6.3 %restore.4 = (f32[2,1024,256]{2,1,0:T(8,128)S(1)}, f32[2,1024,256]{2,1,0:T(8,128)}) custom-call(bf16[2,1024,1024]{2,1,0:T(8,128)(2,1)S(1)} %get-tuple-element.76.normed, bf16[1024,1024]{1,0:T(8,128)(2,1)S(1)} %flip.4.flipped), custom_call_target="tpu_custom_call" | custom-call | flops 42949672 | bytes 83886 | tf_op jit(solution)/shard_map/restore/pallas_call | solution.py:262
  352.1 3.8 flip.5.flipped
  355.9 6.3 %restore.5 = (f32[2,1024,256]{2,1,0:T(8,128)S(1)}, f32[2,1024,256]{2,1,0:T(8,128)}) custom-call(bf16[2,1024,1024]{2,1,0:T(8,128)(2,1)S(1)} %get-tuple-element.76.normed, bf16[1024,1024]{1,0:T(8,128)(2,1)S(1)} %flip.5.flipped), custom_call_target="tpu_custom_call" | custom-call | flops 42949672 | bytes 83886 | tf_op jit(solution)/shard_map/restore/pallas_call | solution.py:262
  362.6 3.7 flip.7.flipped
  366.2 3.7 flip.6.flipped
  370.0 2.0 send.4
  372.0 6.3 %restore.7 = (f32[2,1024,256]{2,1,0:T(8,128)S(1)}, f32[2,1024,256]{2,1,0:T(8,128)}) custom-call(bf16[2,1024,1024]{2,1,0:T(8,128)(2,1)S(1)} %get-tuple-element.76.normed, bf16[1024,1024]{1,0:T(8,128)(2,1)S(1)} %flip.7.flipped), custom_call_target="tpu_custom_call" | custom-call | flops 42949672 | bytes 83886 | tf_op jit(solution)/shard_map/restore/pallas_call | solution.py:262
  378.4 2.9 send.5
  381.3 6.3 %restore.6 = (f32[2,1024,256]{2,1,0:T(8,128)S(1)}, f32[2,1024,256]{2,1,0:T(8,128)}) custom-call(bf16[2,1024,1024]{2,1,0:T(8,128)(2,1)S(1)} %get-tuple-element.76.normed, bf16[1024,1024]{1,0:T(8,128)(2,1)S(1)} %flip.6.flipped), custom_call_target="tpu_custom_call" | custom-call | flops 42949672 | bytes 83886 | tf_op jit(solution)/shard_map/restore/pallas_call | solution.py:262
  389.9 12.9 %collective-permute-done.43.refs_0_ = bf16[1040,256]{1,0:T(8,128)(2,1)S(1)} collective-permute-done((bf16[1040,256]{1,0:T(8,128)(2,1)S(1)}, bf16[1040,256]{1,0:T(8,128)(2,1)S(1)}, u32[]{:S(2)}, u32[]{:S(2)}) %collective-permute-start.43) | collective-permute-done | bytes 532512 | tf_op jit(solution)/shard_map/ppermute | solution.py:485
  404.4 9.6 %expand.7.refs_0_.refs_1_.block = f32[4096,256]{1,0:T(8,128)} custom-call(f32[2,1024,256]{2,1,0:T(8,128)S(1)} %copy-done.14, f32[2,1024,256]{2,1,0:T(8,128)} %collective-permute-done.18.mate, bf16[1040,256]{1,0:T(8,128)(2,1)S(1)} %collective-permute-done.43.refs_0_, bf16[4096,1024]{1,0:T(8,128)(2,1)} %bitcast.13), custom_call_target="tpu_custom_call" | custom-call | flops 42949672 | bytes 125829 | tf_op jit(solution)/shard_map/expand/pallas_call | solution.py:385
  414.0 2.2 copy-done
  420.0 3.0 send.7
  426.8 9.6 %expand.6.refs_0_.refs_1_.block = f32[4096,256]{1,0:T(8,128)} custom-call(f32[2,1024,256]{2,1,0:T(8,128)S(1)} %copy-done.12, f32[2,1024,256]{2,1,0:T(8,128)} %collective-permute-done.19.mate, bf16[1040,256]{1,0:T(8,128)(2,1)S(1)} %collective-permute-done.36.refs_0_, bf16[4096,1024]{1,0:T(8,128)(2,1)} %bitcast.14), custom_call_target="tpu_custom_call" | custom-call | flops 42949672 | bytes 125829 | tf_op jit(solution)/shard_map/expand/pallas_call | solution.py:385
  436.4 2.2 copy-done.2
  442.4 2.3 hop.22
  446.8 9.8 %expand.5.refs_0_.refs_1_.block = f32[4096,256]{1,0:T(8,128)} custom-call(f32[2,1024,256]{2,1,0:T(8,128)S(1)} %get-tuple-element.85.keep, f32[2,1024,256]{2,1,0:T(8,128)} %collective-permute-done.28.mate, bf16[1040,256]{1,0:T(8,128)(2,1)} %collective-permute-done.29.refs_0_, bf16[4096,1024]{1,0:T(8,128)(2,1)} %bitcast.15), custom_call_target="tpu_custom_call" | custom-call | flops 42949672 | bytes 125829 | tf_op jit(solution)/shard_map/expand/pallas_call | solution.py:385
  456.6 2.2 copy-done.4
  461.6 9.4 %expand.4.refs_0_.refs_1_.block = f32[4096,256]{1,0:T(8,128)} custom-call(f32[2,1024,256]{2,1,0:T(8,128)S(1)} %get-tuple-element.77.keep, f32[2,1024,256]{2,1,0:T(8,128)S(1)} %collective-permute-done.20.mate, bf16[1040,256]{1,0:T(8,128)(2,1)} %collective-permute-done.21.refs_0_, bf16[4096,1024]{1,0:T(8,128)(2,1)} %bitcast.16), custom_call_target="tpu_custom_call" | custom-call | flops 42949672 | bytes 125829 | tf_op jit(solution)/shard_map/expand/pallas_call | solution.py:385
  471.0 2.2 copy-done.6
  482.3 8.2 %collective-permute-start.32 = (bf16[1040,256]{1,0:T(8,128)(2,1)S(1)}, bf16[1040,256]{1,0:T(8,128)(2,1)S(1)}, u32[]{:S(2)}, u32[]{:S(2)}) collective-permute-start(bf16[1040,256]{1,0:T(8,128)(2,1)S(1)} %get-tuple-element.89), channel_id=1, source_target_pairs={{0,4},{4,8},{1,5},{5,9},{2,6},{6,10},{3,7},{7,11},{16,20},{20,24},... | collective-permute-start | bytes 1597448 | tf_op jit(solution)/shard_map/ppermute | solution.py:502
  494.1 4.9 collective-permute-start.24
  501.0 5.0 collective-permute-start.48
  507.5 4.2 collective-permute-done.32.refs_2_
  513.0 6.0 %collective-permute-start.41 = (bf16[1040,256]{1,0:T(8,128)(2,1)S(1)}, bf16[1040,256]{1,0:T(8,128)(2,1)S(1)}, u32[]{:S(2)}, u32[]{:S(2)}) collective-permute-start(bf16[1040,256]{1,0:T(8,128)(2,1)S(1)} %get-tuple-element.98), channel_id=1, source_target_pairs={{0,4},{4,8},{8,12},{1,5},{5,9},{9,13},{2,6},{6,10},{10,14},{3,7},{... | collective-permute-start | bytes 1597448 | tf_op jit(solution)/shard_map/ppermute | solution.py:502
  520.5 2.6 collective-permute-done.24.refs_2_
  524.5 6.0 %collective-permute-start.34 = (bf16[1040,256]{1,0:T(8,128)(2,1)S(1)}, bf16[1040,256]{1,0:T(8,128)(2,1)S(1)}, u32[]{:S(2)}, u32[]{:S(2)}) collective-permute-start(bf16[1040,256]{1,0:T(8,128)(2,1)S(1)} %get-tuple-element.91), channel_id=1, source_target_pairs={{0,4},{4,8},{8,12},{1,5},{5,9},{9,13},{2,6},{6,10},{10,14},{3,7},{... | collective-permute-start | bytes 1597448 | tf_op jit(solution)/shard_map/ppermute | solution.py:502
  532.0 2.6 collective-permute-done.48.up
  535.9 6.0 %collective-permute-start.26 = (bf16[1040,256]{1,0:T(8,128)(2,1)S(1)}, bf16[1040,256]{1,0:T(8,128)(2,1)S(1)}, u32[]{:S(2)}, u32[]{:S(2)}) collective-permute-start(bf16[1040,256]{1,0:T(8,128)(2,1)S(1)} %get-tuple-element.83), channel_id=1, source_target_pairs={{0,4},{4,8},{8,12},{1,5},{5,9},{9,13},{2,6},{6,10},{10,14},{3,7},{... | collective-permute-start | bytes 1597448 | tf_op jit(solution)/shard_map/ppermute | solution.py:502
  541.9 4.1 collective-permute-done.41.up
  547.3 2.2 finish.4.refs_0_
  549.5 2.2 finish.5.refs_0_
  551.8 5.6 collective-permute-done.34.up
  557.4 2.2 finish.6.refs_0_
  559.6 6.4 %collective-permute-done.26.up = bf16[1040,256]{1,0:T(8,128)(2,1)S(1)} collective-permute-done((bf16[1040,256]{1,0:T(8,128)(2,1)S(1)}, bf16[1040,256]{1,0:T(8,128)(2,1)S(1)}, u32[]{:S(2)}, u32[]{:S(2)}) %collective-permute-start.26) | collective-permute-done | bytes 532512 | tf_op jit(solution)/shard_map/ppermute | solution.py:502
  566.1 2.2 finish.7
  (124 shorter events, 66.1 us)
Async XLA Ops:
  0.6 49.0 %collective-permute-start = (bf16[1024,1024]{1,0:T(8,128)(2,1)}, bf16[1024,1024]{1,0:T(8,128)(2,1)}, u32[]{:S(2)}, u32[]{:S(2)}) collective-permute-start(bf16[1024,1024]{1,0:T(8,128)(2,1)} %param.8), channel_id=1, source_target_pairs={{0,2},{1,3},{2,0},{3,1},{4,6},{5,7},{6,4},{7,5},{8,10},{9,11},{10,... | collective-permute-start | bytes 6291464 | tf_op jit(solution)/shard_map/ppermute | solution.py:485
  3.6 48.4 %collective-permute-start.3 = (bf16[1024,1024]{1,0:T(8,128)(2,1)}, bf16[1024,1024]{1,0:T(8,128)(2,1)S(1)}, u32[]{:S(2)}, u32[]{:S(2)}) collective-permute-start(bf16[1024,1024]{1,0:T(8,128)(2,1)} %refs_2_.1), channel_id=1, source_target_pairs={{0,4},{4,8},{8,12},{1,5},{5,9},{9,13},{2,6},{6,10},{10,14},{3,7},{... | collective-permute-start | bytes 6291464 | tf_op jit(solution)/shard_map/ppermute | solution.py:502
  7.2 49.0 %collective-permute-start.5 = (bf16[1024,1024]{1,0:T(8,128)(2,1)}, bf16[1024,1024]{1,0:T(8,128)(2,1)}, u32[]{:S(2)}, u32[]{:S(2)}) collective-permute-start(bf16[1024,1024]{1,0:T(8,128)(2,1)} %refs_2_.1), channel_id=1, source_target_pairs={{4,0},{8,4},{12,8},{5,1},{9,5},{13,9},{6,2},{10,6},{14,10},{7,3},{... | collective-permute-start | bytes 6291464 | tf_op jit(solution)/shard_map/ppermute | solution.py:505
  8.5 52.8 %collective-permute-start.1 = (bf16[1024,1024]{1,0:T(8,128)(2,1)}, bf16[1024,1024]{1,0:T(8,128)(2,1)}, u32[]{:S(2)}, u32[]{:S(2)}) collective-permute-start(bf16[1024,1024]{1,0:T(8,128)(2,1)} %param.8), channel_id=1, source_target_pairs={{0,1},{1,0},{2,3},{3,2},{4,5},{5,4},{6,7},{7,6},{8,9},{9,8},{10,11... | collective-permute-start | bytes 6291464 | tf_op jit(solution)/shard_map/ppermute | solution.py:485
  49.6 13.6 %collective-permute-start.2 = (bf16[1024,1024]{1,0:T(8,128)(2,1)}, bf16[1024,1024]{1,0:T(8,128)(2,1)}, u32[]{:S(2)}, u32[]{:S(2)}) collective-permute-start(bf16[1024,1024]{1,0:T(8,128)(2,1)} %collective-permute-done), channel_id=1, source_target_pairs={{0,1},{1,0},{2,3},{3,2},{4,5},{5,4},{6,7},{7,6},{8,9},{9,8},{10,11... | collective-permute-start | bytes 6291464 | tf_op jit(solution)/shard_map/ppermute | solution.py:485
  52.0 13.1 %collective-permute-start.4 = (bf16[1024,1024]{1,0:T(8,128)(2,1)S(1)}, bf16[1024,1024]{1,0:T(8,128)(2,1)}, u32[]{:S(2)}, u32[]{:S(2)}) collective-permute-start(bf16[1024,1024]{1,0:T(8,128)(2,1)S(1)} %collective-permute-done.3.refs_1_), channel_id=1, source_target_pairs={{4,8},{8,12},{5,9},{9,13},{6,10},{10,14},{7,11},{11,15},{20,24},{2... | collective-permute-start | bytes 6291464 | tf_op jit(solution)/shard_map/ppermute | solution.py:502
  56.3 49.4 %collective-permute-start.6 = (bf16[1024,1024]{1,0:T(8,128)(2,1)}, bf16[1024,1024]{1,0:T(8,128)(2,1)}, u32[]{:S(2)}, u32[]{:S(2)}) collective-permute-start(bf16[1024,1024]{1,0:T(8,128)(2,1)} %collective-permute-done.5.refs_3_), channel_id=1, source_target_pairs={{4,0},{8,4},{5,1},{9,5},{6,2},{10,6},{7,3},{11,7},{20,16},{24,20},... | collective-permute-start | bytes 6291464 | tf_op jit(solution)/shard_map/ppermute | solution.py:505
  65.1 3.3 copy-start.17
  105.7 18.0 %collective-permute-start.7 = (bf16[1024,1024]{1,0:T(8,128)(2,1)}, bf16[1024,1024]{1,0:T(8,128)(2,1)}, u32[]{:S(2)}, u32[]{:S(2)}) collective-permute-start(bf16[1024,1024]{1,0:T(8,128)(2,1)} %collective-permute-done.4.refs_0_), channel_id=1, source_target_pairs={{8,12},{9,13},{10,14},{11,15},{24,28},{25,29},{26,30},{27,31}} | collective-permute-start | bytes 6291464 | tf_op jit(solution)/shard_map/ppermute | solution.py:502
  107.8 47.6 %collective-permute-start.8 = (bf16[1024,1024]{1,0:T(8,128)(2,1)}, bf16[1024,1024]{1,0:T(8,128)(2,1)}, u32[]{:S(2)}, u32[]{:S(2)}) collective-permute-start(bf16[1024,1024]{1,0:T(8,128)(2,1)} %collective-permute-done.6.refs_4_), channel_id=1, source_target_pairs={{4,0},{5,1},{6,2},{7,3},{20,16},{21,17},{22,18},{23,19}} | collective-permute-start | bytes 6291464 | tf_op jit(solution)/shard_map/ppermute | solution.py:505
  123.7 41.9 %copy-start.19 = (bf16[1024,1024]{1,0:T(8,128)(2,1)S(1)}, bf16[1024,1024]{1,0:T(8,128)(2,1)}, u32[]{:S(2)}) copy-start(bf16[1024,1024]{1,0:T(8,128)(2,1)} %param.9) | copy-start | bytes 6291460
  165.1 89.7 %collective-permute-start.10 = (bf16[2,1024,1024]{2,1,0:T(8,128)(2,1)}, bf16[2,1024,1024]{2,1,0:T(8,128)(2,1)}, u32[]{:S(2)}, u32[]{:S(2)}) collective-permute-start(bf16[2,1024,1024]{2,1,0:T(8,128)(2,1)} %halfway.3.refs_0_), channel_id=1, source_target_pairs={{0,2},{1,3},{2,0},{3,1},{4,6},{5,7},{6,4},{7,5},{8,10},{9,11},{10,... | collective-permute-start | bytes 12582920 | tf_op jit(solution)/shard_map/ppermute | solution.py:485
  165.6 43.2 %collective-permute-start.12 = (bf16[1024,1024]{1,0:T(8,128)(2,1)S(1)}, bf16[1024,1024]{1,0:T(8,128)(2,1)}, u32[]{:S(2)}, u32[]{:S(2)}) collective-permute-start(bf16[1024,1024]{1,0:T(8,128)(2,1)S(1)} %copy-done.19), channel_id=1, source_target_pairs={{0,4},{4,8},{8,12},{1,5},{5,9},{9,13},{2,6},{6,10},{10,14},{3,7},{... | collective-permute-start | bytes 6291464 | tf_op jit(solution)/shard_map/ppermute | solution.py:502
  168.2 46.1 %collective-permute-start.13 = (bf16[1024,1024]{1,0:T(8,128)(2,1)S(1)}, bf16[1024,1024]{1,0:T(8,128)(2,1)}, u32[]{:S(2)}, u32[]{:S(2)}) collective-permute-start(bf16[1024,1024]{1,0:T(8,128)(2,1)S(1)} %copy-done.19), channel_id=1, source_target_pairs={{4,0},{8,4},{12,8},{5,1},{9,5},{13,9},{6,2},{10,6},{14,10},{7,3},{... | collective-permute-start | bytes 6291464 | tf_op jit(solution)/shard_map/ppermute | solution.py:505
  208.9 58.9 %collective-permute-start.14 = (bf16[1024,1024]{1,0:T(8,128)(2,1)}, bf16[1024,1024]{1,0:T(8,128)(2,1)}, u32[]{:S(2)}, u32[]{:S(2)}) collective-permute-start(bf16[1024,1024]{1,0:T(8,128)(2,1)} %collective-permute-done.12), channel_id=1, source_target_pairs={{4,8},{8,12},{5,9},{9,13},{6,10},{10,14},{7,11},{11,15},{20,24},{2... | collective-permute-start | bytes 6291464 | tf_op jit(solution)/shard_map/ppermute | solution.py:502
  214.4 56.5 %collective-permute-start.15 = (bf16[1024,1024]{1,0:T(8,128)(2,1)}, bf16[1024,1024]{1,0:T(8,128)(2,1)}, u32[]{:S(2)}, u32[]{:S(2)}) collective-permute-start(bf16[1024,1024]{1,0:T(8,128)(2,1)} %collective-permute-done.13), channel_id=1, source_target_pairs={{4,0},{8,4},{5,1},{9,5},{6,2},{10,6},{7,3},{11,7},{20,16},{24,20},... | collective-permute-start | bytes 6291464 | tf_op jit(solution)/shard_map/ppermute | solution.py:505
  215.7 60.6 %collective-permute-start.9 = (bf16[2,1024,1024]{2,1,0:T(8,128)(2,1)}, bf16[2,1024,1024]{2,1,0:T(8,128)(2,1)}, u32[]{:S(2)}, u32[]{:S(2)}) collective-permute-start(bf16[2,1024,1024]{2,1,0:T(8,128)(2,1)} %halfway.3.refs_0_), channel_id=1, source_target_pairs={{0,1},{1,0},{2,3},{3,2},{4,5},{5,4},{6,7},{7,6},{8,9},{9,8},{10,11... | collective-permute-start | bytes 12582920 | tf_op jit(solution)/shard_map/ppermute | solution.py:485
  254.8 21.5 %collective-permute-start.11 = (bf16[2,1024,1024]{2,1,0:T(8,128)(2,1)}, bf16[2,1024,1024]{2,1,0:T(8,128)(2,1)}, u32[]{:S(2)}, u32[]{:S(2)}) collective-permute-start(bf16[2,1024,1024]{2,1,0:T(8,128)(2,1)} %collective-permute-done.10.refs_2_), channel_id=1, source_target_pairs={{0,1},{1,0},{2,3},{3,2},{4,5},{5,4},{6,7},{7,6},{8,9},{9,8},{10,11... | collective-permute-start | bytes 12582920 | tf_op jit(solution)/shard_map/ppermute | solution.py:485
  274.0 50.1 %collective-permute-start.16 = (bf16[1024,1024]{1,0:T(8,128)(2,1)}, bf16[1024,1024]{1,0:T(8,128)(2,1)S(1)}, u32[]{:S(2)}, u32[]{:S(2)}) collective-permute-start(bf16[1024,1024]{1,0:T(8,128)(2,1)} %collective-permute-done.15), channel_id=1, source_target_pairs={{4,0},{5,1},{6,2},{7,3},{20,16},{21,17},{22,18},{23,19}} | collective-permute-start | bytes 6291464 | tf_op jit(solution)/shard_map/ppermute | solution.py:505
  275.3 48.8 %collective-permute-start.17 = (bf16[1024,1024]{1,0:T(8,128)(2,1)}, bf16[1024,1024]{1,0:T(8,128)(2,1)S(1)}, u32[]{:S(2)}, u32[]{:S(2)}) collective-permute-start(bf16[1024,1024]{1,0:T(8,128)(2,1)} %collective-permute-done.14), channel_id=1, source_target_pairs={{8,12},{9,13},{10,14},{11,15},{24,28},{25,29},{26,30},{27,31}} | collective-permute-start | bytes 6291464 | tf_op jit(solution)/shard_map/ppermute | solution.py:502
  300.2 2.0 copy-start.9
  330.7 2.2 copy-start.10
  352.1 17.9 %copy-start.13 = (f32[2,1024,256]{2,1,0:T(8,128)}, f32[2,1024,256]{2,1,0:T(8,128)S(1)}, u32[]{:S(2)}) copy-start(f32[2,1024,256]{2,1,0:T(8,128)S(1)} %get-tuple-element.71.keep) | copy-start | bytes 6291460
  352.1 17.9 %collective-permute-start.18 = (f32[2,1024,256]{2,1,0:T(8,128)}, f32[2,1024,256]{2,1,0:T(8,128)}, u32[]{:S(2)}, u32[]{:S(2)}) collective-permute-start(f32[2,1024,256]{2,1,0:T(8,128)} %get-tuple-element.72), channel_id=1, source_target_pairs={{0,1},{1,0},{2,3},{3,2},{4,5},{5,4},{6,7},{7,6},{8,9},{9,8},{10,11... | collective-permute-start | bytes 6291464 | tf_op jit(solution)/shard_map/ppermute | solution.py:485
  362.2 16.2 %copy-start.11 = (f32[2,1024,256]{2,1,0:T(8,128)}, f32[2,1024,256]{2,1,0:T(8,128)S(1)}, u32[]{:S(2)}) copy-start(f32[2,1024,256]{2,1,0:T(8,128)S(1)} %get-tuple-element.74.keep) | copy-start | bytes 6291460
  362.2 16.2 %collective-permute-start.19 = (f32[2,1024,256]{2,1,0:T(8,128)}, f32[2,1024,256]{2,1,0:T(8,128)}, u32[]{:S(2)}, u32[]{:S(2)}) collective-permute-start(f32[2,1024,256]{2,1,0:T(8,128)} %get-tuple-element.75), channel_id=1, source_target_pairs={{0,1},{1,0},{2,3},{3,2},{4,5},{5,4},{6,7},{7,6},{8,9},{9,8},{10,11... | collective-permute-start | bytes 6291464 | tf_op jit(solution)/shard_map/ppermute | solution.py:485
  378.3 41.8 %collective-permute-start.28 = (f32[2,1024,256]{2,1,0:T(8,128)}, f32[2,1024,256]{2,1,0:T(8,128)}, u32[]{:S(2)}, u32[]{:S(2)}) collective-permute-start(f32[2,1024,256]{2,1,0:T(8,128)} %get-tuple-element.86), channel_id=1, source_target_pairs={{0,1},{1,0},{2,3},{3,2},{4,5},{5,4},{6,7},{7,6},{8,9},{9,8},{10,11... | collective-permute-start | bytes 6291464 | tf_op jit(solution)/shard_map/ppermute | solution.py:485
  387.6 36.0 %collective-permute-start.20 = (f32[2,1024,256]{2,1,0:T(8,128)}, f32[2,1024,256]{2,1,0:T(8,128)S(1)}, u32[]{:S(2)}, u32[]{:S(2)}) collective-permute-start(f32[2,1024,256]{2,1,0:T(8,128)} %get-tuple-element.78), channel_id=1, source_target_pairs={{0,1},{1,0},{2,3},{3,2},{4,5},{5,4},{6,7},{7,6},{8,9},{9,8},{10,11... | collective-permute-start | bytes 6291464 | tf_op jit(solution)/shard_map/ppermute | solution.py:485
  387.9 14.9 %collective-permute-start.43 = (bf16[1040,256]{1,0:T(8,128)(2,1)S(1)}, bf16[1040,256]{1,0:T(8,128)(2,1)S(1)}, u32[]{:S(2)}, u32[]{:S(2)}) collective-permute-start(bf16[1040,256]{1,0:T(8,128)(2,1)S(1)} %send.4), channel_id=1, source_target_pairs={{0,2},{1,3},{2,0},{3,1},{4,6},{5,7},{6,4},{7,5},{8,10},{9,11},{10,... | collective-permute-start | bytes 1597448 | tf_op jit(solution)/shard_map/ppermute | solution.py:485
  388.4 38.3 %collective-permute-start.36 = (bf16[1040,256]{1,0:T(8,128)(2,1)}, bf16[1040,256]{1,0:T(8,128)(2,1)S(1)}, u32[]{:S(2)}, u32[]{:S(2)}) collective-permute-start(bf16[1040,256]{1,0:T(8,128)(2,1)} %send.5), channel_id=1, source_target_pairs={{0,2},{1,3},{2,0},{3,1},{4,6},{5,7},{6,4},{7,5},{8,10},{9,11},{10,... | collective-permute-start | bytes 1597448 | tf_op jit(solution)/shard_map/ppermute | solution.py:485
  414.0 2.2 copy-start
  417.8 23.8 %collective-permute-start.44 = (bf16[1040,256]{1,0:T(8,128)(2,1)}, bf16[1040,256]{1,0:T(8,128)(2,1)S(1)}, u32[]{:S(2)}, u32[]{:S(2)}) collective-permute-start(bf16[1040,256]{1,0:T(8,128)(2,1)} %get-tuple-element.101), channel_id=1, source_target_pairs={{0,4},{1,5},{2,6},{3,7},{16,20},{17,21},{18,22},{19,23}} | collective-permute-start | bytes 1597448 | tf_op jit(solution)/shard_map/ppermute | solution.py:502
  419.1 23.2 %collective-permute-start.45 = (bf16[1040,256]{1,0:T(8,128)(2,1)S(1)}, bf16[1040,256]{1,0:T(8,128)(2,1)S(1)}, u32[]{:S(2)}, u32[]{:S(2)}) collective-permute-start(bf16[1040,256]{1,0:T(8,128)(2,1)S(1)} %get-tuple-element.102), channel_id=1, source_target_pairs={{12,8},{13,9},{14,10},{15,11},{28,24},{29,25},{30,26},{31,27}} | collective-permute-start | bytes 1597448 | tf_op jit(solution)/shard_map/ppermute | solution.py:505
  420.0 6.7 %copy-start.12 = (f32[2,1024,256]{2,1,0:T(8,128)S(1)}, f32[2,1024,256]{2,1,0:T(8,128)}, u32[]{:S(2)}) copy-start(f32[2,1024,256]{2,1,0:T(8,128)} %copy-done.11) | copy-start | bytes 6291460
  423.0 23.7 %collective-permute-start.29 = (bf16[1040,256]{1,0:T(8,128)(2,1)}, bf16[1040,256]{1,0:T(8,128)(2,1)}, u32[]{:S(2)}, u32[]{:S(2)}) collective-permute-start(bf16[1040,256]{1,0:T(8,128)(2,1)} %send.7), channel_id=1, source_target_pairs={{0,2},{1,3},{2,0},{3,1},{4,6},{5,7},{6,4},{7,5},{8,10},{9,11},{10,... | collective-permute-start | bytes 1597448 | tf_op jit(solution)/shard_map/ppermute | solution.py:485
  425.3 35.6 %collective-permute-start.21 = (bf16[1040,256]{1,0:T(8,128)(2,1)}, bf16[1040,256]{1,0:T(8,128)(2,1)}, u32[]{:S(2)}, u32[]{:S(2)}) collective-permute-start(bf16[1040,256]{1,0:T(8,128)(2,1)} %send.6), channel_id=1, source_target_pairs={{0,2},{1,3},{2,0},{3,1},{4,6},{5,7},{6,4},{7,5},{8,10},{9,11},{10,... | collective-permute-start | bytes 1597448 | tf_op jit(solution)/shard_map/ppermute | solution.py:485
  436.4 2.2 copy-start.2
  438.6 3.8 copy-start.1
  440.3 33.7 %collective-permute-start.37 = (bf16[1040,256]{1,0:T(8,128)(2,1)}, bf16[1040,256]{1,0:T(8,128)(2,1)S(1)}, u32[]{:S(2)}, u32[]{:S(2)}) collective-permute-start(bf16[1040,256]{1,0:T(8,128)(2,1)} %get-tuple-element.94), channel_id=1, source_target_pairs={{0,4},{1,5},{2,6},{3,7},{16,20},{17,21},{18,22},{19,23}} | collective-permute-start | bytes 1597448 | tf_op jit(solution)/shard_map/ppermute | solution.py:502
  441.6 33.5 %collective-permute-start.38 = (bf16[1040,256]{1,0:T(8,128)(2,1)}, bf16[1040,256]{1,0:T(8,128)(2,1)S(1)}, u32[]{:S(2)}, u32[]{:S(2)}) collective-permute-start(bf16[1040,256]{1,0:T(8,128)(2,1)} %get-tuple-element.95), channel_id=1, source_target_pairs={{12,8},{13,9},{14,10},{15,11},{28,24},{29,25},{30,26},{31,27}} | collective-permute-start | bytes 1597448 | tf_op jit(solution)/shard_map/ppermute | solution.py:505
  445.4 31.0 %collective-permute-start.46 = (bf16[1040,256]{1,0:T(8,128)(2,1)}, bf16[1040,256]{1,0:T(8,128)(2,1)S(1)}, u32[]{:S(2)}, u32[]{:S(2)}) collective-permute-start(bf16[1040,256]{1,0:T(8,128)(2,1)} %get-tuple-element.103), channel_id=1, source_target_pairs={{0,4},{4,8},{1,5},{5,9},{2,6},{6,10},{3,7},{7,11},{16,20},{20,24},... | collective-permute-start | bytes 1597448 | tf_op jit(solution)/shard_map/ppermute | solution.py:502
  456.6 2.2 copy-start.4
  459.5 19.2 %collective-permute-start.30 = (bf16[1040,256]{1,0:T(8,128)(2,1)S(1)}, bf16[1040,256]{1,0:T(8,128)(2,1)S(1)}, u32[]{:S(2)}, u32[]{:S(2)}) collective-permute-start(bf16[1040,256]{1,0:T(8,128)(2,1)S(1)} %get-tuple-element.87), channel_id=1, source_target_pairs={{0,4},{1,5},{2,6},{3,7},{16,20},{17,21},{18,22},{19,23}} | collective-permute-start | bytes 1597448 | tf_op jit(solution)/shard_map/ppermute | solution.py:502
  460.9 19.2 %collective-permute-start.31 = (bf16[1040,256]{1,0:T(8,128)(2,1)S(1)}, bf16[1040,256]{1,0:T(8,128)(2,1)S(1)}, u32[]{:S(2)}, u32[]{:S(2)}) collective-permute-start(bf16[1040,256]{1,0:T(8,128)(2,1)S(1)} %get-tuple-element.88), channel_id=1, source_target_pairs={{12,8},{13,9},{14,10},{15,11},{28,24},{29,25},{30,26},{31,27}} | collective-permute-start | bytes 1597448 | tf_op jit(solution)/shard_map/ppermute | solution.py:505
  471.0 2.2 copy-start.6
  473.2 4.1 copy-start.3
  474.3 8.0 %collective-permute-start.47 = (bf16[1040,256]{1,0:T(8,128)(2,1)S(1)}, bf16[1040,256]{1,0:T(8,128)(2,1)S(1)}, u32[]{:S(2)}, u32[]{:S(2)}) collective-permute-start(bf16[1040,256]{1,0:T(8,128)(2,1)S(1)} %copy-done.16), channel_id=1, source_target_pairs={{8,4},{12,8},{9,5},{13,9},{10,6},{14,10},{11,7},{15,11},{24,20},{2... | collective-permute-start | bytes 1597448 | tf_op jit(solution)/shard_map/ppermute | solution.py:505
  475.1 15.4 %collective-permute-start.22 = (bf16[1040,256]{1,0:T(8,128)(2,1)S(1)}, bf16[1040,256]{1,0:T(8,128)(2,1)S(1)}, u32[]{:S(2)}, u32[]{:S(2)}) collective-permute-start(bf16[1040,256]{1,0:T(8,128)(2,1)S(1)} %get-tuple-element.79), channel_id=1, source_target_pairs={{0,4},{1,5},{2,6},{3,7},{16,20},{17,21},{18,22},{19,23}} | collective-permute-start | bytes 1597448 | tf_op jit(solution)/shard_map/ppermute | solution.py:502
  476.4 4.4 copy-start.5
  476.4 16.2 %collective-permute-start.23 = (bf16[1040,256]{1,0:T(8,128)(2,1)S(1)}, bf16[1040,256]{1,0:T(8,128)(2,1)S(1)}, u32[]{:S(2)}, u32[]{:S(2)}) collective-permute-start(bf16[1040,256]{1,0:T(8,128)(2,1)S(1)} %get-tuple-element.80), channel_id=1, source_target_pairs={{12,8},{13,9},{14,10},{15,11},{28,24},{29,25},{30,26},{31,27}} | collective-permute-start | bytes 1597448 | tf_op jit(solution)/shard_map/ppermute | solution.py:505
  478.8 21.6 %collective-permute-start.39 = (bf16[1040,256]{1,0:T(8,128)(2,1)S(1)}, bf16[1040,256]{1,0:T(8,128)(2,1)S(1)}, u32[]{:S(2)}, u32[]{:S(2)}) collective-permute-start(bf16[1040,256]{1,0:T(8,128)(2,1)S(1)} %get-tuple-element.96), channel_id=1, source_target_pairs={{0,4},{4,8},{1,5},{5,9},{2,6},{6,10},{3,7},{7,11},{16,20},{20,24},... | collective-permute-start | bytes 1597448 | tf_op jit(solution)/shard_map/ppermute | solution.py:502
  480.1 20.9 %collective-permute-start.40 = (bf16[1040,256]{1,0:T(8,128)(2,1)S(1)}, bf16[1040,256]{1,0:T(8,128)(2,1)S(1)}, u32[]{:S(2)}, u32[]{:S(2)}) collective-permute-start(bf16[1040,256]{1,0:T(8,128)(2,1)S(1)} %get-tuple-element.97), channel_id=1, source_target_pairs={{8,4},{12,8},{9,5},{13,9},{10,6},{14,10},{11,7},{15,11},{24,20},{2... | collective-permute-start | bytes 1597448 | tf_op jit(solution)/shard_map/ppermute | solution.py:505
  482.3 29.4 %collective-permute-start.32 = (bf16[1040,256]{1,0:T(8,128)(2,1)S(1)}, bf16[1040,256]{1,0:T(8,128)(2,1)S(1)}, u32[]{:S(2)}, u32[]{:S(2)}) collective-permute-start(bf16[1040,256]{1,0:T(8,128)(2,1)S(1)} %get-tuple-element.89), channel_id=1, source_target_pairs={{0,4},{4,8},{1,5},{5,9},{2,6},{6,10},{3,7},{7,11},{16,20},{20,24},... | collective-permute-start | bytes 1597448 | tf_op jit(solution)/shard_map/ppermute | solution.py:502
  490.5 22.6 %collective-permute-start.33 = (bf16[1040,256]{1,0:T(8,128)(2,1)S(1)}, bf16[1040,256]{1,0:T(8,128)(2,1)S(1)}, u32[]{:S(2)}, u32[]{:S(2)}) collective-permute-start(bf16[1040,256]{1,0:T(8,128)(2,1)S(1)} %get-tuple-element.90), channel_id=1, source_target_pairs={{8,4},{12,8},{9,5},{13,9},{10,6},{14,10},{11,7},{15,11},{24,20},{2... | collective-permute-start | bytes 1597448 | tf_op jit(solution)/shard_map/ppermute | solution.py:505
  494.1 29.0 %collective-permute-start.24 = (bf16[1040,256]{1,0:T(8,128)(2,1)S(1)}, bf16[1040,256]{1,0:T(8,128)(2,1)S(1)}, u32[]{:S(2)}, u32[]{:S(2)}) collective-permute-start(bf16[1040,256]{1,0:T(8,128)(2,1)S(1)} %get-tuple-element.81), channel_id=1, source_target_pairs={{0,4},{4,8},{1,5},{5,9},{2,6},{6,10},{3,7},{7,11},{16,20},{20,24},... | collective-permute-start | bytes 1597448 | tf_op jit(solution)/shard_map/ppermute | solution.py:502
  500.3 24.1 %collective-permute-start.25 = (bf16[1040,256]{1,0:T(8,128)(2,1)S(1)}, bf16[1040,256]{1,0:T(8,128)(2,1)S(1)}, u32[]{:S(2)}, u32[]{:S(2)}) collective-permute-start(bf16[1040,256]{1,0:T(8,128)(2,1)S(1)} %get-tuple-element.82), channel_id=1, source_target_pairs={{8,4},{12,8},{9,5},{13,9},{10,6},{14,10},{11,7},{15,11},{24,20},{2... | collective-permute-start | bytes 1597448 | tf_op jit(solution)/shard_map/ppermute | solution.py:505
  501.0 33.5 %collective-permute-start.48 = (bf16[1040,256]{1,0:T(8,128)(2,1)S(1)}, bf16[1040,256]{1,0:T(8,128)(2,1)S(1)}, u32[]{:S(2)}, u32[]{:S(2)}) collective-permute-start(bf16[1040,256]{1,0:T(8,128)(2,1)S(1)} %get-tuple-element.105), channel_id=1, source_target_pairs={{0,4},{4,8},{8,12},{1,5},{5,9},{9,13},{2,6},{6,10},{10,14},{3,7},{... | collective-permute-start | bytes 1597448 | tf_op jit(solution)/shard_map/ppermute | solution.py:502
  511.8 24.1 %collective-permute-start.49 = (bf16[1040,256]{1,0:T(8,128)(2,1)S(1)}, bf16[1040,256]{1,0:T(8,128)(2,1)S(1)}, u32[]{:S(2)}, u32[]{:S(2)}) collective-permute-start(bf16[1040,256]{1,0:T(8,128)(2,1)S(1)} %get-tuple-element.106), channel_id=1, source_target_pairs={{4,0},{8,4},{12,8},{5,1},{9,5},{13,9},{6,2},{10,6},{14,10},{7,3},{... | collective-permute-start | bytes 1597448 | tf_op jit(solution)/shard_map/ppermute | solution.py:505
  513.0 32.9 %collective-permute-start.41 = (bf16[1040,256]{1,0:T(8,128)(2,1)S(1)}, bf16[1040,256]{1,0:T(8,128)(2,1)S(1)}, u32[]{:S(2)}, u32[]{:S(2)}) collective-permute-start(bf16[1040,256]{1,0:T(8,128)(2,1)S(1)} %get-tuple-element.98), channel_id=1, source_target_pairs={{0,4},{4,8},{8,12},{1,5},{5,9},{9,13},{2,6},{6,10},{10,14},{3,7},{... | collective-permute-start | bytes 1597448 | tf_op jit(solution)/shard_map/ppermute | solution.py:502
  523.2 26.4 %collective-permute-start.42 = (bf16[1040,256]{1,0:T(8,128)(2,1)S(1)}, bf16[1040,256]{1,0:T(8,128)(2,1)S(1)}, u32[]{:S(2)}, u32[]{:S(2)}) collective-permute-start(bf16[1040,256]{1,0:T(8,128)(2,1)S(1)} %get-tuple-element.99), channel_id=1, source_target_pairs={{4,0},{8,4},{12,8},{5,1},{9,5},{13,9},{6,2},{10,6},{14,10},{7,3},{... | collective-permute-start | bytes 1597448 | tf_op jit(solution)/shard_map/ppermute | solution.py:505
  524.5 32.9 %collective-permute-start.34 = (bf16[1040,256]{1,0:T(8,128)(2,1)S(1)}, bf16[1040,256]{1,0:T(8,128)(2,1)S(1)}, u32[]{:S(2)}, u32[]{:S(2)}) collective-permute-start(bf16[1040,256]{1,0:T(8,128)(2,1)S(1)} %get-tuple-element.91), channel_id=1, source_target_pairs={{0,4},{4,8},{8,12},{1,5},{5,9},{9,13},{2,6},{6,10},{10,14},{3,7},{... | collective-permute-start | bytes 1597448 | tf_op jit(solution)/shard_map/ppermute | solution.py:502
  534.6 22.8 %collective-permute-start.35 = (bf16[1040,256]{1,0:T(8,128)(2,1)S(1)}, bf16[1040,256]{1,0:T(8,128)(2,1)S(1)}, u32[]{:S(2)}, u32[]{:S(2)}) collective-permute-start(bf16[1040,256]{1,0:T(8,128)(2,1)S(1)} %get-tuple-element.92), channel_id=1, source_target_pairs={{4,0},{8,4},{12,8},{5,1},{9,5},{13,9},{6,2},{10,6},{14,10},{7,3},{... | collective-permute-start | bytes 1597448 | tf_op jit(solution)/shard_map/ppermute | solution.py:505
  535.9 30.2 %collective-permute-start.26 = (bf16[1040,256]{1,0:T(8,128)(2,1)S(1)}, bf16[1040,256]{1,0:T(8,128)(2,1)S(1)}, u32[]{:S(2)}, u32[]{:S(2)}) collective-permute-start(bf16[1040,256]{1,0:T(8,128)(2,1)S(1)} %get-tuple-element.83), channel_id=1, source_target_pairs={{0,4},{4,8},{8,12},{1,5},{5,9},{9,13},{2,6},{6,10},{10,14},{3,7},{... | collective-permute-start | bytes 1597448 | tf_op jit(solution)/shard_map/ppermute | solution.py:502
  546.0 20.1 %collective-permute-start.27 = (bf16[1040,256]{1,0:T(8,128)(2,1)S(1)}, bf16[1040,256]{1,0:T(8,128)(2,1)S(1)}, u32[]{:S(2)}, u32[]{:S(2)}) collective-permute-start(bf16[1040,256]{1,0:T(8,128)(2,1)S(1)} %get-tuple-element.84), channel_id=1, source_target_pairs={{4,0},{8,4},{12,8},{5,1},{9,5},{13,9},{6,2},{10,6},{14,10},{7,3},{... | collective-permute-start | bytes 1597448 | tf_op jit(solution)/shard_map/ppermute | solution.py:505
  (6 other events, 7.9 us)

commit v7 on v6

--- a/solution.py
+++ b/solution.py
@@ -38,7 +38,54 @@
     return lax.dot_general(a, b, (dims, ((), ())), preferred_element_type=F32)
 
 
-def halfway_kernel(place_ref, left, *refs, offsets, lines, first, last):
+TOP = 7.5
+
+
+def encode(value, inverse):
+    code = jnp.abs(value) * (inverse * 2.0**TOP)
+    for _ in range(4):
+        code = code * code
+    return jnp.where(value < 0, -code, code).astype(BF16)
+
+
+def decode(code, scale):
+    code = code.astype(F32)
+    size = jnp.abs(code)
+    root = jnp.exp2(jnp.log2(size) * 0.0625 - TOP) * scale
+    root = jnp.where(size > 0, root, 0.0)
+    return jnp.where(code < 0, -root, root)
+
+
+def scale_of(message, depth):
+    return jnp.max(message[depth : depth + EXTRA, :].astype(F32), axis=(0, 1), keepdims=True)
+
+
+def fill(message, total, value_at, tile, again=None):
+    depth, piece = message.shape[0] - EXTRA, message.shape[1]
+
+    def add(i, top):
+        rows = pl.ds(pl.multiple_of(i * tile, tile), tile)
+        value = value_at(rows)
+        if again is None:
+            total[rows, :] = value
+        return jnp.maximum(top, jnp.abs(value))
+
+    top = lax.fori_loop(0, depth // tile, add, jnp.zeros((tile, piece), F32))
+    top = jnp.maximum(jnp.max(top, axis=(0, 1), keepdims=True), 1e-30)
+    scale = jnp.broadcast_to(top, (EXTRA, piece)).astype(BF16)
+    message[depth : depth + EXTRA, :] = scale
+    inverse = 1.0 / jnp.max(scale.astype(F32), axis=(0, 1), keepdims=True)
+
+    def put(i, carry):
+        rows = pl.ds(pl.multiple_of(i * tile, tile), tile)
+        value = total[rows, :] if again is None else again(rows)
+        message[rows, :] = encode(value, inverse)
+        return carry
+
+    lax.fori_loop(0, depth // tile, put, 0)
+
+
+def halfway_kernel(place_ref, left, *refs, offsets, lines, first):
     pieces, refs = refs[: len(offsets)], refs[len(offsets) :]
     total = refs[-1]
     depth = pieces[0].shape[0]
@@ -51,86 +98,85 @@
             rows = left[pl.ds(pl.multiple_of((place + offset) * depth, depth), depth), :]
             total[...] += dot(rows, piece[...], ((0,), (0,)))
 
-    if last:
-        high, low = kernel_split(total[...])
-        refs[-2][0] = high
-        refs[-2][1] = low
-    else:
-        refs[-2][...] = total[...]
-
-
-def halfway(place, left, held, offsets, lines, before, last):
+    refs[-2][...] = total[...]
+
+
+def halfway(place, left, held, offsets, lines, before):
     pieces = [held[offset] for offset in offsets]
-    depth, half = pieces[0].shape
+    depth, width = pieces[0].shape
     inner = left.shape[1]
     tile = min(256, inner)
-    whole = pl.BlockSpec((depth, half), lambda i, s: (0, 0))
-    block = pl.BlockSpec((tile, half), lambda i, s: (i, 0))
+    whole = pl.BlockSpec((depth, width), lambda i, s: (0, 0))
+    block = pl.BlockSpec((tile, width), lambda i, s: (i, 0))
     extra = [] if before is None else [before]
     return pl.pallas_call(
-        functools.partial(
-            halfway_kernel, offsets=offsets, lines=lines, first=before is None, last=last
-        ),
+        functools.partial(halfway_kernel, offsets=offsets, lines=lines, first=before is None),
         grid_spec=pltpu.PrefetchScalarGridSpec(
             num_scalar_prefetch=1,
             grid=(inner // tile,),
             in_specs=[pl.BlockSpec((left.shape[0], tile), lambda i, s: (0, i))]
             + [whole] * len(pieces)
             + [block] * len(extra),
-            out_specs=pl.BlockSpec((2, tile, half), lambda i, s: (0, i, 0)) if last else block,
-            scratch_shapes=[pltpu.VMEM((tile, half), F32)],
-        ),
-        out_shape=jax.ShapeDtypeStruct((2, inner, half), BF16)
-        if last
-        else jax.ShapeDtypeStruct((inner, half), F32),
+            out_specs=block,
+            scratch_shapes=[pltpu.VMEM((tile, width), F32)],
+        ),
+        out_shape=jax.ShapeDtypeStruct((inner, width), F32),
         compiler_params=params(48),
-        cost_estimate=cost(8 * depth * inner * half, 8 * depth * inner),
+        cost_estimate=cost(8 * depth * inner * width, 8 * depth * inner),
         name="halfway",
     )(place, left, *pieces, *extra)
 
 
-def flip_kernel(at_ref, rows, above, below, out, *, far):
-    me, place = at_ref[0], at_ref[1]
-    late = (me ^ pl.program_id(0)) == far - place
-
-    @pl.when(jnp.logical_not(late & ((place == 0) | (place == far))))
-    def _():
-        out[...] = rows[...].T
-
-    @pl.when(late & (place == 0))
-    def _():
-        out[...] = above[...].T
-
-    @pl.when(late & (place == far))
-    def _():
-        out[...] = below[...].T
-
-
-def flip(at, right, above, below, cols, lines, chunk, piece):
-    width = right.shape[1]
-    per = above.shape[0] // piece
-    if per * piece != width:
-        far, per = -1, 1
-    else:
-        far = lines - 1
-    last = pl.BlockSpec((piece, width), lambda d, s: (chunk if per > 1 else 0, 0))
-    return pl.pallas_call(
-        functools.partial(flip_kernel, far=far),
-        grid_spec=pltpu.PrefetchScalarGridSpec(
-            num_scalar_prefetch=1,
-            grid=(cols,),
-            in_specs=[
-                pl.BlockSpec((piece, width), lambda d, s: ((s[0] ^ d) * CHUNKS + chunk, 0)),
-                last,
-                last,
-            ],
-            out_specs=pl.BlockSpec((width, piece), lambda d, s: (0, d)),
-        ),
-        out_shape=jax.ShapeDtypeStruct((width, cols * piece), BF16),
-        compiler_params=params(48),
-        cost_estimate=cost(0, 4 * piece * cols * width),
-        name="flip",
-    )(at, right, above, below)
+def pack_kernel(value, pair, message, *, tile):
+    depth, _ = value.shape
+
+    def value_at(rows):
+        now = value[rows, :]
+        high, low = kernel_split(now)
+        pair[0, rows, :] = high
+        pair[1, rows, :] = low
+        return now
+
+    fill(message, None, value_at, tile, lambda rows: value[rows, :])
+
+
+def pack(value):
+    depth, width = value.shape
+    return pl.pallas_call(
+        functools.partial(pack_kernel, tile=min(16, depth)),
+        out_shape=[
+            jax.ShapeDtypeStruct((2, depth, width), BF16),
+            jax.ShapeDtypeStruct((depth + EXTRA, width), BF16),
+        ],
+        compiler_params=params(32),
+        cost_estimate=cost(400 * depth * width, 10 * depth * width),
+        name="pack",
+    )(value)
+
+
+def unpack_kernel(message, pair, *, tile):
+    _, depth, _ = pair.shape
+    scale = scale_of(message, depth)
+
+    def put(i, carry):
+        rows = pl.ds(pl.multiple_of(i * tile, tile), tile)
+        high, low = kernel_split(decode(message[rows, :], scale))
+        pair[0, rows, :] = high
+        pair[1, rows, :] = low
+        return carry
+
+    lax.fori_loop(0, depth // tile, put, 0)
+
+
+def unpack(message):
+    depth, width = message.shape[0] - EXTRA, message.shape[1]
+    return pl.pallas_call(
+        functools.partial(unpack_kernel, tile=min(16, depth)),
+        out_shape=jax.ShapeDtypeStruct((2, depth, width), BF16),
+        compiler_params=params(32),
+        cost_estimate=cost(400 * depth * width, 6 * depth * width),
+        name="unpack",
+    )(message)
 
 
 def rotate_part_kernel(me_ref, *refs, cols, width):
@@ -244,9 +290,29 @@
     )(at, part, above, below, first, second, *pieces)
 
 
-def restore_kernel(normed, flipped, keep, mate, *, cols):
-    tile = normed.shape[1]
-    piece = keep.shape[2]
+def restore_kernel(at_ref, normed, *refs, cols, far):
+    rows, (above, below, keep, mate, flipped) = refs[:cols], refs[cols:]
+    tile, piece = normed.shape[1], keep.shape[2]
+    me, place = at_ref[0], at_ref[1]
+
+    @pl.when(pl.program_id(0) == 0)
+    def _():
+        for distance in range(cols):
+            here = pl.ds(distance * piece, piece)
+            late = (me ^ distance) == far - place
+
+            @pl.when(jnp.logical_not(late & ((place == 0) | (place == far))))
+            def _(distance=distance, here=here):
+                flipped[:, here] = rows[distance][...].T
+
+            @pl.when(late & (place == 0))
+            def _(here=here):
+                flipped[:, here] = above[...].T
+
+            @pl.when(late & (place == far))
+            def _(here=here):
+                flipped[:, here] = below[...].T
+
     both = dot(normed[...].reshape(2 * tile, normed.shape[2]), flipped[...], ((1,), (0,)))
     term = both[:tile] + both[tile:]
     for distance in range(cols):
@@ -254,69 +320,33 @@
         out[distance // 2] = term[:, distance * piece : (distance + 1) * piece]
 
 
-def restore(normed, flipped, cols):
+def restore(at, normed, right, above, below, cols, lines, chunk, piece):
     _, depth, inner = normed.shape
-    piece = flipped.shape[1] // cols
     tile = min(256, depth)
-    out = pl.BlockSpec((cols // 2, tile, piece), lambda i: (0, i, 0))
-    return pl.pallas_call(
-        functools.partial(restore_kernel, cols=cols),
-        grid=(depth // tile,),
-        in_specs=[
-            pl.BlockSpec((2, tile, inner), lambda i: (0, i, 0)),
-            pl.BlockSpec(flipped.shape, lambda i: (0, 0), pipeline_mode=pl.Buffered(1)),
-        ],
-        out_specs=[out, out],
+    aligned = above.shape[0] == inner
+    far = lines - 1 if aligned else -cols
+    out = pl.BlockSpec((cols // 2, tile, piece), lambda i, s: (0, i, 0))
+
+    def rows(distance):
+        return pl.BlockSpec((piece, inner), lambda i, s: ((s[0] ^ distance) * CHUNKS + chunk, 0))
+
+    last = pl.BlockSpec((piece, inner), lambda i, s: (chunk if aligned else 0, 0))
+    return pl.pallas_call(
+        functools.partial(restore_kernel, cols=cols, far=far),
+        grid_spec=pltpu.PrefetchScalarGridSpec(
+            num_scalar_prefetch=1,
+            grid=(depth // tile,),
+            in_specs=[pl.BlockSpec((2, tile, inner), lambda i, s: (0, i, 0))]
+            + [rows(distance) for distance in range(cols)]
+            + [last, last],
+            out_specs=[out, out],
+            scratch_shapes=[pltpu.VMEM((inner, cols * piece), BF16)],
+        ),
         out_shape=[jax.ShapeDtypeStruct((cols // 2, depth, piece), F32)] * 2,
-        compiler_params=params(24),
+        compiler_params=params(40),
         cost_estimate=cost(4 * depth * inner * piece * cols, 8 * depth * piece * cols),
         name="restore",
-    )(normed, flipped)
-
-
-TOP = 7.5
-
-
-def encode(value, inverse):
-    code = jnp.abs(value) * (inverse * 2.0**TOP)
-    for _ in range(4):
-        code = code * code
-    return jnp.where(value < 0, -code, code).astype(BF16)
-
-
-def decode(code, scale):
-    code = code.astype(F32)
-    size = jnp.abs(code)
-    root = jnp.exp2(jnp.log2(size) * 0.0625 - TOP) * scale
-    root = jnp.where(size > 0, root, 0.0)
-    return jnp.where(code < 0, -root, root)
-
-
-def scale_of(message, depth):
-    return jnp.max(message[depth : depth + EXTRA, :].astype(F32), axis=(0, 1), keepdims=True)
-
-
-def fill(message, total, value_at, tile):
-    depth, piece = total.shape
-
-    def add(i, top):
-        rows = pl.ds(pl.multiple_of(i * tile, tile), tile)
-        value = value_at(rows)
-        total[rows, :] = value
-        return jnp.maximum(top, jnp.abs(value))
-
-    top = lax.fori_loop(0, depth // tile, add, jnp.zeros((tile, piece), F32))
-    top = jnp.maximum(jnp.max(top, axis=(0, 1), keepdims=True), 1e-30)
-    scale = jnp.broadcast_to(top, (EXTRA, piece)).astype(BF16)
-    message[depth : depth + EXTRA, :] = scale
-    inverse = 1.0 / jnp.max(scale.astype(F32), axis=(0, 1), keepdims=True)
-
-    def put(i, carry):
-        rows = pl.ds(pl.multiple_of(i * tile, tile), tile)
-        message[rows, :] = encode(total[rows, :], inverse)
-        return carry
-
-    lax.fori_loop(0, depth // tile, put, 0)
+    )(at, normed, *([right] * cols), above, below)
 
 
 def summed(keep, mate, codes):
@@ -437,7 +467,7 @@
             scratch_shapes=[pltpu.VMEM((depth, piece), F32)],
         ),
         out_shape=[jax.ShapeDtypeStruct((depth + EXTRA, piece), BF16)] * 2,
-        compiler_params=params(16),
+        compiler_params=params(48),
         cost_estimate=cost(400 * depth * piece, 12 * depth * piece),
         name="hop",
     )(place, product, product, *arrived)
@@ -474,7 +504,7 @@
         ),
         out_shape=jax.ShapeDtypeStruct((depth, width), F32),
         input_output_aliases={4: 0} if extra else {},
-        compiler_params=params(16),
+        compiler_params=params(48),
         cost_estimate=cost(400 * depth * piece, 12 * depth * piece),
         name="finish",
     )(at, product, *arrived, *extra)
@@ -525,7 +555,7 @@
                     (left, grads[1 - step], grads[step - 1])
                 )
             walk(grads, step)
-        before = halfway(spot, left, grads, near, lines, None, False)
+        before = halfway(spot, left, grads, near, lines, None)
 
         own, before, grads[-far], grads[far] = barrier(
             (right_basis, before, grads[-far], grads[far])
@@ -540,18 +570,15 @@
 
         right = put(right, 0)
         for step in range(1, lines):
-            if step == far:
-                right, rights[1 - step], rights[step - 1] = barrier(
-                    (right, rights[1 - step], rights[step - 1])
-                )
             walk(rights, step)
             if step < far or depth != width:
                 right = put(put(right, -step), step)
         above, below = rights[far], rights[-far]
 
-        whole = halfway(spot, left, grads, [-far, far], lines, before, True)
-        pieces = by_distance(whole)
-        pieces = [pieces[distance] for distance in range(cols)]
+        pair, message = pack(halfway(spot, left, grads, [-far, far], lines, before))
+        message, rights[-1], rights[1] = barrier((message, rights[-1], rights[1]))
+        pieces = by_distance(message)
+        pieces = [pair] + [unpack(pieces[distance]) for distance in range(1, cols)]
         part = rotate_part(at, pieces, right)
         part, above, below = barrier((part, above, below))
         if depth != width:
@@ -562,23 +589,23 @@
             at, part, pieces, above_now, below_now, first_moment, second_moment, lines
         )
 
-        halves, coded = [], []
+        products, hops = [], []
         for chunk in range(CHUNKS):
             if chunk >= 2:
-                normed, coded[chunk - 2] = barrier((normed, coded[chunk - 2]))
-            flipped = flip(at, right, above, below, cols, lines, chunk, piece)
-            keep, mate = restore(normed, flipped, cols)
+                normed, hops[chunk - 2] = barrier((normed, hops[chunk - 2]))
+            keep, mate = restore(at, normed, right, above, below, cols, lines, chunk, piece)
             mate = swap(mate, 1)
-            halves.append((keep, mate))
-            coded.append([send(keep, mate, distance, []) for distance in range(2, cols, 2)])
-        crossed = [
-            [swap(code, 2 * index + 2) for index, code in enumerate(codes)] for codes in coded
-        ]
-        products = [expand(*halves[c], crossed[c], left) for c in range(CHUNKS)]
+            crossed = [
+                swap(send(keep, mate, distance, []), distance) for distance in range(2, cols, 2)
+            ]
+            products.append(expand(keep, mate, crossed, left))
+            hops.append(hop(spot, products[chunk], (), lines, 1))
         arrived = [()] * CHUNKS
         for step in range(1, lines):
             for chunk, product in enumerate(products):
-                upward, downward = hop(spot, product, arrived[chunk], lines, step)
+                if step > 1:
+                    hops[chunk] = hop(spot, product, arrived[chunk], lines, step)
+                upward, downward = hops[chunk]
                 arrived[chunk] = (
                     up(upward, range(0, step)),
                     down(downward, range(lines - step, lines)),

time: 576 us -> 560 us (0.972)
  waiting for transfers between devices: 258 us -> 211 us
  Pallas kernels: 176 us -> 196 us
  starting transfers between devices: 84.7 us -> 98.3 us
    ppermute x18, waiting for transfers between devices: 68.7 us -> 43.1 us  [up(): return lax.ppermute(value, 'row', [(i, i + 1) for i in senders])]
    ppermute x18, waiting for transfers between devices: 96.6 us -> 76.6 us  [down(): return lax.ppermute(value, 'row', [(i, i - 1) for i in senders])]
    pallas_call x8, Pallas kernels: 40 us -> 55 us  [the longest x4 35.1 us: restore(): pl.pallas_call(functools.partial(restore_kernel, cols=cols, far=far), gri...]
    pallas_call x12, Pallas kernels: 17.4 us -> 29.9 us  [hop(): pl.pallas_call(functools.partial(hop_kernel, lines=lines, step=step, tile...]
    ppermute x18, starting transfers between devices: 57.3 us -> 69.6 us  [up(): return lax.ppermute(value, 'row', [(i, i + 1) for i in senders])]
    dynamic_update_slice x5, local copies, waits for them, and re-layouts: 13.8 us -> 6.3 us  [put(): lax.dynamic_update_slice_in_dim(right, rights[offset], there * depth, 0)]
    unnamed x40 -> x66, local copies, waits for them, and re-layouts: 22.3 us -> 28.8 us
    pallas_call x4, Pallas kernels: 9.57 us -> 3.25 us  [send(): pl.pallas_call(functools.partial(send_kernel, tile=tile), grid=(1,), in_s...]
  transfers between devices with their start and end apart: 50 -> 50, of which waited for: 17 -> 15; matrix products, arithmetic and copies ran while one was open for 5% -> 3% of each run, Pallas kernels for 23% -> 27%
where the time goes in v7:
time: 560 us; the launch traced here: 551 us
  waiting for transfers between devices  211 us (38%)
  Pallas kernels  196 us (35%)
  starting transfers between devices  98.3 us (18%)
  local copies, waits for them, and re-layouts  43.3 us (8%)
    ppermute x14, waiting for transfers between devices, swap(): return lax.ppermute(value, 'col', [(i, i ^ distance) for i in range(cols)])  91.4 us
    ppermute x18, waiting for transfers between devices, down(): return lax.ppermute(value, 'row', [(i, i - 1) for i in senders])  76.6 us
    ppermute x18, starting transfers between devices, up(): return lax.ppermute(value, 'row', [(i, i + 1) for i in senders])  69.6 us
    ppermute x18, waiting for transfers between devices, up(): return lax.ppermute(value, 'row', [(i, i + 1) for i in senders])  43.1 us
    pallas_call x4, Pallas kernels, expand(): pl.pallas_call(functools.partial(expand_kernel, tile=min(64, depth)), gri...  37.3 us
    pallas_call x4, Pallas kernels, restore(): pl.pallas_call(functools.partial(restore_kernel, cols=cols, far=far), gri...  35.1 us
    pallas_call x12, Pallas kernels, hop(): pl.pallas_call(functools.partial(hop_kernel, lines=lines, step=step, tile...  29.9 us
    unnamed x66, local copies, waits for them, and re-layouts  28.8 us
  transfers between devices with their start and end apart: 50, of which 15 were waited for; matrix products, arithmetic and copies ran while one was open for 3% of the time, Pallas kernels for 27%

profile of v7, /device:TPU:0, one launch (start us, length us, event | category | flops | bytes accessed | tf_op | source)
XLA Modules:
  0.0 550.7 jit_solution(2663861783113587064)
XLA Ops:
  0.6 3.0 collective-permute-start
  3.6 3.6 collective-permute-start.3
  8.6 41.0 %collective-permute-done = bf16[1024,1024]{1,0:T(8,128)(2,1)} collective-permute-done((bf16[1024,1024]{1,0:T(8,128)(2,1)}, bf16[1024,1024]{1,0:T(8,128)(2,1)}, u32[]{:S(2)}, u32[]{:S(2)}) %collective-permute-start) | collective-permute-done | bytes 2097184 | tf_op jit(solution)/shard_map/ppermute | solution.py:515
  49.6 2.4 collective-permute-done.3.refs_1_
  52.0 2.0 collective-permute-start.4
  54.0 2.2 collective-permute-done.5.refs_3_
  65.1 3.2 copy-done.26
  68.3 37.4 %collective-permute-done.6.refs_4_ = bf16[1024,1024]{1,0:T(8,128)(2,1)} collective-permute-done((bf16[1024,1024]{1,0:T(8,128)(2,1)}, bf16[1024,1024]{1,0:T(8,128)(2,1)}, u32[]{:S(2)}, u32[]{:S(2)}) %collective-permute-start.6) | collective-permute-done | bytes 2097184 | tf_op jit(solution)/shard_map/ppermute | solution.py:535
  105.7 2.1 collective-permute-start.7
  109.1 14.8 %halfway.2.refs_2_ = f32[1024,1024]{1,0:T(8,128)} custom-call(s32[1]{0:T(128)} %bitcast.1.place_ref.at_ref, bf16[4096,1024]{1,0:T(8,128)(2,1)} %bitcast.11, bf16[1024,1024]{1,0:T(8,128)(2,1)} %collective-permute-done.4.refs_0_, bf16[1024,1024]{1,0:T(8,128)(2,1)S(1)} %collective-permute-done.3.refs_1_, bf16[1024,1024]{1,0:T(8,128)(2,1)} %refs_2_.1, ...), custom_call_target="tpu_custom_call" | custom-call | flops 85899344 | bytes 83886 | tf_op jit(solution)/shard_map/halfway/pallas_call | solution.py:112
  123.9 31.4 %collective-permute-done.8.refs_1_ = bf16[1024,1024]{1,0:T(8,128)(2,1)} collective-permute-done((bf16[1024,1024]{1,0:T(8,128)(2,1)}, bf16[1024,1024]{1,0:T(8,128)(2,1)}, u32[]{:S(2)}, u32[]{:S(2)}) %collective-permute-start.8) | collective-permute-done | bytes 2097184 | tf_op jit(solution)/shard_map/ppermute | solution.py:535
  158.2 9.6 %halfway.3.value = f32[1024,1024]{1,0:T(8,128)} custom-call(s32[1]{0:T(128)} %bitcast.1.place_ref.at_ref, bf16[4096,1024]{1,0:T(8,128)(2,1)} %bitcast.12, bf16[1024,1024]{1,0:T(8,128)(2,1)} %collective-permute-done.7.refs_0_, bf16[1024,1024]{1,0:T(8,128)(2,1)} %collective-permute-done.8.refs_1_, f32[1024,1024]{1,0:T(8,128)} %halfway.2.refs_2_), custom_call_target="tpu_custom_call" | custom-call | flops 85899344 | bytes 83886 | tf_op jit(solution)/shard_map/halfway/pallas_call | solution.py:112
  167.8 2.2 copy-done.12
  170.0 4.4 pack.1
  174.4 2.0 copy-done.11
  176.4 22.4 %collective-permute-done.9 = bf16[1024,1024]{1,0:T(8,128)(2,1)S(1)} collective-permute-done((bf16[1024,1024]{1,0:T(8,128)(2,1)S(1)}, bf16[1024,1024]{1,0:T(8,128)(2,1)S(1)}, u32[]{:S(2)}, u32[]{:S(2)}) %collective-permute-start.9) | collective-permute-done | bytes 2097184 | tf_op jit(solution)/shard_map/ppermute | solution.py:532
  198.8 4.2 collective-permute-done.10
  204.9 2.0 collective-permute-start.14
  206.9 40.6 %collective-permute-done.12.message = bf16[1040,1024]{1,0:T(8,128)(2,1)} collective-permute-done((bf16[1040,1024]{1,0:T(8,128)(2,1)}, bf16[1040,1024]{1,0:T(8,128)(2,1)}, u32[]{:S(2)}, u32[]{:S(2)}) %collective-permute-start.12) | collective-permute-done | bytes 2129952 | tf_op jit(solution)/shard_map/ppermute | solution.py:515
  250.0 2.0 collective-permute-start.17
  253.4 2.0 constant_dynamic-update-slice_fusion.4
  260.3 6.4 %unpack.4.refs_2_ = bf16[2,1024,1024]{2,1,0:T(8,128)(2,1)S(1)} custom-call(bf16[1040,1024]{1,0:T(8,128)(2,1)} %collective-permute-done.12.message), custom_call_target="tpu_custom_call" | custom-call | flops 4194304 | bytes 62914 | tf_op jit(solution)/shard_map/unpack/pallas_call | solution.py:173
  268.6 4.6 unpack.3.refs_1_
  273.2 2.0 copy-done.9
  275.2 4.6 unpack.5.refs_3_
  281.8 23.9 %rotate_part.1.part = f32[1024,1024]{1,0:T(8,128)S(1)} custom-call(s32[2]{0:T(128)S(1)} %pad_add_fusion.me_ref.at_ref, bf16[2,1024,1024]{2,1,0:T(8,128)(2,1)} %copy-done.11, bf16[2,1024,1024]{2,1,0:T(8,128)(2,1)} %copy-done.9, bf16[2,1024,1024]{2,1,0:T(8,128)(2,1)} %copy-done.8, bf16[2,1024,1024]{2,1,0:T(8,128)(2,1)} %copy-done.10, bf16[5120,1024]{1,0:T(8,128)(2,1)} %copy-done.25), custom_call_target="tpu_custom_call" | custom-call | flops 171798688 | bytes 209715 | tf_op jit(solution)/shard_map/rotate_part/pallas_call | solution.py:197
  305.7 13.6 %rotate.1 = (f32[1024,1024]{1,0:T(8,128)}, f32[1024,1024]{1,0:T(8,128)}, bf16[2,1024,1024]{2,1,0:T(8,128)(2,1)S(1)}) custom-call(s32[2]{0:T(128)S(1)} %pad_add_fusion.me_ref.at_ref, f32[1024,1024]{1,0:T(8,128)S(1)} %rotate_part.1.part, bf16[1024,1024]{1,0:T(8,128)(2,1)S(1)} %collective-permute-done.16.above.refs_4_, ...), custom_call_target="tpu_custom_call" | custom-call | flops 42949672 | bytes 314572 | tf_op jit(solution)/shard_map/rotate/pallas_call | solution.py:268
  319.3 8.7 %restore.4 = (f32[2,1024,256]{2,1,0:T(8,128)S(1)}, f32[2,1024,256]{2,1,0:T(8,128)S(1)}) custom-call(s32[2]{0:T(128)S(1)} %pad_add_fusion.me_ref.at_ref, bf16[2,1024,1024]{2,1,0:T(8,128)(2,1)S(1)} %get-tuple-element.82.normed, bf16[5120,1024]{1,0:T(8,128)(2,1)} %copy-done.25, bf16[5120,1024]{1,0:T(8,128)(2,1)} %copy-done.25, bf16[5120,1024]{1,0:T(8,128)(2,1)} %copy-done.25, ...), custom_call_target="tpu_custom_call" | custom-call | flops 42949672 | bytes 83886 | tf_op jit(solution)/shard_map/restore/pallas_call | solution.py:334
  328.1 8.7 %restore.5 = (f32[2,1024,256]{2,1,0:T(8,128)S(1)}, f32[2,1024,256]{2,1,0:T(8,128)S(1)}) custom-call(s32[2]{0:T(128)S(1)} %pad_add_fusion.me_ref.at_ref, bf16[2,1024,1024]{2,1,0:T(8,128)(2,1)S(1)} %get-tuple-element.82.normed, bf16[5120,1024]{1,0:T(8,128)(2,1)} %copy-done.25, bf16[5120,1024]{1,0:T(8,128)(2,1)} %copy-done.25, bf16[5120,1024]{1,0:T(8,128)(2,1)} %copy-done.25, ...), custom_call_target="tpu_custom_call" | custom-call | flops 42949672 | bytes 83886 | tf_op jit(solution)/shard_map/restore/pallas_call | solution.py:334
  344.8 8.4 %collective-permute-done.19.refs_0_ = bf16[1040,256]{1,0:T(8,128)(2,1)S(1)} collective-permute-done((bf16[1040,256]{1,0:T(8,128)(2,1)S(1)}, bf16[1040,256]{1,0:T(8,128)(2,1)S(1)}, u32[]{:S(2)}, u32[]{:S(2)}) %collective-permute-start.19) | collective-permute-done | bytes 532512 | tf_op jit(solution)/shard_map/ppermute | solution.py:515
  354.8 9.3 %expand.4.refs_0_.refs_1_.block = f32[4096,256]{1,0:T(8,128)} custom-call(f32[2,1024,256]{2,1,0:T(8,128)S(1)} %copy-done.20, f32[2,1024,256]{2,1,0:T(8,128)S(1)} %copy-done.22, bf16[1040,256]{1,0:T(8,128)(2,1)S(1)} %collective-permute-done.19.refs_0_, bf16[4096,1024]{1,0:T(8,128)(2,1)} %bitcast.13), custom_call_target="tpu_custom_call" | custom-call | flops 42949672 | bytes 125829 | tf_op jit(solution)/shard_map/expand/pallas_call | solution.py:415
  364.1 2.2 copy-done
  369.7 9.3 %expand.5.refs_0_.refs_1_.block = f32[4096,256]{1,0:T(8,128)} custom-call(f32[2,1024,256]{2,1,0:T(8,128)S(1)} %get-tuple-element.78.keep, f32[2,1024,256]{2,1,0:T(8,128)S(1)} %copy-done.18, bf16[1040,256]{1,0:T(8,128)(2,1)S(1)} %collective-permute-done.21.refs_0_, bf16[4096,1024]{1,0:T(8,128)(2,1)} %bitcast.14), custom_call_target="tpu_custom_call" | custom-call | flops 42949672 | bytes 125829 | tf_op jit(solution)/shard_map/expand/pallas_call | solution.py:415
  379.0 2.2 copy-done.2
  382.9 8.9 %restore.7 = (f32[2,1024,256]{2,1,0:T(8,128)S(1)}, f32[2,1024,256]{2,1,0:T(8,128)S(1)}) custom-call(s32[2]{0:T(128)S(1)} %pad_add_fusion.me_ref.at_ref, bf16[2,1024,1024]{2,1,0:T(8,128)(2,1)S(1)} %get-tuple-element.82.normed, bf16[5120,1024]{1,0:T(8,128)(2,1)} %copy-done.25, bf16[5120,1024]{1,0:T(8,128)(2,1)} %copy-done.25, bf16[5120,1024]{1,0:T(8,128)(2,1)} %copy-done.25, ...), custom_call_target="tpu_custom_call" | custom-call | flops 42949672 | bytes 83886 | tf_op jit(solution)/shard_map/restore/pallas_call | solution.py:334
  392.0 8.7 %restore.6 = (f32[2,1024,256]{2,1,0:T(8,128)S(1)}, f32[2,1024,256]{2,1,0:T(8,128)S(1)}) custom-call(s32[2]{0:T(128)S(1)} %pad_add_fusion.me_ref.at_ref, bf16[2,1024,1024]{2,1,0:T(8,128)(2,1)S(1)} %get-tuple-element.82.normed, bf16[5120,1024]{1,0:T(8,128)(2,1)} %copy-done.25, bf16[5120,1024]{1,0:T(8,128)(2,1)} %copy-done.25, bf16[5120,1024]{1,0:T(8,128)(2,1)} %copy-done.25, ...), custom_call_target="tpu_custom_call" | custom-call | flops 42949672 | bytes 83886 | tf_op jit(solution)/shard_map/restore/pallas_call | solution.py:334
  401.2 3.2 collective-permute-start.44
  410.7 6.4 %collective-permute-done.44.refs_2_ = bf16[1040,256]{1,0:T(8,128)(2,1)S(1)} collective-permute-done((bf16[1040,256]{1,0:T(8,128)(2,1)}, bf16[1040,256]{1,0:T(8,128)(2,1)S(1)}, u32[]{:S(2)}, u32[]{:S(2)}) %collective-permute-start.44) | collective-permute-done | bytes 532512 | tf_op jit(solution)/shard_map/ppermute | solution.py:532
  417.9 3.8 hop.22
  422.5 4.3 collective-permute-start.46
  426.8 9.4 %expand.7.refs_0_.refs_1_.block = f32[4096,256]{1,0:T(8,128)} custom-call(f32[2,1024,256]{2,1,0:T(8,128)S(1)} %copy-done.14, f32[2,1024,256]{2,1,0:T(8,128)S(1)} %copy-done.16, bf16[1040,256]{1,0:T(8,128)(2,1)S(1)} %collective-permute-done.31.refs_0_, bf16[4096,1024]{1,0:T(8,128)(2,1)} %bitcast.15), custom_call_target="tpu_custom_call" | custom-call | flops 42949672 | bytes 125829 | tf_op jit(solution)/shard_map/expand/pallas_call | solution.py:415
  436.2 2.2 copy-done.4
  439.1 4.1 collective-permute-start.32
  443.9 9.4 %expand.6.refs_0_.refs_1_.block = f32[4096,256]{1,0:T(8,128)} custom-call(f32[2,1024,256]{2,1,0:T(8,128)S(1)} %get-tuple-element.83.keep, f32[2,1024,256]{2,1,0:T(8,128)S(1)} %collective-permute-done.22.mate, bf16[1040,256]{1,0:T(8,128)(2,1)S(1)} %collective-permute-done.23.refs_0_, bf16[4096,1024]{1,0:T(8,128)(2,1)} %bitcast.16), custom_call_target="tpu_custom_call" | custom-call | flops 42949672 | bytes 125829 | tf_op jit(solution)/shard_map/expand/pallas_call | solution.py:415
  453.3 2.2 copy-done.6
  459.9 3.0 hop.20
  464.9 3.0 hop.18
  467.9 5.1 collective-permute-start.34
  473.8 3.0 hop.23
  476.8 3.0 hop.15
  479.8 6.6 %collective-permute-start.26 = (bf16[1040,256]{1,0:T(8,128)(2,1)S(1)}, bf16[1040,256]{1,0:T(8,128)(2,1)S(1)}, u32[]{:S(2)}, u32[]{:S(2)}) collective-permute-start(bf16[1040,256]{1,0:T(8,128)(2,1)S(1)} %get-tuple-element.87), channel_id=1, source_target_pairs={{0,4},{4,8},{1,5},{5,9},{2,6},{6,10},{3,7},{7,11},{16,20},{20,24},... | collective-permute-start | bytes 1597448 | tf_op jit(solution)/shard_map/ppermute | solution.py:532
  487.1 5.1 collective-permute-start.48
  492.3 3.0 hop.21
  496.6 8.7 %collective-permute-start.42 = (bf16[1040,256]{1,0:T(8,128)(2,1)S(1)}, bf16[1040,256]{1,0:T(8,128)(2,1)S(1)}, u32[]{:S(2)}, u32[]{:S(2)}) collective-permute-start(bf16[1040,256]{1,0:T(8,128)(2,1)S(1)} %get-tuple-element.103), channel_id=1, source_target_pairs={{0,4},{4,8},{8,12},{1,5},{5,9},{9,13},{2,6},{6,10},{10,14},{3,7},{... | collective-permute-start | bytes 1597448 | tf_op jit(solution)/shard_map/ppermute | solution.py:532
  505.3 3.0 hop.19
  509.7 7.3 %collective-permute-start.36 = (bf16[1040,256]{1,0:T(8,128)(2,1)S(1)}, bf16[1040,256]{1,0:T(8,128)(2,1)S(1)}, u32[]{:S(2)}, u32[]{:S(2)}) collective-permute-start(bf16[1040,256]{1,0:T(8,128)(2,1)S(1)} %get-tuple-element.97), channel_id=1, source_target_pairs={{0,4},{4,8},{8,12},{1,5},{5,9},{9,13},{2,6},{6,10},{10,14},{3,7},{... | collective-permute-start | bytes 1597448 | tf_op jit(solution)/shard_map/ppermute | solution.py:532
  517.0 3.0 hop.16
  521.3 7.1 %collective-permute-start.28 = (bf16[1040,256]{1,0:T(8,128)(2,1)S(1)}, bf16[1040,256]{1,0:T(8,128)(2,1)S(1)}, u32[]{:S(2)}, u32[]{:S(2)}) collective-permute-start(bf16[1040,256]{1,0:T(8,128)(2,1)S(1)} %get-tuple-element.89), channel_id=1, source_target_pairs={{0,4},{4,8},{8,12},{1,5},{5,9},{9,13},{2,6},{6,10},{10,14},{3,7},{... | collective-permute-start | bytes 1597448 | tf_op jit(solution)/shard_map/ppermute | solution.py:532
  530.3 2.2 finish.4.refs_0_
  532.5 2.2 finish.5.refs_0_
  534.8 5.4 collective-permute-done.36.up
  540.1 2.2 finish.6.refs_0_
  542.4 6.1 %collective-permute-done.28.up = bf16[1040,256]{1,0:T(8,128)(2,1)S(1)} collective-permute-done((bf16[1040,256]{1,0:T(8,128)(2,1)S(1)}, bf16[1040,256]{1,0:T(8,128)(2,1)S(1)}, u32[]{:S(2)}, u32[]{:S(2)}) %collective-permute-start.28) | collective-permute-done | bytes 532512 | tf_op jit(solution)/shard_map/ppermute | solution.py:532
  548.5 2.2 finish.7
  (150 shorter events, 66.8 us)
Async XLA Ops:
  0.6 49.0 %collective-permute-start = (bf16[1024,1024]{1,0:T(8,128)(2,1)}, bf16[1024,1024]{1,0:T(8,128)(2,1)}, u32[]{:S(2)}, u32[]{:S(2)}) collective-permute-start(bf16[1024,1024]{1,0:T(8,128)(2,1)} %param.8), channel_id=1, source_target_pairs={{0,2},{1,3},{2,0},{3,1},{4,6},{5,7},{6,4},{7,5},{8,10},{9,11},{10,... | collective-permute-start | bytes 6291464 | tf_op jit(solution)/shard_map/ppermute | solution.py:515
  3.6 48.4 %collective-permute-start.3 = (bf16[1024,1024]{1,0:T(8,128)(2,1)}, bf16[1024,1024]{1,0:T(8,128)(2,1)S(1)}, u32[]{:S(2)}, u32[]{:S(2)}) collective-permute-start(bf16[1024,1024]{1,0:T(8,128)(2,1)} %refs_2_.1), channel_id=1, source_target_pairs={{0,4},{4,8},{8,12},{1,5},{5,9},{9,13},{2,6},{6,10},{10,14},{3,7},{... | collective-permute-start | bytes 6291464 | tf_op jit(solution)/shard_map/ppermute | solution.py:532
  7.2 49.0 %collective-permute-start.5 = (bf16[1024,1024]{1,0:T(8,128)(2,1)}, bf16[1024,1024]{1,0:T(8,128)(2,1)}, u32[]{:S(2)}, u32[]{:S(2)}) collective-permute-start(bf16[1024,1024]{1,0:T(8,128)(2,1)} %refs_2_.1), channel_id=1, source_target_pairs={{4,0},{8,4},{12,8},{5,1},{9,5},{13,9},{6,2},{10,6},{14,10},{7,3},{... | collective-permute-start | bytes 6291464 | tf_op jit(solution)/shard_map/ppermute | solution.py:535
  8.5 52.8 %collective-permute-start.1 = (bf16[1024,1024]{1,0:T(8,128)(2,1)}, bf16[1024,1024]{1,0:T(8,128)(2,1)}, u32[]{:S(2)}, u32[]{:S(2)}) collective-permute-start(bf16[1024,1024]{1,0:T(8,128)(2,1)} %param.8), channel_id=1, source_target_pairs={{0,1},{1,0},{2,3},{3,2},{4,5},{5,4},{6,7},{7,6},{8,9},{9,8},{10,11... | collective-permute-start | bytes 6291464 | tf_op jit(solution)/shard_map/ppermute | solution.py:515
  49.6 13.6 %collective-permute-start.2 = (bf16[1024,1024]{1,0:T(8,128)(2,1)}, bf16[1024,1024]{1,0:T(8,128)(2,1)}, u32[]{:S(2)}, u32[]{:S(2)}) collective-permute-start(bf16[1024,1024]{1,0:T(8,128)(2,1)} %collective-permute-done), channel_id=1, source_target_pairs={{0,1},{1,0},{2,3},{3,2},{4,5},{5,4},{6,7},{7,6},{8,9},{9,8},{10,11... | collective-permute-start | bytes 6291464 | tf_op jit(solution)/shard_map/ppermute | solution.py:515
  52.0 13.1 %collective-permute-start.4 = (bf16[1024,1024]{1,0:T(8,128)(2,1)S(1)}, bf16[1024,1024]{1,0:T(8,128)(2,1)}, u32[]{:S(2)}, u32[]{:S(2)}) collective-permute-start(bf16[1024,1024]{1,0:T(8,128)(2,1)S(1)} %collective-permute-done.3.refs_1_), channel_id=1, source_target_pairs={{4,8},{8,12},{5,9},{9,13},{6,10},{10,14},{7,11},{11,15},{20,24},{2... | collective-permute-start | bytes 6291464 | tf_op jit(solution)/shard_map/ppermute | solution.py:532
  56.3 49.4 %collective-permute-start.6 = (bf16[1024,1024]{1,0:T(8,128)(2,1)}, bf16[1024,1024]{1,0:T(8,128)(2,1)}, u32[]{:S(2)}, u32[]{:S(2)}) collective-permute-start(bf16[1024,1024]{1,0:T(8,128)(2,1)} %collective-permute-done.5.refs_3_), channel_id=1, source_target_pairs={{4,0},{8,4},{5,1},{9,5},{6,2},{10,6},{7,3},{11,7},{20,16},{24,20},... | collective-permute-start | bytes 6291464 | tf_op jit(solution)/shard_map/ppermute | solution.py:535
  105.7 18.2 %collective-permute-start.7 = (bf16[1024,1024]{1,0:T(8,128)(2,1)}, bf16[1024,1024]{1,0:T(8,128)(2,1)}, u32[]{:S(2)}, u32[]{:S(2)}) collective-permute-start(bf16[1024,1024]{1,0:T(8,128)(2,1)} %collective-permute-done.4.refs_0_), channel_id=1, source_target_pairs={{8,12},{9,13},{10,14},{11,15},{24,28},{25,29},{26,30},{27,31}} | collective-permute-start | bytes 6291464 | tf_op jit(solution)/shard_map/ppermute | solution.py:532
  107.8 47.6 %collective-permute-start.8 = (bf16[1024,1024]{1,0:T(8,128)(2,1)}, bf16[1024,1024]{1,0:T(8,128)(2,1)}, u32[]{:S(2)}, u32[]{:S(2)}) collective-permute-start(bf16[1024,1024]{1,0:T(8,128)(2,1)} %collective-permute-done.6.refs_4_), channel_id=1, source_target_pairs={{4,0},{5,1},{6,2},{7,3},{20,16},{21,17},{22,18},{23,19}} | collective-permute-start | bytes 6291464 | tf_op jit(solution)/shard_map/ppermute | solution.py:535
  109.1 46.3 %copy-start.28 = (bf16[1024,1024]{1,0:T(8,128)(2,1)S(1)}, bf16[1024,1024]{1,0:T(8,128)(2,1)}, u32[]{:S(2)}) copy-start(bf16[1024,1024]{1,0:T(8,128)(2,1)} %param.9) | copy-start | bytes 6291460
  155.3 43.5 %collective-permute-start.9 = (bf16[1024,1024]{1,0:T(8,128)(2,1)S(1)}, bf16[1024,1024]{1,0:T(8,128)(2,1)S(1)}, u32[]{:S(2)}, u32[]{:S(2)}) collective-permute-start(bf16[1024,1024]{1,0:T(8,128)(2,1)S(1)} %copy-done.28), channel_id=1, source_target_pairs={{0,4},{4,8},{8,12},{1,5},{5,9},{9,13},{2,6},{6,10},{10,14},{3,7},{... | collective-permute-start | bytes 6291464 | tf_op jit(solution)/shard_map/ppermute | solution.py:532
  156.9 46.2 %collective-permute-start.10 = (bf16[1024,1024]{1,0:T(8,128)(2,1)S(1)}, bf16[1024,1024]{1,0:T(8,128)(2,1)S(1)}, u32[]{:S(2)}, u32[]{:S(2)}) collective-permute-start(bf16[1024,1024]{1,0:T(8,128)(2,1)S(1)} %copy-done.28), channel_id=1, source_target_pairs={{4,0},{8,4},{12,8},{5,1},{9,5},{13,9},{6,2},{10,6},{14,10},{7,3},{... | collective-permute-start | bytes 6291464 | tf_op jit(solution)/shard_map/ppermute | solution.py:535
  198.8 48.6 %copy-start.29 = (bf16[1024,1024]{1,0:T(8,128)(2,1)}, bf16[1024,1024]{1,0:T(8,128)(2,1)S(1)}, u32[]{:S(2)}) copy-start(bf16[1024,1024]{1,0:T(8,128)(2,1)S(1)} %collective-permute-done.9) | copy-start | bytes 6291460
  203.1 46.9 %copy-start.31 = (bf16[1024,1024]{1,0:T(8,128)(2,1)}, bf16[1024,1024]{1,0:T(8,128)(2,1)S(1)}, u32[]{:S(2)}) copy-start(bf16[1024,1024]{1,0:T(8,128)(2,1)S(1)} %collective-permute-done.10) | copy-start | bytes 6291460
  203.1 44.4 %collective-permute-start.12 = (bf16[1040,1024]{1,0:T(8,128)(2,1)}, bf16[1040,1024]{1,0:T(8,128)(2,1)}, u32[]{:S(2)}, u32[]{:S(2)}) collective-permute-start(bf16[1040,1024]{1,0:T(8,128)(2,1)} %get-tuple-element.66), channel_id=1, source_target_pairs={{0,2},{1,3},{2,0},{3,1},{4,6},{5,7},{6,4},{7,5},{8,10},{9,11},{10,... | collective-permute-start | bytes 6389768 | tf_op jit(solution)/shard_map/ppermute | solution.py:515
  203.6 45.1 %collective-permute-start.15 = (bf16[1024,1024]{1,0:T(8,128)(2,1)S(1)}, bf16[1024,1024]{1,0:T(8,128)(2,1)}, u32[]{:S(2)}, u32[]{:S(2)}) collective-permute-start(bf16[1024,1024]{1,0:T(8,128)(2,1)S(1)} %collective-permute-done.10), channel_id=1, source_target_pairs={{4,0},{8,4},{5,1},{9,5},{6,2},{10,6},{7,3},{11,7},{20,16},{24,20},... | collective-permute-start | bytes 6291464 | tf_op jit(solution)/shard_map/ppermute | solution.py:535
  204.9 45.1 %collective-permute-start.14 = (bf16[1024,1024]{1,0:T(8,128)(2,1)S(1)}, bf16[1024,1024]{1,0:T(8,128)(2,1)}, u32[]{:S(2)}, u32[]{:S(2)}) collective-permute-start(bf16[1024,1024]{1,0:T(8,128)(2,1)S(1)} %collective-permute-done.9), channel_id=1, source_target_pairs={{4,8},{8,12},{5,9},{9,13},{6,10},{10,14},{7,11},{11,15},{20,24},{2... | collective-permute-start | bytes 6291464 | tf_op jit(solution)/shard_map/ppermute | solution.py:532
  206.9 61.7 %collective-permute-start.11 = (bf16[1040,1024]{1,0:T(8,128)(2,1)}, bf16[1040,1024]{1,0:T(8,128)(2,1)}, u32[]{:S(2)}, u32[]{:S(2)}) collective-permute-start(bf16[1040,1024]{1,0:T(8,128)(2,1)} %get-tuple-element.66), channel_id=1, source_target_pairs={{0,1},{1,0},{2,3},{3,2},{4,5},{5,4},{6,7},{7,6},{8,9},{9,8},{10,11... | collective-permute-start | bytes 6389768 | tf_op jit(solution)/shard_map/ppermute | solution.py:515
  247.5 27.8 %collective-permute-start.13 = (bf16[1040,1024]{1,0:T(8,128)(2,1)}, bf16[1040,1024]{1,0:T(8,128)(2,1)}, u32[]{:S(2)}, u32[]{:S(2)}) collective-permute-start(bf16[1040,1024]{1,0:T(8,128)(2,1)} %collective-permute-done.12.message), channel_id=1, source_target_pairs={{0,1},{1,0},{2,3},{3,2},{4,5},{5,4},{6,7},{7,6},{8,9},{9,8},{10,11... | collective-permute-start | bytes 6389768 | tf_op jit(solution)/shard_map/ppermute | solution.py:515
  248.7 57.0 %collective-permute-start.16 = (bf16[1024,1024]{1,0:T(8,128)(2,1)}, bf16[1024,1024]{1,0:T(8,128)(2,1)S(1)}, u32[]{:S(2)}, u32[]{:S(2)}) collective-permute-start(bf16[1024,1024]{1,0:T(8,128)(2,1)} %collective-permute-done.15), channel_id=1, source_target_pairs={{4,0},{5,1},{6,2},{7,3},{20,16},{21,17},{22,18},{23,19}} | collective-permute-start | bytes 6291464 | tf_op jit(solution)/shard_map/ppermute | solution.py:535
  250.0 55.7 %collective-permute-start.17 = (bf16[1024,1024]{1,0:T(8,128)(2,1)}, bf16[1024,1024]{1,0:T(8,128)(2,1)}, u32[]{:S(2)}, u32[]{:S(2)}) collective-permute-start(bf16[1024,1024]{1,0:T(8,128)(2,1)} %collective-permute-done.14), channel_id=1, source_target_pairs={{8,12},{9,13},{10,14},{11,15},{24,28},{25,29},{26,30},{27,31}} | collective-permute-start | bytes 6291464 | tf_op jit(solution)/shard_map/ppermute | solution.py:532
  260.3 19.6 %copy-start.25 = (bf16[5120,1024]{1,0:T(8,128)(2,1)}, bf16[5120,1024]{1,0:T(8,128)(2,1)S(1)}, u32[]{:S(2)}) copy-start(bf16[5120,1024]{1,0:T(8,128)(2,1)S(1)} %constant_dynamic-update-slice_fusion.refs_4_.refs_0_.refs_1_.refs_2_.refs_3_) | copy-start | bytes 31457284
  328.0 9.4 %copy-start.19 = (f32[2,1024,256]{2,1,0:T(8,128)}, f32[2,1024,256]{2,1,0:T(8,128)S(1)}, u32[]{:S(2)}) copy-start(f32[2,1024,256]{2,1,0:T(8,128)S(1)} %get-tuple-element.73.keep) | copy-start | bytes 6291460
  328.0 9.4 %collective-permute-start.18 = (f32[2,1024,256]{2,1,0:T(8,128)S(1)}, f32[2,1024,256]{2,1,0:T(8,128)S(1)}, u32[]{:S(2)}, u32[]{:S(2)}) collective-permute-start(f32[2,1024,256]{2,1,0:T(8,128)S(1)} %get-tuple-element.74), channel_id=1, source_target_pairs={{0,1},{1,0},{2,3},{3,2},{4,5},{5,4},{6,7},{7,6},{8,9},{9,8},{10,11... | collective-permute-start | bytes 6291464 | tf_op jit(solution)/shard_map/ppermute | solution.py:515
  336.8 4.3 collective-permute-start.20
  337.4 4.6 copy-start.21
  338.2 15.0 %copy-start.20 = (f32[2,1024,256]{2,1,0:T(8,128)S(1)}, f32[2,1024,256]{2,1,0:T(8,128)}, u32[]{:S(2)}) copy-start(f32[2,1024,256]{2,1,0:T(8,128)} %copy-done.19) | copy-start | bytes 6291460
  338.2 15.0 %collective-permute-start.19 = (bf16[1040,256]{1,0:T(8,128)(2,1)S(1)}, bf16[1040,256]{1,0:T(8,128)(2,1)S(1)}, u32[]{:S(2)}, u32[]{:S(2)}) collective-permute-start(bf16[1040,256]{1,0:T(8,128)(2,1)S(1)} %send.4), channel_id=1, source_target_pairs={{0,2},{1,3},{2,0},{3,1},{4,6},{5,7},{6,4},{7,5},{8,10},{9,11},{10,... | collective-permute-start | bytes 1597448 | tf_op jit(solution)/shard_map/ppermute | solution.py:515
  343.3 24.7 %collective-permute-start.21 = (bf16[1040,256]{1,0:T(8,128)(2,1)S(1)}, bf16[1040,256]{1,0:T(8,128)(2,1)S(1)}, u32[]{:S(2)}, u32[]{:S(2)}) collective-permute-start(bf16[1040,256]{1,0:T(8,128)(2,1)S(1)} %send.5), channel_id=1, source_target_pairs={{0,2},{1,3},{2,0},{3,1},{4,6},{5,7},{6,4},{7,5},{8,10},{9,11},{10,... | collective-permute-start | bytes 1597448 | tf_op jit(solution)/shard_map/ppermute | solution.py:515
  391.9 13.3 %copy-start.13 = (f32[2,1024,256]{2,1,0:T(8,128)}, f32[2,1024,256]{2,1,0:T(8,128)S(1)}, u32[]{:S(2)}) copy-start(f32[2,1024,256]{2,1,0:T(8,128)S(1)} %get-tuple-element.91.keep) | copy-start | bytes 6291460
  391.9 13.2 %collective-permute-start.30 = (f32[2,1024,256]{2,1,0:T(8,128)S(1)}, f32[2,1024,256]{2,1,0:T(8,128)S(1)}, u32[]{:S(2)}, u32[]{:S(2)}) collective-permute-start(f32[2,1024,256]{2,1,0:T(8,128)S(1)} %get-tuple-element.92), channel_id=1, source_target_pairs={{0,1},{1,0},{2,3},{3,2},{4,5},{5,4},{6,7},{7,6},{8,9},{9,8},{10,11... | collective-permute-start | bytes 6291464 | tf_op jit(solution)/shard_map/ppermute | solution.py:515
  400.7 6.8 %collective-permute-start.22 = (f32[2,1024,256]{2,1,0:T(8,128)S(1)}, f32[2,1024,256]{2,1,0:T(8,128)S(1)}, u32[]{:S(2)}, u32[]{:S(2)}) collective-permute-start(f32[2,1024,256]{2,1,0:T(8,128)S(1)} %get-tuple-element.84), channel_id=1, source_target_pairs={{0,1},{1,0},{2,3},{3,2},{4,5},{5,4},{6,7},{7,6},{8,9},{9,8},{10,11... | collective-permute-start | bytes 6291464 | tf_op jit(solution)/shard_map/ppermute | solution.py:515
  401.2 15.9 %collective-permute-start.44 = (bf16[1040,256]{1,0:T(8,128)(2,1)}, bf16[1040,256]{1,0:T(8,128)(2,1)S(1)}, u32[]{:S(2)}, u32[]{:S(2)}) collective-permute-start(bf16[1040,256]{1,0:T(8,128)(2,1)} %get-tuple-element.105), channel_id=1, source_target_pairs={{0,4},{1,5},{2,6},{3,7},{16,20},{17,21},{18,22},{19,23}} | collective-permute-start | bytes 1597448 | tf_op jit(solution)/shard_map/ppermute | solution.py:532
  404.4 13.4 %collective-permute-start.45 = (bf16[1040,256]{1,0:T(8,128)(2,1)}, bf16[1040,256]{1,0:T(8,128)(2,1)S(1)}, u32[]{:S(2)}, u32[]{:S(2)}) collective-permute-start(bf16[1040,256]{1,0:T(8,128)(2,1)} %get-tuple-element.106), channel_id=1, source_target_pairs={{12,8},{13,9},{14,10},{15,11},{28,24},{29,25},{30,26},{31,27}} | collective-permute-start | bytes 1597448 | tf_op jit(solution)/shard_map/ppermute | solution.py:535
  406.0 20.8 %collective-permute-start.31 = (bf16[1040,256]{1,0:T(8,128)(2,1)S(1)}, bf16[1040,256]{1,0:T(8,128)(2,1)S(1)}, u32[]{:S(2)}, u32[]{:S(2)}) collective-permute-start(bf16[1040,256]{1,0:T(8,128)(2,1)S(1)} %send.7), channel_id=1, source_target_pairs={{0,2},{1,3},{2,0},{3,1},{4,6},{5,7},{6,4},{7,5},{8,10},{9,11},{10,... | collective-permute-start | bytes 1597448 | tf_op jit(solution)/shard_map/ppermute | solution.py:515
  408.4 18.4 %copy-start.14 = (f32[2,1024,256]{2,1,0:T(8,128)S(1)}, f32[2,1024,256]{2,1,0:T(8,128)}, u32[]{:S(2)}) copy-start(f32[2,1024,256]{2,1,0:T(8,128)} %copy-done.13) | copy-start | bytes 6291460
  408.4 34.8 %collective-permute-start.23 = (bf16[1040,256]{1,0:T(8,128)(2,1)S(1)}, bf16[1040,256]{1,0:T(8,128)(2,1)S(1)}, u32[]{:S(2)}, u32[]{:S(2)}) collective-permute-start(bf16[1040,256]{1,0:T(8,128)(2,1)S(1)} %send.6), channel_id=1, source_target_pairs={{0,2},{1,3},{2,0},{3,1},{4,6},{5,7},{6,4},{7,5},{8,10},{9,11},{10,... | collective-permute-start | bytes 1597448 | tf_op jit(solution)/shard_map/ppermute | solution.py:515
  409.0 17.8 %copy-start.16 = (f32[2,1024,256]{2,1,0:T(8,128)S(1)}, f32[2,1024,256]{2,1,0:T(8,128)}, u32[]{:S(2)}) copy-start(f32[2,1024,256]{2,1,0:T(8,128)} %copy-done.15) | copy-start | bytes 6291460
  409.0 47.3 %collective-permute-start.38 = (bf16[1040,256]{1,0:T(8,128)(2,1)}, bf16[1040,256]{1,0:T(8,128)(2,1)S(1)}, u32[]{:S(2)}, u32[]{:S(2)}) collective-permute-start(bf16[1040,256]{1,0:T(8,128)(2,1)} %get-tuple-element.99), channel_id=1, source_target_pairs={{0,4},{1,5},{2,6},{3,7},{16,20},{17,21},{18,22},{19,23}} | collective-permute-start | bytes 1597448 | tf_op jit(solution)/shard_map/ppermute | solution.py:532
  417.2 40.1 %collective-permute-start.39 = (bf16[1040,256]{1,0:T(8,128)(2,1)}, bf16[1040,256]{1,0:T(8,128)(2,1)S(1)}, u32[]{:S(2)}, u32[]{:S(2)}) collective-permute-start(bf16[1040,256]{1,0:T(8,128)(2,1)} %get-tuple-element.100), channel_id=1, source_target_pairs={{12,8},{13,9},{14,10},{15,11},{28,24},{29,25},{30,26},{31,27}} | collective-permute-start | bytes 1597448 | tf_op jit(solution)/shard_map/ppermute | solution.py:535
  422.5 36.7 %collective-permute-start.46 = (bf16[1040,256]{1,0:T(8,128)(2,1)}, bf16[1040,256]{1,0:T(8,128)(2,1)S(1)}, u32[]{:S(2)}, u32[]{:S(2)}) collective-permute-start(bf16[1040,256]{1,0:T(8,128)(2,1)} %get-tuple-element.107), channel_id=1, source_target_pairs={{0,4},{4,8},{1,5},{5,9},{2,6},{6,10},{3,7},{7,11},{16,20},{20,24},... | collective-permute-start | bytes 1597448 | tf_op jit(solution)/shard_map/ppermute | solution.py:532
  439.1 23.7 %collective-permute-start.32 = (bf16[1040,256]{1,0:T(8,128)(2,1)S(1)}, bf16[1040,256]{1,0:T(8,128)(2,1)S(1)}, u32[]{:S(2)}, u32[]{:S(2)}) collective-permute-start(bf16[1040,256]{1,0:T(8,128)(2,1)S(1)} %get-tuple-element.93), channel_id=1, source_target_pairs={{0,4},{1,5},{2,6},{3,7},{16,20},{17,21},{18,22},{19,23}} | collective-permute-start | bytes 1597448 | tf_op jit(solution)/shard_map/ppermute | solution.py:532
  443.2 21.0 %collective-permute-start.33 = (bf16[1040,256]{1,0:T(8,128)(2,1)S(1)}, bf16[1040,256]{1,0:T(8,128)(2,1)S(1)}, u32[]{:S(2)}, u32[]{:S(2)}) collective-permute-start(bf16[1040,256]{1,0:T(8,128)(2,1)S(1)} %get-tuple-element.94), channel_id=1, source_target_pairs={{12,8},{13,9},{14,10},{15,11},{28,24},{29,25},{30,26},{31,27}} | collective-permute-start | bytes 1597448 | tf_op jit(solution)/shard_map/ppermute | solution.py:535
  456.5 11.4 %collective-permute-start.47 = (bf16[1040,256]{1,0:T(8,128)(2,1)S(1)}, bf16[1040,256]{1,0:T(8,128)(2,1)S(1)}, u32[]{:S(2)}, u32[]{:S(2)}) collective-permute-start(bf16[1040,256]{1,0:T(8,128)(2,1)S(1)} %copy-done.24), channel_id=1, source_target_pairs={{8,4},{12,8},{9,5},{13,9},{10,6},{14,10},{11,7},{15,11},{24,20},{2... | collective-permute-start | bytes 1597448 | tf_op jit(solution)/shard_map/ppermute | solution.py:535
  457.2 15.8 %collective-permute-start.24 = (bf16[1040,256]{1,0:T(8,128)(2,1)S(1)}, bf16[1040,256]{1,0:T(8,128)(2,1)S(1)}, u32[]{:S(2)}, u32[]{:S(2)}) collective-permute-start(bf16[1040,256]{1,0:T(8,128)(2,1)S(1)} %get-tuple-element.85), channel_id=1, source_target_pairs={{0,4},{1,5},{2,6},{3,7},{16,20},{17,21},{18,22},{19,23}} | collective-permute-start | bytes 1597448 | tf_op jit(solution)/shard_map/ppermute | solution.py:532
  459.2 17.6 %collective-permute-start.25 = (bf16[1040,256]{1,0:T(8,128)(2,1)S(1)}, bf16[1040,256]{1,0:T(8,128)(2,1)S(1)}, u32[]{:S(2)}, u32[]{:S(2)}) collective-permute-start(bf16[1040,256]{1,0:T(8,128)(2,1)S(1)} %get-tuple-element.86), channel_id=1, source_target_pairs={{12,8},{13,9},{14,10},{15,11},{28,24},{29,25},{30,26},{31,27}} | collective-permute-start | bytes 1597448 | tf_op jit(solution)/shard_map/ppermute | solution.py:535
  462.9 23.5 %collective-permute-start.40 = (bf16[1040,256]{1,0:T(8,128)(2,1)S(1)}, bf16[1040,256]{1,0:T(8,128)(2,1)S(1)}, u32[]{:S(2)}, u32[]{:S(2)}) collective-permute-start(bf16[1040,256]{1,0:T(8,128)(2,1)S(1)} %get-tuple-element.101), channel_id=1, source_target_pairs={{0,4},{4,8},{1,5},{5,9},{2,6},{6,10},{3,7},{7,11},{16,20},{20,24},... | collective-permute-start | bytes 1597448 | tf_op jit(solution)/shard_map/ppermute | solution.py:532
  464.2 22.9 %collective-permute-start.41 = (bf16[1040,256]{1,0:T(8,128)(2,1)S(1)}, bf16[1040,256]{1,0:T(8,128)(2,1)S(1)}, u32[]{:S(2)}, u32[]{:S(2)}) collective-permute-start(bf16[1040,256]{1,0:T(8,128)(2,1)S(1)} %get-tuple-element.102), channel_id=1, source_target_pairs={{8,4},{12,8},{9,5},{13,9},{10,6},{14,10},{11,7},{15,11},{24,20},{2... | collective-permute-start | bytes 1597448 | tf_op jit(solution)/shard_map/ppermute | solution.py:535
  467.9 27.4 %collective-permute-start.34 = (bf16[1040,256]{1,0:T(8,128)(2,1)S(1)}, bf16[1040,256]{1,0:T(8,128)(2,1)S(1)}, u32[]{:S(2)}, u32[]{:S(2)}) collective-permute-start(bf16[1040,256]{1,0:T(8,128)(2,1)S(1)} %get-tuple-element.95), channel_id=1, source_target_pairs={{0,4},{4,8},{1,5},{5,9},{2,6},{6,10},{3,7},{7,11},{16,20},{20,24},... | collective-permute-start | bytes 1597448 | tf_op jit(solution)/shard_map/ppermute | solution.py:532
  473.1 23.5 %collective-permute-start.35 = (bf16[1040,256]{1,0:T(8,128)(2,1)S(1)}, bf16[1040,256]{1,0:T(8,128)(2,1)S(1)}, u32[]{:S(2)}, u32[]{:S(2)}) collective-permute-start(bf16[1040,256]{1,0:T(8,128)(2,1)S(1)} %get-tuple-element.96), channel_id=1, source_target_pairs={{8,4},{12,8},{9,5},{13,9},{10,6},{14,10},{11,7},{15,11},{24,20},{2... | collective-permute-start | bytes 1597448 | tf_op jit(solution)/shard_map/ppermute | solution.py:535
  479.8 28.5 %collective-permute-start.26 = (bf16[1040,256]{1,0:T(8,128)(2,1)S(1)}, bf16[1040,256]{1,0:T(8,128)(2,1)S(1)}, u32[]{:S(2)}, u32[]{:S(2)}) collective-permute-start(bf16[1040,256]{1,0:T(8,128)(2,1)S(1)} %get-tuple-element.87), channel_id=1, source_target_pairs={{0,4},{4,8},{1,5},{5,9},{2,6},{6,10},{3,7},{7,11},{16,20},{20,24},... | collective-permute-start | bytes 1597448 | tf_op jit(solution)/shard_map/ppermute | solution.py:532
  486.4 23.2 %collective-permute-start.27 = (bf16[1040,256]{1,0:T(8,128)(2,1)S(1)}, bf16[1040,256]{1,0:T(8,128)(2,1)S(1)}, u32[]{:S(2)}, u32[]{:S(2)}) collective-permute-start(bf16[1040,256]{1,0:T(8,128)(2,1)S(1)} %get-tuple-element.88), channel_id=1, source_target_pairs={{8,4},{12,8},{9,5},{13,9},{10,6},{14,10},{11,7},{15,11},{24,20},{2... | collective-permute-start | bytes 1597448 | tf_op jit(solution)/shard_map/ppermute | solution.py:535
  487.1 32.9 %collective-permute-start.48 = (bf16[1040,256]{1,0:T(8,128)(2,1)S(1)}, bf16[1040,256]{1,0:T(8,128)(2,1)S(1)}, u32[]{:S(2)}, u32[]{:S(2)}) collective-permute-start(bf16[1040,256]{1,0:T(8,128)(2,1)S(1)} %get-tuple-element.109), channel_id=1, source_target_pairs={{0,4},{4,8},{8,12},{1,5},{5,9},{9,13},{2,6},{6,10},{10,14},{3,7},{... | collective-permute-start | bytes 1597448 | tf_op jit(solution)/shard_map/ppermute | solution.py:532
  495.3 26.0 %collective-permute-start.49 = (bf16[1040,256]{1,0:T(8,128)(2,1)S(1)}, bf16[1040,256]{1,0:T(8,128)(2,1)S(1)}, u32[]{:S(2)}, u32[]{:S(2)}) collective-permute-start(bf16[1040,256]{1,0:T(8,128)(2,1)S(1)} %get-tuple-element.110), channel_id=1, source_target_pairs={{4,0},{8,4},{12,8},{5,1},{9,5},{13,9},{6,2},{10,6},{14,10},{7,3},{... | collective-permute-start | bytes 1597448 | tf_op jit(solution)/shard_map/ppermute | solution.py:535
  496.6 32.1 %collective-permute-start.42 = (bf16[1040,256]{1,0:T(8,128)(2,1)S(1)}, bf16[1040,256]{1,0:T(8,128)(2,1)S(1)}, u32[]{:S(2)}, u32[]{:S(2)}) collective-permute-start(bf16[1040,256]{1,0:T(8,128)(2,1)S(1)} %get-tuple-element.103), channel_id=1, source_target_pairs={{0,4},{4,8},{8,12},{1,5},{5,9},{9,13},{2,6},{6,10},{10,14},{3,7},{... | collective-permute-start | bytes 1597448 | tf_op jit(solution)/shard_map/ppermute | solution.py:532
  508.3 24.2 %collective-permute-start.43 = (bf16[1040,256]{1,0:T(8,128)(2,1)S(1)}, bf16[1040,256]{1,0:T(8,128)(2,1)S(1)}, u32[]{:S(2)}, u32[]{:S(2)}) collective-permute-start(bf16[1040,256]{1,0:T(8,128)(2,1)S(1)} %get-tuple-element.104), channel_id=1, source_target_pairs={{4,0},{8,4},{12,8},{5,1},{9,5},{13,9},{6,2},{10,6},{14,10},{7,3},{... | collective-permute-start | bytes 1597448 | tf_op jit(solution)/shard_map/ppermute | solution.py:535
  509.6 20.6 %copy-start.1 = (f32[4096,256]{1,0:T(8,128)S(1)}, f32[4096,256]{1,0:T(8,128)}, u32[]{:S(2)}) copy-start(f32[4096,256]{1,0:T(8,128)} %expand.4.refs_0_.refs_1_.block) | copy-start | bytes 12582916
  509.7 30.5 %collective-permute-start.36 = (bf16[1040,256]{1,0:T(8,128)(2,1)S(1)}, bf16[1040,256]{1,0:T(8,128)(2,1)S(1)}, u32[]{:S(2)}, u32[]{:S(2)}) collective-permute-start(bf16[1040,256]{1,0:T(8,128)(2,1)S(1)} %get-tuple-element.97), channel_id=1, source_target_pairs={{0,4},{4,8},{8,12},{1,5},{5,9},{9,13},{2,6},{6,10},{10,14},{3,7},{... | collective-permute-start | bytes 1597448 | tf_op jit(solution)/shard_map/ppermute | solution.py:532
  520.0 20.1 %collective-permute-start.37 = (bf16[1040,256]{1,0:T(8,128)(2,1)S(1)}, bf16[1040,256]{1,0:T(8,128)(2,1)S(1)}, u32[]{:S(2)}, u32[]{:S(2)}) collective-permute-start(bf16[1040,256]{1,0:T(8,128)(2,1)S(1)} %get-tuple-element.98), channel_id=1, source_target_pairs={{4,0},{8,4},{12,8},{5,1},{9,5},{13,9},{6,2},{10,6},{14,10},{7,3},{... | collective-permute-start | bytes 1597448 | tf_op jit(solution)/shard_map/ppermute | solution.py:535
  521.3 27.1 %collective-permute-start.28 = (bf16[1040,256]{1,0:T(8,128)(2,1)S(1)}, bf16[1040,256]{1,0:T(8,128)(2,1)S(1)}, u32[]{:S(2)}, u32[]{:S(2)}) collective-permute-start(bf16[1040,256]{1,0:T(8,128)(2,1)S(1)} %get-tuple-element.89), channel_id=1, source_target_pairs={{0,4},{4,8},{8,12},{1,5},{5,9},{9,13},{2,6},{6,10},{10,14},{3,7},{... | collective-permute-start | bytes 1597448 | tf_op jit(solution)/shard_map/ppermute | solution.py:532
  528.7 3.8 copy-start.3
  528.7 19.7 %collective-permute-start.29 = (bf16[1040,256]{1,0:T(8,128)(2,1)S(1)}, bf16[1040,256]{1,0:T(8,128)(2,1)S(1)}, u32[]{:S(2)}, u32[]{:S(2)}) collective-permute-start(bf16[1040,256]{1,0:T(8,128)(2,1)S(1)} %get-tuple-element.90), channel_id=1, source_target_pairs={{4,0},{8,4},{12,8},{5,1},{9,5},{13,9},{6,2},{10,6},{14,10},{7,3},{... | collective-permute-start | bytes 1597448 | tf_op jit(solution)/shard_map/ppermute | solution.py:535
  532.5 7.6 %copy-start.5 = (f32[4096,256]{1,0:T(8,128)S(1)}, f32[4096,256]{1,0:T(8,128)}, u32[]{:S(2)}) copy-start(f32[4096,256]{1,0:T(8,128)} %expand.7.refs_0_.refs_1_.block) | copy-start | bytes 12582916
  534.7 13.7 %copy-start.7 = (f32[4096,256]{1,0:T(8,128)S(1)}, f32[4096,256]{1,0:T(8,128)}, u32[]{:S(2)}) copy-start(f32[4096,256]{1,0:T(8,128)} %expand.6.refs_0_.refs_1_.block) | copy-start | bytes 12582916
  (19 other events, 38.4 us)

commit v8 on v7

--- a/solution.py
+++ b/solution.py
@@ -154,9 +154,9 @@
     )(value)
 
 
-def unpack_kernel(message, pair, *, tile):
+def unpack_kernel(message, scales, pair, *, tile):
     _, depth, _ = pair.shape
-    scale = scale_of(message, depth)
+    scale = scale_of(scales, 0)
 
     def put(i, carry):
         rows = pl.ds(pl.multiple_of(i * tile, tile), tile)
@@ -170,13 +170,20 @@
 
 def unpack(message):
     depth, width = message.shape[0] - EXTRA, message.shape[1]
-    return pl.pallas_call(
-        functools.partial(unpack_kernel, tile=min(16, depth)),
+    step = min(256, depth)
+    return pl.pallas_call(
+        functools.partial(unpack_kernel, tile=min(16, step)),
+        grid=(depth // step,),
+        in_specs=[
+            pl.BlockSpec((step, width), lambda i: (i, 0)),
+            pl.BlockSpec((EXTRA, width), lambda i: (depth // EXTRA, 0)),
+        ],
+        out_specs=pl.BlockSpec((2, step, width), lambda i: (0, i, 0)),
         out_shape=jax.ShapeDtypeStruct((2, depth, width), BF16),
-        compiler_params=params(32),
+        compiler_params=params(60),
         cost_estimate=cost(400 * depth * width, 6 * depth * width),
         name="unpack",
-    )(message)
+    )(message, message)
 
 
 def rotate_part_kernel(me_ref, *refs, cols, width):
@@ -568,16 +575,17 @@
             there = jnp.where((there >= 0) & (there < lines), there, lines)
             return lax.dynamic_update_slice_in_dim(right, rights[offset], there * depth, 0)
 
-        right = put(right, 0)
         for step in range(1, lines):
             walk(rights, step)
-            if step < far or depth != width:
-                right = put(put(right, -step), step)
         above, below = rights[far], rights[-far]
 
         pair, message = pack(halfway(spot, left, grads, [-far, far], lines, before))
         message, rights[-1], rights[1] = barrier((message, rights[-1], rights[1]))
         pieces = by_distance(message)
+        right = put(put(put(right, 0), -1), 1)
+        right, pieces[cols - 2] = barrier((right, pieces[cols - 2]))
+        for step in range(2, far if depth == width else lines):
+            right = put(put(right, -step), step)
         pieces = [pair] + [unpack(pieces[distance]) for distance in range(1, cols)]
         part = rotate_part(at, pieces, right)
         part, above, below = barrier((part, above, below))
@@ -589,27 +597,29 @@
             at, part, pieces, above_now, below_now, first_moment, second_moment, lines
         )
 
-        products, hops = [], []
+        def pass_on(product, arrived, step):
+            upward, downward = hop(spot, product, arrived, lines, step)
+            return up(upward, range(0, step)), down(downward, range(lines - step, lines))
+
+        products, arrived = [], []
         for chunk in range(CHUNKS):
             if chunk >= 2:
-                normed, hops[chunk - 2] = barrier((normed, hops[chunk - 2]))
+                step = chunk - 1
+                if step > 1 and step < lines:
+                    arrived[0] = pass_on(products[0], arrived[0], step)
+                normed, arrived[0] = barrier((normed, arrived[0]))
             keep, mate = restore(at, normed, right, above, below, cols, lines, chunk, piece)
             mate = swap(mate, 1)
             crossed = [
                 swap(send(keep, mate, distance, []), distance) for distance in range(2, cols, 2)
             ]
             products.append(expand(keep, mate, crossed, left))
-            hops.append(hop(spot, products[chunk], (), lines, 1))
-        arrived = [()] * CHUNKS
-        for step in range(1, lines):
+            arrived.append(pass_on(products[chunk], (), 1))
+        for step in range(2, lines):
             for chunk, product in enumerate(products):
-                if step > 1:
-                    hops[chunk] = hop(spot, product, arrived[chunk], lines, step)
-                upward, downward = hops[chunk]
-                arrived[chunk] = (
-                    up(upward, range(0, step)),
-                    down(downward, range(lines - step, lines)),
-                )
+                if chunk == 0 and step < CHUNKS - 1:
+                    continue
+                arrived[chunk] = pass_on(product, arrived[chunk], step)
         update = None
         for chunk, product in enumerate(products):
             update = finish(spot, product, arrived[chunk], update, chunk, depth, width)

time: 560 us -> 579 us (1.034); the launches traced: 551 us -> 576 us
  waiting for transfers between devices: 211 us -> 237 us
    ppermute x18, waiting for transfers between devices: 76.6 us -> 95.2 us  [down(): return lax.ppermute(value, 'row', [(i, i - 1) for i in senders])]
    ppermute x14, waiting for transfers between devices: 91.4 us -> 106 us  [swap(): return lax.ppermute(value, 'col', [(i, i ^ distance) for i in range(cols)])]
    unnamed x66 -> x52, local copies, waits for them, and re-layouts: 28.8 us -> 17.6 us
    ppermute x18, waiting for transfers between devices: 43.1 us -> 35.4 us  [up(): return lax.ppermute(value, 'row', [(i, i + 1) for i in senders])]
  transfers between devices with their start and end apart: 50 -> 50, of which waited for: 15 -> 20; matrix products, arithmetic and copies ran while one was open for 3% -> 4% of each run, Pallas kernels for 27% -> 28%
where the time goes in v8:
time: 579 us; the launch traced here: 576 us
  waiting for transfers between devices  237 us (41%)
  Pallas kernels  201 us (35%)
  starting transfers between devices  95.7 us (17%)
  local copies, waits for them, and re-layouts  40.5 us (7%)
    ppermute x14, waiting for transfers between devices, swap(): return lax.ppermute(value, 'col', [(i, i ^ distance) for i in range(cols)])  106 us
    ppermute x18, waiting for transfers between devices, down(): return lax.ppermute(value, 'row', [(i, i - 1) for i in senders])  95.2 us
    ppermute x18, starting transfers between devices, up(): return lax.ppermute(value, 'row', [(i, i + 1) for i in senders])  66.7 us
    pallas_call x4, Pallas kernels, expand(): pl.pallas_call(functools.partial(expand_kernel, tile=min(64, depth)), gri...  37.4 us
    pallas_call x4, Pallas kernels, restore(): pl.pallas_call(functools.partial(restore_kernel, cols=cols, far=far), gri...  36.8 us
    ppermute x18, waiting for transfers between devices, up(): return lax.ppermute(value, 'row', [(i, i + 1) for i in senders])  35.4 us
    pallas_call x12, Pallas kernels, hop(): pl.pallas_call(functools.partial(hop_kernel, lines=lines, step=step, tile...  29 us
    pallas_call x2, Pallas kernels, halfway(): pl.pallas_call(functools.partial(halfway_kernel, offsets=offsets, lines=l...  24.4 us
  transfers between devices with their start and end apart: 50, of which 20 were waited for; matrix products, arithmetic and copies ran while one was open for 4% of the time, Pallas kernels for 28%

profile of v8, /device:TPU:0, one launch (start us, length us, event | category | flops | bytes accessed | tf_op | source)
XLA Modules:
  0.0 575.9 jit_solution(6891659928200733433)
XLA Ops:
  0.6 3.0 collective-permute-start
  3.6 3.6 collective-permute-start.3
  8.6 41.0 %collective-permute-done = bf16[1024,1024]{1,0:T(8,128)(2,1)} collective-permute-done((bf16[1024,1024]{1,0:T(8,128)(2,1)}, bf16[1024,1024]{1,0:T(8,128)(2,1)}, u32[]{:S(2)}, u32[]{:S(2)}) %collective-permute-start) | collective-permute-done | bytes 2097184 | tf_op jit(solution)/shard_map/ppermute | solution.py:522
  49.6 2.4 collective-permute-done.3.refs_1_
  54.0 2.2 collective-permute-done.5.refs_3_
  65.1 3.2 copy-done.18
  68.3 37.4 %collective-permute-done.6.refs_4_ = bf16[1024,1024]{1,0:T(8,128)(2,1)} collective-permute-done((bf16[1024,1024]{1,0:T(8,128)(2,1)}, bf16[1024,1024]{1,0:T(8,128)(2,1)}, u32[]{:S(2)}, u32[]{:S(2)}) %collective-permute-start.6) | collective-permute-done | bytes 2097184 | tf_op jit(solution)/shard_map/ppermute | solution.py:542
  105.7 2.1 collective-permute-start.7
  109.1 14.8 %halfway.2.refs_2_ = f32[1024,1024]{1,0:T(8,128)} custom-call(s32[1]{0:T(128)} %bitcast.1.place_ref.at_ref, bf16[4096,1024]{1,0:T(8,128)(2,1)} %bitcast.11, bf16[1024,1024]{1,0:T(8,128)(2,1)} %collective-permute-done.4.refs_0_, bf16[1024,1024]{1,0:T(8,128)(2,1)S(1)} %collective-permute-done.3.refs_1_, bf16[1024,1024]{1,0:T(8,128)(2,1)} %refs_2_.1, ...), custom_call_target="tpu_custom_call" | custom-call | flops 85899344 | bytes 83886 | tf_op jit(solution)/shard_map/halfway/pallas_call | solution.py:112
  123.9 31.4 %collective-permute-done.8.refs_1_ = bf16[1024,1024]{1,0:T(8,128)(2,1)} collective-permute-done((bf16[1024,1024]{1,0:T(8,128)(2,1)}, bf16[1024,1024]{1,0:T(8,128)(2,1)}, u32[]{:S(2)}, u32[]{:S(2)}) %collective-permute-start.8) | collective-permute-done | bytes 2097184 | tf_op jit(solution)/shard_map/ppermute | solution.py:542
  156.6 4.7 collective-permute-start.9
  161.3 9.6 %halfway.3.value = f32[1024,1024]{1,0:T(8,128)} custom-call(s32[1]{0:T(128)} %bitcast.1.place_ref.at_ref, bf16[4096,1024]{1,0:T(8,128)(2,1)} %bitcast.12, bf16[1024,1024]{1,0:T(8,128)(2,1)} %collective-permute-done.7.refs_0_, bf16[1024,1024]{1,0:T(8,128)(2,1)} %collective-permute-done.8.refs_1_, f32[1024,1024]{1,0:T(8,128)} %halfway.2.refs_2_), custom_call_target="tpu_custom_call" | custom-call | flops 85899344 | bytes 83886 | tf_op jit(solution)/shard_map/halfway/pallas_call | solution.py:112
  170.9 2.2 copy-done.9
  173.1 4.4 pack.1
  179.5 22.2 %collective-permute-done.10 = bf16[1024,1024]{1,0:T(8,128)(2,1)S(1)} collective-permute-done((bf16[1024,1024]{1,0:T(8,128)(2,1)S(1)}, bf16[1024,1024]{1,0:T(8,128)(2,1)S(1)}, u32[]{:S(2)}, u32[]{:S(2)}) %collective-permute-start.10) | collective-permute-done | bytes 2097184 | tf_op jit(solution)/shard_map/ppermute | solution.py:542
  206.6 40.5 %collective-permute-done.12.message.scales = bf16[1040,1024]{1,0:T(8,128)(2,1)} collective-permute-done((bf16[1040,1024]{1,0:T(8,128)(2,1)}, bf16[1040,1024]{1,0:T(8,128)(2,1)}, u32[]{:S(2)}, u32[]{:S(2)}) %collective-permute-start.12) | collective-permute-done | bytes 2129952 | tf_op jit(solution)/shard_map/ppermute | solution.py:522
  252.4 5.3 broadcast_in_dim.24
  263.1 6.0 %unpack.4.refs_2_ = bf16[2,1024,1024]{2,1,0:T(8,128)(2,1)} custom-call(bf16[1040,1024]{1,0:T(8,128)(2,1)} %collective-permute-done.12.message.scales, bf16[1040,1024]{1,0:T(8,128)(2,1)} %collective-permute-done.12.message.scales), custom_call_target="tpu_custom_call" | custom-call | flops 4194304 | bytes 62914 | tf_op jit(solution)/shard_map/unpack/pallas_call | solution.py:174
  269.2 6.1 %unpack.3.refs_1_ = bf16[2,1024,1024]{2,1,0:T(8,128)(2,1)} custom-call(bf16[1040,1024]{1,0:T(8,128)(2,1)} %collective-permute-done.11.message.scales, bf16[1040,1024]{1,0:T(8,128)(2,1)} %collective-permute-done.11.message.scales), custom_call_target="tpu_custom_call" | custom-call | flops 4194304 | bytes 62914 | tf_op jit(solution)/shard_map/unpack/pallas_call | solution.py:174
  275.2 3.1 constant_dynamic-update-slice_fusion.1
  278.3 3.1 constant_dynamic-update-slice_fusion.refs_4_.refs_0_.refs_1_.refs_2_.refs_3_
  281.4 6.1 %unpack.5.refs_3_ = bf16[2,1024,1024]{2,1,0:T(8,128)(2,1)} custom-call(bf16[1040,1024]{1,0:T(8,128)(2,1)} %collective-permute-done.13.message.scales, bf16[1040,1024]{1,0:T(8,128)(2,1)} %collective-permute-done.13.message.scales), custom_call_target="tpu_custom_call" | custom-call | flops 4194304 | bytes 62914 | tf_op jit(solution)/shard_map/unpack/pallas_call | solution.py:174
  287.4 23.9 %rotate_part.1.part = f32[1024,1024]{1,0:T(8,128)S(1)} custom-call(s32[2]{0:T(128)S(1)} %pad_add_fusion.me_ref.at_ref, bf16[2,1024,1024]{2,1,0:T(8,128)(2,1)} %copy-done.8, bf16[2,1024,1024]{2,1,0:T(8,128)(2,1)} %unpack.3.refs_1_, bf16[2,1024,1024]{2,1,0:T(8,128)(2,1)} %unpack.4.refs_2_, bf16[2,1024,1024]{2,1,0:T(8,128)(2,1)} %unpack.5.refs_3_, ...), custom_call_target="tpu_custom_call" | custom-call | flops 171798688 | bytes 209715 | tf_op jit(solution)/shard_map/rotate_part/pallas_call | solution.py:204
  311.3 13.6 %rotate.1 = (f32[1024,1024]{1,0:T(8,128)}, f32[1024,1024]{1,0:T(8,128)}, bf16[2,1024,1024]{2,1,0:T(8,128)(2,1)S(1)}) custom-call(s32[2]{0:T(128)S(1)} %pad_add_fusion.me_ref.at_ref, f32[1024,1024]{1,0:T(8,128)S(1)} %rotate_part.1.part, bf16[1024,1024]{1,0:T(8,128)(2,1)S(1)} %collective-permute-done.16.above.refs_4_, ...), custom_call_target="tpu_custom_call" | custom-call | flops 42949672 | bytes 314572 | tf_op jit(solution)/shard_map/rotate/pallas_call | solution.py:275
  324.9 8.7 %restore.4 = (f32[2,1024,256]{2,1,0:T(8,128)S(1)}, f32[2,1024,256]{2,1,0:T(8,128)S(1)}) custom-call(s32[2]{0:T(128)S(1)} %pad_add_fusion.me_ref.at_ref, bf16[2,1024,1024]{2,1,0:T(8,128)(2,1)S(1)} %get-tuple-element.90.normed, bf16[5120,1024]{1,0:T(8,128)(2,1)} %constant_dynamic-update-slice_fusion.refs_4_.refs_0_.refs_1_.refs_2_.refs_3_, ...), custom_call_target="tpu_custom_call" | custom-call | flops 42949672 | bytes 83886 | tf_op jit(solution)/shard_map/restore/pallas_call | solution.py:341
  333.7 4.1 collective-permute-done.18.mate
  340.2 12.6 %collective-permute-done.19.refs_0_ = bf16[1040,256]{1,0:T(8,128)(2,1)S(1)} collective-permute-done((bf16[1040,256]{1,0:T(8,128)(2,1)S(1)}, bf16[1040,256]{1,0:T(8,128)(2,1)S(1)}, u32[]{:S(2)}, u32[]{:S(2)}) %collective-permute-start.19) | collective-permute-done | bytes 532512 | tf_op jit(solution)/shard_map/ppermute | solution.py:522
  352.9 9.3 %expand.4.refs_0_.refs_1_.block = f32[4096,256]{1,0:T(8,128)} custom-call(f32[2,1024,256]{2,1,0:T(8,128)S(1)} %get-tuple-element.81.keep, f32[2,1024,256]{2,1,0:T(8,128)S(1)} %collective-permute-done.18.mate, bf16[1040,256]{1,0:T(8,128)(2,1)S(1)} %collective-permute-done.19.refs_0_, bf16[4096,1024]{1,0:T(8,128)(2,1)} %bitcast.13), custom_call_target="tpu_custom_call" | custom-call | flops 42949672 | bytes 125829 | tf_op jit(solution)/shard_map/expand/pallas_call | solution.py:422
  362.2 2.2 copy-done
  365.2 4.0 collective-permute-start.20
  369.9 10.1 %collective-permute-done.20.refs_2_ = bf16[1040,256]{1,0:T(8,128)(2,1)S(1)} collective-permute-done((bf16[1040,256]{1,0:T(8,128)(2,1)S(1)}, bf16[1040,256]{1,0:T(8,128)(2,1)S(1)}, u32[]{:S(2)}, u32[]{:S(2)}) %collective-permute-start.20) | collective-permute-done | bytes 532512 | tf_op jit(solution)/shard_map/ppermute | solution.py:539
  380.0 3.0 hop.13
  383.0 4.4 collective-permute-start.22
  388.3 9.4 %restore.7 = (f32[2,1024,256]{2,1,0:T(8,128)S(1)}, f32[2,1024,256]{2,1,0:T(8,128)}) custom-call(s32[2]{0:T(128)S(1)} %pad_add_fusion.me_ref.at_ref, bf16[2,1024,1024]{2,1,0:T(8,128)(2,1)S(1)} %get-tuple-element.90.normed, bf16[5120,1024]{1,0:T(8,128)(2,1)} %constant_dynamic-update-slice_fusion.refs_4_.refs_0_.refs_1_.refs_2_.refs_3_, ...), custom_call_target="tpu_custom_call" | custom-call | flops 42949672 | bytes 83886 | tf_op jit(solution)/shard_map/restore/pallas_call | solution.py:341
  397.7 9.4 %restore.6 = (f32[2,1024,256]{2,1,0:T(8,128)S(1)}, f32[2,1024,256]{2,1,0:T(8,128)}) custom-call(s32[2]{0:T(128)S(1)} %pad_add_fusion.me_ref.at_ref, bf16[2,1024,1024]{2,1,0:T(8,128)(2,1)S(1)} %get-tuple-element.90.normed, bf16[5120,1024]{1,0:T(8,128)(2,1)} %constant_dynamic-update-slice_fusion.refs_4_.refs_0_.refs_1_.refs_2_.refs_3_, ...), custom_call_target="tpu_custom_call" | custom-call | flops 42949672 | bytes 83886 | tf_op jit(solution)/shard_map/restore/pallas_call | solution.py:341
  407.6 9.4 %restore.5 = (f32[2,1024,256]{2,1,0:T(8,128)S(1)}, f32[2,1024,256]{2,1,0:T(8,128)}) custom-call(s32[2]{0:T(128)S(1)} %pad_add_fusion.me_ref.at_ref, bf16[2,1024,1024]{2,1,0:T(8,128)(2,1)S(1)} %get-tuple-element.90.normed, bf16[5120,1024]{1,0:T(8,128)(2,1)} %constant_dynamic-update-slice_fusion.refs_4_.refs_0_.refs_1_.refs_2_.refs_3_, ...), custom_call_target="tpu_custom_call" | custom-call | flops 42949672 | bytes 83886 | tf_op jit(solution)/shard_map/restore/pallas_call | solution.py:341
  424.7 8.0 %collective-permute-done.41.refs_0_ = bf16[1040,256]{1,0:T(8,128)(2,1)S(1)} collective-permute-done((bf16[1040,256]{1,0:T(8,128)(2,1)S(1)}, bf16[1040,256]{1,0:T(8,128)(2,1)S(1)}, u32[]{:S(2)}, u32[]{:S(2)}) %collective-permute-start.41) | collective-permute-done | bytes 532512 | tf_op jit(solution)/shard_map/ppermute | solution.py:522
  432.8 9.3 %expand.7.refs_0_.refs_1_.block = f32[4096,256]{1,0:T(8,128)} custom-call(f32[2,1024,256]{2,1,0:T(8,128)S(1)} %copy-done.15, f32[2,1024,256]{2,1,0:T(8,128)S(1)} %copy-done.17, bf16[1040,256]{1,0:T(8,128)(2,1)S(1)} %collective-permute-done.41.refs_0_, bf16[4096,1024]{1,0:T(8,128)(2,1)} %bitcast.14), custom_call_target="tpu_custom_call" | custom-call | flops 42949672 | bytes 125829 | tf_op jit(solution)/shard_map/expand/pallas_call | solution.py:422
  442.1 2.2 copy-done.2
  446.1 7.4 %collective-permute-start.42 = (bf16[1040,256]{1,0:T(8,128)(2,1)}, bf16[1040,256]{1,0:T(8,128)(2,1)S(1)}, u32[]{:S(2)}, u32[]{:S(2)}) collective-permute-start(bf16[1040,256]{1,0:T(8,128)(2,1)} %get-tuple-element.109), channel_id=1, source_target_pairs={{0,4},{1,5},{2,6},{3,7},{16,20},{17,21},{18,22},{19,23}} | collective-permute-start | bytes 1597448 | tf_op jit(solution)/shard_map/ppermute | solution.py:539
  454.9 9.3 %expand.6.refs_0_.refs_1_.block = f32[4096,256]{1,0:T(8,128)} custom-call(f32[2,1024,256]{2,1,0:T(8,128)S(1)} %copy-done.11, f32[2,1024,256]{2,1,0:T(8,128)S(1)} %copy-done.13, bf16[1040,256]{1,0:T(8,128)(2,1)S(1)} %collective-permute-done.33.refs_0_, bf16[4096,1024]{1,0:T(8,128)(2,1)} %bitcast.15), custom_call_target="tpu_custom_call" | custom-call | flops 42949672 | bytes 125829 | tf_op jit(solution)/shard_map/expand/pallas_call | solution.py:422
  464.2 2.2 copy-done.4
  469.2 9.4 %expand.5.refs_0_.refs_1_.block = f32[4096,256]{1,0:T(8,128)} custom-call(f32[2,1024,256]{2,1,0:T(8,128)S(1)} %get-tuple-element.91.keep, f32[2,1024,256]{2,1,0:T(8,128)S(1)} %collective-permute-done.24.mate, bf16[1040,256]{1,0:T(8,128)(2,1)S(1)} %collective-permute-done.25.refs_0_, bf16[4096,1024]{1,0:T(8,128)(2,1)} %bitcast.16), custom_call_target="tpu_custom_call" | custom-call | flops 42949672 | bytes 125829 | tf_op jit(solution)/shard_map/expand/pallas_call | solution.py:422
  478.6 2.2 copy-done.6
  483.6 3.1 hop.21
  488.8 3.0 hop.18
  491.9 2.8 collective-permute-start.36
  496.1 3.0 hop.23
  499.1 3.0 hop.15
  502.1 6.5 %collective-permute-start.28 = (bf16[1040,256]{1,0:T(8,128)(2,1)S(1)}, bf16[1040,256]{1,0:T(8,128)(2,1)S(1)}, u32[]{:S(2)}, u32[]{:S(2)}) collective-permute-start(bf16[1040,256]{1,0:T(8,128)(2,1)S(1)} %get-tuple-element.95), channel_id=1, source_target_pairs={{0,4},{4,8},{1,5},{5,9},{2,6},{6,10},{3,7},{7,11},{16,20},{20,24},... | collective-permute-start | bytes 1597448 | tf_op jit(solution)/shard_map/ppermute | solution.py:539
  509.3 5.1 collective-permute-start.48
  514.5 3.0 hop.22
  519.5 5.9 %collective-permute-start.46 = (bf16[1040,256]{1,0:T(8,128)(2,1)S(1)}, bf16[1040,256]{1,0:T(8,128)(2,1)S(1)}, u32[]{:S(2)}, u32[]{:S(2)}) collective-permute-start(bf16[1040,256]{1,0:T(8,128)(2,1)S(1)} %get-tuple-element.113), channel_id=1, source_target_pairs={{0,4},{4,8},{8,12},{1,5},{5,9},{9,13},{2,6},{6,10},{10,14},{3,7},{... | collective-permute-start | bytes 1597448 | tf_op jit(solution)/shard_map/ppermute | solution.py:539
  525.5 3.0 hop.19
  531.0 5.3 collective-permute-start.38
  536.3 3.8 hop.16
  542.4 5.0 collective-permute-start.30
  547.4 5.1 collective-permute-done.46.up
  554.0 2.2 finish.4.refs_0_
  556.3 2.2 finish.5.refs_0_
  558.5 5.4 collective-permute-done.38.up
  563.9 2.2 finish.6.refs_0_
  566.1 7.5 %collective-permute-done.30.up = bf16[1040,256]{1,0:T(8,128)(2,1)S(1)} collective-permute-done((bf16[1040,256]{1,0:T(8,128)(2,1)}, bf16[1040,256]{1,0:T(8,128)(2,1)S(1)}, u32[]{:S(2)}, u32[]{:S(2)}) %collective-permute-start.30) | collective-permute-done | bytes 532512 | tf_op jit(solution)/shard_map/ppermute | solution.py:539
  573.7 2.2 finish.7
  (136 shorter events, 66.7 us)
Async XLA Ops:
  0.6 49.0 %collective-permute-start = (bf16[1024,1024]{1,0:T(8,128)(2,1)}, bf16[1024,1024]{1,0:T(8,128)(2,1)}, u32[]{:S(2)}, u32[]{:S(2)}) collective-permute-start(bf16[1024,1024]{1,0:T(8,128)(2,1)} %param.8), channel_id=1, source_target_pairs={{0,2},{1,3},{2,0},{3,1},{4,6},{5,7},{6,4},{7,5},{8,10},{9,11},{10,... | collective-permute-start | bytes 6291464 | tf_op jit(solution)/shard_map/ppermute | solution.py:522
  3.6 48.4 %collective-permute-start.3 = (bf16[1024,1024]{1,0:T(8,128)(2,1)}, bf16[1024,1024]{1,0:T(8,128)(2,1)S(1)}, u32[]{:S(2)}, u32[]{:S(2)}) collective-permute-start(bf16[1024,1024]{1,0:T(8,128)(2,1)} %refs_2_.1), channel_id=1, source_target_pairs={{0,4},{4,8},{8,12},{1,5},{5,9},{9,13},{2,6},{6,10},{10,14},{3,7},{... | collective-permute-start | bytes 6291464 | tf_op jit(solution)/shard_map/ppermute | solution.py:539
  7.2 49.0 %collective-permute-start.5 = (bf16[1024,1024]{1,0:T(8,128)(2,1)}, bf16[1024,1024]{1,0:T(8,128)(2,1)}, u32[]{:S(2)}, u32[]{:S(2)}) collective-permute-start(bf16[1024,1024]{1,0:T(8,128)(2,1)} %refs_2_.1), channel_id=1, source_target_pairs={{4,0},{8,4},{12,8},{5,1},{9,5},{13,9},{6,2},{10,6},{14,10},{7,3},{... | collective-permute-start | bytes 6291464 | tf_op jit(solution)/shard_map/ppermute | solution.py:542
  8.5 52.8 %collective-permute-start.1 = (bf16[1024,1024]{1,0:T(8,128)(2,1)}, bf16[1024,1024]{1,0:T(8,128)(2,1)}, u32[]{:S(2)}, u32[]{:S(2)}) collective-permute-start(bf16[1024,1024]{1,0:T(8,128)(2,1)} %param.8), channel_id=1, source_target_pairs={{0,1},{1,0},{2,3},{3,2},{4,5},{5,4},{6,7},{7,6},{8,9},{9,8},{10,11... | collective-permute-start | bytes 6291464 | tf_op jit(solution)/shard_map/ppermute | solution.py:522
  49.6 13.6 %collective-permute-start.2 = (bf16[1024,1024]{1,0:T(8,128)(2,1)}, bf16[1024,1024]{1,0:T(8,128)(2,1)}, u32[]{:S(2)}, u32[]{:S(2)}) collective-permute-start(bf16[1024,1024]{1,0:T(8,128)(2,1)} %collective-permute-done), channel_id=1, source_target_pairs={{0,1},{1,0},{2,3},{3,2},{4,5},{5,4},{6,7},{7,6},{8,9},{9,8},{10,11... | collective-permute-start | bytes 6291464 | tf_op jit(solution)/shard_map/ppermute | solution.py:522
  52.0 13.1 %collective-permute-start.4 = (bf16[1024,1024]{1,0:T(8,128)(2,1)S(1)}, bf16[1024,1024]{1,0:T(8,128)(2,1)}, u32[]{:S(2)}, u32[]{:S(2)}) collective-permute-start(bf16[1024,1024]{1,0:T(8,128)(2,1)S(1)} %collective-permute-done.3.refs_1_), channel_id=1, source_target_pairs={{4,8},{8,12},{5,9},{9,13},{6,10},{10,14},{7,11},{11,15},{20,24},{2... | collective-permute-start | bytes 6291464 | tf_op jit(solution)/shard_map/ppermute | solution.py:539
  56.3 49.4 %collective-permute-start.6 = (bf16[1024,1024]{1,0:T(8,128)(2,1)}, bf16[1024,1024]{1,0:T(8,128)(2,1)}, u32[]{:S(2)}, u32[]{:S(2)}) collective-permute-start(bf16[1024,1024]{1,0:T(8,128)(2,1)} %collective-permute-done.5.refs_3_), channel_id=1, source_target_pairs={{4,0},{8,4},{5,1},{9,5},{6,2},{10,6},{7,3},{11,7},{20,16},{24,20},... | collective-permute-start | bytes 6291464 | tf_op jit(solution)/shard_map/ppermute | solution.py:542
  105.7 18.2 %collective-permute-start.7 = (bf16[1024,1024]{1,0:T(8,128)(2,1)}, bf16[1024,1024]{1,0:T(8,128)(2,1)}, u32[]{:S(2)}, u32[]{:S(2)}) collective-permute-start(bf16[1024,1024]{1,0:T(8,128)(2,1)} %collective-permute-done.4.refs_0_), channel_id=1, source_target_pairs={{8,12},{9,13},{10,14},{11,15},{24,28},{25,29},{26,30},{27,31}} | collective-permute-start | bytes 6291464 | tf_op jit(solution)/shard_map/ppermute | solution.py:539
  107.8 47.6 %collective-permute-start.8 = (bf16[1024,1024]{1,0:T(8,128)(2,1)}, bf16[1024,1024]{1,0:T(8,128)(2,1)}, u32[]{:S(2)}, u32[]{:S(2)}) collective-permute-start(bf16[1024,1024]{1,0:T(8,128)(2,1)} %collective-permute-done.6.refs_4_), channel_id=1, source_target_pairs={{4,0},{5,1},{6,2},{7,3},{20,16},{21,17},{22,18},{23,19}} | collective-permute-start | bytes 6291464 | tf_op jit(solution)/shard_map/ppermute | solution.py:542
  109.1 46.3 %copy-start.20 = (bf16[1024,1024]{1,0:T(8,128)(2,1)S(1)}, bf16[1024,1024]{1,0:T(8,128)(2,1)}, u32[]{:S(2)}) copy-start(bf16[1024,1024]{1,0:T(8,128)(2,1)} %param.9) | copy-start | bytes 6291460
  155.3 46.3 %collective-permute-start.10 = (bf16[1024,1024]{1,0:T(8,128)(2,1)S(1)}, bf16[1024,1024]{1,0:T(8,128)(2,1)S(1)}, u32[]{:S(2)}, u32[]{:S(2)}) collective-permute-start(bf16[1024,1024]{1,0:T(8,128)(2,1)S(1)} %copy-done.20), channel_id=1, source_target_pairs={{4,0},{8,4},{12,8},{5,1},{9,5},{13,9},{6,2},{10,6},{14,10},{7,3},{... | collective-permute-start | bytes 6291464 | tf_op jit(solution)/shard_map/ppermute | solution.py:542
  156.6 46.2 %collective-permute-start.9 = (bf16[1024,1024]{1,0:T(8,128)(2,1)S(1)}, bf16[1024,1024]{1,0:T(8,128)(2,1)S(1)}, u32[]{:S(2)}, u32[]{:S(2)}) collective-permute-start(bf16[1024,1024]{1,0:T(8,128)(2,1)S(1)} %copy-done.20), channel_id=1, source_target_pairs={{0,4},{4,8},{8,12},{1,5},{5,9},{9,13},{2,6},{6,10},{10,14},{3,7},{... | collective-permute-start | bytes 6291464 | tf_op jit(solution)/shard_map/ppermute | solution.py:539
  201.7 45.4 %copy-start.22 = (bf16[1024,1024]{1,0:T(8,128)(2,1)}, bf16[1024,1024]{1,0:T(8,128)(2,1)S(1)}, u32[]{:S(2)}) copy-start(bf16[1024,1024]{1,0:T(8,128)(2,1)S(1)} %collective-permute-done.10) | copy-start | bytes 6291460
  202.8 46.2 %copy-start.24 = (bf16[1024,1024]{1,0:T(8,128)(2,1)}, bf16[1024,1024]{1,0:T(8,128)(2,1)S(1)}, u32[]{:S(2)}) copy-start(bf16[1024,1024]{1,0:T(8,128)(2,1)S(1)} %collective-permute-done.9) | copy-start | bytes 6291460
  202.8 44.3 %collective-permute-start.12 = (bf16[1040,1024]{1,0:T(8,128)(2,1)}, bf16[1040,1024]{1,0:T(8,128)(2,1)}, u32[]{:S(2)}, u32[]{:S(2)}) collective-permute-start(bf16[1040,1024]{1,0:T(8,128)(2,1)} %get-tuple-element.70), channel_id=1, source_target_pairs={{0,2},{1,3},{2,0},{3,1},{4,6},{5,7},{6,4},{7,5},{8,10},{9,11},{10,... | collective-permute-start | bytes 6389768 | tf_op jit(solution)/shard_map/ppermute | solution.py:522
  203.4 45.7 %collective-permute-start.15 = (bf16[1024,1024]{1,0:T(8,128)(2,1)S(1)}, bf16[1024,1024]{1,0:T(8,128)(2,1)}, u32[]{:S(2)}, u32[]{:S(2)}) collective-permute-start(bf16[1024,1024]{1,0:T(8,128)(2,1)S(1)} %collective-permute-done.10), channel_id=1, source_target_pairs={{4,0},{8,4},{5,1},{9,5},{6,2},{10,6},{7,3},{11,7},{20,16},{24,20},... | collective-permute-start | bytes 6291464 | tf_op jit(solution)/shard_map/ppermute | solution.py:542
  204.7 45.7 %collective-permute-start.14 = (bf16[1024,1024]{1,0:T(8,128)(2,1)S(1)}, bf16[1024,1024]{1,0:T(8,128)(2,1)}, u32[]{:S(2)}, u32[]{:S(2)}) collective-permute-start(bf16[1024,1024]{1,0:T(8,128)(2,1)S(1)} %collective-permute-done.9), channel_id=1, source_target_pairs={{4,8},{8,12},{5,9},{9,13},{6,10},{10,14},{7,11},{11,15},{20,24},{2... | collective-permute-start | bytes 6291464 | tf_op jit(solution)/shard_map/ppermute | solution.py:539
  206.6 62.5 %collective-permute-start.11 = (bf16[1040,1024]{1,0:T(8,128)(2,1)}, bf16[1040,1024]{1,0:T(8,128)(2,1)}, u32[]{:S(2)}, u32[]{:S(2)}) collective-permute-start(bf16[1040,1024]{1,0:T(8,128)(2,1)} %get-tuple-element.70), channel_id=1, source_target_pairs={{0,1},{1,0},{2,3},{3,2},{4,5},{5,4},{6,7},{7,6},{8,9},{9,8},{10,11... | collective-permute-start | bytes 6389768 | tf_op jit(solution)/shard_map/ppermute | solution.py:522
  247.1 34.3 %collective-permute-start.13 = (bf16[1040,1024]{1,0:T(8,128)(2,1)}, bf16[1040,1024]{1,0:T(8,128)(2,1)}, u32[]{:S(2)}, u32[]{:S(2)}) collective-permute-start(bf16[1040,1024]{1,0:T(8,128)(2,1)} %collective-permute-done.12.message.scales), channel_id=1, source_target_pairs={{0,1},{1,0},{2,3},{3,2},{4,5},{5,4},{6,7},{7,6},{8,9},{9,8},{10,11... | collective-permute-start | bytes 6389768 | tf_op jit(solution)/shard_map/ppermute | solution.py:522
  249.1 62.3 %collective-permute-start.16 = (bf16[1024,1024]{1,0:T(8,128)(2,1)}, bf16[1024,1024]{1,0:T(8,128)(2,1)S(1)}, u32[]{:S(2)}, u32[]{:S(2)}) collective-permute-start(bf16[1024,1024]{1,0:T(8,128)(2,1)} %collective-permute-done.15), channel_id=1, source_target_pairs={{4,0},{5,1},{6,2},{7,3},{20,16},{21,17},{22,18},{23,19}} | collective-permute-start | bytes 6291464 | tf_op jit(solution)/shard_map/ppermute | solution.py:542
  250.4 61.0 %collective-permute-start.17 = (bf16[1024,1024]{1,0:T(8,128)(2,1)}, bf16[1024,1024]{1,0:T(8,128)(2,1)}, u32[]{:S(2)}, u32[]{:S(2)}) collective-permute-start(bf16[1024,1024]{1,0:T(8,128)(2,1)} %collective-permute-done.14), channel_id=1, source_target_pairs={{8,12},{9,13},{10,14},{11,15},{24,28},{25,29},{26,30},{27,31}} | collective-permute-start | bytes 6291464 | tf_op jit(solution)/shard_map/ppermute | solution.py:539
  252.4 5.3 copy-start.21
  333.6 4.2 collective-permute-start.18
  338.7 14.2 %collective-permute-start.19 = (bf16[1040,256]{1,0:T(8,128)(2,1)S(1)}, bf16[1040,256]{1,0:T(8,128)(2,1)S(1)}, u32[]{:S(2)}, u32[]{:S(2)}) collective-permute-start(bf16[1040,256]{1,0:T(8,128)(2,1)S(1)} %send.4), channel_id=1, source_target_pairs={{0,2},{1,3},{2,0},{3,1},{4,6},{5,7},{6,4},{7,5},{8,10},{9,11},{10,... | collective-permute-start | bytes 1597448 | tf_op jit(solution)/shard_map/ppermute | solution.py:522
  365.2 14.8 %collective-permute-start.20 = (bf16[1040,256]{1,0:T(8,128)(2,1)S(1)}, bf16[1040,256]{1,0:T(8,128)(2,1)S(1)}, u32[]{:S(2)}, u32[]{:S(2)}) collective-permute-start(bf16[1040,256]{1,0:T(8,128)(2,1)S(1)} %get-tuple-element.83), channel_id=1, source_target_pairs={{0,4},{1,5},{2,6},{3,7},{16,20},{17,21},{18,22},{19,23}} | collective-permute-start | bytes 1597448 | tf_op jit(solution)/shard_map/ppermute | solution.py:539
  369.2 10.8 %collective-permute-start.21 = (bf16[1040,256]{1,0:T(8,128)(2,1)S(1)}, bf16[1040,256]{1,0:T(8,128)(2,1)S(1)}, u32[]{:S(2)}, u32[]{:S(2)}) collective-permute-start(bf16[1040,256]{1,0:T(8,128)(2,1)S(1)} %get-tuple-element.84), channel_id=1, source_target_pairs={{12,8},{13,9},{14,10},{15,11},{28,24},{29,25},{30,26},{31,27}} | collective-permute-start | bytes 1597448 | tf_op jit(solution)/shard_map/ppermute | solution.py:542
  383.0 24.6 %collective-permute-start.22 = (bf16[1040,256]{1,0:T(8,128)(2,1)S(1)}, bf16[1040,256]{1,0:T(8,128)(2,1)S(1)}, u32[]{:S(2)}, u32[]{:S(2)}) collective-permute-start(bf16[1040,256]{1,0:T(8,128)(2,1)S(1)} %get-tuple-element.88), channel_id=1, source_target_pairs={{0,4},{4,8},{1,5},{5,9},{2,6},{6,10},{3,7},{7,11},{16,20},{20,24},... | collective-permute-start | bytes 1597448 | tf_op jit(solution)/shard_map/ppermute | solution.py:539
  387.4 20.2 %collective-permute-start.23 = (bf16[1040,256]{1,0:T(8,128)(2,1)S(1)}, bf16[1040,256]{1,0:T(8,128)(2,1)S(1)}, u32[]{:S(2)}, u32[]{:S(2)}) collective-permute-start(bf16[1040,256]{1,0:T(8,128)(2,1)S(1)} %get-tuple-element.89), channel_id=1, source_target_pairs={{8,4},{12,8},{9,5},{13,9},{10,6},{14,10},{11,7},{15,11},{24,20},{2... | collective-permute-start | bytes 1597448 | tf_op jit(solution)/shard_map/ppermute | solution.py:542
  397.7 19.3 %copy-start.14 = (f32[2,1024,256]{2,1,0:T(8,128)}, f32[2,1024,256]{2,1,0:T(8,128)S(1)}, u32[]{:S(2)}) copy-start(f32[2,1024,256]{2,1,0:T(8,128)S(1)} %get-tuple-element.107.keep) | copy-start | bytes 6291460
  397.7 19.3 %collective-permute-start.40 = (f32[2,1024,256]{2,1,0:T(8,128)}, f32[2,1024,256]{2,1,0:T(8,128)S(1)}, u32[]{:S(2)}, u32[]{:S(2)}) collective-permute-start(f32[2,1024,256]{2,1,0:T(8,128)} %get-tuple-element.108), channel_id=1, source_target_pairs={{0,1},{1,0},{2,3},{3,2},{4,5},{5,4},{6,7},{7,6},{8,9},{9,8},{10,11... | collective-permute-start | bytes 6291464 | tf_op jit(solution)/shard_map/ppermute | solution.py:522
  407.1 12.3 %copy-start.10 = (f32[2,1024,256]{2,1,0:T(8,128)}, f32[2,1024,256]{2,1,0:T(8,128)S(1)}, u32[]{:S(2)}) copy-start(f32[2,1024,256]{2,1,0:T(8,128)S(1)} %get-tuple-element.99.keep) | copy-start | bytes 6291460
  407.1 12.3 %collective-permute-start.32 = (f32[2,1024,256]{2,1,0:T(8,128)}, f32[2,1024,256]{2,1,0:T(8,128)S(1)}, u32[]{:S(2)}, u32[]{:S(2)}) collective-permute-start(f32[2,1024,256]{2,1,0:T(8,128)} %get-tuple-element.100), channel_id=1, source_target_pairs={{0,1},{1,0},{2,3},{3,2},{4,5},{5,4},{6,7},{7,6},{8,9},{9,8},{10,11... | collective-permute-start | bytes 6291464 | tf_op jit(solution)/shard_map/ppermute | solution.py:522
  416.9 4.7 collective-permute-start.24
  417.8 15.0 %collective-permute-start.41 = (bf16[1040,256]{1,0:T(8,128)(2,1)S(1)}, bf16[1040,256]{1,0:T(8,128)(2,1)S(1)}, u32[]{:S(2)}, u32[]{:S(2)}) collective-permute-start(bf16[1040,256]{1,0:T(8,128)(2,1)S(1)} %send.7), channel_id=1, source_target_pairs={{0,2},{1,3},{2,0},{3,1},{4,6},{5,7},{6,4},{7,5},{8,10},{9,11},{10,... | collective-permute-start | bytes 1597448 | tf_op jit(solution)/shard_map/ppermute | solution.py:522
  419.3 3.9 copy-start.12
  419.3 13.4 %copy-start.15 = (f32[2,1024,256]{2,1,0:T(8,128)S(1)}, f32[2,1024,256]{2,1,0:T(8,128)}, u32[]{:S(2)}) copy-start(f32[2,1024,256]{2,1,0:T(8,128)} %copy-done.14) | copy-start | bytes 6291460
  419.3 13.4 %copy-start.17 = (f32[2,1024,256]{2,1,0:T(8,128)S(1)}, f32[2,1024,256]{2,1,0:T(8,128)}, u32[]{:S(2)}) copy-start(f32[2,1024,256]{2,1,0:T(8,128)} %copy-done.16) | copy-start | bytes 6291460
  421.0 33.9 %collective-permute-start.33 = (bf16[1040,256]{1,0:T(8,128)(2,1)}, bf16[1040,256]{1,0:T(8,128)(2,1)S(1)}, u32[]{:S(2)}, u32[]{:S(2)}) collective-permute-start(bf16[1040,256]{1,0:T(8,128)(2,1)} %send.6), channel_id=1, source_target_pairs={{0,2},{1,3},{2,0},{3,1},{4,6},{5,7},{6,4},{7,5},{8,10},{9,11},{10,... | collective-permute-start | bytes 1597448 | tf_op jit(solution)/shard_map/ppermute | solution.py:522
  423.2 46.0 %collective-permute-start.25 = (bf16[1040,256]{1,0:T(8,128)(2,1)}, bf16[1040,256]{1,0:T(8,128)(2,1)S(1)}, u32[]{:S(2)}, u32[]{:S(2)}) collective-permute-start(bf16[1040,256]{1,0:T(8,128)(2,1)} %send.5), channel_id=1, source_target_pairs={{0,2},{1,3},{2,0},{3,1},{4,6},{5,7},{6,4},{7,5},{8,10},{9,11},{10,... | collective-permute-start | bytes 1597448 | tf_op jit(solution)/shard_map/ppermute | solution.py:522
  444.3 10.7 %copy-start.11 = (f32[2,1024,256]{2,1,0:T(8,128)S(1)}, f32[2,1024,256]{2,1,0:T(8,128)}, u32[]{:S(2)}) copy-start(f32[2,1024,256]{2,1,0:T(8,128)} %copy-done.10) | copy-start | bytes 6291460
  444.3 10.7 %copy-start.13 = (f32[2,1024,256]{2,1,0:T(8,128)S(1)}, f32[2,1024,256]{2,1,0:T(8,128)}, u32[]{:S(2)}) copy-start(f32[2,1024,256]{2,1,0:T(8,128)} %copy-done.12) | copy-start | bytes 6291460
  446.1 36.9 %collective-permute-start.42 = (bf16[1040,256]{1,0:T(8,128)(2,1)}, bf16[1040,256]{1,0:T(8,128)(2,1)S(1)}, u32[]{:S(2)}, u32[]{:S(2)}) collective-permute-start(bf16[1040,256]{1,0:T(8,128)(2,1)} %get-tuple-element.109), channel_id=1, source_target_pairs={{0,4},{1,5},{2,6},{3,7},{16,20},{17,21},{18,22},{19,23}} | collective-permute-start | bytes 1597448 | tf_op jit(solution)/shard_map/ppermute | solution.py:539
  453.5 30.2 %collective-permute-start.43 = (bf16[1040,256]{1,0:T(8,128)(2,1)}, bf16[1040,256]{1,0:T(8,128)(2,1)}, u32[]{:S(2)}, u32[]{:S(2)}) collective-permute-start(bf16[1040,256]{1,0:T(8,128)(2,1)} %get-tuple-element.110), channel_id=1, source_target_pairs={{12,8},{13,9},{14,10},{15,11},{28,24},{29,25},{30,26},{31,27}} | collective-permute-start | bytes 1597448 | tf_op jit(solution)/shard_map/ppermute | solution.py:542
  467.2 20.9 %collective-permute-start.34 = (bf16[1040,256]{1,0:T(8,128)(2,1)S(1)}, bf16[1040,256]{1,0:T(8,128)(2,1)S(1)}, u32[]{:S(2)}, u32[]{:S(2)}) collective-permute-start(bf16[1040,256]{1,0:T(8,128)(2,1)S(1)} %get-tuple-element.101), channel_id=1, source_target_pairs={{0,4},{1,5},{2,6},{3,7},{16,20},{17,21},{18,22},{19,23}} | collective-permute-start | bytes 1597448 | tf_op jit(solution)/shard_map/ppermute | solution.py:539
  468.5 20.3 %collective-permute-start.35 = (bf16[1040,256]{1,0:T(8,128)(2,1)S(1)}, bf16[1040,256]{1,0:T(8,128)(2,1)S(1)}, u32[]{:S(2)}, u32[]{:S(2)}) collective-permute-start(bf16[1040,256]{1,0:T(8,128)(2,1)S(1)} %get-tuple-element.102), channel_id=1, source_target_pairs={{12,8},{13,9},{14,10},{15,11},{28,24},{29,25},{30,26},{31,27}} | collective-permute-start | bytes 1597448 | tf_op jit(solution)/shard_map/ppermute | solution.py:542
  481.6 13.8 %collective-permute-start.26 = (bf16[1040,256]{1,0:T(8,128)(2,1)S(1)}, bf16[1040,256]{1,0:T(8,128)(2,1)S(1)}, u32[]{:S(2)}, u32[]{:S(2)}) collective-permute-start(bf16[1040,256]{1,0:T(8,128)(2,1)S(1)} %get-tuple-element.93), channel_id=1, source_target_pairs={{0,4},{1,5},{2,6},{3,7},{16,20},{17,21},{18,22},{19,23}} | collective-permute-start | bytes 1597448 | tf_op jit(solution)/shard_map/ppermute | solution.py:539
  482.9 16.2 %collective-permute-start.27 = (bf16[1040,256]{1,0:T(8,128)(2,1)S(1)}, bf16[1040,256]{1,0:T(8,128)(2,1)S(1)}, u32[]{:S(2)}, u32[]{:S(2)}) collective-permute-start(bf16[1040,256]{1,0:T(8,128)(2,1)S(1)} %get-tuple-element.94), channel_id=1, source_target_pairs={{12,8},{13,9},{14,10},{15,11},{28,24},{29,25},{30,26},{31,27}} | collective-permute-start | bytes 1597448 | tf_op jit(solution)/shard_map/ppermute | solution.py:542
  486.8 21.8 %collective-permute-start.44 = (bf16[1040,256]{1,0:T(8,128)(2,1)S(1)}, bf16[1040,256]{1,0:T(8,128)(2,1)S(1)}, u32[]{:S(2)}, u32[]{:S(2)}) collective-permute-start(bf16[1040,256]{1,0:T(8,128)(2,1)S(1)} %get-tuple-element.111), channel_id=1, source_target_pairs={{0,4},{4,8},{1,5},{5,9},{2,6},{6,10},{3,7},{7,11},{16,20},{20,24},... | collective-permute-start | bytes 1597448 | tf_op jit(solution)/shard_map/ppermute | solution.py:539
  488.1 21.2 %collective-permute-start.45 = (bf16[1040,256]{1,0:T(8,128)(2,1)S(1)}, bf16[1040,256]{1,0:T(8,128)(2,1)S(1)}, u32[]{:S(2)}, u32[]{:S(2)}) collective-permute-start(bf16[1040,256]{1,0:T(8,128)(2,1)S(1)} %get-tuple-element.112), channel_id=1, source_target_pairs={{8,4},{12,8},{9,5},{13,9},{10,6},{14,10},{11,7},{15,11},{24,20},{2... | collective-permute-start | bytes 1597448 | tf_op jit(solution)/shard_map/ppermute | solution.py:542
  491.9 26.4 %collective-permute-start.36 = (bf16[1040,256]{1,0:T(8,128)(2,1)S(1)}, bf16[1040,256]{1,0:T(8,128)(2,1)S(1)}, u32[]{:S(2)}, u32[]{:S(2)}) collective-permute-start(bf16[1040,256]{1,0:T(8,128)(2,1)S(1)} %get-tuple-element.103), channel_id=1, source_target_pairs={{0,4},{4,8},{1,5},{5,9},{2,6},{6,10},{3,7},{7,11},{16,20},{20,24},... | collective-permute-start | bytes 1597448 | tf_op jit(solution)/shard_map/ppermute | solution.py:539
  495.4 24.1 %collective-permute-start.37 = (bf16[1040,256]{1,0:T(8,128)(2,1)S(1)}, bf16[1040,256]{1,0:T(8,128)(2,1)S(1)}, u32[]{:S(2)}, u32[]{:S(2)}) collective-permute-start(bf16[1040,256]{1,0:T(8,128)(2,1)S(1)} %get-tuple-element.104), channel_id=1, source_target_pairs={{8,4},{12,8},{9,5},{13,9},{10,6},{14,10},{11,7},{15,11},{24,20},{2... | collective-permute-start | bytes 1597448 | tf_op jit(solution)/shard_map/ppermute | solution.py:542
  502.1 27.5 %collective-permute-start.28 = (bf16[1040,256]{1,0:T(8,128)(2,1)S(1)}, bf16[1040,256]{1,0:T(8,128)(2,1)S(1)}, u32[]{:S(2)}, u32[]{:S(2)}) collective-permute-start(bf16[1040,256]{1,0:T(8,128)(2,1)S(1)} %get-tuple-element.95), channel_id=1, source_target_pairs={{0,4},{4,8},{1,5},{5,9},{2,6},{6,10},{3,7},{7,11},{16,20},{20,24},... | collective-permute-start | bytes 1597448 | tf_op jit(solution)/shard_map/ppermute | solution.py:539
  508.6 22.3 %collective-permute-start.29 = (bf16[1040,256]{1,0:T(8,128)(2,1)S(1)}, bf16[1040,256]{1,0:T(8,128)(2,1)S(1)}, u32[]{:S(2)}, u32[]{:S(2)}) collective-permute-start(bf16[1040,256]{1,0:T(8,128)(2,1)S(1)} %get-tuple-element.96), channel_id=1, source_target_pairs={{8,4},{12,8},{9,5},{13,9},{10,6},{14,10},{11,7},{15,11},{24,20},{2... | collective-permute-start | bytes 1597448 | tf_op jit(solution)/shard_map/ppermute | solution.py:542
  509.3 31.7 %collective-permute-start.48 = (bf16[1040,256]{1,0:T(8,128)(2,1)S(1)}, bf16[1040,256]{1,0:T(8,128)(2,1)S(1)}, u32[]{:S(2)}, u32[]{:S(2)}) collective-permute-start(bf16[1040,256]{1,0:T(8,128)(2,1)S(1)} %get-tuple-element.117), channel_id=1, source_target_pairs={{0,4},{4,8},{8,12},{1,5},{5,9},{9,13},{2,6},{6,10},{10,14},{3,7},{... | collective-permute-start | bytes 1597448 | tf_op jit(solution)/shard_map/ppermute | solution.py:539
  518.2 24.1 %collective-permute-start.49 = (bf16[1040,256]{1,0:T(8,128)(2,1)S(1)}, bf16[1040,256]{1,0:T(8,128)(2,1)S(1)}, u32[]{:S(2)}, u32[]{:S(2)}) collective-permute-start(bf16[1040,256]{1,0:T(8,128)(2,1)S(1)} %get-tuple-element.118), channel_id=1, source_target_pairs={{4,0},{8,4},{12,8},{5,1},{9,5},{13,9},{6,2},{10,6},{14,10},{7,3},{... | collective-permute-start | bytes 1597448 | tf_op jit(solution)/shard_map/ppermute | solution.py:542
  519.5 32.9 %collective-permute-start.46 = (bf16[1040,256]{1,0:T(8,128)(2,1)S(1)}, bf16[1040,256]{1,0:T(8,128)(2,1)S(1)}, u32[]{:S(2)}, u32[]{:S(2)}) collective-permute-start(bf16[1040,256]{1,0:T(8,128)(2,1)S(1)} %get-tuple-element.113), channel_id=1, source_target_pairs={{0,4},{4,8},{8,12},{1,5},{5,9},{9,13},{2,6},{6,10},{10,14},{3,7},{... | collective-permute-start | bytes 1597448 | tf_op jit(solution)/shard_map/ppermute | solution.py:539
  529.7 26.6 %collective-permute-start.47 = (bf16[1040,256]{1,0:T(8,128)(2,1)S(1)}, bf16[1040,256]{1,0:T(8,128)(2,1)S(1)}, u32[]{:S(2)}, u32[]{:S(2)}) collective-permute-start(bf16[1040,256]{1,0:T(8,128)(2,1)S(1)} %get-tuple-element.114), channel_id=1, source_target_pairs={{4,0},{8,4},{12,8},{5,1},{9,5},{13,9},{6,2},{10,6},{14,10},{7,3},{... | collective-permute-start | bytes 1597448 | tf_op jit(solution)/shard_map/ppermute | solution.py:542
  530.9 23.1 %copy-start.1 = (f32[4096,256]{1,0:T(8,128)S(1)}, f32[4096,256]{1,0:T(8,128)}, u32[]{:S(2)}) copy-start(f32[4096,256]{1,0:T(8,128)} %expand.4.refs_0_.refs_1_.block) | copy-start | bytes 12582916
  531.0 32.9 %collective-permute-start.38 = (bf16[1040,256]{1,0:T(8,128)(2,1)S(1)}, bf16[1040,256]{1,0:T(8,128)(2,1)S(1)}, u32[]{:S(2)}, u32[]{:S(2)}) collective-permute-start(bf16[1040,256]{1,0:T(8,128)(2,1)S(1)} %get-tuple-element.105), channel_id=1, source_target_pairs={{0,4},{4,8},{8,12},{1,5},{5,9},{9,13},{2,6},{6,10},{10,14},{3,7},{... | collective-permute-start | bytes 1597448 | tf_op jit(solution)/shard_map/ppermute | solution.py:539
  541.1 22.8 %collective-permute-start.39 = (bf16[1040,256]{1,0:T(8,128)(2,1)S(1)}, bf16[1040,256]{1,0:T(8,128)(2,1)S(1)}, u32[]{:S(2)}, u32[]{:S(2)}) collective-permute-start(bf16[1040,256]{1,0:T(8,128)(2,1)S(1)} %get-tuple-element.106), channel_id=1, source_target_pairs={{4,0},{8,4},{12,8},{5,1},{9,5},{13,9},{6,2},{10,6},{14,10},{7,3},{... | collective-permute-start | bytes 1597448 | tf_op jit(solution)/shard_map/ppermute | solution.py:542
  542.4 31.3 %collective-permute-start.30 = (bf16[1040,256]{1,0:T(8,128)(2,1)}, bf16[1040,256]{1,0:T(8,128)(2,1)S(1)}, u32[]{:S(2)}, u32[]{:S(2)}) collective-permute-start(bf16[1040,256]{1,0:T(8,128)(2,1)} %get-tuple-element.97), channel_id=1, source_target_pairs={{0,4},{4,8},{8,12},{1,5},{5,9},{9,13},{2,6},{6,10},{10,14},{3,7},{... | collective-permute-start | bytes 1597448 | tf_op jit(solution)/shard_map/ppermute | solution.py:539
  552.5 21.2 %collective-permute-start.31 = (bf16[1040,256]{1,0:T(8,128)(2,1)S(1)}, bf16[1040,256]{1,0:T(8,128)(2,1)S(1)}, u32[]{:S(2)}, u32[]{:S(2)}) collective-permute-start(bf16[1040,256]{1,0:T(8,128)(2,1)S(1)} %get-tuple-element.98), channel_id=1, source_target_pairs={{4,0},{8,4},{12,8},{5,1},{9,5},{13,9},{6,2},{10,6},{14,10},{7,3},{... | collective-permute-start | bytes 1597448 | tf_op jit(solution)/shard_map/ppermute | solution.py:542
  556.3 7.6 %copy-start.5 = (f32[4096,256]{1,0:T(8,128)S(1)}, f32[4096,256]{1,0:T(8,128)}, u32[]{:S(2)}) copy-start(f32[4096,256]{1,0:T(8,128)} %expand.6.refs_0_.refs_1_.block) | copy-start | bytes 12582916
  558.5 15.2 %copy-start.7 = (f32[4096,256]{1,0:T(8,128)S(1)}, f32[4096,256]{1,0:T(8,128)}, u32[]{:S(2)}) copy-start(f32[4096,256]{1,0:T(8,128)} %expand.5.refs_0_.refs_1_.block) | copy-start | bytes 12582916
  (12 other events, 30.1 us)

commit v9 on v8

--- a/solution.py
+++ b/solution.py
@@ -20,8 +20,10 @@
     return pltpu.CompilerParams(vmem_limit_bytes=mib * MIB)
 
 
-def cost(flops, moved):
-    return pl.CostEstimate(flops=int(flops) // 100, bytes_accessed=int(moved) // 100, transcendentals=0)
+def cost(flops, moved, weight=4):
+    return pl.CostEstimate(
+        flops=int(flops * weight), bytes_accessed=int(moved * weight), transcendentals=0
+    )
 
 
 def split(value):
@@ -122,7 +124,7 @@
         ),
         out_shape=jax.ShapeDtypeStruct((inner, width), F32),
         compiler_params=params(48),
-        cost_estimate=cost(8 * depth * inner * width, 8 * depth * inner),
+        cost_estimate=cost(8 * depth * inner * width, 8 * depth * inner, 0.3),
         name="halfway",
     )(place, left, *pieces, *extra)
 
@@ -148,8 +150,8 @@
             jax.ShapeDtypeStruct((2, depth, width), BF16),
             jax.ShapeDtypeStruct((depth + EXTRA, width), BF16),
         ],
-        compiler_params=params(32),
-        cost_estimate=cost(400 * depth * width, 10 * depth * width),
+        compiler_params=params(60),
+        cost_estimate=cost(400 * depth * width, 10 * depth * width, 0.3),
         name="pack",
     )(value)
 
@@ -181,38 +183,81 @@
         out_specs=pl.BlockSpec((2, step, width), lambda i: (0, i, 0)),
         out_shape=jax.ShapeDtypeStruct((2, depth, width), BF16),
         compiler_params=params(60),
-        cost_estimate=cost(400 * depth * width, 6 * depth * width),
+        cost_estimate=cost(400 * depth * width, 6 * depth * width, 0.3),
         name="unpack",
     )(message, message)
 
 
-def rotate_part_kernel(me_ref, *refs, cols, width):
-    pieces, (right, out) = refs[:cols], refs[cols:]
+def put_kernel(there_ref, piece, *refs):
+    right, flipped = refs[-2:]
+    right[...] = piece[...]
+    flipped[0] = piece[...].T
+
+
+def put(there, piece, held, blocks):
+    depth, width = piece.shape
+    extra = [] if held is None else list(held)
+    return pl.pallas_call(
+        put_kernel,
+        grid_spec=pltpu.PrefetchScalarGridSpec(
+            num_scalar_prefetch=1,
+            grid=(1,),
+            in_specs=[pl.BlockSpec((depth, width), lambda i, s: (0, 0))]
+            + [pl.BlockSpec(memory_space=pl.ANY)] * len(extra),
+            out_specs=[
+                pl.BlockSpec((depth, width), lambda i, s: (s[0], 0)),
+                pl.BlockSpec((1, width, depth), lambda i, s: (s[0], 0, 0)),
+            ],
+        ),
+        out_shape=[
+            jax.ShapeDtypeStruct((blocks * depth, width), BF16),
+            jax.ShapeDtypeStruct((blocks, width, depth), BF16),
+        ],
+        input_output_aliases={2: 0, 3: 1} if extra else {},
+        compiler_params=params(60),
+        cost_estimate=cost(0, 6 * depth * width, 0.3),
+        name="put",
+    )(there, piece, *extra)
+
+
+def rotate_part_kernel(at_ref, *refs, cols, width, far):
+    pieces, (right, out, total) = refs[:cols], refs[cols:]
     tile = out.shape[0]
-    total = None
+    me, place = at_ref[0], at_ref[1]
+    total[...] = jnp.zeros_like(total)
     for distance in range(cols):
-        rows = right[pl.ds(pl.multiple_of((me_ref[0] ^ distance) * width, width), width), :]
-        term = dot(pieces[distance][...].reshape(2 * tile, width), rows, ((1,), (0,)))
-        total = term if total is None else total + term
-    out[...] = total[:tile] + total[tile:]
-
-
-def rotate_part(at, pieces, right):
+        block = me ^ distance
+        late = (block == far - place) & ((place == 0) | (place == far))
+
+        @pl.when(jnp.logical_not(late))
+        def _(distance=distance, block=block):
+            rows = right[pl.ds(pl.multiple_of(block * width, width), width), :]
+            total[...] += dot(pieces[distance][...].reshape(2 * tile, width), rows, ((1,), (0,)))
+
+    out[...] = total[:tile, :] + total[tile:, :]
+
+
+def rotate_part(at, pieces, right, far):
     cols = len(pieces)
     _, depth, width = pieces[0].shape
     tile = min(256, depth)
     return pl.pallas_call(
-        functools.partial(rotate_part_kernel, cols=cols, width=width),
+        functools.partial(rotate_part_kernel, cols=cols, width=width, far=far),
         grid_spec=pltpu.PrefetchScalarGridSpec(
             num_scalar_prefetch=1,
             grid=(depth // tile,),
             in_specs=[pl.BlockSpec((2, tile, width), lambda i, s: (0, i, 0))] * cols
-            + [pl.BlockSpec(right.shape, lambda i, s: (0, 0), pipeline_mode=pl.Buffered(1))],
+            + [
+                pl.BlockSpec(
+                    (cols * width, width), lambda i, s: (0, 0), pipeline_mode=pl.Buffered(1)
+                )
+            ],
             out_specs=pl.BlockSpec((tile, width), lambda i, s: (i, 0)),
+            scratch_shapes=[pltpu.VMEM((2 * tile, width), F32)],
         ),
         out_shape=jax.ShapeDtypeStruct((depth, width), F32),
         compiler_params=params(48),
-        cost_estimate=cost(4 * depth * width * width * cols, 20 * depth * width),
+        cost_estimate=cost(4 * depth * width * width * cols, 20 * depth * width, 0.3),
         name="rotate_part",
     )(at, *pieces, right)
 
@@ -297,63 +342,42 @@
     )(at, part, above, below, first, second, *pieces)
 
 
-def restore_kernel(at_ref, normed, *refs, cols, far):
-    rows, (above, below, keep, mate, flipped) = refs[:cols], refs[cols:]
-    tile, piece = normed.shape[1], keep.shape[2]
-    me, place = at_ref[0], at_ref[1]
-
-    @pl.when(pl.program_id(0) == 0)
-    def _():
-        for distance in range(cols):
-            here = pl.ds(distance * piece, piece)
-            late = (me ^ distance) == far - place
-
-            @pl.when(jnp.logical_not(late & ((place == 0) | (place == far))))
-            def _(distance=distance, here=here):
-                flipped[:, here] = rows[distance][...].T
-
-            @pl.when(late & (place == 0))
-            def _(here=here):
-                flipped[:, here] = above[...].T
-
-            @pl.when(late & (place == far))
-            def _(here=here):
-                flipped[:, here] = below[...].T
-
-    both = dot(normed[...].reshape(2 * tile, normed.shape[2]), flipped[...], ((1,), (0,)))
-    term = both[:tile] + both[tile:]
+def restore_kernel(me_ref, normed, *refs, cols):
+    flipped, (keep, mate) = refs[:cols], refs[cols:]
+    tile = normed.shape[1]
+    both = normed[...].reshape(2 * tile, normed.shape[2])
     for distance in range(cols):
-        out = mate if distance % 2 else keep
-        out[distance // 2] = term[:, distance * piece : (distance + 1) * piece]
-
-
-def restore(at, normed, right, above, below, cols, lines, chunk, piece):
+        term = dot(both, flipped[distance][0], ((1,), (0,)))
+        (mate if distance % 2 else keep)[distance // 2] = term[:tile] + term[tile:]
+
+
+def restore(me, normed, flipped, cols, chunk, piece):
     _, depth, inner = normed.shape
+    wide = flipped.shape[2]
     tile = min(256, depth)
-    aligned = above.shape[0] == inner
-    far = lines - 1 if aligned else -cols
     out = pl.BlockSpec((cols // 2, tile, piece), lambda i, s: (0, i, 0))
 
-    def rows(distance):
-        return pl.BlockSpec((piece, inner), lambda i, s: ((s[0] ^ distance) * CHUNKS + chunk, 0))
-
-    last = pl.BlockSpec((piece, inner), lambda i, s: (chunk if aligned else 0, 0))
-    return pl.pallas_call(
-        functools.partial(restore_kernel, cols=cols, far=far),
+    def columns(distance):
+        def at(i, s):
+            start = (s[0] ^ distance) * inner + chunk * piece
+            return start // wide, 0, lax.rem(start, wide) // piece
+
+        return pl.BlockSpec((1, inner, piece), at)
+
+    return pl.pallas_call(
+        functools.partial(restore_kernel, cols=cols),
         grid_spec=pltpu.PrefetchScalarGridSpec(
             num_scalar_prefetch=1,
             grid=(depth // tile,),
             in_specs=[pl.BlockSpec((2, tile, inner), lambda i, s: (0, i, 0))]
-            + [rows(distance) for distance in range(cols)]
-            + [last, last],
+            + [columns(distance) for distance in range(cols)],
             out_specs=[out, out],
-            scratch_shapes=[pltpu.VMEM((inner, cols * piece), BF16)],
         ),
         out_shape=[jax.ShapeDtypeStruct((cols // 2, depth, piece), F32)] * 2,
-        compiler_params=params(40),
+        compiler_params=params(60),
         cost_estimate=cost(4 * depth * inner * piece * cols, 8 * depth * piece * cols),
         name="restore",
-    )(at, normed, *([right] * cols), above, below)
+    )(me, normed, *([flipped] * cols))
 
 
 def summed(keep, mate, codes):
@@ -541,6 +565,9 @@
     def down(value, senders):
         return lax.ppermute(value, "row", [(i, i - 1) for i in senders])
 
+    def after(value, *others):
+        return lax.optimization_barrier((value,) + others)[0]
+
     def walk(held, step):
         held[-step] = up(held[1 - step], range(step - 1, lines - 1))
         held[step] = down(held[step - 1], range(1, lines - step + 1))
@@ -551,6 +578,7 @@
         piece = width // CHUNKS
         far = lines - 1
         spot, at = jnp.reshape(place, (1,)), jnp.stack([me, place])
+        me_now = jnp.reshape(me, (1,))
         barrier = lax.optimization_barrier
         near = [offset for offset in range(-far, far + 1) if abs(offset) < far]
 
@@ -568,58 +596,78 @@
             (right_basis, before, grads[-far], grads[far])
         )
         rights = {0: own}
-        right = jnp.zeros(((lines + 1) * depth, width), BF16)
-
-        def put(right, offset):
-            there = place + offset
-            there = jnp.where((there >= 0) & (there < lines), there, lines)
-            return lax.dynamic_update_slice_in_dim(right, rights[offset], there * depth, 0)
-
         for step in range(1, lines):
             walk(rights, step)
         above, below = rights[far], rights[-far]
 
         pair, message = pack(halfway(spot, left, grads, [-far, far], lines, before))
         message, rights[-1], rights[1] = barrier((message, rights[-1], rights[1]))
-        pieces = by_distance(message)
-        right = put(put(put(right, 0), -1), 1)
-        right, pieces[cols - 2] = barrier((right, pieces[cols - 2]))
-        for step in range(2, far if depth == width else lines):
-            right = put(put(right, -step), step)
-        pieces = [pair] + [unpack(pieces[distance]) for distance in range(1, cols)]
-        part = rotate_part(at, pieces, right)
+        aligned = depth == width
+
+        def put_block(held, offset):
+            there = place + offset
+            there = jnp.where((there >= 0) & (there < lines), there, lines)
+            return put(jnp.reshape(there, (1,)), rights[offset], held, lines + 1)
+
+        held = None
+        for offset in (0, -1, 1):
+            held = put_block(held, offset)
+        pieces = {1: swap(message, 1)}
+        mate_pair = unpack(pieces[1])
+        for distance in range(2, cols, 2):
+            pieces[distance] = after(swap(message, distance), held[1], mate_pair)
+            pieces[distance + 1] = swap(pieces[distance], 1)
+        for step in range(2, far if aligned else lines):
+            held = put_block(put_block(held, -step), step)
+        pieces = [pair, mate_pair] + [unpack(pieces[distance]) for distance in range(2, cols)]
+        part = rotate_part(at, pieces, held[0], far if aligned else -1)
         part, above, below = barrier((part, above, below))
-        if depth != width:
-            above_now, below_now = jnp.zeros_like(above), jnp.zeros_like(below)
-        else:
-            above_now, below_now = above, below
+        if not aligned:
+            above, below = jnp.zeros_like(above), jnp.zeros_like(below)
         new_first, new_second, normed = rotate(
-            at, part, pieces, above_now, below_now, first_moment, second_moment, lines
+            at, part, pieces, above, below, first_moment, second_moment, lines
         )
-
-        def pass_on(product, arrived, step):
-            upward, downward = hop(spot, product, arrived, lines, step)
-            return up(upward, range(0, step)), down(downward, range(lines - step, lines))
-
-        products, arrived = [], []
+        if aligned:
+            last = jnp.where(place == 0, above, below)
+            there = jnp.where((place == 0) | (place == far), far - place, lines)
+            held = put(jnp.reshape(there, (1,)), last, held, lines + 1)
+        flipped = held[1]
+
+        keeps, products, sent, hops = [], [], [], {}
+
+        def running(chunk, step):
+            if step > 1:
+                upward, downward = running(chunk, step - 1)
+                before = (
+                    up(upward, range(0, step - 1)),
+                    down(downward, range(lines - step + 1, lines)),
+                )
+            if (chunk, step) not in hops:
+                arrived = () if step == 1 else before
+                hops[chunk, step] = hop(spot, products[chunk], arrived, lines, step)
+            return hops[chunk, step]
+
         for chunk in range(CHUNKS):
-            if chunk >= 2:
-                step = chunk - 1
-                if step > 1 and step < lines:
-                    arrived[0] = pass_on(products[0], arrived[0], step)
-                normed, arrived[0] = barrier((normed, arrived[0]))
-            keep, mate = restore(at, normed, right, above, below, cols, lines, chunk, piece)
+            ready = after(normed, *sent[-1]) if chunk else normed
+            keep, mate = restore(me_now, ready, flipped, cols, chunk, piece)
             mate = swap(mate, 1)
-            crossed = [
-                swap(send(keep, mate, distance, []), distance) for distance in range(2, cols, 2)
+            if chunk:
+                mate = after(mate, *running(chunk - 1, 1))
+            sent.append([send(keep, mate, distance, []) for distance in range(2, cols, 2)])
+            crossed = [swap(code, 2 * index + 2) for index, code in enumerate(sent[-1])]
+            due = [
+                message
+                for earlier in range(max(0, chunk - 2), chunk)
+                if chunk - earlier + 1 < lines
+                for message in running(earlier, chunk - earlier + 1)
             ]
+            if due and crossed:
+                crossed[0] = after(crossed[0], *due)
             products.append(expand(keep, mate, crossed, left))
-            arrived.append(pass_on(products[chunk], (), 1))
-        for step in range(2, lines):
-            for chunk, product in enumerate(products):
-                if chunk == 0 and step < CHUNKS - 1:
-                    continue
-                arrived[chunk] = pass_on(product, arrived[chunk], step)
+        arrived = []
+        for chunk in range(CHUNKS):
+            upward, downward = running(chunk, far)
+            arrived.append((up(upward, range(0, far)), down(downward, range(1, lines))))
         update = None
         for chunk, product in enumerate(products):
             update = finish(spot, product, arrived[chunk], update, chunk, depth, width)

time: 579 us -> 573 us (0.990)
  Pallas kernels: 201 us -> 226 us
  waiting for transfers between devices: 237 us -> 218 us
  local copies, waits for them, and re-layouts: 40.5 us -> 29.5 us
    ppermute x14, waiting for transfers between devices: 106 us -> 75.5 us  [swap(): return lax.ppermute(value, 'col', [(i, i ^ distance) for i in range(cols)])]
    ppermute x18, waiting for transfers between devices: 35.4 us -> 61.3 us  [up(): return lax.ppermute(value, 'row', [(i, i + 1) for i in senders])]
    pallas_call x4 -> x10, Pallas kernels: 36.8 us -> 59.3 us  [the longest x4 33.4 us: restore(): pl.pallas_call(functools.partial(restore_kernel, cols=cols), grid_spec=pl...]
    ppermute x18, waiting for transfers between devices: 95.2 us -> 81.5 us  [down(): return lax.ppermute(value, 'row', [(i, i - 1) for i in senders])]
    dynamic_update_slice x5 -> x0, local copies, waits for them, and re-layouts: 10.6 us -> none  [put(): lax.dynamic_update_slice_in_dim(right, rights[offset], there * depth, 0)]
    unnamed x52 -> x46, local copies, waits for them, and re-layouts: 17.6 us -> 22.5 us
  transfers between devices with their start and end apart: 50 -> 50, of which waited for: 20 -> 20; matrix products, arithmetic and copies ran while one was open for 4% -> 1% of each run, Pallas kernels for 28% -> 32%
where the time goes in v9:
time: 573 us; the launch traced here: 569 us
  Pallas kernels  226 us (39%)
  waiting for transfers between devices  218 us (38%)
  starting transfers between devices  91.7 us (16%)
  local copies, waits for them, and re-layouts  29.5 us (5%)
    ppermute x18, waiting for transfers between devices, down(): return lax.ppermute(value, 'row', [(i, i - 1) for i in senders])  81.5 us
    ppermute x14, waiting for transfers between devices, swap(): return lax.ppermute(value, 'col', [(i, i ^ distance) for i in range(cols)])  75.5 us
    ppermute x18, starting transfers between devices, up(): return lax.ppermute(value, 'row', [(i, i + 1) for i in senders])  63 us
    ppermute x18, waiting for transfers between devices, up(): return lax.ppermute(value, 'row', [(i, i + 1) for i in senders])  61.3 us
    pallas_call x4, Pallas kernels, expand(): pl.pallas_call(functools.partial(expand_kernel, tile=min(64, depth)), gri...  37.6 us
    pallas_call x4, Pallas kernels, restore(): pl.pallas_call(functools.partial(restore_kernel, cols=cols), grid_spec=pl...  33.4 us
    pallas_call x12, Pallas kernels, hop(): pl.pallas_call(functools.partial(hop_kernel, lines=lines, step=step, tile...  31.2 us
    pallas_call x6, Pallas kernels, put(): pl.pallas_call(put_kernel, grid_spec=pltpu.PrefetchScalarGridSpec(num_sca...  25.8 us
  transfers between devices with their start and end apart: 50, of which 20 were waited for; matrix products, arithmetic and copies ran while one was open for 1% of the time, Pallas kernels for 32%

profile of v9, /device:TPU:0, one launch (start us, length us, event | category | flops | bytes accessed | tf_op | source)
XLA Modules:
  0.0 568.8 jit_solution(53671287084328313)
XLA Ops:
  0.6 3.0 collective-permute-start
  3.6 3.6 collective-permute-start.3
  8.6 41.0 %collective-permute-done = bf16[1024,1024]{1,0:T(8,128)(2,1)} collective-permute-done((bf16[1024,1024]{1,0:T(8,128)(2,1)}, bf16[1024,1024]{1,0:T(8,128)(2,1)}, u32[]{:S(2)}, u32[]{:S(2)}) %collective-permute-start) | collective-permute-done | bytes 2097184 | tf_op jit(solution)/shard_map/ppermute | solution.py:546
  49.6 2.4 collective-permute-done.3.refs_1_
  54.0 2.2 collective-permute-done.5.refs_3_
  65.1 3.3 copy-done.20
  68.4 37.3 %collective-permute-done.6.refs_4_ = bf16[1024,1024]{1,0:T(8,128)(2,1)} collective-permute-done((bf16[1024,1024]{1,0:T(8,128)(2,1)}, bf16[1024,1024]{1,0:T(8,128)(2,1)}, u32[]{:S(2)}, u32[]{:S(2)}) %collective-permute-start.6) | collective-permute-done | bytes 2097184 | tf_op jit(solution)/shard_map/ppermute | solution.py:566
  109.0 14.7 %halfway.2.refs_2_ = f32[1024,1024]{1,0:T(8,128)} custom-call(s32[1]{0:T(128)} %bitcast.1.place_ref.at_ref, bf16[4096,1024]{1,0:T(8,128)(2,1)} %bitcast.17, bf16[1024,1024]{1,0:T(8,128)(2,1)} %collective-permute-done.4.refs_0_, bf16[1024,1024]{1,0:T(8,128)(2,1)S(1)} %collective-permute-done.3.refs_1_, bf16[1024,1024]{1,0:T(8,128)(2,1)} %refs_2_.1, ...), custom_call_target="tpu_custom_call" | custom-call | flops 2576980480 | bytes 2516582 | tf_op jit(solution)/shard_map/halfway/pallas_call | solution.py:114
  123.7 31.6 %collective-permute-done.8.refs_1_ = bf16[1024,1024]{1,0:T(8,128)(2,1)} collective-permute-done((bf16[1024,1024]{1,0:T(8,128)(2,1)}, bf16[1024,1024]{1,0:T(8,128)(2,1)}, u32[]{:S(2)}, u32[]{:S(2)}) %collective-permute-start.8) | collective-permute-done | bytes 2097184 | tf_op jit(solution)/shard_map/ppermute | solution.py:566
  155.2 2.7 collective-permute-start.9
  159.3 9.6 %halfway.3.value = f32[1024,1024]{1,0:T(8,128)} custom-call(s32[1]{0:T(128)} %bitcast.1.place_ref.at_ref, bf16[4096,1024]{1,0:T(8,128)(2,1)} %bitcast.18, bf16[1024,1024]{1,0:T(8,128)(2,1)} %collective-permute-done.7.refs_0_, bf16[1024,1024]{1,0:T(8,128)(2,1)} %collective-permute-done.8.refs_1_, f32[1024,1024]{1,0:T(8,128)} %halfway.2.refs_2_), custom_call_target="tpu_custom_call" | custom-call | flops 2576980480 | bytes 2516582 | tf_op jit(solution)/shard_map/halfway/pallas_call | solution.py:114
  168.9 7.9 %pack.1 = (bf16[2,1024,1024]{2,1,0:T(8,128)(2,1)}, bf16[1040,1024]{1,0:T(8,128)(2,1)}) custom-call(f32[1024,1024]{1,0:T(8,128)} %halfway.3.value), custom_call_target="tpu_custom_call" | custom-call | flops 125829120 | bytes 3145728 | tf_op jit(solution)/shard_map/pack/pallas_call | solution.py:147
  176.8 22.3 %collective-permute-done.9.piece = bf16[1024,1024]{1,0:T(8,128)(2,1)} collective-permute-done((bf16[1024,1024]{1,0:T(8,128)(2,1)}, bf16[1024,1024]{1,0:T(8,128)(2,1)}, u32[]{:S(2)}, u32[]{:S(2)}) %collective-permute-start.9) | collective-permute-done | bytes 2097184 | tf_op jit(solution)/shard_map/ppermute | solution.py:563
  199.1 5.4 collective-permute-done.10.piece
  208.3 4.3 put.6
  212.6 4.3 put.7
  216.8 4.3 put.8
  222.5 6.1 %unpack.3.refs_1_ = bf16[2,1024,1024]{2,1,0:T(8,128)(2,1)} custom-call(bf16[1040,1024]{1,0:T(8,128)(2,1)} %copy-done.21, bf16[1040,1024]{1,0:T(8,128)(2,1)} %copy-done.21), custom_call_target="tpu_custom_call" | custom-call | flops 125829120 | bytes 1887436 | tf_op jit(solution)/shard_map/unpack/pallas_call | solution.py:176
  228.6 24.9 %collective-permute-done.12.message.scales = bf16[1040,1024]{1,0:T(8,128)(2,1)} collective-permute-done((bf16[1040,1024]{1,0:T(8,128)(2,1)}, bf16[1040,1024]{1,0:T(8,128)(2,1)}, u32[]{:S(2)}, u32[]{:S(2)}) %collective-permute-start.12) | collective-permute-done | bytes 2129952 | tf_op jit(solution)/shard_map/ppermute | solution.py:546
  258.3 4.3 put.9
  262.6 4.3 put.10
  266.9 6.0 %unpack.4.refs_2_ = bf16[2,1024,1024]{2,1,0:T(8,128)(2,1)} custom-call(bf16[1040,1024]{1,0:T(8,128)(2,1)} %collective-permute-done.12.message.scales, bf16[1040,1024]{1,0:T(8,128)(2,1)} %collective-permute-done.12.message.scales), custom_call_target="tpu_custom_call" | custom-call | flops 125829120 | bytes 1887436 | tf_op jit(solution)/shard_map/unpack/pallas_call | solution.py:176
  272.9 6.1 %unpack.5.refs_3_ = bf16[2,1024,1024]{2,1,0:T(8,128)(2,1)} custom-call(bf16[1040,1024]{1,0:T(8,128)(2,1)} %collective-permute-done.13.message.scales, bf16[1040,1024]{1,0:T(8,128)(2,1)} %collective-permute-done.13.message.scales), custom_call_target="tpu_custom_call" | custom-call | flops 125829120 | bytes 1887436 | tf_op jit(solution)/shard_map/unpack/pallas_call | solution.py:176
  279.0 21.4 %rotate_part.1.part = f32[1024,1024]{1,0:T(8,128)S(1)} custom-call(s32[2]{0:T(128)S(1)} %pad_add_fusion.at_ref, bf16[2,1024,1024]{2,1,0:T(8,128)(2,1)} %get-tuple-element.80.refs_0_, bf16[2,1024,1024]{2,1,0:T(8,128)(2,1)} %unpack.3.refs_1_, bf16[2,1024,1024]{2,1,0:T(8,128)(2,1)} %unpack.4.refs_2_, bf16[2,1024,1024]{2,1,0:T(8,128)(2,1)} %unpack.5.refs_3_, ...), custom_call_target="tpu_custom_call" | custom-call | flops 5153960960 | bytes 6291456 | tf_op jit(solution)/shard_map/rotate_part/pallas_call | solution.py:244
  300.4 3.6 collective-permute-done.16.above
  305.5 13.6 %rotate.1 = (f32[1024,1024]{1,0:T(8,128)}, f32[1024,1024]{1,0:T(8,128)}, bf16[2,1024,1024]{2,1,0:T(8,128)(2,1)S(1)}) custom-call(s32[2]{0:T(128)S(1)} %pad_add_fusion.at_ref, f32[1024,1024]{1,0:T(8,128)S(1)} %rotate_part.1.part, bf16[1024,1024]{1,0:T(8,128)(2,1)S(1)} %collective-permute-done.16.above, bf16[1024,1024]{1,0:T(8,128)(2,1)} %collective-permute-done.17.below, ...), custom_call_target="tpu_custom_call" | custom-call | flops 17179869184 | bytes 125829120 | tf_op jit(solution)/shard_map/rotate/pallas_call | solution.py:320
  321.1 4.3 put.11
  325.4 8.4 %restore.4 = (f32[2,1024,256]{2,1,0:T(8,128)}, f32[2,1024,256]{2,1,0:T(8,128)}) custom-call(s32[1]{0:T(128)} %bitcast.me_ref, bf16[2,1024,1024]{2,1,0:T(8,128)(2,1)} %copy-done.19, bf16[5,1024,1024]{2,1,0:T(8,128)(2,1)} %get-tuple-element.103.refs_0_.refs_1_.refs_2_.refs_3_, bf16[5,1024,1024]{2,1,0:T(8,128)(2,1)} %get-tuple-element.103.refs_0_.refs_1_.refs_2_.refs_3_, ...), custom_call_target="tpu_custom_call" | custom-call | flops 17179869184 | bytes 33554432 | tf_op jit(solution)/shard_map/restore/pallas_call | solution.py:367
  333.8 4.4 collective-permute-done.18.mate
  338.2 2.3 copy-done.15
  342.9 8.3 %restore.5 = (f32[2,1024,256]{2,1,0:T(8,128)}, f32[2,1024,256]{2,1,0:T(8,128)}) custom-call(s32[1]{0:T(128)} %bitcast.me_ref, bf16[2,1024,1024]{2,1,0:T(8,128)(2,1)} %copy-done.19, bf16[5,1024,1024]{2,1,0:T(8,128)(2,1)} %get-tuple-element.103.refs_0_.refs_1_.refs_2_.refs_3_, bf16[5,1024,1024]{2,1,0:T(8,128)(2,1)} %get-tuple-element.103.refs_0_.refs_1_.refs_2_.refs_3_, ...), custom_call_target="tpu_custom_call" | custom-call | flops 17179869184 | bytes 33554432 | tf_op jit(solution)/shard_map/restore/pallas_call | solution.py:367
  351.3 4.3 collective-permute-done.20.refs_0_
  357.2 9.4 %expand.4.refs_0_.refs_1_.block = f32[4096,256]{1,0:T(8,128)} custom-call(f32[2,1024,256]{2,1,0:T(8,128)S(1)} %copy-done.16, f32[2,1024,256]{2,1,0:T(8,128)S(1)} %copy-done.18, bf16[1040,256]{1,0:T(8,128)(2,1)S(1)} %collective-permute-done.20.refs_0_, bf16[4096,1024]{1,0:T(8,128)(2,1)} %bitcast.19), custom_call_target="tpu_custom_call" | custom-call | flops 17179869184 | bytes 50331648 | tf_op jit(solution)/shard_map/expand/pallas_call | solution.py:446
  370.4 7.1 %collective-permute-start.23 = (bf16[1040,256]{1,0:T(8,128)(2,1)}, bf16[1040,256]{1,0:T(8,128)(2,1)S(1)}, u32[]{:S(2)}, u32[]{:S(2)}) collective-permute-start(bf16[1040,256]{1,0:T(8,128)(2,1)} %get-tuple-element.109), channel_id=1, source_target_pairs={{0,4},{1,5},{2,6},{3,7},{16,20},{17,21},{18,22},{19,23}} | collective-permute-start | bytes 1597448 | tf_op jit(solution)/shard_map/ppermute | solution.py:563
  382.1 8.3 %restore.6 = (f32[2,1024,256]{2,1,0:T(8,128)}, f32[2,1024,256]{2,1,0:T(8,128)}) custom-call(s32[1]{0:T(128)} %bitcast.me_ref, bf16[2,1024,1024]{2,1,0:T(8,128)(2,1)} %copy-done.19, bf16[5,1024,1024]{2,1,0:T(8,128)(2,1)} %get-tuple-element.103.refs_0_.refs_1_.refs_2_.refs_3_, bf16[5,1024,1024]{2,1,0:T(8,128)(2,1)} %get-tuple-element.103.refs_0_.refs_1_.refs_2_.refs_3_, ...), custom_call_target="tpu_custom_call" | custom-call | flops 17179869184 | bytes 33554432 | tf_op jit(solution)/shard_map/restore/pallas_call | solution.py:367
  390.5 4.1 hop.13
  394.6 2.3 collective-permute-start.27
  397.6 9.5 %expand.5.refs_0_.refs_1_.block = f32[4096,256]{1,0:T(8,128)} custom-call(f32[2,1024,256]{2,1,0:T(8,128)S(1)} %copy-done.12, f32[2,1024,256]{2,1,0:T(8,128)S(1)} %copy-done.14, bf16[1040,256]{1,0:T(8,128)(2,1)} %collective-permute-done.22.refs_0_, bf16[4096,1024]{1,0:T(8,128)(2,1)} %bitcast.20), custom_call_target="tpu_custom_call" | custom-call | flops 17179869184 | bytes 50331648 | tf_op jit(solution)/shard_map/expand/pallas_call | solution.py:446
  411.0 4.5 collective-permute-start.29
  421.5 8.4 %restore.7 = (f32[2,1024,256]{2,1,0:T(8,128)}, f32[2,1024,256]{2,1,0:T(8,128)}) custom-call(s32[1]{0:T(128)} %bitcast.me_ref, bf16[2,1024,1024]{2,1,0:T(8,128)(2,1)} %copy-done.19, bf16[5,1024,1024]{2,1,0:T(8,128)(2,1)} %get-tuple-element.103.refs_0_.refs_1_.refs_2_.refs_3_, bf16[5,1024,1024]{2,1,0:T(8,128)(2,1)} %get-tuple-element.103.refs_0_.refs_1_.refs_2_.refs_3_, ...), custom_call_target="tpu_custom_call" | custom-call | flops 17179869184 | bytes 33554432 | tf_op jit(solution)/shard_map/restore/pallas_call | solution.py:367
  429.9 3.8 hop.15
  433.7 3.3 hop.16
  437.0 2.7 collective-permute-start.32
  440.5 9.4 %expand.6.refs_0_.refs_1_.block = f32[4096,256]{1,0:T(8,128)} custom-call(f32[2,1024,256]{2,1,0:T(8,128)S(1)} %copy-done.8, f32[2,1024,256]{2,1,0:T(8,128)S(1)} %copy-done.11, bf16[1040,256]{1,0:T(8,128)(2,1)} %collective-permute-done.26.refs_0_, bf16[4096,1024]{1,0:T(8,128)(2,1)} %bitcast.21), custom_call_target="tpu_custom_call" | custom-call | flops 17179869184 | bytes 50331648 | tf_op jit(solution)/shard_map/expand/pallas_call | solution.py:446
  452.9 3.7 collective-permute-start.34
  458.8 3.0 hop.18
  461.8 6.5 %collective-permute-done.34.refs_2_ = bf16[1040,256]{1,0:T(8,128)(2,1)S(1)} collective-permute-done((bf16[1040,256]{1,0:T(8,128)(2,1)S(1)}, bf16[1040,256]{1,0:T(8,128)(2,1)S(1)}, u32[]{:S(2)}, u32[]{:S(2)}) %collective-permute-start.34) | collective-permute-done | bytes 532512 | tf_op jit(solution)/shard_map/ppermute | solution.py:563
  468.3 3.0 hop.19
  472.2 9.3 %expand.7.refs_0_.refs_1_.block = f32[4096,256]{1,0:T(8,128)} custom-call(f32[2,1024,256]{2,1,0:T(8,128)S(1)} %copy-done.9, f32[2,1024,256]{2,1,0:T(8,128)S(1)} %collective-permute-done.25.mate, bf16[1040,256]{1,0:T(8,128)(2,1)S(1)} %collective-permute-done.31.refs_0_, bf16[4096,1024]{1,0:T(8,128)(2,1)} %bitcast.22), custom_call_target="tpu_custom_call" | custom-call | flops 17179869184 | bytes 50331648 | tf_op jit(solution)/shard_map/expand/pallas_call | solution.py:446
  484.5 2.8 collective-permute-start.36
  489.3 4.9 collective-permute-start.42
  495.0 4.8 collective-permute-done.36.refs_2_
  499.8 3.0 hop.21
  502.8 4.4 collective-permute-start.38
  507.9 3.3 collective-permute-done.48.up
  512.5 10.1 %collective-permute-done.42.refs_2_ = bf16[1040,256]{1,0:T(8,128)(2,1)S(1)} collective-permute-done((bf16[1040,256]{1,0:T(8,128)(2,1)S(1)}, bf16[1040,256]{1,0:T(8,128)(2,1)S(1)}, u32[]{:S(2)}, u32[]{:S(2)}) %collective-permute-start.42) | collective-permute-done | bytes 532512 | tf_op jit(solution)/shard_map/ppermute | solution.py:563
  522.6 4.4 collective-permute-start.46
  528.3 3.0 hop.23
  531.3 2.7 collective-permute-done.38.refs_2_
  534.0 4.4 collective-permute-start.44
  540.0 3.0 hop.22
  543.0 6.0 %collective-permute-start.40 = (bf16[1040,256]{1,0:T(8,128)(2,1)S(1)}, bf16[1040,256]{1,0:T(8,128)(2,1)S(1)}, u32[]{:S(2)}, u32[]{:S(2)}) collective-permute-start(bf16[1040,256]{1,0:T(8,128)(2,1)S(1)} %get-tuple-element.141), channel_id=1, source_target_pairs={{0,4},{4,8},{8,12},{1,5},{5,9},{9,13},{2,6},{6,10},{10,14},{3,7},{... | collective-permute-start | bytes 1597448 | tf_op jit(solution)/shard_map/ppermute | solution.py:563
  550.7 2.2 finish.4.refs_0_
  559.1 7.5 %collective-permute-done.40.up = bf16[1040,256]{1,0:T(8,128)(2,1)S(1)} collective-permute-done((bf16[1040,256]{1,0:T(8,128)(2,1)S(1)}, bf16[1040,256]{1,0:T(8,128)(2,1)S(1)}, u32[]{:S(2)}, u32[]{:S(2)}) %collective-permute-start.40) | collective-permute-done | bytes 532512 | tf_op jit(solution)/shard_map/ppermute | solution.py:563
  (131 shorter events, 80.1 us)
Async XLA Ops:
  0.6 49.0 %collective-permute-start = (bf16[1024,1024]{1,0:T(8,128)(2,1)}, bf16[1024,1024]{1,0:T(8,128)(2,1)}, u32[]{:S(2)}, u32[]{:S(2)}) collective-permute-start(bf16[1024,1024]{1,0:T(8,128)(2,1)} %param.8), channel_id=1, source_target_pairs={{0,2},{1,3},{2,0},{3,1},{4,6},{5,7},{6,4},{7,5},{8,10},{9,11},{10,... | collective-permute-start | bytes 6291464 | tf_op jit(solution)/shard_map/ppermute | solution.py:546
  3.6 48.4 %collective-permute-start.3 = (bf16[1024,1024]{1,0:T(8,128)(2,1)}, bf16[1024,1024]{1,0:T(8,128)(2,1)S(1)}, u32[]{:S(2)}, u32[]{:S(2)}) collective-permute-start(bf16[1024,1024]{1,0:T(8,128)(2,1)} %refs_2_.1), channel_id=1, source_target_pairs={{0,4},{4,8},{8,12},{1,5},{5,9},{9,13},{2,6},{6,10},{10,14},{3,7},{... | collective-permute-start | bytes 6291464 | tf_op jit(solution)/shard_map/ppermute | solution.py:563
  7.2 49.0 %collective-permute-start.5 = (bf16[1024,1024]{1,0:T(8,128)(2,1)}, bf16[1024,1024]{1,0:T(8,128)(2,1)}, u32[]{:S(2)}, u32[]{:S(2)}) collective-permute-start(bf16[1024,1024]{1,0:T(8,128)(2,1)} %refs_2_.1), channel_id=1, source_target_pairs={{4,0},{8,4},{12,8},{5,1},{9,5},{13,9},{6,2},{10,6},{14,10},{7,3},{... | collective-permute-start | bytes 6291464 | tf_op jit(solution)/shard_map/ppermute | solution.py:566
  8.5 52.8 %collective-permute-start.1 = (bf16[1024,1024]{1,0:T(8,128)(2,1)}, bf16[1024,1024]{1,0:T(8,128)(2,1)}, u32[]{:S(2)}, u32[]{:S(2)}) collective-permute-start(bf16[1024,1024]{1,0:T(8,128)(2,1)} %param.8), channel_id=1, source_target_pairs={{0,1},{1,0},{2,3},{3,2},{4,5},{5,4},{6,7},{7,6},{8,9},{9,8},{10,11... | collective-permute-start | bytes 6291464 | tf_op jit(solution)/shard_map/ppermute | solution.py:546
  49.6 13.6 %collective-permute-start.2 = (bf16[1024,1024]{1,0:T(8,128)(2,1)}, bf16[1024,1024]{1,0:T(8,128)(2,1)}, u32[]{:S(2)}, u32[]{:S(2)}) collective-permute-start(bf16[1024,1024]{1,0:T(8,128)(2,1)} %collective-permute-done), channel_id=1, source_target_pairs={{0,1},{1,0},{2,3},{3,2},{4,5},{5,4},{6,7},{7,6},{8,9},{9,8},{10,11... | collective-permute-start | bytes 6291464 | tf_op jit(solution)/shard_map/ppermute | solution.py:546
  52.0 13.1 %collective-permute-start.4 = (bf16[1024,1024]{1,0:T(8,128)(2,1)S(1)}, bf16[1024,1024]{1,0:T(8,128)(2,1)}, u32[]{:S(2)}, u32[]{:S(2)}) collective-permute-start(bf16[1024,1024]{1,0:T(8,128)(2,1)S(1)} %collective-permute-done.3.refs_1_), channel_id=1, source_target_pairs={{4,8},{8,12},{5,9},{9,13},{6,10},{10,14},{7,11},{11,15},{20,24},{2... | collective-permute-start | bytes 6291464 | tf_op jit(solution)/shard_map/ppermute | solution.py:563
  56.3 49.4 %collective-permute-start.6 = (bf16[1024,1024]{1,0:T(8,128)(2,1)}, bf16[1024,1024]{1,0:T(8,128)(2,1)}, u32[]{:S(2)}, u32[]{:S(2)}) collective-permute-start(bf16[1024,1024]{1,0:T(8,128)(2,1)} %collective-permute-done.5.refs_3_), channel_id=1, source_target_pairs={{4,0},{8,4},{5,1},{9,5},{6,2},{10,6},{7,3},{11,7},{20,16},{24,20},... | collective-permute-start | bytes 6291464 | tf_op jit(solution)/shard_map/ppermute | solution.py:566
  65.1 3.3 copy-start.20
  105.7 18.0 %collective-permute-start.7 = (bf16[1024,1024]{1,0:T(8,128)(2,1)}, bf16[1024,1024]{1,0:T(8,128)(2,1)}, u32[]{:S(2)}, u32[]{:S(2)}) collective-permute-start(bf16[1024,1024]{1,0:T(8,128)(2,1)} %collective-permute-done.4.refs_0_), channel_id=1, source_target_pairs={{8,12},{9,13},{10,14},{11,15},{24,28},{25,29},{26,30},{27,31}} | collective-permute-start | bytes 6291464 | tf_op jit(solution)/shard_map/ppermute | solution.py:563
  107.7 47.6 %collective-permute-start.8 = (bf16[1024,1024]{1,0:T(8,128)(2,1)}, bf16[1024,1024]{1,0:T(8,128)(2,1)}, u32[]{:S(2)}, u32[]{:S(2)}) collective-permute-start(bf16[1024,1024]{1,0:T(8,128)(2,1)} %collective-permute-done.6.refs_4_), channel_id=1, source_target_pairs={{4,0},{5,1},{6,2},{7,3},{20,16},{21,17},{22,18},{23,19}} | collective-permute-start | bytes 6291464 | tf_op jit(solution)/shard_map/ppermute | solution.py:566
  155.2 43.8 %collective-permute-start.9 = (bf16[1024,1024]{1,0:T(8,128)(2,1)}, bf16[1024,1024]{1,0:T(8,128)(2,1)}, u32[]{:S(2)}, u32[]{:S(2)}) collective-permute-start(bf16[1024,1024]{1,0:T(8,128)(2,1)} %piece), channel_id=1, source_target_pairs={{0,4},{4,8},{8,12},{1,5},{5,9},{9,13},{2,6},{6,10},{10,14},{3,7},{... | collective-permute-start | bytes 6291464 | tf_op jit(solution)/shard_map/ppermute | solution.py:563
  158.0 46.5 %collective-permute-start.10 = (bf16[1024,1024]{1,0:T(8,128)(2,1)}, bf16[1024,1024]{1,0:T(8,128)(2,1)}, u32[]{:S(2)}, u32[]{:S(2)}) collective-permute-start(bf16[1024,1024]{1,0:T(8,128)(2,1)} %piece), channel_id=1, source_target_pairs={{4,0},{8,4},{12,8},{5,1},{9,5},{13,9},{6,2},{10,6},{14,10},{7,3},{... | collective-permute-start | bytes 6291464 | tf_op jit(solution)/shard_map/ppermute | solution.py:566
  204.5 16.7 %collective-permute-start.11 = (bf16[1040,1024]{1,0:T(8,128)(2,1)}, bf16[1040,1024]{1,0:T(8,128)(2,1)S(1)}, u32[]{:S(2)}, u32[]{:S(2)}) collective-permute-start(bf16[1040,1024]{1,0:T(8,128)(2,1)} %get-tuple-element.83), channel_id=1, source_target_pairs={{0,1},{1,0},{2,3},{3,2},{4,5},{5,4},{6,7},{7,6},{8,9},{9,8},{10,11... | collective-permute-start | bytes 6389768 | tf_op jit(solution)/shard_map/ppermute | solution.py:546
  204.5 49.1 %collective-permute-start.12 = (bf16[1040,1024]{1,0:T(8,128)(2,1)}, bf16[1040,1024]{1,0:T(8,128)(2,1)}, u32[]{:S(2)}, u32[]{:S(2)}) collective-permute-start(bf16[1040,1024]{1,0:T(8,128)(2,1)} %get-tuple-element.83), channel_id=1, source_target_pairs={{0,2},{1,3},{2,0},{3,1},{4,6},{5,7},{6,4},{7,5},{8,10},{9,11},{10,... | collective-permute-start | bytes 6389768 | tf_op jit(solution)/shard_map/ppermute | solution.py:546
  205.0 50.0 %collective-permute-start.14 = (bf16[1024,1024]{1,0:T(8,128)(2,1)}, bf16[1024,1024]{1,0:T(8,128)(2,1)}, u32[]{:S(2)}, u32[]{:S(2)}) collective-permute-start(bf16[1024,1024]{1,0:T(8,128)(2,1)} %collective-permute-done.10.piece), channel_id=1, source_target_pairs={{4,0},{8,4},{5,1},{9,5},{6,2},{10,6},{7,3},{11,7},{20,16},{24,20},... | collective-permute-start | bytes 6291464 | tf_op jit(solution)/shard_map/ppermute | solution.py:566
  206.3 50.0 %collective-permute-start.15 = (bf16[1024,1024]{1,0:T(8,128)(2,1)}, bf16[1024,1024]{1,0:T(8,128)(2,1)}, u32[]{:S(2)}, u32[]{:S(2)}) collective-permute-start(bf16[1024,1024]{1,0:T(8,128)(2,1)} %collective-permute-done.9.piece), channel_id=1, source_target_pairs={{4,8},{8,12},{5,9},{9,13},{6,10},{10,14},{7,11},{11,15},{20,24},{2... | collective-permute-start | bytes 6291464 | tf_op jit(solution)/shard_map/ppermute | solution.py:563
  253.5 19.4 %collective-permute-start.13 = (bf16[1040,1024]{1,0:T(8,128)(2,1)}, bf16[1040,1024]{1,0:T(8,128)(2,1)}, u32[]{:S(2)}, u32[]{:S(2)}) collective-permute-start(bf16[1040,1024]{1,0:T(8,128)(2,1)} %collective-permute-done.12.message.scales), channel_id=1, source_target_pairs={{0,1},{1,0},{2,3},{3,2},{4,5},{5,4},{6,7},{7,6},{8,9},{9,8},{10,11... | collective-permute-start | bytes 6389768 | tf_op jit(solution)/shard_map/ppermute | solution.py:546
  255.0 49.0 %collective-permute-start.16 = (bf16[1024,1024]{1,0:T(8,128)(2,1)}, bf16[1024,1024]{1,0:T(8,128)(2,1)S(1)}, u32[]{:S(2)}, u32[]{:S(2)}) collective-permute-start(bf16[1024,1024]{1,0:T(8,128)(2,1)} %collective-permute-done.14.piece), channel_id=1, source_target_pairs={{4,0},{5,1},{6,2},{7,3},{20,16},{21,17},{22,18},{23,19}} | collective-permute-start | bytes 6291464 | tf_op jit(solution)/shard_map/ppermute | solution.py:566
  256.3 47.7 %collective-permute-start.17 = (bf16[1024,1024]{1,0:T(8,128)(2,1)}, bf16[1024,1024]{1,0:T(8,128)(2,1)}, u32[]{:S(2)}, u32[]{:S(2)}) collective-permute-start(bf16[1024,1024]{1,0:T(8,128)(2,1)} %collective-permute-done.15.piece), channel_id=1, source_target_pairs={{8,12},{9,13},{10,14},{11,15},{24,28},{25,29},{26,30},{27,31}} | collective-permute-start | bytes 6291464 | tf_op jit(solution)/shard_map/ppermute | solution.py:563
  333.8 4.4 collective-permute-start.18
  338.2 3.2 copy-start.17
  338.2 2.3 copy-start.15
  341.4 14.2 %copy-start.16 = (f32[2,1024,256]{2,1,0:T(8,128)S(1)}, f32[2,1024,256]{2,1,0:T(8,128)}, u32[]{:S(2)}) copy-start(f32[2,1024,256]{2,1,0:T(8,128)} %get-tuple-element.104.keep) | copy-start | bytes 6291460
  341.4 14.2 %collective-permute-start.20 = (bf16[1040,256]{1,0:T(8,128)(2,1)S(1)}, bf16[1040,256]{1,0:T(8,128)(2,1)S(1)}, u32[]{:S(2)}, u32[]{:S(2)}) collective-permute-start(bf16[1040,256]{1,0:T(8,128)(2,1)S(1)} %send.4), channel_id=1, source_target_pairs={{0,2},{1,3},{2,0},{3,1},{4,6},{5,7},{6,4},{7,5},{8,10},{9,11},{10,... | collective-permute-start | bytes 1597448 | tf_op jit(solution)/shard_map/ppermute | solution.py:546
  351.3 27.2 %collective-permute-start.19 = (f32[2,1024,256]{2,1,0:T(8,128)}, f32[2,1024,256]{2,1,0:T(8,128)S(1)}, u32[]{:S(2)}, u32[]{:S(2)}) collective-permute-start(f32[2,1024,256]{2,1,0:T(8,128)} %get-tuple-element.108), channel_id=1, source_target_pairs={{0,1},{1,0},{2,3},{3,2},{4,5},{5,4},{6,7},{7,6},{8,9},{9,8},{10,11... | collective-permute-start | bytes 6291464 | tf_op jit(solution)/shard_map/ppermute | solution.py:546
  366.5 2.2 copy-start
  368.7 9.8 %copy-start.12 = (f32[2,1024,256]{2,1,0:T(8,128)S(1)}, f32[2,1024,256]{2,1,0:T(8,128)}, u32[]{:S(2)}) copy-start(f32[2,1024,256]{2,1,0:T(8,128)} %get-tuple-element.107.keep) | copy-start | bytes 6291460
  370.4 20.0 %collective-permute-start.23 = (bf16[1040,256]{1,0:T(8,128)(2,1)}, bf16[1040,256]{1,0:T(8,128)(2,1)S(1)}, u32[]{:S(2)}, u32[]{:S(2)}) collective-permute-start(bf16[1040,256]{1,0:T(8,128)(2,1)} %get-tuple-element.109), channel_id=1, source_target_pairs={{0,4},{1,5},{2,6},{3,7},{16,20},{17,21},{18,22},{19,23}} | collective-permute-start | bytes 1597448 | tf_op jit(solution)/shard_map/ppermute | solution.py:563
  377.5 12.9 %collective-permute-start.24 = (bf16[1040,256]{1,0:T(8,128)(2,1)}, bf16[1040,256]{1,0:T(8,128)(2,1)S(1)}, u32[]{:S(2)}, u32[]{:S(2)}) collective-permute-start(bf16[1040,256]{1,0:T(8,128)(2,1)} %get-tuple-element.110), channel_id=1, source_target_pairs={{12,8},{13,9},{14,10},{15,11},{28,24},{29,25},{30,26},{31,27}} | collective-permute-start | bytes 1597448 | tf_op jit(solution)/shard_map/ppermute | solution.py:566
  380.6 17.0 %collective-permute-start.22 = (bf16[1040,256]{1,0:T(8,128)(2,1)S(1)}, bf16[1040,256]{1,0:T(8,128)(2,1)}, u32[]{:S(2)}, u32[]{:S(2)}) collective-permute-start(bf16[1040,256]{1,0:T(8,128)(2,1)S(1)} %send.5), channel_id=1, source_target_pairs={{0,2},{1,3},{2,0},{3,1},{4,6},{5,7},{6,4},{7,5},{8,10},{9,11},{10,... | collective-permute-start | bytes 1597448 | tf_op jit(solution)/shard_map/ppermute | solution.py:546
  390.4 7.2 %copy-start.14 = (f32[2,1024,256]{2,1,0:T(8,128)S(1)}, f32[2,1024,256]{2,1,0:T(8,128)}, u32[]{:S(2)}) copy-start(f32[2,1024,256]{2,1,0:T(8,128)} %copy-done.13) | copy-start | bytes 6291460
  390.4 26.6 %collective-permute-start.21 = (f32[2,1024,256]{2,1,0:T(8,128)}, f32[2,1024,256]{2,1,0:T(8,128)S(1)}, u32[]{:S(2)}, u32[]{:S(2)}) collective-permute-start(f32[2,1024,256]{2,1,0:T(8,128)} %get-tuple-element.114), channel_id=1, source_target_pairs={{0,1},{1,0},{2,3},{3,2},{4,5},{5,4},{6,7},{7,6},{8,9},{9,8},{10,11... | collective-permute-start | bytes 6291464 | tf_op jit(solution)/shard_map/ppermute | solution.py:546
  394.6 35.3 %collective-permute-start.27 = (bf16[1040,256]{1,0:T(8,128)(2,1)}, bf16[1040,256]{1,0:T(8,128)(2,1)S(1)}, u32[]{:S(2)}, u32[]{:S(2)}) collective-permute-start(bf16[1040,256]{1,0:T(8,128)(2,1)} %get-tuple-element.115), channel_id=1, source_target_pairs={{0,4},{4,8},{1,5},{5,9},{2,6},{6,10},{3,7},{7,11},{16,20},{20,24},... | collective-permute-start | bytes 1597448 | tf_op jit(solution)/shard_map/ppermute | solution.py:563
  396.9 33.0 %collective-permute-start.28 = (bf16[1040,256]{1,0:T(8,128)(2,1)}, bf16[1040,256]{1,0:T(8,128)(2,1)S(1)}, u32[]{:S(2)}, u32[]{:S(2)}) collective-permute-start(bf16[1040,256]{1,0:T(8,128)(2,1)} %get-tuple-element.116), channel_id=1, source_target_pairs={{8,4},{12,8},{9,5},{13,9},{10,6},{14,10},{11,7},{15,11},{24,20},{2... | collective-permute-start | bytes 1597448 | tf_op jit(solution)/shard_map/ppermute | solution.py:566
  409.3 7.8 %copy-start.8 = (f32[2,1024,256]{2,1,0:T(8,128)S(1)}, f32[2,1024,256]{2,1,0:T(8,128)}, u32[]{:S(2)}) copy-start(f32[2,1024,256]{2,1,0:T(8,128)} %get-tuple-element.113.keep) | copy-start | bytes 6291460
  411.0 22.7 %collective-permute-start.29 = (bf16[1040,256]{1,0:T(8,128)(2,1)}, bf16[1040,256]{1,0:T(8,128)(2,1)S(1)}, u32[]{:S(2)}, u32[]{:S(2)}) collective-permute-start(bf16[1040,256]{1,0:T(8,128)(2,1)} %get-tuple-element.118), channel_id=1, source_target_pairs={{0,4},{1,5},{2,6},{3,7},{16,20},{17,21},{18,22},{19,23}} | collective-permute-start | bytes 1597448 | tf_op jit(solution)/shard_map/ppermute | solution.py:563
  415.6 18.2 %collective-permute-start.30 = (bf16[1040,256]{1,0:T(8,128)(2,1)}, bf16[1040,256]{1,0:T(8,128)(2,1)}, u32[]{:S(2)}, u32[]{:S(2)}) collective-permute-start(bf16[1040,256]{1,0:T(8,128)(2,1)} %get-tuple-element.119), channel_id=1, source_target_pairs={{12,8},{13,9},{14,10},{15,11},{28,24},{29,25},{30,26},{31,27}} | collective-permute-start | bytes 1597448 | tf_op jit(solution)/shard_map/ppermute | solution.py:566
  420.0 20.5 %collective-permute-start.26 = (bf16[1040,256]{1,0:T(8,128)(2,1)}, bf16[1040,256]{1,0:T(8,128)(2,1)}, u32[]{:S(2)}, u32[]{:S(2)}) collective-permute-start(bf16[1040,256]{1,0:T(8,128)(2,1)} %send.6), channel_id=1, source_target_pairs={{0,2},{1,3},{2,0},{3,1},{4,6},{5,7},{6,4},{7,5},{8,10},{9,11},{10,... | collective-permute-start | bytes 1597448 | tf_op jit(solution)/shard_map/ppermute | solution.py:546
  429.9 27.5 %collective-permute-start.25 = (f32[2,1024,256]{2,1,0:T(8,128)}, f32[2,1024,256]{2,1,0:T(8,128)S(1)}, u32[]{:S(2)}, u32[]{:S(2)}) collective-permute-start(f32[2,1024,256]{2,1,0:T(8,128)} %get-tuple-element.123), channel_id=1, source_target_pairs={{0,1},{1,0},{2,3},{3,2},{4,5},{5,4},{6,7},{7,6},{8,9},{9,8},{10,11... | collective-permute-start | bytes 6291464 | tf_op jit(solution)/shard_map/ppermute | solution.py:546
  433.7 6.8 %copy-start.11 = (f32[2,1024,256]{2,1,0:T(8,128)S(1)}, f32[2,1024,256]{2,1,0:T(8,128)}, u32[]{:S(2)}) copy-start(f32[2,1024,256]{2,1,0:T(8,128)} %copy-done.10) | copy-start | bytes 6291460
  437.0 21.8 %collective-permute-start.32 = (bf16[1040,256]{1,0:T(8,128)(2,1)S(1)}, bf16[1040,256]{1,0:T(8,128)(2,1)S(1)}, u32[]{:S(2)}, u32[]{:S(2)}) collective-permute-start(bf16[1040,256]{1,0:T(8,128)(2,1)S(1)} %get-tuple-element.126), channel_id=1, source_target_pairs={{0,4},{4,8},{1,5},{5,9},{2,6},{6,10},{3,7},{7,11},{16,20},{20,24},... | collective-permute-start | bytes 1597448 | tf_op jit(solution)/shard_map/ppermute | solution.py:563
  439.8 19.0 %collective-permute-start.33 = (bf16[1040,256]{1,0:T(8,128)(2,1)S(1)}, bf16[1040,256]{1,0:T(8,128)(2,1)S(1)}, u32[]{:S(2)}, u32[]{:S(2)}) collective-permute-start(bf16[1040,256]{1,0:T(8,128)(2,1)S(1)} %get-tuple-element.127), channel_id=1, source_target_pairs={{8,4},{12,8},{9,5},{13,9},{10,6},{14,10},{11,7},{15,11},{24,20},{2... | collective-permute-start | bytes 1597448 | tf_op jit(solution)/shard_map/ppermute | solution.py:566
  452.1 5.2 copy-start.9
  452.9 15.4 %collective-permute-start.34 = (bf16[1040,256]{1,0:T(8,128)(2,1)S(1)}, bf16[1040,256]{1,0:T(8,128)(2,1)S(1)}, u32[]{:S(2)}, u32[]{:S(2)}) collective-permute-start(bf16[1040,256]{1,0:T(8,128)(2,1)S(1)} %get-tuple-element.129), channel_id=1, source_target_pairs={{0,4},{1,5},{2,6},{3,7},{16,20},{17,21},{18,22},{19,23}} | collective-permute-start | bytes 1597448 | tf_op jit(solution)/shard_map/ppermute | solution.py:563
  456.7 11.7 %collective-permute-start.35 = (bf16[1040,256]{1,0:T(8,128)(2,1)S(1)}, bf16[1040,256]{1,0:T(8,128)(2,1)S(1)}, u32[]{:S(2)}, u32[]{:S(2)}) collective-permute-start(bf16[1040,256]{1,0:T(8,128)(2,1)S(1)} %get-tuple-element.130), channel_id=1, source_target_pairs={{12,8},{13,9},{14,10},{15,11},{28,24},{29,25},{30,26},{31,27}} | collective-permute-start | bytes 1597448 | tf_op jit(solution)/shard_map/ppermute | solution.py:566
  458.2 14.0 %collective-permute-start.31 = (bf16[1040,256]{1,0:T(8,128)(2,1)S(1)}, bf16[1040,256]{1,0:T(8,128)(2,1)S(1)}, u32[]{:S(2)}, u32[]{:S(2)}) collective-permute-start(bf16[1040,256]{1,0:T(8,128)(2,1)S(1)} %send.7), channel_id=1, source_target_pairs={{0,2},{1,3},{2,0},{3,1},{4,6},{5,7},{6,4},{7,5},{8,10},{9,11},{10,... | collective-permute-start | bytes 1597448 | tf_op jit(solution)/shard_map/ppermute | solution.py:546
  484.5 15.3 %collective-permute-start.36 = (bf16[1040,256]{1,0:T(8,128)(2,1)S(1)}, bf16[1040,256]{1,0:T(8,128)(2,1)S(1)}, u32[]{:S(2)}, u32[]{:S(2)}) collective-permute-start(bf16[1040,256]{1,0:T(8,128)(2,1)S(1)} %get-tuple-element.137), channel_id=1, source_target_pairs={{0,4},{1,5},{2,6},{3,7},{16,20},{17,21},{18,22},{19,23}} | collective-permute-start | bytes 1597448 | tf_op jit(solution)/shard_map/ppermute | solution.py:563
  487.3 12.5 %collective-permute-start.37 = (bf16[1040,256]{1,0:T(8,128)(2,1)S(1)}, bf16[1040,256]{1,0:T(8,128)(2,1)S(1)}, u32[]{:S(2)}, u32[]{:S(2)}) collective-permute-start(bf16[1040,256]{1,0:T(8,128)(2,1)S(1)} %get-tuple-element.138), channel_id=1, source_target_pairs={{12,8},{13,9},{14,10},{15,11},{28,24},{29,25},{30,26},{31,27}} | collective-permute-start | bytes 1597448 | tf_op jit(solution)/shard_map/ppermute | solution.py:566
  488.0 23.2 %collective-permute-start.48 = (bf16[1040,256]{1,0:T(8,128)(2,1)S(1)}, bf16[1040,256]{1,0:T(8,128)(2,1)S(1)}, u32[]{:S(2)}, u32[]{:S(2)}) collective-permute-start(bf16[1040,256]{1,0:T(8,128)(2,1)S(1)} %get-tuple-element.124), channel_id=1, source_target_pairs={{0,4},{4,8},{8,12},{1,5},{5,9},{9,13},{2,6},{6,10},{10,14},{3,7},{... | collective-permute-start | bytes 1597448 | tf_op jit(solution)/shard_map/ppermute | solution.py:563
  489.3 33.3 %collective-permute-start.42 = (bf16[1040,256]{1,0:T(8,128)(2,1)S(1)}, bf16[1040,256]{1,0:T(8,128)(2,1)S(1)}, u32[]{:S(2)}, u32[]{:S(2)}) collective-permute-start(bf16[1040,256]{1,0:T(8,128)(2,1)S(1)} %get-tuple-element.134), channel_id=1, source_target_pairs={{0,4},{4,8},{1,5},{5,9},{2,6},{6,10},{3,7},{7,11},{16,20},{20,24},... | collective-permute-start | bytes 1597448 | tf_op jit(solution)/shard_map/ppermute | solution.py:563
  494.3 32.8 %collective-permute-start.43 = (bf16[1040,256]{1,0:T(8,128)(2,1)S(1)}, bf16[1040,256]{1,0:T(8,128)(2,1)S(1)}, u32[]{:S(2)}, u32[]{:S(2)}) collective-permute-start(bf16[1040,256]{1,0:T(8,128)(2,1)S(1)} %get-tuple-element.135), channel_id=1, source_target_pairs={{8,4},{12,8},{9,5},{13,9},{10,6},{14,10},{11,7},{15,11},{24,20},{2... | collective-permute-start | bytes 1597448 | tf_op jit(solution)/shard_map/ppermute | solution.py:566
  502.8 31.2 %collective-permute-start.38 = (bf16[1040,256]{1,0:T(8,128)(2,1)S(1)}, bf16[1040,256]{1,0:T(8,128)(2,1)S(1)}, u32[]{:S(2)}, u32[]{:S(2)}) collective-permute-start(bf16[1040,256]{1,0:T(8,128)(2,1)S(1)} %get-tuple-element.139), channel_id=1, source_target_pairs={{0,4},{4,8},{1,5},{5,9},{2,6},{6,10},{3,7},{7,11},{16,20},{20,24},... | collective-permute-start | bytes 1597448 | tf_op jit(solution)/shard_map/ppermute | solution.py:563
  507.2 31.2 %collective-permute-start.39 = (bf16[1040,256]{1,0:T(8,128)(2,1)S(1)}, bf16[1040,256]{1,0:T(8,128)(2,1)S(1)}, u32[]{:S(2)}, u32[]{:S(2)}) collective-permute-start(bf16[1040,256]{1,0:T(8,128)(2,1)S(1)} %get-tuple-element.140), channel_id=1, source_target_pairs={{8,4},{12,8},{9,5},{13,9},{10,6},{14,10},{11,7},{15,11},{24,20},{2... | collective-permute-start | bytes 1597448 | tf_op jit(solution)/shard_map/ppermute | solution.py:566
  511.2 31.8 %collective-permute-start.49 = (bf16[1040,256]{1,0:T(8,128)(2,1)}, bf16[1040,256]{1,0:T(8,128)(2,1)S(1)}, u32[]{:S(2)}, u32[]{:S(2)}) collective-permute-start(bf16[1040,256]{1,0:T(8,128)(2,1)} %get-tuple-element.125), channel_id=1, source_target_pairs={{4,0},{8,4},{12,8},{5,1},{9,5},{13,9},{6,2},{10,6},{14,10},{7,3},{... | collective-permute-start | bytes 1597448 | tf_op jit(solution)/shard_map/ppermute | solution.py:566
  522.6 26.5 %collective-permute-start.46 = (bf16[1040,256]{1,0:T(8,128)(2,1)S(1)}, bf16[1040,256]{1,0:T(8,128)(2,1)S(1)}, u32[]{:S(2)}, u32[]{:S(2)}) collective-permute-start(bf16[1040,256]{1,0:T(8,128)(2,1)S(1)} %get-tuple-element.132), channel_id=1, source_target_pairs={{0,4},{4,8},{8,12},{1,5},{5,9},{9,13},{2,6},{6,10},{10,14},{3,7},{... | collective-permute-start | bytes 1597448 | tf_op jit(solution)/shard_map/ppermute | solution.py:563
  527.0 25.9 %collective-permute-start.47 = (bf16[1040,256]{1,0:T(8,128)(2,1)S(1)}, bf16[1040,256]{1,0:T(8,128)(2,1)S(1)}, u32[]{:S(2)}, u32[]{:S(2)}) collective-permute-start(bf16[1040,256]{1,0:T(8,128)(2,1)S(1)} %get-tuple-element.133), channel_id=1, source_target_pairs={{4,0},{8,4},{12,8},{5,1},{9,5},{13,9},{6,2},{10,6},{14,10},{7,3},{... | collective-permute-start | bytes 1597448 | tf_op jit(solution)/shard_map/ppermute | solution.py:566
  534.0 22.8 %collective-permute-start.44 = (bf16[1040,256]{1,0:T(8,128)(2,1)S(1)}, bf16[1040,256]{1,0:T(8,128)(2,1)S(1)}, u32[]{:S(2)}, u32[]{:S(2)}) collective-permute-start(bf16[1040,256]{1,0:T(8,128)(2,1)S(1)} %get-tuple-element.143), channel_id=1, source_target_pairs={{0,4},{4,8},{8,12},{1,5},{5,9},{9,13},{2,6},{6,10},{10,14},{3,7},{... | collective-permute-start | bytes 1597448 | tf_op jit(solution)/shard_map/ppermute | solution.py:563
  538.4 12.2 %copy-start.1 = (f32[4096,256]{1,0:T(8,128)S(1)}, f32[4096,256]{1,0:T(8,128)}, u32[]{:S(2)}) copy-start(f32[4096,256]{1,0:T(8,128)} %expand.4.refs_0_.refs_1_.block) | copy-start | bytes 12582916
  538.5 18.4 %collective-permute-start.45 = (bf16[1040,256]{1,0:T(8,128)(2,1)S(1)}, bf16[1040,256]{1,0:T(8,128)(2,1)S(1)}, u32[]{:S(2)}, u32[]{:S(2)}) collective-permute-start(bf16[1040,256]{1,0:T(8,128)(2,1)S(1)} %get-tuple-element.144), channel_id=1, source_target_pairs={{4,0},{8,4},{12,8},{5,1},{9,5},{13,9},{6,2},{10,6},{14,10},{7,3},{... | collective-permute-start | bytes 1597448 | tf_op jit(solution)/shard_map/ppermute | solution.py:566
  543.0 23.6 %collective-permute-start.40 = (bf16[1040,256]{1,0:T(8,128)(2,1)S(1)}, bf16[1040,256]{1,0:T(8,128)(2,1)S(1)}, u32[]{:S(2)}, u32[]{:S(2)}) collective-permute-start(bf16[1040,256]{1,0:T(8,128)(2,1)S(1)} %get-tuple-element.141), channel_id=1, source_target_pairs={{0,4},{4,8},{8,12},{1,5},{5,9},{9,13},{2,6},{6,10},{10,14},{3,7},{... | collective-permute-start | bytes 1597448 | tf_op jit(solution)/shard_map/ppermute | solution.py:563
  549.1 3.8 copy-start.3
  549.1 17.5 %collective-permute-start.41 = (bf16[1040,256]{1,0:T(8,128)(2,1)S(1)}, bf16[1040,256]{1,0:T(8,128)(2,1)S(1)}, u32[]{:S(2)}, u32[]{:S(2)}) collective-permute-start(bf16[1040,256]{1,0:T(8,128)(2,1)S(1)} %get-tuple-element.142), channel_id=1, source_target_pairs={{4,0},{8,4},{12,8},{5,1},{9,5},{13,9},{6,2},{10,6},{14,10},{7,3},{... | collective-permute-start | bytes 1597448 | tf_op jit(solution)/shard_map/ppermute | solution.py:566
  552.9 3.9 copy-start.5
  555.2 11.4 %copy-start.7 = (f32[4096,256]{1,0:T(8,128)S(1)}, f32[4096,256]{1,0:T(8,128)}, u32[]{:S(2)}) copy-start(f32[4096,256]{1,0:T(8,128)} %expand.7.refs_0_.refs_1_.block) | copy-start | bytes 12582916
  (9 other events, 15.7 us)

commit v10 on v9

--- a/solution.py
+++ b/solution.py
@@ -336,7 +336,7 @@
             jax.ShapeDtypeStruct((rows, width), F32),
             jax.ShapeDtypeStruct((2, rows, width), BF16),
         ],
-        compiler_params=params(40),
+        compiler_params=params(60),
         cost_estimate=cost(4 * rows * width * depth, 30 * rows * width),
         name="rotate",
     )(at, part, above, below, first, second, *pieces)
@@ -375,7 +375,7 @@
         ),
         out_shape=[jax.ShapeDtypeStruct((cols // 2, depth, piece), F32)] * 2,
         compiler_params=params(60),
-        cost_estimate=cost(4 * depth * inner * piece * cols, 8 * depth * piece * cols),
+        cost_estimate=cost(4 * depth * inner * piece * cols, 8 * depth * piece * cols, 4),
         name="restore",
     )(me, normed, *([flipped] * cols))
 
@@ -411,14 +411,14 @@
         out_shape=jax.ShapeDtypeStruct((depth + EXTRA, piece), BF16),
         scratch_shapes=[pltpu.VMEM((depth, piece), F32)],
         compiler_params=params(16),
-        cost_estimate=cost(400 * depth * piece, 18 * depth * piece),
+        cost_estimate=cost(400 * depth * piece, 18 * depth * piece, 4),
         name="send",
     )(keep, mate, *codes)
 
 
-def expand_kernel(keep, mate, *refs, tile):
-    codes, (left, out, both) = refs[:-3], refs[-3:]
-    depth, piece = both.shape[0], out.shape[1]
+def expand_send_kernel(place_ref, keep, mate, *refs, tile):
+    codes, (left, message, both, total) = refs[:-4], refs[-4:]
+    depth, piece = total.shape
 
     @pl.when(pl.program_id(0) == 0)
     def _():
@@ -431,114 +431,140 @@
             both[rows, piece:] = low
             return carry
 
-        lax.fori_loop(0, depth // tile, put, 0)
-
+        lax.fori_loop(0, both.shape[0] // tile, put, 0)
+
+    product = dot(left[...], both[...], ((1,), (0,)))
+    total[...] = product[:, :piece] + product[:, piece:]
+    fill(message, None, lambda rows: total[rows, :], tile, lambda rows: total[rows, :])
+
+
+def expand_send(place, keep, mate, codes, left, depth):
+    inner, piece = keep.shape[1:]
+    count = left.shape[0] // depth // 2
+    pair = pl.BlockSpec((1, inner, piece), lambda i, s: (0, 0, 0))
+    code = pl.BlockSpec((inner + EXTRA, piece), lambda i, s: (0, 0))
+    return pl.pallas_call(
+        functools.partial(expand_send_kernel, tile=min(64, depth)),
+        grid_spec=pltpu.PrefetchScalarGridSpec(
+            num_scalar_prefetch=1,
+            grid=(count,),
+            in_specs=[pair, pair]
+            + [code] * len(codes)
+            + [pl.BlockSpec((depth, inner), lambda i, s: (s[0] ^ (2 * i + 1), 0))],
+            out_specs=[
+                pl.BlockSpec((None, depth + EXTRA, piece), lambda i, s: (i, 0, 0)),
+                pl.BlockSpec((inner, 2 * piece), lambda i, s: (0, 0)),
+            ],
+            scratch_shapes=[pltpu.VMEM((depth, piece), F32)],
+        ),
+        out_shape=[
+            jax.ShapeDtypeStruct((count, depth + EXTRA, piece), BF16),
+            jax.ShapeDtypeStruct((inner, 2 * piece), BF16),
+        ],
+        compiler_params=params(40),
+        cost_estimate=cost(4 * count * depth * inner * piece, 4 * depth * inner, 4),
+        name="expand_send",
+    )(place, keep, mate, *codes, left)
+
+
+def expand_keep_kernel(place_ref, both, left, out):
+    piece = out.shape[1]
     product = dot(left[...], both[...], ((1,), (0,)))
     out[...] = product[:, :piece] + product[:, piece:]
 
 
-def expand(keep, mate, codes, left):
-    rows, inner = left.shape
-    _, depth, piece = keep.shape
-    step = min(1024, rows)
-    pair = pl.BlockSpec((1, depth, piece), lambda i: (0, 0, 0))
-    message = pl.BlockSpec((depth + EXTRA, piece), lambda i: (0, 0))
-    return pl.pallas_call(
-        functools.partial(expand_kernel, tile=min(64, depth)),
-        grid=(rows // step,),
-        in_specs=[pair, pair]
-        + [message] * len(codes)
-        + [pl.BlockSpec((step, inner), lambda i: (i, 0))],
-        out_specs=pl.BlockSpec((step, piece), lambda i: (i, 0)),
-        out_shape=jax.ShapeDtypeStruct((rows, piece), F32),
-        scratch_shapes=[pltpu.VMEM((depth, 2 * piece), BF16)],
-        compiler_params=params(48),
-        cost_estimate=cost(4 * rows * inner * piece, 4 * rows * piece + 2 * rows * inner),
-        name="expand",
-    )(keep, mate, *codes, left)
-
-
-def hop_kernel(place_ref, *refs, lines, step, tile):
-    blocks, refs = refs[:2], refs[2:]
-    arrived, outs, total = refs[:-3], refs[-3:-1], refs[-1]
-    depth = total.shape[0]
-    sends = (place_ref[0] < step, place_ref[0] >= lines - step)
-    for way in range(2):
-
-        @pl.when(sends[way])
-        def _(way=way):
-            scale = scale_of(arrived[way], depth) if arrived else None
-
-            def value_at(rows):
-                value = blocks[way][rows, :]
-                if arrived:
-                    value = value + decode(arrived[way][rows, :], scale)
-                return value
-
-            fill(outs[way], total, value_at, tile)
-
-
-def hop(place, product, arrived, lines, step):
-    depth, piece = product.shape[0] // lines, product.shape[1]
-    ahead = lines - step
-    message = pl.BlockSpec((depth + EXTRA, piece), lambda i, s: (0, 0))
-    return pl.pallas_call(
-        functools.partial(hop_kernel, lines=lines, step=step, tile=min(64, depth)),
+def expand_keep(place, both, left, depth):
+    inner, piece = both.shape[0], both.shape[1] // 2
+    count = left.shape[0] // depth // 2
+    return pl.pallas_call(
+        expand_keep_kernel,
         grid_spec=pltpu.PrefetchScalarGridSpec(
             num_scalar_prefetch=1,
-            grid=(1,),
+            grid=(count,),
             in_specs=[
-                pl.BlockSpec(
-                    (depth, piece), lambda i, s: (jnp.minimum(s[0] + ahead, lines - 1), 0)
-                ),
-                pl.BlockSpec((depth, piece), lambda i, s: (jnp.maximum(s[0] - ahead, 0), 0)),
-            ]
-            + [message] * len(arrived),
-            out_specs=[message] * 2,
-            scratch_shapes=[pltpu.VMEM((depth, piece), F32)],
-        ),
-        out_shape=[jax.ShapeDtypeStruct((depth + EXTRA, piece), BF16)] * 2,
-        compiler_params=params(48),
-        cost_estimate=cost(400 * depth * piece, 12 * depth * piece),
+                pl.BlockSpec((inner, 2 * piece), lambda i, s: (0, 0)),
+                pl.BlockSpec((depth, inner), lambda i, s: (s[0] ^ (2 * i), 0)),
+            ],
+            out_specs=pl.BlockSpec((None, depth, piece), lambda i, s: (i, 0, 0)),
+        ),
+        out_shape=jax.ShapeDtypeStruct((count, depth, piece), F32),
+        compiler_params=params(60),
+        cost_estimate=cost(4 * count * depth * inner * piece, 4 * depth * inner, 4),
+        name="expand_keep",
+    )(place, both, left)
+
+
+def hop_kernel(kept, *refs, tile):
+    arrived, (message, total) = refs[:-2], refs[-2:]
+    depth = total.shape[0]
+    scales = [scale_of(code, depth) for code in arrived]
+
+    def value_at(rows):
+        value = kept[rows, :]
+        for code, scale in zip(arrived, scales):
+            value = value + decode(code[rows, :], scale)
+        return value
+
+    fill(message, total, value_at, tile)
+
+
+def hop(kept, arrived, step):
+    _, depth, piece = kept.shape
+    count = arrived[-1].shape[0] // 2
+
+    def at(shift):
+        return lambda i: ((2 * i + 1) * 2**shift, 0, 0)
+
+    return pl.pallas_call(
+        functools.partial(hop_kernel, tile=min(64, depth)),
+        grid=(count,),
+        in_specs=[pl.BlockSpec((None, depth, piece), at(step - 1))]
+        + [
+            pl.BlockSpec((None, depth + EXTRA, piece), at(step - 1 - index))
+            for index in range(len(arrived))
+        ],
+        out_specs=pl.BlockSpec((None, depth + EXTRA, piece), lambda i: (i, 0, 0)),
+        out_shape=jax.ShapeDtypeStruct((count, depth + EXTRA, piece), BF16),
+        scratch_shapes=[pltpu.VMEM((depth, piece), F32)],
+        compiler_params=params(40),
+        cost_estimate=cost(400 * count * depth * piece, 12 * count * depth * piece, 4),
         name="hop",
-    )(place, product, product, *arrived)
-
-
-def finish_kernel(at_ref, block, up, down, *refs, tile):
-    out = refs[-1]
+    )(kept, *arrived)
+
+
+def finish_kernel(kept, *refs, tile, terms):
+    arrived, out = refs[:terms], refs[-1]
     depth = out.shape[0]
-    scales = [scale_of(message, depth) for message in (up, down)]
+    scales = [scale_of(code, depth) for code in arrived]
 
     def add(i, carry):
         rows = pl.ds(pl.multiple_of(i * tile, tile), tile)
-        out[rows, :] = (
-            block[rows, :] + decode(up[rows, :], scales[0]) + decode(down[rows, :], scales[1])
-        )
+        value = kept[rows, :]
+        for code, scale in zip(arrived, scales):
+            value = value + decode(code[rows, :], scale)
+        out[rows, :] = value
         return carry
 
     lax.fori_loop(0, depth // tile, add, 0)
 
 
-def finish(at, product, arrived, update, chunk, depth, width):
-    piece = product.shape[1]
-    tile = min(64, depth)
-    message = pl.BlockSpec((depth + EXTRA, piece), lambda i, s: (0, 0))
+def finish(kept, arrived, update, chunk, width):
+    _, depth, piece = kept.shape
     extra = [] if update is None else [update]
-    return pl.pallas_call(
-        functools.partial(finish_kernel, tile=tile),
-        grid_spec=pltpu.PrefetchScalarGridSpec(
-            num_scalar_prefetch=1,
-            grid=(1,),
-            in_specs=[pl.BlockSpec((depth, piece), lambda i, s: (s[0], 0)), message, message]
-            + [pl.BlockSpec(memory_space=pl.ANY)] * len(extra),
-            out_specs=pl.BlockSpec((depth, piece), lambda i, s: (0, chunk)),
-        ),
+    first = lambda i: (0, 0, 0)
+    return pl.pallas_call(
+        functools.partial(finish_kernel, tile=min(64, depth), terms=len(arrived)),
+        grid=(1,),
+        in_specs=[pl.BlockSpec((None, depth, piece), first)]
+        + [pl.BlockSpec((None, depth + EXTRA, piece), first)] * len(arrived)
+        + [pl.BlockSpec(memory_space=pl.ANY)] * len(extra),
+        out_specs=pl.BlockSpec((depth, piece), lambda i: (0, chunk)),
         out_shape=jax.ShapeDtypeStruct((depth, width), F32),
-        input_output_aliases={4: 0} if extra else {},
-        compiler_params=params(48),
-        cost_estimate=cost(400 * depth * piece, 12 * depth * piece),
+        input_output_aliases={1 + len(arrived): 0} if extra else {},
+        compiler_params=params(40),
+        cost_estimate=cost(400 * depth * piece, 12 * depth * piece, 0.1),
         name="finish",
-    )(at, product, *arrived, *extra)
+    )(kept, *arrived, *extra)
 
 
 def build(lines, cols):
@@ -633,44 +659,39 @@
             held = put(jnp.reshape(there, (1,)), last, held, lines + 1)
         flipped = held[1]
 
-        keeps, products, sent, hops = [], [], [], {}
-
-        def running(chunk, step):
-            if step > 1:
-                upward, downward = running(chunk, step - 1)
-                before = (
-                    up(upward, range(0, step - 1)),
-                    down(downward, range(lines - step + 1, lines)),
-                )
-            if (chunk, step) not in hops:
-                arrived = () if step == 1 else before
-                hops[chunk, step] = hop(spot, products[chunk], arrived, lines, step)
-            return hops[chunk, step]
-
+        def cross(value, distance):
+            return lax.ppermute(value, "row", [(i, i ^ distance) for i in range(lines)])
+
+        def later_hops(chunk):
+            kept, arrived = products[chunk]
+            step = 1
+            while 2**step < lines:
+                message = hop(kept, arrived, step)
+                if step == 1:
+                    second[chunk] = message
+                arrived = arrived + [cross(message, 2**step)]
+                step += 1
+            products[chunk] = kept, arrived
+
+        products, sent, outgoing, second = [], [], [], {}
         for chunk in range(CHUNKS):
-            ready = after(normed, *sent[-1]) if chunk else normed
+            ready = after(normed, *products[0][1], outgoing[1]) if chunk >= 2 else normed
             keep, mate = restore(me_now, ready, flipped, cols, chunk, piece)
             mate = swap(mate, 1)
-            if chunk:
-                mate = after(mate, *running(chunk - 1, 1))
             sent.append([send(keep, mate, distance, []) for distance in range(2, cols, 2)])
             crossed = [swap(code, 2 * index + 2) for index, code in enumerate(sent[-1])]
-            due = [
-                message
-                for earlier in range(max(0, chunk - 2), chunk)
-                if chunk - earlier + 1 < lines
-                for message in running(earlier, chunk - earlier + 1)
-            ]
-            if due and crossed:
-                crossed[0] = after(crossed[0], *due)
-            products.append(expand(keep, mate, crossed, left))
-        arrived = []
+            message, both = expand_send(spot, keep, mate, crossed, left, depth)
+            outgoing.append(message)
+            products.append((expand_keep(spot, both, left, depth), [cross(message, 1)]))
+            if chunk == 1:
+                later_hops(0)
+            if chunk == CHUNKS - 1:
+                later_hops(1)
+        update = None
         for chunk in range(CHUNKS):
-            upward, downward = running(chunk, far)
-            arrived.append((up(upward, range(0, far)), down(downward, range(1, lines))))
-        update = None
-        for chunk, product in enumerate(products):
-            update = finish(spot, product, arrived[chunk], update, chunk, depth, width)
+            if chunk >= CHUNKS - 2:
+                later_hops(chunk)
+            update = finish(*products[chunk], update, chunk, width)
         return (new_first, new_second, update)
 
     return local

time: 573 us -> 603 us (1.052)
  waiting for transfers between devices: 218 us -> 300 us
  starting transfers between devices: 91.7 us -> 49.1 us
    ppermute x0 -> x8, waiting for transfers between devices: none -> 115 us  [cross(): return lax.ppermute(value, 'row', [(i, i ^ distance) for i in range(lines)])]
    ppermute x18 -> x6, starting transfers between devices: 63 us -> 13.3 us  [up(): return lax.ppermute(value, 'row', [(i, i + 1) for i in senders])]
    ppermute x18 -> x6, waiting for transfers between devices: 61.3 us -> 25.9 us  [up(): return lax.ppermute(value, 'row', [(i, i + 1) for i in senders])]
    ppermute x0 -> x8, starting transfers between devices: none -> 17.6 us  [cross(): return lax.ppermute(value, 'row', [(i, i ^ distance) for i in range(lines)])]
    ppermute x18 -> x6, starting transfers between devices: 19.9 us -> 7.71 us  [down(): return lax.ppermute(value, 'row', [(i, i - 1) for i in senders])]
    pallas_call x20 -> x16, Pallas kernels: 77.7 us -> 68.5 us  [the longest x4 29.4 us: expand_send(): pl.pallas_call(functools.partial(expand_send_kernel, tile=min(64, depth))...]
    unnamed x46 -> x58, local copies, waits for them, and re-layouts: 22.5 us -> 17.6 us
    ppermute x18 -> x6, waiting for transfers between devices: 81.5 us -> 78 us  [down(): return lax.ppermute(value, 'row', [(i, i - 1) for i in senders])]
  transfers between devices with their start and end apart: 50 -> 34, of which waited for: 20 -> 18; matrix products, arithmetic and copies ran while one was open for 1% -> 1% of each run, Pallas kernels for 32% -> 29%
where the time goes in v10:
time: 603 us; the launch traced here: 602 us
  waiting for transfers between devices  300 us (50%)
  Pallas kernels  224 us (37%)
  starting transfers between devices  49.1 us (8%)
  local copies, waits for them, and re-layouts  24.5 us (4%)
    ppermute x8, waiting for transfers between devices, cross(): return lax.ppermute(value, 'row', [(i, i ^ distance) for i in range(lines)])  115 us
    ppermute x14, waiting for transfers between devices, swap(): return lax.ppermute(value, 'col', [(i, i ^ distance) for i in range(cols)])  81 us
    ppermute x6, waiting for transfers between devices, down(): return lax.ppermute(value, 'row', [(i, i - 1) for i in senders])  78 us
    pallas_call x4, Pallas kernels, restore(): pl.pallas_call(functools.partial(restore_kernel, cols=cols), grid_spec=pl...  33.7 us
    pallas_call x4, Pallas kernels, expand_send(): pl.pallas_call(functools.partial(expand_send_kernel, tile=min(64, depth))...  29.4 us
    pallas_call x6, Pallas kernels, put(): pl.pallas_call(put_kernel, grid_spec=pltpu.PrefetchScalarGridSpec(num_sca...  26.2 us
    ppermute x6, waiting for transfers between devices, up(): return lax.ppermute(value, 'row', [(i, i + 1) for i in senders])  25.9 us
    pallas_call x2, Pallas kernels, halfway(): pl.pallas_call(functools.partial(halfway_kernel, offsets=offsets, lines=l...  24.3 us
  transfers between devices with their start and end apart: 34, of which 18 were waited for; matrix products, arithmetic and copies ran while one was open for 1% of the time, Pallas kernels for 29%

profile of v10, /device:TPU:0, one launch (start us, length us, event | category | flops | bytes accessed | tf_op | source)
XLA Modules:
  0.0 601.5 jit_solution(5890886999815132666)
XLA Ops:
  0.6 3.0 collective-permute-start
  3.6 3.6 collective-permute-start.3
  8.6 41.0 %collective-permute-done = bf16[1024,1024]{1,0:T(8,128)(2,1)} collective-permute-done((bf16[1024,1024]{1,0:T(8,128)(2,1)}, bf16[1024,1024]{1,0:T(8,128)(2,1)}, u32[]{:S(2)}, u32[]{:S(2)}) %collective-permute-start) | collective-permute-done | bytes 2097184 | tf_op jit(solution)/shard_map/ppermute | solution.py:572
  49.6 2.4 collective-permute-done.3.refs_1_
  52.0 2.1 collective-permute-start.4
  54.1 2.1 collective-permute-done.5.refs_3_
  59.5 1.9 bitcast_dynamic-update-slice_fusion.2
  61.3 1.9 bitcast_dynamic-update-slice_fusion.1
  65.1 3.3 copy-done.25
  68.4 37.4 %collective-permute-done.6.refs_4_ = bf16[1024,1024]{1,0:T(8,128)(2,1)} collective-permute-done((bf16[1024,1024]{1,0:T(8,128)(2,1)}, bf16[1024,1024]{1,0:T(8,128)(2,1)}, u32[]{:S(2)}, u32[]{:S(2)}) %collective-permute-start.6) | collective-permute-done | bytes 2097184 | tf_op jit(solution)/shard_map/ppermute | solution.py:592
  105.8 2.0 collective-permute-start.7
  109.1 14.7 %halfway.2.refs_2_ = f32[1024,1024]{1,0:T(8,128)} custom-call(s32[1]{0:T(128)} %bitcast.1.place_ref, bf16[4096,1024]{1,0:T(8,128)(2,1)} %bitcast.17, bf16[1024,1024]{1,0:T(8,128)(2,1)} %collective-permute-done.4.refs_0_, bf16[1024,1024]{1,0:T(8,128)(2,1)S(1)} %collective-permute-done.3.refs_1_, bf16[1024,1024]{1,0:T(8,128)(2,1)} %refs_2_.1, ...), custom_call_target="tpu_custom_call" | custom-call | flops 2576980480 | bytes 2516582 | tf_op jit(solution)/shard_map/halfway/pallas_call | solution.py:114
  123.7 31.6 %collective-permute-done.8.refs_1_ = bf16[1024,1024]{1,0:T(8,128)(2,1)} collective-permute-done((bf16[1024,1024]{1,0:T(8,128)(2,1)}, bf16[1024,1024]{1,0:T(8,128)(2,1)}, u32[]{:S(2)}, u32[]{:S(2)}) %collective-permute-start.8) | collective-permute-done | bytes 2097184 | tf_op jit(solution)/shard_map/ppermute | solution.py:592
  158.2 9.6 %halfway.3.value = f32[1024,1024]{1,0:T(8,128)} custom-call(s32[1]{0:T(128)} %bitcast.1.place_ref, bf16[4096,1024]{1,0:T(8,128)(2,1)} %bitcast.18, bf16[1024,1024]{1,0:T(8,128)(2,1)} %collective-permute-done.7.refs_0_, bf16[1024,1024]{1,0:T(8,128)(2,1)} %collective-permute-done.8.refs_1_, f32[1024,1024]{1,0:T(8,128)} %halfway.2.refs_2_), custom_call_target="tpu_custom_call" | custom-call | flops 2576980480 | bytes 2516582 | tf_op jit(solution)/shard_map/halfway/pallas_call | solution.py:114
  167.8 7.9 %pack.1 = (bf16[2,1024,1024]{2,1,0:T(8,128)(2,1)}, bf16[1040,1024]{1,0:T(8,128)(2,1)}) custom-call(f32[1024,1024]{1,0:T(8,128)} %halfway.3.value), custom_call_target="tpu_custom_call" | custom-call | flops 125829120 | bytes 3145728 | tf_op jit(solution)/shard_map/pack/pallas_call | solution.py:147
  175.7 23.4 %collective-permute-done.9.piece = bf16[1024,1024]{1,0:T(8,128)(2,1)S(1)} collective-permute-done((bf16[1024,1024]{1,0:T(8,128)(2,1)}, bf16[1024,1024]{1,0:T(8,128)(2,1)S(1)}, u32[]{:S(2)}, u32[]{:S(2)}) %collective-permute-start.9) | collective-permute-done | bytes 2097184 | tf_op jit(solution)/shard_map/ppermute | solution.py:589
  199.2 4.2 collective-permute-done.10.piece
  205.2 2.0 collective-permute-start.15
  207.2 4.3 put.6
  211.5 4.4 put.7
  216.0 4.4 put.8
  220.3 6.1 %unpack.3.refs_1_ = bf16[2,1024,1024]{2,1,0:T(8,128)(2,1)} custom-call(bf16[1040,1024]{1,0:T(8,128)(2,1)} %collective-permute-done.11.message.scales, bf16[1040,1024]{1,0:T(8,128)(2,1)} %collective-permute-done.11.message.scales), custom_call_target="tpu_custom_call" | custom-call | flops 125829120 | bytes 1887436 | tf_op jit(solution)/shard_map/unpack/pallas_call | solution.py:176
  226.4 25.9 %collective-permute-done.12.message.scales = bf16[1040,1024]{1,0:T(8,128)(2,1)S(1)} collective-permute-done((bf16[1040,1024]{1,0:T(8,128)(2,1)}, bf16[1040,1024]{1,0:T(8,128)(2,1)S(1)}, u32[]{:S(2)}, u32[]{:S(2)}) %collective-permute-start.12) | collective-permute-done | bytes 2129952 | tf_op jit(solution)/shard_map/ppermute | solution.py:572
  255.2 2.0 collective-permute-start.17
  257.3 4.4 put.9
  261.7 4.3 put.10
  266.1 6.1 %unpack.4.refs_2_ = bf16[2,1024,1024]{2,1,0:T(8,128)(2,1)} custom-call(bf16[1040,1024]{1,0:T(8,128)(2,1)} %copy-done.26, bf16[1040,1024]{1,0:T(8,128)(2,1)} %copy-done.26), custom_call_target="tpu_custom_call" | custom-call | flops 125829120 | bytes 1887436 | tf_op jit(solution)/shard_map/unpack/pallas_call | solution.py:176
  272.1 6.1 %unpack.5.refs_3_ = bf16[2,1024,1024]{2,1,0:T(8,128)(2,1)} custom-call(bf16[1040,1024]{1,0:T(8,128)(2,1)} %collective-permute-done.13.message.scales, bf16[1040,1024]{1,0:T(8,128)(2,1)} %collective-permute-done.13.message.scales), custom_call_target="tpu_custom_call" | custom-call | flops 125829120 | bytes 1887436 | tf_op jit(solution)/shard_map/unpack/pallas_call | solution.py:176
  278.3 21.6 %rotate_part.1.part = f32[1024,1024]{1,0:T(8,128)S(1)} custom-call(s32[2]{0:T(128)S(1)} %pad_add_fusion.at_ref, bf16[2,1024,1024]{2,1,0:T(8,128)(2,1)} %get-tuple-element.56.refs_0_, bf16[2,1024,1024]{2,1,0:T(8,128)(2,1)} %unpack.3.refs_1_, bf16[2,1024,1024]{2,1,0:T(8,128)(2,1)} %unpack.4.refs_2_, bf16[2,1024,1024]{2,1,0:T(8,128)(2,1)} %unpack.5.refs_3_, ...), custom_call_target="tpu_custom_call" | custom-call | flops 5153960960 | bytes 6291456 | tf_op jit(solution)/shard_map/rotate_part/pallas_call | solution.py:244
  299.9 1.9 copy-done.7
  303.1 3.1 broadcast_select_fusion.piece
  306.2 16.3 %rotate.1 = (f32[1024,1024]{1,0:T(8,128)}, f32[1024,1024]{1,0:T(8,128)}, bf16[2,1024,1024]{2,1,0:T(8,128)(2,1)}) custom-call(s32[2]{0:T(128)} %copy-done.18, f32[1024,1024]{1,0:T(8,128)} %copy-done.7, bf16[1024,1024]{1,0:T(8,128)(2,1)} %collective-permute-done.16.above, bf16[1024,1024]{1,0:T(8,128)(2,1)} %collective-permute-done.17.below, ...), custom_call_target="tpu_custom_call" | custom-call | flops 17179869184 | bytes 125829120 | tf_op jit(solution)/shard_map/rotate/pallas_call | solution.py:320
  322.5 4.3 put.11
  326.8 8.4 %restore.4 = (f32[2,1024,256]{2,1,0:T(8,128)}, f32[2,1024,256]{2,1,0:T(8,128)}) custom-call(s32[1]{0:T(128)} %bitcast.me_ref, bf16[2,1024,1024]{2,1,0:T(8,128)(2,1)} %get-tuple-element.87.normed, bf16[5,1024,1024]{2,1,0:T(8,128)(2,1)} %get-tuple-element.79.refs_0_.refs_1_.refs_2_.refs_3_, ...), custom_call_target="tpu_custom_call" | custom-call | flops 17179869184 | bytes 33554432 | tf_op jit(solution)/shard_map/restore/pallas_call | solution.py:367
  335.2 8.5 %restore.5 = (f32[2,1024,256]{2,1,0:T(8,128)}, f32[2,1024,256]{2,1,0:T(8,128)}) custom-call(s32[1]{0:T(128)} %bitcast.me_ref, bf16[2,1024,1024]{2,1,0:T(8,128)(2,1)} %get-tuple-element.87.normed, bf16[5,1024,1024]{2,1,0:T(8,128)(2,1)} %get-tuple-element.79.refs_0_.refs_1_.refs_2_.refs_3_, ...), custom_call_target="tpu_custom_call" | custom-call | flops 17179869184 | bytes 33554432 | tf_op jit(solution)/shard_map/restore/pallas_call | solution.py:367
  344.0 2.2 send.4
  347.8 12.7 %collective-permute-done.19.refs_0_ = bf16[1040,256]{1,0:T(8,128)(2,1)S(1)} collective-permute-done((bf16[1040,256]{1,0:T(8,128)(2,1)S(1)}, bf16[1040,256]{1,0:T(8,128)(2,1)S(1)}, u32[]{:S(2)}, u32[]{:S(2)}) %collective-permute-start.19) | collective-permute-done | bytes 532512 | tf_op jit(solution)/shard_map/ppermute | solution.py:572
  360.5 7.6 %expand_send.4 = (bf16[2,1040,256]{2,1,0:T(8,128)(2,1)}, bf16[1024,512]{1,0:T(8,128)(2,1)S(1)}) custom-call(s32[1]{0:T(128)} %bitcast.1.place_ref, f32[2,1024,256]{2,1,0:T(8,128)S(1)} %copy-done.15, f32[2,1024,256]{2,1,0:T(8,128)} %collective-permute-done.18.mate, bf16[1040,256]{1,0:T(8,128)(2,1)S(1)} %collective-permute-done.19.refs_0_, ...), custom_call_target="tpu_custom_call" | custom-call | flops 8589934592 | bytes 16777216 | tf_op jit(solution)/shard_map/expand_send/pallas_call | solution.py:446
  368.1 7.8 %collective-permute-start.20 = (bf16[2,1040,256]{2,1,0:T(8,128)(2,1)}, bf16[2,1040,256]{2,1,0:T(8,128)(2,1)S(1)}, u32[]{:S(2)}, u32[]{:S(2)}) collective-permute-start(bf16[2,1040,256]{2,1,0:T(8,128)(2,1)} %get-tuple-element.82), channel_id=1, source_target_pairs={{0,4},{4,0},{8,12},{12,8},{1,5},{5,1},{9,13},{13,9},{2,6},{6,2},{1... | collective-permute-start | bytes 3194888 | tf_op jit(solution)/shard_map/ppermute | solution.py:663
  378.8 5.4 expand_keep.4.kept
  384.1 15.0 %collective-permute-done.20.refs_0_ = bf16[2,1040,256]{2,1,0:T(8,128)(2,1)S(1)} collective-permute-done((bf16[2,1040,256]{2,1,0:T(8,128)(2,1)}, bf16[2,1040,256]{2,1,0:T(8,128)(2,1)S(1)}, u32[]{:S(2)}, u32[]{:S(2)}) %collective-permute-start.20) | collective-permute-done | bytes 1064992 | tf_op jit(solution)/shard_map/ppermute | solution.py:663
  402.2 2.5 collective-permute-start.21
  404.8 6.6 %expand_send.5 = (bf16[2,1040,256]{2,1,0:T(8,128)(2,1)S(1)}, bf16[1024,512]{1,0:T(8,128)(2,1)S(1)}) custom-call(s32[1]{0:T(128)} %bitcast.1.place_ref, f32[2,1024,256]{2,1,0:T(8,128)S(1)} %copy-done.9, f32[2,1024,256]{2,1,0:T(8,128)S(1)} %copy-done.13, bf16[1040,256]{1,0:T(8,128)(2,1)} %collective-permute-done.23.refs_0_, bf16[4096,1024]{1,0:T(8,128)(2,1)} %bitcast.21), custom_call_target="tpu_custom_call" | custom-call | flops 8589934592 | bytes 16777216 | tf_op jit(solution)/shard_map/expand_send/pallas_call | solution.py:446
  413.4 14.0 %collective-permute-done.21.refs_1_ = bf16[1,1040,256]{2,1,0:T(8,128)(2,1)S(1)} collective-permute-done((bf16[1,1040,256]{2,1,0:T(8,128)(2,1)S(1)}, bf16[1,1040,256]{2,1,0:T(8,128)(2,1)S(1)}, u32[]{:S(2)}, u32[]{:S(2)}) %collective-permute-start.21) | collective-permute-done | bytes 532512 | tf_op jit(solution)/shard_map/ppermute | solution.py:663
  428.2 8.4 %restore.6 = (f32[2,1024,256]{2,1,0:T(8,128)}, f32[2,1024,256]{2,1,0:T(8,128)}) custom-call(s32[1]{0:T(128)} %bitcast.me_ref, bf16[2,1024,1024]{2,1,0:T(8,128)(2,1)} %get-tuple-element.87.normed, bf16[5,1024,1024]{2,1,0:T(8,128)(2,1)} %get-tuple-element.79.refs_0_.refs_1_.refs_2_.refs_3_, ...), custom_call_target="tpu_custom_call" | custom-call | flops 17179869184 | bytes 33554432 | tf_op jit(solution)/shard_map/restore/pallas_call | solution.py:367
  436.6 8.5 %restore.7 = (f32[2,1024,256]{2,1,0:T(8,128)}, f32[2,1024,256]{2,1,0:T(8,128)}) custom-call(s32[1]{0:T(128)} %bitcast.me_ref, bf16[2,1024,1024]{2,1,0:T(8,128)(2,1)} %get-tuple-element.87.normed, bf16[5,1024,1024]{2,1,0:T(8,128)(2,1)} %get-tuple-element.79.refs_0_.refs_1_.refs_2_.refs_3_, ...), custom_call_target="tpu_custom_call" | custom-call | flops 17179869184 | bytes 33554432 | tf_op jit(solution)/shard_map/restore/pallas_call | solution.py:367
  447.0 2.0 send.6
  450.6 5.4 expand_keep.7.kept
  456.0 15.0 %collective-permute-done.32.refs_0_ = bf16[2,1040,256]{2,1,0:T(8,128)(2,1)S(1)} collective-permute-done((bf16[2,1040,256]{2,1,0:T(8,128)(2,1)S(1)}, bf16[2,1040,256]{2,1,0:T(8,128)(2,1)S(1)}, u32[]{:S(2)}, u32[]{:S(2)}) %collective-permute-start.32) | collective-permute-done | bytes 1064992 | tf_op jit(solution)/shard_map/ppermute | solution.py:663
  472.6 2.3 hop.7
  475.9 2.2 send.7
  479.6 7.7 %expand_send.6 = (bf16[2,1040,256]{2,1,0:T(8,128)(2,1)}, bf16[1024,512]{1,0:T(8,128)(2,1)S(1)}) custom-call(s32[1]{0:T(128)} %bitcast.1.place_ref, f32[2,1024,256]{2,1,0:T(8,128)S(1)} %copy-done.11, f32[2,1024,256]{2,1,0:T(8,128)} %collective-permute-done.24.mate, bf16[1040,256]{1,0:T(8,128)(2,1)} %collective-permute-done.25.refs_0_, bf16[4096,1024]{1,0:T(8,128)(2,1)} %bitcast.23), custom_call_target="tpu_custom_call" | custom-call | flops 8589934592 | bytes 16777216 | tf_op jit(solution)/shard_map/expand_send/pallas_call | solution.py:446
  491.5 7.6 %expand_send.7 = (bf16[2,1040,256]{2,1,0:T(8,128)(2,1)}, bf16[1024,512]{1,0:T(8,128)(2,1)S(1)}) custom-call(s32[1]{0:T(128)} %bitcast.1.place_ref, f32[2,1024,256]{2,1,0:T(8,128)S(1)} %copy-done.8, f32[2,1024,256]{2,1,0:T(8,128)} %collective-permute-done.28.mate, bf16[1040,256]{1,0:T(8,128)(2,1)S(1)} %collective-permute-done.29.refs_0_, ...), custom_call_target="tpu_custom_call" | custom-call | flops 8589934592 | bytes 16777216 | tf_op jit(solution)/shard_map/expand_send/pallas_call | solution.py:446
  501.5 5.3 expand_keep.5.kept
  506.8 5.3 expand_keep.6.kept
  512.2 34.3 %collective-permute-done.30.refs_0_ = bf16[2,1040,256]{2,1,0:T(8,128)(2,1)} collective-permute-done((bf16[2,1040,256]{2,1,0:T(8,128)(2,1)}, bf16[2,1040,256]{2,1,0:T(8,128)(2,1)}, u32[]{:S(2)}, u32[]{:S(2)}) %collective-permute-start.30) | collective-permute-done | bytes 1064992 | tf_op jit(solution)/shard_map/ppermute | solution.py:663
  548.0 2.5 hop.6
  552.4 2.7 collective-permute-start.27
  555.1 2.2 finish.4.refs_2_
  557.3 2.2 finish.5.refs_2_
  559.6 28.4 %collective-permute-done.31.refs_1_ = bf16[1,1040,256]{2,1,0:T(8,128)(2,1)S(1)} collective-permute-done((bf16[1,1040,256]{2,1,0:T(8,128)(2,1)S(1)}, bf16[1,1040,256]{2,1,0:T(8,128)(2,1)S(1)}, u32[]{:S(2)}, u32[]{:S(2)}) %collective-permute-start.31) | collective-permute-done | bytes 532512 | tf_op jit(solution)/shard_map/ppermute | solution.py:663
  588.0 3.3 finish.6.refs_2_
  591.3 8.0 %collective-permute-done.27.refs_1_ = bf16[1,1040,256]{2,1,0:T(8,128)(2,1)S(1)} collective-permute-done((bf16[1,1040,256]{2,1,0:T(8,128)(2,1)S(1)}, bf16[1,1040,256]{2,1,0:T(8,128)(2,1)S(1)}, u32[]{:S(2)}, u32[]{:S(2)}) %collective-permute-start.27) | collective-permute-done | bytes 532512 | tf_op jit(solution)/shard_map/ppermute | solution.py:663
  599.3 2.2 finish.7
  (107 shorter events, 44.7 us)
Async XLA Ops:
  0.6 49.0 %collective-permute-start = (bf16[1024,1024]{1,0:T(8,128)(2,1)}, bf16[1024,1024]{1,0:T(8,128)(2,1)}, u32[]{:S(2)}, u32[]{:S(2)}) collective-permute-start(bf16[1024,1024]{1,0:T(8,128)(2,1)} %param.8), channel_id=1, source_target_pairs={{0,2},{1,3},{2,0},{3,1},{4,6},{5,7},{6,4},{7,5},{8,10},{9,11},{10,... | collective-permute-start | bytes 6291464 | tf_op jit(solution)/shard_map/ppermute | solution.py:572
  3.6 48.4 %collective-permute-start.3 = (bf16[1024,1024]{1,0:T(8,128)(2,1)}, bf16[1024,1024]{1,0:T(8,128)(2,1)S(1)}, u32[]{:S(2)}, u32[]{:S(2)}) collective-permute-start(bf16[1024,1024]{1,0:T(8,128)(2,1)} %refs_2_.1), channel_id=1, source_target_pairs={{0,4},{4,8},{8,12},{1,5},{5,9},{9,13},{2,6},{6,10},{10,14},{3,7},{... | collective-permute-start | bytes 6291464 | tf_op jit(solution)/shard_map/ppermute | solution.py:589
  7.2 49.0 %collective-permute-start.5 = (bf16[1024,1024]{1,0:T(8,128)(2,1)}, bf16[1024,1024]{1,0:T(8,128)(2,1)}, u32[]{:S(2)}, u32[]{:S(2)}) collective-permute-start(bf16[1024,1024]{1,0:T(8,128)(2,1)} %refs_2_.1), channel_id=1, source_target_pairs={{4,0},{8,4},{12,8},{5,1},{9,5},{13,9},{6,2},{10,6},{14,10},{7,3},{... | collective-permute-start | bytes 6291464 | tf_op jit(solution)/shard_map/ppermute | solution.py:592
  8.5 52.8 %collective-permute-start.1 = (bf16[1024,1024]{1,0:T(8,128)(2,1)}, bf16[1024,1024]{1,0:T(8,128)(2,1)}, u32[]{:S(2)}, u32[]{:S(2)}) collective-permute-start(bf16[1024,1024]{1,0:T(8,128)(2,1)} %param.8), channel_id=1, source_target_pairs={{0,1},{1,0},{2,3},{3,2},{4,5},{5,4},{6,7},{7,6},{8,9},{9,8},{10,11... | collective-permute-start | bytes 6291464 | tf_op jit(solution)/shard_map/ppermute | solution.py:572
  49.6 13.6 %collective-permute-start.2 = (bf16[1024,1024]{1,0:T(8,128)(2,1)}, bf16[1024,1024]{1,0:T(8,128)(2,1)}, u32[]{:S(2)}, u32[]{:S(2)}) collective-permute-start(bf16[1024,1024]{1,0:T(8,128)(2,1)} %collective-permute-done), channel_id=1, source_target_pairs={{0,1},{1,0},{2,3},{3,2},{4,5},{5,4},{6,7},{7,6},{8,9},{9,8},{10,11... | collective-permute-start | bytes 6291464 | tf_op jit(solution)/shard_map/ppermute | solution.py:572
  52.0 13.1 %collective-permute-start.4 = (bf16[1024,1024]{1,0:T(8,128)(2,1)S(1)}, bf16[1024,1024]{1,0:T(8,128)(2,1)}, u32[]{:S(2)}, u32[]{:S(2)}) collective-permute-start(bf16[1024,1024]{1,0:T(8,128)(2,1)S(1)} %collective-permute-done.3.refs_1_), channel_id=1, source_target_pairs={{4,8},{8,12},{5,9},{9,13},{6,10},{10,14},{7,11},{11,15},{20,24},{2... | collective-permute-start | bytes 6291464 | tf_op jit(solution)/shard_map/ppermute | solution.py:589
  56.3 49.5 %collective-permute-start.6 = (bf16[1024,1024]{1,0:T(8,128)(2,1)}, bf16[1024,1024]{1,0:T(8,128)(2,1)}, u32[]{:S(2)}, u32[]{:S(2)}) collective-permute-start(bf16[1024,1024]{1,0:T(8,128)(2,1)} %collective-permute-done.5.refs_3_), channel_id=1, source_target_pairs={{4,0},{8,4},{5,1},{9,5},{6,2},{10,6},{7,3},{11,7},{20,16},{24,20},... | collective-permute-start | bytes 6291464 | tf_op jit(solution)/shard_map/ppermute | solution.py:592
  57.6 1.6 copy-start.28
  65.1 3.3 copy-start.25
  105.8 18.0 %collective-permute-start.7 = (bf16[1024,1024]{1,0:T(8,128)(2,1)}, bf16[1024,1024]{1,0:T(8,128)(2,1)}, u32[]{:S(2)}, u32[]{:S(2)}) collective-permute-start(bf16[1024,1024]{1,0:T(8,128)(2,1)} %collective-permute-done.4.refs_0_), channel_id=1, source_target_pairs={{8,12},{9,13},{10,14},{11,15},{24,28},{25,29},{26,30},{27,31}} | collective-permute-start | bytes 6291464 | tf_op jit(solution)/shard_map/ppermute | solution.py:589
  107.8 47.6 %collective-permute-start.8 = (bf16[1024,1024]{1,0:T(8,128)(2,1)}, bf16[1024,1024]{1,0:T(8,128)(2,1)}, u32[]{:S(2)}, u32[]{:S(2)}) collective-permute-start(bf16[1024,1024]{1,0:T(8,128)(2,1)} %collective-permute-done.6.refs_4_), channel_id=1, source_target_pairs={{4,0},{5,1},{6,2},{7,3},{20,16},{21,17},{22,18},{23,19}} | collective-permute-start | bytes 6291464 | tf_op jit(solution)/shard_map/ppermute | solution.py:592
  155.3 43.8 %collective-permute-start.9 = (bf16[1024,1024]{1,0:T(8,128)(2,1)}, bf16[1024,1024]{1,0:T(8,128)(2,1)S(1)}, u32[]{:S(2)}, u32[]{:S(2)}) collective-permute-start(bf16[1024,1024]{1,0:T(8,128)(2,1)} %piece), channel_id=1, source_target_pairs={{0,4},{4,8},{8,12},{1,5},{5,9},{9,13},{2,6},{6,10},{10,14},{3,7},{... | collective-permute-start | bytes 6291464 | tf_op jit(solution)/shard_map/ppermute | solution.py:589
  156.9 46.5 %collective-permute-start.10 = (bf16[1024,1024]{1,0:T(8,128)(2,1)}, bf16[1024,1024]{1,0:T(8,128)(2,1)}, u32[]{:S(2)}, u32[]{:S(2)}) collective-permute-start(bf16[1024,1024]{1,0:T(8,128)(2,1)} %piece), channel_id=1, source_target_pairs={{4,0},{8,4},{12,8},{5,1},{9,5},{13,9},{6,2},{10,6},{14,10},{7,3},{... | collective-permute-start | bytes 6291464 | tf_op jit(solution)/shard_map/ppermute | solution.py:592
  199.2 4.3 copy-start.27
  203.4 16.9 %collective-permute-start.11 = (bf16[1040,1024]{1,0:T(8,128)(2,1)}, bf16[1040,1024]{1,0:T(8,128)(2,1)}, u32[]{:S(2)}, u32[]{:S(2)}) collective-permute-start(bf16[1040,1024]{1,0:T(8,128)(2,1)} %get-tuple-element.59), channel_id=1, source_target_pairs={{0,1},{1,0},{2,3},{3,2},{4,5},{5,4},{6,7},{7,6},{8,9},{9,8},{10,11... | collective-permute-start | bytes 6389768 | tf_op jit(solution)/shard_map/ppermute | solution.py:572
  203.4 49.0 %collective-permute-start.12 = (bf16[1040,1024]{1,0:T(8,128)(2,1)}, bf16[1040,1024]{1,0:T(8,128)(2,1)S(1)}, u32[]{:S(2)}, u32[]{:S(2)}) collective-permute-start(bf16[1040,1024]{1,0:T(8,128)(2,1)} %get-tuple-element.59), channel_id=1, source_target_pairs={{0,2},{1,3},{2,0},{3,1},{4,6},{5,7},{6,4},{7,5},{8,10},{9,11},{10,... | collective-permute-start | bytes 6389768 | tf_op jit(solution)/shard_map/ppermute | solution.py:572
  203.9 50.0 %collective-permute-start.14 = (bf16[1024,1024]{1,0:T(8,128)(2,1)}, bf16[1024,1024]{1,0:T(8,128)(2,1)}, u32[]{:S(2)}, u32[]{:S(2)}) collective-permute-start(bf16[1024,1024]{1,0:T(8,128)(2,1)} %collective-permute-done.10.piece), channel_id=1, source_target_pairs={{4,0},{8,4},{5,1},{9,5},{6,2},{10,6},{7,3},{11,7},{20,16},{24,20},... | collective-permute-start | bytes 6291464 | tf_op jit(solution)/shard_map/ppermute | solution.py:592
  205.2 50.0 %collective-permute-start.15 = (bf16[1024,1024]{1,0:T(8,128)(2,1)}, bf16[1024,1024]{1,0:T(8,128)(2,1)}, u32[]{:S(2)}, u32[]{:S(2)}) collective-permute-start(bf16[1024,1024]{1,0:T(8,128)(2,1)} %copy-done.27), channel_id=1, source_target_pairs={{4,8},{8,12},{5,9},{9,13},{6,10},{10,14},{7,11},{11,15},{20,24},{2... | collective-permute-start | bytes 6291464 | tf_op jit(solution)/shard_map/ppermute | solution.py:589
  252.4 9.4 %copy-start.26 = (bf16[1040,1024]{1,0:T(8,128)(2,1)}, bf16[1040,1024]{1,0:T(8,128)(2,1)S(1)}, u32[]{:S(2)}) copy-start(bf16[1040,1024]{1,0:T(8,128)(2,1)S(1)} %collective-permute-done.12.message.scales) | copy-start | bytes 6389764
  252.4 19.8 %collective-permute-start.13 = (bf16[1040,1024]{1,0:T(8,128)(2,1)S(1)}, bf16[1040,1024]{1,0:T(8,128)(2,1)}, u32[]{:S(2)}, u32[]{:S(2)}) collective-permute-start(bf16[1040,1024]{1,0:T(8,128)(2,1)S(1)} %collective-permute-done.12.message.scales), channel_id=1, source_target_pairs={{0,1},{1,0},{2,3},{3,2},{4,5},{5,4},{6,7},{7,6},{8,9},{9,8},{10,11... | collective-permute-start | bytes 6389768 | tf_op jit(solution)/shard_map/ppermute | solution.py:572
  253.9 49.1 %collective-permute-start.16 = (bf16[1024,1024]{1,0:T(8,128)(2,1)}, bf16[1024,1024]{1,0:T(8,128)(2,1)}, u32[]{:S(2)}, u32[]{:S(2)}) collective-permute-start(bf16[1024,1024]{1,0:T(8,128)(2,1)} %collective-permute-done.14.piece), channel_id=1, source_target_pairs={{4,0},{5,1},{6,2},{7,3},{20,16},{21,17},{22,18},{23,19}} | collective-permute-start | bytes 6291464 | tf_op jit(solution)/shard_map/ppermute | solution.py:592
  255.2 47.8 %collective-permute-start.17 = (bf16[1024,1024]{1,0:T(8,128)(2,1)}, bf16[1024,1024]{1,0:T(8,128)(2,1)}, u32[]{:S(2)}, u32[]{:S(2)}) collective-permute-start(bf16[1024,1024]{1,0:T(8,128)(2,1)} %collective-permute-done.15.piece), channel_id=1, source_target_pairs={{8,12},{9,13},{10,14},{11,15},{24,28},{25,29},{26,30},{27,31}} | collective-permute-start | bytes 6291464 | tf_op jit(solution)/shard_map/ppermute | solution.py:589
  257.3 21.0 %copy-start.18 = (s32[2]{0:T(128)}, s32[2]{0:T(128)S(1)}, u32[]{:S(2)}) copy-start(s32[2]{0:T(128)S(1)} %pad_add_fusion.at_ref) | copy-start | bytes 28
  299.9 2.0 copy-start.7
  335.2 8.9 %copy-start.14 = (f32[2,1024,256]{2,1,0:T(8,128)S(1)}, f32[2,1024,256]{2,1,0:T(8,128)}, u32[]{:S(2)}) copy-start(f32[2,1024,256]{2,1,0:T(8,128)} %get-tuple-element.80.keep) | copy-start | bytes 6291460
  335.2 8.9 %collective-permute-start.18 = (f32[2,1024,256]{2,1,0:T(8,128)}, f32[2,1024,256]{2,1,0:T(8,128)}, u32[]{:S(2)}, u32[]{:S(2)}) collective-permute-start(f32[2,1024,256]{2,1,0:T(8,128)} %get-tuple-element.81), channel_id=1, source_target_pairs={{0,1},{1,0},{2,3},{3,2},{4,5},{5,4},{6,7},{7,6},{8,9},{9,8},{10,11... | collective-permute-start | bytes 6291464 | tf_op jit(solution)/shard_map/ppermute | solution.py:572
  343.7 32.2 %collective-permute-start.22 = (f32[2,1024,256]{2,1,0:T(8,128)}, f32[2,1024,256]{2,1,0:T(8,128)S(1)}, u32[]{:S(2)}, u32[]{:S(2)}) collective-permute-start(f32[2,1024,256]{2,1,0:T(8,128)} %get-tuple-element.85), channel_id=1, source_target_pairs={{0,1},{1,0},{2,3},{3,2},{4,5},{5,4},{6,7},{7,6},{8,9},{9,8},{10,11... | collective-permute-start | bytes 6291464 | tf_op jit(solution)/shard_map/ppermute | solution.py:572
  344.0 16.5 %copy-start.15 = (f32[2,1024,256]{2,1,0:T(8,128)S(1)}, f32[2,1024,256]{2,1,0:T(8,128)}, u32[]{:S(2)}) copy-start(f32[2,1024,256]{2,1,0:T(8,128)} %get-tuple-element.80.keep) | copy-start | bytes 6291460
  346.2 29.7 %copy-start.9 = (f32[2,1024,256]{2,1,0:T(8,128)S(1)}, f32[2,1024,256]{2,1,0:T(8,128)}, u32[]{:S(2)}) copy-start(f32[2,1024,256]{2,1,0:T(8,128)} %get-tuple-element.84.keep) | copy-start | bytes 6291460
  346.2 14.3 %collective-permute-start.19 = (bf16[1040,256]{1,0:T(8,128)(2,1)S(1)}, bf16[1040,256]{1,0:T(8,128)(2,1)S(1)}, u32[]{:S(2)}, u32[]{:S(2)}) collective-permute-start(bf16[1040,256]{1,0:T(8,128)(2,1)S(1)} %send.4), channel_id=1, source_target_pairs={{0,2},{1,3},{2,0},{3,1},{4,6},{5,7},{6,4},{7,5},{8,10},{9,11},{10,... | collective-permute-start | bytes 1597448 | tf_op jit(solution)/shard_map/ppermute | solution.py:572
  368.1 8.7 %copy-start.23 = (bf16[1024,512]{1,0:T(8,128)(2,1)}, bf16[1024,512]{1,0:T(8,128)(2,1)S(1)}, u32[]{:S(2)}) copy-start(bf16[1024,512]{1,0:T(8,128)(2,1)S(1)} %get-tuple-element.83.both) | copy-start | bytes 3145732
  368.1 31.1 %collective-permute-start.20 = (bf16[2,1040,256]{2,1,0:T(8,128)(2,1)}, bf16[2,1040,256]{2,1,0:T(8,128)(2,1)S(1)}, u32[]{:S(2)}, u32[]{:S(2)}) collective-permute-start(bf16[2,1040,256]{2,1,0:T(8,128)(2,1)} %get-tuple-element.82), channel_id=1, source_target_pairs={{0,4},{4,0},{8,12},{12,8},{1,5},{5,1},{9,13},{13,9},{2,6},{6,2},{1... | collective-permute-start | bytes 3194888 | tf_op jit(solution)/shard_map/ppermute | solution.py:663
  375.9 1.4 copy-start.12
  377.3 27.5 %collective-permute-start.23 = (bf16[1040,256]{1,0:T(8,128)(2,1)S(1)}, bf16[1040,256]{1,0:T(8,128)(2,1)}, u32[]{:S(2)}, u32[]{:S(2)}) collective-permute-start(bf16[1040,256]{1,0:T(8,128)(2,1)S(1)} %send.5), channel_id=1, source_target_pairs={{0,2},{1,3},{2,0},{3,1},{4,6},{5,7},{6,4},{7,5},{8,10},{9,11},{10,... | collective-permute-start | bytes 1597448 | tf_op jit(solution)/shard_map/ppermute | solution.py:572
  399.2 1.6 copy-start
  400.8 4.0 copy-start.13
  402.2 25.1 %collective-permute-start.21 = (bf16[1,1040,256]{2,1,0:T(8,128)(2,1)S(1)}, bf16[1,1040,256]{2,1,0:T(8,128)(2,1)S(1)}, u32[]{:S(2)}, u32[]{:S(2)}) collective-permute-start(bf16[1,1040,256]{2,1,0:T(8,128)(2,1)S(1)} %hop.4), channel_id=1, source_target_pairs={{0,8},{4,12},{8,0},{12,4},{1,9},{5,13},{9,1},{13,5},{2,10},{6,14},... | collective-permute-start | bytes 1597448 | tf_op jit(solution)/shard_map/ppermute | solution.py:663
  411.3 1.0 copy-start.19
  412.3 1.0 copy-start.21
  427.3 0.8 copy-start.16
  436.5 8.9 %copy-start.20 = (bf16[2,1040,256]{2,1,0:T(8,128)(2,1)S(1)}, bf16[2,1040,256]{2,1,0:T(8,128)(2,1)}, u32[]{:S(2)}) copy-start(bf16[2,1040,256]{2,1,0:T(8,128)(2,1)} %copy-done.19) | copy-start | bytes 3194884
  436.5 8.9 %collective-permute-start.24 = (f32[2,1024,256]{2,1,0:T(8,128)}, f32[2,1024,256]{2,1,0:T(8,128)}, u32[]{:S(2)}, u32[]{:S(2)}) collective-permute-start(f32[2,1024,256]{2,1,0:T(8,128)} %get-tuple-element.89), channel_id=1, source_target_pairs={{0,1},{1,0},{2,3},{3,2},{4,5},{5,4},{6,7},{7,6},{8,9},{9,8},{10,11... | collective-permute-start | bytes 6291464 | tf_op jit(solution)/shard_map/ppermute | solution.py:572
  445.1 30.8 %collective-permute-start.28 = (f32[2,1024,256]{2,1,0:T(8,128)}, f32[2,1024,256]{2,1,0:T(8,128)}, u32[]{:S(2)}, u32[]{:S(2)}) collective-permute-start(f32[2,1024,256]{2,1,0:T(8,128)} %get-tuple-element.93), channel_id=1, source_target_pairs={{0,1},{1,0},{2,3},{3,2},{4,5},{5,4},{6,7},{7,6},{8,9},{9,8},{10,11... | collective-permute-start | bytes 6291464 | tf_op jit(solution)/shard_map/ppermute | solution.py:572
  445.4 25.5 %collective-permute-start.32 = (bf16[2,1040,256]{2,1,0:T(8,128)(2,1)S(1)}, bf16[2,1040,256]{2,1,0:T(8,128)(2,1)S(1)}, u32[]{:S(2)}, u32[]{:S(2)}) collective-permute-start(bf16[2,1040,256]{2,1,0:T(8,128)(2,1)S(1)} %copy-done.20), channel_id=1, source_target_pairs={{0,4},{4,0},{8,12},{12,8},{1,5},{5,1},{9,13},{13,9},{2,6},{6,2},{1... | collective-permute-start | bytes 3194888 | tf_op jit(solution)/shard_map/ppermute | solution.py:663
  445.4 1.6 copy-start.10
  449.1 30.5 %collective-permute-start.25 = (bf16[1040,256]{1,0:T(8,128)(2,1)S(1)}, bf16[1040,256]{1,0:T(8,128)(2,1)}, u32[]{:S(2)}, u32[]{:S(2)}) collective-permute-start(bf16[1040,256]{1,0:T(8,128)(2,1)S(1)} %send.6), channel_id=1, source_target_pairs={{0,2},{1,3},{2,0},{3,1},{4,6},{5,7},{6,4},{7,5},{8,10},{9,11},{10,... | collective-permute-start | bytes 1597448 | tf_op jit(solution)/shard_map/ppermute | solution.py:572
  471.0 1.6 copy-start.2
  472.6 3.3 copy-start.8
  474.9 82.5 %collective-permute-start.33 = (bf16[1,1040,256]{2,1,0:T(8,128)(2,1)}, bf16[1,1040,256]{2,1,0:T(8,128)(2,1)S(1)}, u32[]{:S(2)}, u32[]{:S(2)}) collective-permute-start(bf16[1,1040,256]{2,1,0:T(8,128)(2,1)} %hop.7), channel_id=1, source_target_pairs={{0,8},{4,12},{8,0},{12,4},{1,9},{5,13},{9,1},{13,5},{2,10},{6,14},... | collective-permute-start | bytes 1597448 | tf_op jit(solution)/shard_map/ppermute | solution.py:663
  475.9 3.8 copy-start.11
  478.1 13.4 %collective-permute-start.29 = (bf16[1040,256]{1,0:T(8,128)(2,1)S(1)}, bf16[1040,256]{1,0:T(8,128)(2,1)S(1)}, u32[]{:S(2)}, u32[]{:S(2)}) collective-permute-start(bf16[1040,256]{1,0:T(8,128)(2,1)S(1)} %send.7), channel_id=1, source_target_pairs={{0,2},{1,3},{2,0},{3,1},{4,6},{5,7},{6,4},{7,5},{8,10},{9,11},{10,... | collective-permute-start | bytes 1597448 | tf_op jit(solution)/shard_map/ppermute | solution.py:572
  487.3 1.0 copy-start.22
  488.4 62.5 %collective-permute-start.26 = (bf16[2,1040,256]{2,1,0:T(8,128)(2,1)}, bf16[2,1040,256]{2,1,0:T(8,128)(2,1)S(1)}, u32[]{:S(2)}, u32[]{:S(2)}) collective-permute-start(bf16[2,1040,256]{2,1,0:T(8,128)(2,1)} %get-tuple-element.91), channel_id=1, source_target_pairs={{0,4},{4,0},{8,12},{12,8},{1,5},{5,1},{9,13},{13,9},{2,6},{6,2},{1... | collective-permute-start | bytes 3194888 | tf_op jit(solution)/shard_map/ppermute | solution.py:663
  499.1 1.0 copy-start.24
  500.1 46.4 %collective-permute-start.30 = (bf16[2,1040,256]{2,1,0:T(8,128)(2,1)}, bf16[2,1040,256]{2,1,0:T(8,128)(2,1)}, u32[]{:S(2)}, u32[]{:S(2)}) collective-permute-start(bf16[2,1040,256]{2,1,0:T(8,128)(2,1)} %get-tuple-element.95), channel_id=1, source_target_pairs={{0,4},{4,0},{8,12},{12,8},{1,5},{5,1},{9,13},{13,9},{2,6},{6,2},{1... | collective-permute-start | bytes 3194888 | tf_op jit(solution)/shard_map/ppermute | solution.py:663
  512.2 38.7 %copy-start.4 = (f32[2,1024,256]{2,1,0:T(8,128)S(1)}, f32[2,1024,256]{2,1,0:T(8,128)}, u32[]{:S(2)}) copy-start(f32[2,1024,256]{2,1,0:T(8,128)} %expand_keep.5.kept) | copy-start | bytes 6291460
  546.4 1.6 copy-start.5
  550.5 4.6 copy-start.1
  550.5 4.6 copy-start.17
  550.5 37.4 %collective-permute-start.31 = (bf16[1,1040,256]{2,1,0:T(8,128)(2,1)S(1)}, bf16[1,1040,256]{2,1,0:T(8,128)(2,1)S(1)}, u32[]{:S(2)}, u32[]{:S(2)}) collective-permute-start(bf16[1,1040,256]{2,1,0:T(8,128)(2,1)S(1)} %hop.6), channel_id=1, source_target_pairs={{0,8},{4,12},{8,0},{12,4},{1,9},{5,13},{9,1},{13,5},{2,10},{6,14},... | collective-permute-start | bytes 1597448 | tf_op jit(solution)/shard_map/ppermute | solution.py:663
  552.3 5.0 copy-start.3
  552.4 47.0 %collective-permute-start.27 = (bf16[1,1040,256]{2,1,0:T(8,128)(2,1)S(1)}, bf16[1,1040,256]{2,1,0:T(8,128)(2,1)S(1)}, u32[]{:S(2)}, u32[]{:S(2)}) collective-permute-start(bf16[1,1040,256]{2,1,0:T(8,128)(2,1)S(1)} %hop.5), channel_id=1, source_target_pairs={{0,8},{4,12},{8,0},{12,4},{1,9},{5,13},{9,1},{13,5},{2,10},{6,14},... | collective-permute-start | bytes 1597448 | tf_op jit(solution)/shard_map/ppermute | solution.py:663
  557.3 30.7 %copy-start.6 = (f32[2,1024,256]{2,1,0:T(8,128)S(1)}, f32[2,1024,256]{2,1,0:T(8,128)}, u32[]{:S(2)}) copy-start(f32[2,1024,256]{2,1,0:T(8,128)} %expand_keep.6.kept) | copy-start | bytes 6291460

commit v11 on v10

--- a/solution.py
+++ b/solution.py
@@ -664,6 +664,8 @@
 
         def later_hops(chunk):
             kept, arrived = products[chunk]
+            if chunk - 1 in second:
+                kept = after(kept, second[chunk - 1])
             step = 1
             while 2**step < lines:
                 message = hop(kept, arrived, step)
@@ -673,20 +675,33 @@
                 step += 1
             products[chunk] = kept, arrived
 
-        products, sent, outgoing, second = [], [], [], {}
-        for chunk in range(CHUNKS):
-            ready = after(normed, *products[0][1], outgoing[1]) if chunk >= 2 else normed
+        products, halves, sent, outgoing, second = [], [], [], [], {}
+
+        def sums(chunk, ready):
             keep, mate = restore(me_now, ready, flipped, cols, chunk, piece)
             mate = swap(mate, 1)
+            halves.append((keep, mate))
             sent.append([send(keep, mate, distance, []) for distance in range(2, cols, 2)])
-            crossed = [swap(code, 2 * index + 2) for index, code in enumerate(sent[-1])]
-            message, both = expand_send(spot, keep, mate, crossed, left, depth)
+
+        def multiply(chunk, *before):
+            codes = [swap(code, 2 * index + 2) for index, code in enumerate(sent[chunk])]
+            if codes and before:
+                codes[0] = after(codes[0], *before)
+            message, both = expand_send(spot, *halves[chunk], codes, left, depth)
             outgoing.append(message)
             products.append((expand_keep(spot, both, left, depth), [cross(message, 1)]))
-            if chunk == 1:
-                later_hops(0)
-            if chunk == CHUNKS - 1:
-                later_hops(1)
+
+        sums(0, normed)
+        sums(1, normed)
+        multiply(0, *sent[1])
+        multiply(1)
+        firsts = [product[1][0] for product in products]
+        later_hops(0)
+        later_hops(1)
+        for chunk in range(2, CHUNKS):
+            sums(chunk, after(normed, second.get(chunk % 2, firsts[chunk % 2]), outgoing[1]))
+        for chunk in range(2, CHUNKS):
+            multiply(chunk)
         update = None
         for chunk in range(CHUNKS):
             if chunk >= CHUNKS - 2:

time: 603 us -> 581 us (0.964)
  waiting for transfers between devices: 300 us -> 278 us
    ppermute x8, waiting for transfers between devices: 115 us -> 86.3 us  [cross(): return lax.ppermute(value, 'row', [(i, i ^ distance) for i in range(lines)])]
    ppermute x14, waiting for transfers between devices: 81 us -> 87.3 us  [swap(): return lax.ppermute(value, 'col', [(i, i ^ distance) for i in range(cols)])]
    unnamed x58 -> x40, local copies, waits for them, and re-layouts: 17.6 us -> 14.5 us
  transfers between devices with their start and end apart: 34 -> 34, of which waited for: 18 -> 19; matrix products, arithmetic and copies ran while one was open for 1% -> 1% of each run, Pallas kernels for 29% -> 31%
where the time goes in v11:
time: 581 us; the launch traced here: 580 us
  waiting for transfers between devices  278 us (48%)
  Pallas kernels  229 us (39%)
  starting transfers between devices  47.2 us (8%)
  local copies, waits for them, and re-layouts  21.5 us (4%)
    ppermute x14, waiting for transfers between devices, swap(): return lax.ppermute(value, 'col', [(i, i ^ distance) for i in range(cols)])  87.3 us
    ppermute x8, waiting for transfers between devices, cross(): return lax.ppermute(value, 'row', [(i, i ^ distance) for i in range(lines)])  86.3 us
    ppermute x6, waiting for transfers between devices, down(): return lax.ppermute(value, 'row', [(i, i - 1) for i in senders])  78.4 us
    pallas_call x4, Pallas kernels, restore(): pl.pallas_call(functools.partial(restore_kernel, cols=cols), grid_spec=pl...  33.6 us
    pallas_call x4, Pallas kernels, expand_send(): pl.pallas_call(functools.partial(expand_send_kernel, tile=min(64, depth))...  29.7 us
    pallas_call x6, Pallas kernels, put(): pl.pallas_call(put_kernel, grid_spec=pltpu.PrefetchScalarGridSpec(num_sca...  26.1 us
    ppermute x6, waiting for transfers between devices, up(): return lax.ppermute(value, 'row', [(i, i + 1) for i in senders])  25.9 us
    pallas_call x2, Pallas kernels, halfway(): pl.pallas_call(functools.partial(halfway_kernel, offsets=offsets, lines=l...  24.3 us
  transfers between devices with their start and end apart: 34, of which 19 were waited for; matrix products, arithmetic and copies ran while one was open for 1% of the time, Pallas kernels for 31%

profile of v11, /device:TPU:0, one launch (start us, length us, event | category | flops | bytes accessed | tf_op | source)
XLA Modules:
  0.0 579.5 jit_solution(5542780185171534176)
XLA Ops:
  0.6 3.0 collective-permute-start
  3.6 3.6 collective-permute-start.3
  8.6 41.0 %collective-permute-done = bf16[1024,1024]{1,0:T(8,128)(2,1)} collective-permute-done((bf16[1024,1024]{1,0:T(8,128)(2,1)}, bf16[1024,1024]{1,0:T(8,128)(2,1)}, u32[]{:S(2)}, u32[]{:S(2)}) %collective-permute-start) | collective-permute-done | bytes 2097184 | tf_op jit(solution)/shard_map/ppermute | solution.py:572
  49.6 2.4 collective-permute-done.3.refs_1_
  52.0 2.1 collective-permute-start.4
  54.1 2.2 collective-permute-done.5.refs_3_
  61.3 1.9 bitcast_dynamic-update-slice_fusion.1
  65.1 3.3 copy-done.16
  68.4 37.4 %collective-permute-done.6.refs_4_ = bf16[1024,1024]{1,0:T(8,128)(2,1)} collective-permute-done((bf16[1024,1024]{1,0:T(8,128)(2,1)}, bf16[1024,1024]{1,0:T(8,128)(2,1)}, u32[]{:S(2)}, u32[]{:S(2)}) %collective-permute-start.6) | collective-permute-done | bytes 2097184 | tf_op jit(solution)/shard_map/ppermute | solution.py:592
  105.8 1.9 collective-permute-start.7
  109.0 14.7 %halfway.2.refs_2_ = f32[1024,1024]{1,0:T(8,128)} custom-call(s32[1]{0:T(128)} %bitcast.1.place_ref, bf16[4096,1024]{1,0:T(8,128)(2,1)} %bitcast.17, bf16[1024,1024]{1,0:T(8,128)(2,1)} %collective-permute-done.4.refs_0_, bf16[1024,1024]{1,0:T(8,128)(2,1)S(1)} %collective-permute-done.3.refs_1_, bf16[1024,1024]{1,0:T(8,128)(2,1)} %refs_2_.1, ...), custom_call_target="tpu_custom_call" | custom-call | flops 2576980480 | bytes 2516582 | tf_op jit(solution)/shard_map/halfway/pallas_call | solution.py:114
  123.7 31.6 %collective-permute-done.8.refs_1_ = bf16[1024,1024]{1,0:T(8,128)(2,1)} collective-permute-done((bf16[1024,1024]{1,0:T(8,128)(2,1)}, bf16[1024,1024]{1,0:T(8,128)(2,1)}, u32[]{:S(2)}, u32[]{:S(2)}) %collective-permute-start.8) | collective-permute-done | bytes 2097184 | tf_op jit(solution)/shard_map/ppermute | solution.py:592
  158.2 9.6 %halfway.3.value = f32[1024,1024]{1,0:T(8,128)} custom-call(s32[1]{0:T(128)} %bitcast.1.place_ref, bf16[4096,1024]{1,0:T(8,128)(2,1)} %bitcast.18, bf16[1024,1024]{1,0:T(8,128)(2,1)} %collective-permute-done.7.refs_0_, bf16[1024,1024]{1,0:T(8,128)(2,1)} %collective-permute-done.8.refs_1_, f32[1024,1024]{1,0:T(8,128)} %halfway.2.refs_2_), custom_call_target="tpu_custom_call" | custom-call | flops 2576980480 | bytes 2516582 | tf_op jit(solution)/shard_map/halfway/pallas_call | solution.py:114
  167.8 7.9 %pack.1 = (bf16[2,1024,1024]{2,1,0:T(8,128)(2,1)}, bf16[1040,1024]{1,0:T(8,128)(2,1)}) custom-call(f32[1024,1024]{1,0:T(8,128)} %halfway.3.value), custom_call_target="tpu_custom_call" | custom-call | flops 125829120 | bytes 3145728 | tf_op jit(solution)/shard_map/pack/pallas_call | solution.py:147
  175.7 23.4 %collective-permute-done.9.piece = bf16[1024,1024]{1,0:T(8,128)(2,1)S(1)} collective-permute-done((bf16[1024,1024]{1,0:T(8,128)(2,1)}, bf16[1024,1024]{1,0:T(8,128)(2,1)S(1)}, u32[]{:S(2)}, u32[]{:S(2)}) %collective-permute-start.9) | collective-permute-done | bytes 2097184 | tf_op jit(solution)/shard_map/ppermute | solution.py:589
  199.1 4.2 collective-permute-done.10.piece
  205.2 2.0 collective-permute-start.15
  207.1 4.3 put.6
  211.5 4.4 put.7
  215.9 4.4 put.8
  220.3 6.1 %unpack.3.refs_1_ = bf16[2,1024,1024]{2,1,0:T(8,128)(2,1)} custom-call(bf16[1040,1024]{1,0:T(8,128)(2,1)} %collective-permute-done.11.message.scales, bf16[1040,1024]{1,0:T(8,128)(2,1)} %collective-permute-done.11.message.scales), custom_call_target="tpu_custom_call" | custom-call | flops 125829120 | bytes 1887436 | tf_op jit(solution)/shard_map/unpack/pallas_call | solution.py:176
  226.3 26.0 %collective-permute-done.12.message.scales = bf16[1040,1024]{1,0:T(8,128)(2,1)S(1)} collective-permute-done((bf16[1040,1024]{1,0:T(8,128)(2,1)}, bf16[1040,1024]{1,0:T(8,128)(2,1)S(1)}, u32[]{:S(2)}, u32[]{:S(2)}) %collective-permute-start.12) | collective-permute-done | bytes 2129952 | tf_op jit(solution)/shard_map/ppermute | solution.py:572
  255.2 2.0 collective-permute-start.17
  257.2 4.4 put.9
  261.6 4.3 put.10
  265.9 6.1 %unpack.4.refs_2_ = bf16[2,1024,1024]{2,1,0:T(8,128)(2,1)} custom-call(bf16[1040,1024]{1,0:T(8,128)(2,1)} %copy-done.17, bf16[1040,1024]{1,0:T(8,128)(2,1)} %copy-done.17), custom_call_target="tpu_custom_call" | custom-call | flops 125829120 | bytes 1887436 | tf_op jit(solution)/shard_map/unpack/pallas_call | solution.py:176
  272.0 6.1 %unpack.5.refs_3_ = bf16[2,1024,1024]{2,1,0:T(8,128)(2,1)} custom-call(bf16[1040,1024]{1,0:T(8,128)(2,1)} %collective-permute-done.13.message.scales, bf16[1040,1024]{1,0:T(8,128)(2,1)} %collective-permute-done.13.message.scales), custom_call_target="tpu_custom_call" | custom-call | flops 125829120 | bytes 1887436 | tf_op jit(solution)/shard_map/unpack/pallas_call | solution.py:176
  278.1 21.5 %rotate_part.1.part = f32[1024,1024]{1,0:T(8,128)S(1)} custom-call(s32[2]{0:T(128)S(1)} %pad_add_fusion.at_ref, bf16[2,1024,1024]{2,1,0:T(8,128)(2,1)} %get-tuple-element.61.refs_0_, bf16[2,1024,1024]{2,1,0:T(8,128)(2,1)} %unpack.3.refs_1_, bf16[2,1024,1024]{2,1,0:T(8,128)(2,1)} %unpack.4.refs_2_, bf16[2,1024,1024]{2,1,0:T(8,128)(2,1)} %unpack.5.refs_3_, ...), custom_call_target="tpu_custom_call" | custom-call | flops 5153960960 | bytes 6291456 | tf_op jit(solution)/shard_map/rotate_part/pallas_call | solution.py:244
  299.6 1.9 copy-done.5
  303.0 3.1 broadcast_select_fusion.piece
  306.1 16.3 %rotate.1 = (f32[1024,1024]{1,0:T(8,128)}, f32[1024,1024]{1,0:T(8,128)}, bf16[2,1024,1024]{2,1,0:T(8,128)(2,1)}) custom-call(s32[2]{0:T(128)} %copy-done.11, f32[1024,1024]{1,0:T(8,128)} %copy-done.5, bf16[1024,1024]{1,0:T(8,128)(2,1)} %collective-permute-done.16.above, bf16[1024,1024]{1,0:T(8,128)(2,1)} %collective-permute-done.17.below, ...), custom_call_target="tpu_custom_call" | custom-call | flops 17179869184 | bytes 125829120 | tf_op jit(solution)/shard_map/rotate/pallas_call | solution.py:320
  322.4 4.3 put.11
  326.7 8.4 %restore.5 = (f32[2,1024,256]{2,1,0:T(8,128)}, f32[2,1024,256]{2,1,0:T(8,128)}) custom-call(s32[1]{0:T(128)} %bitcast.me_ref, bf16[2,1024,1024]{2,1,0:T(8,128)(2,1)} %get-tuple-element.99.normed, bf16[5,1024,1024]{2,1,0:T(8,128)(2,1)} %get-tuple-element.84.refs_0_.refs_1_.refs_2_.refs_3_, ...), custom_call_target="tpu_custom_call" | custom-call | flops 17179869184 | bytes 33554432 | tf_op jit(solution)/shard_map/restore/pallas_call | solution.py:367
  335.1 8.5 %restore.4 = (f32[2,1024,256]{2,1,0:T(8,128)}, f32[2,1024,256]{2,1,0:T(8,128)}) custom-call(s32[1]{0:T(128)} %bitcast.me_ref, bf16[2,1024,1024]{2,1,0:T(8,128)(2,1)} %get-tuple-element.99.normed, bf16[5,1024,1024]{2,1,0:T(8,128)(2,1)} %get-tuple-element.84.refs_0_.refs_1_.refs_2_.refs_3_, ...), custom_call_target="tpu_custom_call" | custom-call | flops 17179869184 | bytes 33554432 | tf_op jit(solution)/shard_map/restore/pallas_call | solution.py:367
  344.0 2.2 send.5
  350.4 10.8 %collective-permute-done.21.refs_0_ = bf16[1040,256]{1,0:T(8,128)(2,1)S(1)} collective-permute-done((bf16[1040,256]{1,0:T(8,128)(2,1)S(1)}, bf16[1040,256]{1,0:T(8,128)(2,1)S(1)}, u32[]{:S(2)}, u32[]{:S(2)}) %collective-permute-start.21) | collective-permute-done | bytes 532512 | tf_op jit(solution)/shard_map/ppermute | solution.py:572
  361.2 7.6 %expand_send.5 = (bf16[2,1040,256]{2,1,0:T(8,128)(2,1)}, bf16[1024,512]{1,0:T(8,128)(2,1)S(1)}) custom-call(s32[1]{0:T(128)} %bitcast.1.place_ref, f32[2,1024,256]{2,1,0:T(8,128)S(1)} %copy-done.10, f32[2,1024,256]{2,1,0:T(8,128)} %collective-permute-done.20.mate, bf16[1040,256]{1,0:T(8,128)(2,1)S(1)} %collective-permute-done.21.refs_0_, ...), custom_call_target="tpu_custom_call" | custom-call | flops 8589934592 | bytes 16777216 | tf_op jit(solution)/shard_map/expand_send/pallas_call | solution.py:446
  369.8 7.6 %collective-permute-start.22 = (bf16[2,1040,256]{2,1,0:T(8,128)(2,1)}, bf16[2,1040,256]{2,1,0:T(8,128)(2,1)S(1)}, u32[]{:S(2)}, u32[]{:S(2)}) collective-permute-start(bf16[2,1040,256]{2,1,0:T(8,128)(2,1)} %get-tuple-element.92), channel_id=1, source_target_pairs={{0,4},{4,0},{8,12},{12,8},{1,5},{5,1},{9,13},{13,9},{2,6},{6,2},{1... | collective-permute-start | bytes 3194888 | tf_op jit(solution)/shard_map/ppermute | solution.py:663
  377.4 7.3 %expand_send.4 = (bf16[2,1040,256]{2,1,0:T(8,128)(2,1)}, bf16[1024,512]{1,0:T(8,128)(2,1)S(1)}) custom-call(s32[1]{0:T(128)} %bitcast.1.place_ref, f32[2,1024,256]{2,1,0:T(8,128)S(1)} %copy-done.9, f32[2,1024,256]{2,1,0:T(8,128)S(1)} %collective-permute-done.18.mate, bf16[1040,256]{1,0:T(8,128)(2,1)S(1)} %collective-permute-done.19.refs_0_, ...), custom_call_target="tpu_custom_call" | custom-call | flops 8589934592 | bytes 16777216 | tf_op jit(solution)/shard_map/expand_send/pallas_call | solution.py:446
  385.7 2.0 collective-permute-start.23
  387.7 5.3 expand_keep.4.kept
  393.0 5.4 expand_keep.5.kept
  398.4 3.6 collective-permute-done.22.refs_0_
  403.6 2.3 hop.4
  405.8 16.9 %collective-permute-done.23.refs_0_ = bf16[2,1040,256]{2,1,0:T(8,128)(2,1)} collective-permute-done((bf16[2,1040,256]{2,1,0:T(8,128)(2,1)}, bf16[2,1040,256]{2,1,0:T(8,128)(2,1)}, u32[]{:S(2)}, u32[]{:S(2)}) %collective-permute-start.23) | collective-permute-done | bytes 1064992 | tf_op jit(solution)/shard_map/ppermute | solution.py:663
  422.8 3.3 hop.5
  426.1 8.3 %restore.7 = (f32[2,1024,256]{2,1,0:T(8,128)}, f32[2,1024,256]{2,1,0:T(8,128)}) custom-call(s32[1]{0:T(128)} %bitcast.me_ref, bf16[2,1024,1024]{2,1,0:T(8,128)(2,1)} %get-tuple-element.99.normed, bf16[5,1024,1024]{2,1,0:T(8,128)(2,1)} %get-tuple-element.84.refs_0_.refs_1_.refs_2_.refs_3_, ...), custom_call_target="tpu_custom_call" | custom-call | flops 17179869184 | bytes 33554432 | tf_op jit(solution)/shard_map/restore/pallas_call | solution.py:367
  434.4 8.4 %restore.6 = (f32[2,1024,256]{2,1,0:T(8,128)}, f32[2,1024,256]{2,1,0:T(8,128)}) custom-call(s32[1]{0:T(128)} %bitcast.me_ref, bf16[2,1024,1024]{2,1,0:T(8,128)(2,1)} %get-tuple-element.99.normed, bf16[5,1024,1024]{2,1,0:T(8,128)(2,1)} %get-tuple-element.84.refs_0_.refs_1_.refs_2_.refs_3_, ...), custom_call_target="tpu_custom_call" | custom-call | flops 17179869184 | bytes 33554432 | tf_op jit(solution)/shard_map/restore/pallas_call | solution.py:367
  444.9 2.2 send.7
  448.6 2.5 collective-permute-start.32
  453.0 9.1 %collective-permute-done.27.refs_0_ = bf16[1040,256]{1,0:T(8,128)(2,1)S(1)} collective-permute-done((bf16[1040,256]{1,0:T(8,128)(2,1)S(1)}, bf16[1040,256]{1,0:T(8,128)(2,1)S(1)}, u32[]{:S(2)}, u32[]{:S(2)}) %collective-permute-start.27) | collective-permute-done | bytes 532512 | tf_op jit(solution)/shard_map/ppermute | solution.py:572
  462.1 7.6 %expand_send.7 = (bf16[2,1040,256]{2,1,0:T(8,128)(2,1)}, bf16[1024,512]{1,0:T(8,128)(2,1)S(1)}) custom-call(s32[1]{0:T(128)} %bitcast.1.place_ref, f32[2,1024,256]{2,1,0:T(8,128)S(1)} %copy-done.8, f32[2,1024,256]{2,1,0:T(8,128)} %collective-permute-done.26.mate, bf16[1040,256]{1,0:T(8,128)(2,1)S(1)} %collective-permute-done.27.refs_0_, ...), custom_call_target="tpu_custom_call" | custom-call | flops 8589934592 | bytes 16777216 | tf_op jit(solution)/shard_map/expand_send/pallas_call | solution.py:446
  472.6 7.3 %expand_send.6 = (bf16[2,1040,256]{2,1,0:T(8,128)(2,1)}, bf16[1024,512]{1,0:T(8,128)(2,1)S(1)}) custom-call(s32[1]{0:T(128)} %bitcast.1.place_ref, f32[2,1024,256]{2,1,0:T(8,128)S(1)} %copy-done.6, f32[2,1024,256]{2,1,0:T(8,128)S(1)} %collective-permute-done.24.mate, bf16[1040,256]{1,0:T(8,128)(2,1)S(1)} %collective-permute-done.25.refs_0_, ...), custom_call_target="tpu_custom_call" | custom-call | flops 8589934592 | bytes 16777216 | tf_op jit(solution)/shard_map/expand_send/pallas_call | solution.py:446
  482.6 5.4 expand_keep.7.kept
  488.0 5.4 expand_keep.6.kept
  493.3 25.6 %collective-permute-done.28.refs_0_ = bf16[2,1040,256]{2,1,0:T(8,128)(2,1)} collective-permute-done((bf16[2,1040,256]{2,1,0:T(8,128)(2,1)}, bf16[2,1040,256]{2,1,0:T(8,128)(2,1)}, u32[]{:S(2)}, u32[]{:S(2)}) %collective-permute-start.28) | collective-permute-done | bytes 1064992 | tf_op jit(solution)/shard_map/ppermute | solution.py:663
  520.5 2.5 hop.6
  523.4 27.1 %collective-permute-done.29.refs_0_ = bf16[2,1040,256]{2,1,0:T(8,128)(2,1)} collective-permute-done((bf16[2,1040,256]{2,1,0:T(8,128)(2,1)}, bf16[2,1040,256]{2,1,0:T(8,128)(2,1)}, u32[]{:S(2)}, u32[]{:S(2)}) %collective-permute-start.29) | collective-permute-done | bytes 1064992 | tf_op jit(solution)/shard_map/ppermute | solution.py:663
  550.4 2.5 hop.7
  553.3 3.3 finish.4.refs_2_
  556.6 3.3 finish.5.refs_2_
  559.8 3.3 finish.6.refs_2_
  563.1 13.1 %collective-permute-done.30.refs_1_ = bf16[1,1040,256]{2,1,0:T(8,128)(2,1)S(1)} collective-permute-done((bf16[1,1040,256]{2,1,0:T(8,128)(2,1)S(1)}, bf16[1,1040,256]{2,1,0:T(8,128)(2,1)S(1)}, u32[]{:S(2)}, u32[]{:S(2)}) %collective-permute-start.30) | collective-permute-done | bytes 532512 | tf_op jit(solution)/shard_map/ppermute | solution.py:663
  576.2 3.3 finish.7
  (89 shorter events, 40.1 us)
Async XLA Ops:
  0.6 49.0 %collective-permute-start = (bf16[1024,1024]{1,0:T(8,128)(2,1)}, bf16[1024,1024]{1,0:T(8,128)(2,1)}, u32[]{:S(2)}, u32[]{:S(2)}) collective-permute-start(bf16[1024,1024]{1,0:T(8,128)(2,1)} %param.8), channel_id=1, source_target_pairs={{0,2},{1,3},{2,0},{3,1},{4,6},{5,7},{6,4},{7,5},{8,10},{9,11},{10,... | collective-permute-start | bytes 6291464 | tf_op jit(solution)/shard_map/ppermute | solution.py:572
  3.6 48.4 %collective-permute-start.3 = (bf16[1024,1024]{1,0:T(8,128)(2,1)}, bf16[1024,1024]{1,0:T(8,128)(2,1)S(1)}, u32[]{:S(2)}, u32[]{:S(2)}) collective-permute-start(bf16[1024,1024]{1,0:T(8,128)(2,1)} %refs_2_.1), channel_id=1, source_target_pairs={{0,4},{4,8},{8,12},{1,5},{5,9},{9,13},{2,6},{6,10},{10,14},{3,7},{... | collective-permute-start | bytes 6291464 | tf_op jit(solution)/shard_map/ppermute | solution.py:589
  7.2 49.0 %collective-permute-start.5 = (bf16[1024,1024]{1,0:T(8,128)(2,1)}, bf16[1024,1024]{1,0:T(8,128)(2,1)}, u32[]{:S(2)}, u32[]{:S(2)}) collective-permute-start(bf16[1024,1024]{1,0:T(8,128)(2,1)} %refs_2_.1), channel_id=1, source_target_pairs={{4,0},{8,4},{12,8},{5,1},{9,5},{13,9},{6,2},{10,6},{14,10},{7,3},{... | collective-permute-start | bytes 6291464 | tf_op jit(solution)/shard_map/ppermute | solution.py:592
  8.5 52.8 %collective-permute-start.1 = (bf16[1024,1024]{1,0:T(8,128)(2,1)}, bf16[1024,1024]{1,0:T(8,128)(2,1)}, u32[]{:S(2)}, u32[]{:S(2)}) collective-permute-start(bf16[1024,1024]{1,0:T(8,128)(2,1)} %param.8), channel_id=1, source_target_pairs={{0,1},{1,0},{2,3},{3,2},{4,5},{5,4},{6,7},{7,6},{8,9},{9,8},{10,11... | collective-permute-start | bytes 6291464 | tf_op jit(solution)/shard_map/ppermute | solution.py:572
  49.6 13.6 %collective-permute-start.2 = (bf16[1024,1024]{1,0:T(8,128)(2,1)}, bf16[1024,1024]{1,0:T(8,128)(2,1)}, u32[]{:S(2)}, u32[]{:S(2)}) collective-permute-start(bf16[1024,1024]{1,0:T(8,128)(2,1)} %collective-permute-done), channel_id=1, source_target_pairs={{0,1},{1,0},{2,3},{3,2},{4,5},{5,4},{6,7},{7,6},{8,9},{9,8},{10,11... | collective-permute-start | bytes 6291464 | tf_op jit(solution)/shard_map/ppermute | solution.py:572
  52.0 13.1 %collective-permute-start.4 = (bf16[1024,1024]{1,0:T(8,128)(2,1)S(1)}, bf16[1024,1024]{1,0:T(8,128)(2,1)}, u32[]{:S(2)}, u32[]{:S(2)}) collective-permute-start(bf16[1024,1024]{1,0:T(8,128)(2,1)S(1)} %collective-permute-done.3.refs_1_), channel_id=1, source_target_pairs={{4,8},{8,12},{5,9},{9,13},{6,10},{10,14},{7,11},{11,15},{20,24},{2... | collective-permute-start | bytes 6291464 | tf_op jit(solution)/shard_map/ppermute | solution.py:589
  56.3 49.5 %collective-permute-start.6 = (bf16[1024,1024]{1,0:T(8,128)(2,1)}, bf16[1024,1024]{1,0:T(8,128)(2,1)}, u32[]{:S(2)}, u32[]{:S(2)}) collective-permute-start(bf16[1024,1024]{1,0:T(8,128)(2,1)} %collective-permute-done.5.refs_3_), channel_id=1, source_target_pairs={{4,0},{8,4},{5,1},{9,5},{6,2},{10,6},{7,3},{11,7},{20,16},{24,20},... | collective-permute-start | bytes 6291464 | tf_op jit(solution)/shard_map/ppermute | solution.py:592
  57.6 1.6 copy-start.19
  65.1 3.3 copy-start.16
  105.8 17.9 %collective-permute-start.7 = (bf16[1024,1024]{1,0:T(8,128)(2,1)}, bf16[1024,1024]{1,0:T(8,128)(2,1)}, u32[]{:S(2)}, u32[]{:S(2)}) collective-permute-start(bf16[1024,1024]{1,0:T(8,128)(2,1)} %collective-permute-done.4.refs_0_), channel_id=1, source_target_pairs={{8,12},{9,13},{10,14},{11,15},{24,28},{25,29},{26,30},{27,31}} | collective-permute-start | bytes 6291464 | tf_op jit(solution)/shard_map/ppermute | solution.py:589
  107.7 47.6 %collective-permute-start.8 = (bf16[1024,1024]{1,0:T(8,128)(2,1)}, bf16[1024,1024]{1,0:T(8,128)(2,1)}, u32[]{:S(2)}, u32[]{:S(2)}) collective-permute-start(bf16[1024,1024]{1,0:T(8,128)(2,1)} %collective-permute-done.6.refs_4_), channel_id=1, source_target_pairs={{4,0},{5,1},{6,2},{7,3},{20,16},{21,17},{22,18},{23,19}} | collective-permute-start | bytes 6291464 | tf_op jit(solution)/shard_map/ppermute | solution.py:592
  155.3 43.8 %collective-permute-start.9 = (bf16[1024,1024]{1,0:T(8,128)(2,1)}, bf16[1024,1024]{1,0:T(8,128)(2,1)S(1)}, u32[]{:S(2)}, u32[]{:S(2)}) collective-permute-start(bf16[1024,1024]{1,0:T(8,128)(2,1)} %piece), channel_id=1, source_target_pairs={{0,4},{4,8},{8,12},{1,5},{5,9},{9,13},{2,6},{6,10},{10,14},{3,7},{... | collective-permute-start | bytes 6291464 | tf_op jit(solution)/shard_map/ppermute | solution.py:589
  156.9 46.5 %collective-permute-start.10 = (bf16[1024,1024]{1,0:T(8,128)(2,1)}, bf16[1024,1024]{1,0:T(8,128)(2,1)}, u32[]{:S(2)}, u32[]{:S(2)}) collective-permute-start(bf16[1024,1024]{1,0:T(8,128)(2,1)} %piece), channel_id=1, source_target_pairs={{4,0},{8,4},{12,8},{5,1},{9,5},{13,9},{6,2},{10,6},{14,10},{7,3},{... | collective-permute-start | bytes 6291464 | tf_op jit(solution)/shard_map/ppermute | solution.py:592
  199.1 4.3 copy-start.18
  203.4 16.9 %collective-permute-start.11 = (bf16[1040,1024]{1,0:T(8,128)(2,1)}, bf16[1040,1024]{1,0:T(8,128)(2,1)}, u32[]{:S(2)}, u32[]{:S(2)}) collective-permute-start(bf16[1040,1024]{1,0:T(8,128)(2,1)} %get-tuple-element.64), channel_id=1, source_target_pairs={{0,1},{1,0},{2,3},{3,2},{4,5},{5,4},{6,7},{7,6},{8,9},{9,8},{10,11... | collective-permute-start | bytes 6389768 | tf_op jit(solution)/shard_map/ppermute | solution.py:572
  203.4 49.0 %collective-permute-start.12 = (bf16[1040,1024]{1,0:T(8,128)(2,1)}, bf16[1040,1024]{1,0:T(8,128)(2,1)S(1)}, u32[]{:S(2)}, u32[]{:S(2)}) collective-permute-start(bf16[1040,1024]{1,0:T(8,128)(2,1)} %get-tuple-element.64), channel_id=1, source_target_pairs={{0,2},{1,3},{2,0},{3,1},{4,6},{5,7},{6,4},{7,5},{8,10},{9,11},{10,... | collective-permute-start | bytes 6389768 | tf_op jit(solution)/shard_map/ppermute | solution.py:572
  203.9 50.0 %collective-permute-start.14 = (bf16[1024,1024]{1,0:T(8,128)(2,1)}, bf16[1024,1024]{1,0:T(8,128)(2,1)}, u32[]{:S(2)}, u32[]{:S(2)}) collective-permute-start(bf16[1024,1024]{1,0:T(8,128)(2,1)} %collective-permute-done.10.piece), channel_id=1, source_target_pairs={{4,0},{8,4},{5,1},{9,5},{6,2},{10,6},{7,3},{11,7},{20,16},{24,20},... | collective-permute-start | bytes 6291464 | tf_op jit(solution)/shard_map/ppermute | solution.py:592
  205.2 50.0 %collective-permute-start.15 = (bf16[1024,1024]{1,0:T(8,128)(2,1)}, bf16[1024,1024]{1,0:T(8,128)(2,1)}, u32[]{:S(2)}, u32[]{:S(2)}) collective-permute-start(bf16[1024,1024]{1,0:T(8,128)(2,1)} %copy-done.18), channel_id=1, source_target_pairs={{4,8},{8,12},{5,9},{9,13},{6,10},{10,14},{7,11},{11,15},{20,24},{2... | collective-permute-start | bytes 6291464 | tf_op jit(solution)/shard_map/ppermute | solution.py:589
  252.3 9.3 %copy-start.17 = (bf16[1040,1024]{1,0:T(8,128)(2,1)}, bf16[1040,1024]{1,0:T(8,128)(2,1)S(1)}, u32[]{:S(2)}) copy-start(bf16[1040,1024]{1,0:T(8,128)(2,1)S(1)} %collective-permute-done.12.message.scales) | copy-start | bytes 6389764
  252.3 19.7 %collective-permute-start.13 = (bf16[1040,1024]{1,0:T(8,128)(2,1)S(1)}, bf16[1040,1024]{1,0:T(8,128)(2,1)}, u32[]{:S(2)}, u32[]{:S(2)}) collective-permute-start(bf16[1040,1024]{1,0:T(8,128)(2,1)S(1)} %collective-permute-done.12.message.scales), channel_id=1, source_target_pairs={{0,1},{1,0},{2,3},{3,2},{4,5},{5,4},{6,7},{7,6},{8,9},{9,8},{10,11... | collective-permute-start | bytes 6389768 | tf_op jit(solution)/shard_map/ppermute | solution.py:572
  253.9 49.1 %collective-permute-start.16 = (bf16[1024,1024]{1,0:T(8,128)(2,1)}, bf16[1024,1024]{1,0:T(8,128)(2,1)}, u32[]{:S(2)}, u32[]{:S(2)}) collective-permute-start(bf16[1024,1024]{1,0:T(8,128)(2,1)} %collective-permute-done.14.piece), channel_id=1, source_target_pairs={{4,0},{5,1},{6,2},{7,3},{20,16},{21,17},{22,18},{23,19}} | collective-permute-start | bytes 6291464 | tf_op jit(solution)/shard_map/ppermute | solution.py:592
  255.2 47.8 %collective-permute-start.17 = (bf16[1024,1024]{1,0:T(8,128)(2,1)}, bf16[1024,1024]{1,0:T(8,128)(2,1)}, u32[]{:S(2)}, u32[]{:S(2)}) collective-permute-start(bf16[1024,1024]{1,0:T(8,128)(2,1)} %collective-permute-done.15.piece), channel_id=1, source_target_pairs={{8,12},{9,13},{10,14},{11,15},{24,28},{25,29},{26,30},{27,31}} | collective-permute-start | bytes 6291464 | tf_op jit(solution)/shard_map/ppermute | solution.py:589
  257.2 20.9 %copy-start.11 = (s32[2]{0:T(128)}, s32[2]{0:T(128)S(1)}, u32[]{:S(2)}) copy-start(s32[2]{0:T(128)S(1)} %pad_add_fusion.at_ref) | copy-start | bytes 28
  299.6 2.0 copy-start.5
  335.1 8.9 %copy-start.10 = (f32[2,1024,256]{2,1,0:T(8,128)S(1)}, f32[2,1024,256]{2,1,0:T(8,128)}, u32[]{:S(2)}) copy-start(f32[2,1024,256]{2,1,0:T(8,128)} %get-tuple-element.88.keep) | copy-start | bytes 6291460
  335.1 8.8 %collective-permute-start.20 = (f32[2,1024,256]{2,1,0:T(8,128)}, f32[2,1024,256]{2,1,0:T(8,128)}, u32[]{:S(2)}, u32[]{:S(2)}) collective-permute-start(f32[2,1024,256]{2,1,0:T(8,128)} %get-tuple-element.89), channel_id=1, source_target_pairs={{0,1},{1,0},{2,3},{3,2},{4,5},{5,4},{6,7},{7,6},{8,9},{9,8},{10,11... | collective-permute-start | bytes 6291464 | tf_op jit(solution)/shard_map/ppermute | solution.py:572
  343.6 4.4 collective-permute-start.18
  344.0 4.0 copy-start.9
  346.2 15.0 %collective-permute-start.21 = (bf16[1040,256]{1,0:T(8,128)(2,1)S(1)}, bf16[1040,256]{1,0:T(8,128)(2,1)S(1)}, u32[]{:S(2)}, u32[]{:S(2)}) collective-permute-start(bf16[1040,256]{1,0:T(8,128)(2,1)S(1)} %send.5), channel_id=1, source_target_pairs={{0,2},{1,3},{2,0},{3,1},{4,6},{5,7},{6,4},{7,5},{8,10},{9,11},{10,... | collective-permute-start | bytes 1597448 | tf_op jit(solution)/shard_map/ppermute | solution.py:572
  348.8 28.5 %collective-permute-start.19 = (bf16[1040,256]{1,0:T(8,128)(2,1)S(1)}, bf16[1040,256]{1,0:T(8,128)(2,1)S(1)}, u32[]{:S(2)}, u32[]{:S(2)}) collective-permute-start(bf16[1040,256]{1,0:T(8,128)(2,1)S(1)} %send.4), channel_id=1, source_target_pairs={{0,2},{1,3},{2,0},{3,1},{4,6},{5,7},{6,4},{7,5},{8,10},{9,11},{10,... | collective-permute-start | bytes 1597448 | tf_op jit(solution)/shard_map/ppermute | solution.py:572
  368.7 1.1 copy-start.12
  369.8 32.2 %collective-permute-start.22 = (bf16[2,1040,256]{2,1,0:T(8,128)(2,1)}, bf16[2,1040,256]{2,1,0:T(8,128)(2,1)S(1)}, u32[]{:S(2)}, u32[]{:S(2)}) collective-permute-start(bf16[2,1040,256]{2,1,0:T(8,128)(2,1)} %get-tuple-element.92), channel_id=1, source_target_pairs={{0,4},{4,0},{8,12},{12,8},{1,5},{5,1},{9,13},{13,9},{2,6},{6,2},{1... | collective-permute-start | bytes 3194888 | tf_op jit(solution)/shard_map/ppermute | solution.py:663
  384.7 1.0 copy-start.15
  385.7 37.1 %collective-permute-start.23 = (bf16[2,1040,256]{2,1,0:T(8,128)(2,1)}, bf16[2,1040,256]{2,1,0:T(8,128)(2,1)}, u32[]{:S(2)}, u32[]{:S(2)}) collective-permute-start(bf16[2,1040,256]{2,1,0:T(8,128)(2,1)} %get-tuple-element.94), channel_id=1, source_target_pairs={{0,4},{4,0},{8,12},{12,8},{1,5},{5,1},{9,13},{13,9},{2,6},{6,2},{1... | collective-permute-start | bytes 3194888 | tf_op jit(solution)/shard_map/ppermute | solution.py:663
  398.4 24.4 %copy-start = (f32[2,1024,256]{2,1,0:T(8,128)S(1)}, f32[2,1024,256]{2,1,0:T(8,128)}, u32[]{:S(2)}) copy-start(f32[2,1024,256]{2,1,0:T(8,128)} %expand_keep.4.kept) | copy-start | bytes 6291460
  402.0 1.6 copy-start.1
  434.4 8.8 %collective-permute-start.26 = (f32[2,1024,256]{2,1,0:T(8,128)}, f32[2,1024,256]{2,1,0:T(8,128)}, u32[]{:S(2)}, u32[]{:S(2)}) collective-permute-start(f32[2,1024,256]{2,1,0:T(8,128)} %get-tuple-element.101), channel_id=1, source_target_pairs={{0,1},{1,0},{2,3},{3,2},{4,5},{5,4},{6,7},{7,6},{8,9},{9,8},{10,11... | collective-permute-start | bytes 6291464 | tf_op jit(solution)/shard_map/ppermute | solution.py:572
  442.8 8.7 %collective-permute-start.24 = (f32[2,1024,256]{2,1,0:T(8,128)}, f32[2,1024,256]{2,1,0:T(8,128)S(1)}, u32[]{:S(2)}, u32[]{:S(2)}) collective-permute-start(f32[2,1024,256]{2,1,0:T(8,128)} %get-tuple-element.97), channel_id=1, source_target_pairs={{0,1},{1,0},{2,3},{3,2},{4,5},{5,4},{6,7},{7,6},{8,9},{9,8},{10,11... | collective-permute-start | bytes 6291464 | tf_op jit(solution)/shard_map/ppermute | solution.py:572
  443.3 1.6 copy-start.7
  444.9 6.7 %copy-start.6 = (f32[2,1024,256]{2,1,0:T(8,128)S(1)}, f32[2,1024,256]{2,1,0:T(8,128)}, u32[]{:S(2)}) copy-start(f32[2,1024,256]{2,1,0:T(8,128)} %get-tuple-element.96.keep) | copy-start | bytes 6291460
  447.1 15.0 %collective-permute-start.27 = (bf16[1040,256]{1,0:T(8,128)(2,1)S(1)}, bf16[1040,256]{1,0:T(8,128)(2,1)S(1)}, u32[]{:S(2)}, u32[]{:S(2)}) collective-permute-start(bf16[1040,256]{1,0:T(8,128)(2,1)S(1)} %send.7), channel_id=1, source_target_pairs={{0,2},{1,3},{2,0},{3,1},{4,6},{5,7},{6,4},{7,5},{8,10},{9,11},{10,... | collective-permute-start | bytes 1597448 | tf_op jit(solution)/shard_map/ppermute | solution.py:572
  448.6 107.9 %collective-permute-start.32 = (bf16[1,1040,256]{2,1,0:T(8,128)(2,1)}, bf16[1,1040,256]{2,1,0:T(8,128)(2,1)S(1)}, u32[]{:S(2)}, u32[]{:S(2)}) collective-permute-start(bf16[1,1040,256]{2,1,0:T(8,128)(2,1)} %hop.5), channel_id=1, source_target_pairs={{0,8},{4,12},{8,0},{12,4},{1,9},{5,13},{9,1},{13,5},{2,10},{6,14},... | collective-permute-start | bytes 1597448 | tf_op jit(solution)/shard_map/ppermute | solution.py:663
  451.1 102.2 %collective-permute-start.33 = (bf16[1,1040,256]{2,1,0:T(8,128)(2,1)}, bf16[1,1040,256]{2,1,0:T(8,128)(2,1)}, u32[]{:S(2)}, u32[]{:S(2)}) collective-permute-start(bf16[1,1040,256]{2,1,0:T(8,128)(2,1)} %hop.4), channel_id=1, source_target_pairs={{0,8},{4,12},{8,0},{12,4},{1,9},{5,13},{9,1},{13,5},{2,10},{6,14},... | collective-permute-start | bytes 1597448 | tf_op jit(solution)/shard_map/ppermute | solution.py:663
  451.5 10.5 %copy-start.8 = (f32[2,1024,256]{2,1,0:T(8,128)S(1)}, f32[2,1024,256]{2,1,0:T(8,128)}, u32[]{:S(2)}) copy-start(f32[2,1024,256]{2,1,0:T(8,128)} %get-tuple-element.100.keep) | copy-start | bytes 6291460
  452.4 20.2 %collective-permute-start.25 = (bf16[1040,256]{1,0:T(8,128)(2,1)S(1)}, bf16[1040,256]{1,0:T(8,128)(2,1)S(1)}, u32[]{:S(2)}, u32[]{:S(2)}) collective-permute-start(bf16[1040,256]{1,0:T(8,128)(2,1)S(1)} %send.6), channel_id=1, source_target_pairs={{0,2},{1,3},{2,0},{3,1},{4,6},{5,7},{6,4},{7,5},{8,10},{9,11},{10,... | collective-permute-start | bytes 1597448 | tf_op jit(solution)/shard_map/ppermute | solution.py:572
  469.7 1.0 copy-start.13
  470.6 48.3 %collective-permute-start.28 = (bf16[2,1040,256]{2,1,0:T(8,128)(2,1)}, bf16[2,1040,256]{2,1,0:T(8,128)(2,1)}, u32[]{:S(2)}, u32[]{:S(2)}) collective-permute-start(bf16[2,1040,256]{2,1,0:T(8,128)(2,1)} %get-tuple-element.104), channel_id=1, source_target_pairs={{0,4},{4,0},{8,12},{12,8},{1,5},{5,1},{9,13},{13,9},{2,6},{6,2},{1... | collective-permute-start | bytes 3194888 | tf_op jit(solution)/shard_map/ppermute | solution.py:663
  479.9 1.0 copy-start.14
  480.9 69.6 %collective-permute-start.29 = (bf16[2,1040,256]{2,1,0:T(8,128)(2,1)}, bf16[2,1040,256]{2,1,0:T(8,128)(2,1)}, u32[]{:S(2)}, u32[]{:S(2)}) collective-permute-start(bf16[2,1040,256]{2,1,0:T(8,128)(2,1)} %get-tuple-element.106), channel_id=1, source_target_pairs={{0,4},{4,0},{8,12},{12,8},{1,5},{5,1},{9,13},{13,9},{2,6},{6,2},{1... | collective-permute-start | bytes 3194888 | tf_op jit(solution)/shard_map/ppermute | solution.py:663
  493.3 57.1 %copy-start.3 = (f32[2,1024,256]{2,1,0:T(8,128)S(1)}, f32[2,1024,256]{2,1,0:T(8,128)}, u32[]{:S(2)}) copy-start(f32[2,1024,256]{2,1,0:T(8,128)} %expand_keep.6.kept) | copy-start | bytes 6291460
  518.9 1.6 copy-start.4
  523.0 30.2 %copy-start.2 = (f32[2,1024,256]{2,1,0:T(8,128)S(1)}, f32[2,1024,256]{2,1,0:T(8,128)}, u32[]{:S(2)}) copy-start(f32[2,1024,256]{2,1,0:T(8,128)} %expand_keep.5.kept) | copy-start | bytes 6291460
  523.0 36.8 %collective-permute-start.31 = (bf16[1,1040,256]{2,1,0:T(8,128)(2,1)S(1)}, bf16[1,1040,256]{2,1,0:T(8,128)(2,1)S(1)}, u32[]{:S(2)}, u32[]{:S(2)}) collective-permute-start(bf16[1,1040,256]{2,1,0:T(8,128)(2,1)S(1)} %hop.6), channel_id=1, source_target_pairs={{0,8},{4,12},{8,0},{12,4},{1,9},{5,13},{9,1},{13,5},{2,10},{6,14},... | collective-permute-start | bytes 1597448 | tf_op jit(solution)/shard_map/ppermute | solution.py:663
  552.9 23.3 %collective-permute-start.30 = (bf16[1,1040,256]{2,1,0:T(8,128)(2,1)S(1)}, bf16[1,1040,256]{2,1,0:T(8,128)(2,1)S(1)}, u32[]{:S(2)}, u32[]{:S(2)}) collective-permute-start(bf16[1,1040,256]{2,1,0:T(8,128)(2,1)S(1)} %hop.7), channel_id=1, source_target_pairs={{0,8},{4,12},{8,0},{12,4},{1,9},{5,13},{9,1},{13,5},{2,10},{6,14},... | collective-permute-start | bytes 1597448 | tf_op jit(solution)/shard_map/ppermute | solution.py:663

commit v12 on v11

--- a/solution.py
+++ b/solution.py
@@ -336,48 +336,57 @@
             jax.ShapeDtypeStruct((rows, width), F32),
             jax.ShapeDtypeStruct((2, rows, width), BF16),
         ],
-        compiler_params=params(60),
+        compiler_params=params(40),
         cost_estimate=cost(4 * rows * width * depth, 30 * rows * width),
         name="rotate",
     )(at, part, above, below, first, second, *pieces)
 
 
-def restore_kernel(me_ref, normed, *refs, cols):
-    flipped, (keep, mate) = refs[:cols], refs[cols:]
+def restore_kernel(me_ref, normed, *refs, cols, spans):
+    flipped, outs = refs[: cols * spans], refs[cols * spans :]
     tile = normed.shape[1]
+    wide = flipped[0].shape[2]
+    piece = outs[0].shape[2]
     both = normed[...].reshape(2 * tile, normed.shape[2])
     for distance in range(cols):
-        term = dot(both, flipped[distance][0], ((1,), (0,)))
-        (mate if distance % 2 else keep)[distance // 2] = term[:tile] + term[tile:]
-
-
-def restore(me, normed, flipped, cols, chunk, piece):
+        for span in range(spans):
+            term = dot(both, flipped[distance * spans + span][0], ((1,), (0,)))
+            term = term[:tile] + term[tile:]
+            for at in range(wide // piece):
+                chunk = span * (wide // piece) + at
+                out = outs[2 * chunk + distance % 2]
+                out[distance // 2] = term[:, at * piece : (at + 1) * piece]
+
+
+def restore(me, normed, flipped, cols, piece):
     _, depth, inner = normed.shape
     wide = flipped.shape[2]
+    spans = inner // wide
     tile = min(256, depth)
     out = pl.BlockSpec((cols // 2, tile, piece), lambda i, s: (0, i, 0))
 
-    def columns(distance):
-        def at(i, s):
-            start = (s[0] ^ distance) * inner + chunk * piece
-            return start // wide, 0, lax.rem(start, wide) // piece
-
-        return pl.BlockSpec((1, inner, piece), at)
-
-    return pl.pallas_call(
-        functools.partial(restore_kernel, cols=cols),
+    def columns(distance, span):
+        return pl.BlockSpec(
+            (1, inner, wide),
+            lambda i, s: ((s[0] ^ distance) * spans + span, 0, 0),
+            pipeline_mode=pl.Buffered(1),
+        )
+
+    outs = pl.pallas_call(
+        functools.partial(restore_kernel, cols=cols, spans=spans),
         grid_spec=pltpu.PrefetchScalarGridSpec(
             num_scalar_prefetch=1,
             grid=(depth // tile,),
             in_specs=[pl.BlockSpec((2, tile, inner), lambda i, s: (0, i, 0))]
-            + [columns(distance) for distance in range(cols)],
-            out_specs=[out, out],
-        ),
-        out_shape=[jax.ShapeDtypeStruct((cols // 2, depth, piece), F32)] * 2,
-        compiler_params=params(60),
-        cost_estimate=cost(4 * depth * inner * piece * cols, 8 * depth * piece * cols, 4),
+            + [columns(distance, span) for distance in range(cols) for span in range(spans)],
+            out_specs=[out] * (2 * CHUNKS),
+        ),
+        out_shape=[jax.ShapeDtypeStruct((cols // 2, depth, piece), F32)] * (2 * CHUNKS),
+        compiler_params=params(44),
+        cost_estimate=cost(4 * depth * inner * inner * cols, 8 * depth * inner * cols),
         name="restore",
-    )(me, normed, *([flipped] * cols))
+    )(me, normed, *([flipped] * (cols * spans)))
+    return [(outs[2 * chunk], outs[2 * chunk + 1]) for chunk in range(CHUNKS)]
 
 
 def summed(keep, mate, codes):
@@ -654,7 +663,7 @@
             at, part, pieces, above, below, first_moment, second_moment, lines
         )
         if aligned:
-            last = jnp.where(place == 0, above, below)
+            last = jnp.where(place == 0, after(above, normed), below)
             there = jnp.where((place == 0) | (place == far), far - place, lines)
             held = put(jnp.reshape(there, (1,)), last, held, lines + 1)
         flipped = held[1]
@@ -677,12 +686,6 @@
 
         products, halves, sent, outgoing, second = [], [], [], [], {}
 
-        def sums(chunk, ready):
-            keep, mate = restore(me_now, ready, flipped, cols, chunk, piece)
-            mate = swap(mate, 1)
-            halves.append((keep, mate))
-            sent.append([send(keep, mate, distance, []) for distance in range(2, cols, 2)])
-
         def multiply(chunk, *before):
             codes = [swap(code, 2 * index + 2) for index, code in enumerate(sent[chunk])]
             if codes and before:
@@ -691,21 +694,15 @@
             outgoing.append(message)
             products.append((expand_keep(spot, both, left, depth), [cross(message, 1)]))
 
-        sums(0, normed)
-        sums(1, normed)
-        multiply(0, *sent[1])
-        multiply(1)
-        firsts = [product[1][0] for product in products]
-        later_hops(0)
-        later_hops(1)
-        for chunk in range(2, CHUNKS):
-            sums(chunk, after(normed, second.get(chunk % 2, firsts[chunk % 2]), outgoing[1]))
-        for chunk in range(2, CHUNKS):
-            multiply(chunk)
+        for keep, mate in restore(me_now, normed, flipped, cols, piece):
+            mate = swap(mate, 1)
+            halves.append((keep, mate))
+            sent.append([send(keep, mate, distance, []) for distance in range(2, cols, 2)])
+        for chunk in range(CHUNKS):
+            multiply(chunk, *(outgoing[-1:]))
         update = None
         for chunk in range(CHUNKS):
-            if chunk >= CHUNKS - 2:
-                later_hops(chunk)
+            later_hops(chunk)
             update = finish(*products[chunk], update, chunk, width)
         return (new_first, new_second, update)
 

time: 581 us -> 550 us (0.947)
  waiting for transfers between devices: 278 us -> 257 us
  Pallas kernels: 229 us -> 211 us
  starting transfers between devices: 47.2 us -> 54.7 us
    ppermute x6, waiting for transfers between devices: 25.9 us -> 3.63 us  [up(): return lax.ppermute(value, 'row', [(i, i + 1) for i in senders])]
    ppermute x6, waiting for transfers between devices: 78.4 us -> 100 us  [down(): return lax.ppermute(value, 'row', [(i, i - 1) for i in senders])]
    ppermute x14, waiting for transfers between devices: 87.3 us -> 75 us  [swap(): return lax.ppermute(value, 'col', [(i, i ^ distance) for i in range(cols)])]
    pallas_call x4 -> x1, Pallas kernels: 33.6 us -> 23.9 us  [restore(): pl.pallas_call(functools.partial(restore_kernel, cols=cols, spans=spans),...]
    ppermute x8, waiting for transfers between devices: 86.3 us -> 78.6 us  [cross(): return lax.ppermute(value, 'row', [(i, i ^ distance) for i in range(lines)])]
  transfers between devices with their start and end apart: 34 -> 34, of which waited for: 19 -> 17; matrix products, arithmetic and copies ran while one was open for 1% -> 1% of each run, Pallas kernels for 31% -> 30%
where the time goes in v12:
time: 550 us; the launch traced here: 549 us
  waiting for transfers between devices  257 us (47%)
  Pallas kernels  211 us (38%)
  starting transfers between devices  54.7 us (10%)
  local copies, waits for them, and re-layouts  22.7 us (4%)
    ppermute x6, waiting for transfers between devices, down(): return lax.ppermute(value, 'row', [(i, i - 1) for i in senders])  100 us
    ppermute x8, waiting for transfers between devices, cross(): return lax.ppermute(value, 'row', [(i, i ^ distance) for i in range(lines)])  78.6 us
    ppermute x14, waiting for transfers between devices, swap(): return lax.ppermute(value, 'col', [(i, i ^ distance) for i in range(cols)])  75 us
    pallas_call x4, Pallas kernels, expand_send(): pl.pallas_call(functools.partial(expand_send_kernel, tile=min(64, depth))...  29.3 us
    pallas_call x6, Pallas kernels, put(): pl.pallas_call(put_kernel, grid_spec=pltpu.PrefetchScalarGridSpec(num_sca...  26.2 us
    pallas_call x2, Pallas kernels, halfway(): pl.pallas_call(functools.partial(halfway_kernel, offsets=offsets, lines=l...  24.3 us
    pallas_call x1, Pallas kernels, restore(): pl.pallas_call(functools.partial(restore_kernel, cols=cols, spans=spans),...  23.9 us
    pallas_call x4, Pallas kernels, expand_keep(): pl.pallas_call(expand_keep_kernel, grid_spec=pltpu.PrefetchScalarGridSpec...  21.6 us
  transfers between devices with their start and end apart: 34, of which 17 were waited for; matrix products, arithmetic and copies ran while one was open for 1% of the time, Pallas kernels for 30%

profile of v12, /device:TPU:0, one launch (start us, length us, event | category | flops | bytes accessed | tf_op | source)
XLA Modules:
  0.0 548.8 jit_solution(1447192539727814111)
XLA Ops:
  0.6 3.0 collective-permute-start
  3.6 3.6 collective-permute-start.3
  8.6 41.0 %collective-permute-done = bf16[1024,1024]{1,0:T(8,128)(2,1)} collective-permute-done((bf16[1024,1024]{1,0:T(8,128)(2,1)}, bf16[1024,1024]{1,0:T(8,128)(2,1)}, u32[]{:S(2)}, u32[]{:S(2)}) %collective-permute-start) | collective-permute-done | bytes 2097184 | tf_op jit(solution)/shard_map/ppermute | solution.py:581
  49.6 2.4 collective-permute-done.3.refs_1_
  52.0 2.0 collective-permute-start.4
  54.0 2.2 collective-permute-done.5.refs_3_
  59.5 1.9 bitcast_dynamic-update-slice_fusion.2
  61.3 1.9 bitcast_dynamic-update-slice_fusion.1
  63.2 1.9 bitcast_dynamic-update-slice_fusion
  65.1 3.3 copy-done.16
  68.4 37.3 %collective-permute-done.6.refs_4_ = bf16[1024,1024]{1,0:T(8,128)(2,1)} collective-permute-done((bf16[1024,1024]{1,0:T(8,128)(2,1)}, bf16[1024,1024]{1,0:T(8,128)(2,1)}, u32[]{:S(2)}, u32[]{:S(2)}) %collective-permute-start.6) | collective-permute-done | bytes 2097184 | tf_op jit(solution)/shard_map/ppermute | solution.py:601
  105.7 2.0 collective-permute-start.7
  109.0 14.7 %halfway.2.refs_2_ = f32[1024,1024]{1,0:T(8,128)} custom-call(s32[1]{0:T(128)} %bitcast.1.place_ref, bf16[4096,1024]{1,0:T(8,128)(2,1)} %bitcast.17, bf16[1024,1024]{1,0:T(8,128)(2,1)} %collective-permute-done.4.refs_0_, bf16[1024,1024]{1,0:T(8,128)(2,1)S(1)} %collective-permute-done.3.refs_1_, bf16[1024,1024]{1,0:T(8,128)(2,1)} %refs_2_.1, ...), custom_call_target="tpu_custom_call" | custom-call | flops 2576980480 | bytes 2516582 | tf_op jit(solution)/shard_map/halfway/pallas_call | solution.py:114
  123.7 31.6 %collective-permute-done.8.refs_1_ = bf16[1024,1024]{1,0:T(8,128)(2,1)} collective-permute-done((bf16[1024,1024]{1,0:T(8,128)(2,1)}, bf16[1024,1024]{1,0:T(8,128)(2,1)}, u32[]{:S(2)}, u32[]{:S(2)}) %collective-permute-start.8) | collective-permute-done | bytes 2097184 | tf_op jit(solution)/shard_map/ppermute | solution.py:601
  156.5 4.7 collective-permute-start.9
  161.2 9.6 %halfway.3.value = f32[1024,1024]{1,0:T(8,128)} custom-call(s32[1]{0:T(128)} %bitcast.1.place_ref, bf16[4096,1024]{1,0:T(8,128)(2,1)} %bitcast.18, bf16[1024,1024]{1,0:T(8,128)(2,1)} %collective-permute-done.7.refs_0_, bf16[1024,1024]{1,0:T(8,128)(2,1)} %collective-permute-done.8.refs_1_, f32[1024,1024]{1,0:T(8,128)} %halfway.2.refs_2_), custom_call_target="tpu_custom_call" | custom-call | flops 2576980480 | bytes 2516582 | tf_op jit(solution)/shard_map/halfway/pallas_call | solution.py:114
  170.8 7.9 %pack.1 = (bf16[2,1024,1024]{2,1,0:T(8,128)(2,1)}, bf16[1040,1024]{1,0:T(8,128)(2,1)}) custom-call(f32[1024,1024]{1,0:T(8,128)} %halfway.3.value), custom_call_target="tpu_custom_call" | custom-call | flops 125829120 | bytes 3145728 | tf_op jit(solution)/shard_map/pack/pallas_call | solution.py:147
  178.8 23.1 %collective-permute-done.10.piece = bf16[1024,1024]{1,0:T(8,128)(2,1)} collective-permute-done((bf16[1024,1024]{1,0:T(8,128)(2,1)}, bf16[1024,1024]{1,0:T(8,128)(2,1)}, u32[]{:S(2)}, u32[]{:S(2)}) %collective-permute-start.10) | collective-permute-done | bytes 2097184 | tf_op jit(solution)/shard_map/ppermute | solution.py:601
  206.3 2.0 collective-permute-start.15
  208.3 4.4 put.6
  212.6 4.4 put.7
  217.0 4.3 put.8
  222.6 6.1 %unpack.3.refs_1_ = bf16[2,1024,1024]{2,1,0:T(8,128)(2,1)} custom-call(bf16[1040,1024]{1,0:T(8,128)(2,1)} %copy-done.17, bf16[1040,1024]{1,0:T(8,128)(2,1)} %copy-done.17), custom_call_target="tpu_custom_call" | custom-call | flops 125829120 | bytes 1887436 | tf_op jit(solution)/shard_map/unpack/pallas_call | solution.py:176
  228.7 24.8 %collective-permute-done.12.message.scales = bf16[1040,1024]{1,0:T(8,128)(2,1)} collective-permute-done((bf16[1040,1024]{1,0:T(8,128)(2,1)}, bf16[1040,1024]{1,0:T(8,128)(2,1)}, u32[]{:S(2)}, u32[]{:S(2)}) %collective-permute-start.12) | collective-permute-done | bytes 2129952 | tf_op jit(solution)/shard_map/ppermute | solution.py:581
  253.5 2.1 collective-permute-done.14.piece
  256.9 2.0 collective-permute-start.17
  258.9 4.4 put.9
  263.3 4.3 put.10
  267.7 6.1 %unpack.4.refs_2_ = bf16[2,1024,1024]{2,1,0:T(8,128)(2,1)} custom-call(bf16[1040,1024]{1,0:T(8,128)(2,1)} %collective-permute-done.12.message.scales, bf16[1040,1024]{1,0:T(8,128)(2,1)} %collective-permute-done.12.message.scales), custom_call_target="tpu_custom_call" | custom-call | flops 125829120 | bytes 1887436 | tf_op jit(solution)/shard_map/unpack/pallas_call | solution.py:176
  273.7 6.1 %unpack.5.refs_3_ = bf16[2,1024,1024]{2,1,0:T(8,128)(2,1)} custom-call(bf16[1040,1024]{1,0:T(8,128)(2,1)} %collective-permute-done.13.message.scales, bf16[1040,1024]{1,0:T(8,128)(2,1)} %collective-permute-done.13.message.scales), custom_call_target="tpu_custom_call" | custom-call | flops 125829120 | bytes 1887436 | tf_op jit(solution)/shard_map/unpack/pallas_call | solution.py:176
  279.8 21.4 %rotate_part.1.part = f32[1024,1024]{1,0:T(8,128)S(1)} custom-call(s32[2]{0:T(128)S(1)} %pad_add_fusion.at_ref, bf16[2,1024,1024]{2,1,0:T(8,128)(2,1)} %get-tuple-element.62.refs_0_, bf16[2,1024,1024]{2,1,0:T(8,128)(2,1)} %unpack.3.refs_1_, bf16[2,1024,1024]{2,1,0:T(8,128)(2,1)} %unpack.4.refs_2_, bf16[2,1024,1024]{2,1,0:T(8,128)(2,1)} %unpack.5.refs_3_, ...), custom_call_target="tpu_custom_call" | custom-call | flops 5153960960 | bytes 6291456 | tf_op jit(solution)/shard_map/rotate_part/pallas_call | solution.py:244
  301.2 3.7 collective-permute-done.16.above
  304.9 13.5 %rotate.1 = (f32[1024,1024]{1,0:T(8,128)}, f32[1024,1024]{1,0:T(8,128)}, bf16[2,1024,1024]{2,1,0:T(8,128)(2,1)S(1)}) custom-call(s32[2]{0:T(128)S(1)} %pad_add_fusion.at_ref, f32[1024,1024]{1,0:T(8,128)S(1)} %rotate_part.1.part, bf16[1024,1024]{1,0:T(8,128)(2,1)S(1)} %collective-permute-done.16.above, bf16[1024,1024]{1,0:T(8,128)(2,1)} %collective-permute-done.17.below, ...), custom_call_target="tpu_custom_call" | custom-call | flops 17179869184 | bytes 125829120 | tf_op jit(solution)/shard_map/rotate/pallas_call | solution.py:320
  318.5 1.7 broadcast_select_fusion.piece
  321.1 4.4 put.11
  325.5 23.9 %restore.1 = (f32[2,1024,256]{2,1,0:T(8,128)S(1)}, f32[2,1024,256]{2,1,0:T(8,128)S(1)}, f32[2,1024,256]{2,1,0:T(8,128)S(1)}, f32[2,1024,256]{2,1,0:T(8,128)S(1)}...) custom-call(s32[1]{0:T(128)} %bitcast.me_ref, ...), custom_call_target="tpu_custom_call" | custom-call | flops 68719476736 | bytes 134217728 | tf_op jit(solution)/shard_map/restore/pallas_call | solution.py:375
  350.4 3.1 collective-permute-done.24.mate
  355.9 3.6 collective-permute-done.22.mate
  366.9 2.5 collective-permute-done.25.refs_0_
  369.4 7.3 %expand_send.4 = (bf16[2,1040,256]{2,1,0:T(8,128)(2,1)}, bf16[1024,512]{1,0:T(8,128)(2,1)S(1)}) custom-call(s32[1]{0:T(128)} %bitcast.1.place_ref, f32[2,1024,256]{2,1,0:T(8,128)S(1)} %get-tuple-element.93.keep, f32[2,1024,256]{2,1,0:T(8,128)S(1)} %collective-permute-done.24.mate, bf16[1040,256]{1,0:T(8,128)(2,1)S(1)} %collective-permute-done.25.refs_0_, ...), custom_call_target="tpu_custom_call" | custom-call | flops 8589934592 | bytes 16777216 | tf_op jit(solution)/shard_map/expand_send/pallas_call | solution.py:455
  376.7 6.3 %collective-permute-start.26 = (bf16[2,1040,256]{2,1,0:T(8,128)(2,1)}, bf16[2,1040,256]{2,1,0:T(8,128)(2,1)S(1)}, u32[]{:S(2)}, u32[]{:S(2)}) collective-permute-start(bf16[2,1040,256]{2,1,0:T(8,128)(2,1)} %get-tuple-element.95), channel_id=1, source_target_pairs={{0,4},{4,0},{8,12},{12,8},{1,5},{5,1},{9,13},{13,9},{2,6},{6,2},{1... | collective-permute-start | bytes 3194888 | tf_op jit(solution)/shard_map/ppermute | solution.py:672
  383.0 7.3 %expand_send.5 = (bf16[2,1040,256]{2,1,0:T(8,128)(2,1)}, bf16[1024,512]{1,0:T(8,128)(2,1)S(1)}) custom-call(s32[1]{0:T(128)} %bitcast.1.place_ref, f32[2,1024,256]{2,1,0:T(8,128)S(1)} %get-tuple-element.91.keep, f32[2,1024,256]{2,1,0:T(8,128)S(1)} %collective-permute-done.22.mate, bf16[1040,256]{1,0:T(8,128)(2,1)S(1)} %collective-permute-done.23.refs_0_, ...), custom_call_target="tpu_custom_call" | custom-call | flops 8589934592 | bytes 16777216 | tf_op jit(solution)/shard_map/expand_send/pallas_call | solution.py:455
  391.3 4.1 collective-permute-start.27
  395.5 5.4 expand_keep.7.kept
  404.1 7.4 %expand_send.6 = (bf16[2,1040,256]{2,1,0:T(8,128)(2,1)}, bf16[1024,512]{1,0:T(8,128)(2,1)S(1)}) custom-call(s32[1]{0:T(128)} %bitcast.1.place_ref, f32[2,1024,256]{2,1,0:T(8,128)S(1)} %copy-done.6, f32[2,1024,256]{2,1,0:T(8,128)S(1)} %copy-done.10, bf16[1040,256]{1,0:T(8,128)(2,1)} %collective-permute-done.21.refs_0_, bf16[4096,1024]{1,0:T(8,128)(2,1)} %bitcast.22), custom_call_target="tpu_custom_call" | custom-call | flops 8589934592 | bytes 16777216 | tf_op jit(solution)/shard_map/expand_send/pallas_call | solution.py:455
  412.4 5.4 expand_keep.6.kept
  419.4 7.4 %expand_send.7 = (bf16[2,1040,256]{2,1,0:T(8,128)(2,1)}, bf16[1024,512]{1,0:T(8,128)(2,1)S(1)}) custom-call(s32[1]{0:T(128)} %bitcast.1.place_ref, f32[2,1024,256]{2,1,0:T(8,128)S(1)} %copy-done.4, f32[2,1024,256]{2,1,0:T(8,128)S(1)} %copy-done.8, bf16[1040,256]{1,0:T(8,128)(2,1)} %collective-permute-done.19.refs_0_, bf16[4096,1024]{1,0:T(8,128)(2,1)} %bitcast.24), custom_call_target="tpu_custom_call" | custom-call | flops 8589934592 | bytes 16777216 | tf_op jit(solution)/shard_map/expand_send/pallas_call | solution.py:455
  427.7 2.0 collective-permute-start.29
  429.8 5.4 expand_keep.5.kept
  435.1 5.5 %expand_keep.4.kept = f32[2,1024,256]{2,1,0:T(8,128)} custom-call(s32[1]{0:T(128)} %bitcast.1.place_ref, bf16[1024,512]{1,0:T(8,128)(2,1)} %copy-done.15, bf16[4096,1024]{1,0:T(8,128)(2,1)} %bitcast.26), custom_call_target="tpu_custom_call" | custom-call | flops 8589934592 | bytes 16777216 | tf_op jit(solution)/shard_map/expand_keep/pallas_call | solution.py:488
  442.1 3.6 collective-permute-start.33
  445.7 2.5 hop.5
  448.4 27.8 %collective-permute-done.28.refs_0_ = bf16[2,1040,256]{2,1,0:T(8,128)(2,1)} collective-permute-done((bf16[2,1040,256]{2,1,0:T(8,128)(2,1)}, bf16[2,1040,256]{2,1,0:T(8,128)(2,1)}, u32[]{:S(2)}, u32[]{:S(2)}) %collective-permute-start.28) | collective-permute-done | bytes 1064992 | tf_op jit(solution)/shard_map/ppermute | solution.py:672
  476.2 2.5 hop.6
  478.7 3.0 collective-permute-start.31
  481.7 16.5 %collective-permute-done.29.refs_0_ = bf16[2,1040,256]{2,1,0:T(8,128)(2,1)} collective-permute-done((bf16[2,1040,256]{2,1,0:T(8,128)(2,1)}, bf16[2,1040,256]{2,1,0:T(8,128)(2,1)}, u32[]{:S(2)}, u32[]{:S(2)}) %collective-permute-start.29) | collective-permute-done | bytes 1064992 | tf_op jit(solution)/shard_map/ppermute | solution.py:672
  498.3 2.5 hop.7
  500.8 1.7 collective-permute-start.30
  502.4 2.2 finish.4.refs_2_
  504.7 3.3 finish.5.refs_2_
  507.9 27.7 %collective-permute-done.31.refs_1_ = bf16[1,1040,256]{2,1,0:T(8,128)(2,1)S(1)} collective-permute-done((bf16[1,1040,256]{2,1,0:T(8,128)(2,1)S(1)}, bf16[1,1040,256]{2,1,0:T(8,128)(2,1)S(1)}, u32[]{:S(2)}, u32[]{:S(2)}) %collective-permute-start.31) | collective-permute-done | bytes 532512 | tf_op jit(solution)/shard_map/ppermute | solution.py:672
  535.7 3.3 finish.6.refs_2_
  539.0 6.6 %collective-permute-done.30.refs_1_ = bf16[1,1040,256]{2,1,0:T(8,128)(2,1)S(1)} collective-permute-done((bf16[1,1040,256]{2,1,0:T(8,128)(2,1)S(1)}, bf16[1,1040,256]{2,1,0:T(8,128)(2,1)S(1)}, u32[]{:S(2)}, u32[]{:S(2)}) %collective-permute-start.30) | collective-permute-done | bytes 532512 | tf_op jit(solution)/shard_map/ppermute | solution.py:672
  545.5 3.3 finish.7
  (86 shorter events, 35.3 us)
Async XLA Ops:
  0.6 49.0 %collective-permute-start = (bf16[1024,1024]{1,0:T(8,128)(2,1)}, bf16[1024,1024]{1,0:T(8,128)(2,1)}, u32[]{:S(2)}, u32[]{:S(2)}) collective-permute-start(bf16[1024,1024]{1,0:T(8,128)(2,1)} %param.8), channel_id=1, source_target_pairs={{0,2},{1,3},{2,0},{3,1},{4,6},{5,7},{6,4},{7,5},{8,10},{9,11},{10,... | collective-permute-start | bytes 6291464 | tf_op jit(solution)/shard_map/ppermute | solution.py:581
  3.6 48.4 %collective-permute-start.3 = (bf16[1024,1024]{1,0:T(8,128)(2,1)}, bf16[1024,1024]{1,0:T(8,128)(2,1)S(1)}, u32[]{:S(2)}, u32[]{:S(2)}) collective-permute-start(bf16[1024,1024]{1,0:T(8,128)(2,1)} %refs_2_.1), channel_id=1, source_target_pairs={{0,4},{4,8},{8,12},{1,5},{5,9},{9,13},{2,6},{6,10},{10,14},{3,7},{... | collective-permute-start | bytes 6291464 | tf_op jit(solution)/shard_map/ppermute | solution.py:598
  7.2 49.0 %collective-permute-start.5 = (bf16[1024,1024]{1,0:T(8,128)(2,1)}, bf16[1024,1024]{1,0:T(8,128)(2,1)}, u32[]{:S(2)}, u32[]{:S(2)}) collective-permute-start(bf16[1024,1024]{1,0:T(8,128)(2,1)} %refs_2_.1), channel_id=1, source_target_pairs={{4,0},{8,4},{12,8},{5,1},{9,5},{13,9},{6,2},{10,6},{14,10},{7,3},{... | collective-permute-start | bytes 6291464 | tf_op jit(solution)/shard_map/ppermute | solution.py:601
  8.5 52.8 %collective-permute-start.1 = (bf16[1024,1024]{1,0:T(8,128)(2,1)}, bf16[1024,1024]{1,0:T(8,128)(2,1)}, u32[]{:S(2)}, u32[]{:S(2)}) collective-permute-start(bf16[1024,1024]{1,0:T(8,128)(2,1)} %param.8), channel_id=1, source_target_pairs={{0,1},{1,0},{2,3},{3,2},{4,5},{5,4},{6,7},{7,6},{8,9},{9,8},{10,11... | collective-permute-start | bytes 6291464 | tf_op jit(solution)/shard_map/ppermute | solution.py:581
  49.6 13.6 %collective-permute-start.2 = (bf16[1024,1024]{1,0:T(8,128)(2,1)}, bf16[1024,1024]{1,0:T(8,128)(2,1)}, u32[]{:S(2)}, u32[]{:S(2)}) collective-permute-start(bf16[1024,1024]{1,0:T(8,128)(2,1)} %collective-permute-done), channel_id=1, source_target_pairs={{0,1},{1,0},{2,3},{3,2},{4,5},{5,4},{6,7},{7,6},{8,9},{9,8},{10,11... | collective-permute-start | bytes 6291464 | tf_op jit(solution)/shard_map/ppermute | solution.py:581
  52.0 13.1 %collective-permute-start.4 = (bf16[1024,1024]{1,0:T(8,128)(2,1)S(1)}, bf16[1024,1024]{1,0:T(8,128)(2,1)}, u32[]{:S(2)}, u32[]{:S(2)}) collective-permute-start(bf16[1024,1024]{1,0:T(8,128)(2,1)S(1)} %collective-permute-done.3.refs_1_), channel_id=1, source_target_pairs={{4,8},{8,12},{5,9},{9,13},{6,10},{10,14},{7,11},{11,15},{20,24},{2... | collective-permute-start | bytes 6291464 | tf_op jit(solution)/shard_map/ppermute | solution.py:598
  56.3 49.4 %collective-permute-start.6 = (bf16[1024,1024]{1,0:T(8,128)(2,1)}, bf16[1024,1024]{1,0:T(8,128)(2,1)}, u32[]{:S(2)}, u32[]{:S(2)}) collective-permute-start(bf16[1024,1024]{1,0:T(8,128)(2,1)} %collective-permute-done.5.refs_3_), channel_id=1, source_target_pairs={{4,0},{8,4},{5,1},{9,5},{6,2},{10,6},{7,3},{11,7},{20,16},{24,20},... | collective-permute-start | bytes 6291464 | tf_op jit(solution)/shard_map/ppermute | solution.py:601
  57.6 1.6 copy-start.19
  65.1 3.3 copy-start.16
  105.7 18.0 %collective-permute-start.7 = (bf16[1024,1024]{1,0:T(8,128)(2,1)}, bf16[1024,1024]{1,0:T(8,128)(2,1)}, u32[]{:S(2)}, u32[]{:S(2)}) collective-permute-start(bf16[1024,1024]{1,0:T(8,128)(2,1)} %collective-permute-done.4.refs_0_), channel_id=1, source_target_pairs={{8,12},{9,13},{10,14},{11,15},{24,28},{25,29},{26,30},{27,31}} | collective-permute-start | bytes 6291464 | tf_op jit(solution)/shard_map/ppermute | solution.py:598
  107.7 47.6 %collective-permute-start.8 = (bf16[1024,1024]{1,0:T(8,128)(2,1)}, bf16[1024,1024]{1,0:T(8,128)(2,1)}, u32[]{:S(2)}, u32[]{:S(2)}) collective-permute-start(bf16[1024,1024]{1,0:T(8,128)(2,1)} %collective-permute-done.6.refs_4_), channel_id=1, source_target_pairs={{4,0},{5,1},{6,2},{7,3},{20,16},{21,17},{22,18},{23,19}} | collective-permute-start | bytes 6291464 | tf_op jit(solution)/shard_map/ppermute | solution.py:601
  155.2 46.6 %collective-permute-start.10 = (bf16[1024,1024]{1,0:T(8,128)(2,1)}, bf16[1024,1024]{1,0:T(8,128)(2,1)}, u32[]{:S(2)}, u32[]{:S(2)}) collective-permute-start(bf16[1024,1024]{1,0:T(8,128)(2,1)} %piece), channel_id=1, source_target_pairs={{4,0},{8,4},{12,8},{5,1},{9,5},{13,9},{6,2},{10,6},{14,10},{7,3},{... | collective-permute-start | bytes 6291464 | tf_op jit(solution)/shard_map/ppermute | solution.py:601
  156.5 46.5 %collective-permute-start.9 = (bf16[1024,1024]{1,0:T(8,128)(2,1)}, bf16[1024,1024]{1,0:T(8,128)(2,1)S(1)}, u32[]{:S(2)}, u32[]{:S(2)}) collective-permute-start(bf16[1024,1024]{1,0:T(8,128)(2,1)} %piece), channel_id=1, source_target_pairs={{0,4},{4,8},{8,12},{1,5},{5,9},{9,13},{2,6},{6,10},{10,14},{3,7},{... | collective-permute-start | bytes 6291464 | tf_op jit(solution)/shard_map/ppermute | solution.py:598
  203.1 1.4 copy-start.18
  204.4 16.9 %collective-permute-start.11 = (bf16[1040,1024]{1,0:T(8,128)(2,1)}, bf16[1040,1024]{1,0:T(8,128)(2,1)S(1)}, u32[]{:S(2)}, u32[]{:S(2)}) collective-permute-start(bf16[1040,1024]{1,0:T(8,128)(2,1)} %get-tuple-element.65), channel_id=1, source_target_pairs={{0,1},{1,0},{2,3},{3,2},{4,5},{5,4},{6,7},{7,6},{8,9},{9,8},{10,11... | collective-permute-start | bytes 6389768 | tf_op jit(solution)/shard_map/ppermute | solution.py:581
  204.4 49.1 %collective-permute-start.12 = (bf16[1040,1024]{1,0:T(8,128)(2,1)}, bf16[1040,1024]{1,0:T(8,128)(2,1)}, u32[]{:S(2)}, u32[]{:S(2)}) collective-permute-start(bf16[1040,1024]{1,0:T(8,128)(2,1)} %get-tuple-element.65), channel_id=1, source_target_pairs={{0,2},{1,3},{2,0},{3,1},{4,6},{5,7},{6,4},{7,5},{8,10},{9,11},{10,... | collective-permute-start | bytes 6389768 | tf_op jit(solution)/shard_map/ppermute | solution.py:581
  205.0 50.6 %collective-permute-start.14 = (bf16[1024,1024]{1,0:T(8,128)(2,1)}, bf16[1024,1024]{1,0:T(8,128)(2,1)}, u32[]{:S(2)}, u32[]{:S(2)}) collective-permute-start(bf16[1024,1024]{1,0:T(8,128)(2,1)} %collective-permute-done.10.piece), channel_id=1, source_target_pairs={{4,0},{8,4},{5,1},{9,5},{6,2},{10,6},{7,3},{11,7},{20,16},{24,20},... | collective-permute-start | bytes 6291464 | tf_op jit(solution)/shard_map/ppermute | solution.py:601
  206.3 50.6 %collective-permute-start.15 = (bf16[1024,1024]{1,0:T(8,128)(2,1)}, bf16[1024,1024]{1,0:T(8,128)(2,1)}, u32[]{:S(2)}, u32[]{:S(2)}) collective-permute-start(bf16[1024,1024]{1,0:T(8,128)(2,1)} %copy-done.18), channel_id=1, source_target_pairs={{4,8},{8,12},{5,9},{9,13},{6,10},{10,14},{7,11},{11,15},{20,24},{2... | collective-permute-start | bytes 6291464 | tf_op jit(solution)/shard_map/ppermute | solution.py:598
  221.3 1.3 copy-start.17
  253.5 20.2 %collective-permute-start.13 = (bf16[1040,1024]{1,0:T(8,128)(2,1)}, bf16[1040,1024]{1,0:T(8,128)(2,1)}, u32[]{:S(2)}, u32[]{:S(2)}) collective-permute-start(bf16[1040,1024]{1,0:T(8,128)(2,1)} %collective-permute-done.12.message.scales), channel_id=1, source_target_pairs={{0,1},{1,0},{2,3},{3,2},{4,5},{5,4},{6,7},{7,6},{8,9},{9,8},{10,11... | collective-permute-start | bytes 6389768 | tf_op jit(solution)/shard_map/ppermute | solution.py:581
  255.6 49.4 %collective-permute-start.16 = (bf16[1024,1024]{1,0:T(8,128)(2,1)}, bf16[1024,1024]{1,0:T(8,128)(2,1)S(1)}, u32[]{:S(2)}, u32[]{:S(2)}) collective-permute-start(bf16[1024,1024]{1,0:T(8,128)(2,1)} %collective-permute-done.14.piece), channel_id=1, source_target_pairs={{4,0},{5,1},{6,2},{7,3},{20,16},{21,17},{22,18},{23,19}} | collective-permute-start | bytes 6291464 | tf_op jit(solution)/shard_map/ppermute | solution.py:601
  256.9 48.1 %collective-permute-start.17 = (bf16[1024,1024]{1,0:T(8,128)(2,1)}, bf16[1024,1024]{1,0:T(8,128)(2,1)}, u32[]{:S(2)}, u32[]{:S(2)}) collective-permute-start(bf16[1024,1024]{1,0:T(8,128)(2,1)} %collective-permute-done.15.piece), channel_id=1, source_target_pairs={{8,12},{9,13},{10,14},{11,15},{24,28},{25,29},{26,30},{27,31}} | collective-permute-start | bytes 6291464 | tf_op jit(solution)/shard_map/ppermute | solution.py:598
  318.5 2.6 copy-start.11
  349.4 4.2 collective-permute-start.24
  349.4 10.2 %collective-permute-start.22 = (f32[2,1024,256]{2,1,0:T(8,128)S(1)}, f32[2,1024,256]{2,1,0:T(8,128)S(1)}, u32[]{:S(2)}, u32[]{:S(2)}) collective-permute-start(f32[2,1024,256]{2,1,0:T(8,128)S(1)} %get-tuple-element.92), channel_id=1, source_target_pairs={{0,1},{1,0},{2,3},{3,2},{4,5},{5,4},{6,7},{7,6},{8,9},{9,8},{10,11... | collective-permute-start | bytes 6291464 | tf_op jit(solution)/shard_map/ppermute | solution.py:581
  349.9 12.0 %collective-permute-start.20 = (f32[2,1024,256]{2,1,0:T(8,128)}, f32[2,1024,256]{2,1,0:T(8,128)S(1)}, u32[]{:S(2)}, u32[]{:S(2)}) collective-permute-start(f32[2,1024,256]{2,1,0:T(8,128)} %get-tuple-element.90), channel_id=1, source_target_pairs={{0,1},{1,0},{2,3},{3,2},{4,5},{5,4},{6,7},{7,6},{8,9},{9,8},{10,11... | collective-permute-start | bytes 6291464 | tf_op jit(solution)/shard_map/ppermute | solution.py:581
  350.0 14.3 %collective-permute-start.18 = (f32[2,1024,256]{2,1,0:T(8,128)}, f32[2,1024,256]{2,1,0:T(8,128)S(1)}, u32[]{:S(2)}, u32[]{:S(2)}) collective-permute-start(f32[2,1024,256]{2,1,0:T(8,128)} %get-tuple-element.88), channel_id=1, source_target_pairs={{0,1},{1,0},{2,3},{3,2},{4,5},{5,4},{6,7},{7,6},{8,9},{9,8},{10,11... | collective-permute-start | bytes 6291464 | tf_op jit(solution)/shard_map/ppermute | solution.py:581
  354.4 15.0 %collective-permute-start.25 = (bf16[1040,256]{1,0:T(8,128)(2,1)S(1)}, bf16[1040,256]{1,0:T(8,128)(2,1)S(1)}, u32[]{:S(2)}, u32[]{:S(2)}) collective-permute-start(bf16[1040,256]{1,0:T(8,128)(2,1)S(1)} %send.7), channel_id=1, source_target_pairs={{0,2},{1,3},{2,0},{3,1},{4,6},{5,7},{6,4},{7,5},{8,10},{9,11},{10,... | collective-permute-start | bytes 1597448 | tf_op jit(solution)/shard_map/ppermute | solution.py:581
  359.6 2.4 copy-start.5
  360.4 22.6 %collective-permute-start.23 = (bf16[1040,256]{1,0:T(8,128)(2,1)S(1)}, bf16[1040,256]{1,0:T(8,128)(2,1)S(1)}, u32[]{:S(2)}, u32[]{:S(2)}) collective-permute-start(bf16[1040,256]{1,0:T(8,128)(2,1)S(1)} %send.6), channel_id=1, source_target_pairs={{0,2},{1,3},{2,0},{3,1},{4,6},{5,7},{6,4},{7,5},{8,10},{9,11},{10,... | collective-permute-start | bytes 1597448 | tf_op jit(solution)/shard_map/ppermute | solution.py:581
  362.0 1.6 copy-start.9
  362.0 2.5 copy-start.4
  363.6 37.3 %collective-permute-start.21 = (bf16[1040,256]{1,0:T(8,128)(2,1)}, bf16[1040,256]{1,0:T(8,128)(2,1)}, u32[]{:S(2)}, u32[]{:S(2)}) collective-permute-start(bf16[1040,256]{1,0:T(8,128)(2,1)} %send.5), channel_id=1, source_target_pairs={{0,2},{1,3},{2,0},{3,1},{4,6},{5,7},{6,4},{7,5},{8,10},{9,11},{10,... | collective-permute-start | bytes 1597448 | tf_op jit(solution)/shard_map/ppermute | solution.py:581
  364.3 1.3 copy-start.7
  365.6 52.2 %collective-permute-start.19 = (bf16[1040,256]{1,0:T(8,128)(2,1)S(1)}, bf16[1040,256]{1,0:T(8,128)(2,1)}, u32[]{:S(2)}, u32[]{:S(2)}) collective-permute-start(bf16[1040,256]{1,0:T(8,128)(2,1)S(1)} %send.4), channel_id=1, source_target_pairs={{0,2},{1,3},{2,0},{3,1},{4,6},{5,7},{6,4},{7,5},{8,10},{9,11},{10,... | collective-permute-start | bytes 1597448 | tf_op jit(solution)/shard_map/ppermute | solution.py:581
  376.7 13.6 %copy-start.14 = (bf16[1024,512]{1,0:T(8,128)(2,1)}, bf16[1024,512]{1,0:T(8,128)(2,1)S(1)}, u32[]{:S(2)}) copy-start(bf16[1024,512]{1,0:T(8,128)(2,1)S(1)} %get-tuple-element.104.both) | copy-start | bytes 3145732
  376.7 64.0 %collective-permute-start.26 = (bf16[2,1040,256]{2,1,0:T(8,128)(2,1)}, bf16[2,1040,256]{2,1,0:T(8,128)(2,1)S(1)}, u32[]{:S(2)}, u32[]{:S(2)}) collective-permute-start(bf16[2,1040,256]{2,1,0:T(8,128)(2,1)} %get-tuple-element.95), channel_id=1, source_target_pairs={{0,4},{4,0},{8,12},{12,8},{1,5},{5,1},{9,13},{13,9},{2,6},{6,2},{1... | collective-permute-start | bytes 3194888 | tf_op jit(solution)/shard_map/ppermute | solution.py:672
  390.3 1.0 copy-start.12
  391.3 54.3 %collective-permute-start.27 = (bf16[2,1040,256]{2,1,0:T(8,128)(2,1)}, bf16[2,1040,256]{2,1,0:T(8,128)(2,1)}, u32[]{:S(2)}, u32[]{:S(2)}) collective-permute-start(bf16[2,1040,256]{2,1,0:T(8,128)(2,1)} %get-tuple-element.97), channel_id=1, source_target_pairs={{0,4},{4,0},{8,12},{12,8},{1,5},{5,1},{9,13},{13,9},{2,6},{6,2},{1... | collective-permute-start | bytes 3194888 | tf_op jit(solution)/shard_map/ppermute | solution.py:672
  400.9 1.6 copy-start.6
  402.5 1.6 copy-start.10
  411.4 1.0 copy-start.13
  412.4 63.8 %collective-permute-start.28 = (bf16[2,1040,256]{2,1,0:T(8,128)(2,1)}, bf16[2,1040,256]{2,1,0:T(8,128)(2,1)}, u32[]{:S(2)}, u32[]{:S(2)}) collective-permute-start(bf16[2,1040,256]{2,1,0:T(8,128)(2,1)} %get-tuple-element.99), channel_id=1, source_target_pairs={{0,4},{4,0},{8,12},{12,8},{1,5},{5,1},{9,13},{13,9},{2,6},{6,2},{1... | collective-permute-start | bytes 3194888 | tf_op jit(solution)/shard_map/ppermute | solution.py:672
  417.8 1.6 copy-start.8
  426.8 1.0 copy-start.15
  427.7 70.5 %collective-permute-start.29 = (bf16[2,1040,256]{2,1,0:T(8,128)(2,1)}, bf16[2,1040,256]{2,1,0:T(8,128)(2,1)}, u32[]{:S(2)}, u32[]{:S(2)}) collective-permute-start(bf16[2,1040,256]{2,1,0:T(8,128)(2,1)} %get-tuple-element.108), channel_id=1, source_target_pairs={{0,4},{4,0},{8,12},{12,8},{1,5},{5,1},{9,13},{13,9},{2,6},{6,2},{1... | collective-permute-start | bytes 3194888 | tf_op jit(solution)/shard_map/ppermute | solution.py:672
  435.1 5.5 %copy-start = (f32[2,1024,256]{2,1,0:T(8,128)S(1)}, f32[2,1024,256]{2,1,0:T(8,128)}, u32[]{:S(2)}) copy-start(f32[2,1024,256]{2,1,0:T(8,128)} %expand_keep.7.kept) | copy-start | bytes 6291460
  440.6 5.0 copy-start.1
  442.1 34.1 %copy-start.3 = (f32[2,1024,256]{2,1,0:T(8,128)S(1)}, f32[2,1024,256]{2,1,0:T(8,128)}, u32[]{:S(2)}) copy-start(f32[2,1024,256]{2,1,0:T(8,128)} %expand_keep.5.kept) | copy-start | bytes 6291460
  442.1 60.3 %collective-permute-start.33 = (bf16[1,1040,256]{2,1,0:T(8,128)(2,1)S(1)}, bf16[1,1040,256]{2,1,0:T(8,128)(2,1)S(1)}, u32[]{:S(2)}, u32[]{:S(2)}) collective-permute-start(bf16[1,1040,256]{2,1,0:T(8,128)(2,1)S(1)} %hop.4), channel_id=1, source_target_pairs={{0,8},{4,12},{8,0},{12,4},{1,9},{5,13},{9,1},{13,5},{2,10},{6,14},... | collective-permute-start | bytes 1597448 | tf_op jit(solution)/shard_map/ppermute | solution.py:672
  448.2 50.1 %copy-start.2 = (f32[2,1024,256]{2,1,0:T(8,128)S(1)}, f32[2,1024,256]{2,1,0:T(8,128)}, u32[]{:S(2)}) copy-start(f32[2,1024,256]{2,1,0:T(8,128)} %expand_keep.4.kept) | copy-start | bytes 6291460
  448.2 56.5 %collective-permute-start.32 = (bf16[1,1040,256]{2,1,0:T(8,128)(2,1)S(1)}, bf16[1,1040,256]{2,1,0:T(8,128)(2,1)S(1)}, u32[]{:S(2)}, u32[]{:S(2)}) collective-permute-start(bf16[1,1040,256]{2,1,0:T(8,128)(2,1)S(1)} %hop.5), channel_id=1, source_target_pairs={{0,8},{4,12},{8,0},{12,4},{1,9},{5,13},{9,1},{13,5},{2,10},{6,14},... | collective-permute-start | bytes 1597448 | tf_op jit(solution)/shard_map/ppermute | solution.py:672
  478.7 57.0 %collective-permute-start.31 = (bf16[1,1040,256]{2,1,0:T(8,128)(2,1)S(1)}, bf16[1,1040,256]{2,1,0:T(8,128)(2,1)S(1)}, u32[]{:S(2)}, u32[]{:S(2)}) collective-permute-start(bf16[1,1040,256]{2,1,0:T(8,128)(2,1)S(1)} %hop.6), channel_id=1, source_target_pairs={{0,8},{4,12},{8,0},{12,4},{1,9},{5,13},{9,1},{13,5},{2,10},{6,14},... | collective-permute-start | bytes 1597448 | tf_op jit(solution)/shard_map/ppermute | solution.py:672
  500.8 44.8 %collective-permute-start.30 = (bf16[1,1040,256]{2,1,0:T(8,128)(2,1)S(1)}, bf16[1,1040,256]{2,1,0:T(8,128)(2,1)S(1)}, u32[]{:S(2)}, u32[]{:S(2)}) collective-permute-start(bf16[1,1040,256]{2,1,0:T(8,128)(2,1)S(1)} %hop.7), channel_id=1, source_target_pairs={{0,8},{4,12},{8,0},{12,4},{1,9},{5,13},{9,1},{13,5},{2,10},{6,14},... | collective-permute-start | bytes 1597448 | tf_op jit(solution)/shard_map/ppermute | solution.py:672

commit v13 on v11

--- a/solution.py
+++ b/solution.py
@@ -336,22 +336,26 @@
             jax.ShapeDtypeStruct((rows, width), F32),
             jax.ShapeDtypeStruct((2, rows, width), BF16),
         ],
-        compiler_params=params(60),
+        compiler_params=params(40),
         cost_estimate=cost(4 * rows * width * depth, 30 * rows * width),
         name="rotate",
     )(at, part, above, below, first, second, *pieces)
 
 
 def restore_kernel(me_ref, normed, *refs, cols):
-    flipped, (keep, mate) = refs[:cols], refs[cols:]
+    flipped, outs = refs[:cols], refs[cols:]
     tile = normed.shape[1]
+    piece = outs[0].shape[2]
     both = normed[...].reshape(2 * tile, normed.shape[2])
     for distance in range(cols):
         term = dot(both, flipped[distance][0], ((1,), (0,)))
-        (mate if distance % 2 else keep)[distance // 2] = term[:tile] + term[tile:]
-
-
-def restore(me, normed, flipped, cols, chunk, piece):
+        term = term[:tile] + term[tile:]
+        for at in range(len(outs) // 2):
+            out = outs[2 * at + distance % 2]
+            out[distance // 2] = term[:, at * piece : (at + 1) * piece]
+
+
+def restore(me, normed, flipped, cols, piece, batch, count):
     _, depth, inner = normed.shape
     wide = flipped.shape[2]
     tile = min(256, depth)
@@ -359,25 +363,28 @@
 
     def columns(distance):
         def at(i, s):
-            start = (s[0] ^ distance) * inner + chunk * piece
-            return start // wide, 0, lax.rem(start, wide) // piece
-
-        return pl.BlockSpec((1, inner, piece), at)
-
-    return pl.pallas_call(
+            start = (s[0] ^ distance) * inner + batch * count * piece
+            return start // wide, 0, lax.rem(start, wide) // (count * piece)
+
+        return pl.BlockSpec((1, inner, count * piece), at, pipeline_mode=pl.Buffered(1))
+
+    outs = pl.pallas_call(
         functools.partial(restore_kernel, cols=cols),
         grid_spec=pltpu.PrefetchScalarGridSpec(
             num_scalar_prefetch=1,
             grid=(depth // tile,),
             in_specs=[pl.BlockSpec((2, tile, inner), lambda i, s: (0, i, 0))]
             + [columns(distance) for distance in range(cols)],
-            out_specs=[out, out],
-        ),
-        out_shape=[jax.ShapeDtypeStruct((cols // 2, depth, piece), F32)] * 2,
-        compiler_params=params(60),
-        cost_estimate=cost(4 * depth * inner * piece * cols, 8 * depth * piece * cols, 4),
+            out_specs=[out] * (2 * count),
+        ),
+        out_shape=[jax.ShapeDtypeStruct((cols // 2, depth, piece), F32)] * (2 * count),
+        compiler_params=params(44),
+        cost_estimate=cost(
+            4 * depth * inner * count * piece * cols, 8 * depth * count * piece * cols
+        ),
         name="restore",
     )(me, normed, *([flipped] * cols))
+    return [(outs[2 * at], outs[2 * at + 1]) for at in range(count)]
 
 
 def summed(keep, mate, codes):
@@ -654,7 +661,7 @@
             at, part, pieces, above, below, first_moment, second_moment, lines
         )
         if aligned:
-            last = jnp.where(place == 0, above, below)
+            last = jnp.where(place == 0, after(above, normed), below)
             there = jnp.where((place == 0) | (place == far), far - place, lines)
             held = put(jnp.reshape(there, (1,)), last, held, lines + 1)
         flipped = held[1]
@@ -666,6 +673,8 @@
             kept, arrived = products[chunk]
             if chunk - 1 in second:
                 kept = after(kept, second[chunk - 1])
+            if chunk + 1 < len(outgoing):
+                kept = after(kept, outgoing[chunk + 1])
             step = 1
             while 2**step < lines:
                 message = hop(kept, arrived, step)
@@ -677,12 +686,6 @@
 
         products, halves, sent, outgoing, second = [], [], [], [], {}
 
-        def sums(chunk, ready):
-            keep, mate = restore(me_now, ready, flipped, cols, chunk, piece)
-            mate = swap(mate, 1)
-            halves.append((keep, mate))
-            sent.append([send(keep, mate, distance, []) for distance in range(2, cols, 2)])
-
         def multiply(chunk, *before):
             codes = [swap(code, 2 * index + 2) for index, code in enumerate(sent[chunk])]
             if codes and before:
@@ -691,17 +694,16 @@
             outgoing.append(message)
             products.append((expand_keep(spot, both, left, depth), [cross(message, 1)]))
 
-        sums(0, normed)
-        sums(1, normed)
-        multiply(0, *sent[1])
-        multiply(1)
-        firsts = [product[1][0] for product in products]
-        later_hops(0)
-        later_hops(1)
-        for chunk in range(2, CHUNKS):
-            sums(chunk, after(normed, second.get(chunk % 2, firsts[chunk % 2]), outgoing[1]))
-        for chunk in range(2, CHUNKS):
-            multiply(chunk)
+        for batch in range(2):
+            ready = after(normed, *sent[0]) if batch else normed
+            for keep, mate in restore(me_now, ready, flipped, cols, piece, batch, CHUNKS // 2):
+                mate = swap(mate, 1)
+                halves.append((keep, mate))
+                sent.append([send(keep, mate, distance, []) for distance in range(2, cols, 2)])
+        for chunk in range(CHUNKS):
+            if chunk >= 2:
+                later_hops(chunk - 2)
+            multiply(chunk, *([second[chunk - 2]] if chunk - 2 in second else outgoing[-1:]))
         update = None
         for chunk in range(CHUNKS):
             if chunk >= CHUNKS - 2:

time: 581 us -> 537 us (0.924)
  waiting for transfers between devices: 278 us -> 234 us
  starting transfers between devices: 47.2 us -> 57.2 us
  Pallas kernels: 229 us -> 220 us
    ppermute x8, waiting for transfers between devices: 86.3 us -> 60.7 us  [cross(): return lax.ppermute(value, 'row', [(i, i ^ distance) for i in range(lines)])]
    ppermute x6, waiting for transfers between devices: 25.9 us -> 3.63 us  [up(): return lax.ppermute(value, 'row', [(i, i + 1) for i in senders])]
    ppermute x6, waiting for transfers between devices: 78.4 us -> 100 us  [down(): return lax.ppermute(value, 'row', [(i, i - 1) for i in senders])]
    ppermute x14, waiting for transfers between devices: 87.3 us -> 70.1 us  [swap(): return lax.ppermute(value, 'col', [(i, i ^ distance) for i in range(cols)])]
    pallas_call x4 -> x2, Pallas kernels: 33.6 us -> 26 us  [restore(): pl.pallas_call(functools.partial(restore_kernel, cols=cols), grid_spec=pl...]
    ppermute x8, starting transfers between devices: 16.7 us -> 23.8 us  [cross(): return lax.ppermute(value, 'row', [(i, i ^ distance) for i in range(lines)])]
    unnamed x40 -> x46, local copies, waits for them, and re-layouts: 14.5 us -> 14.7 us
  transfers between devices with their start and end apart: 34 -> 34, of which waited for: 19 -> 17; matrix products, arithmetic and copies ran while one was open for 1% -> 1% of each run, Pallas kernels for 31% -> 34%
where the time goes in v13:
time: 537 us; the launch traced here: 536 us
  waiting for transfers between devices  234 us (44%)
  Pallas kernels  220 us (41%)
  starting transfers between devices  57.2 us (11%)
  local copies, waits for them, and re-layouts  21.6 us (4%)
    ppermute x6, waiting for transfers between devices, down(): return lax.ppermute(value, 'row', [(i, i - 1) for i in senders])  100 us
    ppermute x14, waiting for transfers between devices, swap(): return lax.ppermute(value, 'col', [(i, i ^ distance) for i in range(cols)])  70.1 us
    ppermute x8, waiting for transfers between devices, cross(): return lax.ppermute(value, 'row', [(i, i ^ distance) for i in range(lines)])  60.7 us
    pallas_call x4, Pallas kernels, expand_send(): pl.pallas_call(functools.partial(expand_send_kernel, tile=min(64, depth))...  30.7 us
    pallas_call x6, Pallas kernels, put(): pl.pallas_call(put_kernel, grid_spec=pltpu.PrefetchScalarGridSpec(num_sca...  26.1 us
    pallas_call x2, Pallas kernels, restore(): pl.pallas_call(functools.partial(restore_kernel, cols=cols), grid_spec=pl...  26 us
    pallas_call x2, Pallas kernels, halfway(): pl.pallas_call(functools.partial(halfway_kernel, offsets=offsets, lines=l...  24.3 us
    ppermute x8, starting transfers between devices, cross(): return lax.ppermute(value, 'row', [(i, i ^ distance) for i in range(lines)])  23.8 us
  transfers between devices with their start and end apart: 34, of which 17 were waited for; matrix products, arithmetic and copies ran while one was open for 1% of the time, Pallas kernels for 34%

profile of v13, /device:TPU:0, one launch (start us, length us, event | category | flops | bytes accessed | tf_op | source)
XLA Modules:
  0.0 535.9 jit_solution(14251923560854002730)
XLA Ops:
  0.6 3.0 collective-permute-start
  3.6 3.6 collective-permute-start.3
  8.6 41.0 %collective-permute-done = bf16[1024,1024]{1,0:T(8,128)(2,1)} collective-permute-done((bf16[1024,1024]{1,0:T(8,128)(2,1)}, bf16[1024,1024]{1,0:T(8,128)(2,1)}, u32[]{:S(2)}, u32[]{:S(2)}) %collective-permute-start) | collective-permute-done | bytes 2097184 | tf_op jit(solution)/shard_map/ppermute | solution.py:579
  49.6 2.4 collective-permute-done.3.refs_1_
  52.0 2.0 collective-permute-start.4
  54.0 2.3 collective-permute-done.5.refs_3_
  59.5 1.9 bitcast_dynamic-update-slice_fusion.2
  63.2 1.9 bitcast_dynamic-update-slice_fusion
  65.1 3.3 copy-done.19
  68.4 37.3 %collective-permute-done.6.refs_4_ = bf16[1024,1024]{1,0:T(8,128)(2,1)} collective-permute-done((bf16[1024,1024]{1,0:T(8,128)(2,1)}, bf16[1024,1024]{1,0:T(8,128)(2,1)}, u32[]{:S(2)}, u32[]{:S(2)}) %collective-permute-start.6) | collective-permute-done | bytes 2097184 | tf_op jit(solution)/shard_map/ppermute | solution.py:599
  105.7 2.0 collective-permute-start.7
  108.9 14.7 %halfway.2.refs_2_ = f32[1024,1024]{1,0:T(8,128)} custom-call(s32[1]{0:T(128)} %bitcast.1.place_ref, bf16[4096,1024]{1,0:T(8,128)(2,1)} %bitcast.17, bf16[1024,1024]{1,0:T(8,128)(2,1)} %collective-permute-done.4.refs_0_, bf16[1024,1024]{1,0:T(8,128)(2,1)S(1)} %collective-permute-done.3.refs_1_, bf16[1024,1024]{1,0:T(8,128)(2,1)} %refs_2_.1, ...), custom_call_target="tpu_custom_call" | custom-call | flops 2576980480 | bytes 2516582 | tf_op jit(solution)/shard_map/halfway/pallas_call | solution.py:114
  123.6 31.6 %collective-permute-done.8.refs_1_ = bf16[1024,1024]{1,0:T(8,128)(2,1)} collective-permute-done((bf16[1024,1024]{1,0:T(8,128)(2,1)}, bf16[1024,1024]{1,0:T(8,128)(2,1)}, u32[]{:S(2)}, u32[]{:S(2)}) %collective-permute-start.8) | collective-permute-done | bytes 2097184 | tf_op jit(solution)/shard_map/ppermute | solution.py:599
  156.5 4.7 collective-permute-start.9
  161.2 9.6 %halfway.3.value = f32[1024,1024]{1,0:T(8,128)} custom-call(s32[1]{0:T(128)} %bitcast.1.place_ref, bf16[4096,1024]{1,0:T(8,128)(2,1)} %bitcast.18, bf16[1024,1024]{1,0:T(8,128)(2,1)} %collective-permute-done.7.refs_0_, bf16[1024,1024]{1,0:T(8,128)(2,1)} %collective-permute-done.8.refs_1_, f32[1024,1024]{1,0:T(8,128)} %halfway.2.refs_2_), custom_call_target="tpu_custom_call" | custom-call | flops 2576980480 | bytes 2516582 | tf_op jit(solution)/shard_map/halfway/pallas_call | solution.py:114
  170.8 7.9 %pack.1 = (bf16[2,1024,1024]{2,1,0:T(8,128)(2,1)}, bf16[1040,1024]{1,0:T(8,128)(2,1)}) custom-call(f32[1024,1024]{1,0:T(8,128)} %halfway.3.value), custom_call_target="tpu_custom_call" | custom-call | flops 125829120 | bytes 3145728 | tf_op jit(solution)/shard_map/pack/pallas_call | solution.py:147
  178.7 23.1 %collective-permute-done.10.piece = bf16[1024,1024]{1,0:T(8,128)(2,1)} collective-permute-done((bf16[1024,1024]{1,0:T(8,128)(2,1)}, bf16[1024,1024]{1,0:T(8,128)(2,1)}, u32[]{:S(2)}, u32[]{:S(2)}) %collective-permute-start.10) | collective-permute-done | bytes 2097184 | tf_op jit(solution)/shard_map/ppermute | solution.py:599
  206.2 2.0 collective-permute-start.15
  208.2 4.4 put.6
  212.6 4.4 put.7
  216.9 4.3 put.8
  222.6 6.1 %unpack.3.refs_1_ = bf16[2,1024,1024]{2,1,0:T(8,128)(2,1)} custom-call(bf16[1040,1024]{1,0:T(8,128)(2,1)} %copy-done.20, bf16[1040,1024]{1,0:T(8,128)(2,1)} %copy-done.20), custom_call_target="tpu_custom_call" | custom-call | flops 125829120 | bytes 1887436 | tf_op jit(solution)/shard_map/unpack/pallas_call | solution.py:176
  228.7 24.8 %collective-permute-done.12.message.scales = bf16[1040,1024]{1,0:T(8,128)(2,1)} collective-permute-done((bf16[1040,1024]{1,0:T(8,128)(2,1)}, bf16[1040,1024]{1,0:T(8,128)(2,1)}, u32[]{:S(2)}, u32[]{:S(2)}) %collective-permute-start.12) | collective-permute-done | bytes 2129952 | tf_op jit(solution)/shard_map/ppermute | solution.py:579
  253.5 2.1 collective-permute-done.14.piece
  256.8 2.0 collective-permute-start.17
  258.9 4.4 put.9
  263.2 4.4 put.10
  267.6 6.1 %unpack.4.refs_2_ = bf16[2,1024,1024]{2,1,0:T(8,128)(2,1)} custom-call(bf16[1040,1024]{1,0:T(8,128)(2,1)} %collective-permute-done.12.message.scales, bf16[1040,1024]{1,0:T(8,128)(2,1)} %collective-permute-done.12.message.scales), custom_call_target="tpu_custom_call" | custom-call | flops 125829120 | bytes 1887436 | tf_op jit(solution)/shard_map/unpack/pallas_call | solution.py:176
  273.7 6.1 %unpack.5.refs_3_ = bf16[2,1024,1024]{2,1,0:T(8,128)(2,1)} custom-call(bf16[1040,1024]{1,0:T(8,128)(2,1)} %collective-permute-done.13.message.scales, bf16[1040,1024]{1,0:T(8,128)(2,1)} %collective-permute-done.13.message.scales), custom_call_target="tpu_custom_call" | custom-call | flops 125829120 | bytes 1887436 | tf_op jit(solution)/shard_map/unpack/pallas_call | solution.py:176
  279.8 21.4 %rotate_part.1.part = f32[1024,1024]{1,0:T(8,128)S(1)} custom-call(s32[2]{0:T(128)S(1)} %pad_add_fusion.at_ref, bf16[2,1024,1024]{2,1,0:T(8,128)(2,1)} %get-tuple-element.66.refs_0_, bf16[2,1024,1024]{2,1,0:T(8,128)(2,1)} %unpack.3.refs_1_, bf16[2,1024,1024]{2,1,0:T(8,128)(2,1)} %unpack.4.refs_2_, bf16[2,1024,1024]{2,1,0:T(8,128)(2,1)} %unpack.5.refs_3_, ...), custom_call_target="tpu_custom_call" | custom-call | flops 5153960960 | bytes 6291456 | tf_op jit(solution)/shard_map/rotate_part/pallas_call | solution.py:244
  301.2 3.7 collective-permute-done.16.above
  304.9 13.5 %rotate.1 = (f32[1024,1024]{1,0:T(8,128)}, f32[1024,1024]{1,0:T(8,128)}, bf16[2,1024,1024]{2,1,0:T(8,128)(2,1)S(1)}) custom-call(s32[2]{0:T(128)S(1)} %pad_add_fusion.at_ref, f32[1024,1024]{1,0:T(8,128)S(1)} %rotate_part.1.part, bf16[1024,1024]{1,0:T(8,128)(2,1)S(1)} %collective-permute-done.16.above, bf16[1024,1024]{1,0:T(8,128)(2,1)} %collective-permute-done.17.below, ...), custom_call_target="tpu_custom_call" | custom-call | flops 17179869184 | bytes 125829120 | tf_op jit(solution)/shard_map/rotate/pallas_call | solution.py:320
  321.1 4.4 put.11
  325.4 12.7 %restore.2 = (f32[2,1024,256]{2,1,0:T(8,128)S(1)}, f32[2,1024,256]{2,1,0:T(8,128)S(1)}, f32[2,1024,256]{2,1,0:T(8,128)S(1)}, f32[2,1024,256]{2,1,0:T(8,128)S(1)}) custom-call(s32[1]{0:T(128)} %bitcast.me_ref, bf16[2,1024,1024]{2,1,0:T(8,128)(2,1)} %copy-done.14, bf16[5,1024,1024]{2,1,0:T(8,128)(2,1)} %get-tuple-element.90.refs_0_.refs_1_.refs_2_.refs_3_, ...), custom_call_target="tpu_custom_call" | custom-call | flops 34359738368 | bytes 67108864 | tf_op jit(solution)/shard_map/restore/pallas_call | solution.py:371
  338.7 3.6 collective-permute-done.18.mate
  348.1 13.3 %restore.3 = (f32[2,1024,256]{2,1,0:T(8,128)S(1)}, f32[2,1024,256]{2,1,0:T(8,128)}, f32[2,1024,256]{2,1,0:T(8,128)S(1)}, f32[2,1024,256]{2,1,0:T(8,128)}) custom-call(s32[1]{0:T(128)} %bitcast.me_ref, bf16[2,1024,1024]{2,1,0:T(8,128)(2,1)} %copy-done.14, bf16[5,1024,1024]{2,1,0:T(8,128)(2,1)} %get-tuple-element.90.refs_0_.refs_1_.refs_2_.refs_3_, ...), custom_call_target="tpu_custom_call" | custom-call | flops 34359738368 | bytes 67108864 | tf_op jit(solution)/shard_map/restore/pallas_call | solution.py:371
  362.1 8.2 %expand_send.4 = (bf16[2,1040,256]{2,1,0:T(8,128)(2,1)}, bf16[1024,512]{1,0:T(8,128)(2,1)S(1)}) custom-call(s32[1]{0:T(128)} %bitcast.1.place_ref, f32[2,1024,256]{2,1,0:T(8,128)S(1)} %get-tuple-element.91.keep, f32[2,1024,256]{2,1,0:T(8,128)S(1)} %collective-permute-done.18.mate, bf16[1040,256]{1,0:T(8,128)(2,1)S(1)} %collective-permute-done.23.refs_0_, ...), custom_call_target="tpu_custom_call" | custom-call | flops 8589934592 | bytes 16777216 | tf_op jit(solution)/shard_map/expand_send/pallas_call | solution.py:453
  371.2 6.3 %collective-permute-start.24 = (bf16[2,1040,256]{2,1,0:T(8,128)(2,1)}, bf16[2,1040,256]{2,1,0:T(8,128)(2,1)S(1)}, u32[]{:S(2)}, u32[]{:S(2)}) collective-permute-start(bf16[2,1040,256]{2,1,0:T(8,128)(2,1)} %get-tuple-element.98), channel_id=1, source_target_pairs={{0,4},{4,0},{8,12},{12,8},{1,5},{5,1},{9,13},{13,9},{2,6},{6,2},{1... | collective-permute-start | bytes 3194888 | tf_op jit(solution)/shard_map/ppermute | solution.py:670
  377.5 5.4 %expand_keep.5.kept = f32[2,1024,256]{2,1,0:T(8,128)} custom-call(s32[1]{0:T(128)} %bitcast.1.place_ref, bf16[1024,512]{1,0:T(8,128)(2,1)} %copy-done.18, bf16[4096,1024]{1,0:T(8,128)(2,1)} %bitcast.20), custom_call_target="tpu_custom_call" | custom-call | flops 8589934592 | bytes 16777216 | tf_op jit(solution)/shard_map/expand_keep/pallas_call | solution.py:486
  386.1 7.3 %expand_send.5 = (bf16[2,1040,256]{2,1,0:T(8,128)(2,1)}, bf16[1024,512]{1,0:T(8,128)(2,1)S(1)}) custom-call(s32[1]{0:T(128)} %bitcast.1.place_ref, f32[2,1024,256]{2,1,0:T(8,128)S(1)} %copy-done.11, f32[2,1024,256]{2,1,0:T(8,128)S(1)} %copy-done.13, bf16[1040,256]{1,0:T(8,128)(2,1)S(1)} %collective-permute-done.22.refs_0_, bf16[4096,1024]{1,0:T(8,128)(2,1)} %bitcast.21), custom_call_target="tpu_custom_call" | custom-call | flops 8589934592 | bytes 16777216 | tf_op jit(solution)/shard_map/expand_send/pallas_call | solution.py:453
  393.4 2.4 send.7
  396.5 5.5 %expand_keep.4.kept = f32[2,1024,256]{2,1,0:T(8,128)} custom-call(s32[1]{0:T(128)} %bitcast.1.place_ref, bf16[1024,512]{1,0:T(8,128)(2,1)} %copy-done.16, bf16[4096,1024]{1,0:T(8,128)(2,1)} %bitcast.22), custom_call_target="tpu_custom_call" | custom-call | flops 8589934592 | bytes 16777216 | tf_op jit(solution)/shard_map/expand_keep/pallas_call | solution.py:486
  402.1 2.2 hop.4
  404.3 5.5 %collective-permute-start.33 = (bf16[1,1040,256]{2,1,0:T(8,128)(2,1)}, bf16[1,1040,256]{2,1,0:T(8,128)(2,1)}, u32[]{:S(2)}, u32[]{:S(2)}) collective-permute-start(bf16[1,1040,256]{2,1,0:T(8,128)(2,1)} %hop.4), channel_id=1, source_target_pairs={{0,8},{4,12},{8,0},{12,4},{1,9},{5,13},{9,1},{13,5},{2,10},{6,14},... | collective-permute-start | bytes 1597448 | tf_op jit(solution)/shard_map/ppermute | solution.py:670
  409.8 2.2 send.5
  413.1 7.7 %expand_send.6 = (bf16[2,1040,256]{2,1,0:T(8,128)(2,1)}, bf16[1024,512]{1,0:T(8,128)(2,1)S(1)}) custom-call(s32[1]{0:T(128)} %bitcast.1.place_ref, f32[2,1024,256]{2,1,0:T(8,128)S(1)} %copy-done.9, f32[2,1024,256]{2,1,0:T(8,128)} %collective-permute-done.25.mate, bf16[1040,256]{1,0:T(8,128)(2,1)} %collective-permute-done.26.refs_0_, bf16[4096,1024]{1,0:T(8,128)(2,1)} %bitcast.23), custom_call_target="tpu_custom_call" | custom-call | flops 8589934592 | bytes 16777216 | tf_op jit(solution)/shard_map/expand_send/pallas_call | solution.py:453
  421.2 15.2 %collective-permute-done.27.refs_0_ = bf16[2,1040,256]{2,1,0:T(8,128)(2,1)} collective-permute-done((bf16[2,1040,256]{2,1,0:T(8,128)(2,1)}, bf16[2,1040,256]{2,1,0:T(8,128)(2,1)}, u32[]{:S(2)}, u32[]{:S(2)}) %collective-permute-start.27) | collective-permute-done | bytes 1064992 | tf_op jit(solution)/shard_map/ppermute | solution.py:670
  436.4 3.3 hop.5
  439.7 3.0 collective-permute-start.32
  442.7 7.5 %expand_send.7 = (bf16[2,1040,256]{2,1,0:T(8,128)(2,1)}, bf16[1024,512]{1,0:T(8,128)(2,1)S(1)}) custom-call(s32[1]{0:T(128)} %bitcast.1.place_ref, f32[2,1024,256]{2,1,0:T(8,128)S(1)} %copy-done.7, f32[2,1024,256]{2,1,0:T(8,128)} %collective-permute-done.19.mate, bf16[1040,256]{1,0:T(8,128)(2,1)S(1)} %collective-permute-done.20.refs_0_, ...), custom_call_target="tpu_custom_call" | custom-call | flops 8589934592 | bytes 16777216 | tf_op jit(solution)/shard_map/expand_send/pallas_call | solution.py:453
  451.3 2.5 collective-permute-start.29
  453.8 5.4 %expand_keep.7.kept = f32[2,1024,256]{2,1,0:T(8,128)} custom-call(s32[1]{0:T(128)} %bitcast.1.place_ref, bf16[1024,512]{1,0:T(8,128)(2,1)} %copy-done.15, bf16[4096,1024]{1,0:T(8,128)(2,1)} %bitcast.25), custom_call_target="tpu_custom_call" | custom-call | flops 8589934592 | bytes 16777216 | tf_op jit(solution)/shard_map/expand_keep/pallas_call | solution.py:486
  459.1 5.3 expand_keep.6.kept
  464.5 6.1 %collective-permute-done.28.refs_0_ = bf16[2,1040,256]{2,1,0:T(8,128)(2,1)} collective-permute-done((bf16[2,1040,256]{2,1,0:T(8,128)(2,1)}, bf16[2,1040,256]{2,1,0:T(8,128)(2,1)}, u32[]{:S(2)}, u32[]{:S(2)}) %collective-permute-start.28) | collective-permute-done | bytes 1064992 | tf_op jit(solution)/shard_map/ppermute | solution.py:670
  472.2 2.5 hop.6
  474.7 3.1 collective-permute-start.31
  477.8 26.2 %collective-permute-done.29.refs_0_ = bf16[2,1040,256]{2,1,0:T(8,128)(2,1)} collective-permute-done((bf16[2,1040,256]{2,1,0:T(8,128)(2,1)}, bf16[2,1040,256]{2,1,0:T(8,128)(2,1)}, u32[]{:S(2)}, u32[]{:S(2)}) %collective-permute-start.29) | collective-permute-done | bytes 1064992 | tf_op jit(solution)/shard_map/ppermute | solution.py:670
  504.0 2.5 hop.7
  506.6 3.1 collective-permute-start.30
  509.6 3.3 finish.4.refs_2_
  512.9 3.4 finish.5.refs_2_
  516.4 3.3 finish.6.refs_2_
  519.6 12.9 %collective-permute-done.30.refs_1_ = bf16[1,1040,256]{2,1,0:T(8,128)(2,1)S(1)} collective-permute-done((bf16[1,1040,256]{2,1,0:T(8,128)(2,1)S(1)}, bf16[1,1040,256]{2,1,0:T(8,128)(2,1)S(1)}, u32[]{:S(2)}, u32[]{:S(2)}) %collective-permute-start.30) | collective-permute-done | bytes 532512 | tf_op jit(solution)/shard_map/ppermute | solution.py:670
  532.6 3.3 finish.7
  (93 shorter events, 34.5 us)
Async XLA Ops:
  0.6 49.0 %collective-permute-start = (bf16[1024,1024]{1,0:T(8,128)(2,1)}, bf16[1024,1024]{1,0:T(8,128)(2,1)}, u32[]{:S(2)}, u32[]{:S(2)}) collective-permute-start(bf16[1024,1024]{1,0:T(8,128)(2,1)} %param.8), channel_id=1, source_target_pairs={{0,2},{1,3},{2,0},{3,1},{4,6},{5,7},{6,4},{7,5},{8,10},{9,11},{10,... | collective-permute-start | bytes 6291464 | tf_op jit(solution)/shard_map/ppermute | solution.py:579
  3.6 48.4 %collective-permute-start.3 = (bf16[1024,1024]{1,0:T(8,128)(2,1)}, bf16[1024,1024]{1,0:T(8,128)(2,1)S(1)}, u32[]{:S(2)}, u32[]{:S(2)}) collective-permute-start(bf16[1024,1024]{1,0:T(8,128)(2,1)} %refs_2_.1), channel_id=1, source_target_pairs={{0,4},{4,8},{8,12},{1,5},{5,9},{9,13},{2,6},{6,10},{10,14},{3,7},{... | collective-permute-start | bytes 6291464 | tf_op jit(solution)/shard_map/ppermute | solution.py:596
  7.2 49.0 %collective-permute-start.5 = (bf16[1024,1024]{1,0:T(8,128)(2,1)}, bf16[1024,1024]{1,0:T(8,128)(2,1)}, u32[]{:S(2)}, u32[]{:S(2)}) collective-permute-start(bf16[1024,1024]{1,0:T(8,128)(2,1)} %refs_2_.1), channel_id=1, source_target_pairs={{4,0},{8,4},{12,8},{5,1},{9,5},{13,9},{6,2},{10,6},{14,10},{7,3},{... | collective-permute-start | bytes 6291464 | tf_op jit(solution)/shard_map/ppermute | solution.py:599
  8.5 52.8 %collective-permute-start.1 = (bf16[1024,1024]{1,0:T(8,128)(2,1)}, bf16[1024,1024]{1,0:T(8,128)(2,1)}, u32[]{:S(2)}, u32[]{:S(2)}) collective-permute-start(bf16[1024,1024]{1,0:T(8,128)(2,1)} %param.8), channel_id=1, source_target_pairs={{0,1},{1,0},{2,3},{3,2},{4,5},{5,4},{6,7},{7,6},{8,9},{9,8},{10,11... | collective-permute-start | bytes 6291464 | tf_op jit(solution)/shard_map/ppermute | solution.py:579
  49.6 13.6 %collective-permute-start.2 = (bf16[1024,1024]{1,0:T(8,128)(2,1)}, bf16[1024,1024]{1,0:T(8,128)(2,1)}, u32[]{:S(2)}, u32[]{:S(2)}) collective-permute-start(bf16[1024,1024]{1,0:T(8,128)(2,1)} %collective-permute-done), channel_id=1, source_target_pairs={{0,1},{1,0},{2,3},{3,2},{4,5},{5,4},{6,7},{7,6},{8,9},{9,8},{10,11... | collective-permute-start | bytes 6291464 | tf_op jit(solution)/shard_map/ppermute | solution.py:579
  52.0 13.1 %collective-permute-start.4 = (bf16[1024,1024]{1,0:T(8,128)(2,1)S(1)}, bf16[1024,1024]{1,0:T(8,128)(2,1)}, u32[]{:S(2)}, u32[]{:S(2)}) collective-permute-start(bf16[1024,1024]{1,0:T(8,128)(2,1)S(1)} %collective-permute-done.3.refs_1_), channel_id=1, source_target_pairs={{4,8},{8,12},{5,9},{9,13},{6,10},{10,14},{7,11},{11,15},{20,24},{2... | collective-permute-start | bytes 6291464 | tf_op jit(solution)/shard_map/ppermute | solution.py:596
  56.3 49.4 %collective-permute-start.6 = (bf16[1024,1024]{1,0:T(8,128)(2,1)}, bf16[1024,1024]{1,0:T(8,128)(2,1)}, u32[]{:S(2)}, u32[]{:S(2)}) collective-permute-start(bf16[1024,1024]{1,0:T(8,128)(2,1)} %collective-permute-done.5.refs_3_), channel_id=1, source_target_pairs={{4,0},{8,4},{5,1},{9,5},{6,2},{10,6},{7,3},{11,7},{20,16},{24,20},... | collective-permute-start | bytes 6291464 | tf_op jit(solution)/shard_map/ppermute | solution.py:599
  57.6 1.6 copy-start.22
  65.1 3.3 copy-start.19
  105.7 17.9 %collective-permute-start.7 = (bf16[1024,1024]{1,0:T(8,128)(2,1)}, bf16[1024,1024]{1,0:T(8,128)(2,1)}, u32[]{:S(2)}, u32[]{:S(2)}) collective-permute-start(bf16[1024,1024]{1,0:T(8,128)(2,1)} %collective-permute-done.4.refs_0_), channel_id=1, source_target_pairs={{8,12},{9,13},{10,14},{11,15},{24,28},{25,29},{26,30},{27,31}} | collective-permute-start | bytes 6291464 | tf_op jit(solution)/shard_map/ppermute | solution.py:596
  107.7 47.6 %collective-permute-start.8 = (bf16[1024,1024]{1,0:T(8,128)(2,1)}, bf16[1024,1024]{1,0:T(8,128)(2,1)}, u32[]{:S(2)}, u32[]{:S(2)}) collective-permute-start(bf16[1024,1024]{1,0:T(8,128)(2,1)} %collective-permute-done.6.refs_4_), channel_id=1, source_target_pairs={{4,0},{5,1},{6,2},{7,3},{20,16},{21,17},{22,18},{23,19}} | collective-permute-start | bytes 6291464 | tf_op jit(solution)/shard_map/ppermute | solution.py:599
  155.2 46.6 %collective-permute-start.10 = (bf16[1024,1024]{1,0:T(8,128)(2,1)}, bf16[1024,1024]{1,0:T(8,128)(2,1)}, u32[]{:S(2)}, u32[]{:S(2)}) collective-permute-start(bf16[1024,1024]{1,0:T(8,128)(2,1)} %piece), channel_id=1, source_target_pairs={{4,0},{8,4},{12,8},{5,1},{9,5},{13,9},{6,2},{10,6},{14,10},{7,3},{... | collective-permute-start | bytes 6291464 | tf_op jit(solution)/shard_map/ppermute | solution.py:599
  156.5 46.5 %collective-permute-start.9 = (bf16[1024,1024]{1,0:T(8,128)(2,1)}, bf16[1024,1024]{1,0:T(8,128)(2,1)S(1)}, u32[]{:S(2)}, u32[]{:S(2)}) collective-permute-start(bf16[1024,1024]{1,0:T(8,128)(2,1)} %piece), channel_id=1, source_target_pairs={{0,4},{4,8},{8,12},{1,5},{5,9},{9,13},{2,6},{6,10},{10,14},{3,7},{... | collective-permute-start | bytes 6291464 | tf_op jit(solution)/shard_map/ppermute | solution.py:596
  203.0 1.4 copy-start.21
  204.4 16.8 %collective-permute-start.11 = (bf16[1040,1024]{1,0:T(8,128)(2,1)}, bf16[1040,1024]{1,0:T(8,128)(2,1)S(1)}, u32[]{:S(2)}, u32[]{:S(2)}) collective-permute-start(bf16[1040,1024]{1,0:T(8,128)(2,1)} %get-tuple-element.69), channel_id=1, source_target_pairs={{0,1},{1,0},{2,3},{3,2},{4,5},{5,4},{6,7},{7,6},{8,9},{9,8},{10,11... | collective-permute-start | bytes 6389768 | tf_op jit(solution)/shard_map/ppermute | solution.py:579
  204.4 49.1 %collective-permute-start.12 = (bf16[1040,1024]{1,0:T(8,128)(2,1)}, bf16[1040,1024]{1,0:T(8,128)(2,1)}, u32[]{:S(2)}, u32[]{:S(2)}) collective-permute-start(bf16[1040,1024]{1,0:T(8,128)(2,1)} %get-tuple-element.69), channel_id=1, source_target_pairs={{0,2},{1,3},{2,0},{3,1},{4,6},{5,7},{6,4},{7,5},{8,10},{9,11},{10,... | collective-permute-start | bytes 6389768 | tf_op jit(solution)/shard_map/ppermute | solution.py:579
  204.9 50.6 %collective-permute-start.14 = (bf16[1024,1024]{1,0:T(8,128)(2,1)}, bf16[1024,1024]{1,0:T(8,128)(2,1)}, u32[]{:S(2)}, u32[]{:S(2)}) collective-permute-start(bf16[1024,1024]{1,0:T(8,128)(2,1)} %collective-permute-done.10.piece), channel_id=1, source_target_pairs={{4,0},{8,4},{5,1},{9,5},{6,2},{10,6},{7,3},{11,7},{20,16},{24,20},... | collective-permute-start | bytes 6291464 | tf_op jit(solution)/shard_map/ppermute | solution.py:599
  206.2 50.6 %collective-permute-start.15 = (bf16[1024,1024]{1,0:T(8,128)(2,1)}, bf16[1024,1024]{1,0:T(8,128)(2,1)}, u32[]{:S(2)}, u32[]{:S(2)}) collective-permute-start(bf16[1024,1024]{1,0:T(8,128)(2,1)} %copy-done.21), channel_id=1, source_target_pairs={{4,8},{8,12},{5,9},{9,13},{6,10},{10,14},{7,11},{11,15},{20,24},{2... | collective-permute-start | bytes 6291464 | tf_op jit(solution)/shard_map/ppermute | solution.py:596
  221.2 1.3 copy-start.20
  253.5 20.2 %collective-permute-start.13 = (bf16[1040,1024]{1,0:T(8,128)(2,1)}, bf16[1040,1024]{1,0:T(8,128)(2,1)}, u32[]{:S(2)}, u32[]{:S(2)}) collective-permute-start(bf16[1040,1024]{1,0:T(8,128)(2,1)} %collective-permute-done.12.message.scales), channel_id=1, source_target_pairs={{0,1},{1,0},{2,3},{3,2},{4,5},{5,4},{6,7},{7,6},{8,9},{9,8},{10,11... | collective-permute-start | bytes 6389768 | tf_op jit(solution)/shard_map/ppermute | solution.py:579
  255.5 49.4 %collective-permute-start.16 = (bf16[1024,1024]{1,0:T(8,128)(2,1)}, bf16[1024,1024]{1,0:T(8,128)(2,1)S(1)}, u32[]{:S(2)}, u32[]{:S(2)}) collective-permute-start(bf16[1024,1024]{1,0:T(8,128)(2,1)} %collective-permute-done.14.piece), channel_id=1, source_target_pairs={{4,0},{5,1},{6,2},{7,3},{20,16},{21,17},{22,18},{23,19}} | collective-permute-start | bytes 6291464 | tf_op jit(solution)/shard_map/ppermute | solution.py:599
  256.8 48.1 %collective-permute-start.17 = (bf16[1024,1024]{1,0:T(8,128)(2,1)}, bf16[1024,1024]{1,0:T(8,128)(2,1)}, u32[]{:S(2)}, u32[]{:S(2)}) collective-permute-start(bf16[1024,1024]{1,0:T(8,128)(2,1)} %collective-permute-done.15.piece), channel_id=1, source_target_pairs={{8,12},{9,13},{10,14},{11,15},{24,28},{25,29},{26,30},{27,31}} | collective-permute-start | bytes 6291464 | tf_op jit(solution)/shard_map/ppermute | solution.py:596
  318.4 2.6 copy-start.14
  338.1 7.2 %copy-start.10 = (f32[2,1024,256]{2,1,0:T(8,128)}, f32[2,1024,256]{2,1,0:T(8,128)S(1)}, u32[]{:S(2)}) copy-start(f32[2,1024,256]{2,1,0:T(8,128)S(1)} %get-tuple-element.96.keep) | copy-start | bytes 6291460
  338.1 4.2 collective-permute-start.18
  338.2 7.1 %collective-permute-start.21 = (f32[2,1024,256]{2,1,0:T(8,128)S(1)}, f32[2,1024,256]{2,1,0:T(8,128)S(1)}, u32[]{:S(2)}, u32[]{:S(2)}) collective-permute-start(f32[2,1024,256]{2,1,0:T(8,128)S(1)} %get-tuple-element.97), channel_id=1, source_target_pairs={{0,1},{1,0},{2,3},{3,2},{4,5},{5,4},{6,7},{7,6},{8,9},{9,8},{10,11... | collective-permute-start | bytes 6291464 | tf_op jit(solution)/shard_map/ppermute | solution.py:579
  343.2 18.9 %collective-permute-start.23 = (bf16[1040,256]{1,0:T(8,128)(2,1)S(1)}, bf16[1040,256]{1,0:T(8,128)(2,1)S(1)}, u32[]{:S(2)}, u32[]{:S(2)}) collective-permute-start(bf16[1040,256]{1,0:T(8,128)(2,1)S(1)} %send.4), channel_id=1, source_target_pairs={{0,2},{1,3},{2,0},{3,1},{4,6},{5,7},{6,4},{7,5},{8,10},{9,11},{10,... | collective-permute-start | bytes 1597448 | tf_op jit(solution)/shard_map/ppermute | solution.py:579
  345.4 1.3 copy-start.12
  346.7 30.9 %collective-permute-start.22 = (bf16[1040,256]{1,0:T(8,128)(2,1)S(1)}, bf16[1040,256]{1,0:T(8,128)(2,1)S(1)}, u32[]{:S(2)}, u32[]{:S(2)}) collective-permute-start(bf16[1040,256]{1,0:T(8,128)(2,1)S(1)} %send.6), channel_id=1, source_target_pairs={{0,2},{1,3},{2,0},{3,1},{4,6},{5,7},{6,4},{7,5},{8,10},{9,11},{10,... | collective-permute-start | bytes 1597448 | tf_op jit(solution)/shard_map/ppermute | solution.py:579
  361.5 8.8 %copy-start.6 = (f32[2,1024,256]{2,1,0:T(8,128)}, f32[2,1024,256]{2,1,0:T(8,128)S(1)}, u32[]{:S(2)}) copy-start(f32[2,1024,256]{2,1,0:T(8,128)S(1)} %get-tuple-element.94.keep) | copy-start | bytes 6291460
  361.5 32.0 %copy-start.8 = (f32[2,1024,256]{2,1,0:T(8,128)}, f32[2,1024,256]{2,1,0:T(8,128)S(1)}, u32[]{:S(2)}) copy-start(f32[2,1024,256]{2,1,0:T(8,128)S(1)} %get-tuple-element.105.keep) | copy-start | bytes 6291460
  361.5 31.9 %collective-permute-start.25 = (f32[2,1024,256]{2,1,0:T(8,128)}, f32[2,1024,256]{2,1,0:T(8,128)}, u32[]{:S(2)}, u32[]{:S(2)}) collective-permute-start(f32[2,1024,256]{2,1,0:T(8,128)} %get-tuple-element.106), channel_id=1, source_target_pairs={{0,1},{1,0},{2,3},{3,2},{4,5},{5,4},{6,7},{7,6},{8,9},{9,8},{10,11... | collective-permute-start | bytes 6291464 | tf_op jit(solution)/shard_map/ppermute | solution.py:579
  361.6 48.3 %collective-permute-start.19 = (f32[2,1024,256]{2,1,0:T(8,128)}, f32[2,1024,256]{2,1,0:T(8,128)}, u32[]{:S(2)}, u32[]{:S(2)}) collective-permute-start(f32[2,1024,256]{2,1,0:T(8,128)} %get-tuple-element.95), channel_id=1, source_target_pairs={{0,1},{1,0},{2,3},{3,2},{4,5},{5,4},{6,7},{7,6},{8,9},{9,8},{10,11... | collective-permute-start | bytes 6291464 | tf_op jit(solution)/shard_map/ppermute | solution.py:579
  370.2 1.0 copy-start.18
  371.2 30.8 %collective-permute-start.24 = (bf16[2,1040,256]{2,1,0:T(8,128)(2,1)}, bf16[2,1040,256]{2,1,0:T(8,128)(2,1)S(1)}, u32[]{:S(2)}, u32[]{:S(2)}) collective-permute-start(bf16[2,1040,256]{2,1,0:T(8,128)(2,1)} %get-tuple-element.98), channel_id=1, source_target_pairs={{0,4},{4,0},{8,12},{12,8},{1,5},{5,1},{9,13},{13,9},{2,6},{6,2},{1... | collective-permute-start | bytes 3194888 | tf_op jit(solution)/shard_map/ppermute | solution.py:670
  382.9 1.6 copy-start.11
  384.5 1.6 copy-start.13
  393.4 2.4 copy-start.16
  393.4 43.0 %collective-permute-start.27 = (bf16[2,1040,256]{2,1,0:T(8,128)(2,1)}, bf16[2,1040,256]{2,1,0:T(8,128)(2,1)}, u32[]{:S(2)}, u32[]{:S(2)}) collective-permute-start(bf16[2,1040,256]{2,1,0:T(8,128)(2,1)} %get-tuple-element.102), channel_id=1, source_target_pairs={{0,4},{4,0},{8,12},{12,8},{1,5},{5,1},{9,13},{13,9},{2,6},{6,2},{1... | collective-permute-start | bytes 3194888 | tf_op jit(solution)/shard_map/ppermute | solution.py:670
  395.9 17.2 %collective-permute-start.26 = (bf16[1040,256]{1,0:T(8,128)(2,1)S(1)}, bf16[1040,256]{1,0:T(8,128)(2,1)}, u32[]{:S(2)}, u32[]{:S(2)}) collective-permute-start(bf16[1040,256]{1,0:T(8,128)(2,1)S(1)} %send.7), channel_id=1, source_target_pairs={{0,2},{1,3},{2,0},{3,1},{4,6},{5,7},{6,4},{7,5},{8,10},{9,11},{10,... | collective-permute-start | bytes 1597448 | tf_op jit(solution)/shard_map/ppermute | solution.py:579
  396.5 5.6 %copy-start = (f32[2,1024,256]{2,1,0:T(8,128)S(1)}, f32[2,1024,256]{2,1,0:T(8,128)}, u32[]{:S(2)}) copy-start(f32[2,1024,256]{2,1,0:T(8,128)} %expand_keep.5.kept) | copy-start | bytes 6291460
  402.0 7.8 %copy-start.7 = (f32[2,1024,256]{2,1,0:T(8,128)S(1)}, f32[2,1024,256]{2,1,0:T(8,128)}, u32[]{:S(2)}) copy-start(f32[2,1024,256]{2,1,0:T(8,128)} %copy-done.6) | copy-start | bytes 6291460
  404.3 105.3 %collective-permute-start.33 = (bf16[1,1040,256]{2,1,0:T(8,128)(2,1)}, bf16[1,1040,256]{2,1,0:T(8,128)(2,1)}, u32[]{:S(2)}, u32[]{:S(2)}) collective-permute-start(bf16[1,1040,256]{2,1,0:T(8,128)(2,1)} %hop.4), channel_id=1, source_target_pairs={{0,8},{4,12},{8,0},{12,4},{1,9},{5,13},{9,1},{13,5},{2,10},{6,14},... | collective-permute-start | bytes 1597448 | tf_op jit(solution)/shard_map/ppermute | solution.py:670
  409.8 3.2 copy-start.9
  412.0 24.4 %copy-start.1 = (f32[2,1024,256]{2,1,0:T(8,128)S(1)}, f32[2,1024,256]{2,1,0:T(8,128)}, u32[]{:S(2)}) copy-start(f32[2,1024,256]{2,1,0:T(8,128)} %expand_keep.4.kept) | copy-start | bytes 6291460
  412.0 30.7 %collective-permute-start.20 = (bf16[1040,256]{1,0:T(8,128)(2,1)S(1)}, bf16[1040,256]{1,0:T(8,128)(2,1)S(1)}, u32[]{:S(2)}, u32[]{:S(2)}) collective-permute-start(bf16[1040,256]{1,0:T(8,128)(2,1)S(1)} %send.5), channel_id=1, source_target_pairs={{0,2},{1,3},{2,0},{3,1},{4,6},{5,7},{6,4},{7,5},{8,10},{9,11},{10,... | collective-permute-start | bytes 1597448 | tf_op jit(solution)/shard_map/ppermute | solution.py:579
  420.8 19.0 %copy-start.15 = (bf16[1024,512]{1,0:T(8,128)(2,1)}, bf16[1024,512]{1,0:T(8,128)(2,1)S(1)}, u32[]{:S(2)}) copy-start(bf16[1024,512]{1,0:T(8,128)(2,1)S(1)} %get-tuple-element.112.both) | copy-start | bytes 3145732
  420.8 49.9 %collective-permute-start.28 = (bf16[2,1040,256]{2,1,0:T(8,128)(2,1)}, bf16[2,1040,256]{2,1,0:T(8,128)(2,1)}, u32[]{:S(2)}, u32[]{:S(2)}) collective-permute-start(bf16[2,1040,256]{2,1,0:T(8,128)(2,1)} %get-tuple-element.108), channel_id=1, source_target_pairs={{0,4},{4,0},{8,12},{12,8},{1,5},{5,1},{9,13},{13,9},{2,6},{6,2},{1... | collective-permute-start | bytes 3194888 | tf_op jit(solution)/shard_map/ppermute | solution.py:670
  439.7 73.2 %collective-permute-start.32 = (bf16[1,1040,256]{2,1,0:T(8,128)(2,1)}, bf16[1,1040,256]{2,1,0:T(8,128)(2,1)S(1)}, u32[]{:S(2)}, u32[]{:S(2)}) collective-permute-start(bf16[1,1040,256]{2,1,0:T(8,128)(2,1)} %hop.5), channel_id=1, source_target_pairs={{0,8},{4,12},{8,0},{12,4},{1,9},{5,13},{9,1},{13,5},{2,10},{6,14},... | collective-permute-start | bytes 1597448 | tf_op jit(solution)/shard_map/ppermute | solution.py:670
  450.3 1.0 copy-start.17
  451.3 52.7 %collective-permute-start.29 = (bf16[2,1040,256]{2,1,0:T(8,128)(2,1)}, bf16[2,1040,256]{2,1,0:T(8,128)(2,1)}, u32[]{:S(2)}, u32[]{:S(2)}) collective-permute-start(bf16[2,1040,256]{2,1,0:T(8,128)(2,1)} %get-tuple-element.114), channel_id=1, source_target_pairs={{0,4},{4,0},{8,12},{12,8},{1,5},{5,1},{9,13},{13,9},{2,6},{6,2},{1... | collective-permute-start | bytes 3194888 | tf_op jit(solution)/shard_map/ppermute | solution.py:670
  464.5 39.5 %copy-start.3 = (f32[2,1024,256]{2,1,0:T(8,128)S(1)}, f32[2,1024,256]{2,1,0:T(8,128)}, u32[]{:S(2)}) copy-start(f32[2,1024,256]{2,1,0:T(8,128)} %expand_keep.6.kept) | copy-start | bytes 6291460
  470.6 1.6 copy-start.4
  474.7 41.6 %collective-permute-start.31 = (bf16[1,1040,256]{2,1,0:T(8,128)(2,1)S(1)}, bf16[1,1040,256]{2,1,0:T(8,128)(2,1)S(1)}, u32[]{:S(2)}, u32[]{:S(2)}) collective-permute-start(bf16[1,1040,256]{2,1,0:T(8,128)(2,1)S(1)} %hop.6), channel_id=1, source_target_pairs={{0,8},{4,12},{8,0},{12,4},{1,9},{5,13},{9,1},{13,5},{2,10},{6,14},... | collective-permute-start | bytes 1597448 | tf_op jit(solution)/shard_map/ppermute | solution.py:670
  506.5 6.4 %copy-start.2 = (f32[2,1024,256]{2,1,0:T(8,128)S(1)}, f32[2,1024,256]{2,1,0:T(8,128)}, u32[]{:S(2)}) copy-start(f32[2,1024,256]{2,1,0:T(8,128)} %expand_keep.4.kept) | copy-start | bytes 6291460
  506.6 26.0 %collective-permute-start.30 = (bf16[1,1040,256]{2,1,0:T(8,128)(2,1)S(1)}, bf16[1,1040,256]{2,1,0:T(8,128)(2,1)S(1)}, u32[]{:S(2)}, u32[]{:S(2)}) collective-permute-start(bf16[1,1040,256]{2,1,0:T(8,128)(2,1)S(1)} %hop.7), channel_id=1, source_target_pairs={{0,8},{4,12},{8,0},{12,4},{1,9},{5,13},{9,1},{13,5},{2,10},{6,14},... | collective-permute-start | bytes 1597448 | tf_op jit(solution)/shard_map/ppermute | solution.py:670
  512.9 3.4 copy-start.5

commit v14 on v13

--- a/solution.py
+++ b/solution.py
@@ -263,7 +263,8 @@
 
 
 def rotate_kernel(at_ref, part, above, below, first, second, *refs, cols, lines):
-    pieces, (new_first, new_second, normed, held, last, arrived) = refs[:cols], refs[cols:]
+    pieces, refs = refs[:cols], refs[cols + 1 :]
+    new_first, new_second, normed, flipped, held, last, arrived = refs
     tile, width = first.shape
     depth = last.shape[0]
     me, place = at_ref[0], at_ref[1]
@@ -290,6 +291,7 @@
                     copy(distance, at).start()
 
         last[...] = jnp.where(place == 0, above[...], below[...])
+        flipped[0] = last[...].T
 
     for at in range(steps):
 
@@ -309,7 +311,7 @@
     normed[1] = low
 
 
-def rotate(at, part, pieces, above, below, first, second, lines):
+def rotate(at, part, pieces, above, below, first, second, flipped, lines):
     cols = len(pieces)
     rows, width = first.shape
     depth = above.shape[0]
@@ -323,8 +325,13 @@
             num_scalar_prefetch=1,
             grid=(rows // tile,),
             in_specs=[block, whole, whole, block, block]
-            + [pl.BlockSpec(memory_space=pl.ANY)] * cols,
-            out_specs=[block, block, pair],
+            + [pl.BlockSpec(memory_space=pl.ANY)] * (cols + 1),
+            out_specs=[
+                block,
+                block,
+                pair,
+                pl.BlockSpec((1, width, depth), lambda i, s: (s[2], 0, 0)),
+            ],
             scratch_shapes=[
                 pltpu.VMEM((2, rows, depth), BF16),
                 pltpu.VMEM((depth, width), BF16),
@@ -335,11 +342,13 @@
             jax.ShapeDtypeStruct((rows, width), F32),
             jax.ShapeDtypeStruct((rows, width), F32),
             jax.ShapeDtypeStruct((2, rows, width), BF16),
+            jax.ShapeDtypeStruct(flipped.shape, BF16),
         ],
-        compiler_params=params(40),
+        input_output_aliases={6 + cols: 3},
+        compiler_params=params(44),
         cost_estimate=cost(4 * rows * width * depth, 30 * rows * width),
         name="rotate",
-    )(at, part, above, below, first, second, *pieces)
+    )(at, part, above, below, first, second, *pieces, flipped)
 
 
 def restore_kernel(me_ref, normed, *refs, cols):
@@ -610,7 +619,9 @@
         depth, width = gradient.shape
         piece = width // CHUNKS
         far = lines - 1
-        spot, at = jnp.reshape(place, (1,)), jnp.stack([me, place])
+        ends = (place == 0) | (place == far) if depth == width else False
+        spot = jnp.reshape(place, (1,))
+        at = jnp.stack([me, place, jnp.where(ends, far - place, lines)])
         me_now = jnp.reshape(me, (1,))
         barrier = lax.optimization_barrier
         near = [offset for offset in range(-far, far + 1) if abs(offset) < far]
@@ -657,14 +668,9 @@
         part, above, below = barrier((part, above, below))
         if not aligned:
             above, below = jnp.zeros_like(above), jnp.zeros_like(below)
-        new_first, new_second, normed = rotate(
-            at, part, pieces, above, below, first_moment, second_moment, lines
+        new_first, new_second, normed, flipped = rotate(
+            at, part, pieces, above, below, first_moment, second_moment, held[1], lines
         )
-        if aligned:
-            last = jnp.where(place == 0, after(above, normed), below)
-            there = jnp.where((place == 0) | (place == far), far - place, lines)
-            held = put(jnp.reshape(there, (1,)), last, held, lines + 1)
-        flipped = held[1]
 
         def cross(value, distance):
             return lax.ppermute(value, "row", [(i, i ^ distance) for i in range(lines)])
@@ -694,12 +700,15 @@
             outgoing.append(message)
             products.append((expand_keep(spot, both, left, depth), [cross(message, 1)]))
 
-        for batch in range(2):
-            ready = after(normed, *sent[0]) if batch else normed
-            for keep, mate in restore(me_now, ready, flipped, cols, piece, batch, CHUNKS // 2):
+        def sums(batch, count, *before):
+            ready = after(normed, *before) if before else normed
+            for keep, mate in restore(me_now, ready, flipped, cols, piece, batch, count):
                 mate = swap(mate, 1)
                 halves.append((keep, mate))
                 sent.append([send(keep, mate, distance, []) for distance in range(2, cols, 2)])
+
+        sums(0, 2)
+        sums(1, 2, *sent[0])
         for chunk in range(CHUNKS):
             if chunk >= 2:
                 later_hops(chunk - 2)

time: 537 us -> 534 us (level)
    pallas_call x6 -> x5, Pallas kernels: 26.1 us -> 21.8 us  [put(): pl.pallas_call(put_kernel, grid_spec=pltpu.PrefetchScalarGridSpec(num_sca...]
    unnamed x46 -> x48, local copies, waits for them, and re-layouts: 14.7 us -> 17.8 us
where the time goes in v14:
time: 534 us; the launch traced here: 533 us
  waiting for transfers between devices  232 us (43%)
  Pallas kernels  217 us (41%)
  starting transfers between devices  57.2 us (11%)
  local copies, waits for them, and re-layouts  24.7 us (5%)
    ppermute x6, waiting for transfers between devices, down(): return lax.ppermute(value, 'row', [(i, i - 1) for i in senders])  98 us
    ppermute x14, waiting for transfers between devices, swap(): return lax.ppermute(value, 'col', [(i, i ^ distance) for i in range(cols)])  70.1 us
    ppermute x8, waiting for transfers between devices, cross(): return lax.ppermute(value, 'row', [(i, i ^ distance) for i in range(lines)])  60.6 us
    pallas_call x4, Pallas kernels, expand_send(): pl.pallas_call(functools.partial(expand_send_kernel, tile=min(64, depth))...  30.7 us
    pallas_call x2, Pallas kernels, restore(): pl.pallas_call(functools.partial(restore_kernel, cols=cols), grid_spec=pl...  26 us
    pallas_call x2, Pallas kernels, halfway(): pl.pallas_call(functools.partial(halfway_kernel, offsets=offsets, lines=l...  24.3 us
    ppermute x8, starting transfers between devices, cross(): return lax.ppermute(value, 'row', [(i, i ^ distance) for i in range(lines)])  23.9 us
    pallas_call x5, Pallas kernels, put(): pl.pallas_call(put_kernel, grid_spec=pltpu.PrefetchScalarGridSpec(num_sca...  21.8 us
  transfers between devices with their start and end apart: 34, of which 17 were waited for; matrix products, arithmetic and copies ran while one was open for 1% of the time, Pallas kernels for 34%

profile of v14, /device:TPU:0, one launch (start us, length us, event | category | flops | bytes accessed | tf_op | source)
XLA Modules:
  0.0 532.6 jit_solution(4835436262567480724)
XLA Ops:
  0.6 3.0 collective-permute-start
  3.6 3.6 collective-permute-start.3
  8.6 41.0 %collective-permute-done = bf16[1024,1024]{1,0:T(8,128)(2,1)} collective-permute-done((bf16[1024,1024]{1,0:T(8,128)(2,1)}, bf16[1024,1024]{1,0:T(8,128)(2,1)}, u32[]{:S(2)}, u32[]{:S(2)}) %collective-permute-start) | collective-permute-done | bytes 2097184 | tf_op jit(solution)/shard_map/ppermute | solution.py:588
  49.6 2.4 collective-permute-done.3.refs_1_
  52.0 2.0 collective-permute-start.4
  54.0 2.3 collective-permute-done.5.refs_3_
  59.5 1.9 bitcast_dynamic-update-slice_fusion.2
  63.2 1.9 bitcast_dynamic-update-slice_fusion
  65.1 3.3 copy-done.20
  68.4 37.3 %collective-permute-done.6.refs_4_ = bf16[1024,1024]{1,0:T(8,128)(2,1)} collective-permute-done((bf16[1024,1024]{1,0:T(8,128)(2,1)}, bf16[1024,1024]{1,0:T(8,128)(2,1)}, u32[]{:S(2)}, u32[]{:S(2)}) %collective-permute-start.6) | collective-permute-done | bytes 2097184 | tf_op jit(solution)/shard_map/ppermute | solution.py:608
  105.7 2.0 collective-permute-start.7
  108.9 14.7 %halfway.2.refs_2_ = f32[1024,1024]{1,0:T(8,128)} custom-call(s32[1]{0:T(128)} %bitcast.1.place_ref, bf16[4096,1024]{1,0:T(8,128)(2,1)} %bitcast.17, bf16[1024,1024]{1,0:T(8,128)(2,1)} %collective-permute-done.4.refs_0_, bf16[1024,1024]{1,0:T(8,128)(2,1)S(1)} %collective-permute-done.3.refs_1_, bf16[1024,1024]{1,0:T(8,128)(2,1)} %refs_2_.1, ...), custom_call_target="tpu_custom_call" | custom-call | flops 2576980480 | bytes 2516582 | tf_op jit(solution)/shard_map/halfway/pallas_call | solution.py:114
  123.6 31.6 %collective-permute-done.8.refs_1_ = bf16[1024,1024]{1,0:T(8,128)(2,1)} collective-permute-done((bf16[1024,1024]{1,0:T(8,128)(2,1)}, bf16[1024,1024]{1,0:T(8,128)(2,1)}, u32[]{:S(2)}, u32[]{:S(2)}) %collective-permute-start.8) | collective-permute-done | bytes 2097184 | tf_op jit(solution)/shard_map/ppermute | solution.py:608
  156.5 4.7 collective-permute-start.9
  161.2 9.6 %halfway.3.value = f32[1024,1024]{1,0:T(8,128)} custom-call(s32[1]{0:T(128)} %bitcast.1.place_ref, bf16[4096,1024]{1,0:T(8,128)(2,1)} %bitcast.18, bf16[1024,1024]{1,0:T(8,128)(2,1)} %collective-permute-done.7.refs_0_, bf16[1024,1024]{1,0:T(8,128)(2,1)} %collective-permute-done.8.refs_1_, f32[1024,1024]{1,0:T(8,128)} %halfway.2.refs_2_), custom_call_target="tpu_custom_call" | custom-call | flops 2576980480 | bytes 2516582 | tf_op jit(solution)/shard_map/halfway/pallas_call | solution.py:114
  170.8 7.9 %pack.1 = (bf16[2,1024,1024]{2,1,0:T(8,128)(2,1)}, bf16[1040,1024]{1,0:T(8,128)(2,1)}) custom-call(f32[1024,1024]{1,0:T(8,128)} %halfway.3.value), custom_call_target="tpu_custom_call" | custom-call | flops 125829120 | bytes 3145728 | tf_op jit(solution)/shard_map/pack/pallas_call | solution.py:147
  178.7 23.1 %collective-permute-done.10.piece = bf16[1024,1024]{1,0:T(8,128)(2,1)} collective-permute-done((bf16[1024,1024]{1,0:T(8,128)(2,1)}, bf16[1024,1024]{1,0:T(8,128)(2,1)}, u32[]{:S(2)}, u32[]{:S(2)}) %collective-permute-start.10) | collective-permute-done | bytes 2097184 | tf_op jit(solution)/shard_map/ppermute | solution.py:608
  206.2 2.0 collective-permute-start.15
  208.2 4.4 put.5
  212.6 4.4 put.6
  216.9 4.3 put.7
  222.6 6.1 %unpack.3.refs_1_ = bf16[2,1024,1024]{2,1,0:T(8,128)(2,1)} custom-call(bf16[1040,1024]{1,0:T(8,128)(2,1)} %copy-done.21, bf16[1040,1024]{1,0:T(8,128)(2,1)} %copy-done.21), custom_call_target="tpu_custom_call" | custom-call | flops 125829120 | bytes 1887436 | tf_op jit(solution)/shard_map/unpack/pallas_call | solution.py:176
  228.7 24.8 %collective-permute-done.12.message.scales = bf16[1040,1024]{1,0:T(8,128)(2,1)} collective-permute-done((bf16[1040,1024]{1,0:T(8,128)(2,1)}, bf16[1040,1024]{1,0:T(8,128)(2,1)}, u32[]{:S(2)}, u32[]{:S(2)}) %collective-permute-start.12) | collective-permute-done | bytes 2129952 | tf_op jit(solution)/shard_map/ppermute | solution.py:588
  253.5 2.1 collective-permute-done.14.piece
  256.8 2.0 collective-permute-start.17
  258.9 4.4 put.8
  263.3 4.4 put.9
  267.6 6.1 %unpack.4.refs_2_ = bf16[2,1024,1024]{2,1,0:T(8,128)(2,1)} custom-call(bf16[1040,1024]{1,0:T(8,128)(2,1)} %collective-permute-done.12.message.scales, bf16[1040,1024]{1,0:T(8,128)(2,1)} %collective-permute-done.12.message.scales), custom_call_target="tpu_custom_call" | custom-call | flops 125829120 | bytes 1887436 | tf_op jit(solution)/shard_map/unpack/pallas_call | solution.py:176
  273.7 6.1 %unpack.5.refs_3_ = bf16[2,1024,1024]{2,1,0:T(8,128)(2,1)} custom-call(bf16[1040,1024]{1,0:T(8,128)(2,1)} %collective-permute-done.13.message.scales, bf16[1040,1024]{1,0:T(8,128)(2,1)} %collective-permute-done.13.message.scales), custom_call_target="tpu_custom_call" | custom-call | flops 125829120 | bytes 1887436 | tf_op jit(solution)/shard_map/unpack/pallas_call | solution.py:176
  279.8 21.4 %rotate_part.1.part = f32[1024,1024]{1,0:T(8,128)S(1)} custom-call(s32[3]{0:T(128)S(1)} %pad_add_fusion.at_ref, bf16[2,1024,1024]{2,1,0:T(8,128)(2,1)} %get-tuple-element.65.refs_0_, bf16[2,1024,1024]{2,1,0:T(8,128)(2,1)} %unpack.3.refs_1_, bf16[2,1024,1024]{2,1,0:T(8,128)(2,1)} %unpack.4.refs_2_, bf16[2,1024,1024]{2,1,0:T(8,128)(2,1)} %unpack.5.refs_3_, ...), custom_call_target="tpu_custom_call" | custom-call | flops 5153960960 | bytes 6291456 | tf_op jit(solution)/shard_map/rotate_part/pallas_call | solution.py:244
  301.2 2.0 copy-done.6
  304.9 15.3 %rotate.1 = (f32[1024,1024]{1,0:T(8,128)}, f32[1024,1024]{1,0:T(8,128)}, bf16[2,1024,1024]{2,1,0:T(8,128)(2,1)S(1)}, bf16[5,1024,1024]{2,1,0:T(8,128)(2,1)}) custom-call(s32[3]{0:T(128)S(1)} %pad_add_fusion.at_ref, f32[1024,1024]{1,0:T(8,128)} %copy-done.6, bf16[1024,1024]{1,0:T(8,128)(2,1)S(1)} %collective-permute-done.16.above, ...), custom_call_target="tpu_custom_call", output_to_operand_aliasing={{3}: (10, {})} | custom-call | flops 17179869184 | bytes 125829120 | tf_op jit(solution)/shard_map/rotate/pallas_call | solution.py:322
  320.2 2.0 copy-done.15
  322.2 12.7 %restore.2 = (f32[2,1024,256]{2,1,0:T(8,128)S(1)}, f32[2,1024,256]{2,1,0:T(8,128)S(1)}, f32[2,1024,256]{2,1,0:T(8,128)S(1)}, f32[2,1024,256]{2,1,0:T(8,128)S(1)}) custom-call(s32[1]{0:T(128)} %bitcast.me_ref, bf16[2,1024,1024]{2,1,0:T(8,128)(2,1)} %copy-done.15, bf16[5,1024,1024]{2,1,0:T(8,128)(2,1)} %get-tuple-element.88.refs_0_.refs_1_.refs_2_.refs_3_, ...), custom_call_target="tpu_custom_call" | custom-call | flops 34359738368 | bytes 67108864 | tf_op jit(solution)/shard_map/restore/pallas_call | solution.py:380
  335.5 3.6 collective-permute-done.18.mate
  344.9 13.3 %restore.3 = (f32[2,1024,256]{2,1,0:T(8,128)S(1)}, f32[2,1024,256]{2,1,0:T(8,128)}, f32[2,1024,256]{2,1,0:T(8,128)S(1)}, f32[2,1024,256]{2,1,0:T(8,128)}) custom-call(s32[1]{0:T(128)} %bitcast.me_ref, bf16[2,1024,1024]{2,1,0:T(8,128)(2,1)} %copy-done.15, bf16[5,1024,1024]{2,1,0:T(8,128)(2,1)} %get-tuple-element.88.refs_0_.refs_1_.refs_2_.refs_3_, ...), custom_call_target="tpu_custom_call" | custom-call | flops 34359738368 | bytes 67108864 | tf_op jit(solution)/shard_map/restore/pallas_call | solution.py:380
  358.8 8.2 %expand_send.4 = (bf16[2,1040,256]{2,1,0:T(8,128)(2,1)}, bf16[1024,512]{1,0:T(8,128)(2,1)S(1)}) custom-call(s32[1]{0:T(128)} %bitcast.1.place_ref, f32[2,1024,256]{2,1,0:T(8,128)S(1)} %get-tuple-element.89.keep, f32[2,1024,256]{2,1,0:T(8,128)S(1)} %collective-permute-done.18.mate, bf16[1040,256]{1,0:T(8,128)(2,1)S(1)} %collective-permute-done.23.refs_0_, ...), custom_call_target="tpu_custom_call" | custom-call | flops 8589934592 | bytes 16777216 | tf_op jit(solution)/shard_map/expand_send/pallas_call | solution.py:462
  368.0 6.2 %collective-permute-start.24 = (bf16[2,1040,256]{2,1,0:T(8,128)(2,1)}, bf16[2,1040,256]{2,1,0:T(8,128)(2,1)S(1)}, u32[]{:S(2)}, u32[]{:S(2)}) collective-permute-start(bf16[2,1040,256]{2,1,0:T(8,128)(2,1)} %get-tuple-element.96), channel_id=1, source_target_pairs={{0,4},{4,0},{8,12},{12,8},{1,5},{5,1},{9,13},{13,9},{2,6},{6,2},{1... | collective-permute-start | bytes 3194888 | tf_op jit(solution)/shard_map/ppermute | solution.py:676
  374.2 5.4 %expand_keep.5.kept = f32[2,1024,256]{2,1,0:T(8,128)} custom-call(s32[1]{0:T(128)} %bitcast.1.place_ref, bf16[1024,512]{1,0:T(8,128)(2,1)} %copy-done.19, bf16[4096,1024]{1,0:T(8,128)(2,1)} %bitcast.20), custom_call_target="tpu_custom_call" | custom-call | flops 8589934592 | bytes 16777216 | tf_op jit(solution)/shard_map/expand_keep/pallas_call | solution.py:495
  382.8 7.3 %expand_send.5 = (bf16[2,1040,256]{2,1,0:T(8,128)(2,1)}, bf16[1024,512]{1,0:T(8,128)(2,1)S(1)}) custom-call(s32[1]{0:T(128)} %bitcast.1.place_ref, f32[2,1024,256]{2,1,0:T(8,128)S(1)} %copy-done.12, f32[2,1024,256]{2,1,0:T(8,128)S(1)} %copy-done.14, bf16[1040,256]{1,0:T(8,128)(2,1)S(1)} %collective-permute-done.22.refs_0_, bf16[4096,1024]{1,0:T(8,128)(2,1)} %bitcast.21), custom_call_target="tpu_custom_call" | custom-call | flops 8589934592 | bytes 16777216 | tf_op jit(solution)/shard_map/expand_send/pallas_call | solution.py:462
  390.1 2.4 send.7
  393.2 5.5 %expand_keep.4.kept = f32[2,1024,256]{2,1,0:T(8,128)} custom-call(s32[1]{0:T(128)} %bitcast.1.place_ref, bf16[1024,512]{1,0:T(8,128)(2,1)} %copy-done.17, bf16[4096,1024]{1,0:T(8,128)(2,1)} %bitcast.22), custom_call_target="tpu_custom_call" | custom-call | flops 8589934592 | bytes 16777216 | tf_op jit(solution)/shard_map/expand_keep/pallas_call | solution.py:495
  398.8 2.2 hop.4
  401.0 5.5 %collective-permute-start.33 = (bf16[1,1040,256]{2,1,0:T(8,128)(2,1)}, bf16[1,1040,256]{2,1,0:T(8,128)(2,1)}, u32[]{:S(2)}, u32[]{:S(2)}) collective-permute-start(bf16[1,1040,256]{2,1,0:T(8,128)(2,1)} %hop.4), channel_id=1, source_target_pairs={{0,8},{4,12},{8,0},{12,4},{1,9},{5,13},{9,1},{13,5},{2,10},{6,14},... | collective-permute-start | bytes 1597448 | tf_op jit(solution)/shard_map/ppermute | solution.py:676
  406.6 2.2 send.5
  409.8 7.7 %expand_send.6 = (bf16[2,1040,256]{2,1,0:T(8,128)(2,1)}, bf16[1024,512]{1,0:T(8,128)(2,1)S(1)}) custom-call(s32[1]{0:T(128)} %bitcast.1.place_ref, f32[2,1024,256]{2,1,0:T(8,128)S(1)} %copy-done.10, f32[2,1024,256]{2,1,0:T(8,128)} %collective-permute-done.25.mate, bf16[1040,256]{1,0:T(8,128)(2,1)} %collective-permute-done.26.refs_0_, bf16[4096,1024]{1,0:T(8,128)(2,1)} %bitcast.23), custom_call_target="tpu_custom_call" | custom-call | flops 8589934592 | bytes 16777216 | tf_op jit(solution)/shard_map/expand_send/pallas_call | solution.py:462
  417.9 15.2 %collective-permute-done.27.refs_0_ = bf16[2,1040,256]{2,1,0:T(8,128)(2,1)} collective-permute-done((bf16[2,1040,256]{2,1,0:T(8,128)(2,1)}, bf16[2,1040,256]{2,1,0:T(8,128)(2,1)}, u32[]{:S(2)}, u32[]{:S(2)}) %collective-permute-start.27) | collective-permute-done | bytes 1064992 | tf_op jit(solution)/shard_map/ppermute | solution.py:676
  433.1 3.3 hop.5
  436.4 3.0 collective-permute-start.32
  439.5 7.5 %expand_send.7 = (bf16[2,1040,256]{2,1,0:T(8,128)(2,1)}, bf16[1024,512]{1,0:T(8,128)(2,1)S(1)}) custom-call(s32[1]{0:T(128)} %bitcast.1.place_ref, f32[2,1024,256]{2,1,0:T(8,128)S(1)} %copy-done.8, f32[2,1024,256]{2,1,0:T(8,128)} %collective-permute-done.19.mate, bf16[1040,256]{1,0:T(8,128)(2,1)S(1)} %collective-permute-done.20.refs_0_, ...), custom_call_target="tpu_custom_call" | custom-call | flops 8589934592 | bytes 16777216 | tf_op jit(solution)/shard_map/expand_send/pallas_call | solution.py:462
  448.0 2.5 collective-permute-start.29
  450.5 5.4 %expand_keep.7.kept = f32[2,1024,256]{2,1,0:T(8,128)} custom-call(s32[1]{0:T(128)} %bitcast.1.place_ref, bf16[1024,512]{1,0:T(8,128)(2,1)} %copy-done.16, bf16[4096,1024]{1,0:T(8,128)(2,1)} %bitcast.25), custom_call_target="tpu_custom_call" | custom-call | flops 8589934592 | bytes 16777216 | tf_op jit(solution)/shard_map/expand_keep/pallas_call | solution.py:495
  455.9 5.3 %expand_keep.6.kept = f32[2,1024,256]{2,1,0:T(8,128)} custom-call(s32[1]{0:T(128)} %bitcast.1.place_ref, bf16[1024,512]{1,0:T(8,128)(2,1)} %copy-done.18, bf16[4096,1024]{1,0:T(8,128)(2,1)} %bitcast.26), custom_call_target="tpu_custom_call" | custom-call | flops 8589934592 | bytes 16777216 | tf_op jit(solution)/shard_map/expand_keep/pallas_call | solution.py:495
  461.2 6.1 %collective-permute-done.28.refs_0_ = bf16[2,1040,256]{2,1,0:T(8,128)(2,1)} collective-permute-done((bf16[2,1040,256]{2,1,0:T(8,128)(2,1)}, bf16[2,1040,256]{2,1,0:T(8,128)(2,1)}, u32[]{:S(2)}, u32[]{:S(2)}) %collective-permute-start.28) | collective-permute-done | bytes 1064992 | tf_op jit(solution)/shard_map/ppermute | solution.py:676
  468.9 2.5 hop.6
  471.4 3.1 collective-permute-start.31
  474.5 26.2 %collective-permute-done.29.refs_0_ = bf16[2,1040,256]{2,1,0:T(8,128)(2,1)} collective-permute-done((bf16[2,1040,256]{2,1,0:T(8,128)(2,1)}, bf16[2,1040,256]{2,1,0:T(8,128)(2,1)}, u32[]{:S(2)}, u32[]{:S(2)}) %collective-permute-start.29) | collective-permute-done | bytes 1064992 | tf_op jit(solution)/shard_map/ppermute | solution.py:676
  500.7 2.5 hop.7
  503.3 3.1 collective-permute-start.30
  506.4 3.3 finish.4.refs_2_
  509.6 3.4 finish.5.refs_2_
  513.1 3.3 finish.6.refs_2_
  516.4 12.9 %collective-permute-done.30.refs_1_ = bf16[1,1040,256]{2,1,0:T(8,128)(2,1)S(1)} collective-permute-done((bf16[1,1040,256]{2,1,0:T(8,128)(2,1)S(1)}, bf16[1,1040,256]{2,1,0:T(8,128)(2,1)S(1)}, u32[]{:S(2)}, u32[]{:S(2)}) %collective-permute-start.30) | collective-permute-done | bytes 532512 | tf_op jit(solution)/shard_map/ppermute | solution.py:676
  529.3 3.3 finish.7
  (93 shorter events, 33.5 us)
Async XLA Ops:
  0.6 49.0 %collective-permute-start = (bf16[1024,1024]{1,0:T(8,128)(2,1)}, bf16[1024,1024]{1,0:T(8,128)(2,1)}, u32[]{:S(2)}, u32[]{:S(2)}) collective-permute-start(bf16[1024,1024]{1,0:T(8,128)(2,1)} %param.8), channel_id=1, source_target_pairs={{0,2},{1,3},{2,0},{3,1},{4,6},{5,7},{6,4},{7,5},{8,10},{9,11},{10,... | collective-permute-start | bytes 6291464 | tf_op jit(solution)/shard_map/ppermute | solution.py:588
  3.6 48.4 %collective-permute-start.3 = (bf16[1024,1024]{1,0:T(8,128)(2,1)}, bf16[1024,1024]{1,0:T(8,128)(2,1)S(1)}, u32[]{:S(2)}, u32[]{:S(2)}) collective-permute-start(bf16[1024,1024]{1,0:T(8,128)(2,1)} %refs_2_.1), channel_id=1, source_target_pairs={{0,4},{4,8},{8,12},{1,5},{5,9},{9,13},{2,6},{6,10},{10,14},{3,7},{... | collective-permute-start | bytes 6291464 | tf_op jit(solution)/shard_map/ppermute | solution.py:605
  7.2 49.0 %collective-permute-start.5 = (bf16[1024,1024]{1,0:T(8,128)(2,1)}, bf16[1024,1024]{1,0:T(8,128)(2,1)}, u32[]{:S(2)}, u32[]{:S(2)}) collective-permute-start(bf16[1024,1024]{1,0:T(8,128)(2,1)} %refs_2_.1), channel_id=1, source_target_pairs={{4,0},{8,4},{12,8},{5,1},{9,5},{13,9},{6,2},{10,6},{14,10},{7,3},{... | collective-permute-start | bytes 6291464 | tf_op jit(solution)/shard_map/ppermute | solution.py:608
  8.5 52.8 %collective-permute-start.1 = (bf16[1024,1024]{1,0:T(8,128)(2,1)}, bf16[1024,1024]{1,0:T(8,128)(2,1)}, u32[]{:S(2)}, u32[]{:S(2)}) collective-permute-start(bf16[1024,1024]{1,0:T(8,128)(2,1)} %param.8), channel_id=1, source_target_pairs={{0,1},{1,0},{2,3},{3,2},{4,5},{5,4},{6,7},{7,6},{8,9},{9,8},{10,11... | collective-permute-start | bytes 6291464 | tf_op jit(solution)/shard_map/ppermute | solution.py:588
  49.6 13.6 %collective-permute-start.2 = (bf16[1024,1024]{1,0:T(8,128)(2,1)}, bf16[1024,1024]{1,0:T(8,128)(2,1)}, u32[]{:S(2)}, u32[]{:S(2)}) collective-permute-start(bf16[1024,1024]{1,0:T(8,128)(2,1)} %collective-permute-done), channel_id=1, source_target_pairs={{0,1},{1,0},{2,3},{3,2},{4,5},{5,4},{6,7},{7,6},{8,9},{9,8},{10,11... | collective-permute-start | bytes 6291464 | tf_op jit(solution)/shard_map/ppermute | solution.py:588
  52.0 13.1 %collective-permute-start.4 = (bf16[1024,1024]{1,0:T(8,128)(2,1)S(1)}, bf16[1024,1024]{1,0:T(8,128)(2,1)}, u32[]{:S(2)}, u32[]{:S(2)}) collective-permute-start(bf16[1024,1024]{1,0:T(8,128)(2,1)S(1)} %collective-permute-done.3.refs_1_), channel_id=1, source_target_pairs={{4,8},{8,12},{5,9},{9,13},{6,10},{10,14},{7,11},{11,15},{20,24},{2... | collective-permute-start | bytes 6291464 | tf_op jit(solution)/shard_map/ppermute | solution.py:605
  56.3 49.4 %collective-permute-start.6 = (bf16[1024,1024]{1,0:T(8,128)(2,1)}, bf16[1024,1024]{1,0:T(8,128)(2,1)}, u32[]{:S(2)}, u32[]{:S(2)}) collective-permute-start(bf16[1024,1024]{1,0:T(8,128)(2,1)} %collective-permute-done.5.refs_3_), channel_id=1, source_target_pairs={{4,0},{8,4},{5,1},{9,5},{6,2},{10,6},{7,3},{11,7},{20,16},{24,20},... | collective-permute-start | bytes 6291464 | tf_op jit(solution)/shard_map/ppermute | solution.py:608
  57.6 1.6 copy-start.23
  65.1 3.3 copy-start.20
  105.7 17.9 %collective-permute-start.7 = (bf16[1024,1024]{1,0:T(8,128)(2,1)}, bf16[1024,1024]{1,0:T(8,128)(2,1)}, u32[]{:S(2)}, u32[]{:S(2)}) collective-permute-start(bf16[1024,1024]{1,0:T(8,128)(2,1)} %collective-permute-done.4.refs_0_), channel_id=1, source_target_pairs={{8,12},{9,13},{10,14},{11,15},{24,28},{25,29},{26,30},{27,31}} | collective-permute-start | bytes 6291464 | tf_op jit(solution)/shard_map/ppermute | solution.py:605
  107.7 47.6 %collective-permute-start.8 = (bf16[1024,1024]{1,0:T(8,128)(2,1)}, bf16[1024,1024]{1,0:T(8,128)(2,1)}, u32[]{:S(2)}, u32[]{:S(2)}) collective-permute-start(bf16[1024,1024]{1,0:T(8,128)(2,1)} %collective-permute-done.6.refs_4_), channel_id=1, source_target_pairs={{4,0},{5,1},{6,2},{7,3},{20,16},{21,17},{22,18},{23,19}} | collective-permute-start | bytes 6291464 | tf_op jit(solution)/shard_map/ppermute | solution.py:608
  155.2 46.6 %collective-permute-start.10 = (bf16[1024,1024]{1,0:T(8,128)(2,1)}, bf16[1024,1024]{1,0:T(8,128)(2,1)}, u32[]{:S(2)}, u32[]{:S(2)}) collective-permute-start(bf16[1024,1024]{1,0:T(8,128)(2,1)} %piece), channel_id=1, source_target_pairs={{4,0},{8,4},{12,8},{5,1},{9,5},{13,9},{6,2},{10,6},{14,10},{7,3},{... | collective-permute-start | bytes 6291464 | tf_op jit(solution)/shard_map/ppermute | solution.py:608
  156.5 46.5 %collective-permute-start.9 = (bf16[1024,1024]{1,0:T(8,128)(2,1)}, bf16[1024,1024]{1,0:T(8,128)(2,1)S(1)}, u32[]{:S(2)}, u32[]{:S(2)}) collective-permute-start(bf16[1024,1024]{1,0:T(8,128)(2,1)} %piece), channel_id=1, source_target_pairs={{0,4},{4,8},{8,12},{1,5},{5,9},{9,13},{2,6},{6,10},{10,14},{3,7},{... | collective-permute-start | bytes 6291464 | tf_op jit(solution)/shard_map/ppermute | solution.py:605
  203.0 1.4 copy-start.22
  204.4 16.8 %collective-permute-start.11 = (bf16[1040,1024]{1,0:T(8,128)(2,1)}, bf16[1040,1024]{1,0:T(8,128)(2,1)S(1)}, u32[]{:S(2)}, u32[]{:S(2)}) collective-permute-start(bf16[1040,1024]{1,0:T(8,128)(2,1)} %get-tuple-element.68), channel_id=1, source_target_pairs={{0,1},{1,0},{2,3},{3,2},{4,5},{5,4},{6,7},{7,6},{8,9},{9,8},{10,11... | collective-permute-start | bytes 6389768 | tf_op jit(solution)/shard_map/ppermute | solution.py:588
  204.4 49.1 %collective-permute-start.12 = (bf16[1040,1024]{1,0:T(8,128)(2,1)}, bf16[1040,1024]{1,0:T(8,128)(2,1)}, u32[]{:S(2)}, u32[]{:S(2)}) collective-permute-start(bf16[1040,1024]{1,0:T(8,128)(2,1)} %get-tuple-element.68), channel_id=1, source_target_pairs={{0,2},{1,3},{2,0},{3,1},{4,6},{5,7},{6,4},{7,5},{8,10},{9,11},{10,... | collective-permute-start | bytes 6389768 | tf_op jit(solution)/shard_map/ppermute | solution.py:588
  204.9 50.6 %collective-permute-start.14 = (bf16[1024,1024]{1,0:T(8,128)(2,1)}, bf16[1024,1024]{1,0:T(8,128)(2,1)}, u32[]{:S(2)}, u32[]{:S(2)}) collective-permute-start(bf16[1024,1024]{1,0:T(8,128)(2,1)} %collective-permute-done.10.piece), channel_id=1, source_target_pairs={{4,0},{8,4},{5,1},{9,5},{6,2},{10,6},{7,3},{11,7},{20,16},{24,20},... | collective-permute-start | bytes 6291464 | tf_op jit(solution)/shard_map/ppermute | solution.py:608
  206.2 50.6 %collective-permute-start.15 = (bf16[1024,1024]{1,0:T(8,128)(2,1)}, bf16[1024,1024]{1,0:T(8,128)(2,1)}, u32[]{:S(2)}, u32[]{:S(2)}) collective-permute-start(bf16[1024,1024]{1,0:T(8,128)(2,1)} %copy-done.22), channel_id=1, source_target_pairs={{4,8},{8,12},{5,9},{9,13},{6,10},{10,14},{7,11},{11,15},{20,24},{2... | collective-permute-start | bytes 6291464 | tf_op jit(solution)/shard_map/ppermute | solution.py:605
  221.2 1.3 copy-start.21
  253.5 20.2 %collective-permute-start.13 = (bf16[1040,1024]{1,0:T(8,128)(2,1)}, bf16[1040,1024]{1,0:T(8,128)(2,1)}, u32[]{:S(2)}, u32[]{:S(2)}) collective-permute-start(bf16[1040,1024]{1,0:T(8,128)(2,1)} %collective-permute-done.12.message.scales), channel_id=1, source_target_pairs={{0,1},{1,0},{2,3},{3,2},{4,5},{5,4},{6,7},{7,6},{8,9},{9,8},{10,11... | collective-permute-start | bytes 6389768 | tf_op jit(solution)/shard_map/ppermute | solution.py:588
  255.5 49.4 %collective-permute-start.16 = (bf16[1024,1024]{1,0:T(8,128)(2,1)}, bf16[1024,1024]{1,0:T(8,128)(2,1)S(1)}, u32[]{:S(2)}, u32[]{:S(2)}) collective-permute-start(bf16[1024,1024]{1,0:T(8,128)(2,1)} %collective-permute-done.14.piece), channel_id=1, source_target_pairs={{4,0},{5,1},{6,2},{7,3},{20,16},{21,17},{22,18},{23,19}} | collective-permute-start | bytes 6291464 | tf_op jit(solution)/shard_map/ppermute | solution.py:608
  256.8 48.1 %collective-permute-start.17 = (bf16[1024,1024]{1,0:T(8,128)(2,1)}, bf16[1024,1024]{1,0:T(8,128)(2,1)}, u32[]{:S(2)}, u32[]{:S(2)}) collective-permute-start(bf16[1024,1024]{1,0:T(8,128)(2,1)} %collective-permute-done.15.piece), channel_id=1, source_target_pairs={{8,12},{9,13},{10,14},{11,15},{24,28},{25,29},{26,30},{27,31}} | collective-permute-start | bytes 6291464 | tf_op jit(solution)/shard_map/ppermute | solution.py:605
  301.2 2.0 copy-start.6
  320.2 2.0 copy-start.15
  334.9 7.2 %copy-start.11 = (f32[2,1024,256]{2,1,0:T(8,128)}, f32[2,1024,256]{2,1,0:T(8,128)S(1)}, u32[]{:S(2)}) copy-start(f32[2,1024,256]{2,1,0:T(8,128)S(1)} %get-tuple-element.94.keep) | copy-start | bytes 6291460
  334.9 4.2 collective-permute-start.18
  335.0 7.1 %collective-permute-start.21 = (f32[2,1024,256]{2,1,0:T(8,128)S(1)}, f32[2,1024,256]{2,1,0:T(8,128)S(1)}, u32[]{:S(2)}, u32[]{:S(2)}) collective-permute-start(f32[2,1024,256]{2,1,0:T(8,128)S(1)} %get-tuple-element.95), channel_id=1, source_target_pairs={{0,1},{1,0},{2,3},{3,2},{4,5},{5,4},{6,7},{7,6},{8,9},{9,8},{10,11... | collective-permute-start | bytes 6291464 | tf_op jit(solution)/shard_map/ppermute | solution.py:588
  340.0 18.9 %collective-permute-start.23 = (bf16[1040,256]{1,0:T(8,128)(2,1)S(1)}, bf16[1040,256]{1,0:T(8,128)(2,1)S(1)}, u32[]{:S(2)}, u32[]{:S(2)}) collective-permute-start(bf16[1040,256]{1,0:T(8,128)(2,1)S(1)} %send.4), channel_id=1, source_target_pairs={{0,2},{1,3},{2,0},{3,1},{4,6},{5,7},{6,4},{7,5},{8,10},{9,11},{10,... | collective-permute-start | bytes 1597448 | tf_op jit(solution)/shard_map/ppermute | solution.py:588
  342.1 1.3 copy-start.13
  343.4 30.8 %collective-permute-start.22 = (bf16[1040,256]{1,0:T(8,128)(2,1)S(1)}, bf16[1040,256]{1,0:T(8,128)(2,1)S(1)}, u32[]{:S(2)}, u32[]{:S(2)}) collective-permute-start(bf16[1040,256]{1,0:T(8,128)(2,1)S(1)} %send.6), channel_id=1, source_target_pairs={{0,2},{1,3},{2,0},{3,1},{4,6},{5,7},{6,4},{7,5},{8,10},{9,11},{10,... | collective-permute-start | bytes 1597448 | tf_op jit(solution)/shard_map/ppermute | solution.py:588
  358.2 8.8 %copy-start.7 = (f32[2,1024,256]{2,1,0:T(8,128)}, f32[2,1024,256]{2,1,0:T(8,128)S(1)}, u32[]{:S(2)}) copy-start(f32[2,1024,256]{2,1,0:T(8,128)S(1)} %get-tuple-element.92.keep) | copy-start | bytes 6291460
  358.2 31.9 %copy-start.9 = (f32[2,1024,256]{2,1,0:T(8,128)}, f32[2,1024,256]{2,1,0:T(8,128)S(1)}, u32[]{:S(2)}) copy-start(f32[2,1024,256]{2,1,0:T(8,128)S(1)} %get-tuple-element.103.keep) | copy-start | bytes 6291460
  358.3 31.9 %collective-permute-start.25 = (f32[2,1024,256]{2,1,0:T(8,128)}, f32[2,1024,256]{2,1,0:T(8,128)}, u32[]{:S(2)}, u32[]{:S(2)}) collective-permute-start(f32[2,1024,256]{2,1,0:T(8,128)} %get-tuple-element.104), channel_id=1, source_target_pairs={{0,1},{1,0},{2,3},{3,2},{4,5},{5,4},{6,7},{7,6},{8,9},{9,8},{10,11... | collective-permute-start | bytes 6291464 | tf_op jit(solution)/shard_map/ppermute | solution.py:588
  358.3 48.2 %collective-permute-start.19 = (f32[2,1024,256]{2,1,0:T(8,128)}, f32[2,1024,256]{2,1,0:T(8,128)}, u32[]{:S(2)}, u32[]{:S(2)}) collective-permute-start(f32[2,1024,256]{2,1,0:T(8,128)} %get-tuple-element.93), channel_id=1, source_target_pairs={{0,1},{1,0},{2,3},{3,2},{4,5},{5,4},{6,7},{7,6},{8,9},{9,8},{10,11... | collective-permute-start | bytes 6291464 | tf_op jit(solution)/shard_map/ppermute | solution.py:588
  367.0 1.0 copy-start.19
  368.0 30.8 %collective-permute-start.24 = (bf16[2,1040,256]{2,1,0:T(8,128)(2,1)}, bf16[2,1040,256]{2,1,0:T(8,128)(2,1)S(1)}, u32[]{:S(2)}, u32[]{:S(2)}) collective-permute-start(bf16[2,1040,256]{2,1,0:T(8,128)(2,1)} %get-tuple-element.96), channel_id=1, source_target_pairs={{0,4},{4,0},{8,12},{12,8},{1,5},{5,1},{9,13},{13,9},{2,6},{6,2},{1... | collective-permute-start | bytes 3194888 | tf_op jit(solution)/shard_map/ppermute | solution.py:676
  379.6 1.6 copy-start.12
  381.2 1.6 copy-start.14
  390.1 2.4 copy-start.17
  390.1 43.0 %collective-permute-start.27 = (bf16[2,1040,256]{2,1,0:T(8,128)(2,1)}, bf16[2,1040,256]{2,1,0:T(8,128)(2,1)}, u32[]{:S(2)}, u32[]{:S(2)}) collective-permute-start(bf16[2,1040,256]{2,1,0:T(8,128)(2,1)} %get-tuple-element.100), channel_id=1, source_target_pairs={{0,4},{4,0},{8,12},{12,8},{1,5},{5,1},{9,13},{13,9},{2,6},{6,2},{1... | collective-permute-start | bytes 3194888 | tf_op jit(solution)/shard_map/ppermute | solution.py:676
  392.6 17.2 %collective-permute-start.26 = (bf16[1040,256]{1,0:T(8,128)(2,1)S(1)}, bf16[1040,256]{1,0:T(8,128)(2,1)}, u32[]{:S(2)}, u32[]{:S(2)}) collective-permute-start(bf16[1040,256]{1,0:T(8,128)(2,1)S(1)} %send.7), channel_id=1, source_target_pairs={{0,2},{1,3},{2,0},{3,1},{4,6},{5,7},{6,4},{7,5},{8,10},{9,11},{10,... | collective-permute-start | bytes 1597448 | tf_op jit(solution)/shard_map/ppermute | solution.py:588
  393.2 5.6 %copy-start = (f32[2,1024,256]{2,1,0:T(8,128)S(1)}, f32[2,1024,256]{2,1,0:T(8,128)}, u32[]{:S(2)}) copy-start(f32[2,1024,256]{2,1,0:T(8,128)} %expand_keep.5.kept) | copy-start | bytes 6291460
  398.7 7.9 %copy-start.8 = (f32[2,1024,256]{2,1,0:T(8,128)S(1)}, f32[2,1024,256]{2,1,0:T(8,128)}, u32[]{:S(2)}) copy-start(f32[2,1024,256]{2,1,0:T(8,128)} %copy-done.7) | copy-start | bytes 6291460
  401.0 105.3 %collective-permute-start.33 = (bf16[1,1040,256]{2,1,0:T(8,128)(2,1)}, bf16[1,1040,256]{2,1,0:T(8,128)(2,1)}, u32[]{:S(2)}, u32[]{:S(2)}) collective-permute-start(bf16[1,1040,256]{2,1,0:T(8,128)(2,1)} %hop.4), channel_id=1, source_target_pairs={{0,8},{4,12},{8,0},{12,4},{1,9},{5,13},{9,1},{13,5},{2,10},{6,14},... | collective-permute-start | bytes 1597448 | tf_op jit(solution)/shard_map/ppermute | solution.py:676
  406.6 3.2 copy-start.10
  408.7 24.4 %copy-start.1 = (f32[2,1024,256]{2,1,0:T(8,128)S(1)}, f32[2,1024,256]{2,1,0:T(8,128)}, u32[]{:S(2)}) copy-start(f32[2,1024,256]{2,1,0:T(8,128)} %expand_keep.4.kept) | copy-start | bytes 6291460
  408.8 30.7 %collective-permute-start.20 = (bf16[1040,256]{1,0:T(8,128)(2,1)S(1)}, bf16[1040,256]{1,0:T(8,128)(2,1)S(1)}, u32[]{:S(2)}, u32[]{:S(2)}) collective-permute-start(bf16[1040,256]{1,0:T(8,128)(2,1)S(1)} %send.5), channel_id=1, source_target_pairs={{0,2},{1,3},{2,0},{3,1},{4,6},{5,7},{6,4},{7,5},{8,10},{9,11},{10,... | collective-permute-start | bytes 1597448 | tf_op jit(solution)/shard_map/ppermute | solution.py:588
  417.5 18.9 %copy-start.16 = (bf16[1024,512]{1,0:T(8,128)(2,1)}, bf16[1024,512]{1,0:T(8,128)(2,1)S(1)}, u32[]{:S(2)}) copy-start(bf16[1024,512]{1,0:T(8,128)(2,1)S(1)} %get-tuple-element.110.both) | copy-start | bytes 3145732
  417.5 49.8 %collective-permute-start.28 = (bf16[2,1040,256]{2,1,0:T(8,128)(2,1)}, bf16[2,1040,256]{2,1,0:T(8,128)(2,1)}, u32[]{:S(2)}, u32[]{:S(2)}) collective-permute-start(bf16[2,1040,256]{2,1,0:T(8,128)(2,1)} %get-tuple-element.106), channel_id=1, source_target_pairs={{0,4},{4,0},{8,12},{12,8},{1,5},{5,1},{9,13},{13,9},{2,6},{6,2},{1... | collective-permute-start | bytes 3194888 | tf_op jit(solution)/shard_map/ppermute | solution.py:676
  436.4 73.2 %collective-permute-start.32 = (bf16[1,1040,256]{2,1,0:T(8,128)(2,1)}, bf16[1,1040,256]{2,1,0:T(8,128)(2,1)S(1)}, u32[]{:S(2)}, u32[]{:S(2)}) collective-permute-start(bf16[1,1040,256]{2,1,0:T(8,128)(2,1)} %hop.5), channel_id=1, source_target_pairs={{0,8},{4,12},{8,0},{12,4},{1,9},{5,13},{9,1},{13,5},{2,10},{6,14},... | collective-permute-start | bytes 1597448 | tf_op jit(solution)/shard_map/ppermute | solution.py:676
  447.0 1.0 copy-start.18
  448.0 52.7 %collective-permute-start.29 = (bf16[2,1040,256]{2,1,0:T(8,128)(2,1)}, bf16[2,1040,256]{2,1,0:T(8,128)(2,1)}, u32[]{:S(2)}, u32[]{:S(2)}) collective-permute-start(bf16[2,1040,256]{2,1,0:T(8,128)(2,1)} %get-tuple-element.112), channel_id=1, source_target_pairs={{0,4},{4,0},{8,12},{12,8},{1,5},{5,1},{9,13},{13,9},{2,6},{6,2},{1... | collective-permute-start | bytes 3194888 | tf_op jit(solution)/shard_map/ppermute | solution.py:676
  461.2 39.5 %copy-start.3 = (f32[2,1024,256]{2,1,0:T(8,128)S(1)}, f32[2,1024,256]{2,1,0:T(8,128)}, u32[]{:S(2)}) copy-start(f32[2,1024,256]{2,1,0:T(8,128)} %expand_keep.6.kept) | copy-start | bytes 6291460
  467.3 1.6 copy-start.4
  471.4 41.6 %collective-permute-start.31 = (bf16[1,1040,256]{2,1,0:T(8,128)(2,1)S(1)}, bf16[1,1040,256]{2,1,0:T(8,128)(2,1)S(1)}, u32[]{:S(2)}, u32[]{:S(2)}) collective-permute-start(bf16[1,1040,256]{2,1,0:T(8,128)(2,1)S(1)} %hop.6), channel_id=1, source_target_pairs={{0,8},{4,12},{8,0},{12,4},{1,9},{5,13},{9,1},{13,5},{2,10},{6,14},... | collective-permute-start | bytes 1597448 | tf_op jit(solution)/shard_map/ppermute | solution.py:676
  503.2 6.4 %copy-start.2 = (f32[2,1024,256]{2,1,0:T(8,128)S(1)}, f32[2,1024,256]{2,1,0:T(8,128)}, u32[]{:S(2)}) copy-start(f32[2,1024,256]{2,1,0:T(8,128)} %expand_keep.4.kept) | copy-start | bytes 6291460
  503.3 26.0 %collective-permute-start.30 = (bf16[1,1040,256]{2,1,0:T(8,128)(2,1)S(1)}, bf16[1,1040,256]{2,1,0:T(8,128)(2,1)S(1)}, u32[]{:S(2)}, u32[]{:S(2)}) collective-permute-start(bf16[1,1040,256]{2,1,0:T(8,128)(2,1)S(1)} %hop.7), channel_id=1, source_target_pairs={{0,8},{4,12},{8,0},{12,4},{1,9},{5,13},{9,1},{13,5},{2,10},{6,14},... | collective-permute-start | bytes 1597448 | tf_op jit(solution)/shard_map/ppermute | solution.py:676
  509.6 3.4 copy-start.5

commit v15 on v14

--- a/solution.py
+++ b/solution.py
@@ -636,16 +636,30 @@
             walk(grads, step)
         before = halfway(spot, left, grads, near, lines, None)
 
+        inner = after(right_basis, grads[1 - far], grads[far - 1])
         own, before, grads[-far], grads[far] = barrier(
             (right_basis, before, grads[-far], grads[far])
         )
-        rights = {0: own}
+        rights = {0: right_basis}
+        inner_up, inner_down, end_up, end_down = inner, inner, own, own
         for step in range(1, lines):
-            walk(rights, step)
+            from_up = up(end_up, [lines - 2])
+            from_down = down(end_down, [1])
+            if step < far:
+                inner_up = up(inner_up, range(step - 1, lines - 2))
+                inner_down = down(inner_down, range(2, lines - step + 1))
+                end_up = after(inner_up, own) if step == 1 else inner_up
+                end_down = after(inner_down, own) if step == 1 else inner_down
+                rights[-step] = jnp.where(place == far, from_up, inner_up)
+                rights[step] = jnp.where(place == 0, from_down, inner_down)
+                if step == 1:
+                    first_blocks = inner_up, inner_down
+            else:
+                rights[-step], rights[step] = from_up, from_down
         above, below = rights[far], rights[-far]
 
         pair, message = pack(halfway(spot, left, grads, [-far, far], lines, before))
-        message, rights[-1], rights[1] = barrier((message, rights[-1], rights[1]))
+        message = after(message, *first_blocks)
         aligned = depth == width
 
         def put_block(held, offset):

time: 534 us -> 536 us (level)
  other arithmetic: 0.08 us -> 12.6 us
  starting transfers between devices: 57.2 us -> 48.6 us
    ppermute x14, waiting for transfers between devices: 70.1 us -> 47.8 us  [swap(): return lax.ppermute(value, 'col', [(i, i ^ distance) for i in range(cols)])]
    ppermute x8, starting transfers between devices: 23.9 us -> 6.06 us  [cross(): return lax.ppermute(value, 'row', [(i, i ^ distance) for i in range(lines)])]
    select_n x0 -> x4, other arithmetic: none -> 12.5 us  [the longest x2 6.26 us: local(): rights[-step] = jnp.where(place == far, from_up, inner_up)]
    ppermute x8, waiting for transfers between devices: 60.6 us -> 73 us  [cross(): return lax.ppermute(value, 'row', [(i, i ^ distance) for i in range(lines)])]
    ppermute x6 -> x8, waiting for transfers between devices: 98 us -> 110 us  [down(): return lax.ppermute(value, 'row', [(i, i - 1) for i in senders])]
    ppermute x6 -> x8, starting transfers between devices: 16.2 us -> 22.6 us  [up(): return lax.ppermute(value, 'row', [(i, i + 1) for i in senders])]
    ppermute x6 -> x8, starting transfers between devices: 7.69 us -> 11.7 us  [down(): return lax.ppermute(value, 'row', [(i, i - 1) for i in senders])]
    unnamed x48 -> x46, local copies, waits for them, and re-layouts: 17.8 us -> 15.1 us
  transfers between devices with their start and end apart: 34 -> 38, of which waited for: 17 -> 14; matrix products, arithmetic and copies ran while one was open for 1% -> 4% of each run, Pallas kernels for 34% -> 34%
where the time goes in v15:
time: 536 us; the launch traced here: 535 us
  waiting for transfers between devices  233 us (43%)
  Pallas kernels  217 us (40%)
  starting transfers between devices  48.6 us (9%)
  local copies, waits for them, and re-layouts  22 us (4%)
  other arithmetic  12.6 us (2%)
    ppermute x8, waiting for transfers between devices, down(): return lax.ppermute(value, 'row', [(i, i - 1) for i in senders])  110 us
    ppermute x8, waiting for transfers between devices, cross(): return lax.ppermute(value, 'row', [(i, i ^ distance) for i in range(lines)])  73 us
    ppermute x14, waiting for transfers between devices, swap(): return lax.ppermute(value, 'col', [(i, i ^ distance) for i in range(cols)])  47.8 us
    pallas_call x4, Pallas kernels, expand_send(): pl.pallas_call(functools.partial(expand_send_kernel, tile=min(64, depth))...  30.7 us
    pallas_call x2, Pallas kernels, restore(): pl.pallas_call(functools.partial(restore_kernel, cols=cols), grid_spec=pl...  26 us
    pallas_call x2, Pallas kernels, halfway(): pl.pallas_call(functools.partial(halfway_kernel, offsets=offsets, lines=l...  24.3 us
    ppermute x8, starting transfers between devices, up(): return lax.ppermute(value, 'row', [(i, i + 1) for i in senders])  22.6 us
    pallas_call x5, Pallas kernels, put(): pl.pallas_call(put_kernel, grid_spec=pltpu.PrefetchScalarGridSpec(num_sca...  21.7 us
  transfers between devices with their start and end apart: 38, of which 14 were waited for; matrix products, arithmetic and copies ran while one was open for 4% of the time, Pallas kernels for 34%

profile of v15, /device:TPU:0, one launch (start us, length us, event | category | flops | bytes accessed | tf_op | source)
XLA Modules:
  0.0 535.0 jit_solution(9534325467792044243)
XLA Ops:
  0.6 3.0 collective-permute-start
  3.6 3.6 collective-permute-start.3
  8.6 41.0 %collective-permute-done = bf16[1024,1024]{1,0:T(8,128)(2,1)} collective-permute-done((bf16[1024,1024]{1,0:T(8,128)(2,1)}, bf16[1024,1024]{1,0:T(8,128)(2,1)}, u32[]{:S(2)}, u32[]{:S(2)}) %collective-permute-start) | collective-permute-done | bytes 2097184 | tf_op jit(solution)/shard_map/ppermute | solution.py:588
  49.6 2.4 collective-permute-done.3.refs_1_
  52.0 2.0 collective-permute-start.4
  54.0 2.3 collective-permute-done.5.refs_3_
  65.1 3.3 copy-done.20
  68.4 37.2 %collective-permute-done.6.refs_4_ = bf16[1024,1024]{1,0:T(8,128)(2,1)} collective-permute-done((bf16[1024,1024]{1,0:T(8,128)(2,1)}, bf16[1024,1024]{1,0:T(8,128)(2,1)}, u32[]{:S(2)}, u32[]{:S(2)}) %collective-permute-start.6) | collective-permute-done | bytes 2097184 | tf_op jit(solution)/shard_map/ppermute | solution.py:608
  105.6 2.0 collective-permute-start.7
  108.9 7.2 %collective-permute-start.9 = (bf16[1024,1024]{1,0:T(8,128)(2,1)}, bf16[1024,1024]{1,0:T(8,128)(2,1)}, u32[]{:S(2)}, u32[]{:S(2)}) collective-permute-start(bf16[1024,1024]{1,0:T(8,128)(2,1)} %piece.1), channel_id=1, source_target_pairs={{0,4},{4,8},{1,5},{5,9},{2,6},{6,10},{3,7},{7,11},{16,20},{20,24},... | collective-permute-start | bytes 6291464 | tf_op jit(solution)/shard_map/ppermute | solution.py:605
  116.1 2.0 collective-permute-start.10
  118.1 14.7 %halfway.2.refs_2_ = f32[1024,1024]{1,0:T(8,128)} custom-call(s32[1]{0:T(128)} %bitcast.1.place_ref, bf16[4096,1024]{1,0:T(8,128)(2,1)} %bitcast.17, bf16[1024,1024]{1,0:T(8,128)(2,1)} %collective-permute-done.4.refs_0_, bf16[1024,1024]{1,0:T(8,128)(2,1)S(1)} %collective-permute-done.3.refs_1_, bf16[1024,1024]{1,0:T(8,128)(2,1)} %refs_2_.1, ...), custom_call_target="tpu_custom_call" | custom-call | flops 2576980480 | bytes 2516582 | tf_op jit(solution)/shard_map/halfway/pallas_call | solution.py:114
  132.8 22.4 %collective-permute-done.8.refs_1_ = bf16[1024,1024]{1,0:T(8,128)(2,1)} collective-permute-done((bf16[1024,1024]{1,0:T(8,128)(2,1)}, bf16[1024,1024]{1,0:T(8,128)(2,1)}, u32[]{:S(2)}, u32[]{:S(2)}) %collective-permute-start.8) | collective-permute-done | bytes 2097184 | tf_op jit(solution)/shard_map/ppermute | solution.py:608
  155.2 2.0 collective-permute-start.14
  158.4 9.6 %halfway.3.value = f32[1024,1024]{1,0:T(8,128)} custom-call(s32[1]{0:T(128)} %bitcast.1.place_ref, bf16[4096,1024]{1,0:T(8,128)(2,1)} %bitcast.18, bf16[1024,1024]{1,0:T(8,128)(2,1)} %collective-permute-done.7.refs_0_, bf16[1024,1024]{1,0:T(8,128)(2,1)} %collective-permute-done.8.refs_1_, f32[1024,1024]{1,0:T(8,128)} %halfway.2.refs_2_), custom_call_target="tpu_custom_call" | custom-call | flops 2576980480 | bytes 2516582 | tf_op jit(solution)/shard_map/halfway/pallas_call | solution.py:114
  168.0 7.9 %pack.1 = (bf16[2,1024,1024]{2,1,0:T(8,128)(2,1)}, bf16[1040,1024]{1,0:T(8,128)(2,1)}) custom-call(f32[1024,1024]{1,0:T(8,128)} %halfway.3.value), custom_call_target="tpu_custom_call" | custom-call | flops 125829120 | bytes 3145728 | tf_op jit(solution)/shard_map/pack/pallas_call | solution.py:147
  176.6 2.0 collective-permute-start.17
  178.6 2.0 collective-permute-start.19
  180.6 4.4 put.5
  184.9 18.8 %collective-permute-done.13 = bf16[1024,1024]{1,0:T(8,128)(2,1)} collective-permute-done((bf16[1024,1024]{1,0:T(8,128)(2,1)}, bf16[1024,1024]{1,0:T(8,128)(2,1)}, u32[]{:S(2)}, u32[]{:S(2)}) %collective-permute-start.13) | collective-permute-done | bytes 2097184 | tf_op jit(solution)/shard_map/ppermute | solution.py:608
  203.8 2.0 collective-permute-start.18
  205.8 3.1 broadcast_select_fusion.1.piece
  208.9 4.3 put.6
  214.5 3.1 broadcast_select_fusion.3.piece
  217.6 4.3 put.7
  221.9 6.1 %unpack.3.refs_1_ = bf16[2,1024,1024]{2,1,0:T(8,128)(2,1)} custom-call(bf16[1040,1024]{1,0:T(8,128)(2,1)} %copy-done.21, bf16[1040,1024]{1,0:T(8,128)(2,1)} %copy-done.21), custom_call_target="tpu_custom_call" | custom-call | flops 125829120 | bytes 1887436 | tf_op jit(solution)/shard_map/unpack/pallas_call | solution.py:176
  229.3 2.0 collective-permute-start.21
  231.4 3.1 broadcast_select_fusion.piece
  234.5 29.4 %collective-permute-done.16 = bf16[1024,1024]{1,0:T(8,128)(2,1)} collective-permute-done((bf16[1024,1024]{1,0:T(8,128)(2,1)}, bf16[1024,1024]{1,0:T(8,128)(2,1)}, u32[]{:S(2)}, u32[]{:S(2)}) %collective-permute-start.16) | collective-permute-done | bytes 2097184 | tf_op jit(solution)/shard_map/ppermute | solution.py:608
  264.0 3.1 broadcast_select_fusion.2.piece
  267.1 4.3 put.8
  271.4 4.3 put.9
  275.8 6.1 %unpack.4.refs_2_ = bf16[2,1024,1024]{2,1,0:T(8,128)(2,1)} custom-call(bf16[1040,1024]{1,0:T(8,128)(2,1)} %collective-permute-done.12.message.scales, bf16[1040,1024]{1,0:T(8,128)(2,1)} %collective-permute-done.12.message.scales), custom_call_target="tpu_custom_call" | custom-call | flops 125829120 | bytes 1887436 | tf_op jit(solution)/shard_map/unpack/pallas_call | solution.py:176
  281.9 6.1 %unpack.5.refs_3_ = bf16[2,1024,1024]{2,1,0:T(8,128)(2,1)} custom-call(bf16[1040,1024]{1,0:T(8,128)(2,1)} %collective-permute-done.15.message.scales, bf16[1040,1024]{1,0:T(8,128)(2,1)} %collective-permute-done.15.message.scales), custom_call_target="tpu_custom_call" | custom-call | flops 125829120 | bytes 1887436 | tf_op jit(solution)/shard_map/unpack/pallas_call | solution.py:176
  288.0 21.4 %rotate_part.1.part = f32[1024,1024]{1,0:T(8,128)S(1)} custom-call(s32[3]{0:T(128)S(1)} %pad_add_fusion.at_ref, bf16[2,1024,1024]{2,1,0:T(8,128)(2,1)} %get-tuple-element.66.refs_0_, bf16[2,1024,1024]{2,1,0:T(8,128)(2,1)} %unpack.3.refs_1_, bf16[2,1024,1024]{2,1,0:T(8,128)(2,1)} %unpack.4.refs_2_, bf16[2,1024,1024]{2,1,0:T(8,128)(2,1)} %unpack.5.refs_3_, ...), custom_call_target="tpu_custom_call" | custom-call | flops 5153960960 | bytes 6291456 | tf_op jit(solution)/shard_map/rotate_part/pallas_call | solution.py:244
  309.4 2.0 copy-done.6
  311.4 15.3 %rotate.1 = (f32[1024,1024]{1,0:T(8,128)}, f32[1024,1024]{1,0:T(8,128)}, bf16[2,1024,1024]{2,1,0:T(8,128)(2,1)S(1)}, bf16[5,1024,1024]{2,1,0:T(8,128)(2,1)}) custom-call(s32[3]{0:T(128)S(1)} %pad_add_fusion.at_ref, f32[1024,1024]{1,0:T(8,128)} %copy-done.6, bf16[1024,1024]{1,0:T(8,128)(2,1)S(1)} %collective-permute-done.20.above, ...), custom_call_target="tpu_custom_call", output_to_operand_aliasing={{3}: (10, {})} | custom-call | flops 17179869184 | bytes 125829120 | tf_op jit(solution)/shard_map/rotate/pallas_call | solution.py:322
  326.7 2.0 copy-done.15
  328.7 12.7 %restore.2 = (f32[2,1024,256]{2,1,0:T(8,128)S(1)}, f32[2,1024,256]{2,1,0:T(8,128)S(1)}, f32[2,1024,256]{2,1,0:T(8,128)S(1)}, f32[2,1024,256]{2,1,0:T(8,128)S(1)}) custom-call(s32[1]{0:T(128)} %bitcast.me_ref, bf16[2,1024,1024]{2,1,0:T(8,128)(2,1)} %copy-done.15, bf16[5,1024,1024]{2,1,0:T(8,128)(2,1)} %get-tuple-element.90.refs_0_.refs_1_.refs_2_.refs_3_, ...), custom_call_target="tpu_custom_call" | custom-call | flops 34359738368 | bytes 67108864 | tf_op jit(solution)/shard_map/restore/pallas_call | solution.py:380
  341.9 3.6 collective-permute-done.22.mate
  350.4 13.3 %restore.3 = (f32[2,1024,256]{2,1,0:T(8,128)S(1)}, f32[2,1024,256]{2,1,0:T(8,128)}, f32[2,1024,256]{2,1,0:T(8,128)S(1)}, f32[2,1024,256]{2,1,0:T(8,128)}) custom-call(s32[1]{0:T(128)} %bitcast.me_ref, bf16[2,1024,1024]{2,1,0:T(8,128)(2,1)} %copy-done.15, bf16[5,1024,1024]{2,1,0:T(8,128)(2,1)} %get-tuple-element.90.refs_0_.refs_1_.refs_2_.refs_3_, ...), custom_call_target="tpu_custom_call" | custom-call | flops 34359738368 | bytes 67108864 | tf_op jit(solution)/shard_map/restore/pallas_call | solution.py:380
  364.3 8.2 %expand_send.4 = (bf16[2,1040,256]{2,1,0:T(8,128)(2,1)}, bf16[1024,512]{1,0:T(8,128)(2,1)S(1)}) custom-call(s32[1]{0:T(128)} %bitcast.1.place_ref, f32[2,1024,256]{2,1,0:T(8,128)S(1)} %get-tuple-element.91.keep, f32[2,1024,256]{2,1,0:T(8,128)S(1)} %collective-permute-done.22.mate, bf16[1040,256]{1,0:T(8,128)(2,1)S(1)} %collective-permute-done.27.refs_0_, ...), custom_call_target="tpu_custom_call" | custom-call | flops 8589934592 | bytes 16777216 | tf_op jit(solution)/shard_map/expand_send/pallas_call | solution.py:462
  373.5 4.5 collective-permute-start.28
  378.0 5.4 %expand_keep.5.kept = f32[2,1024,256]{2,1,0:T(8,128)} custom-call(s32[1]{0:T(128)} %bitcast.1.place_ref, bf16[1024,512]{1,0:T(8,128)(2,1)} %copy-done.19, bf16[4096,1024]{1,0:T(8,128)(2,1)} %bitcast.20), custom_call_target="tpu_custom_call" | custom-call | flops 8589934592 | bytes 16777216 | tf_op jit(solution)/shard_map/expand_keep/pallas_call | solution.py:495
  386.6 7.3 %expand_send.5 = (bf16[2,1040,256]{2,1,0:T(8,128)(2,1)}, bf16[1024,512]{1,0:T(8,128)(2,1)S(1)}) custom-call(s32[1]{0:T(128)} %bitcast.1.place_ref, f32[2,1024,256]{2,1,0:T(8,128)S(1)} %copy-done.12, f32[2,1024,256]{2,1,0:T(8,128)S(1)} %copy-done.14, bf16[1040,256]{1,0:T(8,128)(2,1)S(1)} %collective-permute-done.26.refs_0_, bf16[4096,1024]{1,0:T(8,128)(2,1)} %bitcast.21), custom_call_target="tpu_custom_call" | custom-call | flops 8589934592 | bytes 16777216 | tf_op jit(solution)/shard_map/expand_send/pallas_call | solution.py:462
  394.0 2.4 send.7
  398.0 5.5 %expand_keep.4.kept = f32[2,1024,256]{2,1,0:T(8,128)} custom-call(s32[1]{0:T(128)} %bitcast.1.place_ref, bf16[1024,512]{1,0:T(8,128)(2,1)} %copy-done.17, bf16[4096,1024]{1,0:T(8,128)(2,1)} %bitcast.22), custom_call_target="tpu_custom_call" | custom-call | flops 8589934592 | bytes 16777216 | tf_op jit(solution)/shard_map/expand_keep/pallas_call | solution.py:495
  403.5 2.3 hop.4
  405.7 2.2 send.5
  410.2 7.7 %expand_send.6 = (bf16[2,1040,256]{2,1,0:T(8,128)(2,1)}, bf16[1024,512]{1,0:T(8,128)(2,1)S(1)}) custom-call(s32[1]{0:T(128)} %bitcast.1.place_ref, f32[2,1024,256]{2,1,0:T(8,128)S(1)} %copy-done.10, f32[2,1024,256]{2,1,0:T(8,128)} %collective-permute-done.29.mate, bf16[1040,256]{1,0:T(8,128)(2,1)} %collective-permute-done.30.refs_0_, bf16[4096,1024]{1,0:T(8,128)(2,1)} %bitcast.23), custom_call_target="tpu_custom_call" | custom-call | flops 8589934592 | bytes 16777216 | tf_op jit(solution)/shard_map/expand_send/pallas_call | solution.py:462
  419.2 17.7 %collective-permute-done.31.refs_0_ = bf16[2,1040,256]{2,1,0:T(8,128)(2,1)} collective-permute-done((bf16[2,1040,256]{2,1,0:T(8,128)(2,1)}, bf16[2,1040,256]{2,1,0:T(8,128)(2,1)}, u32[]{:S(2)}, u32[]{:S(2)}) %collective-permute-start.31) | collective-permute-done | bytes 1064992 | tf_op jit(solution)/shard_map/ppermute | solution.py:690
  436.9 3.3 hop.5
  440.2 7.6 %expand_send.7 = (bf16[2,1040,256]{2,1,0:T(8,128)(2,1)}, bf16[1024,512]{1,0:T(8,128)(2,1)S(1)}) custom-call(s32[1]{0:T(128)} %bitcast.1.place_ref, f32[2,1024,256]{2,1,0:T(8,128)S(1)} %copy-done.8, f32[2,1024,256]{2,1,0:T(8,128)} %collective-permute-done.23.mate, bf16[1040,256]{1,0:T(8,128)(2,1)S(1)} %collective-permute-done.24.refs_0_, ...), custom_call_target="tpu_custom_call" | custom-call | flops 8589934592 | bytes 16777216 | tf_op jit(solution)/shard_map/expand_send/pallas_call | solution.py:462
  448.8 5.4 %expand_keep.7.kept = f32[2,1024,256]{2,1,0:T(8,128)} custom-call(s32[1]{0:T(128)} %bitcast.1.place_ref, bf16[1024,512]{1,0:T(8,128)(2,1)} %copy-done.16, bf16[4096,1024]{1,0:T(8,128)(2,1)} %bitcast.25), custom_call_target="tpu_custom_call" | custom-call | flops 8589934592 | bytes 16777216 | tf_op jit(solution)/shard_map/expand_keep/pallas_call | solution.py:495
  454.2 5.3 expand_keep.6.kept
  459.5 11.6 %collective-permute-done.32.refs_0_ = bf16[2,1040,256]{2,1,0:T(8,128)(2,1)} collective-permute-done((bf16[2,1040,256]{2,1,0:T(8,128)(2,1)}, bf16[2,1040,256]{2,1,0:T(8,128)(2,1)}, u32[]{:S(2)}, u32[]{:S(2)}) %collective-permute-start.32) | collective-permute-done | bytes 1064992 | tf_op jit(solution)/shard_map/ppermute | solution.py:690
  472.7 2.5 hop.6
  475.3 29.2 %collective-permute-done.33.refs_0_ = bf16[2,1040,256]{2,1,0:T(8,128)(2,1)} collective-permute-done((bf16[2,1040,256]{2,1,0:T(8,128)(2,1)}, bf16[2,1040,256]{2,1,0:T(8,128)(2,1)}, u32[]{:S(2)}, u32[]{:S(2)}) %collective-permute-start.33) | collective-permute-done | bytes 1064992 | tf_op jit(solution)/shard_map/ppermute | solution.py:690
  504.6 2.5 hop.7
  507.2 3.4 finish.4.refs_2_
  510.6 3.4 finish.5.refs_2_
  514.0 3.3 finish.6.refs_2_
  517.3 14.4 %collective-permute-done.34.refs_1_ = bf16[1,1040,256]{2,1,0:T(8,128)(2,1)S(1)} collective-permute-done((bf16[1,1040,256]{2,1,0:T(8,128)(2,1)S(1)}, bf16[1,1040,256]{2,1,0:T(8,128)(2,1)S(1)}, u32[]{:S(2)}, u32[]{:S(2)}) %collective-permute-start.34) | collective-permute-done | bytes 532512 | tf_op jit(solution)/shard_map/ppermute | solution.py:690
  531.7 3.3 finish.7
  (103 shorter events, 34.0 us)
Async XLA Ops:
  0.6 49.0 %collective-permute-start = (bf16[1024,1024]{1,0:T(8,128)(2,1)}, bf16[1024,1024]{1,0:T(8,128)(2,1)}, u32[]{:S(2)}, u32[]{:S(2)}) collective-permute-start(bf16[1024,1024]{1,0:T(8,128)(2,1)} %param.8), channel_id=1, source_target_pairs={{0,2},{1,3},{2,0},{3,1},{4,6},{5,7},{6,4},{7,5},{8,10},{9,11},{10,... | collective-permute-start | bytes 6291464 | tf_op jit(solution)/shard_map/ppermute | solution.py:588
  3.6 48.4 %collective-permute-start.3 = (bf16[1024,1024]{1,0:T(8,128)(2,1)}, bf16[1024,1024]{1,0:T(8,128)(2,1)S(1)}, u32[]{:S(2)}, u32[]{:S(2)}) collective-permute-start(bf16[1024,1024]{1,0:T(8,128)(2,1)} %refs_2_.1), channel_id=1, source_target_pairs={{0,4},{4,8},{8,12},{1,5},{5,9},{9,13},{2,6},{6,10},{10,14},{3,7},{... | collective-permute-start | bytes 6291464 | tf_op jit(solution)/shard_map/ppermute | solution.py:605
  7.2 49.0 %collective-permute-start.5 = (bf16[1024,1024]{1,0:T(8,128)(2,1)}, bf16[1024,1024]{1,0:T(8,128)(2,1)}, u32[]{:S(2)}, u32[]{:S(2)}) collective-permute-start(bf16[1024,1024]{1,0:T(8,128)(2,1)} %refs_2_.1), channel_id=1, source_target_pairs={{4,0},{8,4},{12,8},{5,1},{9,5},{13,9},{6,2},{10,6},{14,10},{7,3},{... | collective-permute-start | bytes 6291464 | tf_op jit(solution)/shard_map/ppermute | solution.py:608
  8.5 52.8 %collective-permute-start.1 = (bf16[1024,1024]{1,0:T(8,128)(2,1)}, bf16[1024,1024]{1,0:T(8,128)(2,1)}, u32[]{:S(2)}, u32[]{:S(2)}) collective-permute-start(bf16[1024,1024]{1,0:T(8,128)(2,1)} %param.8), channel_id=1, source_target_pairs={{0,1},{1,0},{2,3},{3,2},{4,5},{5,4},{6,7},{7,6},{8,9},{9,8},{10,11... | collective-permute-start | bytes 6291464 | tf_op jit(solution)/shard_map/ppermute | solution.py:588
  49.6 13.6 %collective-permute-start.2 = (bf16[1024,1024]{1,0:T(8,128)(2,1)}, bf16[1024,1024]{1,0:T(8,128)(2,1)}, u32[]{:S(2)}, u32[]{:S(2)}) collective-permute-start(bf16[1024,1024]{1,0:T(8,128)(2,1)} %collective-permute-done), channel_id=1, source_target_pairs={{0,1},{1,0},{2,3},{3,2},{4,5},{5,4},{6,7},{7,6},{8,9},{9,8},{10,11... | collective-permute-start | bytes 6291464 | tf_op jit(solution)/shard_map/ppermute | solution.py:588
  52.0 13.1 %collective-permute-start.4 = (bf16[1024,1024]{1,0:T(8,128)(2,1)S(1)}, bf16[1024,1024]{1,0:T(8,128)(2,1)}, u32[]{:S(2)}, u32[]{:S(2)}) collective-permute-start(bf16[1024,1024]{1,0:T(8,128)(2,1)S(1)} %collective-permute-done.3.refs_1_), channel_id=1, source_target_pairs={{4,8},{8,12},{5,9},{9,13},{6,10},{10,14},{7,11},{11,15},{20,24},{2... | collective-permute-start | bytes 6291464 | tf_op jit(solution)/shard_map/ppermute | solution.py:605
  56.3 49.4 %collective-permute-start.6 = (bf16[1024,1024]{1,0:T(8,128)(2,1)}, bf16[1024,1024]{1,0:T(8,128)(2,1)}, u32[]{:S(2)}, u32[]{:S(2)}) collective-permute-start(bf16[1024,1024]{1,0:T(8,128)(2,1)} %collective-permute-done.5.refs_3_), channel_id=1, source_target_pairs={{4,0},{8,4},{5,1},{9,5},{6,2},{10,6},{7,3},{11,7},{20,16},{24,20},... | collective-permute-start | bytes 6291464 | tf_op jit(solution)/shard_map/ppermute | solution.py:608
  57.6 1.6 copy-start.22
  65.1 3.3 copy-start.20
  105.6 27.1 %collective-permute-start.7 = (bf16[1024,1024]{1,0:T(8,128)(2,1)}, bf16[1024,1024]{1,0:T(8,128)(2,1)}, u32[]{:S(2)}, u32[]{:S(2)}) collective-permute-start(bf16[1024,1024]{1,0:T(8,128)(2,1)} %collective-permute-done.4.refs_0_), channel_id=1, source_target_pairs={{8,12},{9,13},{10,14},{11,15},{24,28},{25,29},{26,30},{27,31}} | collective-permute-start | bytes 6291464 | tf_op jit(solution)/shard_map/ppermute | solution.py:605
  107.6 47.6 %collective-permute-start.8 = (bf16[1024,1024]{1,0:T(8,128)(2,1)}, bf16[1024,1024]{1,0:T(8,128)(2,1)}, u32[]{:S(2)}, u32[]{:S(2)}) collective-permute-start(bf16[1024,1024]{1,0:T(8,128)(2,1)} %collective-permute-done.6.refs_4_), channel_id=1, source_target_pairs={{4,0},{5,1},{6,2},{7,3},{20,16},{21,17},{22,18},{23,19}} | collective-permute-start | bytes 6291464 | tf_op jit(solution)/shard_map/ppermute | solution.py:608
  108.9 67.1 %collective-permute-start.9 = (bf16[1024,1024]{1,0:T(8,128)(2,1)}, bf16[1024,1024]{1,0:T(8,128)(2,1)}, u32[]{:S(2)}, u32[]{:S(2)}) collective-permute-start(bf16[1024,1024]{1,0:T(8,128)(2,1)} %piece.1), channel_id=1, source_target_pairs={{0,4},{4,8},{1,5},{5,9},{2,6},{6,10},{3,7},{7,11},{16,20},{20,24},... | collective-permute-start | bytes 6291464 | tf_op jit(solution)/shard_map/ppermute | solution.py:605
  116.1 59.8 %collective-permute-start.10 = (bf16[1024,1024]{1,0:T(8,128)(2,1)}, bf16[1024,1024]{1,0:T(8,128)(2,1)}, u32[]{:S(2)}, u32[]{:S(2)}) collective-permute-start(bf16[1024,1024]{1,0:T(8,128)(2,1)} %piece.1), channel_id=1, source_target_pairs={{8,4},{12,8},{9,5},{13,9},{10,6},{14,10},{11,7},{15,11},{24,20},{2... | collective-permute-start | bytes 6291464 | tf_op jit(solution)/shard_map/ppermute | solution.py:608
  155.2 23.4 %collective-permute-start.14 = (bf16[1024,1024]{1,0:T(8,128)(2,1)}, bf16[1024,1024]{1,0:T(8,128)(2,1)}, u32[]{:S(2)}, u32[]{:S(2)}) collective-permute-start(bf16[1024,1024]{1,0:T(8,128)(2,1)} %piece.1), channel_id=1, source_target_pairs={{8,12},{9,13},{10,14},{11,15},{24,28},{25,29},{26,30},{27,31}} | collective-permute-start | bytes 6291464 | tf_op jit(solution)/shard_map/ppermute | solution.py:605
  157.1 46.6 %collective-permute-start.13 = (bf16[1024,1024]{1,0:T(8,128)(2,1)}, bf16[1024,1024]{1,0:T(8,128)(2,1)}, u32[]{:S(2)}, u32[]{:S(2)}) collective-permute-start(bf16[1024,1024]{1,0:T(8,128)(2,1)} %piece.1), channel_id=1, source_target_pairs={{4,0},{5,1},{6,2},{7,3},{20,16},{21,17},{22,18},{23,19}} | collective-permute-start | bytes 6291464 | tf_op jit(solution)/shard_map/ppermute | solution.py:608
  176.0 37.2 %collective-permute-start.11 = (bf16[1040,1024]{1,0:T(8,128)(2,1)}, bf16[1040,1024]{1,0:T(8,128)(2,1)S(1)}, u32[]{:S(2)}, u32[]{:S(2)}) collective-permute-start(bf16[1040,1024]{1,0:T(8,128)(2,1)} %get-tuple-element.69), channel_id=1, source_target_pairs={{0,1},{1,0},{2,3},{3,2},{4,5},{5,4},{6,7},{7,6},{8,9},{9,8},{10,11... | collective-permute-start | bytes 6389768 | tf_op jit(solution)/shard_map/ppermute | solution.py:588
  176.0 52.0 %collective-permute-start.12 = (bf16[1040,1024]{1,0:T(8,128)(2,1)}, bf16[1040,1024]{1,0:T(8,128)(2,1)}, u32[]{:S(2)}, u32[]{:S(2)}) collective-permute-start(bf16[1040,1024]{1,0:T(8,128)(2,1)} %get-tuple-element.69), channel_id=1, source_target_pairs={{0,2},{1,3},{2,0},{3,1},{4,6},{5,7},{6,4},{7,5},{8,10},{9,11},{10,... | collective-permute-start | bytes 6389768 | tf_op jit(solution)/shard_map/ppermute | solution.py:588
  176.6 51.5 %collective-permute-start.17 = (bf16[1024,1024]{1,0:T(8,128)(2,1)}, bf16[1024,1024]{1,0:T(8,128)(2,1)}, u32[]{:S(2)}, u32[]{:S(2)}) collective-permute-start(bf16[1024,1024]{1,0:T(8,128)(2,1)} %collective-permute-done.10), channel_id=1, source_target_pairs={{8,4},{9,5},{10,6},{11,7},{24,20},{25,21},{26,22},{27,23}} | collective-permute-start | bytes 6291464 | tf_op jit(solution)/shard_map/ppermute | solution.py:608
  178.6 50.7 %collective-permute-start.19 = (bf16[1024,1024]{1,0:T(8,128)(2,1)}, bf16[1024,1024]{1,0:T(8,128)(2,1)}, u32[]{:S(2)}, u32[]{:S(2)}) collective-permute-start(bf16[1024,1024]{1,0:T(8,128)(2,1)} %collective-permute-done.9), channel_id=1, source_target_pairs={{4,8},{5,9},{6,10},{7,11},{20,24},{21,25},{22,26},{23,27}} | collective-permute-start | bytes 6291464 | tf_op jit(solution)/shard_map/ppermute | solution.py:605
  203.8 27.6 %collective-permute-start.18 = (bf16[1024,1024]{1,0:T(8,128)(2,1)}, bf16[1024,1024]{1,0:T(8,128)(2,1)}, u32[]{:S(2)}, u32[]{:S(2)}) collective-permute-start(bf16[1024,1024]{1,0:T(8,128)(2,1)} %collective-permute-done.9), channel_id=1, source_target_pairs={{8,12},{9,13},{10,14},{11,15},{24,28},{25,29},{26,30},{27,31}} | collective-permute-start | bytes 6291464 | tf_op jit(solution)/shard_map/ppermute | solution.py:605
  213.2 4.4 copy-start.21
  213.2 50.8 %collective-permute-start.16 = (bf16[1024,1024]{1,0:T(8,128)(2,1)}, bf16[1024,1024]{1,0:T(8,128)(2,1)}, u32[]{:S(2)}, u32[]{:S(2)}) collective-permute-start(bf16[1024,1024]{1,0:T(8,128)(2,1)} %collective-permute-done.10), channel_id=1, source_target_pairs={{4,0},{5,1},{6,2},{7,3},{20,16},{21,17},{22,18},{23,19}} | collective-permute-start | bytes 6291464 | tf_op jit(solution)/shard_map/ppermute | solution.py:608
  228.0 53.8 %collective-permute-start.15 = (bf16[1040,1024]{1,0:T(8,128)(2,1)}, bf16[1040,1024]{1,0:T(8,128)(2,1)}, u32[]{:S(2)}, u32[]{:S(2)}) collective-permute-start(bf16[1040,1024]{1,0:T(8,128)(2,1)} %collective-permute-done.12.message.scales), channel_id=1, source_target_pairs={{0,1},{1,0},{2,3},{3,2},{4,5},{5,4},{6,7},{7,6},{8,9},{9,8},{10,11... | collective-permute-start | bytes 6389768 | tf_op jit(solution)/shard_map/ppermute | solution.py:588
  228.0 83.3 %collective-permute-start.20 = (bf16[1024,1024]{1,0:T(8,128)(2,1)}, bf16[1024,1024]{1,0:T(8,128)(2,1)S(1)}, u32[]{:S(2)}, u32[]{:S(2)}) collective-permute-start(bf16[1024,1024]{1,0:T(8,128)(2,1)} %collective-permute-done.17), channel_id=1, source_target_pairs={{4,0},{5,1},{6,2},{7,3},{20,16},{21,17},{22,18},{23,19}} | collective-permute-start | bytes 6291464 | tf_op jit(solution)/shard_map/ppermute | solution.py:608
  229.3 82.0 %collective-permute-start.21 = (bf16[1024,1024]{1,0:T(8,128)(2,1)}, bf16[1024,1024]{1,0:T(8,128)(2,1)}, u32[]{:S(2)}, u32[]{:S(2)}) collective-permute-start(bf16[1024,1024]{1,0:T(8,128)(2,1)} %collective-permute-done.19), channel_id=1, source_target_pairs={{8,12},{9,13},{10,14},{11,15},{24,28},{25,29},{26,30},{27,31}} | collective-permute-start | bytes 6291464 | tf_op jit(solution)/shard_map/ppermute | solution.py:605
  309.4 2.0 copy-start.6
  326.6 2.0 copy-start.15
  341.4 7.2 %copy-start.11 = (f32[2,1024,256]{2,1,0:T(8,128)}, f32[2,1024,256]{2,1,0:T(8,128)S(1)}, u32[]{:S(2)}) copy-start(f32[2,1024,256]{2,1,0:T(8,128)S(1)} %get-tuple-element.96.keep) | copy-start | bytes 6291460
  341.4 4.2 collective-permute-start.22
  341.4 7.1 %collective-permute-start.25 = (f32[2,1024,256]{2,1,0:T(8,128)S(1)}, f32[2,1024,256]{2,1,0:T(8,128)S(1)}, u32[]{:S(2)}, u32[]{:S(2)}) collective-permute-start(f32[2,1024,256]{2,1,0:T(8,128)S(1)} %get-tuple-element.97), channel_id=1, source_target_pairs={{0,1},{1,0},{2,3},{3,2},{4,5},{5,4},{6,7},{7,6},{8,9},{9,8},{10,11... | collective-permute-start | bytes 6291464 | tf_op jit(solution)/shard_map/ppermute | solution.py:588
  346.4 17.9 %collective-permute-start.27 = (bf16[1040,256]{1,0:T(8,128)(2,1)S(1)}, bf16[1040,256]{1,0:T(8,128)(2,1)S(1)}, u32[]{:S(2)}, u32[]{:S(2)}) collective-permute-start(bf16[1040,256]{1,0:T(8,128)(2,1)S(1)} %send.4), channel_id=1, source_target_pairs={{0,2},{1,3},{2,0},{3,1},{4,6},{5,7},{6,4},{7,5},{8,10},{9,11},{10,... | collective-permute-start | bytes 1597448 | tf_op jit(solution)/shard_map/ppermute | solution.py:588
  348.6 1.3 copy-start.13
  349.9 28.1 %collective-permute-start.26 = (bf16[1040,256]{1,0:T(8,128)(2,1)S(1)}, bf16[1040,256]{1,0:T(8,128)(2,1)S(1)}, u32[]{:S(2)}, u32[]{:S(2)}) collective-permute-start(bf16[1040,256]{1,0:T(8,128)(2,1)S(1)} %send.6), channel_id=1, source_target_pairs={{0,2},{1,3},{2,0},{3,1},{4,6},{5,7},{6,4},{7,5},{8,10},{9,11},{10,... | collective-permute-start | bytes 1597448 | tf_op jit(solution)/shard_map/ppermute | solution.py:588
  363.7 8.8 %copy-start.7 = (f32[2,1024,256]{2,1,0:T(8,128)}, f32[2,1024,256]{2,1,0:T(8,128)S(1)}, u32[]{:S(2)}) copy-start(f32[2,1024,256]{2,1,0:T(8,128)S(1)} %get-tuple-element.94.keep) | copy-start | bytes 6291460
  363.7 30.2 %copy-start.9 = (f32[2,1024,256]{2,1,0:T(8,128)}, f32[2,1024,256]{2,1,0:T(8,128)S(1)}, u32[]{:S(2)}) copy-start(f32[2,1024,256]{2,1,0:T(8,128)S(1)} %get-tuple-element.105.keep) | copy-start | bytes 6291460
  363.7 30.2 %collective-permute-start.29 = (f32[2,1024,256]{2,1,0:T(8,128)}, f32[2,1024,256]{2,1,0:T(8,128)}, u32[]{:S(2)}, u32[]{:S(2)}) collective-permute-start(f32[2,1024,256]{2,1,0:T(8,128)} %get-tuple-element.106), channel_id=1, source_target_pairs={{0,1},{1,0},{2,3},{3,2},{4,5},{5,4},{6,7},{7,6},{8,9},{9,8},{10,11... | collective-permute-start | bytes 6291464 | tf_op jit(solution)/shard_map/ppermute | solution.py:588
  363.8 41.9 %collective-permute-start.23 = (f32[2,1024,256]{2,1,0:T(8,128)}, f32[2,1024,256]{2,1,0:T(8,128)}, u32[]{:S(2)}, u32[]{:S(2)}) collective-permute-start(f32[2,1024,256]{2,1,0:T(8,128)} %get-tuple-element.95), channel_id=1, source_target_pairs={{0,1},{1,0},{2,3},{3,2},{4,5},{5,4},{6,7},{7,6},{8,9},{9,8},{10,11... | collective-permute-start | bytes 6291464 | tf_op jit(solution)/shard_map/ppermute | solution.py:588
  372.5 1.0 copy-start.19
  373.5 30.0 %collective-permute-start.28 = (bf16[2,1040,256]{2,1,0:T(8,128)(2,1)}, bf16[2,1040,256]{2,1,0:T(8,128)(2,1)S(1)}, u32[]{:S(2)}, u32[]{:S(2)}) collective-permute-start(bf16[2,1040,256]{2,1,0:T(8,128)(2,1)} %get-tuple-element.98), channel_id=1, source_target_pairs={{0,4},{4,0},{8,12},{12,8},{1,5},{5,1},{9,13},{13,9},{2,6},{6,2},{1... | collective-permute-start | bytes 3194888 | tf_op jit(solution)/shard_map/ppermute | solution.py:690
  383.4 1.6 copy-start.12
  385.0 1.6 copy-start.14
  393.9 2.4 copy-start.17
  393.9 43.0 %collective-permute-start.31 = (bf16[2,1040,256]{2,1,0:T(8,128)(2,1)}, bf16[2,1040,256]{2,1,0:T(8,128)(2,1)}, u32[]{:S(2)}, u32[]{:S(2)}) collective-permute-start(bf16[2,1040,256]{2,1,0:T(8,128)(2,1)} %get-tuple-element.102), channel_id=1, source_target_pairs={{0,4},{4,0},{8,12},{12,8},{1,5},{5,1},{9,13},{13,9},{2,6},{6,2},{1... | collective-permute-start | bytes 3194888 | tf_op jit(solution)/shard_map/ppermute | solution.py:690
  396.4 13.8 %collective-permute-start.30 = (bf16[1040,256]{1,0:T(8,128)(2,1)S(1)}, bf16[1040,256]{1,0:T(8,128)(2,1)}, u32[]{:S(2)}, u32[]{:S(2)}) collective-permute-start(bf16[1040,256]{1,0:T(8,128)(2,1)S(1)} %send.7), channel_id=1, source_target_pairs={{0,2},{1,3},{2,0},{3,1},{4,6},{5,7},{6,4},{7,5},{8,10},{9,11},{10,... | collective-permute-start | bytes 1597448 | tf_op jit(solution)/shard_map/ppermute | solution.py:588
  398.0 5.5 %copy-start = (f32[2,1024,256]{2,1,0:T(8,128)S(1)}, f32[2,1024,256]{2,1,0:T(8,128)}, u32[]{:S(2)}) copy-start(f32[2,1024,256]{2,1,0:T(8,128)} %expand_keep.5.kept) | copy-start | bytes 6291460
  403.4 2.3 copy-start.8
  405.7 101.4 %collective-permute-start.37 = (bf16[1,1040,256]{2,1,0:T(8,128)(2,1)}, bf16[1,1040,256]{2,1,0:T(8,128)(2,1)}, u32[]{:S(2)}, u32[]{:S(2)}) collective-permute-start(bf16[1,1040,256]{2,1,0:T(8,128)(2,1)} %hop.4), channel_id=1, source_target_pairs={{0,8},{4,12},{8,0},{12,4},{1,9},{5,13},{9,1},{13,5},{2,10},{6,14},... | collective-permute-start | bytes 1597448 | tf_op jit(solution)/shard_map/ppermute | solution.py:690
  405.7 4.5 copy-start.10
  407.9 29.0 %copy-start.1 = (f32[2,1024,256]{2,1,0:T(8,128)S(1)}, f32[2,1024,256]{2,1,0:T(8,128)}, u32[]{:S(2)}) copy-start(f32[2,1024,256]{2,1,0:T(8,128)} %expand_keep.4.kept) | copy-start | bytes 6291460
  407.9 32.3 %collective-permute-start.24 = (bf16[1040,256]{1,0:T(8,128)(2,1)S(1)}, bf16[1040,256]{1,0:T(8,128)(2,1)S(1)}, u32[]{:S(2)}, u32[]{:S(2)}) collective-permute-start(bf16[1040,256]{1,0:T(8,128)(2,1)S(1)} %send.5), channel_id=1, source_target_pairs={{0,2},{1,3},{2,0},{3,1},{4,6},{5,7},{6,4},{7,5},{8,10},{9,11},{10,... | collective-permute-start | bytes 1597448 | tf_op jit(solution)/shard_map/ppermute | solution.py:588
  417.9 22.4 %copy-start.16 = (bf16[1024,512]{1,0:T(8,128)(2,1)}, bf16[1024,512]{1,0:T(8,128)(2,1)S(1)}, u32[]{:S(2)}) copy-start(bf16[1024,512]{1,0:T(8,128)(2,1)S(1)} %get-tuple-element.112.both) | copy-start | bytes 3145732
  417.9 53.3 %collective-permute-start.32 = (bf16[2,1040,256]{2,1,0:T(8,128)(2,1)}, bf16[2,1040,256]{2,1,0:T(8,128)(2,1)}, u32[]{:S(2)}, u32[]{:S(2)}) collective-permute-start(bf16[2,1040,256]{2,1,0:T(8,128)(2,1)} %get-tuple-element.108), channel_id=1, source_target_pairs={{0,4},{4,0},{8,12},{12,8},{1,5},{5,1},{9,13},{13,9},{2,6},{6,2},{1... | collective-permute-start | bytes 3194888 | tf_op jit(solution)/shard_map/ppermute | solution.py:690
  440.2 70.3 %collective-permute-start.36 = (bf16[1,1040,256]{2,1,0:T(8,128)(2,1)}, bf16[1,1040,256]{2,1,0:T(8,128)(2,1)S(1)}, u32[]{:S(2)}, u32[]{:S(2)}) collective-permute-start(bf16[1,1040,256]{2,1,0:T(8,128)(2,1)} %hop.5), channel_id=1, source_target_pairs={{0,8},{4,12},{8,0},{12,4},{1,9},{5,13},{9,1},{13,5},{2,10},{6,14},... | collective-permute-start | bytes 1597448 | tf_op jit(solution)/shard_map/ppermute | solution.py:690
  447.8 1.0 copy-start.18
  448.8 55.7 %collective-permute-start.33 = (bf16[2,1040,256]{2,1,0:T(8,128)(2,1)}, bf16[2,1040,256]{2,1,0:T(8,128)(2,1)}, u32[]{:S(2)}, u32[]{:S(2)}) collective-permute-start(bf16[2,1040,256]{2,1,0:T(8,128)(2,1)} %get-tuple-element.114), channel_id=1, source_target_pairs={{0,4},{4,0},{8,12},{12,8},{1,5},{5,1},{9,13},{13,9},{2,6},{6,2},{1... | collective-permute-start | bytes 3194888 | tf_op jit(solution)/shard_map/ppermute | solution.py:690
  459.5 45.0 %copy-start.3 = (f32[2,1024,256]{2,1,0:T(8,128)S(1)}, f32[2,1024,256]{2,1,0:T(8,128)}, u32[]{:S(2)}) copy-start(f32[2,1024,256]{2,1,0:T(8,128)} %expand_keep.6.kept) | copy-start | bytes 6291460
  471.1 1.6 copy-start.4
  475.2 38.8 %collective-permute-start.35 = (bf16[1,1040,256]{2,1,0:T(8,128)(2,1)S(1)}, bf16[1,1040,256]{2,1,0:T(8,128)(2,1)S(1)}, u32[]{:S(2)}, u32[]{:S(2)}) collective-permute-start(bf16[1,1040,256]{2,1,0:T(8,128)(2,1)S(1)} %hop.6), channel_id=1, source_target_pairs={{0,8},{4,12},{8,0},{12,4},{1,9},{5,13},{9,1},{13,5},{2,10},{6,14},... | collective-permute-start | bytes 1597448 | tf_op jit(solution)/shard_map/ppermute | solution.py:690
  507.1 3.5 copy-start.2
  507.1 24.6 %collective-permute-start.34 = (bf16[1,1040,256]{2,1,0:T(8,128)(2,1)S(1)}, bf16[1,1040,256]{2,1,0:T(8,128)(2,1)S(1)}, u32[]{:S(2)}, u32[]{:S(2)}) collective-permute-start(bf16[1,1040,256]{2,1,0:T(8,128)(2,1)S(1)} %hop.7), channel_id=1, source_target_pairs={{0,8},{4,12},{8,0},{12,4},{1,9},{5,13},{9,1},{13,5},{2,10},{6,14},... | collective-permute-start | bytes 1597448 | tf_op jit(solution)/shard_map/ppermute | solution.py:690
  510.6 3.4 copy-start.5

commit v16 on v15

--- a/solution.py
+++ b/solution.py
@@ -675,9 +675,11 @@
         for distance in range(2, cols, 2):
             pieces[distance] = after(swap(message, distance), held[1], mate_pair)
             pieces[distance + 1] = swap(pieces[distance], 1)
+        pieces = [pair, mate_pair] + [unpack(pieces[distance]) for distance in range(2, cols)]
         for step in range(2, far if aligned else lines):
+            rights[-step] = after(rights[-step], *pieces[2:])
+            rights[step] = after(rights[step], *pieces[2:])
             held = put_block(put_block(held, -step), step)
-        pieces = [pair, mate_pair] + [unpack(pieces[distance]) for distance in range(2, cols)]
         part = rotate_part(at, pieces, held[0], far if aligned else -1)
         part, above, below = barrier((part, above, below))
         if not aligned:

time: 536 us -> 537 us (level)
  no operation moved by 1% of the time
where the time goes in v16:
time: 537 us; the launch traced here: 535 us
  waiting for transfers between devices  233 us (43%)
  Pallas kernels  217 us (40%)
  starting transfers between devices  49 us (9%)
  local copies, waits for them, and re-layouts  22.2 us (4%)
  other arithmetic  12.6 us (2%)
    ppermute x8, waiting for transfers between devices, down(): return lax.ppermute(value, 'row', [(i, i - 1) for i in senders])  110 us
    ppermute x8, waiting for transfers between devices, cross(): return lax.ppermute(value, 'row', [(i, i ^ distance) for i in range(lines)])  73 us
    ppermute x14, waiting for transfers between devices, swap(): return lax.ppermute(value, 'col', [(i, i ^ distance) for i in range(cols)])  47.6 us
    pallas_call x4, Pallas kernels, expand_send(): pl.pallas_call(functools.partial(expand_send_kernel, tile=min(64, depth))...  30.7 us
    pallas_call x2, Pallas kernels, restore(): pl.pallas_call(functools.partial(restore_kernel, cols=cols), grid_spec=pl...  26 us
    pallas_call x2, Pallas kernels, halfway(): pl.pallas_call(functools.partial(halfway_kernel, offsets=offsets, lines=l...  24.3 us
    ppermute x8, starting transfers between devices, up(): return lax.ppermute(value, 'row', [(i, i + 1) for i in senders])  22.8 us
    pallas_call x4, Pallas kernels, expand_keep(): pl.pallas_call(expand_keep_kernel, grid_spec=pltpu.PrefetchScalarGridSpec...  21.6 us
  transfers between devices with their start and end apart: 38, of which 14 were waited for; matrix products, arithmetic and copies ran while one was open for 4% of the time, Pallas kernels for 34%

profile of v16, /device:TPU:0, one launch (start us, length us, event | category | flops | bytes accessed | tf_op | source)
XLA Modules:
  0.0 535.1 jit_solution(9397827147302201032)
XLA Ops:
  0.6 3.0 collective-permute-start
  3.6 3.6 collective-permute-start.3
  8.6 41.0 %collective-permute-done = bf16[1024,1024]{1,0:T(8,128)(2,1)} collective-permute-done((bf16[1024,1024]{1,0:T(8,128)(2,1)}, bf16[1024,1024]{1,0:T(8,128)(2,1)}, u32[]{:S(2)}, u32[]{:S(2)}) %collective-permute-start) | collective-permute-done | bytes 2097184 | tf_op jit(solution)/shard_map/ppermute | solution.py:588
  49.6 2.4 collective-permute-done.3.refs_1_
  52.0 2.1 collective-permute-start.4
  54.1 2.2 collective-permute-done.5.refs_3_
  65.1 3.3 copy-done.20
  68.4 37.4 %collective-permute-done.6.refs_4_ = bf16[1024,1024]{1,0:T(8,128)(2,1)} collective-permute-done((bf16[1024,1024]{1,0:T(8,128)(2,1)}, bf16[1024,1024]{1,0:T(8,128)(2,1)}, u32[]{:S(2)}, u32[]{:S(2)}) %collective-permute-start.6) | collective-permute-done | bytes 2097184 | tf_op jit(solution)/shard_map/ppermute | solution.py:608
  105.8 2.0 collective-permute-start.7
  109.1 7.2 %collective-permute-start.9 = (bf16[1024,1024]{1,0:T(8,128)(2,1)}, bf16[1024,1024]{1,0:T(8,128)(2,1)}, u32[]{:S(2)}, u32[]{:S(2)}) collective-permute-start(bf16[1024,1024]{1,0:T(8,128)(2,1)} %piece.1), channel_id=1, source_target_pairs={{0,4},{4,8},{1,5},{5,9},{2,6},{6,10},{3,7},{7,11},{16,20},{20,24},... | collective-permute-start | bytes 6291464 | tf_op jit(solution)/shard_map/ppermute | solution.py:605
  116.3 2.0 collective-permute-start.10
  118.2 14.7 %halfway.2.refs_2_ = f32[1024,1024]{1,0:T(8,128)} custom-call(s32[1]{0:T(128)} %bitcast.1.place_ref, bf16[4096,1024]{1,0:T(8,128)(2,1)} %bitcast.17, bf16[1024,1024]{1,0:T(8,128)(2,1)} %collective-permute-done.4.refs_0_, bf16[1024,1024]{1,0:T(8,128)(2,1)S(1)} %collective-permute-done.3.refs_1_, bf16[1024,1024]{1,0:T(8,128)(2,1)} %refs_2_.1, ...), custom_call_target="tpu_custom_call" | custom-call | flops 2576980480 | bytes 2516582 | tf_op jit(solution)/shard_map/halfway/pallas_call | solution.py:114
  132.9 22.4 %collective-permute-done.8.refs_1_ = bf16[1024,1024]{1,0:T(8,128)(2,1)} collective-permute-done((bf16[1024,1024]{1,0:T(8,128)(2,1)}, bf16[1024,1024]{1,0:T(8,128)(2,1)}, u32[]{:S(2)}, u32[]{:S(2)}) %collective-permute-start.8) | collective-permute-done | bytes 2097184 | tf_op jit(solution)/shard_map/ppermute | solution.py:608
  155.3 2.0 collective-permute-start.14
  158.6 9.6 %halfway.3.value = f32[1024,1024]{1,0:T(8,128)} custom-call(s32[1]{0:T(128)} %bitcast.1.place_ref, bf16[4096,1024]{1,0:T(8,128)(2,1)} %bitcast.18, bf16[1024,1024]{1,0:T(8,128)(2,1)} %collective-permute-done.7.refs_0_, bf16[1024,1024]{1,0:T(8,128)(2,1)} %collective-permute-done.8.refs_1_, f32[1024,1024]{1,0:T(8,128)} %halfway.2.refs_2_), custom_call_target="tpu_custom_call" | custom-call | flops 2576980480 | bytes 2516582 | tf_op jit(solution)/shard_map/halfway/pallas_call | solution.py:114
  168.2 7.9 %pack.1 = (bf16[2,1024,1024]{2,1,0:T(8,128)(2,1)}, bf16[1040,1024]{1,0:T(8,128)(2,1)}) custom-call(f32[1024,1024]{1,0:T(8,128)} %halfway.3.value), custom_call_target="tpu_custom_call" | custom-call | flops 125829120 | bytes 3145728 | tf_op jit(solution)/shard_map/pack/pallas_call | solution.py:147
  176.7 2.0 collective-permute-start.17
  178.7 2.0 collective-permute-start.19
  180.8 4.3 put.5
  185.1 18.8 %collective-permute-done.13 = bf16[1024,1024]{1,0:T(8,128)(2,1)} collective-permute-done((bf16[1024,1024]{1,0:T(8,128)(2,1)}, bf16[1024,1024]{1,0:T(8,128)(2,1)}, u32[]{:S(2)}, u32[]{:S(2)}) %collective-permute-start.13) | collective-permute-done | bytes 2097184 | tf_op jit(solution)/shard_map/ppermute | solution.py:608
  203.9 2.0 collective-permute-start.18
  205.9 3.1 broadcast_select_fusion.1.piece
  209.0 4.3 put.6
  214.6 3.1 broadcast_select_fusion.3.piece
  217.7 4.4 put.7
  222.1 6.1 %unpack.3.refs_1_ = bf16[2,1024,1024]{2,1,0:T(8,128)(2,1)} custom-call(bf16[1040,1024]{1,0:T(8,128)(2,1)} %copy-done.21, bf16[1040,1024]{1,0:T(8,128)(2,1)} %copy-done.21), custom_call_target="tpu_custom_call" | custom-call | flops 125829120 | bytes 1887436 | tf_op jit(solution)/shard_map/unpack/pallas_call | solution.py:176
  229.4 2.0 collective-permute-start.21
  231.6 3.1 broadcast_select_fusion.piece
  234.7 29.4 %collective-permute-done.16 = bf16[1024,1024]{1,0:T(8,128)(2,1)} collective-permute-done((bf16[1024,1024]{1,0:T(8,128)(2,1)}, bf16[1024,1024]{1,0:T(8,128)(2,1)}, u32[]{:S(2)}, u32[]{:S(2)}) %collective-permute-start.16) | collective-permute-done | bytes 2097184 | tf_op jit(solution)/shard_map/ppermute | solution.py:608
  264.0 3.1 broadcast_select_fusion.2.piece
  267.2 6.1 %unpack.4.refs_2_ = bf16[2,1024,1024]{2,1,0:T(8,128)(2,1)} custom-call(bf16[1040,1024]{1,0:T(8,128)(2,1)} %collective-permute-done.12.message.scales, bf16[1040,1024]{1,0:T(8,128)(2,1)} %collective-permute-done.12.message.scales), custom_call_target="tpu_custom_call" | custom-call | flops 125829120 | bytes 1887436 | tf_op jit(solution)/shard_map/unpack/pallas_call | solution.py:176
  273.3 6.1 %unpack.5.refs_3_ = bf16[2,1024,1024]{2,1,0:T(8,128)(2,1)} custom-call(bf16[1040,1024]{1,0:T(8,128)(2,1)} %collective-permute-done.15.message.scales, bf16[1040,1024]{1,0:T(8,128)(2,1)} %collective-permute-done.15.message.scales), custom_call_target="tpu_custom_call" | custom-call | flops 125829120 | bytes 1887436 | tf_op jit(solution)/shard_map/unpack/pallas_call | solution.py:176
  279.4 4.3 put.8
  283.6 4.4 put.9
  288.0 21.4 %rotate_part.1.part = f32[1024,1024]{1,0:T(8,128)S(1)} custom-call(s32[3]{0:T(128)S(1)} %pad_add_fusion.at_ref, bf16[2,1024,1024]{2,1,0:T(8,128)(2,1)} %get-tuple-element.68.refs_0_, bf16[2,1024,1024]{2,1,0:T(8,128)(2,1)} %unpack.3.refs_1_, bf16[2,1024,1024]{2,1,0:T(8,128)(2,1)} %unpack.4.refs_2_, bf16[2,1024,1024]{2,1,0:T(8,128)(2,1)} %unpack.5.refs_3_, ...), custom_call_target="tpu_custom_call" | custom-call | flops 5153960960 | bytes 6291456 | tf_op jit(solution)/shard_map/rotate_part/pallas_call | solution.py:244
  309.4 2.1 copy-done.6
  311.5 15.3 %rotate.1 = (f32[1024,1024]{1,0:T(8,128)}, f32[1024,1024]{1,0:T(8,128)}, bf16[2,1024,1024]{2,1,0:T(8,128)(2,1)S(1)}, bf16[5,1024,1024]{2,1,0:T(8,128)(2,1)}) custom-call(s32[3]{0:T(128)S(1)} %pad_add_fusion.at_ref, f32[1024,1024]{1,0:T(8,128)} %copy-done.6, bf16[1024,1024]{1,0:T(8,128)(2,1)S(1)} %collective-permute-done.20.above, ...), custom_call_target="tpu_custom_call", output_to_operand_aliasing={{3}: (10, {})} | custom-call | flops 17179869184 | bytes 125829120 | tf_op jit(solution)/shard_map/rotate/pallas_call | solution.py:322
  326.8 2.0 copy-done.15
  328.8 12.7 %restore.2 = (f32[2,1024,256]{2,1,0:T(8,128)S(1)}, f32[2,1024,256]{2,1,0:T(8,128)S(1)}, f32[2,1024,256]{2,1,0:T(8,128)S(1)}, f32[2,1024,256]{2,1,0:T(8,128)S(1)}) custom-call(s32[1]{0:T(128)} %bitcast.me_ref, bf16[2,1024,1024]{2,1,0:T(8,128)(2,1)} %copy-done.15, bf16[5,1024,1024]{2,1,0:T(8,128)(2,1)} %get-tuple-element.94.refs_0_.refs_1_.refs_2_.refs_3_, ...), custom_call_target="tpu_custom_call" | custom-call | flops 34359738368 | bytes 67108864 | tf_op jit(solution)/shard_map/restore/pallas_call | solution.py:380
  342.1 3.6 collective-permute-done.22.mate
  350.6 13.3 %restore.3 = (f32[2,1024,256]{2,1,0:T(8,128)S(1)}, f32[2,1024,256]{2,1,0:T(8,128)}, f32[2,1024,256]{2,1,0:T(8,128)S(1)}, f32[2,1024,256]{2,1,0:T(8,128)}) custom-call(s32[1]{0:T(128)} %bitcast.me_ref, bf16[2,1024,1024]{2,1,0:T(8,128)(2,1)} %copy-done.15, bf16[5,1024,1024]{2,1,0:T(8,128)(2,1)} %get-tuple-element.94.refs_0_.refs_1_.refs_2_.refs_3_, ...), custom_call_target="tpu_custom_call" | custom-call | flops 34359738368 | bytes 67108864 | tf_op jit(solution)/shard_map/restore/pallas_call | solution.py:380
  364.6 8.2 %expand_send.4 = (bf16[2,1040,256]{2,1,0:T(8,128)(2,1)}, bf16[1024,512]{1,0:T(8,128)(2,1)S(1)}) custom-call(s32[1]{0:T(128)} %bitcast.1.place_ref, f32[2,1024,256]{2,1,0:T(8,128)S(1)} %get-tuple-element.95.keep, f32[2,1024,256]{2,1,0:T(8,128)S(1)} %collective-permute-done.22.mate, bf16[1040,256]{1,0:T(8,128)(2,1)S(1)} %collective-permute-done.27.refs_0_, ...), custom_call_target="tpu_custom_call" | custom-call | flops 8589934592 | bytes 16777216 | tf_op jit(solution)/shard_map/expand_send/pallas_call | solution.py:462
  373.7 4.4 collective-permute-start.28
  378.1 5.4 %expand_keep.5.kept = f32[2,1024,256]{2,1,0:T(8,128)} custom-call(s32[1]{0:T(128)} %bitcast.1.place_ref, bf16[1024,512]{1,0:T(8,128)(2,1)} %copy-done.19, bf16[4096,1024]{1,0:T(8,128)(2,1)} %bitcast.20), custom_call_target="tpu_custom_call" | custom-call | flops 8589934592 | bytes 16777216 | tf_op jit(solution)/shard_map/expand_keep/pallas_call | solution.py:495
  386.7 7.3 %expand_send.5 = (bf16[2,1040,256]{2,1,0:T(8,128)(2,1)}, bf16[1024,512]{1,0:T(8,128)(2,1)S(1)}) custom-call(s32[1]{0:T(128)} %bitcast.1.place_ref, f32[2,1024,256]{2,1,0:T(8,128)S(1)} %copy-done.12, f32[2,1024,256]{2,1,0:T(8,128)S(1)} %copy-done.14, bf16[1040,256]{1,0:T(8,128)(2,1)S(1)} %collective-permute-done.26.refs_0_, bf16[4096,1024]{1,0:T(8,128)(2,1)} %bitcast.21), custom_call_target="tpu_custom_call" | custom-call | flops 8589934592 | bytes 16777216 | tf_op jit(solution)/shard_map/expand_send/pallas_call | solution.py:462
  394.2 2.2 send.7
  398.0 5.5 %expand_keep.4.kept = f32[2,1024,256]{2,1,0:T(8,128)} custom-call(s32[1]{0:T(128)} %bitcast.1.place_ref, bf16[1024,512]{1,0:T(8,128)(2,1)} %copy-done.17, bf16[4096,1024]{1,0:T(8,128)(2,1)} %bitcast.22), custom_call_target="tpu_custom_call" | custom-call | flops 8589934592 | bytes 16777216 | tf_op jit(solution)/shard_map/expand_keep/pallas_call | solution.py:495
  403.5 2.3 hop.4
  405.8 2.2 send.5
  410.2 7.7 %expand_send.6 = (bf16[2,1040,256]{2,1,0:T(8,128)(2,1)}, bf16[1024,512]{1,0:T(8,128)(2,1)S(1)}) custom-call(s32[1]{0:T(128)} %bitcast.1.place_ref, f32[2,1024,256]{2,1,0:T(8,128)S(1)} %copy-done.10, f32[2,1024,256]{2,1,0:T(8,128)} %collective-permute-done.29.mate, bf16[1040,256]{1,0:T(8,128)(2,1)} %collective-permute-done.30.refs_0_, bf16[4096,1024]{1,0:T(8,128)(2,1)} %bitcast.23), custom_call_target="tpu_custom_call" | custom-call | flops 8589934592 | bytes 16777216 | tf_op jit(solution)/shard_map/expand_send/pallas_call | solution.py:462
  419.2 17.8 %collective-permute-done.31.refs_0_ = bf16[2,1040,256]{2,1,0:T(8,128)(2,1)} collective-permute-done((bf16[2,1040,256]{2,1,0:T(8,128)(2,1)}, bf16[2,1040,256]{2,1,0:T(8,128)(2,1)}, u32[]{:S(2)}, u32[]{:S(2)}) %collective-permute-start.31) | collective-permute-done | bytes 1064992 | tf_op jit(solution)/shard_map/ppermute | solution.py:692
  437.0 3.3 hop.5
  440.4 7.6 %expand_send.7 = (bf16[2,1040,256]{2,1,0:T(8,128)(2,1)}, bf16[1024,512]{1,0:T(8,128)(2,1)S(1)}) custom-call(s32[1]{0:T(128)} %bitcast.1.place_ref, f32[2,1024,256]{2,1,0:T(8,128)S(1)} %copy-done.8, f32[2,1024,256]{2,1,0:T(8,128)} %collective-permute-done.23.mate, bf16[1040,256]{1,0:T(8,128)(2,1)S(1)} %collective-permute-done.24.refs_0_, ...), custom_call_target="tpu_custom_call" | custom-call | flops 8589934592 | bytes 16777216 | tf_op jit(solution)/shard_map/expand_send/pallas_call | solution.py:462
  449.0 5.4 %expand_keep.7.kept = f32[2,1024,256]{2,1,0:T(8,128)} custom-call(s32[1]{0:T(128)} %bitcast.1.place_ref, bf16[1024,512]{1,0:T(8,128)(2,1)} %copy-done.16, bf16[4096,1024]{1,0:T(8,128)(2,1)} %bitcast.25), custom_call_target="tpu_custom_call" | custom-call | flops 8589934592 | bytes 16777216 | tf_op jit(solution)/shard_map/expand_keep/pallas_call | solution.py:495
  454.3 5.3 expand_keep.6.kept
  459.7 11.6 %collective-permute-done.32.refs_0_ = bf16[2,1040,256]{2,1,0:T(8,128)(2,1)} collective-permute-done((bf16[2,1040,256]{2,1,0:T(8,128)(2,1)}, bf16[2,1040,256]{2,1,0:T(8,128)(2,1)}, u32[]{:S(2)}, u32[]{:S(2)}) %collective-permute-start.32) | collective-permute-done | bytes 1064992 | tf_op jit(solution)/shard_map/ppermute | solution.py:692
  472.8 2.5 hop.6
  475.4 29.2 %collective-permute-done.33.refs_0_ = bf16[2,1040,256]{2,1,0:T(8,128)(2,1)} collective-permute-done((bf16[2,1040,256]{2,1,0:T(8,128)(2,1)}, bf16[2,1040,256]{2,1,0:T(8,128)(2,1)}, u32[]{:S(2)}, u32[]{:S(2)}) %collective-permute-start.33) | collective-permute-done | bytes 1064992 | tf_op jit(solution)/shard_map/ppermute | solution.py:692
  504.7 2.5 hop.7
  507.3 3.4 finish.4.refs_2_
  510.7 3.4 finish.5.refs_2_
  514.1 3.3 finish.6.refs_2_
  517.4 14.4 %collective-permute-done.34.refs_1_ = bf16[1,1040,256]{2,1,0:T(8,128)(2,1)S(1)} collective-permute-done((bf16[1,1040,256]{2,1,0:T(8,128)(2,1)S(1)}, bf16[1,1040,256]{2,1,0:T(8,128)(2,1)S(1)}, u32[]{:S(2)}, u32[]{:S(2)}) %collective-permute-start.34) | collective-permute-done | bytes 532512 | tf_op jit(solution)/shard_map/ppermute | solution.py:692
  531.8 3.3 finish.7
  (103 shorter events, 34.3 us)
Async XLA Ops:
  0.6 49.0 %collective-permute-start = (bf16[1024,1024]{1,0:T(8,128)(2,1)}, bf16[1024,1024]{1,0:T(8,128)(2,1)}, u32[]{:S(2)}, u32[]{:S(2)}) collective-permute-start(bf16[1024,1024]{1,0:T(8,128)(2,1)} %param.8), channel_id=1, source_target_pairs={{0,2},{1,3},{2,0},{3,1},{4,6},{5,7},{6,4},{7,5},{8,10},{9,11},{10,... | collective-permute-start | bytes 6291464 | tf_op jit(solution)/shard_map/ppermute | solution.py:588
  3.6 48.4 %collective-permute-start.3 = (bf16[1024,1024]{1,0:T(8,128)(2,1)}, bf16[1024,1024]{1,0:T(8,128)(2,1)S(1)}, u32[]{:S(2)}, u32[]{:S(2)}) collective-permute-start(bf16[1024,1024]{1,0:T(8,128)(2,1)} %refs_2_.1), channel_id=1, source_target_pairs={{0,4},{4,8},{8,12},{1,5},{5,9},{9,13},{2,6},{6,10},{10,14},{3,7},{... | collective-permute-start | bytes 6291464 | tf_op jit(solution)/shard_map/ppermute | solution.py:605
  7.2 49.0 %collective-permute-start.5 = (bf16[1024,1024]{1,0:T(8,128)(2,1)}, bf16[1024,1024]{1,0:T(8,128)(2,1)}, u32[]{:S(2)}, u32[]{:S(2)}) collective-permute-start(bf16[1024,1024]{1,0:T(8,128)(2,1)} %refs_2_.1), channel_id=1, source_target_pairs={{4,0},{8,4},{12,8},{5,1},{9,5},{13,9},{6,2},{10,6},{14,10},{7,3},{... | collective-permute-start | bytes 6291464 | tf_op jit(solution)/shard_map/ppermute | solution.py:608
  8.5 52.8 %collective-permute-start.1 = (bf16[1024,1024]{1,0:T(8,128)(2,1)}, bf16[1024,1024]{1,0:T(8,128)(2,1)}, u32[]{:S(2)}, u32[]{:S(2)}) collective-permute-start(bf16[1024,1024]{1,0:T(8,128)(2,1)} %param.8), channel_id=1, source_target_pairs={{0,1},{1,0},{2,3},{3,2},{4,5},{5,4},{6,7},{7,6},{8,9},{9,8},{10,11... | collective-permute-start | bytes 6291464 | tf_op jit(solution)/shard_map/ppermute | solution.py:588
  49.6 13.6 %collective-permute-start.2 = (bf16[1024,1024]{1,0:T(8,128)(2,1)}, bf16[1024,1024]{1,0:T(8,128)(2,1)}, u32[]{:S(2)}, u32[]{:S(2)}) collective-permute-start(bf16[1024,1024]{1,0:T(8,128)(2,1)} %collective-permute-done), channel_id=1, source_target_pairs={{0,1},{1,0},{2,3},{3,2},{4,5},{5,4},{6,7},{7,6},{8,9},{9,8},{10,11... | collective-permute-start | bytes 6291464 | tf_op jit(solution)/shard_map/ppermute | solution.py:588
  52.0 13.1 %collective-permute-start.4 = (bf16[1024,1024]{1,0:T(8,128)(2,1)S(1)}, bf16[1024,1024]{1,0:T(8,128)(2,1)}, u32[]{:S(2)}, u32[]{:S(2)}) collective-permute-start(bf16[1024,1024]{1,0:T(8,128)(2,1)S(1)} %collective-permute-done.3.refs_1_), channel_id=1, source_target_pairs={{4,8},{8,12},{5,9},{9,13},{6,10},{10,14},{7,11},{11,15},{20,24},{2... | collective-permute-start | bytes 6291464 | tf_op jit(solution)/shard_map/ppermute | solution.py:605
  56.3 49.5 %collective-permute-start.6 = (bf16[1024,1024]{1,0:T(8,128)(2,1)}, bf16[1024,1024]{1,0:T(8,128)(2,1)}, u32[]{:S(2)}, u32[]{:S(2)}) collective-permute-start(bf16[1024,1024]{1,0:T(8,128)(2,1)} %collective-permute-done.5.refs_3_), channel_id=1, source_target_pairs={{4,0},{8,4},{5,1},{9,5},{6,2},{10,6},{7,3},{11,7},{20,16},{24,20},... | collective-permute-start | bytes 6291464 | tf_op jit(solution)/shard_map/ppermute | solution.py:608
  57.6 1.6 copy-start.22
  65.1 3.3 copy-start.20
  105.8 27.1 %collective-permute-start.7 = (bf16[1024,1024]{1,0:T(8,128)(2,1)}, bf16[1024,1024]{1,0:T(8,128)(2,1)}, u32[]{:S(2)}, u32[]{:S(2)}) collective-permute-start(bf16[1024,1024]{1,0:T(8,128)(2,1)} %collective-permute-done.4.refs_0_), channel_id=1, source_target_pairs={{8,12},{9,13},{10,14},{11,15},{24,28},{25,29},{26,30},{27,31}} | collective-permute-start | bytes 6291464 | tf_op jit(solution)/shard_map/ppermute | solution.py:605
  107.8 47.6 %collective-permute-start.8 = (bf16[1024,1024]{1,0:T(8,128)(2,1)}, bf16[1024,1024]{1,0:T(8,128)(2,1)}, u32[]{:S(2)}, u32[]{:S(2)}) collective-permute-start(bf16[1024,1024]{1,0:T(8,128)(2,1)} %collective-permute-done.6.refs_4_), channel_id=1, source_target_pairs={{4,0},{5,1},{6,2},{7,3},{20,16},{21,17},{22,18},{23,19}} | collective-permute-start | bytes 6291464 | tf_op jit(solution)/shard_map/ppermute | solution.py:608
  109.1 67.1 %collective-permute-start.9 = (bf16[1024,1024]{1,0:T(8,128)(2,1)}, bf16[1024,1024]{1,0:T(8,128)(2,1)}, u32[]{:S(2)}, u32[]{:S(2)}) collective-permute-start(bf16[1024,1024]{1,0:T(8,128)(2,1)} %piece.1), channel_id=1, source_target_pairs={{0,4},{4,8},{1,5},{5,9},{2,6},{6,10},{3,7},{7,11},{16,20},{20,24},... | collective-permute-start | bytes 6291464 | tf_op jit(solution)/shard_map/ppermute | solution.py:605
  116.3 59.9 %collective-permute-start.10 = (bf16[1024,1024]{1,0:T(8,128)(2,1)}, bf16[1024,1024]{1,0:T(8,128)(2,1)}, u32[]{:S(2)}, u32[]{:S(2)}) collective-permute-start(bf16[1024,1024]{1,0:T(8,128)(2,1)} %piece.1), channel_id=1, source_target_pairs={{8,4},{12,8},{9,5},{13,9},{10,6},{14,10},{11,7},{15,11},{24,20},{2... | collective-permute-start | bytes 6291464 | tf_op jit(solution)/shard_map/ppermute | solution.py:608
  155.3 23.4 %collective-permute-start.14 = (bf16[1024,1024]{1,0:T(8,128)(2,1)}, bf16[1024,1024]{1,0:T(8,128)(2,1)}, u32[]{:S(2)}, u32[]{:S(2)}) collective-permute-start(bf16[1024,1024]{1,0:T(8,128)(2,1)} %piece.1), channel_id=1, source_target_pairs={{8,12},{9,13},{10,14},{11,15},{24,28},{25,29},{26,30},{27,31}} | collective-permute-start | bytes 6291464 | tf_op jit(solution)/shard_map/ppermute | solution.py:605
  157.3 46.6 %collective-permute-start.13 = (bf16[1024,1024]{1,0:T(8,128)(2,1)}, bf16[1024,1024]{1,0:T(8,128)(2,1)}, u32[]{:S(2)}, u32[]{:S(2)}) collective-permute-start(bf16[1024,1024]{1,0:T(8,128)(2,1)} %piece.1), channel_id=1, source_target_pairs={{4,0},{5,1},{6,2},{7,3},{20,16},{21,17},{22,18},{23,19}} | collective-permute-start | bytes 6291464 | tf_op jit(solution)/shard_map/ppermute | solution.py:608
  176.1 37.2 %collective-permute-start.11 = (bf16[1040,1024]{1,0:T(8,128)(2,1)}, bf16[1040,1024]{1,0:T(8,128)(2,1)S(1)}, u32[]{:S(2)}, u32[]{:S(2)}) collective-permute-start(bf16[1040,1024]{1,0:T(8,128)(2,1)} %get-tuple-element.71), channel_id=1, source_target_pairs={{0,1},{1,0},{2,3},{3,2},{4,5},{5,4},{6,7},{7,6},{8,9},{9,8},{10,11... | collective-permute-start | bytes 6389768 | tf_op jit(solution)/shard_map/ppermute | solution.py:588
  176.1 52.0 %collective-permute-start.12 = (bf16[1040,1024]{1,0:T(8,128)(2,1)}, bf16[1040,1024]{1,0:T(8,128)(2,1)}, u32[]{:S(2)}, u32[]{:S(2)}) collective-permute-start(bf16[1040,1024]{1,0:T(8,128)(2,1)} %get-tuple-element.71), channel_id=1, source_target_pairs={{0,2},{1,3},{2,0},{3,1},{4,6},{5,7},{6,4},{7,5},{8,10},{9,11},{10,... | collective-permute-start | bytes 6389768 | tf_op jit(solution)/shard_map/ppermute | solution.py:588
  176.7 51.4 %collective-permute-start.17 = (bf16[1024,1024]{1,0:T(8,128)(2,1)}, bf16[1024,1024]{1,0:T(8,128)(2,1)}, u32[]{:S(2)}, u32[]{:S(2)}) collective-permute-start(bf16[1024,1024]{1,0:T(8,128)(2,1)} %collective-permute-done.10), channel_id=1, source_target_pairs={{8,4},{9,5},{10,6},{11,7},{24,20},{25,21},{26,22},{27,23}} | collective-permute-start | bytes 6291464 | tf_op jit(solution)/shard_map/ppermute | solution.py:608
  178.7 50.7 %collective-permute-start.19 = (bf16[1024,1024]{1,0:T(8,128)(2,1)}, bf16[1024,1024]{1,0:T(8,128)(2,1)}, u32[]{:S(2)}, u32[]{:S(2)}) collective-permute-start(bf16[1024,1024]{1,0:T(8,128)(2,1)} %collective-permute-done.9), channel_id=1, source_target_pairs={{4,8},{5,9},{6,10},{7,11},{20,24},{21,25},{22,26},{23,27}} | collective-permute-start | bytes 6291464 | tf_op jit(solution)/shard_map/ppermute | solution.py:605
  203.9 27.6 %collective-permute-start.18 = (bf16[1024,1024]{1,0:T(8,128)(2,1)}, bf16[1024,1024]{1,0:T(8,128)(2,1)}, u32[]{:S(2)}, u32[]{:S(2)}) collective-permute-start(bf16[1024,1024]{1,0:T(8,128)(2,1)} %collective-permute-done.9), channel_id=1, source_target_pairs={{8,12},{9,13},{10,14},{11,15},{24,28},{25,29},{26,30},{27,31}} | collective-permute-start | bytes 6291464 | tf_op jit(solution)/shard_map/ppermute | solution.py:605
  213.3 4.4 copy-start.21
  213.3 50.8 %collective-permute-start.16 = (bf16[1024,1024]{1,0:T(8,128)(2,1)}, bf16[1024,1024]{1,0:T(8,128)(2,1)}, u32[]{:S(2)}, u32[]{:S(2)}) collective-permute-start(bf16[1024,1024]{1,0:T(8,128)(2,1)} %collective-permute-done.10), channel_id=1, source_target_pairs={{4,0},{5,1},{6,2},{7,3},{20,16},{21,17},{22,18},{23,19}} | collective-permute-start | bytes 6291464 | tf_op jit(solution)/shard_map/ppermute | solution.py:608
  228.1 45.2 %collective-permute-start.15 = (bf16[1040,1024]{1,0:T(8,128)(2,1)}, bf16[1040,1024]{1,0:T(8,128)(2,1)}, u32[]{:S(2)}, u32[]{:S(2)}) collective-permute-start(bf16[1040,1024]{1,0:T(8,128)(2,1)} %collective-permute-done.12.message.scales), channel_id=1, source_target_pairs={{0,1},{1,0},{2,3},{3,2},{4,5},{5,4},{6,7},{7,6},{8,9},{9,8},{10,11... | collective-permute-start | bytes 6389768 | tf_op jit(solution)/shard_map/ppermute | solution.py:588
  228.1 83.4 %collective-permute-start.20 = (bf16[1024,1024]{1,0:T(8,128)(2,1)}, bf16[1024,1024]{1,0:T(8,128)(2,1)S(1)}, u32[]{:S(2)}, u32[]{:S(2)}) collective-permute-start(bf16[1024,1024]{1,0:T(8,128)(2,1)} %collective-permute-done.17), channel_id=1, source_target_pairs={{4,0},{5,1},{6,2},{7,3},{20,16},{21,17},{22,18},{23,19}} | collective-permute-start | bytes 6291464 | tf_op jit(solution)/shard_map/ppermute | solution.py:608
  229.4 82.1 %collective-permute-start.21 = (bf16[1024,1024]{1,0:T(8,128)(2,1)}, bf16[1024,1024]{1,0:T(8,128)(2,1)}, u32[]{:S(2)}, u32[]{:S(2)}) collective-permute-start(bf16[1024,1024]{1,0:T(8,128)(2,1)} %collective-permute-done.19), channel_id=1, source_target_pairs={{8,12},{9,13},{10,14},{11,15},{24,28},{25,29},{26,30},{27,31}} | collective-permute-start | bytes 6291464 | tf_op jit(solution)/shard_map/ppermute | solution.py:605
  309.4 2.1 copy-start.6
  326.8 2.0 copy-start.15
  341.5 7.2 %copy-start.11 = (f32[2,1024,256]{2,1,0:T(8,128)}, f32[2,1024,256]{2,1,0:T(8,128)S(1)}, u32[]{:S(2)}) copy-start(f32[2,1024,256]{2,1,0:T(8,128)S(1)} %get-tuple-element.100.keep) | copy-start | bytes 6291460
  341.5 4.2 collective-permute-start.22
  341.6 7.1 %collective-permute-start.25 = (f32[2,1024,256]{2,1,0:T(8,128)S(1)}, f32[2,1024,256]{2,1,0:T(8,128)S(1)}, u32[]{:S(2)}, u32[]{:S(2)}) collective-permute-start(f32[2,1024,256]{2,1,0:T(8,128)S(1)} %get-tuple-element.101), channel_id=1, source_target_pairs={{0,1},{1,0},{2,3},{3,2},{4,5},{5,4},{6,7},{7,6},{8,9},{9,8},{10,11... | collective-permute-start | bytes 6291464 | tf_op jit(solution)/shard_map/ppermute | solution.py:588
  346.6 18.0 %collective-permute-start.27 = (bf16[1040,256]{1,0:T(8,128)(2,1)S(1)}, bf16[1040,256]{1,0:T(8,128)(2,1)S(1)}, u32[]{:S(2)}, u32[]{:S(2)}) collective-permute-start(bf16[1040,256]{1,0:T(8,128)(2,1)S(1)} %send.4), channel_id=1, source_target_pairs={{0,2},{1,3},{2,0},{3,1},{4,6},{5,7},{6,4},{7,5},{8,10},{9,11},{10,... | collective-permute-start | bytes 1597448 | tf_op jit(solution)/shard_map/ppermute | solution.py:588
  348.7 1.4 copy-start.13
  350.1 28.0 %collective-permute-start.26 = (bf16[1040,256]{1,0:T(8,128)(2,1)S(1)}, bf16[1040,256]{1,0:T(8,128)(2,1)S(1)}, u32[]{:S(2)}, u32[]{:S(2)}) collective-permute-start(bf16[1040,256]{1,0:T(8,128)(2,1)S(1)} %send.6), channel_id=1, source_target_pairs={{0,2},{1,3},{2,0},{3,1},{4,6},{5,7},{6,4},{7,5},{8,10},{9,11},{10,... | collective-permute-start | bytes 1597448 | tf_op jit(solution)/shard_map/ppermute | solution.py:588
  364.0 8.8 %copy-start.7 = (f32[2,1024,256]{2,1,0:T(8,128)}, f32[2,1024,256]{2,1,0:T(8,128)S(1)}, u32[]{:S(2)}) copy-start(f32[2,1024,256]{2,1,0:T(8,128)S(1)} %get-tuple-element.98.keep) | copy-start | bytes 6291460
  364.0 30.2 %copy-start.9 = (f32[2,1024,256]{2,1,0:T(8,128)}, f32[2,1024,256]{2,1,0:T(8,128)S(1)}, u32[]{:S(2)}) copy-start(f32[2,1024,256]{2,1,0:T(8,128)S(1)} %get-tuple-element.109.keep) | copy-start | bytes 6291460
  364.0 30.2 %collective-permute-start.29 = (f32[2,1024,256]{2,1,0:T(8,128)}, f32[2,1024,256]{2,1,0:T(8,128)}, u32[]{:S(2)}, u32[]{:S(2)}) collective-permute-start(f32[2,1024,256]{2,1,0:T(8,128)} %get-tuple-element.110), channel_id=1, source_target_pairs={{0,1},{1,0},{2,3},{3,2},{4,5},{5,4},{6,7},{7,6},{8,9},{9,8},{10,11... | collective-permute-start | bytes 6291464 | tf_op jit(solution)/shard_map/ppermute | solution.py:588
  364.1 41.7 %collective-permute-start.23 = (f32[2,1024,256]{2,1,0:T(8,128)}, f32[2,1024,256]{2,1,0:T(8,128)}, u32[]{:S(2)}, u32[]{:S(2)}) collective-permute-start(f32[2,1024,256]{2,1,0:T(8,128)} %get-tuple-element.99), channel_id=1, source_target_pairs={{0,1},{1,0},{2,3},{3,2},{4,5},{5,4},{6,7},{7,6},{8,9},{9,8},{10,11... | collective-permute-start | bytes 6291464 | tf_op jit(solution)/shard_map/ppermute | solution.py:588
  372.7 1.0 copy-start.19
  373.7 29.8 %collective-permute-start.28 = (bf16[2,1040,256]{2,1,0:T(8,128)(2,1)}, bf16[2,1040,256]{2,1,0:T(8,128)(2,1)S(1)}, u32[]{:S(2)}, u32[]{:S(2)}) collective-permute-start(bf16[2,1040,256]{2,1,0:T(8,128)(2,1)} %get-tuple-element.102), channel_id=1, source_target_pairs={{0,4},{4,0},{8,12},{12,8},{1,5},{5,1},{9,13},{13,9},{2,6},{6,2},{1... | collective-permute-start | bytes 3194888 | tf_op jit(solution)/shard_map/ppermute | solution.py:692
  383.5 1.6 copy-start.12
  385.1 1.6 copy-start.14
  394.0 2.4 copy-start.17
  394.0 43.0 %collective-permute-start.31 = (bf16[2,1040,256]{2,1,0:T(8,128)(2,1)}, bf16[2,1040,256]{2,1,0:T(8,128)(2,1)}, u32[]{:S(2)}, u32[]{:S(2)}) collective-permute-start(bf16[2,1040,256]{2,1,0:T(8,128)(2,1)} %get-tuple-element.106), channel_id=1, source_target_pairs={{0,4},{4,0},{8,12},{12,8},{1,5},{5,1},{9,13},{13,9},{2,6},{6,2},{1... | collective-permute-start | bytes 3194888 | tf_op jit(solution)/shard_map/ppermute | solution.py:692
  396.4 13.8 %collective-permute-start.30 = (bf16[1040,256]{1,0:T(8,128)(2,1)S(1)}, bf16[1040,256]{1,0:T(8,128)(2,1)}, u32[]{:S(2)}, u32[]{:S(2)}) collective-permute-start(bf16[1040,256]{1,0:T(8,128)(2,1)S(1)} %send.7), channel_id=1, source_target_pairs={{0,2},{1,3},{2,0},{3,1},{4,6},{5,7},{6,4},{7,5},{8,10},{9,11},{10,... | collective-permute-start | bytes 1597448 | tf_op jit(solution)/shard_map/ppermute | solution.py:588
  398.0 5.5 %copy-start = (f32[2,1024,256]{2,1,0:T(8,128)S(1)}, f32[2,1024,256]{2,1,0:T(8,128)}, u32[]{:S(2)}) copy-start(f32[2,1024,256]{2,1,0:T(8,128)} %expand_keep.5.kept) | copy-start | bytes 6291460
  403.5 2.3 copy-start.8
  405.8 101.5 %collective-permute-start.37 = (bf16[1,1040,256]{2,1,0:T(8,128)(2,1)}, bf16[1,1040,256]{2,1,0:T(8,128)(2,1)}, u32[]{:S(2)}, u32[]{:S(2)}) collective-permute-start(bf16[1,1040,256]{2,1,0:T(8,128)(2,1)} %hop.4), channel_id=1, source_target_pairs={{0,8},{4,12},{8,0},{12,4},{1,9},{5,13},{9,1},{13,5},{2,10},{6,14},... | collective-permute-start | bytes 1597448 | tf_op jit(solution)/shard_map/ppermute | solution.py:692
  405.8 4.4 copy-start.10
  408.0 29.0 %copy-start.1 = (f32[2,1024,256]{2,1,0:T(8,128)S(1)}, f32[2,1024,256]{2,1,0:T(8,128)}, u32[]{:S(2)}) copy-start(f32[2,1024,256]{2,1,0:T(8,128)} %expand_keep.4.kept) | copy-start | bytes 6291460
  408.0 32.4 %collective-permute-start.24 = (bf16[1040,256]{1,0:T(8,128)(2,1)S(1)}, bf16[1040,256]{1,0:T(8,128)(2,1)S(1)}, u32[]{:S(2)}, u32[]{:S(2)}) collective-permute-start(bf16[1040,256]{1,0:T(8,128)(2,1)S(1)} %send.5), channel_id=1, source_target_pairs={{0,2},{1,3},{2,0},{3,1},{4,6},{5,7},{6,4},{7,5},{8,10},{9,11},{10,... | collective-permute-start | bytes 1597448 | tf_op jit(solution)/shard_map/ppermute | solution.py:588
  417.9 22.5 %copy-start.16 = (bf16[1024,512]{1,0:T(8,128)(2,1)}, bf16[1024,512]{1,0:T(8,128)(2,1)S(1)}, u32[]{:S(2)}) copy-start(bf16[1024,512]{1,0:T(8,128)(2,1)S(1)} %get-tuple-element.116.both) | copy-start | bytes 3145732
  417.9 53.4 %collective-permute-start.32 = (bf16[2,1040,256]{2,1,0:T(8,128)(2,1)}, bf16[2,1040,256]{2,1,0:T(8,128)(2,1)}, u32[]{:S(2)}, u32[]{:S(2)}) collective-permute-start(bf16[2,1040,256]{2,1,0:T(8,128)(2,1)} %get-tuple-element.112), channel_id=1, source_target_pairs={{0,4},{4,0},{8,12},{12,8},{1,5},{5,1},{9,13},{13,9},{2,6},{6,2},{1... | collective-permute-start | bytes 3194888 | tf_op jit(solution)/shard_map/ppermute | solution.py:692
  440.4 70.3 %collective-permute-start.36 = (bf16[1,1040,256]{2,1,0:T(8,128)(2,1)}, bf16[1,1040,256]{2,1,0:T(8,128)(2,1)S(1)}, u32[]{:S(2)}, u32[]{:S(2)}) collective-permute-start(bf16[1,1040,256]{2,1,0:T(8,128)(2,1)} %hop.5), channel_id=1, source_target_pairs={{0,8},{4,12},{8,0},{12,4},{1,9},{5,13},{9,1},{13,5},{2,10},{6,14},... | collective-permute-start | bytes 1597448 | tf_op jit(solution)/shard_map/ppermute | solution.py:692
  448.0 1.0 copy-start.18
  449.0 55.7 %collective-permute-start.33 = (bf16[2,1040,256]{2,1,0:T(8,128)(2,1)}, bf16[2,1040,256]{2,1,0:T(8,128)(2,1)}, u32[]{:S(2)}, u32[]{:S(2)}) collective-permute-start(bf16[2,1040,256]{2,1,0:T(8,128)(2,1)} %get-tuple-element.118), channel_id=1, source_target_pairs={{0,4},{4,0},{8,12},{12,8},{1,5},{5,1},{9,13},{13,9},{2,6},{6,2},{1... | collective-permute-start | bytes 3194888 | tf_op jit(solution)/shard_map/ppermute | solution.py:692
  459.7 45.0 %copy-start.3 = (f32[2,1024,256]{2,1,0:T(8,128)S(1)}, f32[2,1024,256]{2,1,0:T(8,128)}, u32[]{:S(2)}) copy-start(f32[2,1024,256]{2,1,0:T(8,128)} %expand_keep.6.kept) | copy-start | bytes 6291460
  471.2 1.6 copy-start.4
  475.3 38.8 %collective-permute-start.35 = (bf16[1,1040,256]{2,1,0:T(8,128)(2,1)S(1)}, bf16[1,1040,256]{2,1,0:T(8,128)(2,1)S(1)}, u32[]{:S(2)}, u32[]{:S(2)}) collective-permute-start(bf16[1,1040,256]{2,1,0:T(8,128)(2,1)S(1)} %hop.6), channel_id=1, source_target_pairs={{0,8},{4,12},{8,0},{12,4},{1,9},{5,13},{9,1},{13,5},{2,10},{6,14},... | collective-permute-start | bytes 1597448 | tf_op jit(solution)/shard_map/ppermute | solution.py:692
  507.2 3.5 copy-start.2
  507.2 24.6 %collective-permute-start.34 = (bf16[1,1040,256]{2,1,0:T(8,128)(2,1)S(1)}, bf16[1,1040,256]{2,1,0:T(8,128)(2,1)S(1)}, u32[]{:S(2)}, u32[]{:S(2)}) collective-permute-start(bf16[1,1040,256]{2,1,0:T(8,128)(2,1)S(1)} %hop.7), channel_id=1, source_target_pairs={{0,8},{4,12},{8,0},{12,4},{1,9},{5,13},{9,1},{13,5},{2,10},{6,14},... | collective-permute-start | bytes 1597448 | tf_op jit(solution)/shard_map/ppermute | solution.py:692
  510.7 3.4 copy-start.5
